TPU v7x, 32 devices: a whole 2x2x4 slice. The times are simulated.
32 devices in a mesh: kv: 4 (over y, x), blk: 8 (over z, core).
Axes of the slice: x: 2, y: 2, z: 4, core: 2. Of those that a mesh axis runs over, the one named last changes fastest.
Arguments:
- queries: bfloat16 [32, 4096], P('blk', 'kv'), may hold values from -120 to 120
- cache_keys: bfloat16 [32, 4096, 4, 128], P('blk', None, 'kv'), may hold values from -5 to 5
- cache_values: bfloat16 [32, 4096, 4, 128], P('blk', None, 'kv'), may hold values from -6 to 6
- lengths: int32 [32], replicated, may hold values from 1 to 32768, as said below
- sinks: float32 [32], P('kv'), may hold values from 5 to 11
- out_proj: bfloat16 [4096, 2048], P('kv'), may hold values from -0.09375 to 0.09375
- decode_resid: bfloat16 [32, 2048], P(('blk', 'kv')), may hold values from -4 to 4
- prefill_hidden: bfloat16 [32, 111, 2048], P(('blk', 'kv')), may hold values from -6 to 6
- norm_gain: float32 [2048], replicated, may hold values from 0.1 to 1.9
- router: bfloat16 [2048, 32], replicated, may hold values from -80 to 80
- routes: int32 [32, 112, 8], P(('blk', 'kv')), may hold values from 0 to 31, all different within a row; in each aligned block of 112 rows (0 to 111, 112 to 223, ..., all dimensions but the last counted through in order) at most 56 rows name the same one
- expert_gate: bfloat16 [32, 2048, 768], P(('kv', 'blk')), may hold values from -0.125 to 0.125
- expert_up: bfloat16 [32, 2048, 768], P(('kv', 'blk')), may hold values from -0.125 to 0.125
- expert_down: bfloat16 [32, 768, 2048], P(('kv', 'blk')), may hold values from -0.21875 to 0.21875
Outputs:
- layer_out: bfloat16 [32, 112, 2048], P(('blk', 'kv'))
Inputs may be any that keep to these rules, and one draw needn't show every extreme that they name: `lengths`: at least one request has exactly 32768 cached positions. `routes`: within the rows of one device (112 rows, aligned blocks) no expert is named by more than 56 rows, and in every draw some expert reaches 56 in some block.
All inputs are finite; a program needn't handle non-finite values.
Results may differ from a plain program's by a relative error of at most 0.0094.
Values may be sent and summed in bfloat16 or wider, within the bound.
No kernel may reach another device: no remote copies, remote signals or barrier semaphores. Data moves between devices by JAX's collectives and lax.ppermute only.
A program may use at most 128 MiB of HBM per device.

v0:
```python
import math

import jax
import jax.numpy as jnp
from jax import lax
from jax.sharding import PartitionSpec as P

NEG_FILL = -1e30
EPSILON = 1e-06


def expert_block(slots, gate_weights, up_weights, down_weights):
    local_count = gate_weights.shape[0]
    slot_shape = slots.shape
    grouped = slots.reshape(slot_shape[0] // local_count, local_count, slot_shape[1], slot_shape[2])
    gate_act = jnp.einsum(
        "secd,edf->secf", grouped, gate_weights, preferred_element_type=jnp.float32
    )
    up_act = jnp.einsum("secd,edf->secf", grouped, up_weights, preferred_element_type=jnp.float32)
    inner_act = (jax.nn.silu(gate_act) * up_act).astype(jnp.bfloat16)
    result = jnp.einsum(
        "secf,efd->secd", inner_act, down_weights, preferred_element_type=jnp.float32
    )
    return result.astype(jnp.bfloat16).reshape(slot_shape)


def route_weights(rows, ids, router):
    experts = router.shape[1]
    logits = jnp.dot(rows, router, preferred_element_type=jnp.float32)
    one_hot = ids[..., None] == jnp.arange(experts, dtype=jnp.int32)
    chosen = jnp.sum(jnp.where(one_hot, logits[:, None, :], 0.0), axis=2)
    return (jax.nn.softmax(chosen, axis=1), one_hot)


def body(
    queries,
    cache_keys,
    cache_values,
    lengths,
    sinks,
    out_proj,
    decode_resid,
    prefill_hidden,
    norm_gain,
    router,
    routes,
    expert_gate,
    expert_up,
    expert_down,
):
    my_block = lax.axis_index("blk")
    per_block = queries.shape[0]
    head_count = sinks.shape[0]
    head_dim = cache_keys.shape[3]
    window = cache_keys.shape[1]
    grouped_q = queries.reshape(per_block, head_count, head_dim)
    key_rows = cache_keys[:, :, 0, :]
    value_rows = cache_values[:, :, 0, :]
    my_lengths = lax.dynamic_slice_in_dim(lengths, my_block * per_block, per_block)
    scores = jnp.einsum("rgd,rjd->rgj", grouped_q, key_rows, preferred_element_type=jnp.float32) * (
        1.0 / math.sqrt(head_dim)
    )
    first_valid = window - jnp.minimum(my_lengths, window)
    is_valid = (jnp.arange(window, dtype=jnp.int32)[None, :] >= first_valid[:, None])[:, None, :]
    masked = jnp.where(is_valid, scores, NEG_FILL)
    top_limit = jnp.maximum(jnp.max(masked, axis=2), sinks[None, :])
    weights = jnp.where(is_valid, jnp.exp(masked - top_limit[..., None]), 0.0)
    denominator = jnp.sum(weights, axis=2) + jnp.exp(sinks[None, :] - top_limit)
    numerator = jnp.einsum(
        "rgj,rjd->rgd", weights.astype(jnp.bfloat16), value_rows, preferred_element_type=jnp.float32
    )
    attended = (
        (numerator / denominator[..., None])
        .astype(jnp.bfloat16)
        .reshape(per_block, head_count * head_dim)
    )
    partial_proj = jnp.dot(attended, out_proj, preferred_element_type=jnp.float32)
    projected = lax.psum_scatter(partial_proj, "kv", scatter_dimension=0, tiled=True)
    decoded = (decode_resid.astype(jnp.float32) + projected).astype(jnp.bfloat16)
    hidden = jnp.concatenate([decoded, prefill_hidden[0]], axis=0)
    hidden_f = hidden.astype(jnp.float32)
    mean_sq = jnp.mean(hidden_f * hidden_f, axis=1, keepdims=True)
    normed = (hidden_f * lax.rsqrt(mean_sq + EPSILON) * norm_gain).astype(jnp.bfloat16)
    experts = router.shape[1]
    chosen_ids = routes[0]
    tokens = chosen_ids.shape[0]
    top_k = chosen_ids.shape[1]
    model_width = hidden.shape[1]
    capacity = max(2, (2 * tokens * top_k + experts - 1) // experts)
    gate_probs, one_hot = route_weights(normed, chosen_ids, router)
    flat_ids = chosen_ids.reshape(-1)
    flat_hot = one_hot.reshape(tokens * top_k, experts).astype(jnp.int32)
    before = jnp.cumsum(flat_hot, axis=0) - flat_hot
    slot_rank = jnp.sum(before * flat_hot, axis=1)
    slot_index = flat_ids * capacity + slot_rank
    outgoing = (
        jnp.zeros((experts * capacity, model_width), jnp.bfloat16)
        .at[slot_index]
        .set(jnp.repeat(normed, top_k, axis=0))
    )
    outgoing = outgoing.reshape(experts, capacity, model_width)
    processed = expert_block(
        lax.all_to_all(outgoing, ("kv", "blk"), split_axis=0, concat_axis=0, tiled=True),
        expert_gate,
        expert_up,
        expert_down,
    )
    returned = lax.all_to_all(processed, ("kv", "blk"), split_axis=0, concat_axis=0, tiled=True)
    results = returned.reshape(experts * capacity, model_width)[slot_index]
    results = results.astype(jnp.float32).reshape(tokens, top_k, model_width)
    combined = jnp.sum(gate_probs[..., None] * results, axis=1)
    layer_sum = (hidden_f + combined).astype(jnp.bfloat16)
    return layer_sum[None]


def solution(mesh):
    return jax.shard_map(
        body,
        mesh=mesh,
        in_specs=(
            P("blk", "kv"),
            P("blk", None, "kv", None),
            P("blk", None, "kv", None),
            P(),
            P("kv"),
            P("kv", None),
            P(("blk", "kv"), None),
            P(("blk", "kv"), None, None),
            P(),
            P(),
            P(("blk", "kv"), None, None),
            P(("kv", "blk"), None, None),
            P(("kv", "blk"), None, None),
            P(("kv", "blk"), None, None),
        ),
        out_specs=P(("blk", "kv"), None, None),
        check_vma=False,
    )
```

profile of v0, /device:TPU:0, one launch (start us, length us, event | category | flops | bytes accessed | tf_op | source)
XLA Modules:
  0.0 426.5 jit_solution(826708153984742358)
XLA Ops:
  0.0 0.0 copy-start
  0.0 0.0 copy-start.9
  0.0 0.9 broadcast_multiply_fusion
  0.9 0.9 copy.31
  1.8 0.1 eq.42
  1.9 0.1 eq.38
  1.9 0.7 minimum_subtract_fusion
  2.7 0.1 iota_compare_fusion.3
  2.8 0.1 copy.30
  2.9 0.1 mul.73
  3.0 2.0 reduce-window.6
  5.0 0.3 slice_reduce_fusion
  5.3 0.0 copy-start.2
  5.3 0.0 copy-start.3
  5.4 3.6 fusion.56
  9.0 0.0 copy-done.9
  9.0 0.3 fusion.35
  9.3 0.0 copy-done.2
  9.3 0.0 copy-start.11
  9.3 0.0 copy-start.8
  9.3 0.0 copy-start.7
  9.3 0.7 fusion.24
  10.1 0.0 copy-done.3
  10.1 0.7 fusion.45
  10.7 17.7 %all-reduce = f32[4,2048]{1,0:T(4,128)S(1)} all-reduce(f32[4,2048]{1,0:T(4,128)S(1)} %fusion.45), channel_id=2, replica_groups=mesh['kv'=4,'blk'=8] {'kv'}, use_global_device_ids=true, to_apply=%region_2.3.clone | all-reduce | flops 8192 | bytes 65536
  28.5 0.0 copy-done.11
  28.5 0.6 dynamic-slice
  29.1 0.0 copy-done.8
  29.1 0.7 fusion.50
  29.8 1.3 fusion.27
  31.1 0.1 fusion.43
  31.2 0.0 copy-done.7
  31.2 2.0 fusion.29
  33.3 11.5 %scatter_custom_fusion = bf16[1792,2048]{1,0:T(8,128)(2,1)} fusion(s32[896]{0:T(1024)S(1)} %fusion.53, bf16[]{:T(256)} %constant.13.clone.1, bf16[112,2048]{1,0:T(8,128)(2,1)} %fusion.29), kind=kCustom, calls=%fused_computation.17 | custom fusion | bytes 7798786 | tf_op jit(solution)/shard_map/scatter | solution.py:99
  44.7 0.0 copy-start.10
  44.7 166.4 %all_to_all.10 = bf16[32,56,2048]{2,1,0:T(8,128)(2,1)S(1)} all-to-all(bf16[32,56,2048]{2,1,0:T(8,128)(2,1)} %bitcast.119), channel_id=1, replica_groups=mesh['kv'=4,'blk'=8] {'kv','blk'}, dimensions={0} | all-to-all | bytes 14680064 | tf_op jit(solution)/shard_map/all_to_all | solution.py:103
  211.1 0.0 copy-start.1
  211.1 3.0 copy-done.1
  214.2 0.0 copy-done.10
  214.2 7.6 %fusion.13 = f32[32,56,768]{2,1,0:T(8,128)} fusion(bf16[32,56,2048]{2,1,0:T(8,128)(2,1)S(1)} %all_to_all.10, bf16[1,2048,768]{2,1,0:T(8,128)(2,1)S(1)} %copy-done.10), kind=kOutput, calls=%fused_computation.21 | convolution fusion | flops 5637144576 | bytes 15990784 | tf_op jit(solution)/shard_map/secd,edf->secf/dot_general | solution.py:19
  221.8 0.0 copy-done
  221.8 19.2 %convolution_convert_fusion = bf16[32,56,2048]{2,1,0:T(8,128)(2,1)} fusion(bf16[1,768,2048]{2,1,0:T(8,128)(2,1)S(1)} %copy-done, f32[32,56,768]{2,1,0:T(8,128)} %fusion.13, bf16[32,56,2048]{2,1,0:T(8,128)(2,1)} %copy-done.1, bf16[1,2048,768]{2,1,0:T(8,128)(2,1)} %param.25), kind=kOutput, calls=%fused_computation.11 | convolution fusion | flops 11286216704 | bytes 26476544 | tf_op jit(solution)/shard_map/secf,efd->secd/dot_general | solution.py:21
  240.9 0.0 copy-start.5
  240.9 0.0 copy-start.6
  240.9 4.0 all-to-all-start.1
  244.9 0.0 copy-done.5
  244.9 1.3 fusion.57
  246.2 0.0 copy-done.6
  246.3 0.1 copy.29
  246.4 160.7 %all-to-all-done.1 = bf16[32,56,2048]{2,1,0:T(8,128)(2,1)} async-done(((bf16[32,56,2048]{2,1,0:T(8,128)(2,1)}), bf16[32,56,2048]{2,1,0:T(8,128)(2,1)}, u32[]{:S(2)}, u32[]{:S(2)}) %all-to-all-start.1) | async-done | bytes 7340064 | tf_op jit(solution)/shard_map/all_to_all | solution.py:108
  407.2 12.8 %gather_fusion = bf16[896,2048]{1,0:T(8,128)(2,1)} fusion(bf16[1792,2048]{1,0:T(8,128)(2,1)} %bitcast.23, s32[1024]{0:T(1024)S(1)} %pad_clamp_fusion), kind=kCustom, calls=%fused_computation | custom fusion | bytes 7343616 | tf_op jit(solution)/shard_map/gather | solution.py:109
  420.0 0.0 copy-start.4
  420.0 5.6 %fusion = f32[112,2048]{1,0:T(8,128)S(1)} fusion(bf16[896,2048]{1,0:T(8,128)(2,1)} %gather_fusion, f32[112,8]{1,0:T(8,128)S(1)} %copy.29), kind=kLoop, calls=%fused_computation.3 | loop fusion | flops 5275648 | bytes 4591104 | tf_op jit(solution)/shard_map/reduce_sum | solution.py:111
  425.6 0.0 copy-done.4
  425.6 0.9 fusion.30
  (11 shorter events, 0.2 us)
Async XLA Ops:
  0.0 221.8 %copy-start = (bf16[1,768,2048]{2,1,0:T(8,128)(2,1)S(1)}, bf16[1,768,2048]{2,1,0:T(8,128)(2,1)}, u32[]{:S(2)}) copy-start(bf16[1,768,2048]{2,1,0:T(8,128)(2,1)} %param.27) | copy-start | bytes 9437188
  0.0 9.0 %copy-start.9 = (f32[8]{0:T(128)S(1)}, f32[8]{0:T(128)}, u32[]{:S(2)}) copy-start(f32[8]{0:T(128)} %param.18) | copy-start | bytes 100
  5.3 3.9 copy-start.2
  5.3 4.7 %copy-start.3 = (bf16[1024,2048]{1,0:T(8,128)(2,1)S(1)}, bf16[1024,2048]{1,0:T(8,128)(2,1)}, u32[]{:S(2)}) copy-start(bf16[1024,2048]{1,0:T(8,128)(2,1)} %param.19) | copy-start | bytes 12582916
  9.3 19.2 %copy-start.11 = (u32[32]{0:T(128)S(1)}, u32[32]{0:T(128)}, u32[]{:S(2)}) copy-start(u32[32]{0:T(128)} %constant.51) | copy-start | bytes 388
  9.3 19.8 %copy-start.8 = (bf16[1,2048]{1,0:T(2,128)(2,1)S(1)}, bf16[1,2048]{1,0:T(2,128)(2,1)}, u32[]{:S(2)}) copy-start(bf16[1,2048]{1,0:T(2,128)(2,1)} %param.20) | copy-start | bytes 12292
  9.3 21.9 %copy-start.7 = (f32[2048]{0:T(1024)S(1)}, f32[2048]{0:T(1024)}, u32[]{:S(2)}) copy-start(f32[2048]{0:T(1024)} %param.22) | copy-start | bytes 24580
  44.7 169.4 %copy-start.10 = (bf16[1,2048,768]{2,1,0:T(8,128)(2,1)S(1)}, bf16[1,2048,768]{2,1,0:T(8,128)(2,1)}, u32[]{:S(2)}) copy-start(bf16[1,2048,768]{2,1,0:T(8,128)(2,1)} %param.26) | copy-start | bytes 9437188
  211.1 3.0 copy-start.1
  240.9 4.0 copy-start.5
  240.9 5.3 %copy-start.6 = (s32[1,112,8]{1,2,0:T(8,128)S(1)}, s32[1,112,8]{1,2,0:T(8,128)}, u32[]{:S(2)}) copy-start(s32[1,112,8]{1,2,0:T(8,128)} %param.24) | copy-start | bytes 10756
  240.9 166.2 %all-to-all-start.1 = ((bf16[32,56,2048]{2,1,0:T(8,128)(2,1)}), bf16[32,56,2048]{2,1,0:T(8,128)(2,1)}, u32[]{:S(2)}, u32[]{:S(2)}) async-start(bf16[32,56,2048]{2,1,0:T(8,128)(2,1)} %convolution_convert_fusion), calls=%async_computation.1 | async-start | bytes 14680064 | tf_op jit(solution)/shard_map/all_to_all | solution.py:108
  420.0 5.6 %copy-start.4 = (bf16[1,111,2048]{2,1,0:T(8,128)(2,1)S(1)}, bf16[1,111,2048]{2,1,0:T(8,128)(2,1)}, u32[]{:S(2)}) copy-start(bf16[1,111,2048]{2,1,0:T(8,128)(2,1)} %param.21) | copy-start | bytes 1363972
where the time goes:
time: 427 us
  blocking collectives  184 us (43%)
  waiting for transfers between devices  161 us (38%)
  matrix products  33 us (8%)
  local copies, waits for them, and re-layouts  29.6 us (7%)
  other arithmetic  14.8 us (3%)
    all_to_all x1, blocking collectives, body(): lax.all_to_all(outgoing, ('kv', 'blk'), split_axis=0, concat_axis=0, tile...  166 us
    all_to_all x1, waiting for transfers between devices, body(): lax.all_to_all(processed, ('kv', 'blk'), split_axis=0, concat_axis=0, til...  161 us
    dot_general x1, matrix products, expert_block(): jnp.einsum('secf,efd->secd', inner_act, down_weights, preferred_element_t...  19.2 us
    unnamed x1, blocking collectives  17.7 us
    gather x1, local copies, waits for them, and re-layouts, body(): results = returned.reshape(experts * capacity, model_width)[slot_index]  12.8 us
    scatter x1, local copies, waits for them, and re-layouts, body(): outgoing = jnp.zeros((experts * capacity, model_width), jnp.bfloat16).at[...  11.5 us
  transfers between devices with their start and end apart: 1, of which 1 were waited for; matrix products, arithmetic and copies ran while one was open for 0% of the time, Pallas kernels for 0%

commit v1 on v0

v1 whole, which is shorter than its diff:
```python
import math

import jax
import jax.numpy as jnp
from jax import lax
from jax.experimental import pallas as pl
from jax.experimental.pallas import tpu as pltpu
from jax.sharding import PartitionSpec as P

NEG_FILL = -1e30
EPSILON = 1e-06
AXES = ("blk", "kv")


def attend(queries, cache_keys, cache_values, lengths, sinks):
    my_block = lax.axis_index("blk")
    per_block = queries.shape[0]
    head_count = sinks.shape[0]
    head_dim = cache_keys.shape[3]
    window = cache_keys.shape[1]
    grouped_q = queries.reshape(per_block, head_count, head_dim)
    key_rows = cache_keys[:, :, 0, :]
    value_rows = cache_values[:, :, 0, :]
    my_lengths = lax.dynamic_slice_in_dim(lengths, my_block * per_block, per_block)
    scores = jnp.einsum("rgd,rjd->rgj", grouped_q, key_rows, preferred_element_type=jnp.float32) * (
        1.0 / math.sqrt(head_dim)
    )
    first_valid = window - jnp.minimum(my_lengths, window)
    is_valid = (jnp.arange(window, dtype=jnp.int32)[None, :] >= first_valid[:, None])[:, None, :]
    masked = jnp.where(is_valid, scores, NEG_FILL)
    top_limit = jnp.maximum(jnp.max(masked, axis=2), sinks[None, :])
    weights = jnp.where(is_valid, jnp.exp(masked - top_limit[..., None]), 0.0)
    denominator = jnp.sum(weights, axis=2) + jnp.exp(sinks[None, :] - top_limit)
    numerator = jnp.einsum(
        "rgj,rjd->rgd", weights.astype(jnp.bfloat16), value_rows, preferred_element_type=jnp.float32
    )
    return (
        (numerator / denominator[..., None])
        .astype(jnp.bfloat16)
        .reshape(per_block, head_count * head_dim)
    )


def prepare_kernel(hidden_ref, gain_ref, router_ref, routes_ref, out_ref):
    width = hidden_ref.shape[1]
    experts = router_ref.shape[1]
    hidden = hidden_ref[...].astype(jnp.float32)
    mean_sq = jnp.mean(hidden * hidden, axis=1, keepdims=True)
    normed = (hidden * lax.rsqrt(mean_sq + EPSILON) * gain_ref[...]).astype(jnp.bfloat16)
    out_ref[:, :width] = normed
    logits = jnp.dot(normed, router_ref[...], preferred_element_type=jnp.float32)
    lane = lax.broadcasted_iota(jnp.int32, logits.shape, 1)
    routes = routes_ref[...]
    chosen = jnp.zeros(logits.shape, jnp.bool_)
    for k in range(routes.shape[1]):
        chosen = chosen | (lane == routes[:, k : k + 1])
    top = jnp.max(jnp.where(chosen, logits, NEG_FILL), axis=1, keepdims=True)
    raised = jnp.where(chosen, jnp.exp(jnp.minimum(logits - top, 0.0)), 0.0)
    gates = raised / jnp.sum(raised, axis=1, keepdims=True)
    high = gates.astype(jnp.bfloat16).astype(jnp.float32)
    low = gates - high
    rest = out_ref.shape[1] - width - 2 * experts
    parts = [high, low]
    if rest:
        parts.append(jnp.zeros((high.shape[0], rest), jnp.float32))
    out_ref[:, width:] = jnp.concatenate(parts, axis=1).astype(jnp.bfloat16)


def prepare(hidden, norm_gain, router, routes):
    rows, width = hidden.shape
    extra = -(-2 * router.shape[1] // 128) * 128
    return pl.pallas_call(
        prepare_kernel,
        out_shape=jax.ShapeDtypeStruct((rows, width + extra), jnp.bfloat16),
        compiler_params=pltpu.CompilerParams(vmem_limit_bytes=32 << 20),
        name="prepare",
    )(hidden, norm_gain.reshape(1, width), router, routes)


def expert_kernel(expert_ref, rows_ref, gate_ref, up_ref, down_ref, out_ref):
    width = gate_ref.shape[0]
    payload = rows_ref[...]
    rows = payload[:, :width]
    tail = payload[:, width:].astype(jnp.float32)
    lane = lax.broadcasted_iota(jnp.int32, tail.shape, 1)
    expert = expert_ref[0]
    experts = expert_ref[1]
    mine = (lane == expert) | (lane == expert + experts)
    weight = jnp.sum(jnp.where(mine, tail, 0.0), axis=1, keepdims=True)
    gate_act = jnp.dot(rows, gate_ref[...], preferred_element_type=jnp.float32)
    up_act = jnp.dot(rows, up_ref[...], preferred_element_type=jnp.float32)
    inner = (gate_act / (1.0 + jnp.exp(-gate_act)) * up_act).astype(jnp.bfloat16)
    result = jnp.dot(inner, down_ref[...], preferred_element_type=jnp.float32)
    out_ref[...] = (weight * result).astype(jnp.bfloat16)


def run_expert(expert, rows, gate_weights, up_weights, down_weights):
    total, padded = rows.shape
    width, hidden_units = gate_weights.shape
    tile = 256
    return pl.pallas_call(
        expert_kernel,
        grid_spec=pltpu.PrefetchScalarGridSpec(
            num_scalar_prefetch=1,
            grid=(total // tile,),
            in_specs=[
                pl.BlockSpec((tile, padded), lambda i, e: (i, 0)),
                pl.BlockSpec((width, hidden_units), lambda i, e: (0, 0), pipeline_mode=pl.Buffered(1)),
                pl.BlockSpec((width, hidden_units), lambda i, e: (0, 0), pipeline_mode=pl.Buffered(1)),
                pl.BlockSpec((hidden_units, width), lambda i, e: (0, 0), pipeline_mode=pl.Buffered(1)),
            ],
            out_specs=pl.BlockSpec((tile, width), lambda i, e: (i, 0)),
        ),
        out_shape=jax.ShapeDtypeStruct((total, width), jnp.bfloat16),
        compiler_params=pltpu.CompilerParams(vmem_limit_bytes=48 << 20),
        name="expert",
    )(expert, rows, gate_weights, up_weights, down_weights)


def chunk_cuts(tokens, devices):
    step = (tokens // 2 + 15) // 16 * 16 if devices <= 32 else 32
    return [(start, min(start + step, tokens)) for start in range(0, tokens, step)]


def body(
    queries,
    cache_keys,
    cache_values,
    lengths,
    sinks,
    out_proj,
    decode_resid,
    prefill_hidden,
    norm_gain,
    router,
    routes,
    expert_gate,
    expert_up,
    expert_down,
):
    experts = router.shape[1]
    ids = routes[0]
    tokens = ids.shape[0]
    prefill = prefill_hidden[0]
    devices = lax.axis_size(AXES)
    cuts = chunk_cuts(tokens, devices)
    my_expert = lax.axis_index("kv") * lax.axis_size("blk") + lax.axis_index("blk")
    expert = jnp.stack([my_expert, jnp.int32(experts)]).astype(jnp.int32)
    weights = (expert_gate[0], expert_up[0], expert_down[0])

    attended = attend(queries, cache_keys, cache_values, lengths, sinks)
    partial_proj = jnp.dot(attended, out_proj, preferred_element_type=jnp.float32)
    projected = lax.psum_scatter(partial_proj, "kv", scatter_dimension=0, tiled=True)
    decoded = (decode_resid.astype(jnp.float32) + projected).astype(jnp.bfloat16)
    hidden = jnp.concatenate([prefill, decoded], axis=0)
    ids = jnp.concatenate([ids[1:], ids[:1]], axis=0)
    gathered = []
    for start, stop in cuts:
        source = prefill[start:stop] if stop < tokens else hidden[start:stop]
        sent = prepare(source, norm_gain, router, ids[start:stop])
        gathered.append(lax.all_gather(sent, AXES, axis=0, tiled=True))
    returned = []
    for rows in gathered:
        sums = run_expert(expert, rows, *weights)
        returned.append(lax.psum_scatter(sums, AXES, scatter_dimension=0, tiled=True))
    combined = jnp.concatenate(returned, axis=0)
    layer_sum = (hidden.astype(jnp.float32) + combined.astype(jnp.float32)).astype(jnp.bfloat16)
    layer_sum = jnp.concatenate([layer_sum[-1:], layer_sum[:-1]], axis=0)
    return layer_sum[None]


def solution(mesh):
    return jax.shard_map(
        body,
        mesh=mesh,
        in_specs=(
            P("blk", "kv"),
            P("blk", None, "kv", None),
            P("blk", None, "kv", None),
            P(),
            P("kv"),
            P("kv", None),
            P(("blk", "kv"), None),
            P(("blk", "kv"), None, None),
            P(),
            P(),
            P(("blk", "kv"), None, None),
            P(("kv", "blk"), None, None),
            P(("kv", "blk"), None, None),
            P(("kv", "blk"), None, None),
        ),
        out_specs=P(("blk", "kv"), None, None),
        check_vma=False,
    )
```

time: 427 us -> 503 us (1.18)
  waiting for transfers between devices: 161 us -> 405 us
  blocking collectives: 184 us -> 17.9 us
  Pallas kernels: 0 us -> 48.9 us
  matrix products: 33 us -> 5.16 us
  local copies, waits for them, and re-layouts: 29.6 us -> 6.53 us
  between operations: 0.2 us -> 13.3 us
  other arithmetic: 14.8 us -> 5.03 us
    reduce_scatter x0 -> x2, waiting for transfers between devices: none -> 278 us  [body(): lax.psum_scatter(sums, AXES, scatter_dimension=0, tiled=True)]
    all_to_all x1 -> x0, blocking collectives: 166 us -> none  [body(): lax.all_to_all(outgoing, ('kv', 'blk'), split_axis=0, concat_axis=0, tile...]
    all_to_all x1 -> x0, waiting for transfers between devices: 161 us -> none  [body(): lax.all_to_all(processed, ('kv', 'blk'), split_axis=0, concat_axis=0, til...]
    all_gather x0 -> x2, waiting for transfers between devices: none -> 127 us  [body(): gathered.append(lax.all_gather(sent, AXES, axis=0, tiled=True))]
    pallas_call x0 -> x4, Pallas kernels: none -> 48.9 us  [the longest x2 46.4 us: run_expert(): pl.pallas_call(expert_kernel, grid_spec=pltpu.PrefetchScalarGridSpec(num_...]
    dot_general x5 -> x2, matrix products: 32.4 us -> 4.51 us  [the longest x1 3.77 us: attend(): jnp.einsum('rgd,rjd->rgj', grouped_q, key_rows, preferred_element_type=jn...]
    gather x1 -> x0, local copies, waits for them, and re-layouts: 12.8 us -> none  [body(): results = returned.reshape(experts * capacity, model_width)[slot_index]]
    scatter x1 -> x0, local copies, waits for them, and re-layouts: 11.5 us -> none  [body(): outgoing = jnp.zeros((experts * capacity, model_width), jnp.bfloat16).at[...]
  transfers between devices with their start and end apart: 1 -> 4, of which waited for: 1 -> 4; matrix products, arithmetic and copies ran while one was open for 0% -> 0% of each run, Pallas kernels for 0% -> 9%
where the time goes in v1:
time: 503 us; the launch traced here: 502 us
  waiting for transfers between devices  405 us (81%)
  Pallas kernels  48.9 us (10%)
  blocking collectives  17.9 us (4%)
  between operations  13.3 us (3%)
  local copies, waits for them, and re-layouts  6.53 us (1%)
  matrix products  5.16 us (1%)
  other arithmetic  5.03 us (1%)
    reduce_scatter x2, waiting for transfers between devices, body(): lax.psum_scatter(sums, AXES, scatter_dimension=0, tiled=True)  278 us
    all_gather x2, waiting for transfers between devices, body(): gathered.append(lax.all_gather(sent, AXES, axis=0, tiled=True))  127 us
    pallas_call x2, Pallas kernels, run_expert(): pl.pallas_call(expert_kernel, grid_spec=pltpu.PrefetchScalarGridSpec(num_...  46.4 us
    unnamed x1, blocking collectives  17.9 us
  transfers between devices with their start and end apart: 4, of which 4 were waited for; matrix products, arithmetic and copies ran while one was open for 0% of the time, Pallas kernels for 9%

profile of v1, /device:TPU:0, one launch (start us, length us, event | category | flops | bytes accessed | tf_op | source)
XLA Modules:
  0.0 502.2 jit_solution(6902174679264605542)
XLA Ops:
  6.5 0.0 copy-start.10
  6.5 0.0 all-gather.5.cloned.1.call-start
  6.5 0.8 slice.42
  7.3 0.8 slice_reduce_fusion
  8.1 0.0 copy-start.4
  8.1 0.9 minimum_subtract_fusion
  9.0 0.1 iota_compare_fusion
  9.1 0.0 copy-start.5
  9.1 3.8 fusion.27
  12.9 0.0 copy-done.10
  12.9 0.3 fusion.13
  13.2 0.0 copy-done.4
  13.2 0.0 copy-start.7
  13.2 0.0 copy-start.11
  13.2 0.0 copy-start.9
  13.2 0.0 copy-start.3
  13.2 0.7 fusion.10
  14.0 0.0 copy-done.5
  14.0 0.0 copy-start.8
  14.0 0.0 copy-start
  14.0 0.7 fusion.20
  14.6 17.9 %all-reduce = f32[4,2048]{1,0:T(4,128)S(1)} all-reduce(f32[4,2048]{1,0:T(4,128)S(1)} %fusion.20), channel_id=2, replica_groups=mesh['kv'=4,'blk'=8] {'kv'}, use_global_device_ids=true, to_apply=%region_2.3.clone | all-reduce | flops 8192 | bytes 65536
  32.5 0.0 copy-done.7
  32.5 1.0 copy.25.router_ref
  33.5 0.1 copy.29
  33.6 0.0 copy-done.11
  33.6 0.6 dynamic-slice
  34.2 0.0 copy-done.9
  34.2 0.7 fusion.25
  34.9 1.0 fusion.19.hidden_ref
  35.9 0.0 copy-done.3
  35.9 0.0 copy-start.1
  35.9 1.0 copy-done.1
  36.9 1.3 prepare.3
  38.2 0.0 all-gather.5.cloned.1.call-update
  38.2 0.0 all-gather.3.cloned.1.call-start
  38.3 0.0 copy-done.8
  38.3 0.1 slice.39
  38.3 0.1 copy.28
  38.4 1.0 slice_bitcast_fusion.hidden_ref
  39.4 0.0 copy-start.2
  39.4 1.0 copy-done.2
  40.5 1.3 prepare.2
  41.7 0.0 all-gather.3.cloned.1.call-update
  41.8 0.0 reduce-scatter.5.cloned.1.call-start
  41.8 0.1 pad_add_fusion.1.expert_ref
  41.9 67.0 %all-gather.5.cloned.1.call-done.rows_ref = bf16[1536,2176]{1,0:T(8,128)(2,1)} async-done(((bf16[48,2176]{1,0:T(8,128)(2,1)}), bf16[1536,2176]{1,0:T(8,128)(2,1)}) %all-gather.5.cloned.1.call-update) | async-done | bytes 6684688 | tf_op jit(solution)/shard_map/all_gather | solution.py:161
  108.9 0.0 copy-done
  108.9 20.6 %expert.3 = bf16[1536,2048]{1,0:T(8,128)(2,1)} custom-call(s32[2]{0:T(128)S(1)} %pad_add_fusion.1.expert_ref, bf16[1536,2176]{1,0:T(8,128)(2,1)} %all-gather.5.cloned.1.call-done.rows_ref, bf16[2048,768]{1,0:T(8,128)(2,1)S(1)} %bitcast.41, bf16[2048,768]{1,0:T(8,128)(2,1)} %bitcast.46, bf16[768,2048]{1,0:T(8,128)(2,1)} %bitcast.48), custom_call_target="tpu_custom_call" | custom-call | tf_op jit(solution)/shard_map/expert/pallas_call | solution.py:101
  129.5 0.0 reduce-scatter.5.cloned.1.call-update
  129.5 0.0 reduce-scatter.3.cloned.1.call-start
  129.5 60.4 %all-gather.3.cloned.1.call-done.rows_ref = bf16[2048,2176]{1,0:T(8,128)(2,1)} async-done(((bf16[64,2176]{1,0:T(8,128)(2,1)}), bf16[2048,2176]{1,0:T(8,128)(2,1)}) %all-gather.3.cloned.1.call-update) | async-done | bytes 8912912 | tf_op jit(solution)/shard_map/all_gather | solution.py:161
  189.9 25.8 %expert.2 = bf16[2048,2048]{1,0:T(8,128)(2,1)} custom-call(s32[2]{0:T(128)S(1)} %pad_add_fusion.1.expert_ref, bf16[2048,2176]{1,0:T(8,128)(2,1)} %all-gather.3.cloned.1.call-done.rows_ref, bf16[2048,768]{1,0:T(8,128)(2,1)S(1)} %bitcast.42, bf16[2048,768]{1,0:T(8,128)(2,1)} %bitcast.47, bf16[768,2048]{1,0:T(8,128)(2,1)} %bitcast.49), custom_call_target="tpu_custom_call" | custom-call | tf_op jit(solution)/shard_map/expert/pallas_call | solution.py:101
  215.7 0.0 copy-start.6
  215.7 0.0 reduce-scatter.3.cloned.1.call-update
  215.8 92.8 %reduce-scatter.5.cloned.1.call-done = bf16[48,2048]{1,0:T(8,128)(2,1)} async-done(((bf16[1536,2048]{1,0:T(8,128)(2,1)}), bf16[48,2048]{1,0:T(8,128)(2,1)}) %reduce-scatter.5.cloned.1.call-update) | async-done | bytes 196624 | tf_op jit(solution)/shard_map/reduce_scatter | solution.py:165
  308.5 185.0 %reduce-scatter.3.cloned.1.call-done = bf16[64,2048]{1,0:T(8,128)(2,1)} async-done(((bf16[2048,2048]{1,0:T(8,128)(2,1)}), bf16[64,2048]{1,0:T(8,128)(2,1)}) %reduce-scatter.3.cloned.1.call-update) | async-done | bytes 262160 | tf_op jit(solution)/shard_map/reduce_scatter | solution.py:165
  493.5 0.0 copy-done.6
  493.5 1.2 add_convert_fusion
  494.7 0.9 maximum_bitcast_fusion
  (4 shorter events, 0.0 us)
Async XLA Ops:
  6.5 6.3 %copy-start.10 = (f32[8]{0:T(128)S(1)}, f32[8]{0:T(128)}, u32[]{:S(2)}) copy-start(f32[8]{0:T(128)} %param.18) | copy-start | bytes 100
  6.5 102.4 %all-gather.5.cloned.1.call-start = ((), (), s32[]{:S(2)}) async-start(), calls=%async_computation.4 | async-start | bytes 6893568 | tf_op jit(solution)/shard_map/all_gather | solution.py:161
  8.1 5.1 %copy-start.4 = (bf16[4,4096,1,128]{3,1,2,0:T(8,128)(2,1)S(1)}, bf16[4,4096,1,128]{3,1,2,0:T(8,128)(2,1)}, u32[]{:S(2)}) copy-start(bf16[4,4096,1,128]{3,1,2,0:T(8,128)(2,1)} %param.16) | copy-start | bytes 12582916
  9.1 4.9 copy-start.5
  13.2 19.4 %copy-start.7 = (bf16[2048,32]{0,1:T(8,128)(2,1)S(1)}, bf16[2048,32]{0,1:T(8,128)(2,1)}, u32[]{:S(2)}) copy-start(bf16[2048,32]{0,1:T(8,128)(2,1)} %param.23) | copy-start | bytes 393220
  13.2 20.5 %copy-start.11 = (u32[32]{0:T(128)S(1)}, u32[32]{0:T(128)}, u32[]{:S(2)}) copy-start(u32[32]{0:T(128)} %constant.39) | copy-start | bytes 388
  13.2 21.0 %copy-start.9 = (bf16[1,2048]{1,0:T(2,128)(2,1)S(1)}, bf16[1,2048]{1,0:T(2,128)(2,1)}, u32[]{:S(2)}) copy-start(bf16[1,2048]{1,0:T(2,128)(2,1)} %param.20) | copy-start | bytes 12292
  13.2 22.7 %copy-start.3 = (f32[2048]{0:T(1024)S(1)}, f32[2048]{0:T(1024)}, u32[]{:S(2)}) copy-start(f32[2048]{0:T(1024)} %param.22) | copy-start | bytes 24580
  14.0 24.3 %copy-start.8 = (s32[1,112,8]{1,2,0:T(8,128)S(1)}, s32[1,112,8]{1,2,0:T(8,128)}, u32[]{:S(2)}) copy-start(s32[1,112,8]{1,2,0:T(8,128)} %param.24) | copy-start | bytes 10756
  14.0 94.9 %copy-start = (bf16[1,2048,768]{2,1,0:T(8,128)(2,1)S(1)}, bf16[1,2048,768]{2,1,0:T(8,128)(2,1)}, u32[]{:S(2)}) copy-start(bf16[1,2048,768]{2,1,0:T(8,128)(2,1)} %param.25) | copy-start | bytes 9437188
  35.9 1.0 copy-start.1
  38.2 151.7 %all-gather.3.cloned.1.call-start = ((), (), s32[]{:S(2)}) async-start(), calls=%async_computation.2 | async-start | bytes 9191424 | tf_op jit(solution)/shard_map/all_gather | solution.py:161
  39.4 1.0 copy-start.2
  41.8 266.8 %reduce-scatter.5.cloned.1.call-start = ((), (), s32[]{:S(2)}) async-start(), calls=%async_computation.5 | async-start | bytes 6488064 | tf_op jit(solution)/shard_map/reduce_scatter | solution.py:165
  129.5 364.0 %reduce-scatter.3.cloned.1.call-start = ((), (), s32[]{:S(2)}) async-start(), calls=%async_computation.3 | async-start | bytes 8650752 | tf_op jit(solution)/shard_map/reduce_scatter | solution.py:165
  215.7 277.8 %copy-start.6 = (bf16[1,111,2048]{2,1,0:T(8,128)(2,1)S(1)}, bf16[1,111,2048]{2,1,0:T(8,128)(2,1)}, u32[]{:S(2)}) copy-start(bf16[1,111,2048]{2,1,0:T(8,128)(2,1)} %param.21) | copy-start | bytes 1363972
Sparse Core Ops, SparseCore 0:
  38.3 70.5 all-gather.4
  111.8 78.0 all-gather.2
  195.6 112.9 reduce-scatter.4
  310.8 182.6 reduce-scatter.2

commit v2 on v1

--- a/solution.py
+++ b/solution.py
@@ -117,12 +117,240 @@
     )(expert, rows, gate_weights, up_weights, down_weights)
 
 
+def plane_kernel(
+    ids_ref,
+    own_ref,
+    x_ref,
+    y_ref,
+    d0_ref,
+    d1_ref,
+    gate0_ref,
+    up0_ref,
+    down0_ref,
+    gate1_ref,
+    up1_ref,
+    down1_ref,
+    own_out,
+    x_out,
+    y_out,
+    d0_out,
+    d1_out,
+    rows,
+    gates,
+    ups,
+    downs,
+    inner,
+    sums,
+    row_sem,
+    weight_sem,
+    out_sem,
+):
+    width = sums.shape[1]
+    units = gates.shape[2]
+    tile = 256
+    out_tile = 512
+    sources = (own_ref, x_ref, y_ref, d0_ref, d1_ref)
+    targets = (own_out, x_out, y_out, d0_out, d1_out)
+    starts = []
+    at = 0
+    for ref in sources:
+        starts.append(at)
+        at += ref.shape[0]
+    row_copies = [
+        pltpu.make_async_copy(ref, rows.at[pl.ds(start, ref.shape[0])], row_sem.at[i])
+        for i, (ref, start) in enumerate(zip(sources, starts))
+    ]
+    weight_copies = []
+    for e, (gate, up) in enumerate(((gate0_ref, up0_ref), (gate1_ref, up1_ref))):
+        for j in range(units // tile):
+            part = pl.ds(j * tile, tile)
+            for source, target in ((gate, gates), (up, ups)):
+                weight_copies.append(
+                    pltpu.make_async_copy(
+                        source.at[:, part], target.at[e, :, part], weight_sem.at[len(weight_copies)]
+                    )
+                )
+    first_down = len(weight_copies)
+    for j in range(width // out_tile):
+        part = pl.ds(j * out_tile, out_tile)
+        for e, down in enumerate((down0_ref, down1_ref)):
+            weight_copies.append(
+                pltpu.make_async_copy(
+                    down.at[:, part], downs.at[e, :, part], weight_sem.at[len(weight_copies)]
+                )
+            )
+    for copy in row_copies + weight_copies:
+        copy.start()
+    for copy in row_copies:
+        copy.wait()
+    tail = rows[:, width:].astype(jnp.float32)
+    lane = lax.broadcasted_iota(jnp.int32, tail.shape, 1)
+    experts = ids_ref[2]
+    at = 0
+    for e in range(2):
+        mine = (lane == ids_ref[e]) | (lane == ids_ref[e] + experts)
+        weight = jnp.sum(jnp.where(mine, tail, 0.0), axis=1, keepdims=True)
+        for j in range(units // tile):
+            weight_copies[at].wait()
+            weight_copies[at + 1].wait()
+            at += 2
+            part = pl.ds(j * tile, tile)
+            gate_act = jnp.dot(
+                rows[:, :width], gates[e, :, part], preferred_element_type=jnp.float32
+            )
+            up_act = jnp.dot(rows[:, :width], ups[e, :, part], preferred_element_type=jnp.float32)
+            act = gate_act / (1.0 + jnp.exp(-gate_act)) * up_act * weight
+            inner[:, pl.ds(e * units + j * tile, tile)] = act.astype(jnp.bfloat16)
+    out_copies = []
+    for j in range(width // out_tile):
+        weight_copies[first_down + 2 * j].wait()
+        weight_copies[first_down + 2 * j + 1].wait()
+        part = pl.ds(j * out_tile, out_tile)
+        result = jnp.dot(inner[:, :units], downs[0, :, part], preferred_element_type=jnp.float32)
+        result += jnp.dot(inner[:, units:], downs[1, :, part], preferred_element_type=jnp.float32)
+        sums[:, part] = result.astype(jnp.bfloat16)
+        for ref, start in zip(targets, starts):
+            copy = pltpu.make_async_copy(
+                sums.at[pl.ds(start, ref.shape[0]), part],
+                ref.at[:, part],
+                out_sem.at[len(out_copies)],
+            )
+            copy.start()
+            out_copies.append(copy)
+    for copy in out_copies:
+        copy.wait()
+
+
+def run_plane(ids, blocks, own_weights, other_weights):
+    width, units = own_weights[0].shape
+    padded = blocks[0].shape[1]
+    total = sum(block.shape[0] for block in blocks)
+    kept = jnp.bfloat16
+    return pl.pallas_call(
+        plane_kernel,
+        in_specs=[pl.BlockSpec(memory_space=pltpu.SMEM)] + [pl.BlockSpec(memory_space=pl.ANY)] * 11,
+        out_specs=[pl.BlockSpec(memory_space=pl.ANY)] * 5,
+        out_shape=[jax.ShapeDtypeStruct((block.shape[0], width), kept) for block in blocks],
+        scratch_shapes=[
+            pltpu.VMEM((total, padded), kept),
+            pltpu.VMEM((2, width, units), kept),
+            pltpu.VMEM((2, width, units), kept),
+            pltpu.VMEM((2, units, width), kept),
+            pltpu.VMEM((total, 2 * units), kept),
+            pltpu.VMEM((total, width), kept),
+            pltpu.SemaphoreType.DMA((5,)),
+            pltpu.SemaphoreType.DMA((4 * (units // 256) + 2 * (width // 512),)),
+            pltpu.SemaphoreType.DMA((5 * (width // 512),)),
+        ],
+        compiler_params=pltpu.CompilerParams(vmem_limit_bytes=48 << 20),
+        name="plane",
+    )(ids, *blocks, *own_weights, *other_weights)
+
+
+def along_x(value):
+    return lax.ppermute(value, "kv", [(i, i ^ 1) for i in range(4)])
+
+
+def along_y(value):
+    return lax.ppermute(value, "kv", [(i, i ^ 2) for i in range(4)])
+
+
+def along_diagonal(value):
+    return lax.ppermute(value, "kv", [(i, i ^ 3) for i in range(4)])
+
+
+def around_z(value):
+    return lax.ppermute(value, "blk", [(i, (i + 2) % 8) for i in range(8)])
+
+
+def across_chip(value):
+    return lax.ppermute(value, "blk", [(i, i ^ 1) for i in range(8)])
+
+
+def added(*parts):
+    total = parts[0].astype(jnp.float32)
+    for part in parts[1:]:
+        total = total + part.astype(jnp.float32)
+    return total
+
+
+def permuted_plan(
+    queries,
+    cache_keys,
+    cache_values,
+    lengths,
+    sinks,
+    out_proj,
+    decode_resid,
+    prefill_hidden,
+    norm_gain,
+    router,
+    routes,
+    expert_gate,
+    expert_up,
+    expert_down,
+):
+    experts = router.shape[1]
+    ids = routes[0]
+    tokens = ids.shape[0]
+    own_weights = (expert_gate[0], expert_up[0], expert_down[0])
+    other_weights = tuple(across_chip(w) for w in own_weights)
+    my_kv = lax.axis_index("kv")
+    my_blk = lax.axis_index("blk")
+    first_expert = my_kv * 8
+    expert_ids = jnp.stack(
+        [first_expert + my_blk, first_expert + (my_blk ^ 1), jnp.int32(experts)]
+    ).astype(jnp.int32)
+
+    attended = attend(queries, cache_keys, cache_values, lengths, sinks)
+    partial_proj = jnp.dot(attended, out_proj, preferred_element_type=jnp.float32)
+
+    def row_of(index):
+        return lax.dynamic_slice_in_dim(partial_proj, index, 1)
+
+    projected = (
+        row_of(my_kv)
+        + along_x(row_of(my_kv ^ 1))
+        + along_y(row_of(my_kv ^ 2))
+        + along_diagonal(row_of(my_kv ^ 3))
+    )
+    decoded = (decode_resid.astype(jnp.float32) + projected).astype(jnp.bfloat16)
+    hidden = jnp.concatenate([decoded, prefill_hidden[0]], axis=0)
+    block = prepare(hidden, norm_gain, router, ids)
+    layer_sum = hidden.astype(jnp.float32)
+    carried = None
+    long = (tokens // 2 + 15) // 16 * 16
+    for step in range(4):
+        cut = long if step % 2 == 0 else tokens - long
+        from_x = along_x(block)
+        from_y = along_y(block)
+        diagonal_0 = along_y(from_x[:cut])
+        diagonal_1 = along_x(from_y[cut:])
+        following = around_z(block) if step < 3 else None
+        own, to_x, to_y, far_0, far_1 = run_plane(
+            expert_ids, (block, from_x, from_y, diagonal_0, diagonal_1), own_weights, other_weights
+        )
+        passed_0 = along_y(far_0)
+        passed_1 = along_x(far_1)
+        to_x = jnp.concatenate([added(to_x[:cut], passed_0), to_x[cut:].astype(jnp.float32)], axis=0)
+        to_y = jnp.concatenate([to_y[:cut].astype(jnp.float32), added(to_y[cut:], passed_1)], axis=0)
+        back_x = along_x(to_x.astype(jnp.bfloat16))
+        back_y = along_y(to_y.astype(jnp.bfloat16))
+        if step == 0:
+            layer_sum = added(layer_sum, own, back_x, back_y)
+        else:
+            parts = (own, back_x, back_y) + ((carried,) if step > 1 else ())
+            carried = around_z(added(*parts).astype(jnp.bfloat16))
+        block = following
+    return added(layer_sum, carried).astype(jnp.bfloat16)[None]
+
+
 def chunk_cuts(tokens, devices):
-    step = (tokens // 2 + 15) // 16 * 16 if devices <= 32 else 32
+    step = (tokens // 2 + 15) // 16 * 16 if devices < 128 else 32
     return [(start, min(start + step, tokens)) for start in range(0, tokens, step)]
 
 
-def body(
+def gathered_plan(
     queries,
     cache_keys,
     cache_values,
@@ -170,8 +398,9 @@
 
 
 def solution(mesh):
+    plan = permuted_plan if (mesh.shape["kv"], mesh.shape["blk"]) == (4, 8) else gathered_plan
     return jax.shard_map(
-        body,
+        plan,
         mesh=mesh,
         in_specs=(
             P("blk", "kv"),

time: 503 us -> 248 us (0.49)
  waiting for transfers between devices: 405 us -> 120 us
  starting transfers between devices: 0.13 us -> 44.3 us
  blocking collectives: 17.9 us -> 0 us
  Pallas kernels: 48.9 us -> 63.6 us
  between operations: 13.3 us -> 0.57 us
    reduce_scatter x2 -> x0, waiting for transfers between devices: 278 us -> none  [body(): lax.psum_scatter(sums, AXES, scatter_dimension=0, tiled=True)]
    all_gather x2 -> x0, waiting for transfers between devices: 127 us -> none  [body(): gathered.append(lax.all_gather(sent, AXES, axis=0, tiled=True))]
    ppermute x0 -> x44, waiting for transfers between devices: none -> 120 us  [the longest x6 45.1 us: around_z(): return lax.ppermute(value, 'blk', [(i, (i + 2) % 8) for i in range(8)])]
    ppermute x0 -> x44, starting transfers between devices: none -> 44.3 us  [the longest x17 20.1 us: along_y(): return lax.ppermute(value, 'kv', [(i, i ^ 2) for i in range(4)])]
    unnamed x1 -> x0, blocking collectives: 17.9 us -> none
    pallas_call x2 -> x4, Pallas kernels: 46.4 us -> 62.9 us  [run_plane(): pl.pallas_call(plane_kernel, in_specs=[pl.BlockSpec(memory_space=pltpu.SM...]
  transfers between devices with their start and end apart: 4 -> 44, of which waited for: 4 -> 21; matrix products, arithmetic and copies ran while one was open for 0% -> 2% of each run, Pallas kernels for 9% -> 26%
where the time goes in v2:
time: 248 us
  waiting for transfers between devices  120 us (48%)
  Pallas kernels  63.6 us (26%)
  starting transfers between devices  44.3 us (18%)
  local copies, waits for them, and re-layouts  9.74 us (4%)
  matrix products  5.18 us (2%)
  other arithmetic  4.12 us (2%)
    pallas_call x4, Pallas kernels, run_plane(): pl.pallas_call(plane_kernel, in_specs=[pl.BlockSpec(memory_space=pltpu.SM...  62.9 us
    ppermute x6, waiting for transfers between devices, around_z(): return lax.ppermute(value, 'blk', [(i, (i + 2) % 8) for i in range(8)])  45.1 us
    ppermute x17, waiting for transfers between devices, along_y(): return lax.ppermute(value, 'kv', [(i, i ^ 2) for i in range(4)])  39.5 us
    ppermute x17, waiting for transfers between devices, along_x(): return lax.ppermute(value, 'kv', [(i, i ^ 1) for i in range(4)])  35.5 us
    ppermute x17, starting transfers between devices, along_y(): return lax.ppermute(value, 'kv', [(i, i ^ 2) for i in range(4)])  20.1 us
    ppermute x17, starting transfers between devices, along_x(): return lax.ppermute(value, 'kv', [(i, i ^ 1) for i in range(4)])  17.9 us
    unnamed x44, local copies, waits for them, and re-layouts  7.1 us
  transfers between devices with their start and end apart: 44, of which 21 were waited for; matrix products, arithmetic and copies ran while one was open for 2% of the time, Pallas kernels for 26%

profile of v2, /device:TPU:0, one launch (start us, length us, event | category | flops | bytes accessed | tf_op | source)
XLA Modules:
  0.0 247.7 jit_solution(5367477011101087836)
XLA Ops:
  0.0 0.9 minimum_subtract_fusion
  1.0 3.8 %fusion.26 = (f32[4,8]{1,0:T(4,128)S(1)}, f32[4,8,4096]{2,1,0:T(8,128)S(1)}) fusion(bf16[4,4096,1,128]{3,1,2,0:T(8,128)(2,1)} %param.15, bf16[1,4,8,128]{3,1,2,0:T(4,128)(2,1)} %bitcast.55, pred[4,4096]{1,0:T(4,128)(4,1)S(1)} %iota_compare_fusion), kind=kOutput, calls=%fused_computation.51 | convolution fusion | flops 33947616 | bytes 4743296 | tf_op jit(solution)/shard_map/rgd,rjd->rgj/dot_general | solution.py:25
  5.1 0.7 fusion.10
  5.9 0.7 fusion.20
  6.6 4.0 %collective-permute-start.2 = (f32[1,2048]{1,0:T(1,128)S(1)}, f32[1,2048]{1,0:T(1,128)S(1)}, u32[]{:S(2)}, u32[]{:S(2)}) collective-permute-start(f32[1,2048]{1,0:T(1,128)S(1)} %get-tuple-element.46), channel_id=1, source_target_pairs={{0,24},{8,16},{16,8},{24,0},{1,25},{9,17},{17,9},{25,1},{2,26},{10... | collective-permute-start | bytes 24584 | tf_op jit(solution)/shard_map/ppermute | solution.py:259
  12.2 2.0 collective-permute-done.1
  14.9 0.7 prepare.1.own_ref
  15.6 1.6 collective-permute-start.14
  17.7 11.3 %collective-permute-done.14.own_ref = bf16[112,2176]{1,0:T(8,128)(2,1)S(1)} collective-permute-done((bf16[112,2176]{1,0:T(8,128)(2,1)S(1)}, bf16[112,2176]{1,0:T(8,128)(2,1)S(1)}, u32[]{:S(2)}, u32[]{:S(2)}) %collective-permute-start.14) | collective-permute-done | bytes 487456 | tf_op jit(solution)/shard_map/ppermute | solution.py:263
  29.0 1.5 collective-permute-start.4
  30.5 1.5 collective-permute-start.33
  32.0 8.3 %collective-permute-done.4.y_ref = bf16[112,2176]{1,0:T(8,128)(2,1)S(1)} collective-permute-done((bf16[112,2176]{1,0:T(8,128)(2,1)S(1)}, bf16[112,2176]{1,0:T(8,128)(2,1)S(1)}, u32[]{:S(2)}, u32[]{:S(2)}) %collective-permute-start.4) | collective-permute-done | bytes 487456 | tf_op jit(solution)/shard_map/ppermute | solution.py:255
  40.3 1.5 collective-permute-start.34
  41.8 0.8 copy-done.2
  42.6 9.0 %collective-permute-done.34.y_ref = bf16[112,2176]{1,0:T(8,128)(2,1)S(1)} collective-permute-done((bf16[112,2176]{1,0:T(8,128)(2,1)S(1)}, bf16[112,2176]{1,0:T(8,128)(2,1)S(1)}, u32[]{:S(2)}, u32[]{:S(2)}) %collective-permute-start.34) | collective-permute-done | bytes 487456 | tf_op jit(solution)/shard_map/ppermute | solution.py:255
  51.6 1.5 collective-permute-start.35
  53.6 2.3 collective-permute-start.25
  55.9 1.6 collective-permute-done.35.d0_ref
  57.4 0.7 copy-done.10
  58.1 2.0 collective-permute-start.36
  60.1 9.4 %collective-permute-done.36.d1_ref = bf16[64,2176]{1,0:T(8,128)(2,1)S(1)} collective-permute-done((bf16[64,2176]{1,0:T(8,128)(2,1)S(1)}, bf16[64,2176]{1,0:T(8,128)(2,1)S(1)}, u32[]{:S(2)}, u32[]{:S(2)}) %collective-permute-start.36) | collective-permute-done | bytes 278560 | tf_op jit(solution)/shard_map/ppermute | solution.py:251
  69.5 0.7 copy-done.8
  70.3 1.2 collective-permute-start.26
  71.5 9.4 %collective-permute-done.16.own_ref = bf16[112,2176]{1,0:T(8,128)(2,1)S(1)} collective-permute-done((bf16[112,2176]{1,0:T(8,128)(2,1)S(1)}, bf16[112,2176]{1,0:T(8,128)(2,1)S(1)}, u32[]{:S(2)}, u32[]{:S(2)}) %collective-permute-start.16) | collective-permute-done | bytes 487456 | tf_op jit(solution)/shard_map/ppermute | solution.py:263
  80.9 1.7 collective-permute-start.17
  82.6 1.3 collective-permute-start.18
  83.9 0.8 copy-done.6
  84.6 0.7 slice.101
  85.3 0.8 copy-done
  86.1 5.9 %collective-permute-done.17.x_ref = bf16[112,2176]{1,0:T(8,128)(2,1)} collective-permute-done((bf16[112,2176]{1,0:T(8,128)(2,1)S(1)}, bf16[112,2176]{1,0:T(8,128)(2,1)}, u32[]{:S(2)}, u32[]{:S(2)}) %collective-permute-start.17) | collective-permute-done | bytes 487456 | tf_op jit(solution)/shard_map/ppermute | solution.py:251
  92.0 1.7 collective-permute-start.28
  93.7 0.7 slice.100
  94.7 1.0 collective-permute-start.27
  95.8 0.9 slice.98
  96.8 3.6 %collective-permute-done.28.d1_ref = bf16[48,2176]{1,0:T(8,128)(2,1)} collective-permute-done((bf16[48,2176]{1,0:T(8,128)(2,1)}, bf16[48,2176]{1,0:T(8,128)(2,1)}, u32[]{:S(2)}, u32[]{:S(2)}) %collective-permute-start.28) | collective-permute-done | bytes 208928 | tf_op jit(solution)/shard_map/ppermute | solution.py:251
  100.3 1.6 collective-permute-start.5
  101.9 1.5 collective-permute-start.6
  103.4 0.7 collective-permute-start.19
  104.5 1.0 copy-done.3
  105.5 1.0 copy-done.9
  106.5 0.9 copy-done.11
  107.4 14.6 %plane.7 = (bf16[112,2048]{1,0:T(8,128)(2,1)S(1)}, bf16[112,2048]{1,0:T(8,128)(2,1)S(1)}, bf16[112,2048]{1,0:T(8,128)(2,1)S(1)}, bf16[48,2048]{1,0:T(8,128)(2,1)S(1)}, bf16[64,2048]{1,0:T(8,128)(2,1)S(1)}) custom-call(s32[3]{0:T(128)S(1)} %pad_add_fusion.ids_ref, bf16[112,2176]{1,0:T(8,128)(2,1)S(1)} %copy-done.3, ...), custom_call_target="tpu_custom_call" | custom-call | tf_op jit(solution)/shard_map/plane/pallas_call | solution.py:229
  122.0 1.7 collective-permute-start.37
  123.8 19.4 %plane.6 = (bf16[112,2048]{1,0:T(8,128)(2,1)S(1)}, bf16[112,2048]{1,0:T(8,128)(2,1)S(1)}, bf16[112,2048]{1,0:T(8,128)(2,1)S(1)}, bf16[64,2048]{1,0:T(8,128)(2,1)S(1)}, bf16[48,2048]{1,0:T(8,128)(2,1)S(1)}) custom-call(s32[3]{0:T(128)S(1)} %pad_add_fusion.ids_ref, bf16[112,2176]{1,0:T(8,128)(2,1)S(1)} %copy-done.5, ...), custom_call_target="tpu_custom_call" | custom-call | tf_op jit(solution)/shard_map/plane/pallas_call | solution.py:229
  143.3 1.5 collective-permute-start.39
  145.4 14.2 %plane.5 = (bf16[112,2048]{1,0:T(8,128)(2,1)S(1)}, bf16[112,2048]{1,0:T(8,128)(2,1)S(1)}, bf16[112,2048]{1,0:T(8,128)(2,1)S(1)}, bf16[48,2048]{1,0:T(8,128)(2,1)S(1)}, bf16[64,2048]{1,0:T(8,128)(2,1)S(1)}) custom-call(s32[3]{0:T(128)S(1)} %pad_add_fusion.ids_ref, bf16[112,2176]{1,0:T(8,128)(2,1)S(1)} %copy-done.7, ...), custom_call_target="tpu_custom_call" | custom-call | tf_op jit(solution)/shard_map/plane/pallas_call | solution.py:229
  160.1 1.8 collective-permute-start.23
  161.9 14.7 %plane.4 = (bf16[112,2048]{1,0:T(8,128)(2,1)S(1)}, bf16[112,2048]{1,0:T(8,128)(2,1)S(1)}, bf16[112,2048]{1,0:T(8,128)(2,1)S(1)}, bf16[64,2048]{1,0:T(8,128)(2,1)S(1)}, bf16[48,2048]{1,0:T(8,128)(2,1)S(1)}) custom-call(s32[3]{0:T(128)S(1)} %pad_add_fusion.ids_ref, bf16[112,2176]{1,0:T(8,128)(2,1)S(1)} %prepare.1.own_ref, ...), custom_call_target="tpu_custom_call" | custom-call | tf_op jit(solution)/shard_map/plane/pallas_call | solution.py:229
  176.6 1.3 collective-permute-start.21
  178.0 0.6 collective-permute-start.12
  178.8 5.8 %collective-permute-done.21 = bf16[48,2048]{1,0:T(8,128)(2,1)S(1)} collective-permute-done((bf16[48,2048]{1,0:T(8,128)(2,1)S(1)}, bf16[48,2048]{1,0:T(8,128)(2,1)S(1)}, u32[]{:S(2)}, u32[]{:S(2)}) %collective-permute-start.21) | collective-permute-done | bytes 196640 | tf_op jit(solution)/shard_map/ppermute | solution.py:255
  184.5 1.3 collective-permute-start.10
  187.3 1.7 collective-permute-start.40
  189.1 9.4 %collective-permute-done.38 = bf16[112,2048]{1,0:T(8,128)(2,1)S(1)} collective-permute-done((bf16[112,2048]{1,0:T(8,128)(2,1)S(1)}, bf16[112,2048]{1,0:T(8,128)(2,1)S(1)}, u32[]{:S(2)}, u32[]{:S(2)}) %collective-permute-start.38) | collective-permute-done | bytes 458784 | tf_op jit(solution)/shard_map/ppermute | solution.py:251
  198.5 0.9 collective-permute-start.22
  199.4 11.2 %collective-permute-done.40 = bf16[112,2048]{1,0:T(8,128)(2,1)S(1)} collective-permute-done((bf16[112,2048]{1,0:T(8,128)(2,1)S(1)}, bf16[112,2048]{1,0:T(8,128)(2,1)S(1)}, u32[]{:S(2)}, u32[]{:S(2)}) %collective-permute-start.40) | collective-permute-done | bytes 458784 | tf_op jit(solution)/shard_map/ppermute | solution.py:255
  211.0 1.4 collective-permute-start.13
  212.3 6.7 %collective-permute-done.30 = bf16[112,2048]{1,0:T(8,128)(2,1)S(1)} collective-permute-done((bf16[112,2048]{1,0:T(8,128)(2,1)S(1)}, bf16[112,2048]{1,0:T(8,128)(2,1)S(1)}, u32[]{:S(2)}, u32[]{:S(2)}) %collective-permute-start.30) | collective-permute-done | bytes 458784 | tf_op jit(solution)/shard_map/ppermute | solution.py:251
  219.0 0.8 collective-permute-start.24
  219.8 5.4 %collective-permute-done.41 = bf16[112,2048]{1,0:T(8,128)(2,1)S(1)} collective-permute-done((bf16[112,2048]{1,0:T(8,128)(2,1)S(1)}, bf16[112,2048]{1,0:T(8,128)(2,1)S(1)}, u32[]{:S(2)}, u32[]{:S(2)}) %collective-permute-start.41) | collective-permute-done | bytes 458784 | tf_op jit(solution)/shard_map/ppermute | solution.py:263
  226.0 1.5 collective-permute-done.24
  227.5 8.4 %collective-permute-done.42 = bf16[112,2048]{1,0:T(8,128)(2,1)S(1)} collective-permute-done((bf16[112,2048]{1,0:T(8,128)(2,1)S(1)}, bf16[112,2048]{1,0:T(8,128)(2,1)S(1)}, u32[]{:S(2)}, u32[]{:S(2)}) %collective-permute-start.42) | collective-permute-done | bytes 458784 | tf_op jit(solution)/shard_map/ppermute | solution.py:263
  236.2 10.2 %collective-permute-done.43 = bf16[112,2048]{1,0:T(8,128)(2,1)S(1)} collective-permute-done((bf16[112,2048]{1,0:T(8,128)(2,1)S(1)}, bf16[112,2048]{1,0:T(8,128)(2,1)S(1)}, u32[]{:S(2)}, u32[]{:S(2)}) %collective-permute-start.43) | collective-permute-done | bytes 458784 | tf_op jit(solution)/shard_map/ppermute | solution.py:263
  246.5 1.2 fusion.13
  (121 shorter events, 8.7 us)
Async XLA Ops:
  0.0 4.8 %copy-start.20 = (f32[8]{0:T(128)S(1)}, f32[8]{0:T(128)}, u32[]{:S(2)}) copy-start(f32[8]{0:T(128)} %param.18) | copy-start | bytes 100
  0.0 5.1 %copy-start.13 = (bf16[4,4096,1,128]{3,1,2,0:T(8,128)(2,1)S(1)}, bf16[4,4096,1,128]{3,1,2,0:T(8,128)(2,1)}, u32[]{:S(2)}) copy-start(bf16[4,4096,1,128]{3,1,2,0:T(8,128)(2,1)} %param.16) | copy-start | bytes 12582916
  1.0 4.9 %copy-start.14 = (bf16[1024,2048]{1,0:T(8,128)(2,1)S(1)}, bf16[1024,2048]{1,0:T(8,128)(2,1)}, u32[]{:S(2)}) copy-start(bf16[1024,2048]{1,0:T(8,128)(2,1)} %param.19) | copy-start | bytes 12582916
  5.1 6.6 %copy-start.17 = (bf16[2048,32]{0,1:T(8,128)(2,1)S(1)}, bf16[2048,32]{0,1:T(8,128)(2,1)}, u32[]{:S(2)}) copy-start(bf16[2048,32]{0,1:T(8,128)(2,1)} %param.23) | copy-start | bytes 393220
  5.1 6.9 %copy-start.19 = (s32[1,112,8]{1,2,0:T(8,128)S(1)}, s32[1,112,8]{1,2,0:T(8,128)}, u32[]{:S(2)}) copy-start(s32[1,112,8]{1,2,0:T(8,128)} %param.24) | copy-start | bytes 10756
  5.1 9.6 %copy-start.18 = (bf16[1,2048]{1,0:T(2,128)(2,1)S(1)}, bf16[1,2048]{1,0:T(2,128)(2,1)}, u32[]{:S(2)}) copy-start(bf16[1,2048]{1,0:T(2,128)(2,1)} %param.20) | copy-start | bytes 12292
  5.1 9.6 %copy-start.15 = (bf16[1,111,2048]{2,1,0:T(8,128)(2,1)S(1)}, bf16[1,111,2048]{2,1,0:T(8,128)(2,1)}, u32[]{:S(2)}) copy-start(bf16[1,111,2048]{2,1,0:T(8,128)(2,1)} %param.21) | copy-start | bytes 1363972
  5.1 9.7 %copy-start.12 = (f32[2048]{0:T(1024)S(1)}, f32[2048]{0:T(1024)}, u32[]{:S(2)}) copy-start(f32[2048]{0:T(1024)} %param.22) | copy-start | bytes 24580
  6.6 5.6 %collective-permute-start.2 = (f32[1,2048]{1,0:T(1,128)S(1)}, f32[1,2048]{1,0:T(1,128)S(1)}, u32[]{:S(2)}, u32[]{:S(2)}) collective-permute-start(f32[1,2048]{1,0:T(1,128)S(1)} %get-tuple-element.46), channel_id=1, source_target_pairs={{0,24},{8,16},{16,8},{24,0},{1,25},{9,17},{17,9},{25,1},{2,26},{10... | collective-permute-start | bytes 24584 | tf_op jit(solution)/shard_map/ppermute | solution.py:259
  10.5 3.7 %collective-permute-start.1 = (f32[1,2048]{1,0:T(1,128)S(1)}, f32[1,2048]{1,0:T(1,128)S(1)}, u32[]{:S(2)}, u32[]{:S(2)}) collective-permute-start(f32[1,2048]{1,0:T(1,128)S(1)} %get-tuple-element.47), channel_id=1, source_target_pairs={{0,16},{8,24},{16,0},{24,8},{1,17},{9,25},{17,1},{25,9},{2,18},{10... | collective-permute-start | bytes 24584 | tf_op jit(solution)/shard_map/ppermute | solution.py:255
  11.0 3.7 %collective-permute-start = (f32[1,2048]{1,0:T(1,128)S(1)}, f32[1,2048]{1,0:T(1,128)S(1)}, u32[]{:S(2)}, u32[]{:S(2)}) collective-permute-start(f32[1,2048]{1,0:T(1,128)S(1)} %get-tuple-element.45), channel_id=1, source_target_pairs={{0,8},{8,0},{16,24},{24,16},{1,9},{9,1},{17,25},{25,17},{2,10},{10... | collective-permute-start | bytes 24584 | tf_op jit(solution)/shard_map/ppermute | solution.py:251
  11.2 90.8 %collective-permute-start.7 = (bf16[2048,768]{1,0:T(8,128)(2,1)}, bf16[2048,768]{1,0:T(8,128)(2,1)}, u32[]{:S(2)}, u32[]{:S(2)}) collective-permute-start(bf16[2048,768]{1,0:T(8,128)(2,1)} %bitcast.38), channel_id=1, source_target_pairs={{0,1},{1,0},{2,3},{3,2},{4,5},{5,4},{6,7},{7,6},{8,9},{9,8},{10,11... | collective-permute-start | bytes 9437192 | tf_op jit(solution)/shard_map/ppermute | solution.py:267
  11.2 92.2 %collective-permute-start.8 = (bf16[2048,768]{1,0:T(8,128)(2,1)}, bf16[2048,768]{1,0:T(8,128)(2,1)}, u32[]{:S(2)}, u32[]{:S(2)}) collective-permute-start(bf16[2048,768]{1,0:T(8,128)(2,1)} %bitcast.43), channel_id=1, source_target_pairs={{0,1},{1,0},{2,3},{3,2},{4,5},{5,4},{6,7},{7,6},{8,9},{9,8},{10,11... | collective-permute-start | bytes 9437192 | tf_op jit(solution)/shard_map/ppermute | solution.py:267
  12.2 92.0 %collective-permute-start.9 = (bf16[768,2048]{1,0:T(8,128)(2,1)}, bf16[768,2048]{1,0:T(8,128)(2,1)}, u32[]{:S(2)}, u32[]{:S(2)}) collective-permute-start(bf16[768,2048]{1,0:T(8,128)(2,1)} %bitcast.48), channel_id=1, source_target_pairs={{0,1},{1,0},{2,3},{3,2},{4,5},{5,4},{6,7},{7,6},{8,9},{9,8},{10,11... | collective-permute-start | bytes 9437192 | tf_op jit(solution)/shard_map/ppermute | solution.py:267
  15.6 13.4 %collective-permute-start.14 = (bf16[112,2176]{1,0:T(8,128)(2,1)S(1)}, bf16[112,2176]{1,0:T(8,128)(2,1)S(1)}, u32[]{:S(2)}, u32[]{:S(2)}) collective-permute-start(bf16[112,2176]{1,0:T(8,128)(2,1)S(1)} %prepare.1.own_ref), channel_id=1, source_target_pairs={{0,2},{1,3},{2,4},{3,5},{4,6},{5,7},{6,0},{7,1},{8,10},{9,11},{10,... | collective-permute-start | bytes 1462280 | tf_op jit(solution)/shard_map/ppermute | solution.py:263
  17.2 13.3 %collective-permute-start.3 = (bf16[112,2176]{1,0:T(8,128)(2,1)S(1)}, bf16[112,2176]{1,0:T(8,128)(2,1)S(1)}, u32[]{:S(2)}, u32[]{:S(2)}) collective-permute-start(bf16[112,2176]{1,0:T(8,128)(2,1)S(1)} %prepare.1.own_ref), channel_id=1, source_target_pairs={{0,8},{8,0},{16,24},{24,16},{1,9},{9,1},{17,25},{25,17},{2,10},{10... | collective-permute-start | bytes 1462280 | tf_op jit(solution)/shard_map/ppermute | solution.py:251
  29.0 11.3 %collective-permute-start.4 = (bf16[112,2176]{1,0:T(8,128)(2,1)S(1)}, bf16[112,2176]{1,0:T(8,128)(2,1)S(1)}, u32[]{:S(2)}, u32[]{:S(2)}) collective-permute-start(bf16[112,2176]{1,0:T(8,128)(2,1)S(1)} %prepare.1.own_ref), channel_id=1, source_target_pairs={{0,16},{8,24},{16,0},{24,8},{1,17},{9,25},{17,1},{25,9},{2,18},{10... | collective-permute-start | bytes 1462280 | tf_op jit(solution)/shard_map/ppermute | solution.py:255
  30.5 11.3 %collective-permute-start.33 = (bf16[112,2176]{1,0:T(8,128)(2,1)S(1)}, bf16[112,2176]{1,0:T(8,128)(2,1)S(1)}, u32[]{:S(2)}, u32[]{:S(2)}) collective-permute-start(bf16[112,2176]{1,0:T(8,128)(2,1)S(1)} %collective-permute-done.14.own_ref), channel_id=1, source_target_pairs={{0,8},{8,0},{16,24},{24,16},{1,9},{9,1},{17,25},{25,17},{2,10},{10... | collective-permute-start | bytes 1462280 | tf_op jit(solution)/shard_map/ppermute | solution.py:251
  40.3 11.3 %collective-permute-start.34 = (bf16[112,2176]{1,0:T(8,128)(2,1)S(1)}, bf16[112,2176]{1,0:T(8,128)(2,1)S(1)}, u32[]{:S(2)}, u32[]{:S(2)}) collective-permute-start(bf16[112,2176]{1,0:T(8,128)(2,1)S(1)} %collective-permute-done.14.own_ref), channel_id=1, source_target_pairs={{0,16},{8,24},{16,0},{24,8},{1,17},{9,25},{17,1},{25,9},{2,18},{10... | collective-permute-start | bytes 1462280 | tf_op jit(solution)/shard_map/ppermute | solution.py:255
  41.8 11.7 %collective-permute-start.15 = (bf16[112,2176]{1,0:T(8,128)(2,1)S(1)}, bf16[112,2176]{1,0:T(8,128)(2,1)S(1)}, u32[]{:S(2)}, u32[]{:S(2)}) collective-permute-start(bf16[112,2176]{1,0:T(8,128)(2,1)S(1)} %collective-permute-done.14.own_ref), channel_id=1, source_target_pairs={{0,2},{1,3},{2,4},{3,5},{4,6},{5,7},{6,0},{7,1},{8,10},{9,11},{10,... | collective-permute-start | bytes 1462280 | tf_op jit(solution)/shard_map/ppermute | solution.py:263
  41.8 0.8 copy-start.2
  51.6 5.8 %collective-permute-start.35 = (bf16[48,2176]{1,0:T(8,128)(2,1)S(1)}, bf16[48,2176]{1,0:T(8,128)(2,1)S(1)}, u32[]{:S(2)}, u32[]{:S(2)}) collective-permute-start(bf16[48,2176]{1,0:T(8,128)(2,1)S(1)} %slice.102), channel_id=1, source_target_pairs={{0,16},{8,24},{16,0},{24,8},{1,17},{9,25},{17,1},{25,9},{2,18},{10... | collective-permute-start | bytes 626696 | tf_op jit(solution)/shard_map/ppermute | solution.py:255
  53.6 29.0 %copy-start.4 = (bf16[112,2176]{1,0:T(8,128)(2,1)}, bf16[112,2176]{1,0:T(8,128)(2,1)S(1)}, u32[]{:S(2)}) copy-start(bf16[112,2176]{1,0:T(8,128)(2,1)S(1)} %collective-permute-done.15.own_ref) | copy-start | bytes 1462276
  53.6 16.7 %collective-permute-start.25 = (bf16[112,2176]{1,0:T(8,128)(2,1)S(1)}, bf16[112,2176]{1,0:T(8,128)(2,1)S(1)}, u32[]{:S(2)}, u32[]{:S(2)}) collective-permute-start(bf16[112,2176]{1,0:T(8,128)(2,1)S(1)} %collective-permute-done.15.own_ref), channel_id=1, source_target_pairs={{0,8},{8,0},{16,24},{24,16},{1,9},{9,1},{17,25},{25,17},{2,10},{10... | collective-permute-start | bytes 1462280 | tf_op jit(solution)/shard_map/ppermute | solution.py:251
  58.1 11.5 %collective-permute-start.36 = (bf16[64,2176]{1,0:T(8,128)(2,1)S(1)}, bf16[64,2176]{1,0:T(8,128)(2,1)S(1)}, u32[]{:S(2)}, u32[]{:S(2)}) collective-permute-start(bf16[64,2176]{1,0:T(8,128)(2,1)S(1)} %slice.103), channel_id=1, source_target_pairs={{0,8},{8,0},{16,24},{24,16},{1,9},{9,1},{17,25},{25,17},{2,10},{10... | collective-permute-start | bytes 835592 | tf_op jit(solution)/shard_map/ppermute | solution.py:251
  69.5 0.7 copy-start.8
  70.3 10.6 %collective-permute-start.16 = (bf16[112,2176]{1,0:T(8,128)(2,1)S(1)}, bf16[112,2176]{1,0:T(8,128)(2,1)S(1)}, u32[]{:S(2)}, u32[]{:S(2)}) collective-permute-start(bf16[112,2176]{1,0:T(8,128)(2,1)S(1)} %collective-permute-done.15.own_ref), channel_id=1, source_target_pairs={{0,2},{1,3},{2,4},{3,5},{4,6},{5,7},{6,0},{7,1},{8,10},{9,11},{10,... | collective-permute-start | bytes 1462280 | tf_op jit(solution)/shard_map/ppermute | solution.py:263
  70.3 12.3 %collective-permute-start.26 = (bf16[112,2176]{1,0:T(8,128)(2,1)S(1)}, bf16[112,2176]{1,0:T(8,128)(2,1)S(1)}, u32[]{:S(2)}, u32[]{:S(2)}) collective-permute-start(bf16[112,2176]{1,0:T(8,128)(2,1)S(1)} %collective-permute-done.15.own_ref), channel_id=1, source_target_pairs={{0,16},{8,24},{16,0},{24,8},{1,17},{9,25},{17,1},{25,9},{2,18},{10... | collective-permute-start | bytes 1462280 | tf_op jit(solution)/shard_map/ppermute | solution.py:255
  80.9 11.1 %collective-permute-start.17 = (bf16[112,2176]{1,0:T(8,128)(2,1)S(1)}, bf16[112,2176]{1,0:T(8,128)(2,1)}, u32[]{:S(2)}, u32[]{:S(2)}) collective-permute-start(bf16[112,2176]{1,0:T(8,128)(2,1)S(1)} %collective-permute-done.16.own_ref), channel_id=1, source_target_pairs={{0,8},{8,0},{16,24},{24,16},{1,9},{9,1},{17,25},{25,17},{2,10},{10... | collective-permute-start | bytes 1462280 | tf_op jit(solution)/shard_map/ppermute | solution.py:251
  82.6 12.1 %collective-permute-start.18 = (bf16[112,2176]{1,0:T(8,128)(2,1)S(1)}, bf16[112,2176]{1,0:T(8,128)(2,1)S(1)}, u32[]{:S(2)}, u32[]{:S(2)}) collective-permute-start(bf16[112,2176]{1,0:T(8,128)(2,1)S(1)} %collective-permute-done.16.own_ref), channel_id=1, source_target_pairs={{0,16},{8,24},{16,0},{24,8},{1,17},{9,25},{17,1},{25,9},{2,18},{10... | collective-permute-start | bytes 1462280 | tf_op jit(solution)/shard_map/ppermute | solution.py:255
  83.9 0.8 copy-start.6
  85.3 0.8 copy-start
  92.0 8.3 %collective-permute-start.28 = (bf16[48,2176]{1,0:T(8,128)(2,1)}, bf16[48,2176]{1,0:T(8,128)(2,1)}, u32[]{:S(2)}, u32[]{:S(2)}) collective-permute-start(bf16[48,2176]{1,0:T(8,128)(2,1)} %slice.101), channel_id=1, source_target_pairs={{0,8},{8,0},{16,24},{24,16},{1,9},{9,1},{17,25},{25,17},{2,10},{10... | collective-permute-start | bytes 626696 | tf_op jit(solution)/shard_map/ppermute | solution.py:251
  94.7 27.3 %collective-permute-start.27 = (bf16[64,2176]{1,0:T(8,128)(2,1)}, bf16[64,2176]{1,0:T(8,128)(2,1)}, u32[]{:S(2)}, u32[]{:S(2)}) collective-permute-start(bf16[64,2176]{1,0:T(8,128)(2,1)} %slice.100), channel_id=1, source_target_pairs={{0,16},{8,24},{16,0},{24,8},{1,17},{9,25},{17,1},{25,9},{2,18},{10... | collective-permute-start | bytes 835592 | tf_op jit(solution)/shard_map/ppermute | solution.py:255
  100.3 59.7 %collective-permute-start.5 = (bf16[64,2176]{1,0:T(8,128)(2,1)S(1)}, bf16[64,2176]{1,0:T(8,128)(2,1)S(1)}, u32[]{:S(2)}, u32[]{:S(2)}) collective-permute-start(bf16[64,2176]{1,0:T(8,128)(2,1)S(1)} %slice.96), channel_id=1, source_target_pairs={{0,16},{8,24},{16,0},{24,8},{1,17},{9,25},{17,1},{25,9},{2,18},{10... | collective-permute-start | bytes 835592 | tf_op jit(solution)/shard_map/ppermute | solution.py:255
  101.9 57.6 %collective-permute-start.6 = (bf16[48,2176]{1,0:T(8,128)(2,1)S(1)}, bf16[48,2176]{1,0:T(8,128)(2,1)S(1)}, u32[]{:S(2)}, u32[]{:S(2)}) collective-permute-start(bf16[48,2176]{1,0:T(8,128)(2,1)S(1)} %slice.97), channel_id=1, source_target_pairs={{0,8},{8,0},{16,24},{24,16},{1,9},{9,1},{17,25},{25,17},{2,10},{10... | collective-permute-start | bytes 626696 | tf_op jit(solution)/shard_map/ppermute | solution.py:251
  103.4 39.9 %collective-permute-start.19 = (bf16[48,2176]{1,0:T(8,128)(2,1)S(1)}, bf16[48,2176]{1,0:T(8,128)(2,1)S(1)}, u32[]{:S(2)}, u32[]{:S(2)}) collective-permute-start(bf16[48,2176]{1,0:T(8,128)(2,1)S(1)} %slice.98), channel_id=1, source_target_pairs={{0,16},{8,24},{16,0},{24,8},{1,17},{9,25},{17,1},{25,9},{2,18},{10... | collective-permute-start | bytes 626696 | tf_op jit(solution)/shard_map/ppermute | solution.py:255
  104.2 40.6 %collective-permute-start.20 = (bf16[64,2176]{1,0:T(8,128)(2,1)S(1)}, bf16[64,2176]{1,0:T(8,128)(2,1)S(1)}, u32[]{:S(2)}, u32[]{:S(2)}) collective-permute-start(bf16[64,2176]{1,0:T(8,128)(2,1)S(1)} %slice.99), channel_id=1, source_target_pairs={{0,8},{8,0},{16,24},{24,16},{1,9},{9,1},{17,25},{25,17},{2,10},{10... | collective-permute-start | bytes 835592 | tf_op jit(solution)/shard_map/ppermute | solution.py:251
  104.5 1.0 copy-start.3
  105.5 1.0 copy-start.9
  106.5 0.9 copy-start.11
  107.4 16.4 %copy-start.1 = (bf16[112,2176]{1,0:T(8,128)(2,1)S(1)}, bf16[112,2176]{1,0:T(8,128)(2,1)}, u32[]{:S(2)}) copy-start(bf16[112,2176]{1,0:T(8,128)(2,1)} %copy-done) | copy-start | bytes 1462276
  107.4 16.4 %copy-start.5 = (bf16[112,2176]{1,0:T(8,128)(2,1)S(1)}, bf16[112,2176]{1,0:T(8,128)(2,1)}, u32[]{:S(2)}) copy-start(bf16[112,2176]{1,0:T(8,128)(2,1)} %copy-done.4) | copy-start | bytes 1462276
  122.0 54.6 %collective-permute-start.37 = (bf16[48,2048]{1,0:T(8,128)(2,1)S(1)}, bf16[48,2048]{1,0:T(8,128)(2,1)S(1)}, u32[]{:S(2)}, u32[]{:S(2)}) collective-permute-start(bf16[48,2048]{1,0:T(8,128)(2,1)S(1)} %get-tuple-element.42), channel_id=1, source_target_pairs={{0,16},{8,24},{16,0},{24,8},{1,17},{9,25},{17,1},{25,9},{2,18},{10... | collective-permute-start | bytes 589832 | tf_op jit(solution)/shard_map/ppermute | solution.py:255
  123.8 21.6 %copy-start.7 = (bf16[112,2176]{1,0:T(8,128)(2,1)S(1)}, bf16[112,2176]{1,0:T(8,128)(2,1)}, u32[]{:S(2)}) copy-start(bf16[112,2176]{1,0:T(8,128)(2,1)} %copy-done.6) | copy-start | bytes 1462276
  143.3 43.4 %collective-permute-start.39 = (bf16[64,2048]{1,0:T(8,128)(2,1)S(1)}, bf16[64,2048]{1,0:T(8,128)(2,1)S(1)}, u32[]{:S(2)}, u32[]{:S(2)}) collective-permute-start(bf16[64,2048]{1,0:T(8,128)(2,1)S(1)} %get-tuple-element.44), channel_id=1, source_target_pairs={{0,8},{8,0},{16,24},{24,16},{1,9},{9,1},{17,25},{25,17},{2,10},{10... | collective-permute-start | bytes 786440 | tf_op jit(solution)/shard_map/ppermute | solution.py:251
  144.8 33.2 %collective-permute-start.31 = (bf16[48,2048]{1,0:T(8,128)(2,1)S(1)}, bf16[48,2048]{1,0:T(8,128)(2,1)S(1)}, u32[]{:S(2)}, u32[]{:S(2)}) collective-permute-start(bf16[48,2048]{1,0:T(8,128)(2,1)S(1)} %get-tuple-element.39), channel_id=1, source_target_pairs={{0,8},{8,0},{16,24},{24,16},{1,9},{9,1},{17,25},{25,17},{2,10},{10... | collective-permute-start | bytes 589832 | tf_op jit(solution)/shard_map/ppermute | solution.py:251
  159.6 27.7 %collective-permute-start.29 = (bf16[64,2048]{1,0:T(8,128)(2,1)S(1)}, bf16[64,2048]{1,0:T(8,128)(2,1)S(1)}, u32[]{:S(2)}, u32[]{:S(2)}) collective-permute-start(bf16[64,2048]{1,0:T(8,128)(2,1)S(1)} %get-tuple-element.37), channel_id=1, source_target_pairs={{0,16},{8,24},{16,0},{24,8},{1,17},{9,25},{17,1},{25,9},{2,18},{10... | collective-permute-start | bytes 786440 | tf_op jit(solution)/shard_map/ppermute | solution.py:255
  160.1 50.7 %collective-permute-start.23 = (bf16[64,2048]{1,0:T(8,128)(2,1)S(1)}, bf16[64,2048]{1,0:T(8,128)(2,1)S(1)}, u32[]{:S(2)}, u32[]{:S(2)}) collective-permute-start(bf16[64,2048]{1,0:T(8,128)(2,1)S(1)} %get-tuple-element.34), channel_id=1, source_target_pairs={{0,8},{8,0},{16,24},{24,16},{1,9},{9,1},{17,25},{25,17},{2,10},{10... | collective-permute-start | bytes 786440 | tf_op jit(solution)/shard_map/ppermute | solution.py:251
  176.6 7.9 %collective-permute-start.21 = (bf16[48,2048]{1,0:T(8,128)(2,1)S(1)}, bf16[48,2048]{1,0:T(8,128)(2,1)S(1)}, u32[]{:S(2)}, u32[]{:S(2)}) collective-permute-start(bf16[48,2048]{1,0:T(8,128)(2,1)S(1)} %get-tuple-element.32), channel_id=1, source_target_pairs={{0,16},{8,24},{16,0},{24,8},{1,17},{9,25},{17,1},{25,9},{2,18},{10... | collective-permute-start | bytes 589832 | tf_op jit(solution)/shard_map/ppermute | solution.py:255
  178.0 7.9 %collective-permute-start.12 = (bf16[48,2048]{1,0:T(8,128)(2,1)S(1)}, bf16[48,2048]{1,0:T(8,128)(2,1)S(1)}, u32[]{:S(2)}, u32[]{:S(2)}) collective-permute-start(bf16[48,2048]{1,0:T(8,128)(2,1)S(1)} %get-tuple-element.29), channel_id=1, source_target_pairs={{0,8},{8,0},{16,24},{24,16},{1,9},{9,1},{17,25},{25,17},{2,10},{10... | collective-permute-start | bytes 589832 | tf_op jit(solution)/shard_map/ppermute | solution.py:251
  184.5 41.1 %collective-permute-start.10 = (bf16[64,2048]{1,0:T(8,128)(2,1)S(1)}, bf16[64,2048]{1,0:T(8,128)(2,1)S(1)}, u32[]{:S(2)}, u32[]{:S(2)}) collective-permute-start(bf16[64,2048]{1,0:T(8,128)(2,1)S(1)} %get-tuple-element.27), channel_id=1, source_target_pairs={{0,16},{8,24},{16,0},{24,8},{1,17},{9,25},{17,1},{25,9},{2,18},{10... | collective-permute-start | bytes 786440 | tf_op jit(solution)/shard_map/ppermute | solution.py:255
  185.9 12.5 %collective-permute-start.38 = (bf16[112,2048]{1,0:T(8,128)(2,1)S(1)}, bf16[112,2048]{1,0:T(8,128)(2,1)S(1)}, u32[]{:S(2)}, u32[]{:S(2)}) collective-permute-start(bf16[112,2048]{1,0:T(8,128)(2,1)S(1)} %pad_maximum_fusion.7), channel_id=1, source_target_pairs={{0,8},{8,0},{16,24},{24,16},{1,9},{9,1},{17,25},{25,17},{2,10},{10... | collective-permute-start | bytes 1376264 | tf_op jit(solution)/shard_map/ppermute | solution.py:251
  186.7 24.2 %collective-permute-start.32 = (bf16[112,2048]{1,0:T(8,128)(2,1)S(1)}, bf16[112,2048]{1,0:T(8,128)(2,1)S(1)}, u32[]{:S(2)}, u32[]{:S(2)}) collective-permute-start(bf16[112,2048]{1,0:T(8,128)(2,1)S(1)} %pad_maximum_fusion.6), channel_id=1, source_target_pairs={{0,16},{8,24},{16,0},{24,8},{1,17},{9,25},{17,1},{25,9},{2,18},{10... | collective-permute-start | bytes 1376264 | tf_op jit(solution)/shard_map/ppermute | solution.py:255
  187.3 23.3 %collective-permute-start.40 = (bf16[112,2048]{1,0:T(8,128)(2,1)S(1)}, bf16[112,2048]{1,0:T(8,128)(2,1)S(1)}, u32[]{:S(2)}, u32[]{:S(2)}) collective-permute-start(bf16[112,2048]{1,0:T(8,128)(2,1)S(1)} %pad_maximum_fusion.8), channel_id=1, source_target_pairs={{0,16},{8,24},{16,0},{24,8},{1,17},{9,25},{17,1},{25,9},{2,18},{10... | collective-permute-start | bytes 1376264 | tf_op jit(solution)/shard_map/ppermute | solution.py:255
  198.5 27.6 %collective-permute-start.22 = (bf16[112,2048]{1,0:T(8,128)(2,1)S(1)}, bf16[112,2048]{1,0:T(8,128)(2,1)S(1)}, u32[]{:S(2)}, u32[]{:S(2)}) collective-permute-start(bf16[112,2048]{1,0:T(8,128)(2,1)S(1)} %pad_maximum_fusion.3), channel_id=1, source_target_pairs={{0,8},{8,0},{16,24},{24,16},{1,9},{9,1},{17,25},{25,17},{2,10},{10... | collective-permute-start | bytes 1376264 | tf_op jit(solution)/shard_map/ppermute | solution.py:251
  210.6 8.5 %collective-permute-start.30 = (bf16[112,2048]{1,0:T(8,128)(2,1)S(1)}, bf16[112,2048]{1,0:T(8,128)(2,1)S(1)}, u32[]{:S(2)}, u32[]{:S(2)}) collective-permute-start(bf16[112,2048]{1,0:T(8,128)(2,1)S(1)} %pad_maximum_fusion.5), channel_id=1, source_target_pairs={{0,8},{8,0},{16,24},{24,16},{1,9},{9,1},{17,25},{25,17},{2,10},{10... | collective-permute-start | bytes 1376264 | tf_op jit(solution)/shard_map/ppermute | solution.py:251
  210.7 35.7 %copy-start.16 = (bf16[1,111,2048]{2,1,0:T(8,128)(2,1)S(1)}, bf16[1,111,2048]{2,1,0:T(8,128)(2,1)}, u32[]{:S(2)}) copy-start(bf16[1,111,2048]{2,1,0:T(8,128)(2,1)} %param.21) | copy-start | bytes 1363972
  210.8 14.5 %collective-permute-start.41 = (bf16[112,2048]{1,0:T(8,128)(2,1)S(1)}, bf16[112,2048]{1,0:T(8,128)(2,1)S(1)}, u32[]{:S(2)}, u32[]{:S(2)}) collective-permute-start(bf16[112,2048]{1,0:T(8,128)(2,1)S(1)} %add_convert_fusion.3), channel_id=1, source_target_pairs={{0,2},{1,3},{2,4},{3,5},{4,6},{5,7},{6,0},{7,1},{8,10},{9,11},{10,... | collective-permute-start | bytes 1376264 | tf_op jit(solution)/shard_map/ppermute | solution.py:263
  211.0 25.3 %collective-permute-start.13 = (bf16[112,2048]{1,0:T(8,128)(2,1)S(1)}, bf16[112,2048]{1,0:T(8,128)(2,1)S(1)}, u32[]{:S(2)}, u32[]{:S(2)}) collective-permute-start(bf16[112,2048]{1,0:T(8,128)(2,1)S(1)} %pad_maximum_fusion.2), channel_id=1, source_target_pairs={{0,16},{8,24},{16,0},{24,8},{1,17},{9,25},{17,1},{25,9},{2,18},{10... | collective-permute-start | bytes 1376264 | tf_op jit(solution)/shard_map/ppermute | solution.py:255
  219.0 8.5 %collective-permute-start.24 = (bf16[112,2048]{1,0:T(8,128)(2,1)S(1)}, bf16[112,2048]{1,0:T(8,128)(2,1)S(1)}, u32[]{:S(2)}, u32[]{:S(2)}) collective-permute-start(bf16[112,2048]{1,0:T(8,128)(2,1)S(1)} %pad_maximum_fusion.4), channel_id=1, source_target_pairs={{0,16},{8,24},{16,0},{24,8},{1,17},{9,25},{17,1},{25,9},{2,18},{10... | collective-permute-start | bytes 1376264 | tf_op jit(solution)/shard_map/ppermute | solution.py:255
  225.5 10.3 %collective-permute-start.42 = (bf16[112,2048]{1,0:T(8,128)(2,1)S(1)}, bf16[112,2048]{1,0:T(8,128)(2,1)S(1)}, u32[]{:S(2)}, u32[]{:S(2)}) collective-permute-start(bf16[112,2048]{1,0:T(8,128)(2,1)S(1)} %add_convert_fusion.2), channel_id=1, source_target_pairs={{0,2},{1,3},{2,4},{3,5},{4,6},{5,7},{6,0},{7,1},{8,10},{9,11},{10,... | collective-permute-start | bytes 1376264 | tf_op jit(solution)/shard_map/ppermute | solution.py:263
  225.7 10.5 %collective-permute-start.11 = (bf16[112,2048]{1,0:T(8,128)(2,1)S(1)}, bf16[112,2048]{1,0:T(8,128)(2,1)S(1)}, u32[]{:S(2)}, u32[]{:S(2)}) collective-permute-start(bf16[112,2048]{1,0:T(8,128)(2,1)S(1)} %pad_maximum_fusion.1), channel_id=1, source_target_pairs={{0,8},{8,0},{16,24},{24,16},{1,9},{9,1},{17,25},{25,17},{2,10},{10... | collective-permute-start | bytes 1376264 | tf_op jit(solution)/shard_map/ppermute | solution.py:251
  236.2 10.3 %collective-permute-start.43 = (bf16[112,2048]{1,0:T(8,128)(2,1)S(1)}, bf16[112,2048]{1,0:T(8,128)(2,1)S(1)}, u32[]{:S(2)}, u32[]{:S(2)}) collective-permute-start(bf16[112,2048]{1,0:T(8,128)(2,1)S(1)} %add_convert_fusion.1), channel_id=1, source_target_pairs={{0,2},{1,3},{2,4},{3,5},{4,6},{5,7},{6,0},{7,1},{8,10},{9,11},{10,... | collective-permute-start | bytes 1376264 | tf_op jit(solution)/shard_map/ppermute | solution.py:263
  (1 other events, 0.7 us)

commit v3 on v2

--- a/solution.py
+++ b/solution.py
@@ -1,3 +1,4 @@
+import functools
 import math
 
 import jax
@@ -117,66 +118,42 @@
     )(expert, rows, gate_weights, up_weights, down_weights)
 
 
-def plane_kernel(
-    ids_ref,
-    own_ref,
-    x_ref,
-    y_ref,
-    d0_ref,
-    d1_ref,
-    gate0_ref,
-    up0_ref,
-    down0_ref,
-    gate1_ref,
-    up1_ref,
-    down1_ref,
-    own_out,
-    x_out,
-    y_out,
-    d0_out,
-    d1_out,
-    rows,
-    gates,
-    ups,
-    downs,
-    inner,
-    sums,
-    row_sem,
-    weight_sem,
-    out_sem,
-):
+def plane_kernel(piece_rows, block_rows, *refs):
+    refs = list(refs)
+    ids_ref = refs.pop(0)
+    sources = [refs.pop(0) for _ in piece_rows]
+    gate_ref, up_ref, down_ref = [refs.pop(0) for _ in range(3)]
+    targets = [refs.pop(0) for _ in block_rows]
+    rows, gates, ups, downs, inner, sums, row_sem, weight_sem, out_sem = refs
     width = sums.shape[1]
     units = gates.shape[2]
     tile = 256
     out_tile = 512
-    sources = (own_ref, x_ref, y_ref, d0_ref, d1_ref)
-    targets = (own_out, x_out, y_out, d0_out, d1_out)
-    starts = []
+    row_copies = []
     at = 0
-    for ref in sources:
-        starts.append(at)
-        at += ref.shape[0]
-    row_copies = [
-        pltpu.make_async_copy(ref, rows.at[pl.ds(start, ref.shape[0])], row_sem.at[i])
-        for i, (ref, start) in enumerate(zip(sources, starts))
-    ]
+    for ref, count in zip(sources, piece_rows):
+        copy = pltpu.make_async_copy(ref, rows.at[pl.ds(at, count)], row_sem.at[len(row_copies)])
+        row_copies.append(copy)
+        at += count
     weight_copies = []
-    for e, (gate, up) in enumerate(((gate0_ref, up0_ref), (gate1_ref, up1_ref))):
+    for e in range(2):
         for j in range(units // tile):
             part = pl.ds(j * tile, tile)
-            for source, target in ((gate, gates), (up, ups)):
+            for source, target in ((gate_ref, gates), (up_ref, ups)):
                 weight_copies.append(
                     pltpu.make_async_copy(
-                        source.at[:, part], target.at[e, :, part], weight_sem.at[len(weight_copies)]
+                        source.at[e, :, part], target.at[e, :, part], weight_sem.at[len(weight_copies)]
                     )
                 )
     first_down = len(weight_copies)
     for j in range(width // out_tile):
         part = pl.ds(j * out_tile, out_tile)
-        for e, down in enumerate((down0_ref, down1_ref)):
+        for e in range(2):
             weight_copies.append(
                 pltpu.make_async_copy(
-                    down.at[:, part], downs.at[e, :, part], weight_sem.at[len(weight_copies)]
+                    down_ref.at[e, :, part],
+                    downs.at[e, :, part],
+                    weight_sem.at[len(weight_copies)],
                 )
             )
     for copy in row_copies + weight_copies:
@@ -209,28 +186,30 @@
         result = jnp.dot(inner[:, :units], downs[0, :, part], preferred_element_type=jnp.float32)
         result += jnp.dot(inner[:, units:], downs[1, :, part], preferred_element_type=jnp.float32)
         sums[:, part] = result.astype(jnp.bfloat16)
-        for ref, start in zip(targets, starts):
+        at = 0
+        for ref, count in zip(targets, block_rows):
             copy = pltpu.make_async_copy(
-                sums.at[pl.ds(start, ref.shape[0]), part],
-                ref.at[:, part],
-                out_sem.at[len(out_copies)],
+                sums.at[pl.ds(at, count), part], ref.at[:, part], out_sem.at[len(out_copies)]
             )
             copy.start()
             out_copies.append(copy)
+            at += count
     for copy in out_copies:
         copy.wait()
 
 
-def run_plane(ids, blocks, own_weights, other_weights):
-    width, units = own_weights[0].shape
-    padded = blocks[0].shape[1]
-    total = sum(block.shape[0] for block in blocks)
+def run_plane(ids, pieces, block_rows, weights):
+    _, width, units = weights[0].shape
+    padded = pieces[0].shape[1]
+    piece_rows = tuple(piece.shape[0] for piece in pieces)
+    total = sum(piece_rows)
     kept = jnp.bfloat16
+    anywhere = pl.BlockSpec(memory_space=pl.ANY)
     return pl.pallas_call(
-        plane_kernel,
-        in_specs=[pl.BlockSpec(memory_space=pltpu.SMEM)] + [pl.BlockSpec(memory_space=pl.ANY)] * 11,
-        out_specs=[pl.BlockSpec(memory_space=pl.ANY)] * 5,
-        out_shape=[jax.ShapeDtypeStruct((block.shape[0], width), kept) for block in blocks],
+        functools.partial(plane_kernel, piece_rows, block_rows),
+        in_specs=[pl.BlockSpec(memory_space=pltpu.SMEM)] + [anywhere] * (len(pieces) + 3),
+        out_specs=[anywhere] * len(block_rows),
+        out_shape=[jax.ShapeDtypeStruct((count, width), kept) for count in block_rows],
         scratch_shapes=[
             pltpu.VMEM((total, padded), kept),
             pltpu.VMEM((2, width, units), kept),
@@ -238,13 +217,35 @@
             pltpu.VMEM((2, units, width), kept),
             pltpu.VMEM((total, 2 * units), kept),
             pltpu.VMEM((total, width), kept),
-            pltpu.SemaphoreType.DMA((5,)),
+            pltpu.SemaphoreType.DMA((len(pieces),)),
             pltpu.SemaphoreType.DMA((4 * (units // 256) + 2 * (width // 512),)),
-            pltpu.SemaphoreType.DMA((5 * (width // 512),)),
+            pltpu.SemaphoreType.DMA((len(block_rows) * (width // 512),)),
         ],
         compiler_params=pltpu.CompilerParams(vmem_limit_bytes=48 << 20),
+        cost_estimate=pl.CostEstimate(
+            flops=12 * total * width * units, bytes_accessed=24 << 20, transcendentals=total * units
+        ),
         name="plane",
-    )(ids, *blocks, *own_weights, *other_weights)
+    )(ids, *pieces, *weights)
+
+
+def merge_kernel(cut, x_ref, y_ref, passed_0_ref, passed_1_ref, x_out, y_out):
+    def sum_of(one, other):
+        return (one.astype(jnp.float32) + other.astype(jnp.float32)).astype(jnp.bfloat16)
+
+    x_out[:cut, :] = sum_of(x_ref[:cut, :], passed_0_ref[...])
+    x_out[cut:, :] = x_ref[cut:, :]
+    y_out[:cut, :] = y_ref[:cut, :]
+    y_out[cut:, :] = sum_of(y_ref[cut:, :], passed_1_ref[...])
+
+
+def merge_passed(cut, to_x, to_y, passed_0, passed_1):
+    return pl.pallas_call(
+        functools.partial(merge_kernel, cut),
+        out_shape=[jax.ShapeDtypeStruct(to_x.shape, to_x.dtype)] * 2,
+        compiler_params=pltpu.CompilerParams(vmem_limit_bytes=16 << 20),
+        name="merge",
+    )(to_x, to_y, passed_0, passed_1)
 
 
 def along_x(value):
@@ -255,16 +256,17 @@
     return lax.ppermute(value, "kv", [(i, i ^ 2) for i in range(4)])
 
 
-def along_diagonal(value):
-    return lax.ppermute(value, "kv", [(i, i ^ 3) for i in range(4)])
-
-
 def around_z(value):
     return lax.ppermute(value, "blk", [(i, (i + 2) % 8) for i in range(8)])
 
 
-def across_chip(value):
-    return lax.ppermute(value, "blk", [(i, i ^ 1) for i in range(8)])
+def both_cores(value):
+    pairs = [[i, i + 1] for i in range(0, 8, 2)]
+    return lax.all_gather(value, "blk", axis_index_groups=pairs, axis=0, tiled=True)
+
+
+def fence(*values):
+    return lax.optimization_barrier(values)
 
 
 def added(*parts):
@@ -293,55 +295,117 @@
     experts = router.shape[1]
     ids = routes[0]
     tokens = ids.shape[0]
-    own_weights = (expert_gate[0], expert_up[0], expert_down[0])
-    other_weights = tuple(across_chip(w) for w in own_weights)
+    weights = tuple(both_cores(w) for w in (expert_gate, expert_up, expert_down))
     my_kv = lax.axis_index("kv")
     my_blk = lax.axis_index("blk")
-    first_expert = my_kv * 8
-    expert_ids = jnp.stack(
-        [first_expert + my_blk, first_expert + (my_blk ^ 1), jnp.int32(experts)]
-    ).astype(jnp.int32)
+    first_expert = my_kv * 8 + my_blk // 2 * 2
+    expert_ids = jnp.stack([first_expert, first_expert + 1, jnp.int32(experts)]).astype(jnp.int32)
+
+    late = 16
+    prefill = prefill_hidden[0]
+    body = prepare(prefill[late - 1 :], norm_gain, router, ids[late:])
+    body, queries = fence(body, queries)
+    body_sides = along_x(body), along_y(body)
+    body_next = around_z(body)
 
     attended = attend(queries, cache_keys, cache_values, lengths, sinks)
     partial_proj = jnp.dot(attended, out_proj, preferred_element_type=jnp.float32)
-
-    def row_of(index):
-        return lax.dynamic_slice_in_dim(partial_proj, index, 1)
-
-    projected = (
-        row_of(my_kv)
-        + along_x(row_of(my_kv ^ 1))
-        + along_y(row_of(my_kv ^ 2))
-        + along_diagonal(row_of(my_kv ^ 3))
-    )
+    partial_proj = jnp.concatenate(
+        [lax.dynamic_slice_in_dim(partial_proj, my_kv ^ other, 1) for other in (0, 2, 1, 3)], axis=0
+    )
+    pair = partial_proj[:2] + along_x(partial_proj[2:])
+    projected = pair[:1] + along_y(pair[1:])
     decoded = (decode_resid.astype(jnp.float32) + projected).astype(jnp.bfloat16)
-    hidden = jnp.concatenate([decoded, prefill_hidden[0]], axis=0)
-    block = prepare(hidden, norm_gain, router, ids)
-    layer_sum = hidden.astype(jnp.float32)
+    decoded, body_sides, body_next = fence(decoded, body_sides, body_next)
+    hidden = jnp.concatenate([decoded, prefill], axis=0)
+    head = prepare(
+        jnp.concatenate([decoded, prefill[: late - 1]], axis=0), norm_gain, router, ids[:late]
+    )
+    head_sides = along_x(head), along_y(head)
+    head_next = around_z(head)
+    head_sides, head_next = fence(head_sides, head_next)
+
+    long = (tokens // 2 + 15) // 16 * 16
+    cuts = [long, tokens - long, long, tokens - long]
+    blocks = [None, jnp.concatenate([head_next, body_next], axis=0), None, None]
+    sides = [None] * 4
+    corners = [None] * 4
+    sums = [None] * 4
+    passed = [None] * 4
+    back = [None] * 4
+
+    def spread(step):
+        sides[step] = along_x(blocks[step]), along_y(blocks[step])
+        if step < 3:
+            blocks[step + 1] = around_z(blocks[step])
+
+    def spread_corners(step):
+        cut = cuts[step]
+        if step == 0:
+            by_y = jnp.concatenate([head_sides[0], body_sides[0][: cut - late]], axis=0)
+            by_x = body_sides[1][cut - late :]
+        else:
+            by_y, by_x = sides[step][0][:cut], sides[step][1][cut:]
+        corners[step] = along_y(by_y), along_x(by_x)
+
+    def apply(step):
+        if step == 0:
+            pieces = (head, body, head_sides[0], body_sides[0], head_sides[1], body_sides[1])
+        else:
+            pieces = (blocks[step],) + sides[step]
+        counts = (tokens, tokens, tokens, cuts[step], tokens - cuts[step])
+        sums[step] = run_plane(expert_ids, pieces + corners[step], counts, weights)
+
+    def return_corners(step):
+        passed[step] = along_y(sums[step][3]), along_x(sums[step][4])
+
+    def return_sides(step):
+        to_x, to_y = merge_passed(cuts[step], sums[step][1], sums[step][2], *passed[step])
+        back[step] = along_x(to_x), along_y(to_y)
+
+    spread_corners(0)
+    spread(1)
+    corners[0], sides[1], blocks[2] = fence(corners[0], sides[1], blocks[2])
+
+    spread_corners(1)
+    spread(2)
+    apply(0)
+    corners[1], sides[2], blocks[3], sums[0] = fence(corners[1], sides[2], blocks[3], sums[0])
+
+    spread_corners(2)
+    spread(3)
+    far_0 = along_y(sums[0][3])
+    apply(1)
+    corners[2], sides[3], far_0, sums[0], sums[1] = fence(
+        corners[2], sides[3], far_0, sums[0], sums[1]
+    )
+
+    spread_corners(3)
+    passed[0] = far_0, along_x(sums[0][4])
+    return_corners(1)
+    apply(2)
+    corners[3], passed[0], passed[1], sums[0], sums[1], sums[2] = fence(
+        corners[3], passed[0], passed[1], sums[0], sums[1], sums[2]
+    )
+
+    return_sides(0)
+    return_corners(2)
+    apply(3)
+    back[0], passed[2], sums[1], sums[2], sums[3] = fence(
+        back[0], passed[2], sums[1], sums[2], sums[3]
+    )
+
+    return_corners(3)
+    return_sides(1)
+    layer_sum = added(hidden, sums[0][0], *back[0])
+    passed[3], back[1], sums[2], sums[3] = fence(passed[3], back[1], sums[2], sums[3])
+
+    return_sides(2)
+    return_sides(3)
     carried = None
-    long = (tokens // 2 + 15) // 16 * 16
-    for step in range(4):
-        cut = long if step % 2 == 0 else tokens - long
-        from_x = along_x(block)
-        from_y = along_y(block)
-        diagonal_0 = along_y(from_x[:cut])
-        diagonal_1 = along_x(from_y[cut:])
-        following = around_z(block) if step < 3 else None
-        own, to_x, to_y, far_0, far_1 = run_plane(
-            expert_ids, (block, from_x, from_y, diagonal_0, diagonal_1), own_weights, other_weights
-        )
-        passed_0 = along_y(far_0)
-        passed_1 = along_x(far_1)
-        to_x = jnp.concatenate([added(to_x[:cut], passed_0), to_x[cut:].astype(jnp.float32)], axis=0)
-        to_y = jnp.concatenate([to_y[:cut].astype(jnp.float32), added(to_y[cut:], passed_1)], axis=0)
-        back_x = along_x(to_x.astype(jnp.bfloat16))
-        back_y = along_y(to_y.astype(jnp.bfloat16))
-        if step == 0:
-            layer_sum = added(layer_sum, own, back_x, back_y)
-        else:
-            parts = (own, back_x, back_y) + ((carried,) if step > 1 else ())
-            carried = around_z(added(*parts).astype(jnp.bfloat16))
-        block = following
+    for step in range(1, 4):
+        parts = (sums[step][0],) + back[step] + ((carried,) if step > 1 else ())
+        carried = around_z(added(*parts).astype(jnp.bfloat16))
     return added(layer_sum, carried).astype(jnp.bfloat16)[None]
 
 

time: 248 us -> 213 us (0.86)
  waiting for transfers between devices: 120 us -> 80.2 us
  between operations: 0.57 us -> 13.6 us
  Pallas kernels: 63.6 us -> 59.1 us
    ppermute x6 -> x7, waiting for transfers between devices: 45.1 us -> 27.5 us  [around_z(): return lax.ppermute(value, 'blk', [(i, (i + 2) % 8) for i in range(8)])]
    ppermute x17 -> x18, waiting for transfers between devices: 39.5 us -> 22.3 us  [along_y(): return lax.ppermute(value, 'kv', [(i, i ^ 2) for i in range(4)])]
    ppermute x17 -> x18, waiting for transfers between devices: 35.5 us -> 23.3 us  [along_x(): return lax.ppermute(value, 'kv', [(i, i ^ 1) for i in range(4)])]
    pallas_call x4 -> x8, Pallas kernels: 62.9 us -> 57.9 us  [the longest x4 57.4 us: run_plane(): pl.pallas_call(functools.partial(plane_kernel, piece_rows, block_rows), i...]
    all_gather x0 -> x3, waiting for transfers between devices: none -> 5 us  [both_cores(): lax.all_gather(value, 'blk', axis_index_groups=pairs, axis=0, tiled=True)]
    ppermute x4 -> x0, starting transfers between devices: 4.48 us -> none  [the longest x1 3.96 us: along_diagonal(): return lax.ppermute(value, 'kv', [(i, i ^ 3) for i in range(4)])]
    ppermute x6 -> x7, starting transfers between devices: 1.81 us -> 6.01 us  [around_z(): return lax.ppermute(value, 'blk', [(i, (i + 2) % 8) for i in range(8)])]
    unnamed x44 -> x33, local copies, waits for them, and re-layouts: 7.1 us -> 4.16 us
  transfers between devices with their start and end apart: 44 -> 46, of which waited for: 21 -> 15; matrix products, arithmetic and copies ran while one was open for 2% -> 5% of each run, Pallas kernels for 26% -> 28%
where the time goes in v3:
time: 213 us; the launch traced here: 212 us
  waiting for transfers between devices  80.2 us (38%)
  Pallas kernels  59.1 us (28%)
  starting transfers between devices  43 us (20%)
  between operations  13.6 us (6%)
  local copies, waits for them, and re-layouts  7.64 us (4%)
  matrix products  5.6 us (3%)
  other arithmetic  3.28 us (2%)
    pallas_call x4, Pallas kernels, run_plane(): pl.pallas_call(functools.partial(plane_kernel, piece_rows, block_rows), i...  57.4 us
    ppermute x7, waiting for transfers between devices, around_z(): return lax.ppermute(value, 'blk', [(i, (i + 2) % 8) for i in range(8)])  27.5 us
    ppermute x18, waiting for transfers between devices, along_x(): return lax.ppermute(value, 'kv', [(i, i ^ 1) for i in range(4)])  23.3 us
    ppermute x18, waiting for transfers between devices, along_y(): return lax.ppermute(value, 'kv', [(i, i ^ 2) for i in range(4)])  22.3 us
    ppermute x18, starting transfers between devices, along_x(): return lax.ppermute(value, 'kv', [(i, i ^ 1) for i in range(4)])  19.1 us
    ppermute x18, starting transfers between devices, along_y(): return lax.ppermute(value, 'kv', [(i, i ^ 2) for i in range(4)])  17.8 us
    ppermute x7, starting transfers between devices, around_z(): return lax.ppermute(value, 'blk', [(i, (i + 2) % 8) for i in range(8)])  6.01 us
    all_gather x3, waiting for transfers between devices, both_cores(): lax.all_gather(value, 'blk', axis_index_groups=pairs, axis=0, tiled=True)  5 us
  transfers between devices with their start and end apart: 46, of which 15 were waited for; matrix products, arithmetic and copies ran while one was open for 5% of the time, Pallas kernels for 28%

profile of v3, /device:TPU:0, one launch (start us, length us, event | category | flops | bytes accessed | tf_op | source)
XLA Modules:
  0.0 212.4 jit_solution(7039061214839256143)
XLA Ops:
  6.5 0.7 all-gather.4.cloned.1.call-update
  7.4 0.7 all-gather.6.cloned.1.call-update
  8.1 0.7 all-gather.8.cloned.1.call-update
  9.4 0.7 prepare.2.refs_2_
  10.1 3.0 %collective-permute-start.2 = (bf16[96,2176]{1,0:T(8,128)(2,1)S(1)}, bf16[96,2176]{1,0:T(8,128)(2,1)S(1)}, u32[]{:S(2)}, u32[]{:S(2)}) collective-permute-start(bf16[96,2176]{1,0:T(8,128)(2,1)S(1)} %prepare.2.refs_2_), channel_id=1, source_target_pairs={{0,8},{8,0},{16,24},{24,16},{1,9},{9,1},{17,25},{25,17},{2,10},{10... | collective-permute-start | bytes 1253384 | tf_op jit(solution)/shard_map/ppermute | solution.py:252
  13.1 1.5 collective-permute-start.3
  14.6 1.6 collective-permute-start.4
  16.4 4.2 %fusion.28 = (f32[4,8]{1,0:T(4,128)S(1)}, f32[4,8,4096]{2,1,0:T(8,128)S(1)}) fusion(bf16[4,4096,1,128]{3,1,2,0:T(8,128)(2,1)} %param.15, bf16[1,4,8,128]{3,1,2,0:T(4,128)(2,1)S(1)} %bitcast.43, pred[4,4096]{1,0:T(4,128)(4,1)S(1)} %iota_compare_fusion), kind=kOutput, calls=%fused_computation.46 | convolution fusion | flops 33947616 | bytes 4743296 | tf_op jit(solution)/shard_map/rgd,rjd->rgj/dot_general | solution.py:26
  20.9 0.7 fusion.10
  21.6 1.1 copy-done.6
  22.7 0.7 fusion.20
  23.6 3.7 %collective-permute-done = f32[2,2048]{1,0:T(2,128)S(1)} collective-permute-done((f32[2,2048]{1,0:T(2,128)S(1)}, f32[2,2048]{1,0:T(2,128)S(1)}, u32[]{:S(2)}, u32[]{:S(2)}) %collective-permute-start) | collective-permute-done | bytes 16416 | tf_op jit(solution)/shard_map/ppermute | solution.py:252
  27.5 3.6 %collective-permute-done.1 = f32[1,2048]{1,0:T(1,128)S(1)} collective-permute-done((f32[1,2048]{1,0:T(1,128)S(1)}, f32[1,2048]{1,0:T(1,128)S(1)}, u32[]{:S(2)}, u32[]{:S(2)}) %collective-permute-start.1) | collective-permute-done | bytes 8224 | tf_op jit(solution)/shard_map/ppermute | solution.py:256
  31.8 1.6 collective-permute-start.7
  33.4 2.8 %collective-permute-done.5.refs_3_ = bf16[16,2176]{1,0:T(8,128)(2,1)S(1)} collective-permute-done((bf16[16,2176]{1,0:T(8,128)(2,1)S(1)}, bf16[16,2176]{1,0:T(8,128)(2,1)S(1)}, u32[]{:S(2)}, u32[]{:S(2)}) %collective-permute-start.5) | collective-permute-done | bytes 69664 | tf_op jit(solution)/shard_map/ppermute | solution.py:252
  36.2 1.8 collective-permute-done.7
  38.1 2.0 collective-permute-start.10
  40.0 2.7 %collective-permute-start.11 = (bf16[112,2176]{1,0:T(8,128)(2,1)S(1)}, bf16[112,2176]{1,0:T(8,128)(2,1)S(1)}, u32[]{:S(2)}, u32[]{:S(2)}) collective-permute-start(bf16[112,2176]{1,0:T(8,128)(2,1)S(1)} %constant_dynamic-update-slice_fusion.refs_1_), channel_id=1, source_target_pairs={{0,16},{8,24},{16,0},{24,8},{1,17},{9,25},{17,1},{25,9},{2,18},{10... | collective-permute-start | bytes 1462280 | tf_op jit(solution)/shard_map/ppermute | solution.py:256
  42.7 0.7 pad_maximum_fusion
  43.4 0.7 slice.69
  44.4 7.7 %collective-permute-done.9.refs_8_ = bf16[48,2176]{1,0:T(8,128)(2,1)S(1)} collective-permute-done((bf16[48,2176]{1,0:T(8,128)(2,1)}, bf16[48,2176]{1,0:T(8,128)(2,1)S(1)}, u32[]{:S(2)}, u32[]{:S(2)}) %collective-permute-start.9) | collective-permute-done | bytes 208928 | tf_op jit(solution)/shard_map/ppermute | solution.py:252
  52.1 0.7 copy-done.3
  52.7 3.8 %collective-permute-done.8.refs_7_ = bf16[64,2176]{1,0:T(8,128)(2,1)S(1)} collective-permute-done((bf16[64,2176]{1,0:T(8,128)(2,1)}, bf16[64,2176]{1,0:T(8,128)(2,1)S(1)}, u32[]{:S(2)}, u32[]{:S(2)}) %collective-permute-start.8) | collective-permute-done | bytes 278560 | tf_op jit(solution)/shard_map/ppermute | solution.py:256
  56.6 0.8 collective-permute-start.15
  57.4 1.7 collective-permute-start.16
  59.4 0.7 slice.71
  60.1 1.7 collective-permute-start.14
  61.8 0.7 slice.70
  62.5 5.0 %all-gather.8.cloned.1.call-done.refs_11_.refs_8_ = bf16[2,768,2048]{2,1,0:T(8,128)(2,1)} async-done(((bf16[1,768,2048]{2,1,0:T(8,128)(2,1)}), bf16[2,768,2048]{2,1,0:T(8,128)(2,1)}) %all-gather.8.cloned.1.call-update) | async-done | bytes 6291472 | tf_op jit(solution)/shard_map/all_gather | solution.py:265
  67.5 0.9 copy-done.4
  68.5 14.6 %plane.4 = (bf16[112,2048]{1,0:T(8,128)(2,1)S(1)}, bf16[112,2048]{1,0:T(8,128)(2,1)S(1)}, bf16[112,2048]{1,0:T(8,128)(2,1)S(1)}, bf16[64,2048]{1,0:T(8,128)(2,1)S(1)}, bf16[48,2048]{1,0:T(8,128)(2,1)S(1)}) custom-call(s32[3]{0:T(128)S(1)} %pad_add_fusion.refs_0_, bf16[16,2176]{1,0:T(8,128)(2,1)S(1)} %prepare.3.refs_1_, bf16[96,2176]{1,0:T(8,128)(2,1)S(1)} %prepare.2.refs_2_, ...), custom_call_target="tpu_custom_call" | custom-call | flops 8455716864 | bytes 25165824 | tf_op jit(solution)/shard_map/plane/pallas_call | solution.py:208
  83.2 1.8 collective-permute-start.20
  85.0 1.5 collective-permute-start.21
  86.5 0.6 collective-permute-start.18
  87.1 0.9 slice.73
  88.4 1.7 collective-permute-start.22
  90.1 1.0 copy-done.2
  91.1 14.5 %plane.5 = (bf16[112,2048]{1,0:T(8,128)(2,1)S(1)}, bf16[112,2048]{1,0:T(8,128)(2,1)S(1)}, bf16[112,2048]{1,0:T(8,128)(2,1)S(1)}, bf16[48,2048]{1,0:T(8,128)(2,1)S(1)}, bf16[64,2048]{1,0:T(8,128)(2,1)S(1)}) custom-call(s32[3]{0:T(128)S(1)} %pad_add_fusion.refs_0_, bf16[112,2176]{1,0:T(8,128)(2,1)S(1)} %copy-done.2, ...), custom_call_target="tpu_custom_call" | custom-call | flops 8455716864 | bytes 25165824 | tf_op jit(solution)/shard_map/plane/pallas_call | solution.py:208
  105.6 4.2 %collective-permute-done.22.passed_0_ref = bf16[64,2048]{1,0:T(8,128)(2,1)S(1)} collective-permute-done((bf16[64,2048]{1,0:T(8,128)(2,1)S(1)}, bf16[64,2048]{1,0:T(8,128)(2,1)S(1)}, u32[]{:S(2)}, u32[]{:S(2)}) %collective-permute-start.22) | collective-permute-done | bytes 262176 | tf_op jit(solution)/shard_map/ppermute | solution.py:256
  110.3 1.7 collective-permute-start.23
  112.0 1.5 collective-permute-start.27
  113.5 0.6 collective-permute-start.25
  114.4 13.9 %plane.6 = (bf16[112,2048]{1,0:T(8,128)(2,1)S(1)}, bf16[112,2048]{1,0:T(8,128)(2,1)S(1)}, bf16[112,2048]{1,0:T(8,128)(2,1)S(1)}, bf16[64,2048]{1,0:T(8,128)(2,1)S(1)}, bf16[48,2048]{1,0:T(8,128)(2,1)S(1)}) custom-call(s32[3]{0:T(128)S(1)} %pad_add_fusion.refs_0_, bf16[112,2176]{1,0:T(8,128)(2,1)} %collective-permute-done.12.refs_1_, ...), custom_call_target="tpu_custom_call" | custom-call | flops 8455716864 | bytes 25165824 | tf_op jit(solution)/shard_map/plane/pallas_call | solution.py:208
  128.5 1.7 collective-permute-start.28
  130.2 1.5 collective-permute-start.29
  131.7 0.6 collective-permute-start.30
  132.6 14.4 %plane.7 = (bf16[112,2048]{1,0:T(8,128)(2,1)S(1)}, bf16[112,2048]{1,0:T(8,128)(2,1)S(1)}, bf16[112,2048]{1,0:T(8,128)(2,1)S(1)}, bf16[48,2048]{1,0:T(8,128)(2,1)S(1)}, bf16[64,2048]{1,0:T(8,128)(2,1)S(1)}) custom-call(s32[3]{0:T(128)S(1)} %pad_add_fusion.refs_0_, bf16[112,2176]{1,0:T(8,128)(2,1)} %collective-permute-done.17.refs_1_, ...), custom_call_target="tpu_custom_call" | custom-call | flops 8455716864 | bytes 25165824 | tf_op jit(solution)/shard_map/plane/pallas_call | solution.py:208
  147.2 1.7 collective-permute-start.34
  148.9 1.5 collective-permute-start.35
  150.4 0.6 collective-permute-start.33
  151.3 10.6 %collective-permute-done.32.passed_0_ref = bf16[48,2048]{1,0:T(8,128)(2,1)S(1)} collective-permute-done((bf16[48,2048]{1,0:T(8,128)(2,1)S(1)}, bf16[48,2048]{1,0:T(8,128)(2,1)S(1)}, u32[]{:S(2)}, u32[]{:S(2)}) %collective-permute-start.32) | collective-permute-done | bytes 196640 | tf_op jit(solution)/shard_map/ppermute | solution.py:256
  161.9 1.4 collective-permute-done.33.passed_1_ref
  163.5 1.7 collective-permute-start.38
  165.2 1.5 collective-permute-start.39
  166.9 1.5 collective-permute-start.40
  168.5 0.6 collective-permute-start.36
  169.2 0.6 collective-permute-start.37
  169.7 7.0 %collective-permute-done.38 = bf16[112,2048]{1,0:T(8,128)(2,1)S(1)} collective-permute-done((bf16[112,2048]{1,0:T(8,128)(2,1)S(1)}, bf16[112,2048]{1,0:T(8,128)(2,1)S(1)}, u32[]{:S(2)}, u32[]{:S(2)}) %collective-permute-start.38) | collective-permute-done | bytes 458784 | tf_op jit(solution)/shard_map/ppermute | solution.py:252
  176.8 3.0 %collective-permute-done.40 = bf16[112,2048]{1,0:T(8,128)(2,1)S(1)} collective-permute-done((bf16[112,2048]{1,0:T(8,128)(2,1)S(1)}, bf16[112,2048]{1,0:T(8,128)(2,1)S(1)}, u32[]{:S(2)}, u32[]{:S(2)}) %collective-permute-start.40) | collective-permute-done | bytes 458784 | tf_op jit(solution)/shard_map/ppermute | solution.py:260
  180.1 1.0 collective-permute-start.41
  181.1 0.6 collective-permute-done.36
  181.7 12.4 %collective-permute-done.41 = bf16[112,2048]{1,0:T(8,128)(2,1)S(1)} collective-permute-done((bf16[112,2048]{1,0:T(8,128)(2,1)S(1)}, bf16[112,2048]{1,0:T(8,128)(2,1)S(1)}, u32[]{:S(2)}, u32[]{:S(2)}) %collective-permute-start.41) | collective-permute-done | bytes 458784 | tf_op jit(solution)/shard_map/ppermute | solution.py:260
  194.4 10.3 %collective-permute-done.42 = bf16[112,2048]{1,0:T(8,128)(2,1)S(1)} collective-permute-done((bf16[112,2048]{1,0:T(8,128)(2,1)S(1)}, bf16[112,2048]{1,0:T(8,128)(2,1)S(1)}, u32[]{:S(2)}, u32[]{:S(2)}) %collective-permute-start.42) | collective-permute-done | bytes 458784 | tf_op jit(solution)/shard_map/ppermute | solution.py:260
  204.7 1.2 fusion.13
  (108 shorter events, 6.0 us)
Async XLA Ops:
  6.5 2.3 %copy-start.7 = (bf16[1,111,2048]{2,1,0:T(8,128)(2,1)S(1)}, bf16[1,111,2048]{2,1,0:T(8,128)(2,1)}, u32[]{:S(2)}) copy-start(bf16[1,111,2048]{2,1,0:T(8,128)(2,1)} %param.21) | copy-start | bytes 1363972
  6.5 56.0 %all-gather.4.cloned.1.call-start = ((), (), s32[]{:S(2)}) async-start(), calls=%async_computation | async-start | bytes 9437184 | tf_op jit(solution)/shard_map/all_gather | solution.py:265
  7.3 1.7 copy-start.9
  7.3 1.9 copy-start.10
  7.3 2.1 copy-start
  7.3 8.9 %copy-start.14 = (s32[32]{0:T(128)S(1)}, s32[32]{0:T(128)}, u32[]{:S(2)}) copy-start(s32[32]{0:T(128)} %param.17) | copy-start | bytes 388
  7.3 9.1 %copy-start.11 = (bf16[4,1024]{1,0:T(4,128)(2,1)S(1)}, bf16[4,1024]{1,0:T(4,128)(2,1)}, u32[]{:S(2)}) copy-start(bf16[4,1024]{1,0:T(4,128)(2,1)} %param.14) | copy-start | bytes 24580
  7.3 55.2 %all-gather.6.cloned.1.call-start = ((), (), s32[]{:S(2)}) async-start(), calls=%async_computation.1 | async-start | bytes 9437184 | tf_op jit(solution)/shard_map/all_gather | solution.py:265
  8.1 59.5 %all-gather.8.cloned.1.call-start = ((), (), s32[]{:S(2)}) async-start(), calls=%async_computation.2 | async-start | bytes 9437184 | tf_op jit(solution)/shard_map/all_gather | solution.py:265
  8.8 11.8 %copy-start.13 = (f32[8]{0:T(128)S(1)}, f32[8]{0:T(128)}, u32[]{:S(2)}) copy-start(f32[8]{0:T(128)} %param.18) | copy-start | bytes 100
  10.1 21.1 %collective-permute-start.2 = (bf16[96,2176]{1,0:T(8,128)(2,1)S(1)}, bf16[96,2176]{1,0:T(8,128)(2,1)S(1)}, u32[]{:S(2)}, u32[]{:S(2)}) collective-permute-start(bf16[96,2176]{1,0:T(8,128)(2,1)S(1)} %prepare.2.refs_2_), channel_id=1, source_target_pairs={{0,8},{8,0},{16,24},{24,16},{1,9},{9,1},{17,25},{25,17},{2,10},{10... | collective-permute-start | bytes 1253384 | tf_op jit(solution)/shard_map/ppermute | solution.py:252
  13.1 18.1 %collective-permute-start.3 = (bf16[96,2176]{1,0:T(8,128)(2,1)S(1)}, bf16[96,2176]{1,0:T(8,128)(2,1)S(1)}, u32[]{:S(2)}, u32[]{:S(2)}) collective-permute-start(bf16[96,2176]{1,0:T(8,128)(2,1)S(1)} %prepare.2.refs_2_), channel_id=1, source_target_pairs={{0,16},{8,24},{16,0},{24,8},{1,17},{9,25},{17,1},{25,9},{2,18},{10... | collective-permute-start | bytes 1253384 | tf_op jit(solution)/shard_map/ppermute | solution.py:256
  14.6 16.6 %collective-permute-start.4 = (bf16[96,2176]{1,0:T(8,128)(2,1)S(1)}, bf16[96,2176]{1,0:T(8,128)(2,1)S(1)}, u32[]{:S(2)}, u32[]{:S(2)}) collective-permute-start(bf16[96,2176]{1,0:T(8,128)(2,1)S(1)} %prepare.2.refs_2_), channel_id=1, source_target_pairs={{0,2},{1,3},{2,4},{3,5},{4,6},{5,7},{6,0},{7,1},{8,10},{9,11},{10,... | collective-permute-start | bytes 1253384 | tf_op jit(solution)/shard_map/ppermute | solution.py:260
  16.2 4.7 %copy-start.5 = (bf16[4,4096,1,128]{3,1,2,0:T(8,128)(2,1)S(1)}, bf16[4,4096,1,128]{3,1,2,0:T(8,128)(2,1)}, u32[]{:S(2)}) copy-start(bf16[4,4096,1,128]{3,1,2,0:T(8,128)(2,1)} %param.16) | copy-start | bytes 12582916
  16.4 6.4 %copy-start.6 = (bf16[1024,2048]{1,0:T(8,128)(2,1)S(1)}, bf16[1024,2048]{1,0:T(8,128)(2,1)}, u32[]{:S(2)}) copy-start(bf16[1024,2048]{1,0:T(8,128)(2,1)} %param.19) | copy-start | bytes 12582916
  20.9 10.2 %copy-start.12 = (bf16[1,2048]{1,0:T(2,128)(2,1)S(1)}, bf16[1,2048]{1,0:T(2,128)(2,1)}, u32[]{:S(2)}) copy-start(bf16[1,2048]{1,0:T(2,128)(2,1)} %param.20) | copy-start | bytes 12292
  23.5 3.8 %collective-permute-start = (f32[2,2048]{1,0:T(2,128)S(1)}, f32[2,2048]{1,0:T(2,128)S(1)}, u32[]{:S(2)}, u32[]{:S(2)}) collective-permute-start(f32[2,2048]{1,0:T(2,128)S(1)} %pad_maximum_fusion.2), channel_id=1, source_target_pairs={{0,8},{8,0},{16,24},{24,16},{1,9},{9,1},{17,25},{25,17},{2,10},{10... | collective-permute-start | bytes 49160 | tf_op jit(solution)/shard_map/ppermute | solution.py:252
  27.3 3.8 %collective-permute-start.1 = (f32[1,2048]{1,0:T(1,128)S(1)}, f32[1,2048]{1,0:T(1,128)S(1)}, u32[]{:S(2)}, u32[]{:S(2)}) collective-permute-start(f32[1,2048]{1,0:T(1,128)S(1)} %slice.77), channel_id=1, source_target_pairs={{0,16},{8,24},{16,0},{24,8},{1,17},{9,25},{17,1},{25,9},{2,18},{10... | collective-permute-start | bytes 24584 | tf_op jit(solution)/shard_map/ppermute | solution.py:256
  31.7 4.5 %collective-permute-start.5 = (bf16[16,2176]{1,0:T(8,128)(2,1)S(1)}, bf16[16,2176]{1,0:T(8,128)(2,1)S(1)}, u32[]{:S(2)}, u32[]{:S(2)}) collective-permute-start(bf16[16,2176]{1,0:T(8,128)(2,1)S(1)} %prepare.3.refs_1_), channel_id=1, source_target_pairs={{0,8},{8,0},{16,24},{24,16},{1,9},{9,1},{17,25},{25,17},{2,10},{10... | collective-permute-start | bytes 208904 | tf_op jit(solution)/shard_map/ppermute | solution.py:252
  31.8 4.4 %collective-permute-start.6 = (bf16[16,2176]{1,0:T(8,128)(2,1)S(1)}, bf16[16,2176]{1,0:T(8,128)(2,1)S(1)}, u32[]{:S(2)}, u32[]{:S(2)}) collective-permute-start(bf16[16,2176]{1,0:T(8,128)(2,1)S(1)} %prepare.3.refs_1_), channel_id=1, source_target_pairs={{0,16},{8,24},{16,0},{24,8},{1,17},{9,25},{17,1},{25,9},{2,18},{10... | collective-permute-start | bytes 208904 | tf_op jit(solution)/shard_map/ppermute | solution.py:256
  31.8 6.2 %collective-permute-start.7 = (bf16[16,2176]{1,0:T(8,128)(2,1)S(1)}, bf16[16,2176]{1,0:T(8,128)(2,1)S(1)}, u32[]{:S(2)}, u32[]{:S(2)}) collective-permute-start(bf16[16,2176]{1,0:T(8,128)(2,1)S(1)} %prepare.3.refs_1_), channel_id=1, source_target_pairs={{0,2},{1,3},{2,4},{3,5},{4,6},{5,7},{6,0},{7,1},{8,10},{9,11},{10,... | collective-permute-start | bytes 208904 | tf_op jit(solution)/shard_map/ppermute | solution.py:260
  38.1 18.5 %copy-start.1 = (bf16[112,2176]{1,0:T(8,128)(2,1)}, bf16[112,2176]{1,0:T(8,128)(2,1)S(1)}, u32[]{:S(2)}) copy-start(bf16[112,2176]{1,0:T(8,128)(2,1)S(1)} %constant_dynamic-update-slice_fusion.refs_1_) | copy-start | bytes 1462276
  38.1 18.5 %collective-permute-start.10 = (bf16[112,2176]{1,0:T(8,128)(2,1)S(1)}, bf16[112,2176]{1,0:T(8,128)(2,1)S(1)}, u32[]{:S(2)}, u32[]{:S(2)}) collective-permute-start(bf16[112,2176]{1,0:T(8,128)(2,1)S(1)} %constant_dynamic-update-slice_fusion.refs_1_), channel_id=1, source_target_pairs={{0,8},{8,0},{16,24},{24,16},{1,9},{9,1},{17,25},{25,17},{2,10},{10... | collective-permute-start | bytes 1462280 | tf_op jit(solution)/shard_map/ppermute | solution.py:252
  40.0 16.6 %collective-permute-start.11 = (bf16[112,2176]{1,0:T(8,128)(2,1)S(1)}, bf16[112,2176]{1,0:T(8,128)(2,1)S(1)}, u32[]{:S(2)}, u32[]{:S(2)}) collective-permute-start(bf16[112,2176]{1,0:T(8,128)(2,1)S(1)} %constant_dynamic-update-slice_fusion.refs_1_), channel_id=1, source_target_pairs={{0,16},{8,24},{16,0},{24,8},{1,17},{9,25},{17,1},{25,9},{2,18},{10... | collective-permute-start | bytes 1462280 | tf_op jit(solution)/shard_map/ppermute | solution.py:256
  42.7 13.9 %collective-permute-start.12 = (bf16[112,2176]{1,0:T(8,128)(2,1)S(1)}, bf16[112,2176]{1,0:T(8,128)(2,1)}, u32[]{:S(2)}, u32[]{:S(2)}) collective-permute-start(bf16[112,2176]{1,0:T(8,128)(2,1)S(1)} %constant_dynamic-update-slice_fusion.refs_1_), channel_id=1, source_target_pairs={{0,2},{1,3},{2,4},{3,5},{4,6},{5,7},{6,0},{7,1},{8,10},{9,11},{10,... | collective-permute-start | bytes 1462280 | tf_op jit(solution)/shard_map/ppermute | solution.py:260
  43.4 13.2 %collective-permute-start.8 = (bf16[64,2176]{1,0:T(8,128)(2,1)}, bf16[64,2176]{1,0:T(8,128)(2,1)S(1)}, u32[]{:S(2)}, u32[]{:S(2)}) collective-permute-start(bf16[64,2176]{1,0:T(8,128)(2,1)} %pad_maximum_fusion), channel_id=1, source_target_pairs={{0,16},{8,24},{16,0},{24,8},{1,17},{9,25},{17,1},{25,9},{2,18},{10... | collective-permute-start | bytes 835592 | tf_op jit(solution)/shard_map/ppermute | solution.py:256
  44.1 7.9 %collective-permute-start.9 = (bf16[48,2176]{1,0:T(8,128)(2,1)}, bf16[48,2176]{1,0:T(8,128)(2,1)S(1)}, u32[]{:S(2)}, u32[]{:S(2)}) collective-permute-start(bf16[48,2176]{1,0:T(8,128)(2,1)} %slice.69), channel_id=1, source_target_pairs={{0,8},{8,0},{16,24},{24,16},{1,9},{9,1},{17,25},{25,17},{2,10},{10... | collective-permute-start | bytes 626696 | tf_op jit(solution)/shard_map/ppermute | solution.py:252
  52.1 0.7 copy-start.3
  56.6 26.5 %collective-permute-start.15 = (bf16[112,2176]{1,0:T(8,128)(2,1)}, bf16[112,2176]{1,0:T(8,128)(2,1)S(1)}, u32[]{:S(2)}, u32[]{:S(2)}) collective-permute-start(bf16[112,2176]{1,0:T(8,128)(2,1)} %collective-permute-done.12.refs_1_), channel_id=1, source_target_pairs={{0,8},{8,0},{16,24},{24,16},{1,9},{9,1},{17,25},{25,17},{2,10},{10... | collective-permute-start | bytes 1462280 | tf_op jit(solution)/shard_map/ppermute | solution.py:252
  57.4 25.7 %collective-permute-start.16 = (bf16[112,2176]{1,0:T(8,128)(2,1)}, bf16[112,2176]{1,0:T(8,128)(2,1)}, u32[]{:S(2)}, u32[]{:S(2)}) collective-permute-start(bf16[112,2176]{1,0:T(8,128)(2,1)} %collective-permute-done.12.refs_1_), channel_id=1, source_target_pairs={{0,16},{8,24},{16,0},{24,8},{1,17},{9,25},{17,1},{25,9},{2,18},{10... | collective-permute-start | bytes 1462280 | tf_op jit(solution)/shard_map/ppermute | solution.py:256
  59.1 24.0 %collective-permute-start.17 = (bf16[112,2176]{1,0:T(8,128)(2,1)}, bf16[112,2176]{1,0:T(8,128)(2,1)}, u32[]{:S(2)}, u32[]{:S(2)}) collective-permute-start(bf16[112,2176]{1,0:T(8,128)(2,1)} %collective-permute-done.12.refs_1_), channel_id=1, source_target_pairs={{0,2},{1,3},{2,4},{3,5},{4,6},{5,7},{6,0},{7,1},{8,10},{9,11},{10,... | collective-permute-start | bytes 1462280 | tf_op jit(solution)/shard_map/ppermute | solution.py:260
  60.1 23.0 %collective-permute-start.14 = (bf16[64,2176]{1,0:T(8,128)(2,1)}, bf16[64,2176]{1,0:T(8,128)(2,1)S(1)}, u32[]{:S(2)}, u32[]{:S(2)}) collective-permute-start(bf16[64,2176]{1,0:T(8,128)(2,1)} %slice.71), channel_id=1, source_target_pairs={{0,8},{8,0},{16,24},{24,16},{1,9},{9,1},{17,25},{25,17},{2,10},{10... | collective-permute-start | bytes 835592 | tf_op jit(solution)/shard_map/ppermute | solution.py:252
  62.5 20.6 %collective-permute-start.13 = (bf16[48,2176]{1,0:T(8,128)(2,1)}, bf16[48,2176]{1,0:T(8,128)(2,1)}, u32[]{:S(2)}, u32[]{:S(2)}) collective-permute-start(bf16[48,2176]{1,0:T(8,128)(2,1)} %slice.70), channel_id=1, source_target_pairs={{0,16},{8,24},{16,0},{24,8},{1,17},{9,25},{17,1},{25,9},{2,18},{10... | collective-permute-start | bytes 626696 | tf_op jit(solution)/shard_map/ppermute | solution.py:256
  67.5 0.9 copy-start.4
  83.2 26.7 %collective-permute-start.20 = (bf16[112,2176]{1,0:T(8,128)(2,1)}, bf16[112,2176]{1,0:T(8,128)(2,1)S(1)}, u32[]{:S(2)}, u32[]{:S(2)}) collective-permute-start(bf16[112,2176]{1,0:T(8,128)(2,1)} %collective-permute-done.17.refs_1_), channel_id=1, source_target_pairs={{0,8},{8,0},{16,24},{24,16},{1,9},{9,1},{17,25},{25,17},{2,10},{10... | collective-permute-start | bytes 1462280 | tf_op jit(solution)/shard_map/ppermute | solution.py:252
  85.0 24.9 %collective-permute-start.21 = (bf16[112,2176]{1,0:T(8,128)(2,1)}, bf16[112,2176]{1,0:T(8,128)(2,1)S(1)}, u32[]{:S(2)}, u32[]{:S(2)}) collective-permute-start(bf16[112,2176]{1,0:T(8,128)(2,1)} %collective-permute-done.17.refs_1_), channel_id=1, source_target_pairs={{0,16},{8,24},{16,0},{24,8},{1,17},{9,25},{17,1},{25,9},{2,18},{10... | collective-permute-start | bytes 1462280 | tf_op jit(solution)/shard_map/ppermute | solution.py:256
  86.5 23.3 %collective-permute-start.18 = (bf16[64,2176]{1,0:T(8,128)(2,1)S(1)}, bf16[64,2176]{1,0:T(8,128)(2,1)S(1)}, u32[]{:S(2)}, u32[]{:S(2)}) collective-permute-start(bf16[64,2176]{1,0:T(8,128)(2,1)S(1)} %slice.72), channel_id=1, source_target_pairs={{0,16},{8,24},{16,0},{24,8},{1,17},{9,25},{17,1},{25,9},{2,18},{10... | collective-permute-start | bytes 835592 | tf_op jit(solution)/shard_map/ppermute | solution.py:256
  88.0 17.6 %collective-permute-start.19 = (bf16[48,2176]{1,0:T(8,128)(2,1)S(1)}, bf16[48,2176]{1,0:T(8,128)(2,1)S(1)}, u32[]{:S(2)}, u32[]{:S(2)}) collective-permute-start(bf16[48,2176]{1,0:T(8,128)(2,1)S(1)} %slice.73), channel_id=1, source_target_pairs={{0,8},{8,0},{16,24},{24,16},{1,9},{9,1},{17,25},{25,17},{2,10},{10... | collective-permute-start | bytes 626696 | tf_op jit(solution)/shard_map/ppermute | solution.py:252
  88.4 21.4 %collective-permute-start.22 = (bf16[64,2048]{1,0:T(8,128)(2,1)S(1)}, bf16[64,2048]{1,0:T(8,128)(2,1)S(1)}, u32[]{:S(2)}, u32[]{:S(2)}) collective-permute-start(bf16[64,2048]{1,0:T(8,128)(2,1)S(1)} %get-tuple-element.135), channel_id=1, source_target_pairs={{0,16},{8,24},{16,0},{24,8},{1,17},{9,25},{17,1},{25,9},{2,18},{10... | collective-permute-start | bytes 786440 | tf_op jit(solution)/shard_map/ppermute | solution.py:256
  90.1 1.0 copy-start.2
  109.9 18.5 %collective-permute-start.24 = (bf16[64,2176]{1,0:T(8,128)(2,1)S(1)}, bf16[64,2176]{1,0:T(8,128)(2,1)S(1)}, u32[]{:S(2)}, u32[]{:S(2)}) collective-permute-start(bf16[64,2176]{1,0:T(8,128)(2,1)S(1)} %slice.75), channel_id=1, source_target_pairs={{0,8},{8,0},{16,24},{24,16},{1,9},{9,1},{17,25},{25,17},{2,10},{10... | collective-permute-start | bytes 835592 | tf_op jit(solution)/shard_map/ppermute | solution.py:252
  110.3 18.0 %collective-permute-start.23 = (bf16[48,2176]{1,0:T(8,128)(2,1)S(1)}, bf16[48,2176]{1,0:T(8,128)(2,1)S(1)}, u32[]{:S(2)}, u32[]{:S(2)}) collective-permute-start(bf16[48,2176]{1,0:T(8,128)(2,1)S(1)} %slice.74), channel_id=1, source_target_pairs={{0,16},{8,24},{16,0},{24,8},{1,17},{9,25},{17,1},{25,9},{2,18},{10... | collective-permute-start | bytes 626696 | tf_op jit(solution)/shard_map/ppermute | solution.py:256
  112.0 16.3 %collective-permute-start.27 = (bf16[64,2048]{1,0:T(8,128)(2,1)S(1)}, bf16[64,2048]{1,0:T(8,128)(2,1)S(1)}, u32[]{:S(2)}, u32[]{:S(2)}) collective-permute-start(bf16[64,2048]{1,0:T(8,128)(2,1)S(1)} %get-tuple-element.152), channel_id=1, source_target_pairs={{0,8},{8,0},{16,24},{24,16},{1,9},{9,1},{17,25},{25,17},{2,10},{10... | collective-permute-start | bytes 786440 | tf_op jit(solution)/shard_map/ppermute | solution.py:252
  113.5 14.8 %collective-permute-start.25 = (bf16[48,2048]{1,0:T(8,128)(2,1)S(1)}, bf16[48,2048]{1,0:T(8,128)(2,1)S(1)}, u32[]{:S(2)}, u32[]{:S(2)}) collective-permute-start(bf16[48,2048]{1,0:T(8,128)(2,1)S(1)} %get-tuple-element.150), channel_id=1, source_target_pairs={{0,8},{8,0},{16,24},{24,16},{1,9},{9,1},{17,25},{25,17},{2,10},{10... | collective-permute-start | bytes 589832 | tf_op jit(solution)/shard_map/ppermute | solution.py:252
  114.1 14.3 %collective-permute-start.26 = (bf16[48,2048]{1,0:T(8,128)(2,1)S(1)}, bf16[48,2048]{1,0:T(8,128)(2,1)S(1)}, u32[]{:S(2)}, u32[]{:S(2)}) collective-permute-start(bf16[48,2048]{1,0:T(8,128)(2,1)S(1)} %get-tuple-element.151), channel_id=1, source_target_pairs={{0,16},{8,24},{16,0},{24,8},{1,17},{9,25},{17,1},{25,9},{2,18},{10... | collective-permute-start | bytes 589832 | tf_op jit(solution)/shard_map/ppermute | solution.py:256
  128.5 18.5 %collective-permute-start.28 = (bf16[112,2048]{1,0:T(8,128)(2,1)S(1)}, bf16[112,2048]{1,0:T(8,128)(2,1)S(1)}, u32[]{:S(2)}, u32[]{:S(2)}) collective-permute-start(bf16[112,2048]{1,0:T(8,128)(2,1)S(1)} %get-tuple-element.171), channel_id=1, source_target_pairs={{0,8},{8,0},{16,24},{24,16},{1,9},{9,1},{17,25},{25,17},{2,10},{10... | collective-permute-start | bytes 1376264 | tf_op jit(solution)/shard_map/ppermute | solution.py:252
  130.2 16.8 %collective-permute-start.29 = (bf16[112,2048]{1,0:T(8,128)(2,1)S(1)}, bf16[112,2048]{1,0:T(8,128)(2,1)S(1)}, u32[]{:S(2)}, u32[]{:S(2)}) collective-permute-start(bf16[112,2048]{1,0:T(8,128)(2,1)S(1)} %get-tuple-element.172), channel_id=1, source_target_pairs={{0,16},{8,24},{16,0},{24,8},{1,17},{9,25},{17,1},{25,9},{2,18},{10... | collective-permute-start | bytes 1376264 | tf_op jit(solution)/shard_map/ppermute | solution.py:256
  131.7 15.3 %collective-permute-start.30 = (bf16[64,2048]{1,0:T(8,128)(2,1)S(1)}, bf16[64,2048]{1,0:T(8,128)(2,1)S(1)}, u32[]{:S(2)}, u32[]{:S(2)}) collective-permute-start(bf16[64,2048]{1,0:T(8,128)(2,1)S(1)} %get-tuple-element.173), channel_id=1, source_target_pairs={{0,16},{8,24},{16,0},{24,8},{1,17},{9,25},{17,1},{25,9},{2,18},{10... | collective-permute-start | bytes 786440 | tf_op jit(solution)/shard_map/ppermute | solution.py:256
  132.3 14.8 %collective-permute-start.31 = (bf16[48,2048]{1,0:T(8,128)(2,1)S(1)}, bf16[48,2048]{1,0:T(8,128)(2,1)S(1)}, u32[]{:S(2)}, u32[]{:S(2)}) collective-permute-start(bf16[48,2048]{1,0:T(8,128)(2,1)S(1)} %get-tuple-element.174), channel_id=1, source_target_pairs={{0,8},{8,0},{16,24},{24,16},{1,9},{9,1},{17,25},{25,17},{2,10},{10... | collective-permute-start | bytes 589832 | tf_op jit(solution)/shard_map/ppermute | solution.py:252
  147.2 16.2 %collective-permute-start.34 = (bf16[112,2048]{1,0:T(8,128)(2,1)S(1)}, bf16[112,2048]{1,0:T(8,128)(2,1)S(1)}, u32[]{:S(2)}, u32[]{:S(2)}) collective-permute-start(bf16[112,2048]{1,0:T(8,128)(2,1)S(1)} %get-tuple-element.196), channel_id=1, source_target_pairs={{0,8},{8,0},{16,24},{24,16},{1,9},{9,1},{17,25},{25,17},{2,10},{10... | collective-permute-start | bytes 1376264 | tf_op jit(solution)/shard_map/ppermute | solution.py:252
  148.9 14.4 %collective-permute-start.35 = (bf16[112,2048]{1,0:T(8,128)(2,1)S(1)}, bf16[112,2048]{1,0:T(8,128)(2,1)S(1)}, u32[]{:S(2)}, u32[]{:S(2)}) collective-permute-start(bf16[112,2048]{1,0:T(8,128)(2,1)S(1)} %get-tuple-element.197), channel_id=1, source_target_pairs={{0,16},{8,24},{16,0},{24,8},{1,17},{9,25},{17,1},{25,9},{2,18},{10... | collective-permute-start | bytes 1376264 | tf_op jit(solution)/shard_map/ppermute | solution.py:256
  150.4 13.0 %collective-permute-start.33 = (bf16[64,2048]{1,0:T(8,128)(2,1)S(1)}, bf16[64,2048]{1,0:T(8,128)(2,1)S(1)}, u32[]{:S(2)}, u32[]{:S(2)}) collective-permute-start(bf16[64,2048]{1,0:T(8,128)(2,1)S(1)} %get-tuple-element.191), channel_id=1, source_target_pairs={{0,8},{8,0},{16,24},{24,16},{1,9},{9,1},{17,25},{25,17},{2,10},{10... | collective-permute-start | bytes 786440 | tf_op jit(solution)/shard_map/ppermute | solution.py:252
  150.9 11.0 %collective-permute-start.32 = (bf16[48,2048]{1,0:T(8,128)(2,1)S(1)}, bf16[48,2048]{1,0:T(8,128)(2,1)S(1)}, u32[]{:S(2)}, u32[]{:S(2)}) collective-permute-start(bf16[48,2048]{1,0:T(8,128)(2,1)S(1)} %get-tuple-element.190), channel_id=1, source_target_pairs={{0,16},{8,24},{16,0},{24,8},{1,17},{9,25},{17,1},{25,9},{2,18},{10... | collective-permute-start | bytes 589832 | tf_op jit(solution)/shard_map/ppermute | solution.py:256
  163.5 41.2 %copy-start.8 = (bf16[1,111,2048]{2,1,0:T(8,128)(2,1)S(1)}, bf16[1,111,2048]{2,1,0:T(8,128)(2,1)}, u32[]{:S(2)}) copy-start(bf16[1,111,2048]{2,1,0:T(8,128)(2,1)} %param.21) | copy-start | bytes 1363972
  163.5 13.3 %collective-permute-start.38 = (bf16[112,2048]{1,0:T(8,128)(2,1)S(1)}, bf16[112,2048]{1,0:T(8,128)(2,1)S(1)}, u32[]{:S(2)}, u32[]{:S(2)}) collective-permute-start(bf16[112,2048]{1,0:T(8,128)(2,1)S(1)} %get-tuple-element.216), channel_id=1, source_target_pairs={{0,8},{8,0},{16,24},{24,16},{1,9},{9,1},{17,25},{25,17},{2,10},{10... | collective-permute-start | bytes 1376264 | tf_op jit(solution)/shard_map/ppermute | solution.py:252
  165.2 11.5 %collective-permute-start.39 = (bf16[112,2048]{1,0:T(8,128)(2,1)S(1)}, bf16[112,2048]{1,0:T(8,128)(2,1)S(1)}, u32[]{:S(2)}, u32[]{:S(2)}) collective-permute-start(bf16[112,2048]{1,0:T(8,128)(2,1)S(1)} %get-tuple-element.217), channel_id=1, source_target_pairs={{0,16},{8,24},{16,0},{24,8},{1,17},{9,25},{17,1},{25,9},{2,18},{10... | collective-permute-start | bytes 1376264 | tf_op jit(solution)/shard_map/ppermute | solution.py:256
  166.9 12.9 %collective-permute-start.40 = (bf16[112,2048]{1,0:T(8,128)(2,1)S(1)}, bf16[112,2048]{1,0:T(8,128)(2,1)S(1)}, u32[]{:S(2)}, u32[]{:S(2)}) collective-permute-start(bf16[112,2048]{1,0:T(8,128)(2,1)S(1)} %add_convert_fusion.3), channel_id=1, source_target_pairs={{0,2},{1,3},{2,4},{3,5},{4,6},{5,7},{6,0},{7,1},{8,10},{9,11},{10,... | collective-permute-start | bytes 1376264 | tf_op jit(solution)/shard_map/ppermute | solution.py:260
  168.5 13.1 %collective-permute-start.36 = (bf16[112,2048]{1,0:T(8,128)(2,1)S(1)}, bf16[112,2048]{1,0:T(8,128)(2,1)S(1)}, u32[]{:S(2)}, u32[]{:S(2)}) collective-permute-start(bf16[112,2048]{1,0:T(8,128)(2,1)S(1)} %get-tuple-element.209), channel_id=1, source_target_pairs={{0,8},{8,0},{16,24},{24,16},{1,9},{9,1},{17,25},{25,17},{2,10},{10... | collective-permute-start | bytes 1376264 | tf_op jit(solution)/shard_map/ppermute | solution.py:252
  169.2 12.5 %collective-permute-start.37 = (bf16[112,2048]{1,0:T(8,128)(2,1)S(1)}, bf16[112,2048]{1,0:T(8,128)(2,1)S(1)}, u32[]{:S(2)}, u32[]{:S(2)}) collective-permute-start(bf16[112,2048]{1,0:T(8,128)(2,1)S(1)} %get-tuple-element.210), channel_id=1, source_target_pairs={{0,16},{8,24},{16,0},{24,8},{1,17},{9,25},{17,1},{25,9},{2,18},{10... | collective-permute-start | bytes 1376264 | tf_op jit(solution)/shard_map/ppermute | solution.py:256
  180.1 14.0 %collective-permute-start.41 = (bf16[112,2048]{1,0:T(8,128)(2,1)S(1)}, bf16[112,2048]{1,0:T(8,128)(2,1)S(1)}, u32[]{:S(2)}, u32[]{:S(2)}) collective-permute-start(bf16[112,2048]{1,0:T(8,128)(2,1)S(1)} %add_convert_fusion.2), channel_id=1, source_target_pairs={{0,2},{1,3},{2,4},{3,5},{4,6},{5,7},{6,0},{7,1},{8,10},{9,11},{10,... | collective-permute-start | bytes 1376264 | tf_op jit(solution)/shard_map/ppermute | solution.py:260
  194.4 10.3 %collective-permute-start.42 = (bf16[112,2048]{1,0:T(8,128)(2,1)S(1)}, bf16[112,2048]{1,0:T(8,128)(2,1)S(1)}, u32[]{:S(2)}, u32[]{:S(2)}) collective-permute-start(bf16[112,2048]{1,0:T(8,128)(2,1)S(1)} %add_convert_fusion.1), channel_id=1, source_target_pairs={{0,2},{1,3},{2,4},{3,5},{4,6},{5,7},{6,0},{7,1},{8,10},{9,11},{10,... | collective-permute-start | bytes 1376264 | tf_op jit(solution)/shard_map/ppermute | solution.py:260
Sparse Core Ops, SparseCore 0:
  8.9 19.4 all-gather.3
  29.9 18.0 all-gather.5
  49.6 17.9 all-gather.7

commit v4 on v1

--- a/solution.py
+++ b/solution.py
@@ -1,3 +1,4 @@
+import functools
 import math
 
 import jax
@@ -9,6 +10,7 @@
 
 NEG_FILL = -1e30
 EPSILON = 1e-06
+NOT_CHOSEN = -256.0
 AXES = ("blk", "kv")
 
 
@@ -41,7 +43,7 @@
     )
 
 
-def prepare_kernel(hidden_ref, gain_ref, router_ref, routes_ref, out_ref):
+def prepare_kernel(ranking, hidden_ref, gain_ref, router_ref, routes_ref, out_ref):
     width = hidden_ref.shape[1]
     experts = router_ref.shape[1]
     hidden = hidden_ref[...].astype(jnp.float32)
@@ -58,19 +60,30 @@
     raised = jnp.where(chosen, jnp.exp(jnp.minimum(logits - top, 0.0)), 0.0)
     gates = raised / jnp.sum(raised, axis=1, keepdims=True)
     high = gates.astype(jnp.bfloat16).astype(jnp.float32)
-    low = gates - high
-    rest = out_ref.shape[1] - width - 2 * experts
-    parts = [high, low]
+    parts = [high, gates - high]
+    if ranking == "block":
+        rows = logits.shape[0]
+        row = lax.broadcasted_iota(jnp.int32, (rows, rows), 0)
+        earlier = lax.broadcasted_iota(jnp.int32, (rows, rows), 1) < row
+        ranks = jnp.dot(
+            jnp.where(earlier, 1.0, 0.0).astype(jnp.bfloat16),
+            jnp.where(chosen, 1.0, 0.0).astype(jnp.bfloat16),
+            preferred_element_type=jnp.float32,
+        )
+        parts.append(jnp.where(chosen, ranks, NOT_CHOSEN))
+    elif ranking == "first":
+        parts.append(jnp.where(chosen, 0.0, NOT_CHOSEN))
+    rest = out_ref.shape[1] - width - len(parts) * experts
     if rest:
         parts.append(jnp.zeros((high.shape[0], rest), jnp.float32))
     out_ref[:, width:] = jnp.concatenate(parts, axis=1).astype(jnp.bfloat16)
 
 
-def prepare(hidden, norm_gain, router, routes):
+def prepare(hidden, norm_gain, router, routes, ranking=None):
     rows, width = hidden.shape
-    extra = -(-2 * router.shape[1] // 128) * 128
+    extra = -(-(3 if ranking else 2) * router.shape[1] // 128) * 128
     return pl.pallas_call(
-        prepare_kernel,
+        functools.partial(prepare_kernel, ranking),
         out_shape=jax.ShapeDtypeStruct((rows, width + extra), jnp.bfloat16),
         compiler_params=pltpu.CompilerParams(vmem_limit_bytes=32 << 20),
         name="prepare",
@@ -117,12 +130,359 @@
     )(expert, rows, gate_weights, up_weights, down_weights)
 
 
+def plane_kernel(cap, piece_rows, block_rows, *refs):
+    refs = list(refs)
+    ids_ref = refs.pop(0)
+    decode_ref = refs.pop(0)
+    sources = [refs.pop(0) for _ in piece_rows]
+    weight_refs = [refs.pop(0) for _ in range(6)]
+    targets = [refs.pop(0) for _ in block_rows]
+    decodes, rows, weights, downs, slots, inner, results, spread, sums, row_sem, weight_sem, out_sem = refs
+    width = sums.shape[1]
+    tokens = block_rows[0]
+    pair_rows = 2 * tokens
+    pair_slots = 2 * cap
+    row_copies = [pltpu.make_async_copy(decode_ref, decodes, row_sem.at[len(sources)])]
+    at = 0
+    for i, (ref, count) in enumerate(zip(sources, piece_rows)):
+        copy = pltpu.make_async_copy(ref, rows.at[pl.ds(at, count)], row_sem.at[i])
+        row_copies.append(copy)
+        at += count
+    up_copies = [
+        pltpu.make_async_copy(weight_refs[3 * e + i], weights.at[2 * e + i], weight_sem.at[2 * e + i])
+        for e in range(2)
+        for i in range(2)
+    ]
+    down_copies = [
+        pltpu.make_async_copy(weight_refs[3 * e + 2], downs.at[e], weight_sem.at[4 + e])
+        for e in range(2)
+    ]
+    for copy in row_copies + up_copies + down_copies:
+        copy.start()
+    for copy in row_copies:
+        copy.wait()
+    few = decodes.shape[0]
+    is_first = lax.broadcasted_iota(jnp.int32, (few, 1), 0) == 0
+    for j in range(4):
+        part = pl.ds(j * tokens, few)
+        decode_row = decodes[...].astype(jnp.float32)[j : j + 1]
+        kept = rows[part, :].astype(jnp.float32)
+        rows[part, :] = jnp.where(is_first, decode_row, kept).astype(jnp.bfloat16)
+
+    experts = ids_ref[2]
+    extra = rows.shape[1] - width
+    lanes = lax.broadcasted_iota(jnp.int32, (8, extra), 1)
+    line = lax.broadcasted_iota(jnp.int32, (8, extra), 0)
+    wanted = ((line == 0) & (lanes == ids_ref[0] + 2 * experts)) | (
+        (line == 1) & (lanes == ids_ref[1] + 2 * experts)
+    )
+    wanted = jnp.where(wanted, 1.0, 0.0).astype(jnp.bfloat16)
+    for p in range(2):
+        part = pl.ds(p * pair_rows, pair_rows)
+        tail = rows[part, width:]
+        ranks = lax.dot_general(
+            wanted, tail, (((1,), (1,)), ((), ())), preferred_element_type=jnp.float32
+        )
+        second = lax.broadcasted_iota(jnp.int32, (1, pair_rows), 1) >= tokens
+        shift = jnp.where(second, float(cap), 0.0)
+        slot = lax.broadcasted_iota(jnp.int32, (2 * pair_slots, pair_rows), 0).astype(jnp.float32)
+        taken = (slot == ranks[0:1] + shift) | (slot == ranks[1:2] + shift + float(pair_slots))
+        taken = jnp.where(taken, 1.0, 0.0).astype(jnp.bfloat16)
+        picked = jnp.dot(taken, rows[part, :], preferred_element_type=jnp.float32)
+        picked = picked.astype(jnp.bfloat16)
+        for e in range(2):
+            slots[e, pl.ds(p * pair_slots, pair_slots), :] = picked[e * pair_slots : (e + 1) * pair_slots]
+        tail = tail.astype(jnp.float32)
+        lane = lax.broadcasted_iota(jnp.int32, tail.shape, 1)
+        second = lax.broadcasted_iota(jnp.int32, (pair_rows, 1), 0) >= tokens
+        shift = jnp.where(second, float(cap), 0.0)
+        slot = lax.broadcasted_iota(jnp.int32, (pair_rows, 2 * pair_slots), 1).astype(jnp.float32)
+        back = jnp.zeros(slot.shape, jnp.bool_)
+        for e in range(2):
+            mine = lane == ids_ref[e] + 2 * experts
+            rank = jnp.sum(jnp.where(mine, tail, 0.0), axis=1, keepdims=True)
+            back = back | (slot == rank + shift + float(e * pair_slots))
+        spread[p] = jnp.where(back, 1.0, 0.0).astype(jnp.bfloat16)
+
+    for e in range(2):
+        tail = slots[e, :, width:].astype(jnp.float32)
+        lane = lax.broadcasted_iota(jnp.int32, tail.shape, 1)
+        mine = (lane == ids_ref[e]) | (lane == ids_ref[e] + experts)
+        weight = jnp.sum(jnp.where(mine, tail, 0.0), axis=1, keepdims=True)
+        up_copies[2 * e].wait()
+        gate_act = jnp.dot(
+            slots[e, :, :width], weights[2 * e], preferred_element_type=jnp.float32
+        )
+        up_copies[2 * e + 1].wait()
+        up_act = jnp.dot(
+            slots[e, :, :width], weights[2 * e + 1], preferred_element_type=jnp.float32
+        )
+        act = gate_act / (1.0 + jnp.exp(-gate_act)) * up_act * weight
+        inner[e] = act.astype(jnp.bfloat16)
+    for e in range(2):
+        down_copies[e].wait()
+        result = jnp.dot(inner[e], downs[e], preferred_element_type=jnp.float32)
+        result = result.astype(jnp.bfloat16)
+        for p in range(2):
+            results[p, pl.ds(e * pair_slots, pair_slots), :] = result[p * pair_slots : (p + 1) * pair_slots]
+    out_copies = []
+    at = 0
+    for p in range(2):
+        part = pl.ds(p * pair_rows, pair_rows)
+        total = jnp.dot(spread[p], results[p], preferred_element_type=jnp.float32)
+        sums[part, :] = total.astype(jnp.bfloat16)
+        while len(out_copies) < len(targets) and at < (p + 1) * pair_rows:
+            count = block_rows[len(out_copies)]
+            copy = pltpu.make_async_copy(
+                sums.at[pl.ds(at, count)], targets[len(out_copies)], out_sem.at[len(out_copies)]
+            )
+            copy.start()
+            out_copies.append(copy)
+            at += count
+    for copy in out_copies:
+        copy.wait()
+
+
+def run_plane(ids, cap, decodes, pieces, block_rows, weights):
+    width, units = weights[0].shape
+    padded = pieces[0].shape[1]
+    piece_rows = tuple(piece.shape[0] for piece in pieces)
+    total = sum(piece_rows)
+    kept = jnp.bfloat16
+    anywhere = pl.BlockSpec(memory_space=pl.ANY)
+    return pl.pallas_call(
+        functools.partial(plane_kernel, cap, piece_rows, block_rows),
+        in_specs=[pl.BlockSpec(memory_space=pltpu.SMEM)] + [anywhere] * (len(pieces) + 7),
+        out_specs=[anywhere] * len(block_rows),
+        out_shape=[jax.ShapeDtypeStruct((count, width), kept) for count in block_rows],
+        scratch_shapes=[
+            pltpu.VMEM(decodes.shape, kept),
+            pltpu.VMEM((total, padded), kept),
+            pltpu.VMEM((4, width, units), kept),
+            pltpu.VMEM((2, units, width), kept),
+            pltpu.VMEM((2, 4 * cap, padded), kept),
+            pltpu.VMEM((2, 4 * cap, units), kept),
+            pltpu.VMEM((2, 4 * cap, width), kept),
+            pltpu.VMEM((2, total // 2, 4 * cap), kept),
+            pltpu.VMEM((total, width), kept),
+            pltpu.SemaphoreType.DMA((len(pieces) + 1,)),
+            pltpu.SemaphoreType.DMA((6,)),
+            pltpu.SemaphoreType.DMA((len(block_rows),)),
+        ],
+        compiler_params=pltpu.CompilerParams(vmem_limit_bytes=48 << 20),
+        cost_estimate=pl.CostEstimate(
+            flops=12 * total * width * units, bytes_accessed=24 << 20, transcendentals=total * units
+        ),
+        name="plane",
+    )(ids, decodes, *pieces, *weights)
+
+
+def merge_kernel(cut, x_ref, y_ref, passed_0_ref, passed_1_ref, x_out, y_out):
+    def sum_of(one, other):
+        return (one.astype(jnp.float32) + other.astype(jnp.float32)).astype(jnp.bfloat16)
+
+    x_out[:cut, :] = sum_of(x_ref[:cut, :], passed_0_ref[...])
+    x_out[cut:, :] = x_ref[cut:, :]
+    y_out[:cut, :] = y_ref[:cut, :]
+    y_out[cut:, :] = sum_of(y_ref[cut:, :], passed_1_ref[...])
+
+
+def merge_passed(cut, to_x, to_y, passed_0, passed_1):
+    return pl.pallas_call(
+        functools.partial(merge_kernel, cut),
+        out_shape=[jax.ShapeDtypeStruct(to_x.shape, to_x.dtype)] * 2,
+        compiler_params=pltpu.CompilerParams(vmem_limit_bytes=16 << 20),
+        name="merge",
+    )(to_x, to_y, passed_0, passed_1)
+
+
+def along_x(value):
+    return lax.ppermute(value, "kv", [(i, i ^ 1) for i in range(4)])
+
+
+def along_y(value):
+    return lax.ppermute(value, "kv", [(i, i ^ 2) for i in range(4)])
+
+
+def around_z(value):
+    return lax.ppermute(value, "blk", [(i, (i + 2) % 8) for i in range(8)])
+
+
+def across_chip(value):
+    return lax.ppermute(value, "blk", [(i, i ^ 1) for i in range(8)])
+
+
+def fence(*values):
+    return lax.optimization_barrier(values)
+
+
+def added(*parts):
+    total = parts[0].astype(jnp.float32)
+    for part in parts[1:]:
+        total = total + part.astype(jnp.float32)
+    return total
+
+
+def permuted_plan(
+    queries,
+    cache_keys,
+    cache_values,
+    lengths,
+    sinks,
+    out_proj,
+    decode_resid,
+    prefill_hidden,
+    norm_gain,
+    router,
+    routes,
+    expert_gate,
+    expert_up,
+    expert_down,
+):
+    experts = router.shape[1]
+    ids = routes[0]
+    tokens = ids.shape[0]
+    my_kv = lax.axis_index("kv")
+    my_blk = lax.axis_index("blk")
+    first_expert = my_kv * 8
+    expert_ids = jnp.stack(
+        [first_expert + my_blk, first_expert + (my_blk ^ 1), jnp.int32(experts)]
+    ).astype(jnp.int32)
+    cap = (2 * tokens * ids.shape[1] + experts - 1) // experts
+    long = (tokens // 2 + 15) // 16 * 16
+    cuts = [long, tokens - long, long, tokens - long]
+    blocks = [None] * 4
+    sides = [None] * 4
+    corners = [None] * 4
+    decodes = [None] * 4
+    sums = [None] * 4
+    passed = [None] * 4
+    back = [None] * 4
+
+    def spread_sides(step):
+        sides[step] = along_x(blocks[step]), along_y(blocks[step])
+
+    def spread_corners(step):
+        cut = cuts[step]
+        corners[step] = along_y(sides[step][0][:cut]), along_x(sides[step][1][cut:])
+
+    def apply(step):
+        counts = (tokens, tokens, tokens, cuts[step], tokens - cuts[step])
+        pieces = (blocks[step],) + sides[step] + corners[step]
+        sums[step] = run_plane(expert_ids, cap, decodes[step], pieces, counts, weights)
+
+    def return_corners(step):
+        passed[step] = along_y(sums[step][3]), along_x(sums[step][4])
+
+    def return_sides(step):
+        to_x, to_y = merge_passed(cuts[step], sums[step][1], sums[step][2], *passed[step])
+        back[step] = along_x(to_x), along_y(to_y)
+
+    prefill = prefill_hidden[0]
+    nothing = jnp.zeros((1, prefill.shape[1]), prefill.dtype)
+    blocks[0] = prepare(
+        jnp.concatenate([nothing, prefill], axis=0), norm_gain, router, ids, "block"
+    )
+    blocks[0], queries, cache_keys, expert_gate, expert_up = fence(
+        blocks[0], queries, cache_keys, expert_gate, expert_up
+    )
+    spread_sides(0)
+    blocks[1] = around_z(blocks[0])
+    other_gate = across_chip(expert_gate[0])
+    other_up = across_chip(expert_up[0])
+
+    attended = attend(queries, cache_keys, cache_values, lengths, sinks)
+    partial_proj = jnp.dot(attended, out_proj, preferred_element_type=jnp.float32)
+    is_mine = jnp.arange(4)[:, None] == my_kv
+    partial_proj += jnp.where(is_mine, decode_resid.astype(jnp.float32), 0.0)
+    width = partial_proj.shape[1]
+    ids_row = jnp.pad(ids[:1].astype(jnp.float32), ((0, 0), (0, width - ids.shape[1])))
+    shared = jnp.concatenate([partial_proj, jnp.where(is_mine, ids_row, 0.0)], axis=0)
+
+    shared, other_gate = fence(shared, other_gate)
+    shared = shared + along_x(shared)
+    sides[0], blocks[1], shared, expert_down = fence(sides[0], blocks[1], shared, expert_down)
+
+    spread_sides(1)
+    blocks[2] = around_z(blocks[1])
+    other_down = across_chip(expert_down[0])
+    sides[1], sides[0], blocks[2], shared = fence(sides[1], sides[0], blocks[2], shared)
+
+    spread_corners(0)
+    shared = shared + along_y(shared)
+    order = [my_kv ^ j for j in range(4)]
+    decoded = jnp.concatenate(
+        [lax.dynamic_slice_in_dim(shared, index, 1) for index in order], axis=0
+    ).astype(jnp.bfloat16)
+    decode_ids = jnp.concatenate(
+        [lax.dynamic_slice_in_dim(shared, 4 + index, 1) for index in order], axis=0
+    )[:, : ids.shape[1]].astype(jnp.int32)
+    hidden = jnp.concatenate([decoded[:1], prefill], axis=0)
+    decodes[0] = prepare(
+        jnp.pad(decoded, ((0, 12), (0, 0))),
+        norm_gain,
+        router,
+        jnp.pad(decode_ids, ((0, 12), (0, 0))),
+        "first",
+    )
+    corners[0], sides[1], blocks[2], decodes[0], other_up, other_down = fence(
+        corners[0], sides[1], blocks[2], decodes[0], other_up, other_down
+    )
+    weights = (expert_gate[0], expert_up[0], expert_down[0], other_gate, other_up, other_down)
+
+    spread_corners(1)
+    spread_sides(2)
+    arrived = around_z(jnp.concatenate([blocks[2], decodes[0]], axis=0))
+    apply(0)
+    corners[1], sides[2], arrived, sums[0] = fence(corners[1], sides[2], arrived, sums[0])
+    blocks[3], decodes[1] = arrived[:tokens], arrived[tokens:]
+
+    spread_corners(2)
+    spread_sides(3)
+    decodes[2] = around_z(decodes[1])
+    apply(1)
+    corners[2], sides[3], decodes[2], sums[1] = fence(corners[2], sides[3], decodes[2], sums[1])
+
+    spread_corners(3)
+    decodes[3] = around_z(decodes[2])
+    return_corners(1)
+    apply(2)
+    corners[3], decodes[3], passed[1], sums[1], sums[2] = fence(
+        corners[3], decodes[3], passed[1], sums[1], sums[2]
+    )
+
+    return_sides(1)
+    return_corners(2)
+    apply(3)
+    back[1], passed[2], sums[1], sums[2], sums[3] = fence(
+        back[1], passed[2], sums[1], sums[2], sums[3]
+    )
+
+    return_sides(2)
+    return_corners(3)
+    carried = around_z(added(sums[1][0], *back[1]).astype(jnp.bfloat16))
+    back[2], passed[3], carried, sums[2], sums[3], sums[0] = fence(
+        back[2], passed[3], carried, sums[2], sums[3], sums[0]
+    )
+
+    return_sides(3)
+    return_corners(0)
+    carried = around_z(added(sums[2][0], *back[2], carried).astype(jnp.bfloat16))
+    back[3], passed[0], carried, sums[3], sums[0] = fence(
+        back[3], passed[0], carried, sums[3], sums[0]
+    )
+
+    return_sides(0)
+    carried = around_z(added(sums[3][0], *back[3], carried).astype(jnp.bfloat16))
+    return added(hidden, sums[0][0], *back[0], carried).astype(jnp.bfloat16)[None]
+
+
 def chunk_cuts(tokens, devices):
-    step = (tokens // 2 + 15) // 16 * 16 if devices <= 32 else 32
+    step = (tokens // 2 + 15) // 16 * 16 if devices < 128 else 32
     return [(start, min(start + step, tokens)) for start in range(0, tokens, step)]
 
 
-def body(
+def gathered_plan(
     queries,
     cache_keys,
     cache_values,
@@ -170,8 +530,9 @@
 
 
 def solution(mesh):
+    plan = permuted_plan if (mesh.shape["kv"], mesh.shape["blk"]) == (4, 8) else gathered_plan
     return jax.shard_map(
-        body,
+        plan,
         mesh=mesh,
         in_specs=(
             P("blk", "kv"),

time: 503 us -> 167 us (0.33)
  waiting for transfers between devices: 405 us -> 57.2 us
  starting transfers between devices: 0.13 us -> 45.3 us
  blocking collectives: 17.9 us -> 0 us
  between operations: 13.3 us -> 0.45 us
    reduce_scatter x2 -> x0, waiting for transfers between devices: 278 us -> none  [body(): lax.psum_scatter(sums, AXES, scatter_dimension=0, tiled=True)]
    all_gather x2 -> x0, waiting for transfers between devices: 127 us -> none  [body(): gathered.append(lax.all_gather(sent, AXES, axis=0, tiled=True))]
    ppermute x0 -> x45, waiting for transfers between devices: none -> 57.2 us  [the longest x17 32.3 us: along_x(): return lax.ppermute(value, 'kv', [(i, i ^ 1) for i in range(4)])]
    ppermute x0 -> x45, starting transfers between devices: none -> 45.3 us  [the longest x17 19 us: along_x(): return lax.ppermute(value, 'kv', [(i, i ^ 1) for i in range(4)])]
    unnamed x1 -> x0, blocking collectives: 17.9 us -> none
    pallas_call x4 -> x10, Pallas kernels: 48.9 us -> 49.2 us  [the longest x4 47.5 us: run_plane(): pl.pallas_call(functools.partial(plane_kernel, cap, piece_rows, block_row...]
  transfers between devices with their start and end apart: 4 -> 45, of which waited for: 4 -> 16; matrix products, arithmetic and copies ran while one was open for 0% -> 5% of each run, Pallas kernels for 9% -> 29%
where the time goes in v4:
time: 167 us; the launch traced here: 166 us
  waiting for transfers between devices  57.2 us (34%)
  Pallas kernels  49.2 us (29%)
  starting transfers between devices  45.3 us (27%)
  matrix products  5.14 us (3%)
  other arithmetic  5.02 us (3%)
  local copies, waits for them, and re-layouts  4.14 us (2%)
    pallas_call x4, Pallas kernels, run_plane(): pl.pallas_call(functools.partial(plane_kernel, cap, piece_rows, block_row...  47.5 us
    ppermute x17, waiting for transfers between devices, along_x(): return lax.ppermute(value, 'kv', [(i, i ^ 1) for i in range(4)])  32.3 us
    ppermute x17, waiting for transfers between devices, along_y(): return lax.ppermute(value, 'kv', [(i, i ^ 2) for i in range(4)])  20.4 us
    ppermute x17, starting transfers between devices, along_x(): return lax.ppermute(value, 'kv', [(i, i ^ 1) for i in range(4)])  19 us
    ppermute x17, starting transfers between devices, along_y(): return lax.ppermute(value, 'kv', [(i, i ^ 2) for i in range(4)])  16.7 us
    ppermute x8, starting transfers between devices, around_z(): return lax.ppermute(value, 'blk', [(i, (i + 2) % 8) for i in range(8)])  9.18 us
    ppermute x8, waiting for transfers between devices, around_z(): return lax.ppermute(value, 'blk', [(i, (i + 2) % 8) for i in range(8)])  4.52 us
    dot_general x1, matrix products, attend(): jnp.einsum('rgd,rjd->rgj', grouped_q, key_rows, preferred_element_type=jn...  3.76 us
  transfers between devices with their start and end apart: 45, of which 16 were waited for; matrix products, arithmetic and copies ran while one was open for 5% of the time, Pallas kernels for 29%

profile of v4, /device:TPU:0, one launch (start us, length us, event | category | flops | bytes accessed | tf_op | source)
XLA Modules:
  0.0 166.4 jit_solution(14910096737019670938)
XLA Ops:
  0.0 1.2 copy.16.router_ref
  1.2 0.8 copy.15
  2.0 1.1 concatenate.19.hidden_ref
  3.2 0.7 copy-done
  3.9 0.7 prepare.2.refs_2_
  4.6 3.0 %collective-permute-start = (bf16[112,2176]{1,0:T(8,128)(2,1)S(1)}, bf16[112,2176]{1,0:T(8,128)(2,1)S(1)}, u32[]{:S(2)}, u32[]{:S(2)}) collective-permute-start(bf16[112,2176]{1,0:T(8,128)(2,1)S(1)} %prepare.2.refs_2_), channel_id=1, source_target_pairs={{0,8},{8,0},{16,24},{24,16},{1,9},{9,1},{17,25},{25,17},{2,10},{10... | collective-permute-start | bytes 1462280 | tf_op jit(solution)/shard_map/ppermute | solution.py:300
  7.6 1.5 collective-permute-start.1
  9.1 1.6 collective-permute-start.2
  10.7 0.8 convert_reduce_fusion
  11.5 0.7 broadcast_in_dim.77
  12.2 0.9 minimum_subtract_fusion
  13.2 3.8 %fusion.33 = (f32[4,8]{1,0:T(4,128)S(1)}, f32[4,8,4096]{2,1,0:T(8,128)S(1)}) fusion(bf16[4,4096,1,128]{3,1,2,0:T(8,128)(2,1)} %param.15, bf16[1,4,8,128]{3,1,2,0:T(4,128)(2,1)} %bitcast.46, pred[4,4096]{1,0:T(4,128)(4,1)S(1)} %iota_compare_fusion.1), kind=kOutput, calls=%fused_computation.55 | convolution fusion | flops 33947616 | bytes 4743296 | tf_op jit(solution)/shard_map/rgd,rjd->rgj/dot_general | solution.py:27
  17.3 0.7 fusion.10
  18.1 0.7 convolution_add_fusion
  18.8 0.6 collective-permute-start.4
  19.6 3.7 %collective-permute-done.4 = f32[8,2048]{1,0:T(8,128)S(1)} collective-permute-done((f32[8,2048]{1,0:T(8,128)S(1)}, f32[8,2048]{1,0:T(8,128)S(1)}, u32[]{:S(2)}, u32[]{:S(2)}) %collective-permute-start.4) | collective-permute-done | bytes 65568 | tf_op jit(solution)/shard_map/ppermute | solution.py:300
  23.5 0.6 collective-permute-start.5
  24.1 0.5 collective-permute-start.6
  24.6 1.6 collective-permute-start.7
  26.2 11.1 %collective-permute-done.5.refs_3_ = bf16[112,2176]{1,0:T(8,128)(2,1)S(1)} collective-permute-done((bf16[112,2176]{1,0:T(8,128)(2,1)}, bf16[112,2176]{1,0:T(8,128)(2,1)S(1)}, u32[]{:S(2)}, u32[]{:S(2)}) %collective-permute-start.5) | collective-permute-done | bytes 487456 | tf_op jit(solution)/shard_map/ppermute | solution.py:300
  37.5 2.0 %collective-permute-done.7.refs_2_ = bf16[112,2176]{1,0:T(8,128)(2,1)S(1)} collective-permute-done((bf16[112,2176]{1,0:T(8,128)(2,1)}, bf16[112,2176]{1,0:T(8,128)(2,1)S(1)}, u32[]{:S(2)}, u32[]{:S(2)}) %collective-permute-start.7) | collective-permute-done | bytes 487456 | tf_op jit(solution)/shard_map/ppermute | solution.py:308
  39.5 1.5 collective-permute-start.8
  41.1 0.6 collective-permute-start.9
  41.7 1.6 collective-permute-start.10
  43.3 1.1 collective-permute-done.8
  44.6 0.5 prepare.3.refs_1_
  45.2 2.5 %collective-permute-done.10.refs_6_ = bf16[48,2176]{1,0:T(8,128)(2,1)S(1)} collective-permute-done((bf16[48,2176]{1,0:T(8,128)(2,1)S(1)}, bf16[48,2176]{1,0:T(8,128)(2,1)S(1)}, u32[]{:S(2)}, u32[]{:S(2)}) %collective-permute-start.10) | collective-permute-done | bytes 208928 | tf_op jit(solution)/shard_map/ppermute | solution.py:300
  47.6 1.6 collective-permute-done.9.refs_5_
  49.2 1.5 collective-permute-start.15
  50.7 0.8 collective-permute-start.16
  51.7 0.6 collective-permute-start.14
  52.3 1.3 collective-permute-start.13
  53.6 11.9 %plane.4 = (bf16[112,2048]{1,0:T(8,128)(2,1)S(1)}, bf16[112,2048]{1,0:T(8,128)(2,1)S(1)}, bf16[112,2048]{1,0:T(8,128)(2,1)S(1)}, bf16[64,2048]{1,0:T(8,128)(2,1)S(1)}, bf16[48,2048]{1,0:T(8,128)(2,1)S(1)}) custom-call(s32[3]{0:T(128)S(1)} %pad_add_fusion.refs_0_, bf16[16,2176]{1,0:T(8,128)(2,1)S(1)} %prepare.3.refs_1_, ...), custom_call_target="tpu_custom_call" | custom-call | flops 8455716864 | bytes 25165824 | tf_op jit(solution)/shard_map/plane/pallas_call | solution.py:253
  65.5 1.0 collective-permute-done.13.refs_5_
  66.8 1.6 collective-permute-start.20
  68.8 1.7 %collective-permute-start.18 = (bf16[64,2176]{1,0:T(8,128)(2,1)S(1)}, bf16[64,2176]{1,0:T(8,128)(2,1)S(1)}, u32[]{:S(2)}, u32[]{:S(2)}) collective-permute-start(bf16[64,2176]{1,0:T(8,128)(2,1)S(1)} %slice.47), channel_id=1, source_target_pairs={{0,16},{8,24},{16,0},{24,8},{1,17},{9,25},{17,1},{25,9},{2,18},{10... | collective-permute-start | bytes 835592 | tf_op jit(solution)/shard_map/ppermute | solution.py:304
  70.5 0.6 collective-permute-start.19
  71.2 11.6 %plane.5 = (bf16[112,2048]{1,0:T(8,128)(2,1)S(1)}, bf16[112,2048]{1,0:T(8,128)(2,1)S(1)}, bf16[112,2048]{1,0:T(8,128)(2,1)S(1)}, bf16[48,2048]{1,0:T(8,128)(2,1)S(1)}, bf16[64,2048]{1,0:T(8,128)(2,1)S(1)}) custom-call(s32[3]{0:T(128)S(1)} %pad_add_fusion.refs_0_, bf16[16,2176]{1,0:T(8,128)(2,1)S(1)} %slice.50.refs_1_, ...), custom_call_target="tpu_custom_call" | custom-call | flops 8455716864 | bytes 25165824 | tf_op jit(solution)/shard_map/plane/pallas_call | solution.py:253
  82.8 2.4 %collective-permute-done.18.refs_5_ = bf16[64,2176]{1,0:T(8,128)(2,1)S(1)} collective-permute-done((bf16[64,2176]{1,0:T(8,128)(2,1)S(1)}, bf16[64,2176]{1,0:T(8,128)(2,1)S(1)}, u32[]{:S(2)}, u32[]{:S(2)}) %collective-permute-start.18) | collective-permute-done | bytes 278560 | tf_op jit(solution)/shard_map/ppermute | solution.py:304
  85.7 2.0 %collective-permute-start.27 = (bf16[64,2048]{1,0:T(8,128)(2,1)S(1)}, bf16[64,2048]{1,0:T(8,128)(2,1)S(1)}, u32[]{:S(2)}, u32[]{:S(2)}) collective-permute-start(bf16[64,2048]{1,0:T(8,128)(2,1)S(1)} %get-tuple-element.173), channel_id=1, source_target_pairs={{0,8},{8,0},{16,24},{24,16},{1,9},{9,1},{17,25},{25,17},{2,10},{10... | collective-permute-start | bytes 786440 | tf_op jit(solution)/shard_map/ppermute | solution.py:300
  87.7 1.7 %collective-permute-start.26 = (bf16[48,2048]{1,0:T(8,128)(2,1)S(1)}, bf16[48,2048]{1,0:T(8,128)(2,1)S(1)}, u32[]{:S(2)}, u32[]{:S(2)}) collective-permute-start(bf16[48,2048]{1,0:T(8,128)(2,1)S(1)} %get-tuple-element.172), channel_id=1, source_target_pairs={{0,16},{8,24},{16,0},{24,8},{1,17},{9,25},{17,1},{25,9},{2,18},{10... | collective-permute-start | bytes 589832 | tf_op jit(solution)/shard_map/ppermute | solution.py:304
  89.5 11.9 %plane.6 = (bf16[112,2048]{1,0:T(8,128)(2,1)S(1)}, bf16[112,2048]{1,0:T(8,128)(2,1)S(1)}, bf16[112,2048]{1,0:T(8,128)(2,1)S(1)}, bf16[64,2048]{1,0:T(8,128)(2,1)S(1)}, bf16[48,2048]{1,0:T(8,128)(2,1)S(1)}) custom-call(s32[3]{0:T(128)S(1)} %pad_add_fusion.refs_0_, bf16[16,2176]{1,0:T(8,128)(2,1)S(1)} %collective-permute-done.22.refs_1_, ...), custom_call_target="tpu_custom_call" | custom-call | flops 8455716864 | bytes 25165824 | tf_op jit(solution)/shard_map/plane/pallas_call | solution.py:253
  101.5 0.5 collective-permute-start.28
  102.4 1.6 collective-permute-start.30
  104.0 1.6 collective-permute-start.31
  105.6 12.1 %plane.7 = (bf16[112,2048]{1,0:T(8,128)(2,1)S(1)}, bf16[112,2048]{1,0:T(8,128)(2,1)S(1)}, bf16[112,2048]{1,0:T(8,128)(2,1)S(1)}, bf16[48,2048]{1,0:T(8,128)(2,1)S(1)}, bf16[64,2048]{1,0:T(8,128)(2,1)S(1)}) custom-call(s32[3]{0:T(128)S(1)} %pad_add_fusion.refs_0_, bf16[16,2176]{1,0:T(8,128)(2,1)S(1)} %collective-permute-done.25.refs_1_, ...), custom_call_target="tpu_custom_call" | custom-call | flops 8455716864 | bytes 25165824 | tf_op jit(solution)/shard_map/plane/pallas_call | solution.py:253
  118.0 1.3 collective-permute-start.36
  119.4 1.6 collective-permute-start.32
  121.0 0.8 collective-permute-start.33
  121.8 0.5 collective-permute-start.35
  122.3 1.2 collective-permute-start.34
  123.5 10.8 %collective-permute-done.34.passed_0_ref = bf16[48,2048]{1,0:T(8,128)(2,1)S(1)} collective-permute-done((bf16[48,2048]{1,0:T(8,128)(2,1)S(1)}, bf16[48,2048]{1,0:T(8,128)(2,1)S(1)}, u32[]{:S(2)}, u32[]{:S(2)}) %collective-permute-start.34) | collective-permute-done | bytes 196640 | tf_op jit(solution)/shard_map/ppermute | solution.py:304
  134.6 1.0 collective-permute-start.41
  135.7 1.5 collective-permute-start.37
  137.6 1.7 %collective-permute-start.39 = (bf16[64,2048]{1,0:T(8,128)(2,1)S(1)}, bf16[64,2048]{1,0:T(8,128)(2,1)S(1)}, u32[]{:S(2)}, u32[]{:S(2)}) collective-permute-start(bf16[64,2048]{1,0:T(8,128)(2,1)S(1)} %get-tuple-element.230), channel_id=1, source_target_pairs={{0,16},{8,24},{16,0},{24,8},{1,17},{9,25},{17,1},{25,9},{2,18},{10... | collective-permute-start | bytes 786440 | tf_op jit(solution)/shard_map/ppermute | solution.py:304
  139.2 0.6 collective-permute-start.40
  139.9 11.0 %collective-permute-done.40.passed_1_ref = bf16[48,2048]{1,0:T(8,128)(2,1)S(1)} collective-permute-done((bf16[48,2048]{1,0:T(8,128)(2,1)S(1)}, bf16[48,2048]{1,0:T(8,128)(2,1)S(1)}, u32[]{:S(2)}, u32[]{:S(2)}) %collective-permute-start.40) | collective-permute-done | bytes 196640 | tf_op jit(solution)/shard_map/ppermute | solution.py:300
  150.8 2.6 %collective-permute-done.39.passed_0_ref = bf16[64,2048]{1,0:T(8,128)(2,1)S(1)} collective-permute-done((bf16[64,2048]{1,0:T(8,128)(2,1)S(1)}, bf16[64,2048]{1,0:T(8,128)(2,1)S(1)}, u32[]{:S(2)}, u32[]{:S(2)}) %collective-permute-start.39) | collective-permute-done | bytes 262176 | tf_op jit(solution)/shard_map/ppermute | solution.py:304
  153.6 0.7 collective-permute-start.42
  154.8 3.6 %collective-permute-start.44 = (bf16[112,2048]{1,0:T(8,128)(2,1)S(1)}, bf16[112,2048]{1,0:T(8,128)(2,1)S(1)}, u32[]{:S(2)}, u32[]{:S(2)}) collective-permute-start(bf16[112,2048]{1,0:T(8,128)(2,1)S(1)} %add_convert_fusion.1), channel_id=1, source_target_pairs={{0,2},{1,3},{2,4},{3,5},{4,6},{5,7},{6,0},{7,1},{8,10},{9,11},{10,... | collective-permute-start | bytes 1376264 | tf_op jit(solution)/shard_map/ppermute | solution.py:308
  158.4 3.7 %collective-permute-done.42 = bf16[112,2048]{1,0:T(8,128)(2,1)S(1)} collective-permute-done((bf16[112,2048]{1,0:T(8,128)(2,1)S(1)}, bf16[112,2048]{1,0:T(8,128)(2,1)S(1)}, u32[]{:S(2)}, u32[]{:S(2)}) %collective-permute-start.42) | collective-permute-done | bytes 458784 | tf_op jit(solution)/shard_map/ppermute | solution.py:300
  162.1 0.6 collective-permute-done.43
  162.7 2.5 %collective-permute-done.44 = bf16[112,2048]{1,0:T(8,128)(2,1)S(1)} collective-permute-done((bf16[112,2048]{1,0:T(8,128)(2,1)S(1)}, bf16[112,2048]{1,0:T(8,128)(2,1)S(1)}, u32[]{:S(2)}, u32[]{:S(2)}) %collective-permute-start.44) | collective-permute-done | bytes 458784 | tf_op jit(solution)/shard_map/ppermute | solution.py:308
  165.2 1.2 fusion.13
  (88 shorter events, 5.2 us)
Async XLA Ops:
  0.0 17.0 %copy-start.5 = (f32[8]{0:T(128)S(1)}, f32[8]{0:T(128)}, u32[]{:S(2)}) copy-start(f32[8]{0:T(128)} %param.18) | copy-start | bytes 100
  3.2 0.7 copy-start
  4.6 18.8 %collective-permute-start = (bf16[112,2176]{1,0:T(8,128)(2,1)S(1)}, bf16[112,2176]{1,0:T(8,128)(2,1)S(1)}, u32[]{:S(2)}, u32[]{:S(2)}) collective-permute-start(bf16[112,2176]{1,0:T(8,128)(2,1)S(1)} %prepare.2.refs_2_), channel_id=1, source_target_pairs={{0,8},{8,0},{16,24},{24,16},{1,9},{9,1},{17,25},{25,17},{2,10},{10... | collective-permute-start | bytes 1462280 | tf_op jit(solution)/shard_map/ppermute | solution.py:300
  7.6 15.8 %collective-permute-start.1 = (bf16[112,2176]{1,0:T(8,128)(2,1)S(1)}, bf16[112,2176]{1,0:T(8,128)(2,1)S(1)}, u32[]{:S(2)}, u32[]{:S(2)}) collective-permute-start(bf16[112,2176]{1,0:T(8,128)(2,1)S(1)} %prepare.2.refs_2_), channel_id=1, source_target_pairs={{0,16},{8,24},{16,0},{24,8},{1,17},{9,25},{17,1},{25,9},{2,18},{10... | collective-permute-start | bytes 1462280 | tf_op jit(solution)/shard_map/ppermute | solution.py:304
  9.1 14.3 %collective-permute-start.2 = (bf16[112,2176]{1,0:T(8,128)(2,1)S(1)}, bf16[112,2176]{1,0:T(8,128)(2,1)}, u32[]{:S(2)}, u32[]{:S(2)}) collective-permute-start(bf16[112,2176]{1,0:T(8,128)(2,1)S(1)} %prepare.2.refs_2_), channel_id=1, source_target_pairs={{0,2},{1,3},{2,4},{3,5},{4,6},{5,7},{6,0},{7,1},{8,10},{9,11},{10,... | collective-permute-start | bytes 1462280 | tf_op jit(solution)/shard_map/ppermute | solution.py:308
  10.7 8.1 %collective-permute-start.3 = (bf16[2048,768]{1,0:T(8,128)(2,1)}, bf16[2048,768]{1,0:T(8,128)(2,1)}, u32[]{:S(2)}, u32[]{:S(2)}) collective-permute-start(bf16[2048,768]{1,0:T(8,128)(2,1)} %bitcast.48), channel_id=1, source_target_pairs={{0,1},{1,0},{2,3},{3,2},{4,5},{5,4},{6,7},{7,6},{8,9},{9,8},{10,11... | collective-permute-start | bytes 9437192 | tf_op jit(solution)/shard_map/ppermute | solution.py:312
  12.2 5.1 %copy-start.2 = (bf16[4,4096,1,128]{3,1,2,0:T(8,128)(2,1)S(1)}, bf16[4,4096,1,128]{3,1,2,0:T(8,128)(2,1)}, u32[]{:S(2)}) copy-start(bf16[4,4096,1,128]{3,1,2,0:T(8,128)(2,1)} %param.16) | copy-start | bytes 12582916
  13.2 4.9 %copy-start.3 = (bf16[1024,2048]{1,0:T(8,128)(2,1)S(1)}, bf16[1024,2048]{1,0:T(8,128)(2,1)}, u32[]{:S(2)}) copy-start(bf16[1024,2048]{1,0:T(8,128)(2,1)} %param.19) | copy-start | bytes 12582916
  18.0 26.6 %copy-start.1 = (f32[2048]{0:T(1024)S(1)}, f32[2048]{0:T(1024)}, u32[]{:S(2)}) copy-start(f32[2048]{0:T(1024)} %param.22) | copy-start | bytes 24580
  18.8 4.6 %collective-permute-start.4 = (f32[8,2048]{1,0:T(8,128)S(1)}, f32[8,2048]{1,0:T(8,128)S(1)}, u32[]{:S(2)}, u32[]{:S(2)}) collective-permute-start(f32[8,2048]{1,0:T(8,128)S(1)} %pad_maximum_fusion.1), channel_id=1, source_target_pairs={{0,8},{8,0},{16,24},{24,16},{1,9},{9,1},{17,25},{25,17},{2,10},{10... | collective-permute-start | bytes 196616 | tf_op jit(solution)/shard_map/ppermute | solution.py:300
  19.4 25.8 %collective-permute-start.11 = (bf16[2048,768]{1,0:T(8,128)(2,1)}, bf16[2048,768]{1,0:T(8,128)(2,1)}, u32[]{:S(2)}, u32[]{:S(2)}) collective-permute-start(bf16[2048,768]{1,0:T(8,128)(2,1)} %bitcast.8.refs_8_), channel_id=1, source_target_pairs={{0,1},{1,0},{2,3},{3,2},{4,5},{5,4},{6,7},{7,6},{8,9},{9,8},{10,11... | collective-permute-start | bytes 9437192 | tf_op jit(solution)/shard_map/ppermute | solution.py:312
  23.4 25.8 %collective-permute-start.12 = (bf16[768,2048]{1,0:T(8,128)(2,1)}, bf16[768,2048]{1,0:T(8,128)(2,1)}, u32[]{:S(2)}, u32[]{:S(2)}) collective-permute-start(bf16[768,2048]{1,0:T(8,128)(2,1)} %bitcast.9.refs_9_), channel_id=1, source_target_pairs={{0,1},{1,0},{2,3},{3,2},{4,5},{5,4},{6,7},{7,6},{8,9},{9,8},{10,11... | collective-permute-start | bytes 9437192 | tf_op jit(solution)/shard_map/ppermute | solution.py:312
  23.5 13.8 %collective-permute-start.5 = (bf16[112,2176]{1,0:T(8,128)(2,1)}, bf16[112,2176]{1,0:T(8,128)(2,1)S(1)}, u32[]{:S(2)}, u32[]{:S(2)}) collective-permute-start(bf16[112,2176]{1,0:T(8,128)(2,1)} %collective-permute-done.2.refs_2_), channel_id=1, source_target_pairs={{0,8},{8,0},{16,24},{24,16},{1,9},{9,1},{17,25},{25,17},{2,10},{10... | collective-permute-start | bytes 1462280 | tf_op jit(solution)/shard_map/ppermute | solution.py:300
  24.1 13.4 %collective-permute-start.6 = (bf16[112,2176]{1,0:T(8,128)(2,1)}, bf16[112,2176]{1,0:T(8,128)(2,1)S(1)}, u32[]{:S(2)}, u32[]{:S(2)}) collective-permute-start(bf16[112,2176]{1,0:T(8,128)(2,1)} %collective-permute-done.2.refs_2_), channel_id=1, source_target_pairs={{0,16},{8,24},{16,0},{24,8},{1,17},{9,25},{17,1},{25,9},{2,18},{10... | collective-permute-start | bytes 1462280 | tf_op jit(solution)/shard_map/ppermute | solution.py:304
  24.6 14.9 %collective-permute-start.7 = (bf16[112,2176]{1,0:T(8,128)(2,1)}, bf16[112,2176]{1,0:T(8,128)(2,1)S(1)}, u32[]{:S(2)}, u32[]{:S(2)}) collective-permute-start(bf16[112,2176]{1,0:T(8,128)(2,1)} %collective-permute-done.2.refs_2_), channel_id=1, source_target_pairs={{0,2},{1,3},{2,4},{3,5},{4,6},{5,7},{6,0},{7,1},{8,10},{9,11},{10,... | collective-permute-start | bytes 1462280 | tf_op jit(solution)/shard_map/ppermute | solution.py:308
  39.5 4.9 %collective-permute-start.8 = (f32[8,2048]{1,0:T(8,128)S(1)}, f32[8,2048]{1,0:T(8,128)S(1)}, u32[]{:S(2)}, u32[]{:S(2)}) collective-permute-start(f32[8,2048]{1,0:T(8,128)S(1)} %add.116), channel_id=1, source_target_pairs={{0,16},{8,24},{16,0},{24,8},{1,17},{9,25},{17,1},{25,9},{2,18},{10... | collective-permute-start | bytes 196616 | tf_op jit(solution)/shard_map/ppermute | solution.py:304
  41.1 8.1 %collective-permute-start.9 = (bf16[64,2176]{1,0:T(8,128)(2,1)S(1)}, bf16[64,2176]{1,0:T(8,128)(2,1)S(1)}, u32[]{:S(2)}, u32[]{:S(2)}) collective-permute-start(bf16[64,2176]{1,0:T(8,128)(2,1)S(1)} %slice.42), channel_id=1, source_target_pairs={{0,16},{8,24},{16,0},{24,8},{1,17},{9,25},{17,1},{25,9},{2,18},{10... | collective-permute-start | bytes 835592 | tf_op jit(solution)/shard_map/ppermute | solution.py:304
  41.7 5.9 %collective-permute-start.10 = (bf16[48,2176]{1,0:T(8,128)(2,1)S(1)}, bf16[48,2176]{1,0:T(8,128)(2,1)S(1)}, u32[]{:S(2)}, u32[]{:S(2)}) collective-permute-start(bf16[48,2176]{1,0:T(8,128)(2,1)S(1)} %slice.43), channel_id=1, source_target_pairs={{0,8},{8,0},{16,24},{24,16},{1,9},{9,1},{17,25},{25,17},{2,10},{10... | collective-permute-start | bytes 626696 | tf_op jit(solution)/shard_map/ppermute | solution.py:300
  49.2 17.5 %collective-permute-start.15 = (bf16[112,2176]{1,0:T(8,128)(2,1)S(1)}, bf16[112,2176]{1,0:T(8,128)(2,1)S(1)}, u32[]{:S(2)}, u32[]{:S(2)}) collective-permute-start(bf16[112,2176]{1,0:T(8,128)(2,1)S(1)} %collective-permute-done.7.refs_2_), channel_id=1, source_target_pairs={{0,8},{8,0},{16,24},{24,16},{1,9},{9,1},{17,25},{25,17},{2,10},{10... | collective-permute-start | bytes 1462280 | tf_op jit(solution)/shard_map/ppermute | solution.py:300
  50.7 16.0 %collective-permute-start.16 = (bf16[112,2176]{1,0:T(8,128)(2,1)S(1)}, bf16[112,2176]{1,0:T(8,128)(2,1)S(1)}, u32[]{:S(2)}, u32[]{:S(2)}) collective-permute-start(bf16[112,2176]{1,0:T(8,128)(2,1)S(1)} %collective-permute-done.7.refs_2_), channel_id=1, source_target_pairs={{0,16},{8,24},{16,0},{24,8},{1,17},{9,25},{17,1},{25,9},{2,18},{10... | collective-permute-start | bytes 1462280 | tf_op jit(solution)/shard_map/ppermute | solution.py:304
  51.6 15.2 %collective-permute-start.17 = (bf16[128,2176]{1,0:T(8,128)(2,1)S(1)}, bf16[128,2176]{1,0:T(8,128)(2,1)S(1)}, u32[]{:S(2)}, u32[]{:S(2)}) collective-permute-start(bf16[128,2176]{1,0:T(8,128)(2,1)S(1)} %pad_maximum_fusion), channel_id=1, source_target_pairs={{0,2},{1,3},{2,4},{3,5},{4,6},{5,7},{6,0},{7,1},{8,10},{9,11},{10,... | collective-permute-start | bytes 1671176 | tf_op jit(solution)/shard_map/ppermute | solution.py:308
  51.7 15.1 %collective-permute-start.14 = (bf16[64,2176]{1,0:T(8,128)(2,1)S(1)}, bf16[64,2176]{1,0:T(8,128)(2,1)S(1)}, u32[]{:S(2)}, u32[]{:S(2)}) collective-permute-start(bf16[64,2176]{1,0:T(8,128)(2,1)S(1)} %slice.46), channel_id=1, source_target_pairs={{0,8},{8,0},{16,24},{24,16},{1,9},{9,1},{17,25},{25,17},{2,10},{10... | collective-permute-start | bytes 835592 | tf_op jit(solution)/shard_map/ppermute | solution.py:300
  52.3 14.2 %collective-permute-start.13 = (bf16[48,2176]{1,0:T(8,128)(2,1)S(1)}, bf16[48,2176]{1,0:T(8,128)(2,1)S(1)}, u32[]{:S(2)}, u32[]{:S(2)}) collective-permute-start(bf16[48,2176]{1,0:T(8,128)(2,1)S(1)} %slice.45), channel_id=1, source_target_pairs={{0,16},{8,24},{16,0},{24,8},{1,17},{9,25},{17,1},{25,9},{2,18},{10... | collective-permute-start | bytes 626696 | tf_op jit(solution)/shard_map/ppermute | solution.py:304
  66.8 18.4 %collective-permute-start.20 = (bf16[112,2176]{1,0:T(8,128)(2,1)S(1)}, bf16[112,2176]{1,0:T(8,128)(2,1)S(1)}, u32[]{:S(2)}, u32[]{:S(2)}) collective-permute-start(bf16[112,2176]{1,0:T(8,128)(2,1)S(1)} %slice.49.refs_2_), channel_id=1, source_target_pairs={{0,8},{8,0},{16,24},{24,16},{1,9},{9,1},{17,25},{25,17},{2,10},{10... | collective-permute-start | bytes 1462280 | tf_op jit(solution)/shard_map/ppermute | solution.py:300
  68.4 16.8 %collective-permute-start.21 = (bf16[112,2176]{1,0:T(8,128)(2,1)S(1)}, bf16[112,2176]{1,0:T(8,128)(2,1)S(1)}, u32[]{:S(2)}, u32[]{:S(2)}) collective-permute-start(bf16[112,2176]{1,0:T(8,128)(2,1)S(1)} %slice.49.refs_2_), channel_id=1, source_target_pairs={{0,16},{8,24},{16,0},{24,8},{1,17},{9,25},{17,1},{25,9},{2,18},{10... | collective-permute-start | bytes 1462280 | tf_op jit(solution)/shard_map/ppermute | solution.py:304
  68.8 16.4 %collective-permute-start.18 = (bf16[64,2176]{1,0:T(8,128)(2,1)S(1)}, bf16[64,2176]{1,0:T(8,128)(2,1)S(1)}, u32[]{:S(2)}, u32[]{:S(2)}) collective-permute-start(bf16[64,2176]{1,0:T(8,128)(2,1)S(1)} %slice.47), channel_id=1, source_target_pairs={{0,16},{8,24},{16,0},{24,8},{1,17},{9,25},{17,1},{25,9},{2,18},{10... | collective-permute-start | bytes 835592 | tf_op jit(solution)/shard_map/ppermute | solution.py:304
  70.5 12.3 %collective-permute-start.19 = (bf16[48,2176]{1,0:T(8,128)(2,1)S(1)}, bf16[48,2176]{1,0:T(8,128)(2,1)S(1)}, u32[]{:S(2)}, u32[]{:S(2)}) collective-permute-start(bf16[48,2176]{1,0:T(8,128)(2,1)S(1)} %slice.48), channel_id=1, source_target_pairs={{0,8},{8,0},{16,24},{24,16},{1,9},{9,1},{17,25},{25,17},{2,10},{10... | collective-permute-start | bytes 626696 | tf_op jit(solution)/shard_map/ppermute | solution.py:300
  71.1 11.7 %collective-permute-start.22 = (bf16[16,2176]{1,0:T(8,128)(2,1)S(1)}, bf16[16,2176]{1,0:T(8,128)(2,1)S(1)}, u32[]{:S(2)}, u32[]{:S(2)}) collective-permute-start(bf16[16,2176]{1,0:T(8,128)(2,1)S(1)} %slice.50.refs_1_), channel_id=1, source_target_pairs={{0,2},{1,3},{2,4},{3,5},{4,6},{5,7},{6,0},{7,1},{8,10},{9,11},{10,... | collective-permute-start | bytes 208904 | tf_op jit(solution)/shard_map/ppermute | solution.py:308
  85.3 16.1 %collective-permute-start.24 = (bf16[64,2176]{1,0:T(8,128)(2,1)S(1)}, bf16[64,2176]{1,0:T(8,128)(2,1)S(1)}, u32[]{:S(2)}, u32[]{:S(2)}) collective-permute-start(bf16[64,2176]{1,0:T(8,128)(2,1)S(1)} %slice.52), channel_id=1, source_target_pairs={{0,8},{8,0},{16,24},{24,16},{1,9},{9,1},{17,25},{25,17},{2,10},{10... | collective-permute-start | bytes 835592 | tf_op jit(solution)/shard_map/ppermute | solution.py:300
  85.4 16.0 %collective-permute-start.23 = (bf16[48,2176]{1,0:T(8,128)(2,1)S(1)}, bf16[48,2176]{1,0:T(8,128)(2,1)S(1)}, u32[]{:S(2)}, u32[]{:S(2)}) collective-permute-start(bf16[48,2176]{1,0:T(8,128)(2,1)S(1)} %slice.51), channel_id=1, source_target_pairs={{0,16},{8,24},{16,0},{24,8},{1,17},{9,25},{17,1},{25,9},{2,18},{10... | collective-permute-start | bytes 626696 | tf_op jit(solution)/shard_map/ppermute | solution.py:304
  85.7 15.7 %collective-permute-start.27 = (bf16[64,2048]{1,0:T(8,128)(2,1)S(1)}, bf16[64,2048]{1,0:T(8,128)(2,1)S(1)}, u32[]{:S(2)}, u32[]{:S(2)}) collective-permute-start(bf16[64,2048]{1,0:T(8,128)(2,1)S(1)} %get-tuple-element.173), channel_id=1, source_target_pairs={{0,8},{8,0},{16,24},{24,16},{1,9},{9,1},{17,25},{25,17},{2,10},{10... | collective-permute-start | bytes 786440 | tf_op jit(solution)/shard_map/ppermute | solution.py:300
  87.7 13.7 %collective-permute-start.26 = (bf16[48,2048]{1,0:T(8,128)(2,1)S(1)}, bf16[48,2048]{1,0:T(8,128)(2,1)S(1)}, u32[]{:S(2)}, u32[]{:S(2)}) collective-permute-start(bf16[48,2048]{1,0:T(8,128)(2,1)S(1)} %get-tuple-element.172), channel_id=1, source_target_pairs={{0,16},{8,24},{16,0},{24,8},{1,17},{9,25},{17,1},{25,9},{2,18},{10... | collective-permute-start | bytes 589832 | tf_op jit(solution)/shard_map/ppermute | solution.py:304
  89.5 11.9 %collective-permute-start.25 = (bf16[16,2176]{1,0:T(8,128)(2,1)S(1)}, bf16[16,2176]{1,0:T(8,128)(2,1)S(1)}, u32[]{:S(2)}, u32[]{:S(2)}) collective-permute-start(bf16[16,2176]{1,0:T(8,128)(2,1)S(1)} %collective-permute-done.22.refs_1_), channel_id=1, source_target_pairs={{0,2},{1,3},{2,4},{3,5},{4,6},{5,7},{6,0},{7,1},{8,10},{9,11},{10,... | collective-permute-start | bytes 208904 | tf_op jit(solution)/shard_map/ppermute | solution.py:308
  101.5 16.3 %collective-permute-start.28 = (bf16[112,2048]{1,0:T(8,128)(2,1)S(1)}, bf16[112,2048]{1,0:T(8,128)(2,1)S(1)}, u32[]{:S(2)}, u32[]{:S(2)}) collective-permute-start(bf16[112,2048]{1,0:T(8,128)(2,1)S(1)} %get-tuple-element.188), channel_id=1, source_target_pairs={{0,8},{8,0},{16,24},{24,16},{1,9},{9,1},{17,25},{25,17},{2,10},{10... | collective-permute-start | bytes 1376264 | tf_op jit(solution)/shard_map/ppermute | solution.py:300
  102.0 15.8 %collective-permute-start.29 = (bf16[112,2048]{1,0:T(8,128)(2,1)S(1)}, bf16[112,2048]{1,0:T(8,128)(2,1)S(1)}, u32[]{:S(2)}, u32[]{:S(2)}) collective-permute-start(bf16[112,2048]{1,0:T(8,128)(2,1)S(1)} %get-tuple-element.189), channel_id=1, source_target_pairs={{0,16},{8,24},{16,0},{24,8},{1,17},{9,25},{17,1},{25,9},{2,18},{10... | collective-permute-start | bytes 1376264 | tf_op jit(solution)/shard_map/ppermute | solution.py:304
  102.4 15.4 %collective-permute-start.30 = (bf16[64,2048]{1,0:T(8,128)(2,1)S(1)}, bf16[64,2048]{1,0:T(8,128)(2,1)S(1)}, u32[]{:S(2)}, u32[]{:S(2)}) collective-permute-start(bf16[64,2048]{1,0:T(8,128)(2,1)S(1)} %get-tuple-element.190), channel_id=1, source_target_pairs={{0,16},{8,24},{16,0},{24,8},{1,17},{9,25},{17,1},{25,9},{2,18},{10... | collective-permute-start | bytes 786440 | tf_op jit(solution)/shard_map/ppermute | solution.py:304
  104.0 13.7 %collective-permute-start.31 = (bf16[48,2048]{1,0:T(8,128)(2,1)S(1)}, bf16[48,2048]{1,0:T(8,128)(2,1)S(1)}, u32[]{:S(2)}, u32[]{:S(2)}) collective-permute-start(bf16[48,2048]{1,0:T(8,128)(2,1)S(1)} %get-tuple-element.191), channel_id=1, source_target_pairs={{0,8},{8,0},{16,24},{24,16},{1,9},{9,1},{17,25},{25,17},{2,10},{10... | collective-permute-start | bytes 589832 | tf_op jit(solution)/shard_map/ppermute | solution.py:300
  118.0 47.2 %copy-start.4 = (bf16[1,111,2048]{2,1,0:T(8,128)(2,1)S(1)}, bf16[1,111,2048]{2,1,0:T(8,128)(2,1)}, u32[]{:S(2)}) copy-start(bf16[1,111,2048]{2,1,0:T(8,128)(2,1)} %param.21) | copy-start | bytes 1363972
  118.0 16.3 %collective-permute-start.36 = (bf16[112,2048]{1,0:T(8,128)(2,1)S(1)}, bf16[112,2048]{1,0:T(8,128)(2,1)S(1)}, u32[]{:S(2)}, u32[]{:S(2)}) collective-permute-start(bf16[112,2048]{1,0:T(8,128)(2,1)S(1)} %add_convert_fusion.3), channel_id=1, source_target_pairs={{0,2},{1,3},{2,4},{3,5},{4,6},{5,7},{6,0},{7,1},{8,10},{9,11},{10,... | collective-permute-start | bytes 1376264 | tf_op jit(solution)/shard_map/ppermute | solution.py:308
  119.4 14.9 %collective-permute-start.32 = (bf16[112,2048]{1,0:T(8,128)(2,1)S(1)}, bf16[112,2048]{1,0:T(8,128)(2,1)S(1)}, u32[]{:S(2)}, u32[]{:S(2)}) collective-permute-start(bf16[112,2048]{1,0:T(8,128)(2,1)S(1)} %get-tuple-element.208), channel_id=1, source_target_pairs={{0,8},{8,0},{16,24},{24,16},{1,9},{9,1},{17,25},{25,17},{2,10},{10... | collective-permute-start | bytes 1376264 | tf_op jit(solution)/shard_map/ppermute | solution.py:300
  121.0 13.4 %collective-permute-start.33 = (bf16[112,2048]{1,0:T(8,128)(2,1)S(1)}, bf16[112,2048]{1,0:T(8,128)(2,1)S(1)}, u32[]{:S(2)}, u32[]{:S(2)}) collective-permute-start(bf16[112,2048]{1,0:T(8,128)(2,1)S(1)} %get-tuple-element.209), channel_id=1, source_target_pairs={{0,16},{8,24},{16,0},{24,8},{1,17},{9,25},{17,1},{25,9},{2,18},{10... | collective-permute-start | bytes 1376264 | tf_op jit(solution)/shard_map/ppermute | solution.py:304
  121.8 12.5 %collective-permute-start.35 = (bf16[64,2048]{1,0:T(8,128)(2,1)S(1)}, bf16[64,2048]{1,0:T(8,128)(2,1)S(1)}, u32[]{:S(2)}, u32[]{:S(2)}) collective-permute-start(bf16[64,2048]{1,0:T(8,128)(2,1)S(1)} %get-tuple-element.211), channel_id=1, source_target_pairs={{0,8},{8,0},{16,24},{24,16},{1,9},{9,1},{17,25},{25,17},{2,10},{10... | collective-permute-start | bytes 786440 | tf_op jit(solution)/shard_map/ppermute | solution.py:300
  122.3 12.0 %collective-permute-start.34 = (bf16[48,2048]{1,0:T(8,128)(2,1)S(1)}, bf16[48,2048]{1,0:T(8,128)(2,1)S(1)}, u32[]{:S(2)}, u32[]{:S(2)}) collective-permute-start(bf16[48,2048]{1,0:T(8,128)(2,1)S(1)} %get-tuple-element.210), channel_id=1, source_target_pairs={{0,16},{8,24},{16,0},{24,8},{1,17},{9,25},{17,1},{25,9},{2,18},{10... | collective-permute-start | bytes 589832 | tf_op jit(solution)/shard_map/ppermute | solution.py:304
  134.6 18.8 %collective-permute-start.41 = (bf16[112,2048]{1,0:T(8,128)(2,1)S(1)}, bf16[112,2048]{1,0:T(8,128)(2,1)S(1)}, u32[]{:S(2)}, u32[]{:S(2)}) collective-permute-start(bf16[112,2048]{1,0:T(8,128)(2,1)S(1)} %add_convert_fusion.2), channel_id=1, source_target_pairs={{0,2},{1,3},{2,4},{3,5},{4,6},{5,7},{6,0},{7,1},{8,10},{9,11},{10,... | collective-permute-start | bytes 1376264 | tf_op jit(solution)/shard_map/ppermute | solution.py:308
  135.7 17.7 %collective-permute-start.37 = (bf16[112,2048]{1,0:T(8,128)(2,1)S(1)}, bf16[112,2048]{1,0:T(8,128)(2,1)S(1)}, u32[]{:S(2)}, u32[]{:S(2)}) collective-permute-start(bf16[112,2048]{1,0:T(8,128)(2,1)S(1)} %get-tuple-element.228), channel_id=1, source_target_pairs={{0,8},{8,0},{16,24},{24,16},{1,9},{9,1},{17,25},{25,17},{2,10},{10... | collective-permute-start | bytes 1376264 | tf_op jit(solution)/shard_map/ppermute | solution.py:300
  137.2 16.2 %collective-permute-start.38 = (bf16[112,2048]{1,0:T(8,128)(2,1)S(1)}, bf16[112,2048]{1,0:T(8,128)(2,1)S(1)}, u32[]{:S(2)}, u32[]{:S(2)}) collective-permute-start(bf16[112,2048]{1,0:T(8,128)(2,1)S(1)} %get-tuple-element.229), channel_id=1, source_target_pairs={{0,16},{8,24},{16,0},{24,8},{1,17},{9,25},{17,1},{25,9},{2,18},{10... | collective-permute-start | bytes 1376264 | tf_op jit(solution)/shard_map/ppermute | solution.py:304
  137.6 15.8 %collective-permute-start.39 = (bf16[64,2048]{1,0:T(8,128)(2,1)S(1)}, bf16[64,2048]{1,0:T(8,128)(2,1)S(1)}, u32[]{:S(2)}, u32[]{:S(2)}) collective-permute-start(bf16[64,2048]{1,0:T(8,128)(2,1)S(1)} %get-tuple-element.230), channel_id=1, source_target_pairs={{0,16},{8,24},{16,0},{24,8},{1,17},{9,25},{17,1},{25,9},{2,18},{10... | collective-permute-start | bytes 786440 | tf_op jit(solution)/shard_map/ppermute | solution.py:304
  139.2 11.6 %collective-permute-start.40 = (bf16[48,2048]{1,0:T(8,128)(2,1)S(1)}, bf16[48,2048]{1,0:T(8,128)(2,1)S(1)}, u32[]{:S(2)}, u32[]{:S(2)}) collective-permute-start(bf16[48,2048]{1,0:T(8,128)(2,1)S(1)} %get-tuple-element.231), channel_id=1, source_target_pairs={{0,8},{8,0},{16,24},{24,16},{1,9},{9,1},{17,25},{25,17},{2,10},{10... | collective-permute-start | bytes 589832 | tf_op jit(solution)/shard_map/ppermute | solution.py:300
  153.6 8.5 %collective-permute-start.42 = (bf16[112,2048]{1,0:T(8,128)(2,1)S(1)}, bf16[112,2048]{1,0:T(8,128)(2,1)S(1)}, u32[]{:S(2)}, u32[]{:S(2)}) collective-permute-start(bf16[112,2048]{1,0:T(8,128)(2,1)S(1)} %get-tuple-element.245), channel_id=1, source_target_pairs={{0,8},{8,0},{16,24},{24,16},{1,9},{9,1},{17,25},{25,17},{2,10},{10... | collective-permute-start | bytes 1376264 | tf_op jit(solution)/shard_map/ppermute | solution.py:300
  154.2 8.5 %collective-permute-start.43 = (bf16[112,2048]{1,0:T(8,128)(2,1)S(1)}, bf16[112,2048]{1,0:T(8,128)(2,1)S(1)}, u32[]{:S(2)}, u32[]{:S(2)}) collective-permute-start(bf16[112,2048]{1,0:T(8,128)(2,1)S(1)} %get-tuple-element.246), channel_id=1, source_target_pairs={{0,16},{8,24},{16,0},{24,8},{1,17},{9,25},{17,1},{25,9},{2,18},{10... | collective-permute-start | bytes 1376264 | tf_op jit(solution)/shard_map/ppermute | solution.py:304
  154.8 10.4 %collective-permute-start.44 = (bf16[112,2048]{1,0:T(8,128)(2,1)S(1)}, bf16[112,2048]{1,0:T(8,128)(2,1)S(1)}, u32[]{:S(2)}, u32[]{:S(2)}) collective-permute-start(bf16[112,2048]{1,0:T(8,128)(2,1)S(1)} %add_convert_fusion.1), channel_id=1, source_target_pairs={{0,2},{1,3},{2,4},{3,5},{4,6},{5,7},{6,0},{7,1},{8,10},{9,11},{10,... | collective-permute-start | bytes 1376264 | tf_op jit(solution)/shard_map/ppermute | solution.py:308

commit v5 on v4

--- a/solution.py
+++ b/solution.py
@@ -43,51 +43,62 @@
     )
 
 
-def prepare_kernel(ranking, hidden_ref, gain_ref, router_ref, routes_ref, out_ref):
-    width = hidden_ref.shape[1]
-    experts = router_ref.shape[1]
-    hidden = hidden_ref[...].astype(jnp.float32)
+def prepare_kernel(ranking, hidden_ref, gain_ref, router_ref, routes_ref, out_ref, *scratch):
+    experts, width = router_ref.shape
+    if scratch:
+        (shifted,) = scratch
+        shifted[0:1, :] = jnp.zeros((1, width), jnp.float32)
+        shifted[1:, :] = hidden_ref[...].astype(jnp.float32)
+        hidden = shifted[...]
+    else:
+        hidden = hidden_ref[...].astype(jnp.float32)
+    rows = hidden.shape[0]
     mean_sq = jnp.mean(hidden * hidden, axis=1, keepdims=True)
     normed = (hidden * lax.rsqrt(mean_sq + EPSILON) * gain_ref[...]).astype(jnp.bfloat16)
     out_ref[:, :width] = normed
-    logits = jnp.dot(normed, router_ref[...], preferred_element_type=jnp.float32)
-    lane = lax.broadcasted_iota(jnp.int32, logits.shape, 1)
+    by_lanes = (((1,), (1,)), ((), ()))
+    logits = lax.dot_general(normed, router_ref[...], by_lanes, preferred_element_type=jnp.float32)
+    expert = lax.broadcasted_iota(jnp.int32, (experts, rows), 0)
     routes = routes_ref[...]
-    chosen = jnp.zeros(logits.shape, jnp.bool_)
-    for k in range(routes.shape[1]):
-        chosen = chosen | (lane == routes[:, k : k + 1])
-    top = jnp.max(jnp.where(chosen, logits, NEG_FILL), axis=1, keepdims=True)
-    raised = jnp.where(chosen, jnp.exp(jnp.minimum(logits - top, 0.0)), 0.0)
+    chosen = jnp.zeros(expert.shape, jnp.bool_)
+    for k in range(routes.shape[0]):
+        chosen = chosen | (expert == routes[k : k + 1, :])
+    chosen = jnp.where(chosen, 1.0, 0.0).astype(jnp.bfloat16)
+    row = lax.broadcasted_iota(jnp.int32, (rows, rows), 0)
+    other = lax.broadcasted_iota(jnp.int32, (rows, rows), 1)
+
+    def of_rows(taken):
+        taken = jnp.where(taken, 1.0, 0.0).astype(jnp.bfloat16)
+        return lax.dot_general(taken, chosen, by_lanes, preferred_element_type=jnp.float32)
+
+    mine = of_rows(row == other) > 0.5
+    top = jnp.max(jnp.where(mine, logits, NEG_FILL), axis=1, keepdims=True)
+    raised = jnp.where(mine, jnp.exp(jnp.minimum(logits - top, 0.0)), 0.0)
     gates = raised / jnp.sum(raised, axis=1, keepdims=True)
     high = gates.astype(jnp.bfloat16).astype(jnp.float32)
     parts = [high, gates - high]
     if ranking == "block":
-        rows = logits.shape[0]
-        row = lax.broadcasted_iota(jnp.int32, (rows, rows), 0)
-        earlier = lax.broadcasted_iota(jnp.int32, (rows, rows), 1) < row
-        ranks = jnp.dot(
-            jnp.where(earlier, 1.0, 0.0).astype(jnp.bfloat16),
-            jnp.where(chosen, 1.0, 0.0).astype(jnp.bfloat16),
-            preferred_element_type=jnp.float32,
-        )
-        parts.append(jnp.where(chosen, ranks, NOT_CHOSEN))
+        parts.append(jnp.where(mine, of_rows(other < row), NOT_CHOSEN))
     elif ranking == "first":
-        parts.append(jnp.where(chosen, 0.0, NOT_CHOSEN))
+        parts.append(jnp.where(mine, 0.0, NOT_CHOSEN))
     rest = out_ref.shape[1] - width - len(parts) * experts
     if rest:
-        parts.append(jnp.zeros((high.shape[0], rest), jnp.float32))
+        parts.append(jnp.zeros((rows, rest), jnp.float32))
     out_ref[:, width:] = jnp.concatenate(parts, axis=1).astype(jnp.bfloat16)
 
 
 def prepare(hidden, norm_gain, router, routes, ranking=None):
-    rows, width = hidden.shape
+    width = hidden.shape[1]
+    rows = routes.shape[0]
     extra = -(-(3 if ranking else 2) * router.shape[1] // 128) * 128
+    shifted = rows > hidden.shape[0]
     return pl.pallas_call(
         functools.partial(prepare_kernel, ranking),
         out_shape=jax.ShapeDtypeStruct((rows, width + extra), jnp.bfloat16),
+        scratch_shapes=[pltpu.VMEM((rows, width), jnp.float32)] if shifted else [],
         compiler_params=pltpu.CompilerParams(vmem_limit_bytes=32 << 20),
         name="prepare",
-    )(hidden, norm_gain.reshape(1, width), router, routes)
+    )(hidden, norm_gain.reshape(1, width), router.T, routes.T)
 
 
 def expert_kernel(expert_ref, rows_ref, gate_ref, up_ref, down_ref, out_ref):
@@ -177,60 +188,76 @@
         (line == 1) & (lanes == ids_ref[1] + 2 * experts)
     )
     wanted = jnp.where(wanted, 1.0, 0.0).astype(jnp.bfloat16)
+    pairs = [pl.ds(p * pair_rows, pair_rows) for p in range(2)]
+
+    def shift_of(shape, axis):
+        second = lax.broadcasted_iota(jnp.int32, shape, axis) >= tokens
+        return jnp.where(second, float(cap), 0.0)
+
     for p in range(2):
-        part = pl.ds(p * pair_rows, pair_rows)
-        tail = rows[part, width:]
         ranks = lax.dot_general(
-            wanted, tail, (((1,), (1,)), ((), ())), preferred_element_type=jnp.float32
+            wanted, rows[pairs[p], width:], (((1,), (1,)), ((), ())), preferred_element_type=jnp.float32
         )
-        second = lax.broadcasted_iota(jnp.int32, (1, pair_rows), 1) >= tokens
-        shift = jnp.where(second, float(cap), 0.0)
+        ranks += shift_of(ranks.shape, 1)
         slot = lax.broadcasted_iota(jnp.int32, (2 * pair_slots, pair_rows), 0).astype(jnp.float32)
-        taken = (slot == ranks[0:1] + shift) | (slot == ranks[1:2] + shift + float(pair_slots))
+        taken = (slot == ranks[0:1]) | (slot == ranks[1:2] + float(pair_slots))
         taken = jnp.where(taken, 1.0, 0.0).astype(jnp.bfloat16)
-        picked = jnp.dot(taken, rows[part, :], preferred_element_type=jnp.float32)
+        picked = jnp.dot(taken, rows[pairs[p], :], preferred_element_type=jnp.float32)
         picked = picked.astype(jnp.bfloat16)
         for e in range(2):
             slots[e, pl.ds(p * pair_slots, pair_slots), :] = picked[e * pair_slots : (e + 1) * pair_slots]
-        tail = tail.astype(jnp.float32)
+
+    def make_spread(p):
+        tail = rows[pairs[p], width:].astype(jnp.float32)
         lane = lax.broadcasted_iota(jnp.int32, tail.shape, 1)
-        second = lax.broadcasted_iota(jnp.int32, (pair_rows, 1), 0) >= tokens
-        shift = jnp.where(second, float(cap), 0.0)
         slot = lax.broadcasted_iota(jnp.int32, (pair_rows, 2 * pair_slots), 1).astype(jnp.float32)
         back = jnp.zeros(slot.shape, jnp.bool_)
         for e in range(2):
             mine = lane == ids_ref[e] + 2 * experts
             rank = jnp.sum(jnp.where(mine, tail, 0.0), axis=1, keepdims=True)
-            back = back | (slot == rank + shift + float(e * pair_slots))
+            back = back | (slot == rank + shift_of(rank.shape, 0) + float(e * pair_slots))
         spread[p] = jnp.where(back, 1.0, 0.0).astype(jnp.bfloat16)
 
-    for e in range(2):
+    def weight_of(e):
         tail = slots[e, :, width:].astype(jnp.float32)
         lane = lax.broadcasted_iota(jnp.int32, tail.shape, 1)
         mine = (lane == ids_ref[e]) | (lane == ids_ref[e] + experts)
-        weight = jnp.sum(jnp.where(mine, tail, 0.0), axis=1, keepdims=True)
-        up_copies[2 * e].wait()
-        gate_act = jnp.dot(
-            slots[e, :, :width], weights[2 * e], preferred_element_type=jnp.float32
-        )
-        up_copies[2 * e + 1].wait()
-        up_act = jnp.dot(
-            slots[e, :, :width], weights[2 * e + 1], preferred_element_type=jnp.float32
-        )
-        act = gate_act / (1.0 + jnp.exp(-gate_act)) * up_act * weight
+        return jnp.sum(jnp.where(mine, tail, 0.0), axis=1, keepdims=True)
+
+    def product(e, i):
+        return jnp.dot(slots[e, :, :width], weights[2 * e + i], preferred_element_type=jnp.float32)
+
+    def activate(e, gate_act, up_act):
+        act = gate_act / (1.0 + jnp.exp(-gate_act)) * up_act * weight_of(e)
         inner[e] = act.astype(jnp.bfloat16)
-    for e in range(2):
-        down_copies[e].wait()
+
+    def finish(e):
         result = jnp.dot(inner[e], downs[e], preferred_element_type=jnp.float32)
         result = result.astype(jnp.bfloat16)
         for p in range(2):
             results[p, pl.ds(e * pair_slots, pair_slots), :] = result[p * pair_slots : (p + 1) * pair_slots]
+
+    up_copies[0].wait()
+    gate_0 = product(0, 0)
+    make_spread(0)
+    up_copies[1].wait()
+    up_0 = product(0, 1)
+    make_spread(1)
+    up_copies[2].wait()
+    activate(0, gate_0, up_0)
+    gate_1 = product(1, 0)
+    up_copies[3].wait()
+    up_1 = product(1, 1)
+    down_copies[0].wait()
+    finish(0)
+    activate(1, gate_1, up_1)
+    down_copies[1].wait()
+    finish(1)
     out_copies = []
     at = 0
     for p in range(2):
-        part = pl.ds(p * pair_rows, pair_rows)
         total = jnp.dot(spread[p], results[p], preferred_element_type=jnp.float32)
-        sums[part, :] = total.astype(jnp.bfloat16)
+        sums[pairs[p], :] = total.astype(jnp.bfloat16)
         while len(out_copies) < len(targets) and at < (p + 1) * pair_rows:
             count = block_rows[len(out_copies)]
             copy = pltpu.make_async_copy(
@@ -302,6 +329,10 @@
 
 def along_y(value):
     return lax.ppermute(value, "kv", [(i, i ^ 2) for i in range(4)])
+
+
+def along_diagonal(value):
+    return lax.ppermute(value, "kv", [(i, i ^ 3) for i in range(4)])
 
 
 def around_z(value):
@@ -379,14 +410,12 @@
         back[step] = along_x(to_x), along_y(to_y)
 
     prefill = prefill_hidden[0]
-    nothing = jnp.zeros((1, prefill.shape[1]), prefill.dtype)
-    blocks[0] = prepare(
-        jnp.concatenate([nothing, prefill], axis=0), norm_gain, router, ids, "block"
-    )
+    blocks[0] = prepare(prefill, norm_gain, router, ids, "block")
     blocks[0], queries, cache_keys, expert_gate, expert_up = fence(
         blocks[0], queries, cache_keys, expert_gate, expert_up
     )
     spread_sides(0)
+    corners[0] = (along_diagonal(blocks[0]),)
     blocks[1] = around_z(blocks[0])
     other_gate = across_chip(expert_gate[0])
     other_up = across_chip(expert_up[0])
@@ -401,14 +430,13 @@
 
     shared, other_gate = fence(shared, other_gate)
     shared = shared + along_x(shared)
-    sides[0], blocks[1], shared, expert_down = fence(sides[0], blocks[1], shared, expert_down)
+    sides[0], corners[0], blocks[1], shared, expert_down = fence(
+        sides[0], corners[0], blocks[1], shared, expert_down
+    )
 
     spread_sides(1)
     blocks[2] = around_z(blocks[1])
     other_down = across_chip(expert_down[0])
-    sides[1], sides[0], blocks[2], shared = fence(sides[1], sides[0], blocks[2], shared)
-
-    spread_corners(0)
     shared = shared + along_y(shared)
     order = [my_kv ^ j for j in range(4)]
     decoded = jnp.concatenate(
@@ -425,9 +453,7 @@
         jnp.pad(decode_ids, ((0, 12), (0, 0))),
         "first",
     )
-    corners[0], sides[1], blocks[2], decodes[0], other_up, other_down = fence(
-        corners[0], sides[1], blocks[2], decodes[0], other_up, other_down
-    )
+    sides[1], blocks[2], decodes[0], other_up = fence(sides[1], blocks[2], decodes[0], other_up)
     weights = (expert_gate[0], expert_up[0], expert_down[0], other_gate, other_up, other_down)
 
     spread_corners(1)

time: 167 us -> 174 us (1.042)
  local copies, waits for them, and re-layouts: 4.14 us -> 7.31 us
  starting transfers between devices: 45.3 us -> 48 us
    unnamed x14 -> x28, local copies, waits for them, and re-layouts: 2.74 us -> 7.01 us
    ppermute x17 -> x16, waiting for transfers between devices: 20.4 us -> 17.5 us  [along_y(): return lax.ppermute(value, 'kv', [(i, i ^ 2) for i in range(4)])]
    ppermute x17 -> x16, waiting for transfers between devices: 32.3 us -> 35.1 us  [along_x(): return lax.ppermute(value, 'kv', [(i, i ^ 1) for i in range(4)])]
    ppermute x17 -> x16, starting transfers between devices: 19 us -> 20.3 us  [along_x(): return lax.ppermute(value, 'kv', [(i, i ^ 1) for i in range(4)])]
    ppermute x17 -> x16, starting transfers between devices: 16.7 us -> 17.3 us  [along_y(): return lax.ppermute(value, 'kv', [(i, i ^ 2) for i in range(4)])]
  transfers between devices with their start and end apart: 45 -> 44, of which waited for: 16 -> 11; matrix products, arithmetic and copies ran while one was open for 5% -> 5% of each run, Pallas kernels for 29% -> 28%
where the time goes in v5:
time: 174 us
  waiting for transfers between devices  58.5 us (34%)
  Pallas kernels  50.1 us (29%)
  starting transfers between devices  48 us (28%)
  local copies, waits for them, and re-layouts  7.31 us (4%)
  matrix products  5.14 us (3%)
  other arithmetic  4.33 us (2%)
    pallas_call x4, Pallas kernels, run_plane(): pl.pallas_call(functools.partial(plane_kernel, cap, piece_rows, block_row...  48.4 us
    ppermute x16, waiting for transfers between devices, along_x(): return lax.ppermute(value, 'kv', [(i, i ^ 1) for i in range(4)])  35.1 us
    ppermute x16, starting transfers between devices, along_x(): return lax.ppermute(value, 'kv', [(i, i ^ 1) for i in range(4)])  20.3 us
    ppermute x16, waiting for transfers between devices, along_y(): return lax.ppermute(value, 'kv', [(i, i ^ 2) for i in range(4)])  17.5 us
    ppermute x16, starting transfers between devices, along_y(): return lax.ppermute(value, 'kv', [(i, i ^ 2) for i in range(4)])  17.3 us
    ppermute x8, starting transfers between devices, around_z(): return lax.ppermute(value, 'blk', [(i, (i + 2) % 8) for i in range(8)])  9.79 us
    unnamed x28, local copies, waits for them, and re-layouts  7.01 us
    ppermute x8, waiting for transfers between devices, around_z(): return lax.ppermute(value, 'blk', [(i, (i + 2) % 8) for i in range(8)])  5.94 us
  transfers between devices with their start and end apart: 44, of which 11 were waited for; matrix products, arithmetic and copies ran while one was open for 5% of the time, Pallas kernels for 28%

profile of v5, /device:TPU:0, one launch (start us, length us, event | category | flops | bytes accessed | tf_op | source)
XLA Modules:
  0.0 173.9 jit_solution(5880620992150440542)
XLA Ops:
  0.0 1.0 copy-done
  1.0 0.9 copy-done.2
  1.9 0.7 copy-done.4
  2.6 0.7 copy-done.6
  3.3 0.8 prepare.2.refs_2_
  4.1 3.0 %collective-permute-start = (bf16[112,2176]{1,0:T(8,128)(2,1)S(1)}, bf16[112,2176]{1,0:T(8,128)(2,1)S(1)}, u32[]{:S(2)}, u32[]{:S(2)}) collective-permute-start(bf16[112,2176]{1,0:T(8,128)(2,1)S(1)} %prepare.2.refs_2_), channel_id=1, source_target_pairs={{0,8},{8,0},{16,24},{24,16},{1,9},{9,1},{17,25},{25,17},{2,10},{10... | collective-permute-start | bytes 1462280 | tf_op jit(solution)/shard_map/ppermute | solution.py:327
  7.1 1.5 collective-permute-start.1
  8.6 2.0 %collective-permute-start.3 = (bf16[112,2176]{1,0:T(8,128)(2,1)S(1)}, bf16[112,2176]{1,0:T(8,128)(2,1)S(1)}, u32[]{:S(2)}, u32[]{:S(2)}) collective-permute-start(bf16[112,2176]{1,0:T(8,128)(2,1)S(1)} %prepare.2.refs_2_), channel_id=1, source_target_pairs={{0,2},{1,3},{2,4},{3,5},{4,6},{5,7},{6,0},{7,1},{8,10},{9,11},{10,... | collective-permute-start | bytes 1462280 | tf_op jit(solution)/shard_map/ppermute | solution.py:339
  10.8 0.7 broadcast_in_dim.76
  11.5 0.9 minimum_subtract_fusion
  12.5 3.8 %fusion.33 = (f32[4,8]{1,0:T(4,128)S(1)}, f32[4,8,4096]{2,1,0:T(8,128)S(1)}) fusion(bf16[4,4096,1,128]{3,1,2,0:T(8,128)(2,1)} %param.15, bf16[1,4,8,128]{3,1,2,0:T(4,128)(2,1)} %bitcast.53, pred[4,4096]{1,0:T(4,128)(4,1)S(1)} %iota_compare_fusion.1), kind=kOutput, calls=%fused_computation.56 | convolution fusion | flops 33947616 | bytes 4743296 | tf_op jit(solution)/shard_map/rgd,rjd->rgj/dot_general | solution.py:27
  16.6 0.7 fusion.10
  17.3 0.7 convolution_add_fusion
  18.1 1.6 collective-permute-start.5
  19.7 10.5 %collective-permute-done.5 = f32[8,2048]{1,0:T(8,128)S(1)} collective-permute-done((f32[8,2048]{1,0:T(8,128)S(1)}, f32[8,2048]{1,0:T(8,128)S(1)}, u32[]{:S(2)}, u32[]{:S(2)}) %collective-permute-start.5) | collective-permute-done | bytes 65568 | tf_op jit(solution)/shard_map/ppermute | solution.py:327
  30.2 0.8 copy-done.7
  31.0 0.8 copy-done.9
  32.3 1.8 %collective-permute-start.6 = (f32[8,2048]{1,0:T(8,128)S(1)}, f32[8,2048]{1,0:T(8,128)S(1)}, u32[]{:S(2)}, u32[]{:S(2)}) collective-permute-start(f32[8,2048]{1,0:T(8,128)S(1)} %add.114), channel_id=1, source_target_pairs={{0,16},{8,24},{16,0},{24,8},{1,17},{9,25},{17,1},{25,9},{2,18},{10... | collective-permute-start | bytes 196616 | tf_op jit(solution)/shard_map/ppermute | solution.py:331
  34.1 1.4 collective-permute-start.7
  35.6 0.5 collective-permute-start.8
  36.5 1.8 %collective-permute-start.9 = (bf16[112,2176]{1,0:T(8,128)(2,1)S(1)}, bf16[112,2176]{1,0:T(8,128)(2,1)S(1)}, u32[]{:S(2)}, u32[]{:S(2)}) collective-permute-start(bf16[112,2176]{1,0:T(8,128)(2,1)S(1)} %collective-permute-done.3.refs_2_), channel_id=1, source_target_pairs={{0,2},{1,3},{2,4},{3,5},{4,6},{5,7},{6,0},{7,1},{8,10},{9,11},{10,... | collective-permute-start | bytes 1462280 | tf_op jit(solution)/shard_map/ppermute | solution.py:339
  39.1 7.8 %collective-permute-done.7.refs_3_ = bf16[112,2176]{1,0:T(8,128)(2,1)S(1)} collective-permute-done((bf16[112,2176]{1,0:T(8,128)(2,1)S(1)}, bf16[112,2176]{1,0:T(8,128)(2,1)S(1)}, u32[]{:S(2)}, u32[]{:S(2)}) %collective-permute-start.7) | collective-permute-done | bytes 487456 | tf_op jit(solution)/shard_map/ppermute | solution.py:327
  46.9 1.2 collective-permute-done.8.refs_4_
  48.1 2.5 %collective-permute-done.9.refs_2_ = bf16[112,2176]{1,0:T(8,128)(2,1)S(1)} collective-permute-done((bf16[112,2176]{1,0:T(8,128)(2,1)S(1)}, bf16[112,2176]{1,0:T(8,128)(2,1)S(1)}, u32[]{:S(2)}, u32[]{:S(2)}) %collective-permute-start.9) | collective-permute-done | bytes 487456 | tf_op jit(solution)/shard_map/ppermute | solution.py:339
  50.6 1.5 collective-permute-start.13
  52.0 1.5 collective-permute-start.14
  53.7 0.6 collective-permute-start.12
  54.3 0.6 collective-permute-start.11
  54.9 1.0 copy-done.8
  55.9 1.0 copy-done.10
  57.0 12.0 %plane.4 = (bf16[112,2048]{1,0:T(8,128)(2,1)S(1)}, bf16[112,2048]{1,0:T(8,128)(2,1)S(1)}, bf16[112,2048]{1,0:T(8,128)(2,1)S(1)}, bf16[64,2048]{1,0:T(8,128)(2,1)S(1)}, bf16[48,2048]{1,0:T(8,128)(2,1)S(1)}) custom-call(s32[3]{0:T(128)S(1)} %pad_add_fusion.refs_0_, bf16[16,2176]{1,0:T(8,128)(2,1)S(1)} %prepare.3.refs_1_, ...), custom_call_target="tpu_custom_call" | custom-call | flops 8455716864 | bytes 25165824 | tf_op jit(solution)/shard_map/plane/pallas_call | solution.py:280
  69.1 1.6 collective-permute-start.19
  70.7 1.5 collective-permute-start.20
  72.1 0.6 collective-permute-start.17
  72.8 0.6 collective-permute-start.18
  73.4 1.3 collective-permute-start.21
  74.7 12.0 %plane.5 = (bf16[112,2048]{1,0:T(8,128)(2,1)S(1)}, bf16[112,2048]{1,0:T(8,128)(2,1)S(1)}, bf16[112,2048]{1,0:T(8,128)(2,1)S(1)}, bf16[48,2048]{1,0:T(8,128)(2,1)S(1)}, bf16[64,2048]{1,0:T(8,128)(2,1)S(1)}) custom-call(s32[3]{0:T(128)S(1)} %pad_add_fusion.refs_0_, bf16[16,2176]{1,0:T(8,128)(2,1)S(1)} %slice.42.refs_1_, ...), custom_call_target="tpu_custom_call" | custom-call | flops 8455716864 | bytes 25165824 | tf_op jit(solution)/shard_map/plane/pallas_call | solution.py:280
  86.8 1.6 collective-permute-start.23
  88.4 1.5 collective-permute-start.22
  89.9 0.6 collective-permute-start.26
  91.0 1.6 collective-permute-start.24
  92.6 12.0 %plane.6 = (bf16[112,2048]{1,0:T(8,128)(2,1)S(1)}, bf16[112,2048]{1,0:T(8,128)(2,1)S(1)}, bf16[112,2048]{1,0:T(8,128)(2,1)S(1)}, bf16[64,2048]{1,0:T(8,128)(2,1)S(1)}, bf16[48,2048]{1,0:T(8,128)(2,1)S(1)}) custom-call(s32[3]{0:T(128)S(1)} %pad_add_fusion.refs_0_, bf16[16,2176]{1,0:T(8,128)(2,1)S(1)} %collective-permute-done.21.refs_1_, ...), custom_call_target="tpu_custom_call" | custom-call | flops 8455716864 | bytes 25165824 | tf_op jit(solution)/shard_map/plane/pallas_call | solution.py:280
  104.8 1.6 collective-permute-start.27
  106.3 1.5 collective-permute-start.28
  107.8 0.5 collective-permute-start.29
  108.9 12.3 %plane.7 = (bf16[112,2048]{1,0:T(8,128)(2,1)S(1)}, bf16[112,2048]{1,0:T(8,128)(2,1)S(1)}, bf16[112,2048]{1,0:T(8,128)(2,1)S(1)}, bf16[48,2048]{1,0:T(8,128)(2,1)S(1)}, bf16[64,2048]{1,0:T(8,128)(2,1)S(1)}) custom-call(s32[3]{0:T(128)S(1)} %pad_add_fusion.refs_0_, bf16[16,2176]{1,0:T(8,128)(2,1)S(1)} %collective-permute-done.24.refs_1_, ...), custom_call_target="tpu_custom_call" | custom-call | flops 8455716864 | bytes 25165824 | tf_op jit(solution)/shard_map/plane/pallas_call | solution.py:280
  121.4 2.1 %collective-permute-start.35 = (bf16[112,2048]{1,0:T(8,128)(2,1)S(1)}, bf16[112,2048]{1,0:T(8,128)(2,1)S(1)}, u32[]{:S(2)}, u32[]{:S(2)}) collective-permute-start(bf16[112,2048]{1,0:T(8,128)(2,1)S(1)} %add_convert_fusion.3), channel_id=1, source_target_pairs={{0,2},{1,3},{2,4},{3,5},{4,6},{5,7},{6,0},{7,1},{8,10},{9,11},{10,... | collective-permute-start | bytes 1376264 | tf_op jit(solution)/shard_map/ppermute | solution.py:339
  123.7 1.6 collective-permute-start.31
  125.3 1.5 collective-permute-start.32
  126.7 0.6 collective-permute-start.34
  127.8 13.3 %collective-permute-done.33.passed_0_ref = bf16[48,2048]{1,0:T(8,128)(2,1)S(1)} collective-permute-done((bf16[48,2048]{1,0:T(8,128)(2,1)S(1)}, bf16[48,2048]{1,0:T(8,128)(2,1)S(1)}, u32[]{:S(2)}, u32[]{:S(2)}) %collective-permute-start.33) | collective-permute-done | bytes 196640 | tf_op jit(solution)/shard_map/ppermute | solution.py:331
  141.4 0.8 collective-permute-start.40
  142.4 1.0 collective-permute-start.36
  143.3 1.4 collective-permute-start.37
  144.7 0.6 collective-permute-start.38
  145.4 1.1 collective-permute-start.39
  146.5 11.4 %collective-permute-done.39.passed_1_ref = bf16[48,2048]{1,0:T(8,128)(2,1)S(1)} collective-permute-done((bf16[48,2048]{1,0:T(8,128)(2,1)S(1)}, bf16[48,2048]{1,0:T(8,128)(2,1)S(1)}, u32[]{:S(2)}, u32[]{:S(2)}) %collective-permute-start.39) | collective-permute-done | bytes 196640 | tf_op jit(solution)/shard_map/ppermute | solution.py:327
  157.9 1.2 collective-permute-done.38.passed_0_ref
  159.2 1.6 collective-permute-start.41
  160.8 1.3 collective-permute-start.42
  162.4 5.3 %collective-permute-done.41 = bf16[112,2048]{1,0:T(8,128)(2,1)S(1)} collective-permute-done((bf16[112,2048]{1,0:T(8,128)(2,1)S(1)}, bf16[112,2048]{1,0:T(8,128)(2,1)S(1)}, u32[]{:S(2)}, u32[]{:S(2)}) %collective-permute-start.41) | collective-permute-done | bytes 458784 | tf_op jit(solution)/shard_map/ppermute | solution.py:327
  167.8 1.5 collective-permute-done.42
  169.3 3.4 %collective-permute-done.43 = bf16[112,2048]{1,0:T(8,128)(2,1)S(1)} collective-permute-done((bf16[112,2048]{1,0:T(8,128)(2,1)S(1)}, bf16[112,2048]{1,0:T(8,128)(2,1)S(1)}, u32[]{:S(2)}, u32[]{:S(2)}) %collective-permute-start.43) | collective-permute-done | bytes 458784 | tf_op jit(solution)/shard_map/ppermute | solution.py:339
  172.7 1.2 fusion.13
  (98 shorter events, 5.6 us)
Async XLA Ops:
  0.0 16.3 %copy-start.13 = (f32[8]{0:T(128)S(1)}, f32[8]{0:T(128)}, u32[]{:S(2)}) copy-start(f32[8]{0:T(128)} %param.18) | copy-start | bytes 100
  0.0 1.0 copy-start
  1.0 0.9 copy-start.2
  1.9 0.7 copy-start.4
  2.6 0.7 copy-start.6
  4.1 26.0 %collective-permute-start = (bf16[112,2176]{1,0:T(8,128)(2,1)S(1)}, bf16[112,2176]{1,0:T(8,128)(2,1)S(1)}, u32[]{:S(2)}, u32[]{:S(2)}) collective-permute-start(bf16[112,2176]{1,0:T(8,128)(2,1)S(1)} %prepare.2.refs_2_), channel_id=1, source_target_pairs={{0,8},{8,0},{16,24},{24,16},{1,9},{9,1},{17,25},{25,17},{2,10},{10... | collective-permute-start | bytes 1462280 | tf_op jit(solution)/shard_map/ppermute | solution.py:327
  7.1 23.1 %collective-permute-start.1 = (bf16[112,2176]{1,0:T(8,128)(2,1)S(1)}, bf16[112,2176]{1,0:T(8,128)(2,1)S(1)}, u32[]{:S(2)}, u32[]{:S(2)}) collective-permute-start(bf16[112,2176]{1,0:T(8,128)(2,1)S(1)} %prepare.2.refs_2_), channel_id=1, source_target_pairs={{0,16},{8,24},{16,0},{24,8},{1,17},{9,25},{17,1},{25,9},{2,18},{10... | collective-permute-start | bytes 1462280 | tf_op jit(solution)/shard_map/ppermute | solution.py:331
  8.6 22.4 %collective-permute-start.2 = (bf16[112,2176]{1,0:T(8,128)(2,1)S(1)}, bf16[112,2176]{1,0:T(8,128)(2,1)S(1)}, u32[]{:S(2)}, u32[]{:S(2)}) collective-permute-start(bf16[112,2176]{1,0:T(8,128)(2,1)S(1)} %prepare.2.refs_2_), channel_id=1, source_target_pairs={{0,24},{8,16},{16,8},{24,0},{1,25},{9,17},{17,9},{25,1},{2,26},{10... | collective-permute-start | bytes 1462280 | tf_op jit(solution)/shard_map/ppermute | solution.py:335
  8.6 23.1 %collective-permute-start.3 = (bf16[112,2176]{1,0:T(8,128)(2,1)S(1)}, bf16[112,2176]{1,0:T(8,128)(2,1)S(1)}, u32[]{:S(2)}, u32[]{:S(2)}) collective-permute-start(bf16[112,2176]{1,0:T(8,128)(2,1)S(1)} %prepare.2.refs_2_), channel_id=1, source_target_pairs={{0,2},{1,3},{2,4},{3,5},{4,6},{5,7},{6,0},{7,1},{8,10},{9,11},{10,... | collective-permute-start | bytes 1462280 | tf_op jit(solution)/shard_map/ppermute | solution.py:339
  10.7 7.4 %collective-permute-start.4 = (bf16[2048,768]{1,0:T(8,128)(2,1)}, bf16[2048,768]{1,0:T(8,128)(2,1)}, u32[]{:S(2)}, u32[]{:S(2)}) collective-permute-start(bf16[2048,768]{1,0:T(8,128)(2,1)} %bitcast.55), channel_id=1, source_target_pairs={{0,1},{1,0},{2,3},{3,2},{4,5},{5,4},{6,7},{7,6},{8,9},{9,8},{10,11... | collective-permute-start | bytes 9437192 | tf_op jit(solution)/shard_map/ppermute | solution.py:343
  11.5 5.1 %copy-start.11 = (bf16[4,4096,1,128]{3,1,2,0:T(8,128)(2,1)S(1)}, bf16[4,4096,1,128]{3,1,2,0:T(8,128)(2,1)}, u32[]{:S(2)}) copy-start(bf16[4,4096,1,128]{3,1,2,0:T(8,128)(2,1)} %param.16) | copy-start | bytes 12582916
  12.5 4.8 %copy-start.12 = (bf16[1024,2048]{1,0:T(8,128)(2,1)S(1)}, bf16[1024,2048]{1,0:T(8,128)(2,1)}, u32[]{:S(2)}) copy-start(bf16[1024,2048]{1,0:T(8,128)(2,1)} %param.19) | copy-start | bytes 12582916
  16.6 22.1 %copy-start.3 = (bf16[2048,32]{0,1:T(8,128)(2,1)S(1)}, bf16[2048,32]{0,1:T(8,128)(2,1)}, u32[]{:S(2)}) copy-start(bf16[2048,32]{0,1:T(8,128)(2,1)} %param.23) | copy-start | bytes 393220
  16.6 22.1 %copy-start.5 = (f32[2048]{0:T(1024)S(1)}, f32[2048]{0:T(1024)}, u32[]{:S(2)}) copy-start(f32[2048]{0:T(1024)} %param.22) | copy-start | bytes 24580
  18.1 12.0 %collective-permute-start.5 = (f32[8,2048]{1,0:T(8,128)S(1)}, f32[8,2048]{1,0:T(8,128)S(1)}, u32[]{:S(2)}, u32[]{:S(2)}) collective-permute-start(f32[8,2048]{1,0:T(8,128)S(1)} %pad_maximum_fusion.1), channel_id=1, source_target_pairs={{0,8},{8,0},{16,24},{24,16},{1,9},{9,1},{17,25},{25,17},{2,10},{10... | collective-permute-start | bytes 196616 | tf_op jit(solution)/shard_map/ppermute | solution.py:327
  30.1 9.0 %collective-permute-start.10 = (bf16[2048,768]{1,0:T(8,128)(2,1)}, bf16[2048,768]{1,0:T(8,128)(2,1)}, u32[]{:S(2)}, u32[]{:S(2)}) collective-permute-start(bf16[2048,768]{1,0:T(8,128)(2,1)} %bitcast.11.refs_7_.refs_8_), channel_id=1, source_target_pairs={{0,1},{1,0},{2,3},{3,2},{4,5},{5,4},{6,7},{7,6},{8,9},{9,8},{10,11... | collective-permute-start | bytes 9437192 | tf_op jit(solution)/shard_map/ppermute | solution.py:343
  30.2 0.8 copy-start.7
  31.0 0.8 copy-start.9
  31.8 22.6 %collective-permute-start.16 = (bf16[768,2048]{1,0:T(8,128)(2,1)}, bf16[768,2048]{1,0:T(8,128)(2,1)}, u32[]{:S(2)}, u32[]{:S(2)}) collective-permute-start(bf16[768,2048]{1,0:T(8,128)(2,1)} %bitcast.14.refs_8_.refs_9_), channel_id=1, source_target_pairs={{0,1},{1,0},{2,3},{3,2},{4,5},{5,4},{6,7},{7,6},{8,9},{9,8},{10,11... | collective-permute-start | bytes 9437192 | tf_op jit(solution)/shard_map/ppermute | solution.py:343
  32.3 4.3 %collective-permute-start.6 = (f32[8,2048]{1,0:T(8,128)S(1)}, f32[8,2048]{1,0:T(8,128)S(1)}, u32[]{:S(2)}, u32[]{:S(2)}) collective-permute-start(f32[8,2048]{1,0:T(8,128)S(1)} %add.114), channel_id=1, source_target_pairs={{0,16},{8,24},{16,0},{24,8},{1,17},{9,25},{17,1},{25,9},{2,18},{10... | collective-permute-start | bytes 196616 | tf_op jit(solution)/shard_map/ppermute | solution.py:331
  34.1 12.8 %collective-permute-start.7 = (bf16[112,2176]{1,0:T(8,128)(2,1)S(1)}, bf16[112,2176]{1,0:T(8,128)(2,1)S(1)}, u32[]{:S(2)}, u32[]{:S(2)}) collective-permute-start(bf16[112,2176]{1,0:T(8,128)(2,1)S(1)} %collective-permute-done.3.refs_2_), channel_id=1, source_target_pairs={{0,8},{8,0},{16,24},{24,16},{1,9},{9,1},{17,25},{25,17},{2,10},{10... | collective-permute-start | bytes 1462280 | tf_op jit(solution)/shard_map/ppermute | solution.py:327
  35.6 12.5 %collective-permute-start.8 = (bf16[112,2176]{1,0:T(8,128)(2,1)S(1)}, bf16[112,2176]{1,0:T(8,128)(2,1)S(1)}, u32[]{:S(2)}, u32[]{:S(2)}) collective-permute-start(bf16[112,2176]{1,0:T(8,128)(2,1)S(1)} %collective-permute-done.3.refs_2_), channel_id=1, source_target_pairs={{0,16},{8,24},{16,0},{24,8},{1,17},{9,25},{17,1},{25,9},{2,18},{10... | collective-permute-start | bytes 1462280 | tf_op jit(solution)/shard_map/ppermute | solution.py:331
  36.5 14.0 %collective-permute-start.9 = (bf16[112,2176]{1,0:T(8,128)(2,1)S(1)}, bf16[112,2176]{1,0:T(8,128)(2,1)S(1)}, u32[]{:S(2)}, u32[]{:S(2)}) collective-permute-start(bf16[112,2176]{1,0:T(8,128)(2,1)S(1)} %collective-permute-done.3.refs_2_), channel_id=1, source_target_pairs={{0,2},{1,3},{2,4},{3,5},{4,6},{5,7},{6,0},{7,1},{8,10},{9,11},{10,... | collective-permute-start | bytes 1462280 | tf_op jit(solution)/shard_map/ppermute | solution.py:339
  50.6 18.4 %collective-permute-start.13 = (bf16[112,2176]{1,0:T(8,128)(2,1)S(1)}, bf16[112,2176]{1,0:T(8,128)(2,1)S(1)}, u32[]{:S(2)}, u32[]{:S(2)}) collective-permute-start(bf16[112,2176]{1,0:T(8,128)(2,1)S(1)} %collective-permute-done.9.refs_2_), channel_id=1, source_target_pairs={{0,8},{8,0},{16,24},{24,16},{1,9},{9,1},{17,25},{25,17},{2,10},{10... | collective-permute-start | bytes 1462280 | tf_op jit(solution)/shard_map/ppermute | solution.py:327
  52.0 17.0 %collective-permute-start.14 = (bf16[112,2176]{1,0:T(8,128)(2,1)S(1)}, bf16[112,2176]{1,0:T(8,128)(2,1)S(1)}, u32[]{:S(2)}, u32[]{:S(2)}) collective-permute-start(bf16[112,2176]{1,0:T(8,128)(2,1)S(1)} %collective-permute-done.9.refs_2_), channel_id=1, source_target_pairs={{0,16},{8,24},{16,0},{24,8},{1,17},{9,25},{17,1},{25,9},{2,18},{10... | collective-permute-start | bytes 1462280 | tf_op jit(solution)/shard_map/ppermute | solution.py:331
  53.6 15.5 %collective-permute-start.15 = (bf16[128,2176]{1,0:T(8,128)(2,1)S(1)}, bf16[128,2176]{1,0:T(8,128)(2,1)S(1)}, u32[]{:S(2)}, u32[]{:S(2)}) collective-permute-start(bf16[128,2176]{1,0:T(8,128)(2,1)S(1)} %pad_maximum_fusion), channel_id=1, source_target_pairs={{0,2},{1,3},{2,4},{3,5},{4,6},{5,7},{6,0},{7,1},{8,10},{9,11},{10,... | collective-permute-start | bytes 1671176 | tf_op jit(solution)/shard_map/ppermute | solution.py:339
  53.7 15.3 %collective-permute-start.12 = (bf16[64,2176]{1,0:T(8,128)(2,1)S(1)}, bf16[64,2176]{1,0:T(8,128)(2,1)S(1)}, u32[]{:S(2)}, u32[]{:S(2)}) collective-permute-start(bf16[64,2176]{1,0:T(8,128)(2,1)S(1)} %slice.38), channel_id=1, source_target_pairs={{0,8},{8,0},{16,24},{24,16},{1,9},{9,1},{17,25},{25,17},{2,10},{10... | collective-permute-start | bytes 835592 | tf_op jit(solution)/shard_map/ppermute | solution.py:327
  54.3 14.6 %collective-permute-start.11 = (bf16[48,2176]{1,0:T(8,128)(2,1)S(1)}, bf16[48,2176]{1,0:T(8,128)(2,1)S(1)}, u32[]{:S(2)}, u32[]{:S(2)}) collective-permute-start(bf16[48,2176]{1,0:T(8,128)(2,1)S(1)} %slice.37), channel_id=1, source_target_pairs={{0,16},{8,24},{16,0},{24,8},{1,17},{9,25},{17,1},{25,9},{2,18},{10... | collective-permute-start | bytes 626696 | tf_op jit(solution)/shard_map/ppermute | solution.py:331
  54.9 1.0 copy-start.8
  55.9 1.0 copy-start.10
  69.1 17.6 %collective-permute-start.19 = (bf16[112,2176]{1,0:T(8,128)(2,1)S(1)}, bf16[112,2176]{1,0:T(8,128)(2,1)S(1)}, u32[]{:S(2)}, u32[]{:S(2)}) collective-permute-start(bf16[112,2176]{1,0:T(8,128)(2,1)S(1)} %slice.41.refs_2_), channel_id=1, source_target_pairs={{0,8},{8,0},{16,24},{24,16},{1,9},{9,1},{17,25},{25,17},{2,10},{10... | collective-permute-start | bytes 1462280 | tf_op jit(solution)/shard_map/ppermute | solution.py:327
  70.7 16.1 %collective-permute-start.20 = (bf16[112,2176]{1,0:T(8,128)(2,1)S(1)}, bf16[112,2176]{1,0:T(8,128)(2,1)S(1)}, u32[]{:S(2)}, u32[]{:S(2)}) collective-permute-start(bf16[112,2176]{1,0:T(8,128)(2,1)S(1)} %slice.41.refs_2_), channel_id=1, source_target_pairs={{0,16},{8,24},{16,0},{24,8},{1,17},{9,25},{17,1},{25,9},{2,18},{10... | collective-permute-start | bytes 1462280 | tf_op jit(solution)/shard_map/ppermute | solution.py:331
  72.1 14.6 %collective-permute-start.17 = (bf16[64,2176]{1,0:T(8,128)(2,1)S(1)}, bf16[64,2176]{1,0:T(8,128)(2,1)S(1)}, u32[]{:S(2)}, u32[]{:S(2)}) collective-permute-start(bf16[64,2176]{1,0:T(8,128)(2,1)S(1)} %slice.39), channel_id=1, source_target_pairs={{0,16},{8,24},{16,0},{24,8},{1,17},{9,25},{17,1},{25,9},{2,18},{10... | collective-permute-start | bytes 835592 | tf_op jit(solution)/shard_map/ppermute | solution.py:331
  72.8 13.9 %collective-permute-start.18 = (bf16[48,2176]{1,0:T(8,128)(2,1)S(1)}, bf16[48,2176]{1,0:T(8,128)(2,1)S(1)}, u32[]{:S(2)}, u32[]{:S(2)}) collective-permute-start(bf16[48,2176]{1,0:T(8,128)(2,1)S(1)} %slice.40), channel_id=1, source_target_pairs={{0,8},{8,0},{16,24},{24,16},{1,9},{9,1},{17,25},{25,17},{2,10},{10... | collective-permute-start | bytes 626696 | tf_op jit(solution)/shard_map/ppermute | solution.py:327
  73.4 13.3 %collective-permute-start.21 = (bf16[16,2176]{1,0:T(8,128)(2,1)S(1)}, bf16[16,2176]{1,0:T(8,128)(2,1)S(1)}, u32[]{:S(2)}, u32[]{:S(2)}) collective-permute-start(bf16[16,2176]{1,0:T(8,128)(2,1)S(1)} %slice.42.refs_1_), channel_id=1, source_target_pairs={{0,2},{1,3},{2,4},{3,5},{4,6},{5,7},{6,0},{7,1},{8,10},{9,11},{10,... | collective-permute-start | bytes 208904 | tf_op jit(solution)/shard_map/ppermute | solution.py:339
  86.8 17.9 %collective-permute-start.23 = (bf16[64,2176]{1,0:T(8,128)(2,1)S(1)}, bf16[64,2176]{1,0:T(8,128)(2,1)S(1)}, u32[]{:S(2)}, u32[]{:S(2)}) collective-permute-start(bf16[64,2176]{1,0:T(8,128)(2,1)S(1)} %slice.44), channel_id=1, source_target_pairs={{0,8},{8,0},{16,24},{24,16},{1,9},{9,1},{17,25},{25,17},{2,10},{10... | collective-permute-start | bytes 835592 | tf_op jit(solution)/shard_map/ppermute | solution.py:327
  88.4 16.3 %collective-permute-start.22 = (bf16[48,2176]{1,0:T(8,128)(2,1)S(1)}, bf16[48,2176]{1,0:T(8,128)(2,1)S(1)}, u32[]{:S(2)}, u32[]{:S(2)}) collective-permute-start(bf16[48,2176]{1,0:T(8,128)(2,1)S(1)} %slice.43), channel_id=1, source_target_pairs={{0,16},{8,24},{16,0},{24,8},{1,17},{9,25},{17,1},{25,9},{2,18},{10... | collective-permute-start | bytes 626696 | tf_op jit(solution)/shard_map/ppermute | solution.py:331
  89.9 14.7 %collective-permute-start.26 = (bf16[64,2048]{1,0:T(8,128)(2,1)S(1)}, bf16[64,2048]{1,0:T(8,128)(2,1)S(1)}, u32[]{:S(2)}, u32[]{:S(2)}) collective-permute-start(bf16[64,2048]{1,0:T(8,128)(2,1)S(1)} %get-tuple-element.157), channel_id=1, source_target_pairs={{0,8},{8,0},{16,24},{24,16},{1,9},{9,1},{17,25},{25,17},{2,10},{10... | collective-permute-start | bytes 786440 | tf_op jit(solution)/shard_map/ppermute | solution.py:327
  90.5 14.1 %collective-permute-start.25 = (bf16[48,2048]{1,0:T(8,128)(2,1)S(1)}, bf16[48,2048]{1,0:T(8,128)(2,1)S(1)}, u32[]{:S(2)}, u32[]{:S(2)}) collective-permute-start(bf16[48,2048]{1,0:T(8,128)(2,1)S(1)} %get-tuple-element.156), channel_id=1, source_target_pairs={{0,16},{8,24},{16,0},{24,8},{1,17},{9,25},{17,1},{25,9},{2,18},{10... | collective-permute-start | bytes 589832 | tf_op jit(solution)/shard_map/ppermute | solution.py:331
  91.0 13.6 %collective-permute-start.24 = (bf16[16,2176]{1,0:T(8,128)(2,1)S(1)}, bf16[16,2176]{1,0:T(8,128)(2,1)S(1)}, u32[]{:S(2)}, u32[]{:S(2)}) collective-permute-start(bf16[16,2176]{1,0:T(8,128)(2,1)S(1)} %collective-permute-done.21.refs_1_), channel_id=1, source_target_pairs={{0,2},{1,3},{2,4},{3,5},{4,6},{5,7},{6,0},{7,1},{8,10},{9,11},{10,... | collective-permute-start | bytes 208904 | tf_op jit(solution)/shard_map/ppermute | solution.py:339
  104.8 16.4 %collective-permute-start.27 = (bf16[112,2048]{1,0:T(8,128)(2,1)S(1)}, bf16[112,2048]{1,0:T(8,128)(2,1)S(1)}, u32[]{:S(2)}, u32[]{:S(2)}) collective-permute-start(bf16[112,2048]{1,0:T(8,128)(2,1)S(1)} %get-tuple-element.172), channel_id=1, source_target_pairs={{0,8},{8,0},{16,24},{24,16},{1,9},{9,1},{17,25},{25,17},{2,10},{10... | collective-permute-start | bytes 1376264 | tf_op jit(solution)/shard_map/ppermute | solution.py:327
  106.3 14.9 %collective-permute-start.28 = (bf16[112,2048]{1,0:T(8,128)(2,1)S(1)}, bf16[112,2048]{1,0:T(8,128)(2,1)S(1)}, u32[]{:S(2)}, u32[]{:S(2)}) collective-permute-start(bf16[112,2048]{1,0:T(8,128)(2,1)S(1)} %get-tuple-element.173), channel_id=1, source_target_pairs={{0,16},{8,24},{16,0},{24,8},{1,17},{9,25},{17,1},{25,9},{2,18},{10... | collective-permute-start | bytes 1376264 | tf_op jit(solution)/shard_map/ppermute | solution.py:331
  107.8 13.4 %collective-permute-start.29 = (bf16[64,2048]{1,0:T(8,128)(2,1)S(1)}, bf16[64,2048]{1,0:T(8,128)(2,1)S(1)}, u32[]{:S(2)}, u32[]{:S(2)}) collective-permute-start(bf16[64,2048]{1,0:T(8,128)(2,1)S(1)} %get-tuple-element.174), channel_id=1, source_target_pairs={{0,16},{8,24},{16,0},{24,8},{1,17},{9,25},{17,1},{25,9},{2,18},{10... | collective-permute-start | bytes 786440 | tf_op jit(solution)/shard_map/ppermute | solution.py:331
  108.4 12.8 %collective-permute-start.30 = (bf16[48,2048]{1,0:T(8,128)(2,1)S(1)}, bf16[48,2048]{1,0:T(8,128)(2,1)S(1)}, u32[]{:S(2)}, u32[]{:S(2)}) collective-permute-start(bf16[48,2048]{1,0:T(8,128)(2,1)S(1)} %get-tuple-element.175), channel_id=1, source_target_pairs={{0,8},{8,0},{16,24},{24,16},{1,9},{9,1},{17,25},{25,17},{2,10},{10... | collective-permute-start | bytes 589832 | tf_op jit(solution)/shard_map/ppermute | solution.py:327
  121.4 51.3 %copy-start.1 = (bf16[1,111,2048]{2,1,0:T(8,128)(2,1)S(1)}, bf16[1,111,2048]{2,1,0:T(8,128)(2,1)}, u32[]{:S(2)}) copy-start(bf16[1,111,2048]{2,1,0:T(8,128)(2,1)} %param.21) | copy-start | bytes 1363972
  121.4 19.6 %collective-permute-start.35 = (bf16[112,2048]{1,0:T(8,128)(2,1)S(1)}, bf16[112,2048]{1,0:T(8,128)(2,1)S(1)}, u32[]{:S(2)}, u32[]{:S(2)}) collective-permute-start(bf16[112,2048]{1,0:T(8,128)(2,1)S(1)} %add_convert_fusion.3), channel_id=1, source_target_pairs={{0,2},{1,3},{2,4},{3,5},{4,6},{5,7},{6,0},{7,1},{8,10},{9,11},{10,... | collective-permute-start | bytes 1376264 | tf_op jit(solution)/shard_map/ppermute | solution.py:339
  123.7 17.4 %collective-permute-start.31 = (bf16[112,2048]{1,0:T(8,128)(2,1)S(1)}, bf16[112,2048]{1,0:T(8,128)(2,1)S(1)}, u32[]{:S(2)}, u32[]{:S(2)}) collective-permute-start(bf16[112,2048]{1,0:T(8,128)(2,1)S(1)} %get-tuple-element.192), channel_id=1, source_target_pairs={{0,8},{8,0},{16,24},{24,16},{1,9},{9,1},{17,25},{25,17},{2,10},{10... | collective-permute-start | bytes 1376264 | tf_op jit(solution)/shard_map/ppermute | solution.py:327
  125.3 15.8 %collective-permute-start.32 = (bf16[112,2048]{1,0:T(8,128)(2,1)S(1)}, bf16[112,2048]{1,0:T(8,128)(2,1)S(1)}, u32[]{:S(2)}, u32[]{:S(2)}) collective-permute-start(bf16[112,2048]{1,0:T(8,128)(2,1)S(1)} %get-tuple-element.193), channel_id=1, source_target_pairs={{0,16},{8,24},{16,0},{24,8},{1,17},{9,25},{17,1},{25,9},{2,18},{10... | collective-permute-start | bytes 1376264 | tf_op jit(solution)/shard_map/ppermute | solution.py:331
  126.7 14.4 %collective-permute-start.34 = (bf16[64,2048]{1,0:T(8,128)(2,1)S(1)}, bf16[64,2048]{1,0:T(8,128)(2,1)S(1)}, u32[]{:S(2)}, u32[]{:S(2)}) collective-permute-start(bf16[64,2048]{1,0:T(8,128)(2,1)S(1)} %get-tuple-element.195), channel_id=1, source_target_pairs={{0,8},{8,0},{16,24},{24,16},{1,9},{9,1},{17,25},{25,17},{2,10},{10... | collective-permute-start | bytes 786440 | tf_op jit(solution)/shard_map/ppermute | solution.py:327
  127.3 13.8 %collective-permute-start.33 = (bf16[48,2048]{1,0:T(8,128)(2,1)S(1)}, bf16[48,2048]{1,0:T(8,128)(2,1)S(1)}, u32[]{:S(2)}, u32[]{:S(2)}) collective-permute-start(bf16[48,2048]{1,0:T(8,128)(2,1)S(1)} %get-tuple-element.194), channel_id=1, source_target_pairs={{0,16},{8,24},{16,0},{24,8},{1,17},{9,25},{17,1},{25,9},{2,18},{10... | collective-permute-start | bytes 589832 | tf_op jit(solution)/shard_map/ppermute | solution.py:331
  141.4 17.7 %collective-permute-start.40 = (bf16[112,2048]{1,0:T(8,128)(2,1)S(1)}, bf16[112,2048]{1,0:T(8,128)(2,1)S(1)}, u32[]{:S(2)}, u32[]{:S(2)}) collective-permute-start(bf16[112,2048]{1,0:T(8,128)(2,1)S(1)} %add_convert_fusion.2), channel_id=1, source_target_pairs={{0,2},{1,3},{2,4},{3,5},{4,6},{5,7},{6,0},{7,1},{8,10},{9,11},{10,... | collective-permute-start | bytes 1376264 | tf_op jit(solution)/shard_map/ppermute | solution.py:339
  142.4 16.7 %collective-permute-start.36 = (bf16[112,2048]{1,0:T(8,128)(2,1)S(1)}, bf16[112,2048]{1,0:T(8,128)(2,1)S(1)}, u32[]{:S(2)}, u32[]{:S(2)}) collective-permute-start(bf16[112,2048]{1,0:T(8,128)(2,1)S(1)} %get-tuple-element.212), channel_id=1, source_target_pairs={{0,8},{8,0},{16,24},{24,16},{1,9},{9,1},{17,25},{25,17},{2,10},{10... | collective-permute-start | bytes 1376264 | tf_op jit(solution)/shard_map/ppermute | solution.py:327
  143.3 15.8 %collective-permute-start.37 = (bf16[112,2048]{1,0:T(8,128)(2,1)S(1)}, bf16[112,2048]{1,0:T(8,128)(2,1)S(1)}, u32[]{:S(2)}, u32[]{:S(2)}) collective-permute-start(bf16[112,2048]{1,0:T(8,128)(2,1)S(1)} %get-tuple-element.213), channel_id=1, source_target_pairs={{0,16},{8,24},{16,0},{24,8},{1,17},{9,25},{17,1},{25,9},{2,18},{10... | collective-permute-start | bytes 1376264 | tf_op jit(solution)/shard_map/ppermute | solution.py:331
  144.7 14.4 %collective-permute-start.38 = (bf16[64,2048]{1,0:T(8,128)(2,1)S(1)}, bf16[64,2048]{1,0:T(8,128)(2,1)S(1)}, u32[]{:S(2)}, u32[]{:S(2)}) collective-permute-start(bf16[64,2048]{1,0:T(8,128)(2,1)S(1)} %get-tuple-element.214), channel_id=1, source_target_pairs={{0,16},{8,24},{16,0},{24,8},{1,17},{9,25},{17,1},{25,9},{2,18},{10... | collective-permute-start | bytes 786440 | tf_op jit(solution)/shard_map/ppermute | solution.py:331
  145.4 12.6 %collective-permute-start.39 = (bf16[48,2048]{1,0:T(8,128)(2,1)S(1)}, bf16[48,2048]{1,0:T(8,128)(2,1)S(1)}, u32[]{:S(2)}, u32[]{:S(2)}) collective-permute-start(bf16[48,2048]{1,0:T(8,128)(2,1)S(1)} %get-tuple-element.215), channel_id=1, source_target_pairs={{0,8},{8,0},{16,24},{24,16},{1,9},{9,1},{17,25},{25,17},{2,10},{10... | collective-permute-start | bytes 589832 | tf_op jit(solution)/shard_map/ppermute | solution.py:327
  159.2 8.5 %collective-permute-start.41 = (bf16[112,2048]{1,0:T(8,128)(2,1)S(1)}, bf16[112,2048]{1,0:T(8,128)(2,1)S(1)}, u32[]{:S(2)}, u32[]{:S(2)}) collective-permute-start(bf16[112,2048]{1,0:T(8,128)(2,1)S(1)} %get-tuple-element.229), channel_id=1, source_target_pairs={{0,8},{8,0},{16,24},{24,16},{1,9},{9,1},{17,25},{25,17},{2,10},{10... | collective-permute-start | bytes 1376264 | tf_op jit(solution)/shard_map/ppermute | solution.py:327
  160.8 8.5 %collective-permute-start.42 = (bf16[112,2048]{1,0:T(8,128)(2,1)S(1)}, bf16[112,2048]{1,0:T(8,128)(2,1)S(1)}, u32[]{:S(2)}, u32[]{:S(2)}) collective-permute-start(bf16[112,2048]{1,0:T(8,128)(2,1)S(1)} %get-tuple-element.230), channel_id=1, source_target_pairs={{0,16},{8,24},{16,0},{24,8},{1,17},{9,25},{17,1},{25,9},{2,18},{10... | collective-permute-start | bytes 1376264 | tf_op jit(solution)/shard_map/ppermute | solution.py:331
  162.4 10.3 %collective-permute-start.43 = (bf16[112,2048]{1,0:T(8,128)(2,1)S(1)}, bf16[112,2048]{1,0:T(8,128)(2,1)S(1)}, u32[]{:S(2)}, u32[]{:S(2)}) collective-permute-start(bf16[112,2048]{1,0:T(8,128)(2,1)S(1)} %add_convert_fusion.1), channel_id=1, source_target_pairs={{0,2},{1,3},{2,4},{3,5},{4,6},{5,7},{6,0},{7,1},{8,10},{9,11},{10,... | collective-permute-start | bytes 1376264 | tf_op jit(solution)/shard_map/ppermute | solution.py:339

commit v6 on v5

--- a/solution.py
+++ b/solution.py
@@ -148,7 +148,7 @@
     sources = [refs.pop(0) for _ in piece_rows]
     weight_refs = [refs.pop(0) for _ in range(6)]
     targets = [refs.pop(0) for _ in block_rows]
-    decodes, rows, weights, downs, slots, inner, results, spread, sums, row_sem, weight_sem, out_sem = refs
+    decodes, rows, slots, inner, results, spread, sums, row_sem, out_sem = refs
     width = sums.shape[1]
     tokens = block_rows[0]
     pair_rows = 2 * tokens
@@ -159,16 +159,7 @@
         copy = pltpu.make_async_copy(ref, rows.at[pl.ds(at, count)], row_sem.at[i])
         row_copies.append(copy)
         at += count
-    up_copies = [
-        pltpu.make_async_copy(weight_refs[3 * e + i], weights.at[2 * e + i], weight_sem.at[2 * e + i])
-        for e in range(2)
-        for i in range(2)
-    ]
-    down_copies = [
-        pltpu.make_async_copy(weight_refs[3 * e + 2], downs.at[e], weight_sem.at[4 + e])
-        for e in range(2)
-    ]
-    for copy in row_copies + up_copies + down_copies:
+    for copy in row_copies:
         copy.start()
     for copy in row_copies:
         copy.wait()
@@ -225,33 +216,27 @@
         return jnp.sum(jnp.where(mine, tail, 0.0), axis=1, keepdims=True)
 
     def product(e, i):
-        return jnp.dot(slots[e, :, :width], weights[2 * e + i], preferred_element_type=jnp.float32)
+        return jnp.dot(slots[e, :, :width], weight_refs[3 * e + i][...], preferred_element_type=jnp.float32)
 
     def activate(e, gate_act, up_act):
         act = gate_act / (1.0 + jnp.exp(-gate_act)) * up_act * weight_of(e)
         inner[e] = act.astype(jnp.bfloat16)
 
     def finish(e):
-        result = jnp.dot(inner[e], downs[e], preferred_element_type=jnp.float32)
+        result = jnp.dot(inner[e], weight_refs[3 * e + 2][...], preferred_element_type=jnp.float32)
         result = result.astype(jnp.bfloat16)
         for p in range(2):
             results[p, pl.ds(e * pair_slots, pair_slots), :] = result[p * pair_slots : (p + 1) * pair_slots]
 
-    up_copies[0].wait()
     gate_0 = product(0, 0)
     make_spread(0)
-    up_copies[1].wait()
     up_0 = product(0, 1)
     make_spread(1)
-    up_copies[2].wait()
     activate(0, gate_0, up_0)
     gate_1 = product(1, 0)
-    up_copies[3].wait()
     up_1 = product(1, 1)
-    down_copies[0].wait()
     finish(0)
     activate(1, gate_1, up_1)
-    down_copies[1].wait()
     finish(1)
     out_copies = []
     at = 0
@@ -279,24 +264,23 @@
     anywhere = pl.BlockSpec(memory_space=pl.ANY)
     return pl.pallas_call(
         functools.partial(plane_kernel, cap, piece_rows, block_rows),
-        in_specs=[pl.BlockSpec(memory_space=pltpu.SMEM)] + [anywhere] * (len(pieces) + 7),
+        in_specs=[pl.BlockSpec(memory_space=pltpu.SMEM)]
+        + [anywhere] * (len(pieces) + 1)
+        + [pl.BlockSpec(memory_space=pltpu.VMEM)] * 6,
         out_specs=[anywhere] * len(block_rows),
         out_shape=[jax.ShapeDtypeStruct((count, width), kept) for count in block_rows],
         scratch_shapes=[
             pltpu.VMEM(decodes.shape, kept),
             pltpu.VMEM((total, padded), kept),
-            pltpu.VMEM((4, width, units), kept),
-            pltpu.VMEM((2, units, width), kept),
             pltpu.VMEM((2, 4 * cap, padded), kept),
             pltpu.VMEM((2, 4 * cap, units), kept),
             pltpu.VMEM((2, 4 * cap, width), kept),
             pltpu.VMEM((2, total // 2, 4 * cap), kept),
             pltpu.VMEM((total, width), kept),
             pltpu.SemaphoreType.DMA((len(pieces) + 1,)),
-            pltpu.SemaphoreType.DMA((6,)),
             pltpu.SemaphoreType.DMA((len(block_rows),)),
         ],
-        compiler_params=pltpu.CompilerParams(vmem_limit_bytes=48 << 20),
+        compiler_params=pltpu.CompilerParams(vmem_limit_bytes=24 << 20),
         cost_estimate=pl.CostEstimate(
             flops=12 * total * width * units, bytes_accessed=24 << 20, transcendentals=total * units
         ),
@@ -329,10 +313,6 @@
 
 def along_y(value):
     return lax.ppermute(value, "kv", [(i, i ^ 2) for i in range(4)])
-
-
-def along_diagonal(value):
-    return lax.ppermute(value, "kv", [(i, i ^ 3) for i in range(4)])
 
 
 def around_z(value):
@@ -415,7 +395,6 @@
         blocks[0], queries, cache_keys, expert_gate, expert_up
     )
     spread_sides(0)
-    corners[0] = (along_diagonal(blocks[0]),)
     blocks[1] = around_z(blocks[0])
     other_gate = across_chip(expert_gate[0])
     other_up = across_chip(expert_up[0])
@@ -430,13 +409,14 @@
 
     shared, other_gate = fence(shared, other_gate)
     shared = shared + along_x(shared)
-    sides[0], corners[0], blocks[1], shared, expert_down = fence(
-        sides[0], corners[0], blocks[1], shared, expert_down
-    )
+    sides[0], blocks[1], shared, expert_down = fence(sides[0], blocks[1], shared, expert_down)
 
     spread_sides(1)
     blocks[2] = around_z(blocks[1])
     other_down = across_chip(expert_down[0])
+    sides[1], sides[0], blocks[2], shared = fence(sides[1], sides[0], blocks[2], shared)
+
+    spread_corners(0)
     shared = shared + along_y(shared)
     order = [my_kv ^ j for j in range(4)]
     decoded = jnp.concatenate(
@@ -453,7 +433,9 @@
         jnp.pad(decode_ids, ((0, 12), (0, 0))),
         "first",
     )
-    sides[1], blocks[2], decodes[0], other_up = fence(sides[1], blocks[2], decodes[0], other_up)
+    corners[0], sides[1], blocks[2], decodes[0], other_up, other_down = fence(
+        corners[0], sides[1], blocks[2], decodes[0], other_up, other_down
+    )
     weights = (expert_gate[0], expert_up[0], expert_down[0], other_gate, other_up, other_down)
 
     spread_corners(1)

time: 174 us -> 180 us (1.034)
  Pallas kernels: 50.1 us -> 59.2 us
  waiting for transfers between devices: 58.5 us -> 54.9 us
    pallas_call x4, Pallas kernels: 48.4 us -> 57.5 us  [run_plane(): pl.pallas_call(functools.partial(plane_kernel, cap, piece_rows, block_row...]
    ppermute x16 -> x17, waiting for transfers between devices: 17.5 us -> 16.1 us  [along_y(): return lax.ppermute(value, 'kv', [(i, i ^ 2) for i in range(4)])]
    ppermute x16 -> x17, waiting for transfers between devices: 35.1 us -> 33.8 us  [along_x(): return lax.ppermute(value, 'kv', [(i, i ^ 1) for i in range(4)])]
    ppermute x16 -> x17, starting transfers between devices: 20.3 us -> 19.3 us  [along_x(): return lax.ppermute(value, 'kv', [(i, i ^ 1) for i in range(4)])]
    ppermute x16 -> x17, starting transfers between devices: 17.3 us -> 17.2 us  [along_y(): return lax.ppermute(value, 'kv', [(i, i ^ 2) for i in range(4)])]
  transfers between devices with their start and end apart: 44 -> 45, of which waited for: 11 -> 12; matrix products, arithmetic and copies ran while one was open for 5% -> 6% of each run, Pallas kernels for 28% -> 32%
where the time goes in v6:
time: 180 us
  Pallas kernels  59.2 us (33%)
  waiting for transfers between devices  54.9 us (30%)
  starting transfers between devices  46.3 us (26%)
  local copies, waits for them, and re-layouts  7.79 us (4%)
  other arithmetic  5.78 us (3%)
  matrix products  5.13 us (3%)
    pallas_call x4, Pallas kernels, run_plane(): pl.pallas_call(functools.partial(plane_kernel, cap, piece_rows, block_row...  57.5 us
    ppermute x17, waiting for transfers between devices, along_x(): return lax.ppermute(value, 'kv', [(i, i ^ 1) for i in range(4)])  33.8 us
    ppermute x17, starting transfers between devices, along_x(): return lax.ppermute(value, 'kv', [(i, i ^ 1) for i in range(4)])  19.3 us
    ppermute x17, starting transfers between devices, along_y(): return lax.ppermute(value, 'kv', [(i, i ^ 2) for i in range(4)])  17.2 us
    ppermute x17, waiting for transfers between devices, along_y(): return lax.ppermute(value, 'kv', [(i, i ^ 2) for i in range(4)])  16.1 us
    ppermute x8, starting transfers between devices, around_z(): return lax.ppermute(value, 'blk', [(i, (i + 2) % 8) for i in range(8)])  9.44 us
    unnamed x28, local copies, waits for them, and re-layouts  6.05 us
    ppermute x8, waiting for transfers between devices, around_z(): return lax.ppermute(value, 'blk', [(i, (i + 2) % 8) for i in range(8)])  5 us
  transfers between devices with their start and end apart: 45, of which 12 were waited for; matrix products, arithmetic and copies ran while one was open for 6% of the time, Pallas kernels for 32%

profile of v6, /device:TPU:0, one launch (start us, length us, event | category | flops | bytes accessed | tf_op | source)
XLA Modules:
  0.0 179.6 jit_solution(9368856544466575120)
XLA Ops:
  0.0 1.0 copy-done
  1.0 0.9 copy-done.2
  1.9 0.7 copy-done.4
  2.6 0.7 copy-done.6
  3.3 0.8 prepare.2.refs_2_
  4.1 3.0 %collective-permute-start = (bf16[112,2176]{1,0:T(8,128)(2,1)S(1)}, bf16[112,2176]{1,0:T(8,128)(2,1)S(1)}, u32[]{:S(2)}, u32[]{:S(2)}) collective-permute-start(bf16[112,2176]{1,0:T(8,128)(2,1)S(1)} %prepare.2.refs_2_), channel_id=1, source_target_pairs={{0,8},{8,0},{16,24},{24,16},{1,9},{9,1},{17,25},{25,17},{2,10},{10... | collective-permute-start | bytes 1462280 | tf_op jit(solution)/shard_map/ppermute | solution.py:311
  7.1 1.5 collective-permute-start.1
  8.6 1.6 collective-permute-start.2
  10.3 0.7 broadcast_in_dim.76
  11.0 0.9 minimum_subtract_fusion
  12.0 3.8 %fusion.33 = (f32[4,8]{1,0:T(4,128)S(1)}, f32[4,8,4096]{2,1,0:T(8,128)S(1)}) fusion(bf16[4,4096,1,128]{3,1,2,0:T(8,128)(2,1)} %param.15, bf16[1,4,8,128]{3,1,2,0:T(4,128)(2,1)} %bitcast.58, pred[4,4096]{1,0:T(4,128)(4,1)S(1)} %iota_compare_fusion.1), kind=kOutput, calls=%fused_computation.56 | convolution fusion | flops 33947616 | bytes 4743296 | tf_op jit(solution)/shard_map/rgd,rjd->rgj/dot_general | solution.py:27
  16.1 0.7 fusion.10
  16.9 0.7 convolution_add_fusion
  17.6 0.6 collective-permute-start.4
  18.5 3.7 %collective-permute-done.4 = f32[8,2048]{1,0:T(8,128)S(1)} collective-permute-done((f32[8,2048]{1,0:T(8,128)S(1)}, f32[8,2048]{1,0:T(8,128)S(1)}, u32[]{:S(2)}, u32[]{:S(2)}) %collective-permute-start.4) | collective-permute-done | bytes 65568 | tf_op jit(solution)/shard_map/ppermute | solution.py:311
  22.2 0.6 add.114
  24.0 1.6 collective-permute-start.7
  25.6 0.8 copy-done.9
  26.4 10.1 %collective-permute-done.5.refs_3_ = bf16[112,2176]{1,0:T(8,128)(2,1)S(1)} collective-permute-done((bf16[112,2176]{1,0:T(8,128)(2,1)S(1)}, bf16[112,2176]{1,0:T(8,128)(2,1)S(1)}, u32[]{:S(2)}, u32[]{:S(2)}) %collective-permute-start.5) | collective-permute-done | bytes 487456 | tf_op jit(solution)/shard_map/ppermute | solution.py:311
  36.7 2.0 %collective-permute-done.7.refs_2_ = bf16[112,2176]{1,0:T(8,128)(2,1)S(1)} collective-permute-done((bf16[112,2176]{1,0:T(8,128)(2,1)S(1)}, bf16[112,2176]{1,0:T(8,128)(2,1)S(1)}, u32[]{:S(2)}, u32[]{:S(2)}) %collective-permute-start.7) | collective-permute-done | bytes 487456 | tf_op jit(solution)/shard_map/ppermute | solution.py:319
  38.7 1.5 collective-permute-start.8
  40.3 0.7 slice.42
  41.6 0.7 slice.43
  42.3 1.5 collective-permute-start.10
  43.8 0.8 add.115
  45.4 3.0 %collective-permute-done.10.refs_6_ = bf16[48,2176]{1,0:T(8,128)(2,1)} collective-permute-done((bf16[48,2176]{1,0:T(8,128)(2,1)}, bf16[48,2176]{1,0:T(8,128)(2,1)}, u32[]{:S(2)}, u32[]{:S(2)}) %collective-permute-start.10) | collective-permute-done | bytes 208928 | tf_op jit(solution)/shard_map/ppermute | solution.py:311
  48.4 0.8 collective-permute-done.9.refs_5_
  49.2 1.5 collective-permute-start.15
  50.7 0.7 collective-permute-start.16
  52.2 1.3 collective-permute-start.13
  53.5 1.9 %copy-done.7 = bf16[1,2048,768]{2,1,0:T(8,128)(2,1)S(1)} copy-done((bf16[1,2048,768]{2,1,0:T(8,128)(2,1)S(1)}, bf16[1,2048,768]{2,1,0:T(8,128)(2,1)}, u32[]{:S(2)}) %copy-start.7) | copy-done | bytes 3145752
  55.4 15.0 %plane.4 = (bf16[112,2048]{1,0:T(8,128)(2,1)S(1)}, bf16[112,2048]{1,0:T(8,128)(2,1)S(1)}, bf16[112,2048]{1,0:T(8,128)(2,1)S(1)}, bf16[64,2048]{1,0:T(8,128)(2,1)S(1)}, bf16[48,2048]{1,0:T(8,128)(2,1)S(1)}) custom-call(s32[3]{0:T(128)S(1)} %pad_add_fusion.refs_0_, bf16[16,2176]{1,0:T(8,128)(2,1)S(1)} %prepare.3.refs_1_, ...), custom_call_target="tpu_custom_call" | custom-call | flops 8455716864 | bytes 25165824 | tf_op jit(solution)/shard_map/plane/pallas_call | solution.py:265
  70.6 1.6 collective-permute-start.20
  72.1 0.7 collective-permute-start.21
  72.9 1.4 collective-permute-start.18
  74.8 1.3 collective-permute-start.22
  76.2 14.2 %plane.5 = (bf16[112,2048]{1,0:T(8,128)(2,1)S(1)}, bf16[112,2048]{1,0:T(8,128)(2,1)S(1)}, bf16[112,2048]{1,0:T(8,128)(2,1)S(1)}, bf16[48,2048]{1,0:T(8,128)(2,1)S(1)}, bf16[64,2048]{1,0:T(8,128)(2,1)S(1)}) custom-call(s32[3]{0:T(128)S(1)} %pad_add_fusion.refs_0_, bf16[16,2176]{1,0:T(8,128)(2,1)S(1)} %slice.50.refs_1_, bf16[112,2176]{1,0:T(8,128)(2,1)S(1)} %copy-done.10, ...), custom_call_target="tpu_custom_call" | custom-call | flops 8455716864 | bytes 25165824 | tf_op jit(solution)/shard_map/plane/pallas_call | solution.py:265
  90.4 1.6 collective-permute-start.24
  92.0 0.8 collective-permute-start.23
  93.4 1.3 collective-permute-start.26
  95.1 14.2 %plane.6 = (bf16[112,2048]{1,0:T(8,128)(2,1)S(1)}, bf16[112,2048]{1,0:T(8,128)(2,1)S(1)}, bf16[112,2048]{1,0:T(8,128)(2,1)S(1)}, bf16[64,2048]{1,0:T(8,128)(2,1)S(1)}, bf16[48,2048]{1,0:T(8,128)(2,1)S(1)}) custom-call(s32[3]{0:T(128)S(1)} %pad_add_fusion.refs_0_, bf16[16,2176]{1,0:T(8,128)(2,1)S(1)} %collective-permute-done.22.refs_1_, ...), custom_call_target="tpu_custom_call" | custom-call | flops 8455716864 | bytes 25165824 | tf_op jit(solution)/shard_map/plane/pallas_call | solution.py:265
  109.5 1.4 collective-permute-start.28
  110.8 0.7 collective-permute-start.29
  111.6 1.3 collective-permute-start.30
  112.9 0.7 collective-permute-start.31
  113.6 14.2 %plane.7 = (bf16[112,2048]{1,0:T(8,128)(2,1)S(1)}, bf16[112,2048]{1,0:T(8,128)(2,1)S(1)}, bf16[112,2048]{1,0:T(8,128)(2,1)S(1)}, bf16[48,2048]{1,0:T(8,128)(2,1)S(1)}, bf16[64,2048]{1,0:T(8,128)(2,1)S(1)}) custom-call(s32[3]{0:T(128)S(1)} %pad_add_fusion.refs_0_, bf16[16,2176]{1,0:T(8,128)(2,1)S(1)} %collective-permute-done.25.refs_1_, ...), custom_call_target="tpu_custom_call" | custom-call | flops 8455716864 | bytes 25165824 | tf_op jit(solution)/shard_map/plane/pallas_call | solution.py:265
  128.0 3.4 %collective-permute-start.36 = (bf16[112,2048]{1,0:T(8,128)(2,1)S(1)}, bf16[112,2048]{1,0:T(8,128)(2,1)S(1)}, u32[]{:S(2)}, u32[]{:S(2)}) collective-permute-start(bf16[112,2048]{1,0:T(8,128)(2,1)S(1)} %add_convert_fusion.3), channel_id=1, source_target_pairs={{0,2},{1,3},{2,4},{3,5},{4,6},{5,7},{6,0},{7,1},{8,10},{9,11},{10,... | collective-permute-start | bytes 1376264 | tf_op jit(solution)/shard_map/ppermute | solution.py:319
  131.5 1.6 collective-permute-start.32
  133.1 0.7 collective-permute-start.33
  134.4 1.3 collective-permute-start.34
  135.7 12.3 %collective-permute-done.34.passed_0_ref = bf16[48,2048]{1,0:T(8,128)(2,1)S(1)} collective-permute-done((bf16[48,2048]{1,0:T(8,128)(2,1)S(1)}, bf16[48,2048]{1,0:T(8,128)(2,1)S(1)}, u32[]{:S(2)}, u32[]{:S(2)}) %collective-permute-start.34) | collective-permute-done | bytes 196640 | tf_op jit(solution)/shard_map/ppermute | solution.py:315
  148.5 1.2 collective-permute-start.37
  149.6 0.8 collective-permute-start.38
  150.5 1.2 collective-permute-start.39
  151.7 0.9 collective-permute-start.40
  152.6 11.4 %collective-permute-done.40.passed_1_ref = bf16[48,2048]{1,0:T(8,128)(2,1)S(1)} collective-permute-done((bf16[48,2048]{1,0:T(8,128)(2,1)S(1)}, bf16[48,2048]{1,0:T(8,128)(2,1)S(1)}, u32[]{:S(2)}, u32[]{:S(2)}) %collective-permute-start.40) | collective-permute-done | bytes 196640 | tf_op jit(solution)/shard_map/ppermute | solution.py:311
  164.0 1.8 %collective-permute-done.39.passed_0_ref = bf16[64,2048]{1,0:T(8,128)(2,1)S(1)} collective-permute-done((bf16[64,2048]{1,0:T(8,128)(2,1)S(1)}, bf16[64,2048]{1,0:T(8,128)(2,1)S(1)}, u32[]{:S(2)}, u32[]{:S(2)}) %collective-permute-start.39) | collective-permute-done | bytes 262176 | tf_op jit(solution)/shard_map/ppermute | solution.py:315
  166.0 1.0 collective-permute-start.42
  167.0 0.8 collective-permute-start.43
  168.1 1.0 collective-permute-start.44
  169.0 5.5 %collective-permute-done.42 = bf16[112,2048]{1,0:T(8,128)(2,1)S(1)} collective-permute-done((bf16[112,2048]{1,0:T(8,128)(2,1)S(1)}, bf16[112,2048]{1,0:T(8,128)(2,1)S(1)}, u32[]{:S(2)}, u32[]{:S(2)}) %collective-permute-start.42) | collective-permute-done | bytes 458784 | tf_op jit(solution)/shard_map/ppermute | solution.py:311
  174.5 0.9 collective-permute-done.43
  175.4 3.0 %collective-permute-done.44 = bf16[112,2048]{1,0:T(8,128)(2,1)S(1)} collective-permute-done((bf16[112,2048]{1,0:T(8,128)(2,1)S(1)}, bf16[112,2048]{1,0:T(8,128)(2,1)S(1)}, u32[]{:S(2)}, u32[]{:S(2)}) %collective-permute-start.44) | collective-permute-done | bytes 458784 | tf_op jit(solution)/shard_map/ppermute | solution.py:319
  178.4 1.2 fusion.13
  (102 shorter events, 8.0 us)
Async XLA Ops:
  0.0 15.8 %copy-start.13 = (f32[8]{0:T(128)S(1)}, f32[8]{0:T(128)}, u32[]{:S(2)}) copy-start(f32[8]{0:T(128)} %param.18) | copy-start | bytes 100
  0.0 1.0 copy-start
  1.0 0.9 copy-start.2
  1.9 0.7 copy-start.4
  2.6 0.7 copy-start.6
  4.1 18.7 %collective-permute-start = (bf16[112,2176]{1,0:T(8,128)(2,1)S(1)}, bf16[112,2176]{1,0:T(8,128)(2,1)S(1)}, u32[]{:S(2)}, u32[]{:S(2)}) collective-permute-start(bf16[112,2176]{1,0:T(8,128)(2,1)S(1)} %prepare.2.refs_2_), channel_id=1, source_target_pairs={{0,8},{8,0},{16,24},{24,16},{1,9},{9,1},{17,25},{25,17},{2,10},{10... | collective-permute-start | bytes 1462280 | tf_op jit(solution)/shard_map/ppermute | solution.py:311
  7.1 15.7 %collective-permute-start.1 = (bf16[112,2176]{1,0:T(8,128)(2,1)S(1)}, bf16[112,2176]{1,0:T(8,128)(2,1)S(1)}, u32[]{:S(2)}, u32[]{:S(2)}) collective-permute-start(bf16[112,2176]{1,0:T(8,128)(2,1)S(1)} %prepare.2.refs_2_), channel_id=1, source_target_pairs={{0,16},{8,24},{16,0},{24,8},{1,17},{9,25},{17,1},{25,9},{2,18},{10... | collective-permute-start | bytes 1462280 | tf_op jit(solution)/shard_map/ppermute | solution.py:315
  8.6 14.2 %collective-permute-start.2 = (bf16[112,2176]{1,0:T(8,128)(2,1)S(1)}, bf16[112,2176]{1,0:T(8,128)(2,1)S(1)}, u32[]{:S(2)}, u32[]{:S(2)}) collective-permute-start(bf16[112,2176]{1,0:T(8,128)(2,1)S(1)} %prepare.2.refs_2_), channel_id=1, source_target_pairs={{0,2},{1,3},{2,4},{3,5},{4,6},{5,7},{6,0},{7,1},{8,10},{9,11},{10,... | collective-permute-start | bytes 1462280 | tf_op jit(solution)/shard_map/ppermute | solution.py:319
  10.2 7.4 %collective-permute-start.3 = (bf16[2048,768]{1,0:T(8,128)(2,1)}, bf16[2048,768]{1,0:T(8,128)(2,1)}, u32[]{:S(2)}, u32[]{:S(2)}) collective-permute-start(bf16[2048,768]{1,0:T(8,128)(2,1)} %bitcast.51), channel_id=1, source_target_pairs={{0,1},{1,0},{2,3},{3,2},{4,5},{5,4},{6,7},{7,6},{8,9},{9,8},{10,11... | collective-permute-start | bytes 9437192 | tf_op jit(solution)/shard_map/ppermute | solution.py:323
  11.0 5.1 %copy-start.11 = (bf16[4,4096,1,128]{3,1,2,0:T(8,128)(2,1)S(1)}, bf16[4,4096,1,128]{3,1,2,0:T(8,128)(2,1)}, u32[]{:S(2)}) copy-start(bf16[4,4096,1,128]{3,1,2,0:T(8,128)(2,1)} %param.16) | copy-start | bytes 12582916
  12.0 4.9 %copy-start.12 = (bf16[1024,2048]{1,0:T(8,128)(2,1)S(1)}, bf16[1024,2048]{1,0:T(8,128)(2,1)}, u32[]{:S(2)}) copy-start(bf16[1024,2048]{1,0:T(8,128)(2,1)} %param.19) | copy-start | bytes 12582916
  16.8 28.1 %copy-start.3 = (bf16[2048,32]{0,1:T(8,128)(2,1)S(1)}, bf16[2048,32]{0,1:T(8,128)(2,1)}, u32[]{:S(2)}) copy-start(bf16[2048,32]{0,1:T(8,128)(2,1)} %param.23) | copy-start | bytes 393220
  16.8 28.1 %copy-start.5 = (f32[2048]{0:T(1024)S(1)}, f32[2048]{0:T(1024)}, u32[]{:S(2)}) copy-start(f32[2048]{0:T(1024)} %param.22) | copy-start | bytes 24580
  17.6 4.6 %collective-permute-start.4 = (f32[8,2048]{1,0:T(8,128)S(1)}, f32[8,2048]{1,0:T(8,128)S(1)}, u32[]{:S(2)}, u32[]{:S(2)}) collective-permute-start(f32[8,2048]{1,0:T(8,128)S(1)} %pad_maximum_fusion.1), channel_id=1, source_target_pairs={{0,8},{8,0},{16,24},{24,16},{1,9},{9,1},{17,25},{25,17},{2,10},{10... | collective-permute-start | bytes 196616 | tf_op jit(solution)/shard_map/ppermute | solution.py:311
  18.2 27.2 %collective-permute-start.11 = (bf16[2048,768]{1,0:T(8,128)(2,1)}, bf16[2048,768]{1,0:T(8,128)(2,1)}, u32[]{:S(2)}, u32[]{:S(2)}) collective-permute-start(bf16[2048,768]{1,0:T(8,128)(2,1)} %bitcast.11.refs_8_), channel_id=1, source_target_pairs={{0,1},{1,0},{2,3},{3,2},{4,5},{5,4},{6,7},{7,6},{8,9},{9,8},{10,11... | collective-permute-start | bytes 9437192 | tf_op jit(solution)/shard_map/ppermute | solution.py:323
  22.8 26.4 %collective-permute-start.12 = (bf16[768,2048]{1,0:T(8,128)(2,1)}, bf16[768,2048]{1,0:T(8,128)(2,1)}, u32[]{:S(2)}, u32[]{:S(2)}) collective-permute-start(bf16[768,2048]{1,0:T(8,128)(2,1)} %bitcast.12.refs_9_), channel_id=1, source_target_pairs={{0,1},{1,0},{2,3},{3,2},{4,5},{5,4},{6,7},{7,6},{8,9},{9,8},{10,11... | collective-permute-start | bytes 9437192 | tf_op jit(solution)/shard_map/ppermute | solution.py:323
  22.9 13.5 %collective-permute-start.5 = (bf16[112,2176]{1,0:T(8,128)(2,1)S(1)}, bf16[112,2176]{1,0:T(8,128)(2,1)S(1)}, u32[]{:S(2)}, u32[]{:S(2)}) collective-permute-start(bf16[112,2176]{1,0:T(8,128)(2,1)S(1)} %collective-permute-done.2.refs_2_), channel_id=1, source_target_pairs={{0,8},{8,0},{16,24},{24,16},{1,9},{9,1},{17,25},{25,17},{2,10},{10... | collective-permute-start | bytes 1462280 | tf_op jit(solution)/shard_map/ppermute | solution.py:311
  23.5 13.2 %collective-permute-start.6 = (bf16[112,2176]{1,0:T(8,128)(2,1)S(1)}, bf16[112,2176]{1,0:T(8,128)(2,1)S(1)}, u32[]{:S(2)}, u32[]{:S(2)}) collective-permute-start(bf16[112,2176]{1,0:T(8,128)(2,1)S(1)} %collective-permute-done.2.refs_2_), channel_id=1, source_target_pairs={{0,16},{8,24},{16,0},{24,8},{1,17},{9,25},{17,1},{25,9},{2,18},{10... | collective-permute-start | bytes 1462280 | tf_op jit(solution)/shard_map/ppermute | solution.py:315
  24.0 14.7 %collective-permute-start.7 = (bf16[112,2176]{1,0:T(8,128)(2,1)S(1)}, bf16[112,2176]{1,0:T(8,128)(2,1)S(1)}, u32[]{:S(2)}, u32[]{:S(2)}) collective-permute-start(bf16[112,2176]{1,0:T(8,128)(2,1)S(1)} %collective-permute-done.2.refs_2_), channel_id=1, source_target_pairs={{0,2},{1,3},{2,4},{3,5},{4,6},{5,7},{6,0},{7,1},{8,10},{9,11},{10,... | collective-permute-start | bytes 1462280 | tf_op jit(solution)/shard_map/ppermute | solution.py:319
  25.6 0.8 copy-start.9
  38.7 5.1 %collective-permute-start.8 = (f32[8,2048]{1,0:T(8,128)}, f32[8,2048]{1,0:T(8,128)S(1)}, u32[]{:S(2)}, u32[]{:S(2)}) collective-permute-start(f32[8,2048]{1,0:T(8,128)} %add.114), channel_id=1, source_target_pairs={{0,16},{8,24},{16,0},{24,8},{1,17},{9,25},{17,1},{25,9},{2,18},{10... | collective-permute-start | bytes 196616 | tf_op jit(solution)/shard_map/ppermute | solution.py:315
  41.1 8.1 %collective-permute-start.9 = (bf16[64,2176]{1,0:T(8,128)(2,1)}, bf16[64,2176]{1,0:T(8,128)(2,1)S(1)}, u32[]{:S(2)}, u32[]{:S(2)}) collective-permute-start(bf16[64,2176]{1,0:T(8,128)(2,1)} %slice.42), channel_id=1, source_target_pairs={{0,16},{8,24},{16,0},{24,8},{1,17},{9,25},{17,1},{25,9},{2,18},{10... | collective-permute-start | bytes 835592 | tf_op jit(solution)/shard_map/ppermute | solution.py:315
  42.3 6.1 %collective-permute-start.10 = (bf16[48,2176]{1,0:T(8,128)(2,1)}, bf16[48,2176]{1,0:T(8,128)(2,1)}, u32[]{:S(2)}, u32[]{:S(2)}) collective-permute-start(bf16[48,2176]{1,0:T(8,128)(2,1)} %slice.43), channel_id=1, source_target_pairs={{0,8},{8,0},{16,24},{24,16},{1,9},{9,1},{17,25},{25,17},{2,10},{10... | collective-permute-start | bytes 626696 | tf_op jit(solution)/shard_map/ppermute | solution.py:311
  49.2 21.3 %collective-permute-start.15 = (bf16[112,2176]{1,0:T(8,128)(2,1)S(1)}, bf16[112,2176]{1,0:T(8,128)(2,1)S(1)}, u32[]{:S(2)}, u32[]{:S(2)}) collective-permute-start(bf16[112,2176]{1,0:T(8,128)(2,1)S(1)} %collective-permute-done.7.refs_2_), channel_id=1, source_target_pairs={{0,8},{8,0},{16,24},{24,16},{1,9},{9,1},{17,25},{25,17},{2,10},{10... | collective-permute-start | bytes 1462280 | tf_op jit(solution)/shard_map/ppermute | solution.py:311
  50.7 19.8 %collective-permute-start.16 = (bf16[112,2176]{1,0:T(8,128)(2,1)S(1)}, bf16[112,2176]{1,0:T(8,128)(2,1)S(1)}, u32[]{:S(2)}, u32[]{:S(2)}) collective-permute-start(bf16[112,2176]{1,0:T(8,128)(2,1)S(1)} %collective-permute-done.7.refs_2_), channel_id=1, source_target_pairs={{0,16},{8,24},{16,0},{24,8},{1,17},{9,25},{17,1},{25,9},{2,18},{10... | collective-permute-start | bytes 1462280 | tf_op jit(solution)/shard_map/ppermute | solution.py:315
  51.5 19.0 %collective-permute-start.17 = (bf16[128,2176]{1,0:T(8,128)(2,1)S(1)}, bf16[128,2176]{1,0:T(8,128)(2,1)S(1)}, u32[]{:S(2)}, u32[]{:S(2)}) collective-permute-start(bf16[128,2176]{1,0:T(8,128)(2,1)S(1)} %pad_maximum_fusion), channel_id=1, source_target_pairs={{0,2},{1,3},{2,4},{3,5},{4,6},{5,7},{6,0},{7,1},{8,10},{9,11},{10,... | collective-permute-start | bytes 1671176 | tf_op jit(solution)/shard_map/ppermute | solution.py:319
  51.6 18.9 %collective-permute-start.14 = (bf16[64,2176]{1,0:T(8,128)(2,1)S(1)}, bf16[64,2176]{1,0:T(8,128)(2,1)S(1)}, u32[]{:S(2)}, u32[]{:S(2)}) collective-permute-start(bf16[64,2176]{1,0:T(8,128)(2,1)S(1)} %slice.46), channel_id=1, source_target_pairs={{0,8},{8,0},{16,24},{24,16},{1,9},{9,1},{17,25},{25,17},{2,10},{10... | collective-permute-start | bytes 835592 | tf_op jit(solution)/shard_map/ppermute | solution.py:311
  52.2 18.3 %collective-permute-start.13 = (bf16[48,2176]{1,0:T(8,128)(2,1)S(1)}, bf16[48,2176]{1,0:T(8,128)(2,1)S(1)}, u32[]{:S(2)}, u32[]{:S(2)}) collective-permute-start(bf16[48,2176]{1,0:T(8,128)(2,1)S(1)} %slice.45), channel_id=1, source_target_pairs={{0,16},{8,24},{16,0},{24,8},{1,17},{9,25},{17,1},{25,9},{2,18},{10... | collective-permute-start | bytes 626696 | tf_op jit(solution)/shard_map/ppermute | solution.py:315
  53.5 1.9 %copy-start.7 = (bf16[1,2048,768]{2,1,0:T(8,128)(2,1)S(1)}, bf16[1,2048,768]{2,1,0:T(8,128)(2,1)}, u32[]{:S(2)}) copy-start(bf16[1,2048,768]{2,1,0:T(8,128)(2,1)} %param.25) | copy-start | bytes 9437188
  55.4 20.8 %copy-start.8 = (bf16[1,2048,768]{2,1,0:T(8,128)(2,1)S(1)}, bf16[1,2048,768]{2,1,0:T(8,128)(2,1)}, u32[]{:S(2)}) copy-start(bf16[1,2048,768]{2,1,0:T(8,128)(2,1)} %param.25) | copy-start | bytes 9437188
  55.4 20.8 %copy-start.10 = (bf16[112,2176]{1,0:T(8,128)(2,1)S(1)}, bf16[112,2176]{1,0:T(8,128)(2,1)}, u32[]{:S(2)}) copy-start(bf16[112,2176]{1,0:T(8,128)(2,1)} %copy-done.9) | copy-start | bytes 1462276
  70.6 19.8 %collective-permute-start.20 = (bf16[112,2176]{1,0:T(8,128)(2,1)S(1)}, bf16[112,2176]{1,0:T(8,128)(2,1)S(1)}, u32[]{:S(2)}, u32[]{:S(2)}) collective-permute-start(bf16[112,2176]{1,0:T(8,128)(2,1)S(1)} %slice.49.refs_2_), channel_id=1, source_target_pairs={{0,8},{8,0},{16,24},{24,16},{1,9},{9,1},{17,25},{25,17},{2,10},{10... | collective-permute-start | bytes 1462280 | tf_op jit(solution)/shard_map/ppermute | solution.py:311
  72.1 18.3 %collective-permute-start.21 = (bf16[112,2176]{1,0:T(8,128)(2,1)S(1)}, bf16[112,2176]{1,0:T(8,128)(2,1)S(1)}, u32[]{:S(2)}, u32[]{:S(2)}) collective-permute-start(bf16[112,2176]{1,0:T(8,128)(2,1)S(1)} %slice.49.refs_2_), channel_id=1, source_target_pairs={{0,16},{8,24},{16,0},{24,8},{1,17},{9,25},{17,1},{25,9},{2,18},{10... | collective-permute-start | bytes 1462280 | tf_op jit(solution)/shard_map/ppermute | solution.py:315
  72.9 17.5 %collective-permute-start.18 = (bf16[64,2176]{1,0:T(8,128)(2,1)S(1)}, bf16[64,2176]{1,0:T(8,128)(2,1)S(1)}, u32[]{:S(2)}, u32[]{:S(2)}) collective-permute-start(bf16[64,2176]{1,0:T(8,128)(2,1)S(1)} %slice.47), channel_id=1, source_target_pairs={{0,16},{8,24},{16,0},{24,8},{1,17},{9,25},{17,1},{25,9},{2,18},{10... | collective-permute-start | bytes 835592 | tf_op jit(solution)/shard_map/ppermute | solution.py:315
  74.2 16.1 %collective-permute-start.19 = (bf16[48,2176]{1,0:T(8,128)(2,1)S(1)}, bf16[48,2176]{1,0:T(8,128)(2,1)S(1)}, u32[]{:S(2)}, u32[]{:S(2)}) collective-permute-start(bf16[48,2176]{1,0:T(8,128)(2,1)S(1)} %slice.48), channel_id=1, source_target_pairs={{0,8},{8,0},{16,24},{24,16},{1,9},{9,1},{17,25},{25,17},{2,10},{10... | collective-permute-start | bytes 626696 | tf_op jit(solution)/shard_map/ppermute | solution.py:311
  74.8 15.5 %collective-permute-start.22 = (bf16[16,2176]{1,0:T(8,128)(2,1)S(1)}, bf16[16,2176]{1,0:T(8,128)(2,1)S(1)}, u32[]{:S(2)}, u32[]{:S(2)}) collective-permute-start(bf16[16,2176]{1,0:T(8,128)(2,1)S(1)} %slice.50.refs_1_), channel_id=1, source_target_pairs={{0,2},{1,3},{2,4},{3,5},{4,6},{5,7},{6,0},{7,1},{8,10},{9,11},{10,... | collective-permute-start | bytes 208904 | tf_op jit(solution)/shard_map/ppermute | solution.py:319
  90.4 18.9 %collective-permute-start.24 = (bf16[64,2176]{1,0:T(8,128)(2,1)S(1)}, bf16[64,2176]{1,0:T(8,128)(2,1)S(1)}, u32[]{:S(2)}, u32[]{:S(2)}) collective-permute-start(bf16[64,2176]{1,0:T(8,128)(2,1)S(1)} %slice.52), channel_id=1, source_target_pairs={{0,8},{8,0},{16,24},{24,16},{1,9},{9,1},{17,25},{25,17},{2,10},{10... | collective-permute-start | bytes 835592 | tf_op jit(solution)/shard_map/ppermute | solution.py:311
  92.0 17.3 %collective-permute-start.23 = (bf16[48,2176]{1,0:T(8,128)(2,1)S(1)}, bf16[48,2176]{1,0:T(8,128)(2,1)S(1)}, u32[]{:S(2)}, u32[]{:S(2)}) collective-permute-start(bf16[48,2176]{1,0:T(8,128)(2,1)S(1)} %slice.51), channel_id=1, source_target_pairs={{0,16},{8,24},{16,0},{24,8},{1,17},{9,25},{17,1},{25,9},{2,18},{10... | collective-permute-start | bytes 626696 | tf_op jit(solution)/shard_map/ppermute | solution.py:315
  92.8 16.5 %collective-permute-start.27 = (bf16[64,2048]{1,0:T(8,128)(2,1)S(1)}, bf16[64,2048]{1,0:T(8,128)(2,1)S(1)}, u32[]{:S(2)}, u32[]{:S(2)}) collective-permute-start(bf16[64,2048]{1,0:T(8,128)(2,1)S(1)} %get-tuple-element.173), channel_id=1, source_target_pairs={{0,8},{8,0},{16,24},{24,16},{1,9},{9,1},{17,25},{25,17},{2,10},{10... | collective-permute-start | bytes 786440 | tf_op jit(solution)/shard_map/ppermute | solution.py:311
  93.4 15.9 %collective-permute-start.26 = (bf16[48,2048]{1,0:T(8,128)(2,1)S(1)}, bf16[48,2048]{1,0:T(8,128)(2,1)S(1)}, u32[]{:S(2)}, u32[]{:S(2)}) collective-permute-start(bf16[48,2048]{1,0:T(8,128)(2,1)S(1)} %get-tuple-element.172), channel_id=1, source_target_pairs={{0,16},{8,24},{16,0},{24,8},{1,17},{9,25},{17,1},{25,9},{2,18},{10... | collective-permute-start | bytes 589832 | tf_op jit(solution)/shard_map/ppermute | solution.py:315
  94.7 14.6 %collective-permute-start.25 = (bf16[16,2176]{1,0:T(8,128)(2,1)S(1)}, bf16[16,2176]{1,0:T(8,128)(2,1)S(1)}, u32[]{:S(2)}, u32[]{:S(2)}) collective-permute-start(bf16[16,2176]{1,0:T(8,128)(2,1)S(1)} %collective-permute-done.22.refs_1_), channel_id=1, source_target_pairs={{0,2},{1,3},{2,4},{3,5},{4,6},{5,7},{6,0},{7,1},{8,10},{9,11},{10,... | collective-permute-start | bytes 208904 | tf_op jit(solution)/shard_map/ppermute | solution.py:319
  109.5 18.3 %collective-permute-start.28 = (bf16[112,2048]{1,0:T(8,128)(2,1)S(1)}, bf16[112,2048]{1,0:T(8,128)(2,1)S(1)}, u32[]{:S(2)}, u32[]{:S(2)}) collective-permute-start(bf16[112,2048]{1,0:T(8,128)(2,1)S(1)} %get-tuple-element.188), channel_id=1, source_target_pairs={{0,8},{8,0},{16,24},{24,16},{1,9},{9,1},{17,25},{25,17},{2,10},{10... | collective-permute-start | bytes 1376264 | tf_op jit(solution)/shard_map/ppermute | solution.py:311
  110.8 16.9 %collective-permute-start.29 = (bf16[112,2048]{1,0:T(8,128)(2,1)S(1)}, bf16[112,2048]{1,0:T(8,128)(2,1)S(1)}, u32[]{:S(2)}, u32[]{:S(2)}) collective-permute-start(bf16[112,2048]{1,0:T(8,128)(2,1)S(1)} %get-tuple-element.189), channel_id=1, source_target_pairs={{0,16},{8,24},{16,0},{24,8},{1,17},{9,25},{17,1},{25,9},{2,18},{10... | collective-permute-start | bytes 1376264 | tf_op jit(solution)/shard_map/ppermute | solution.py:315
  111.6 16.2 %collective-permute-start.30 = (bf16[64,2048]{1,0:T(8,128)(2,1)S(1)}, bf16[64,2048]{1,0:T(8,128)(2,1)S(1)}, u32[]{:S(2)}, u32[]{:S(2)}) collective-permute-start(bf16[64,2048]{1,0:T(8,128)(2,1)S(1)} %get-tuple-element.190), channel_id=1, source_target_pairs={{0,16},{8,24},{16,0},{24,8},{1,17},{9,25},{17,1},{25,9},{2,18},{10... | collective-permute-start | bytes 786440 | tf_op jit(solution)/shard_map/ppermute | solution.py:315
  112.9 14.9 %collective-permute-start.31 = (bf16[48,2048]{1,0:T(8,128)(2,1)S(1)}, bf16[48,2048]{1,0:T(8,128)(2,1)S(1)}, u32[]{:S(2)}, u32[]{:S(2)}) collective-permute-start(bf16[48,2048]{1,0:T(8,128)(2,1)S(1)} %get-tuple-element.191), channel_id=1, source_target_pairs={{0,8},{8,0},{16,24},{24,16},{1,9},{9,1},{17,25},{25,17},{2,10},{10... | collective-permute-start | bytes 589832 | tf_op jit(solution)/shard_map/ppermute | solution.py:311
  128.0 50.4 %copy-start.1 = (bf16[1,111,2048]{2,1,0:T(8,128)(2,1)S(1)}, bf16[1,111,2048]{2,1,0:T(8,128)(2,1)}, u32[]{:S(2)}) copy-start(bf16[1,111,2048]{2,1,0:T(8,128)(2,1)} %param.21) | copy-start | bytes 1363972
  128.0 19.9 %collective-permute-start.36 = (bf16[112,2048]{1,0:T(8,128)(2,1)S(1)}, bf16[112,2048]{1,0:T(8,128)(2,1)S(1)}, u32[]{:S(2)}, u32[]{:S(2)}) collective-permute-start(bf16[112,2048]{1,0:T(8,128)(2,1)S(1)} %add_convert_fusion.3), channel_id=1, source_target_pairs={{0,2},{1,3},{2,4},{3,5},{4,6},{5,7},{6,0},{7,1},{8,10},{9,11},{10,... | collective-permute-start | bytes 1376264 | tf_op jit(solution)/shard_map/ppermute | solution.py:319
  131.5 16.4 %collective-permute-start.32 = (bf16[112,2048]{1,0:T(8,128)(2,1)S(1)}, bf16[112,2048]{1,0:T(8,128)(2,1)S(1)}, u32[]{:S(2)}, u32[]{:S(2)}) collective-permute-start(bf16[112,2048]{1,0:T(8,128)(2,1)S(1)} %get-tuple-element.208), channel_id=1, source_target_pairs={{0,8},{8,0},{16,24},{24,16},{1,9},{9,1},{17,25},{25,17},{2,10},{10... | collective-permute-start | bytes 1376264 | tf_op jit(solution)/shard_map/ppermute | solution.py:311
  133.1 14.9 %collective-permute-start.33 = (bf16[112,2048]{1,0:T(8,128)(2,1)S(1)}, bf16[112,2048]{1,0:T(8,128)(2,1)S(1)}, u32[]{:S(2)}, u32[]{:S(2)}) collective-permute-start(bf16[112,2048]{1,0:T(8,128)(2,1)S(1)} %get-tuple-element.209), channel_id=1, source_target_pairs={{0,16},{8,24},{16,0},{24,8},{1,17},{9,25},{17,1},{25,9},{2,18},{10... | collective-permute-start | bytes 1376264 | tf_op jit(solution)/shard_map/ppermute | solution.py:315
  133.8 14.1 %collective-permute-start.35 = (bf16[64,2048]{1,0:T(8,128)(2,1)S(1)}, bf16[64,2048]{1,0:T(8,128)(2,1)S(1)}, u32[]{:S(2)}, u32[]{:S(2)}) collective-permute-start(bf16[64,2048]{1,0:T(8,128)(2,1)S(1)} %get-tuple-element.211), channel_id=1, source_target_pairs={{0,8},{8,0},{16,24},{24,16},{1,9},{9,1},{17,25},{25,17},{2,10},{10... | collective-permute-start | bytes 786440 | tf_op jit(solution)/shard_map/ppermute | solution.py:311
  134.4 13.6 %collective-permute-start.34 = (bf16[48,2048]{1,0:T(8,128)(2,1)S(1)}, bf16[48,2048]{1,0:T(8,128)(2,1)S(1)}, u32[]{:S(2)}, u32[]{:S(2)}) collective-permute-start(bf16[48,2048]{1,0:T(8,128)(2,1)S(1)} %get-tuple-element.210), channel_id=1, source_target_pairs={{0,16},{8,24},{16,0},{24,8},{1,17},{9,25},{17,1},{25,9},{2,18},{10... | collective-permute-start | bytes 589832 | tf_op jit(solution)/shard_map/ppermute | solution.py:315
  148.3 17.6 %collective-permute-start.41 = (bf16[112,2048]{1,0:T(8,128)(2,1)S(1)}, bf16[112,2048]{1,0:T(8,128)(2,1)S(1)}, u32[]{:S(2)}, u32[]{:S(2)}) collective-permute-start(bf16[112,2048]{1,0:T(8,128)(2,1)S(1)} %add_convert_fusion.2), channel_id=1, source_target_pairs={{0,2},{1,3},{2,4},{3,5},{4,6},{5,7},{6,0},{7,1},{8,10},{9,11},{10,... | collective-permute-start | bytes 1376264 | tf_op jit(solution)/shard_map/ppermute | solution.py:319
  148.5 17.4 %collective-permute-start.37 = (bf16[112,2048]{1,0:T(8,128)(2,1)S(1)}, bf16[112,2048]{1,0:T(8,128)(2,1)S(1)}, u32[]{:S(2)}, u32[]{:S(2)}) collective-permute-start(bf16[112,2048]{1,0:T(8,128)(2,1)S(1)} %get-tuple-element.228), channel_id=1, source_target_pairs={{0,8},{8,0},{16,24},{24,16},{1,9},{9,1},{17,25},{25,17},{2,10},{10... | collective-permute-start | bytes 1376264 | tf_op jit(solution)/shard_map/ppermute | solution.py:311
  149.6 16.2 %collective-permute-start.38 = (bf16[112,2048]{1,0:T(8,128)(2,1)S(1)}, bf16[112,2048]{1,0:T(8,128)(2,1)S(1)}, u32[]{:S(2)}, u32[]{:S(2)}) collective-permute-start(bf16[112,2048]{1,0:T(8,128)(2,1)S(1)} %get-tuple-element.229), channel_id=1, source_target_pairs={{0,16},{8,24},{16,0},{24,8},{1,17},{9,25},{17,1},{25,9},{2,18},{10... | collective-permute-start | bytes 1376264 | tf_op jit(solution)/shard_map/ppermute | solution.py:315
  150.5 15.4 %collective-permute-start.39 = (bf16[64,2048]{1,0:T(8,128)(2,1)S(1)}, bf16[64,2048]{1,0:T(8,128)(2,1)S(1)}, u32[]{:S(2)}, u32[]{:S(2)}) collective-permute-start(bf16[64,2048]{1,0:T(8,128)(2,1)S(1)} %get-tuple-element.230), channel_id=1, source_target_pairs={{0,16},{8,24},{16,0},{24,8},{1,17},{9,25},{17,1},{25,9},{2,18},{10... | collective-permute-start | bytes 786440 | tf_op jit(solution)/shard_map/ppermute | solution.py:315
  151.7 12.4 %collective-permute-start.40 = (bf16[48,2048]{1,0:T(8,128)(2,1)S(1)}, bf16[48,2048]{1,0:T(8,128)(2,1)S(1)}, u32[]{:S(2)}, u32[]{:S(2)}) collective-permute-start(bf16[48,2048]{1,0:T(8,128)(2,1)S(1)} %get-tuple-element.231), channel_id=1, source_target_pairs={{0,8},{8,0},{16,24},{24,16},{1,9},{9,1},{17,25},{25,17},{2,10},{10... | collective-permute-start | bytes 589832 | tf_op jit(solution)/shard_map/ppermute | solution.py:311
  166.0 8.5 %collective-permute-start.42 = (bf16[112,2048]{1,0:T(8,128)(2,1)S(1)}, bf16[112,2048]{1,0:T(8,128)(2,1)S(1)}, u32[]{:S(2)}, u32[]{:S(2)}) collective-permute-start(bf16[112,2048]{1,0:T(8,128)(2,1)S(1)} %get-tuple-element.245), channel_id=1, source_target_pairs={{0,8},{8,0},{16,24},{24,16},{1,9},{9,1},{17,25},{25,17},{2,10},{10... | collective-permute-start | bytes 1376264 | tf_op jit(solution)/shard_map/ppermute | solution.py:311
  167.0 8.5 %collective-permute-start.43 = (bf16[112,2048]{1,0:T(8,128)(2,1)S(1)}, bf16[112,2048]{1,0:T(8,128)(2,1)S(1)}, u32[]{:S(2)}, u32[]{:S(2)}) collective-permute-start(bf16[112,2048]{1,0:T(8,128)(2,1)S(1)} %get-tuple-element.246), channel_id=1, source_target_pairs={{0,16},{8,24},{16,0},{24,8},{1,17},{9,25},{17,1},{25,9},{2,18},{10... | collective-permute-start | bytes 1376264 | tf_op jit(solution)/shard_map/ppermute | solution.py:315
  168.1 10.3 %collective-permute-start.44 = (bf16[112,2048]{1,0:T(8,128)(2,1)S(1)}, bf16[112,2048]{1,0:T(8,128)(2,1)S(1)}, u32[]{:S(2)}, u32[]{:S(2)}) collective-permute-start(bf16[112,2048]{1,0:T(8,128)(2,1)S(1)} %add_convert_fusion.1), channel_id=1, source_target_pairs={{0,2},{1,3},{2,4},{3,5},{4,6},{5,7},{6,0},{7,1},{8,10},{9,11},{10,... | collective-permute-start | bytes 1376264 | tf_op jit(solution)/shard_map/ppermute | solution.py:319

commit v7 on v5

--- a/solution.py
+++ b/solution.py
@@ -304,19 +304,20 @@
     )(ids, decodes, *pieces, *weights)
 
 
-def merge_kernel(cut, x_ref, y_ref, passed_0_ref, passed_1_ref, x_out, y_out):
+def merge_kernel(cut, at_0, at_1, x_ref, y_ref, passed_0_ref, passed_1_ref, x_out, y_out):
     def sum_of(one, other):
         return (one.astype(jnp.float32) + other.astype(jnp.float32)).astype(jnp.bfloat16)
 
-    x_out[:cut, :] = sum_of(x_ref[:cut, :], passed_0_ref[...])
+    rest = x_ref.shape[0] - cut
+    x_out[:cut, :] = sum_of(x_ref[:cut, :], passed_0_ref[at_0 : at_0 + cut, :])
     x_out[cut:, :] = x_ref[cut:, :]
     y_out[:cut, :] = y_ref[:cut, :]
-    y_out[cut:, :] = sum_of(y_ref[cut:, :], passed_1_ref[...])
-
-
-def merge_passed(cut, to_x, to_y, passed_0, passed_1):
+    y_out[cut:, :] = sum_of(y_ref[cut:, :], passed_1_ref[at_1 : at_1 + rest, :])
+
+
+def merge_passed(cut, to_x, to_y, passed_0, passed_1, at_0=0, at_1=0):
     return pl.pallas_call(
-        functools.partial(merge_kernel, cut),
+        functools.partial(merge_kernel, cut, at_0, at_1),
         out_shape=[jax.ShapeDtypeStruct(to_x.shape, to_x.dtype)] * 2,
         compiler_params=pltpu.CompilerParams(vmem_limit_bytes=16 << 20),
         name="merge",
@@ -329,10 +330,6 @@
 
 def along_y(value):
     return lax.ppermute(value, "kv", [(i, i ^ 2) for i in range(4)])
-
-
-def along_diagonal(value):
-    return lax.ppermute(value, "kv", [(i, i ^ 3) for i in range(4)])
 
 
 def around_z(value):
@@ -409,14 +406,6 @@
         to_x, to_y = merge_passed(cuts[step], sums[step][1], sums[step][2], *passed[step])
         back[step] = along_x(to_x), along_y(to_y)
 
-    prefill = prefill_hidden[0]
-    blocks[0] = prepare(prefill, norm_gain, router, ids, "block")
-    blocks[0], queries, cache_keys, expert_gate, expert_up = fence(
-        blocks[0], queries, cache_keys, expert_gate, expert_up
-    )
-    spread_sides(0)
-    corners[0] = (along_diagonal(blocks[0]),)
-    blocks[1] = around_z(blocks[0])
     other_gate = across_chip(expert_gate[0])
     other_up = across_chip(expert_up[0])
 
@@ -428,16 +417,23 @@
     ids_row = jnp.pad(ids[:1].astype(jnp.float32), ((0, 0), (0, width - ids.shape[1])))
     shared = jnp.concatenate([partial_proj, jnp.where(is_mine, ids_row, 0.0)], axis=0)
 
-    shared, other_gate = fence(shared, other_gate)
+    prefill = prefill_hidden[0]
+    blocks[0] = prepare(prefill, norm_gain, router, ids, "block")
+    blocks[0], shared, other_gate = fence(blocks[0], shared, other_gate)
     shared = shared + along_x(shared)
-    sides[0], corners[0], blocks[1], shared, expert_down = fence(
-        sides[0], corners[0], blocks[1], shared, expert_down
-    )
-
+    spread_sides(0)
+    blocks[1] = around_z(blocks[0])
+    shared = shared + along_y(shared)
+    sides[0], blocks[1], shared, other_gate, other_up, expert_down = fence(
+        sides[0], blocks[1], shared, other_gate, other_up, expert_down
+    )
+
+    other_down = across_chip(expert_down[0])
     spread_sides(1)
     blocks[2] = around_z(blocks[1])
-    other_down = across_chip(expert_down[0])
-    shared = shared + along_y(shared)
+    by_y, by_x = sides[0][0][: cuts[0]], sides[0][1][cuts[0] :]
+    by_y, other_down = fence(by_y, other_down)
+    corners[0] = along_y(by_y), along_x(by_x)
     order = [my_kv ^ j for j in range(4)]
     decoded = jnp.concatenate(
         [lax.dynamic_slice_in_dim(shared, index, 1) for index in order], axis=0
@@ -453,7 +449,9 @@
         jnp.pad(decode_ids, ((0, 12), (0, 0))),
         "first",
     )
-    sides[1], blocks[2], decodes[0], other_up = fence(sides[1], blocks[2], decodes[0], other_up)
+    corners[0], sides[1], blocks[2], decodes[0], other_down = fence(
+        corners[0], sides[1], blocks[2], decodes[0], other_down
+    )
     weights = (expert_gate[0], expert_up[0], expert_down[0], other_gate, other_up, other_down)
 
     spread_corners(1)
@@ -467,15 +465,20 @@
     spread_sides(3)
     decodes[2] = around_z(decodes[1])
     apply(1)
-    corners[2], sides[3], decodes[2], sums[1] = fence(corners[2], sides[3], decodes[2], sums[1])
+    corners[2], sides[3], decodes[2], sums[0], sums[1] = fence(
+        corners[2], sides[3], decodes[2], sums[0], sums[1]
+    )
 
     spread_corners(3)
     decodes[3] = around_z(decodes[2])
-    return_corners(1)
+    by_y = along_y(jnp.concatenate([sums[0][3], sums[1][3]], axis=0))
+    by_x = along_x(jnp.concatenate([sums[0][4], sums[1][4]], axis=0))
+    passed[0] = by_y, by_x
     apply(2)
-    corners[3], decodes[3], passed[1], sums[1], sums[2] = fence(
-        corners[3], decodes[3], passed[1], sums[1], sums[2]
-    )
+    corners[3], decodes[3], passed[0], sums[1], sums[2] = fence(
+        corners[3], decodes[3], passed[0], sums[1], sums[2]
+    )
+    passed[1] = passed[0] + (cuts[0], tokens - cuts[0])
 
     return_sides(1)
     return_corners(2)
@@ -484,20 +487,12 @@
         back[1], passed[2], sums[1], sums[2], sums[3]
     )
 
+    return_corners(3)
     return_sides(2)
-    return_corners(3)
     carried = around_z(added(sums[1][0], *back[1]).astype(jnp.bfloat16))
-    back[2], passed[3], carried, sums[2], sums[3], sums[0] = fence(
-        back[2], passed[3], carried, sums[2], sums[3], sums[0]
-    )
-
     return_sides(3)
-    return_corners(0)
     carried = around_z(added(sums[2][0], *back[2], carried).astype(jnp.bfloat16))
-    back[3], passed[0], carried, sums[3], sums[0] = fence(
-        back[3], passed[0], carried, sums[3], sums[0]
-    )
-
+    back[3], passed[0], sums[0] = fence(back[3], passed[0], sums[0])
     return_sides(0)
     carried = around_z(added(sums[3][0], *back[3], carried).astype(jnp.bfloat16))
     return added(hidden, sums[0][0], *back[0], carried).astype(jnp.bfloat16)[None]

time: 174 us -> 175 us (level)
  waiting for transfers between devices: 58.5 us -> 67.3 us
  starting transfers between devices: 48 us -> 43.3 us
  local copies, waits for them, and re-layouts: 7.31 us -> 3.66 us
    ppermute x16, waiting for transfers between devices: 35.1 us -> 41.8 us  [along_x(): return lax.ppermute(value, 'kv', [(i, i ^ 1) for i in range(4)])]
    ppermute x16, starting transfers between devices: 17.3 us -> 13.6 us  [along_y(): return lax.ppermute(value, 'kv', [(i, i ^ 2) for i in range(4)])]
    unnamed x28 -> x20, local copies, waits for them, and re-layouts: 7.01 us -> 3.33 us
    ppermute x16, starting transfers between devices: 20.3 us -> 17.1 us  [along_x(): return lax.ppermute(value, 'kv', [(i, i ^ 1) for i in range(4)])]
    ppermute x8, starting transfers between devices: 9.79 us -> 12 us  [around_z(): return lax.ppermute(value, 'blk', [(i, (i + 2) % 8) for i in range(8)])]
    ppermute x16, waiting for transfers between devices: 17.5 us -> 19.3 us  [along_y(): return lax.ppermute(value, 'kv', [(i, i ^ 2) for i in range(4)])]
  transfers between devices with their start and end apart: 44 -> 43, of which waited for: 11 -> 15; matrix products, arithmetic and copies ran while one was open for 5% -> 5% of each run, Pallas kernels for 28% -> 29%
where the time goes in v7:
time: 175 us
  waiting for transfers between devices  67.3 us (38%)
  Pallas kernels  49.8 us (28%)
  starting transfers between devices  43.3 us (25%)
  matrix products  5.25 us (3%)
  other arithmetic  4.94 us (3%)
  local copies, waits for them, and re-layouts  3.66 us (2%)
    pallas_call x4, Pallas kernels, run_plane(): pl.pallas_call(functools.partial(plane_kernel, cap, piece_rows, block_row...  48.1 us
    ppermute x16, waiting for transfers between devices, along_x(): return lax.ppermute(value, 'kv', [(i, i ^ 1) for i in range(4)])  41.8 us
    ppermute x16, waiting for transfers between devices, along_y(): return lax.ppermute(value, 'kv', [(i, i ^ 2) for i in range(4)])  19.3 us
    ppermute x16, starting transfers between devices, along_x(): return lax.ppermute(value, 'kv', [(i, i ^ 1) for i in range(4)])  17.1 us
    ppermute x16, starting transfers between devices, along_y(): return lax.ppermute(value, 'kv', [(i, i ^ 2) for i in range(4)])  13.6 us
    ppermute x8, starting transfers between devices, around_z(): return lax.ppermute(value, 'blk', [(i, (i + 2) % 8) for i in range(8)])  12 us
    ppermute x8, waiting for transfers between devices, around_z(): return lax.ppermute(value, 'blk', [(i, (i + 2) % 8) for i in range(8)])  4.6 us
    dot_general x1, matrix products, attend(): jnp.einsum('rgd,rjd->rgj', grouped_q, key_rows, preferred_element_type=jn...  3.86 us
  transfers between devices with their start and end apart: 43, of which 15 were waited for; matrix products, arithmetic and copies ran while one was open for 5% of the time, Pallas kernels for 29%

profile of v7, /device:TPU:0, one launch (start us, length us, event | category | flops | bytes accessed | tf_op | source)
XLA Modules:
  0.0 174.6 jit_solution(5555677524147739049)
XLA Ops:
  0.5 0.7 minimum_subtract_fusion
  1.3 0.7 broadcast_in_dim.76
  2.1 0.8 convert_reduce_fusion
  2.9 1.0 copy-done
  3.9 0.9 copy-done.2
  4.8 0.7 copy-done.4
  5.5 0.7 copy-done.6
  6.2 0.8 prepare.2.refs_2_
  7.0 3.9 %fusion.33 = (f32[4,8]{1,0:T(4,128)S(1)}, f32[4,8,4096]{2,1,0:T(8,128)S(1)}) fusion(bf16[4,4096,1,128]{3,1,2,0:T(8,128)(2,1)} %param.15, bf16[1,4,8,128]{3,1,2,0:T(4,128)(2,1)} %bitcast.53, pred[4,4096]{1,0:T(4,128)(4,1)S(1)} %iota_compare_fusion.1), kind=kOutput, calls=%fused_computation.58 | convolution fusion | flops 33947616 | bytes 4743296 | tf_op jit(solution)/shard_map/rgd,rjd->rgj/dot_general | solution.py:27
  11.1 0.7 fusion.10
  11.9 0.7 convolution_add_fusion
  12.7 3.1 %collective-permute-start.3 = (bf16[112,2176]{1,0:T(8,128)(2,1)S(1)}, bf16[112,2176]{1,0:T(8,128)(2,1)}, u32[]{:S(2)}, u32[]{:S(2)}) collective-permute-start(bf16[112,2176]{1,0:T(8,128)(2,1)S(1)} %prepare.2.refs_2_), channel_id=1, source_target_pairs={{0,2},{1,3},{2,4},{3,5},{4,6},{5,7},{6,0},{7,1},{8,10},{9,11},{10,... | collective-permute-start | bytes 1462280 | tf_op jit(solution)/shard_map/ppermute | solution.py:336
  15.7 1.5 collective-permute-start.2
  17.3 1.5 collective-permute-start.1
  18.8 0.5 collective-permute-start.4
  19.3 11.9 %collective-permute-done.4 = f32[8,2048]{1,0:T(8,128)S(1)} collective-permute-done((f32[8,2048]{1,0:T(8,128)S(1)}, f32[8,2048]{1,0:T(8,128)S(1)}, u32[]{:S(2)}, u32[]{:S(2)}) %collective-permute-start.4) | collective-permute-done | bytes 65568 | tf_op jit(solution)/shard_map/ppermute | solution.py:328
  31.2 0.6 collective-permute-start.5
  31.8 3.8 %collective-permute-done.5 = f32[8,2048]{1,0:T(8,128)S(1)} collective-permute-done((f32[8,2048]{1,0:T(8,128)S(1)}, f32[8,2048]{1,0:T(8,128)S(1)}, u32[]{:S(2)}, u32[]{:S(2)}) %collective-permute-start.5) | collective-permute-done | bytes 65568 | tf_op jit(solution)/shard_map/ppermute | solution.py:332
  35.8 1.6 collective-permute-start.12
  37.9 1.5 collective-permute-start.10
  39.6 0.6 collective-permute-start.9
  40.2 1.5 collective-permute-done.7.refs_12_
  42.8 12.8 %collective-permute-done.9.refs_6_ = bf16[48,2176]{1,0:T(8,128)(2,1)S(1)} collective-permute-done((bf16[48,2176]{1,0:T(8,128)(2,1)S(1)}, bf16[48,2176]{1,0:T(8,128)(2,1)S(1)}, u32[]{:S(2)}, u32[]{:S(2)}) %collective-permute-start.9) | collective-permute-done | bytes 208928 | tf_op jit(solution)/shard_map/ppermute | solution.py:328
  55.5 1.2 collective-permute-done.8.refs_5_
  56.8 0.5 collective-permute-start.16
  57.3 1.5 collective-permute-start.15
  58.8 1.6 collective-permute-start.13
  60.4 0.6 collective-permute-start.14
  61.1 1.6 collective-permute-start.17
  62.7 12.0 %plane.4 = (bf16[112,2048]{1,0:T(8,128)(2,1)S(1)}, bf16[112,2048]{1,0:T(8,128)(2,1)S(1)}, bf16[112,2048]{1,0:T(8,128)(2,1)S(1)}, bf16[64,2048]{1,0:T(8,128)(2,1)S(1)}, bf16[48,2048]{1,0:T(8,128)(2,1)S(1)}) custom-call(s32[3]{0:T(128)S(1)} %pad_add_fusion.refs_0_, bf16[16,2176]{1,0:T(8,128)(2,1)S(1)} %prepare.3.refs_1_, ...), custom_call_target="tpu_custom_call" | custom-call | flops 8455716864 | bytes 25165824 | tf_op jit(solution)/shard_map/plane/pallas_call | solution.py:280
  74.7 0.6 collective-permute-done.14.refs_6_
  75.7 1.3 collective-permute-start.21
  77.0 1.5 collective-permute-start.20
  78.5 1.6 collective-permute-start.22
  80.1 0.6 collective-permute-start.19
  80.7 0.6 collective-permute-start.18
  81.3 11.7 %plane.5 = (bf16[112,2048]{1,0:T(8,128)(2,1)S(1)}, bf16[112,2048]{1,0:T(8,128)(2,1)S(1)}, bf16[112,2048]{1,0:T(8,128)(2,1)S(1)}, bf16[48,2048]{1,0:T(8,128)(2,1)S(1)}, bf16[64,2048]{1,0:T(8,128)(2,1)S(1)}) custom-call(s32[3]{0:T(128)S(1)} %pad_add_fusion.refs_0_, bf16[16,2176]{1,0:T(8,128)(2,1)S(1)} %slice.50.refs_1_, ...), custom_call_target="tpu_custom_call" | custom-call | flops 8455716864 | bytes 25165824 | tf_op jit(solution)/shard_map/plane/pallas_call | solution.py:280
  93.1 1.3 collective-permute-start.25
  94.4 1.5 collective-permute-start.23
  95.9 1.6 collective-permute-start.24
  97.5 0.6 collective-permute-start.27
  98.1 0.7 collective-permute-start.26
  98.8 12.0 %plane.6 = (bf16[112,2048]{1,0:T(8,128)(2,1)S(1)}, bf16[112,2048]{1,0:T(8,128)(2,1)S(1)}, bf16[112,2048]{1,0:T(8,128)(2,1)S(1)}, bf16[64,2048]{1,0:T(8,128)(2,1)S(1)}, bf16[48,2048]{1,0:T(8,128)(2,1)S(1)}) custom-call(s32[3]{0:T(128)S(1)} %pad_add_fusion.refs_0_, bf16[16,2176]{1,0:T(8,128)(2,1)S(1)} %collective-permute-done.22.refs_1_, ...), custom_call_target="tpu_custom_call" | custom-call | flops 8455716864 | bytes 25165824 | tf_op jit(solution)/shard_map/plane/pallas_call | solution.py:280
  110.9 1.7 collective-permute-done.27.passed_1_ref
  112.6 1.5 collective-permute-start.31
  114.2 0.6 collective-permute-start.28
  114.8 2.0 %collective-permute-start.29 = (bf16[112,2048]{1,0:T(8,128)(2,1)S(1)}, bf16[112,2048]{1,0:T(8,128)(2,1)S(1)}, u32[]{:S(2)}, u32[]{:S(2)}) collective-permute-start(bf16[112,2048]{1,0:T(8,128)(2,1)S(1)} %get-tuple-element.171), channel_id=1, source_target_pairs={{0,16},{8,24},{16,0},{24,8},{1,17},{9,25},{17,1},{25,9},{2,18},{10... | collective-permute-start | bytes 1376264 | tf_op jit(solution)/shard_map/ppermute | solution.py:332
  116.8 12.3 %plane.7 = (bf16[112,2048]{1,0:T(8,128)(2,1)S(1)}, bf16[112,2048]{1,0:T(8,128)(2,1)S(1)}, bf16[112,2048]{1,0:T(8,128)(2,1)S(1)}, bf16[48,2048]{1,0:T(8,128)(2,1)S(1)}, bf16[64,2048]{1,0:T(8,128)(2,1)S(1)}) custom-call(s32[3]{0:T(128)S(1)} %pad_add_fusion.refs_0_, bf16[16,2176]{1,0:T(8,128)(2,1)S(1)} %collective-permute-done.25.refs_1_, ...), custom_call_target="tpu_custom_call" | custom-call | flops 8455716864 | bytes 25165824 | tf_op jit(solution)/shard_map/plane/pallas_call | solution.py:280
  129.4 0.7 collective-permute-start.40
  130.2 1.6 collective-permute-start.38
  131.8 0.5 collective-permute-start.33
  132.4 2.0 %collective-permute-start.32 = (bf16[48,2048]{1,0:T(8,128)(2,1)S(1)}, bf16[48,2048]{1,0:T(8,128)(2,1)S(1)}, u32[]{:S(2)}, u32[]{:S(2)}) collective-permute-start(bf16[48,2048]{1,0:T(8,128)(2,1)S(1)} %get-tuple-element.188), channel_id=1, source_target_pairs={{0,16},{8,24},{16,0},{24,8},{1,17},{9,25},{17,1},{25,9},{2,18},{10... | collective-permute-start | bytes 589832 | tf_op jit(solution)/shard_map/ppermute | solution.py:332
  134.3 12.5 %collective-permute-done.32.passed_0_ref = bf16[48,2048]{1,0:T(8,128)(2,1)S(1)} collective-permute-done((bf16[48,2048]{1,0:T(8,128)(2,1)S(1)}, bf16[48,2048]{1,0:T(8,128)(2,1)S(1)}, u32[]{:S(2)}, u32[]{:S(2)}) %collective-permute-start.32) | collective-permute-done | bytes 196640 | tf_op jit(solution)/shard_map/ppermute | solution.py:332
  147.0 1.2 collective-permute-start.34
  148.5 1.6 collective-permute-start.41
  150.1 9.6 %collective-permute-done.34 = bf16[112,2048]{1,0:T(8,128)(2,1)S(1)} collective-permute-done((bf16[112,2048]{1,0:T(8,128)(2,1)S(1)}, bf16[112,2048]{1,0:T(8,128)(2,1)S(1)}, u32[]{:S(2)}, u32[]{:S(2)}) %collective-permute-start.34) | collective-permute-done | bytes 458784 | tf_op jit(solution)/shard_map/ppermute | solution.py:328
  159.7 0.6 collective-permute-done.35
  160.4 1.3 collective-permute-start.36
  161.9 0.9 collective-permute-done.41
  163.1 0.6 collective-permute-start.42
  163.8 5.1 %collective-permute-done.36 = bf16[112,2048]{1,0:T(8,128)(2,1)S(1)} collective-permute-done((bf16[112,2048]{1,0:T(8,128)(2,1)S(1)}, bf16[112,2048]{1,0:T(8,128)(2,1)S(1)}, u32[]{:S(2)}, u32[]{:S(2)}) %collective-permute-start.36) | collective-permute-done | bytes 458784 | tf_op jit(solution)/shard_map/ppermute | solution.py:328
  168.9 1.2 collective-permute-done.37
  170.1 3.4 %collective-permute-done.42 = bf16[112,2048]{1,0:T(8,128)(2,1)S(1)} collective-permute-done((bf16[112,2048]{1,0:T(8,128)(2,1)S(1)}, bf16[112,2048]{1,0:T(8,128)(2,1)S(1)}, u32[]{:S(2)}, u32[]{:S(2)}) %collective-permute-start.42) | collective-permute-done | bytes 458784 | tf_op jit(solution)/shard_map/ppermute | solution.py:336
  173.5 1.2 fusion.13
  (92 shorter events, 5.2 us)
Async XLA Ops:
  0.0 10.8 %copy-start.9 = (f32[8]{0:T(128)S(1)}, f32[8]{0:T(128)}, u32[]{:S(2)}) copy-start(f32[8]{0:T(128)} %param.18) | copy-start | bytes 100
  0.0 12.7 %collective-permute-start = (bf16[2048,768]{1,0:T(8,128)(2,1)}, bf16[2048,768]{1,0:T(8,128)(2,1)}, u32[]{:S(2)}, u32[]{:S(2)}) collective-permute-start(bf16[2048,768]{1,0:T(8,128)(2,1)} %bitcast.55), channel_id=1, source_target_pairs={{0,1},{1,0},{2,3},{3,2},{4,5},{5,4},{6,7},{7,6},{8,9},{9,8},{10,11... | collective-permute-start | bytes 9437192 | tf_op jit(solution)/shard_map/ppermute | solution.py:340
  0.5 35.1 %collective-permute-start.6 = (bf16[2048,768]{1,0:T(8,128)(2,1)}, bf16[2048,768]{1,0:T(8,128)(2,1)}, u32[]{:S(2)}, u32[]{:S(2)}) collective-permute-start(bf16[2048,768]{1,0:T(8,128)(2,1)} %bitcast.60), channel_id=1, source_target_pairs={{0,1},{1,0},{2,3},{3,2},{4,5},{5,4},{6,7},{7,6},{8,9},{9,8},{10,11... | collective-permute-start | bytes 9437192 | tf_op jit(solution)/shard_map/ppermute | solution.py:340
  2.9 1.0 copy-start
  3.9 0.9 copy-start.2
  4.8 0.7 copy-start.4
  5.5 0.7 copy-start.6
  6.2 5.0 %copy-start.7 = (bf16[4,4096,1,128]{3,1,2,0:T(8,128)(2,1)S(1)}, bf16[4,4096,1,128]{3,1,2,0:T(8,128)(2,1)}, u32[]{:S(2)}) copy-start(bf16[4,4096,1,128]{3,1,2,0:T(8,128)(2,1)} %param.16) | copy-start | bytes 12582916
  7.0 4.9 %copy-start.8 = (bf16[1024,2048]{1,0:T(8,128)(2,1)S(1)}, bf16[1024,2048]{1,0:T(8,128)(2,1)}, u32[]{:S(2)}) copy-start(bf16[1024,2048]{1,0:T(8,128)(2,1)} %param.19) | copy-start | bytes 12582916
  11.9 30.4 %copy-start.3 = (bf16[2048,32]{0,1:T(8,128)(2,1)S(1)}, bf16[2048,32]{0,1:T(8,128)(2,1)}, u32[]{:S(2)}) copy-start(bf16[2048,32]{0,1:T(8,128)(2,1)} %param.23) | copy-start | bytes 393220
  11.9 30.4 %copy-start.5 = (f32[2048]{0:T(1024)S(1)}, f32[2048]{0:T(1024)}, u32[]{:S(2)}) copy-start(f32[2048]{0:T(1024)} %param.22) | copy-start | bytes 24580
  12.7 22.9 %collective-permute-start.3 = (bf16[112,2176]{1,0:T(8,128)(2,1)S(1)}, bf16[112,2176]{1,0:T(8,128)(2,1)}, u32[]{:S(2)}, u32[]{:S(2)}) collective-permute-start(bf16[112,2176]{1,0:T(8,128)(2,1)S(1)} %prepare.2.refs_2_), channel_id=1, source_target_pairs={{0,2},{1,3},{2,4},{3,5},{4,6},{5,7},{6,0},{7,1},{8,10},{9,11},{10,... | collective-permute-start | bytes 1462280 | tf_op jit(solution)/shard_map/ppermute | solution.py:336
  15.7 19.8 %collective-permute-start.2 = (bf16[112,2176]{1,0:T(8,128)(2,1)S(1)}, bf16[112,2176]{1,0:T(8,128)(2,1)S(1)}, u32[]{:S(2)}, u32[]{:S(2)}) collective-permute-start(bf16[112,2176]{1,0:T(8,128)(2,1)S(1)} %prepare.2.refs_2_), channel_id=1, source_target_pairs={{0,16},{8,24},{16,0},{24,8},{1,17},{9,25},{17,1},{25,9},{2,18},{10... | collective-permute-start | bytes 1462280 | tf_op jit(solution)/shard_map/ppermute | solution.py:332
  17.3 18.3 %collective-permute-start.1 = (bf16[112,2176]{1,0:T(8,128)(2,1)S(1)}, bf16[112,2176]{1,0:T(8,128)(2,1)S(1)}, u32[]{:S(2)}, u32[]{:S(2)}) collective-permute-start(bf16[112,2176]{1,0:T(8,128)(2,1)S(1)} %prepare.2.refs_2_), channel_id=1, source_target_pairs={{0,8},{8,0},{16,24},{24,16},{1,9},{9,1},{17,25},{25,17},{2,10},{10... | collective-permute-start | bytes 1462280 | tf_op jit(solution)/shard_map/ppermute | solution.py:328
  18.8 12.5 %collective-permute-start.4 = (f32[8,2048]{1,0:T(8,128)S(1)}, f32[8,2048]{1,0:T(8,128)S(1)}, u32[]{:S(2)}, u32[]{:S(2)}) collective-permute-start(f32[8,2048]{1,0:T(8,128)S(1)} %pad_maximum_fusion.3), channel_id=1, source_target_pairs={{0,8},{8,0},{16,24},{24,16},{1,9},{9,1},{17,25},{25,17},{2,10},{10... | collective-permute-start | bytes 196616 | tf_op jit(solution)/shard_map/ppermute | solution.py:328
  31.2 4.3 %collective-permute-start.5 = (f32[8,2048]{1,0:T(8,128)S(1)}, f32[8,2048]{1,0:T(8,128)S(1)}, u32[]{:S(2)}, u32[]{:S(2)}) collective-permute-start(f32[8,2048]{1,0:T(8,128)S(1)} %add.114), channel_id=1, source_target_pairs={{0,16},{8,24},{16,0},{24,8},{1,17},{9,25},{17,1},{25,9},{2,18},{10... | collective-permute-start | bytes 196616 | tf_op jit(solution)/shard_map/ppermute | solution.py:332
  35.6 6.1 %collective-permute-start.7 = (bf16[768,2048]{1,0:T(8,128)(2,1)}, bf16[768,2048]{1,0:T(8,128)(2,1)}, u32[]{:S(2)}, u32[]{:S(2)}) collective-permute-start(bf16[768,2048]{1,0:T(8,128)(2,1)} %bitcast.11.refs_9_), channel_id=1, source_target_pairs={{0,1},{1,0},{2,3},{3,2},{4,5},{5,4},{6,7},{7,6},{8,9},{9,8},{10,11... | collective-permute-start | bytes 9437192 | tf_op jit(solution)/shard_map/ppermute | solution.py:340
  35.8 19.7 %collective-permute-start.12 = (bf16[112,2176]{1,0:T(8,128)(2,1)}, bf16[112,2176]{1,0:T(8,128)(2,1)S(1)}, u32[]{:S(2)}, u32[]{:S(2)}) collective-permute-start(bf16[112,2176]{1,0:T(8,128)(2,1)} %collective-permute-done.3.refs_2_), channel_id=1, source_target_pairs={{0,2},{1,3},{2,4},{3,5},{4,6},{5,7},{6,0},{7,1},{8,10},{9,11},{10,... | collective-permute-start | bytes 1462280 | tf_op jit(solution)/shard_map/ppermute | solution.py:336
  37.4 18.1 %collective-permute-start.11 = (bf16[112,2176]{1,0:T(8,128)(2,1)}, bf16[112,2176]{1,0:T(8,128)(2,1)S(1)}, u32[]{:S(2)}, u32[]{:S(2)}) collective-permute-start(bf16[112,2176]{1,0:T(8,128)(2,1)} %collective-permute-done.3.refs_2_), channel_id=1, source_target_pairs={{0,16},{8,24},{16,0},{24,8},{1,17},{9,25},{17,1},{25,9},{2,18},{10... | collective-permute-start | bytes 1462280 | tf_op jit(solution)/shard_map/ppermute | solution.py:332
  37.9 17.6 %collective-permute-start.10 = (bf16[112,2176]{1,0:T(8,128)(2,1)}, bf16[112,2176]{1,0:T(8,128)(2,1)S(1)}, u32[]{:S(2)}, u32[]{:S(2)}) collective-permute-start(bf16[112,2176]{1,0:T(8,128)(2,1)} %collective-permute-done.3.refs_2_), channel_id=1, source_target_pairs={{0,8},{8,0},{16,24},{24,16},{1,9},{9,1},{17,25},{25,17},{2,10},{10... | collective-permute-start | bytes 1462280 | tf_op jit(solution)/shard_map/ppermute | solution.py:328
  39.6 16.0 %collective-permute-start.9 = (bf16[48,2176]{1,0:T(8,128)(2,1)S(1)}, bf16[48,2176]{1,0:T(8,128)(2,1)S(1)}, u32[]{:S(2)}, u32[]{:S(2)}) collective-permute-start(bf16[48,2176]{1,0:T(8,128)(2,1)S(1)} %slice.43), channel_id=1, source_target_pairs={{0,8},{8,0},{16,24},{24,16},{1,9},{9,1},{17,25},{25,17},{2,10},{10... | collective-permute-start | bytes 626696 | tf_op jit(solution)/shard_map/ppermute | solution.py:328
  41.7 15.1 %collective-permute-start.8 = (bf16[64,2176]{1,0:T(8,128)(2,1)S(1)}, bf16[64,2176]{1,0:T(8,128)(2,1)S(1)}, u32[]{:S(2)}, u32[]{:S(2)}) collective-permute-start(bf16[64,2176]{1,0:T(8,128)(2,1)S(1)} %slice.42), channel_id=1, source_target_pairs={{0,16},{8,24},{16,0},{24,8},{1,17},{9,25},{17,1},{25,9},{2,18},{10... | collective-permute-start | bytes 835592 | tf_op jit(solution)/shard_map/ppermute | solution.py:332
  56.8 18.6 %collective-permute-start.16 = (bf16[112,2176]{1,0:T(8,128)(2,1)S(1)}, bf16[112,2176]{1,0:T(8,128)(2,1)S(1)}, u32[]{:S(2)}, u32[]{:S(2)}) collective-permute-start(bf16[112,2176]{1,0:T(8,128)(2,1)S(1)} %collective-permute-done.12.refs_2_), channel_id=1, source_target_pairs={{0,16},{8,24},{16,0},{24,8},{1,17},{9,25},{17,1},{25,9},{2,18},{10... | collective-permute-start | bytes 1462280 | tf_op jit(solution)/shard_map/ppermute | solution.py:332
  57.3 18.1 %collective-permute-start.15 = (bf16[112,2176]{1,0:T(8,128)(2,1)S(1)}, bf16[112,2176]{1,0:T(8,128)(2,1)S(1)}, u32[]{:S(2)}, u32[]{:S(2)}) collective-permute-start(bf16[112,2176]{1,0:T(8,128)(2,1)S(1)} %collective-permute-done.12.refs_2_), channel_id=1, source_target_pairs={{0,8},{8,0},{16,24},{24,16},{1,9},{9,1},{17,25},{25,17},{2,10},{10... | collective-permute-start | bytes 1462280 | tf_op jit(solution)/shard_map/ppermute | solution.py:328
  58.8 15.9 %collective-permute-start.13 = (bf16[48,2176]{1,0:T(8,128)(2,1)S(1)}, bf16[48,2176]{1,0:T(8,128)(2,1)S(1)}, u32[]{:S(2)}, u32[]{:S(2)}) collective-permute-start(bf16[48,2176]{1,0:T(8,128)(2,1)S(1)} %slice.45), channel_id=1, source_target_pairs={{0,16},{8,24},{16,0},{24,8},{1,17},{9,25},{17,1},{25,9},{2,18},{10... | collective-permute-start | bytes 626696 | tf_op jit(solution)/shard_map/ppermute | solution.py:332
  60.4 15.0 %collective-permute-start.14 = (bf16[64,2176]{1,0:T(8,128)(2,1)S(1)}, bf16[64,2176]{1,0:T(8,128)(2,1)S(1)}, u32[]{:S(2)}, u32[]{:S(2)}) collective-permute-start(bf16[64,2176]{1,0:T(8,128)(2,1)S(1)} %slice.46), channel_id=1, source_target_pairs={{0,8},{8,0},{16,24},{24,16},{1,9},{9,1},{17,25},{25,17},{2,10},{10... | collective-permute-start | bytes 835592 | tf_op jit(solution)/shard_map/ppermute | solution.py:328
  61.1 14.6 %collective-permute-start.17 = (bf16[128,2176]{1,0:T(8,128)(2,1)S(1)}, bf16[128,2176]{1,0:T(8,128)(2,1)S(1)}, u32[]{:S(2)}, u32[]{:S(2)}) collective-permute-start(bf16[128,2176]{1,0:T(8,128)(2,1)S(1)} %pad_maximum_fusion), channel_id=1, source_target_pairs={{0,2},{1,3},{2,4},{3,5},{4,6},{5,7},{6,0},{7,1},{8,10},{9,11},{10,... | collective-permute-start | bytes 1671176 | tf_op jit(solution)/shard_map/ppermute | solution.py:336
  75.7 17.4 %collective-permute-start.21 = (bf16[112,2176]{1,0:T(8,128)(2,1)S(1)}, bf16[112,2176]{1,0:T(8,128)(2,1)S(1)}, u32[]{:S(2)}, u32[]{:S(2)}) collective-permute-start(bf16[112,2176]{1,0:T(8,128)(2,1)S(1)} %slice.49.refs_2_), channel_id=1, source_target_pairs={{0,16},{8,24},{16,0},{24,8},{1,17},{9,25},{17,1},{25,9},{2,18},{10... | collective-permute-start | bytes 1462280 | tf_op jit(solution)/shard_map/ppermute | solution.py:332
  77.0 16.1 %collective-permute-start.20 = (bf16[112,2176]{1,0:T(8,128)(2,1)S(1)}, bf16[112,2176]{1,0:T(8,128)(2,1)S(1)}, u32[]{:S(2)}, u32[]{:S(2)}) collective-permute-start(bf16[112,2176]{1,0:T(8,128)(2,1)S(1)} %slice.49.refs_2_), channel_id=1, source_target_pairs={{0,8},{8,0},{16,24},{24,16},{1,9},{9,1},{17,25},{25,17},{2,10},{10... | collective-permute-start | bytes 1462280 | tf_op jit(solution)/shard_map/ppermute | solution.py:328
  78.5 14.6 %collective-permute-start.22 = (bf16[16,2176]{1,0:T(8,128)(2,1)S(1)}, bf16[16,2176]{1,0:T(8,128)(2,1)S(1)}, u32[]{:S(2)}, u32[]{:S(2)}) collective-permute-start(bf16[16,2176]{1,0:T(8,128)(2,1)S(1)} %slice.50.refs_1_), channel_id=1, source_target_pairs={{0,2},{1,3},{2,4},{3,5},{4,6},{5,7},{6,0},{7,1},{8,10},{9,11},{10,... | collective-permute-start | bytes 208904 | tf_op jit(solution)/shard_map/ppermute | solution.py:336
  80.1 13.0 %collective-permute-start.19 = (bf16[48,2176]{1,0:T(8,128)(2,1)S(1)}, bf16[48,2176]{1,0:T(8,128)(2,1)S(1)}, u32[]{:S(2)}, u32[]{:S(2)}) collective-permute-start(bf16[48,2176]{1,0:T(8,128)(2,1)S(1)} %slice.48), channel_id=1, source_target_pairs={{0,8},{8,0},{16,24},{24,16},{1,9},{9,1},{17,25},{25,17},{2,10},{10... | collective-permute-start | bytes 626696 | tf_op jit(solution)/shard_map/ppermute | solution.py:328
  80.7 12.4 %collective-permute-start.18 = (bf16[64,2176]{1,0:T(8,128)(2,1)S(1)}, bf16[64,2176]{1,0:T(8,128)(2,1)S(1)}, u32[]{:S(2)}, u32[]{:S(2)}) collective-permute-start(bf16[64,2176]{1,0:T(8,128)(2,1)S(1)} %slice.47), channel_id=1, source_target_pairs={{0,16},{8,24},{16,0},{24,8},{1,17},{9,25},{17,1},{25,9},{2,18},{10... | collective-permute-start | bytes 835592 | tf_op jit(solution)/shard_map/ppermute | solution.py:332
  93.1 17.7 %collective-permute-start.25 = (bf16[16,2176]{1,0:T(8,128)(2,1)S(1)}, bf16[16,2176]{1,0:T(8,128)(2,1)S(1)}, u32[]{:S(2)}, u32[]{:S(2)}) collective-permute-start(bf16[16,2176]{1,0:T(8,128)(2,1)S(1)} %collective-permute-done.22.refs_1_), channel_id=1, source_target_pairs={{0,2},{1,3},{2,4},{3,5},{4,6},{5,7},{6,0},{7,1},{8,10},{9,11},{10,... | collective-permute-start | bytes 208904 | tf_op jit(solution)/shard_map/ppermute | solution.py:336
  94.4 16.5 %collective-permute-start.23 = (bf16[48,2176]{1,0:T(8,128)(2,1)S(1)}, bf16[48,2176]{1,0:T(8,128)(2,1)S(1)}, u32[]{:S(2)}, u32[]{:S(2)}) collective-permute-start(bf16[48,2176]{1,0:T(8,128)(2,1)S(1)} %slice.51), channel_id=1, source_target_pairs={{0,16},{8,24},{16,0},{24,8},{1,17},{9,25},{17,1},{25,9},{2,18},{10... | collective-permute-start | bytes 626696 | tf_op jit(solution)/shard_map/ppermute | solution.py:332
  95.9 15.0 %collective-permute-start.24 = (bf16[64,2176]{1,0:T(8,128)(2,1)S(1)}, bf16[64,2176]{1,0:T(8,128)(2,1)S(1)}, u32[]{:S(2)}, u32[]{:S(2)}) collective-permute-start(bf16[64,2176]{1,0:T(8,128)(2,1)S(1)} %slice.52), channel_id=1, source_target_pairs={{0,8},{8,0},{16,24},{24,16},{1,9},{9,1},{17,25},{25,17},{2,10},{10... | collective-permute-start | bytes 835592 | tf_op jit(solution)/shard_map/ppermute | solution.py:328
  97.5 15.1 %collective-permute-start.27 = (bf16[112,2048]{1,0:T(8,128)(2,1)S(1)}, bf16[112,2048]{1,0:T(8,128)(2,1)S(1)}, u32[]{:S(2)}, u32[]{:S(2)}) collective-permute-start(bf16[112,2048]{1,0:T(8,128)(2,1)S(1)} %pad_maximum_fusion.2), channel_id=1, source_target_pairs={{0,8},{8,0},{16,24},{24,16},{1,9},{9,1},{17,25},{25,17},{2,10},{10... | collective-permute-start | bytes 1376264 | tf_op jit(solution)/shard_map/ppermute | solution.py:328
  98.1 14.5 %collective-permute-start.26 = (bf16[112,2048]{1,0:T(8,128)(2,1)S(1)}, bf16[112,2048]{1,0:T(8,128)(2,1)S(1)}, u32[]{:S(2)}, u32[]{:S(2)}) collective-permute-start(bf16[112,2048]{1,0:T(8,128)(2,1)S(1)} %pad_maximum_fusion.1), channel_id=1, source_target_pairs={{0,16},{8,24},{16,0},{24,8},{1,17},{9,25},{17,1},{25,9},{2,18},{10... | collective-permute-start | bytes 1376264 | tf_op jit(solution)/shard_map/ppermute | solution.py:332
  112.6 16.6 %collective-permute-start.31 = (bf16[48,2048]{1,0:T(8,128)(2,1)S(1)}, bf16[48,2048]{1,0:T(8,128)(2,1)S(1)}, u32[]{:S(2)}, u32[]{:S(2)}) collective-permute-start(bf16[48,2048]{1,0:T(8,128)(2,1)S(1)} %get-tuple-element.173), channel_id=1, source_target_pairs={{0,8},{8,0},{16,24},{24,16},{1,9},{9,1},{17,25},{25,17},{2,10},{10... | collective-permute-start | bytes 589832 | tf_op jit(solution)/shard_map/ppermute | solution.py:328
  114.1 15.1 %collective-permute-start.30 = (bf16[64,2048]{1,0:T(8,128)(2,1)S(1)}, bf16[64,2048]{1,0:T(8,128)(2,1)S(1)}, u32[]{:S(2)}, u32[]{:S(2)}) collective-permute-start(bf16[64,2048]{1,0:T(8,128)(2,1)S(1)} %get-tuple-element.172), channel_id=1, source_target_pairs={{0,16},{8,24},{16,0},{24,8},{1,17},{9,25},{17,1},{25,9},{2,18},{10... | collective-permute-start | bytes 786440 | tf_op jit(solution)/shard_map/ppermute | solution.py:332
  114.2 14.9 %collective-permute-start.28 = (bf16[112,2048]{1,0:T(8,128)(2,1)S(1)}, bf16[112,2048]{1,0:T(8,128)(2,1)S(1)}, u32[]{:S(2)}, u32[]{:S(2)}) collective-permute-start(bf16[112,2048]{1,0:T(8,128)(2,1)S(1)} %get-tuple-element.170), channel_id=1, source_target_pairs={{0,8},{8,0},{16,24},{24,16},{1,9},{9,1},{17,25},{25,17},{2,10},{10... | collective-permute-start | bytes 1376264 | tf_op jit(solution)/shard_map/ppermute | solution.py:328
  114.8 14.4 %collective-permute-start.29 = (bf16[112,2048]{1,0:T(8,128)(2,1)S(1)}, bf16[112,2048]{1,0:T(8,128)(2,1)S(1)}, u32[]{:S(2)}, u32[]{:S(2)}) collective-permute-start(bf16[112,2048]{1,0:T(8,128)(2,1)S(1)} %get-tuple-element.171), channel_id=1, source_target_pairs={{0,16},{8,24},{16,0},{24,8},{1,17},{9,25},{17,1},{25,9},{2,18},{10... | collective-permute-start | bytes 1376264 | tf_op jit(solution)/shard_map/ppermute | solution.py:332
  129.4 18.8 %collective-permute-start.40 = (bf16[112,2048]{1,0:T(8,128)(2,1)S(1)}, bf16[112,2048]{1,0:T(8,128)(2,1)S(1)}, u32[]{:S(2)}, u32[]{:S(2)}) collective-permute-start(bf16[112,2048]{1,0:T(8,128)(2,1)S(1)} %add_convert_fusion.3), channel_id=1, source_target_pairs={{0,2},{1,3},{2,4},{3,5},{4,6},{5,7},{6,0},{7,1},{8,10},{9,11},{10,... | collective-permute-start | bytes 1376264 | tf_op jit(solution)/shard_map/ppermute | solution.py:336
  130.2 43.3 %copy-start.1 = (bf16[1,111,2048]{2,1,0:T(8,128)(2,1)S(1)}, bf16[1,111,2048]{2,1,0:T(8,128)(2,1)}, u32[]{:S(2)}) copy-start(bf16[1,111,2048]{2,1,0:T(8,128)(2,1)} %param.21) | copy-start | bytes 1363972
  130.2 18.0 %collective-permute-start.38 = (bf16[112,2048]{1,0:T(8,128)(2,1)S(1)}, bf16[112,2048]{1,0:T(8,128)(2,1)S(1)}, u32[]{:S(2)}, u32[]{:S(2)}) collective-permute-start(bf16[112,2048]{1,0:T(8,128)(2,1)S(1)} %get-tuple-element.210), channel_id=1, source_target_pairs={{0,8},{8,0},{16,24},{24,16},{1,9},{9,1},{17,25},{25,17},{2,10},{10... | collective-permute-start | bytes 1376264 | tf_op jit(solution)/shard_map/ppermute | solution.py:328
  131.8 16.4 %collective-permute-start.39 = (bf16[112,2048]{1,0:T(8,128)(2,1)S(1)}, bf16[112,2048]{1,0:T(8,128)(2,1)S(1)}, u32[]{:S(2)}, u32[]{:S(2)}) collective-permute-start(bf16[112,2048]{1,0:T(8,128)(2,1)S(1)} %get-tuple-element.211), channel_id=1, source_target_pairs={{0,16},{8,24},{16,0},{24,8},{1,17},{9,25},{17,1},{25,9},{2,18},{10... | collective-permute-start | bytes 1376264 | tf_op jit(solution)/shard_map/ppermute | solution.py:332
  131.8 15.0 %collective-permute-start.33 = (bf16[64,2048]{1,0:T(8,128)(2,1)S(1)}, bf16[64,2048]{1,0:T(8,128)(2,1)S(1)}, u32[]{:S(2)}, u32[]{:S(2)}) collective-permute-start(bf16[64,2048]{1,0:T(8,128)(2,1)S(1)} %get-tuple-element.189), channel_id=1, source_target_pairs={{0,8},{8,0},{16,24},{24,16},{1,9},{9,1},{17,25},{25,17},{2,10},{10... | collective-permute-start | bytes 786440 | tf_op jit(solution)/shard_map/ppermute | solution.py:328
  132.4 14.5 %collective-permute-start.32 = (bf16[48,2048]{1,0:T(8,128)(2,1)S(1)}, bf16[48,2048]{1,0:T(8,128)(2,1)S(1)}, u32[]{:S(2)}, u32[]{:S(2)}) collective-permute-start(bf16[48,2048]{1,0:T(8,128)(2,1)S(1)} %get-tuple-element.188), channel_id=1, source_target_pairs={{0,16},{8,24},{16,0},{24,8},{1,17},{9,25},{17,1},{25,9},{2,18},{10... | collective-permute-start | bytes 589832 | tf_op jit(solution)/shard_map/ppermute | solution.py:332
  147.0 12.7 %collective-permute-start.34 = (bf16[112,2048]{1,0:T(8,128)(2,1)S(1)}, bf16[112,2048]{1,0:T(8,128)(2,1)S(1)}, u32[]{:S(2)}, u32[]{:S(2)}) collective-permute-start(bf16[112,2048]{1,0:T(8,128)(2,1)S(1)} %get-tuple-element.190), channel_id=1, source_target_pairs={{0,8},{8,0},{16,24},{24,16},{1,9},{9,1},{17,25},{25,17},{2,10},{10... | collective-permute-start | bytes 1376264 | tf_op jit(solution)/shard_map/ppermute | solution.py:328
  148.1 12.1 %collective-permute-start.35 = (bf16[112,2048]{1,0:T(8,128)(2,1)S(1)}, bf16[112,2048]{1,0:T(8,128)(2,1)S(1)}, u32[]{:S(2)}, u32[]{:S(2)}) collective-permute-start(bf16[112,2048]{1,0:T(8,128)(2,1)S(1)} %get-tuple-element.191), channel_id=1, source_target_pairs={{0,16},{8,24},{16,0},{24,8},{1,17},{9,25},{17,1},{25,9},{2,18},{10... | collective-permute-start | bytes 1376264 | tf_op jit(solution)/shard_map/ppermute | solution.py:332
  148.5 14.4 %collective-permute-start.41 = (bf16[112,2048]{1,0:T(8,128)(2,1)S(1)}, bf16[112,2048]{1,0:T(8,128)(2,1)S(1)}, u32[]{:S(2)}, u32[]{:S(2)}) collective-permute-start(bf16[112,2048]{1,0:T(8,128)(2,1)S(1)} %add_convert_fusion.2), channel_id=1, source_target_pairs={{0,2},{1,3},{2,4},{3,5},{4,6},{5,7},{6,0},{7,1},{8,10},{9,11},{10,... | collective-permute-start | bytes 1376264 | tf_op jit(solution)/shard_map/ppermute | solution.py:336
  160.4 8.5 %collective-permute-start.36 = (bf16[112,2048]{1,0:T(8,128)(2,1)S(1)}, bf16[112,2048]{1,0:T(8,128)(2,1)S(1)}, u32[]{:S(2)}, u32[]{:S(2)}) collective-permute-start(bf16[112,2048]{1,0:T(8,128)(2,1)S(1)} %get-tuple-element.200), channel_id=1, source_target_pairs={{0,8},{8,0},{16,24},{24,16},{1,9},{9,1},{17,25},{25,17},{2,10},{10... | collective-permute-start | bytes 1376264 | tf_op jit(solution)/shard_map/ppermute | solution.py:328
  161.6 8.5 %collective-permute-start.37 = (bf16[112,2048]{1,0:T(8,128)(2,1)S(1)}, bf16[112,2048]{1,0:T(8,128)(2,1)S(1)}, u32[]{:S(2)}, u32[]{:S(2)}) collective-permute-start(bf16[112,2048]{1,0:T(8,128)(2,1)S(1)} %get-tuple-element.201), channel_id=1, source_target_pairs={{0,16},{8,24},{16,0},{24,8},{1,17},{9,25},{17,1},{25,9},{2,18},{10... | collective-permute-start | bytes 1376264 | tf_op jit(solution)/shard_map/ppermute | solution.py:332
  163.1 10.3 %collective-permute-start.42 = (bf16[112,2048]{1,0:T(8,128)(2,1)S(1)}, bf16[112,2048]{1,0:T(8,128)(2,1)S(1)}, u32[]{:S(2)}, u32[]{:S(2)}) collective-permute-start(bf16[112,2048]{1,0:T(8,128)(2,1)S(1)} %add_convert_fusion.1), channel_id=1, source_target_pairs={{0,2},{1,3},{2,4},{3,5},{4,6},{5,7},{6,0},{7,1},{8,10},{9,11},{10,... | collective-permute-start | bytes 1376264 | tf_op jit(solution)/shard_map/ppermute | solution.py:336

commit v8 on v5

--- a/solution.py
+++ b/solution.py
@@ -41,6 +41,21 @@
         .astype(jnp.bfloat16)
         .reshape(per_block, head_count * head_dim)
     )
+
+
+def fetched_prepare_kernel(ranking, hidden_in, gain_in, router_in, routes_in, out_ref, *scratch):
+    shifted, hidden_ref, gain_ref, router_ref, routes_ref, sems = scratch
+    sources = (hidden_in, gain_in, router_in, routes_in)
+    targets = (hidden_ref, gain_ref, router_ref, routes_ref)
+    copies = [
+        pltpu.make_async_copy(source, target, sems.at[i])
+        for i, (source, target) in enumerate(zip(sources, targets))
+    ]
+    for copy in copies:
+        copy.start()
+    for copy in copies:
+        copy.wait()
+    prepare_kernel(ranking, *targets, out_ref, shifted)
 
 
 def prepare_kernel(ranking, hidden_ref, gain_ref, router_ref, routes_ref, out_ref, *scratch):
@@ -91,14 +106,24 @@
     width = hidden.shape[1]
     rows = routes.shape[0]
     extra = -(-(3 if ranking else 2) * router.shape[1] // 128) * 128
-    shifted = rows > hidden.shape[0]
+    operands = (hidden, norm_gain.reshape(1, width), router.T, routes.T)
+    fetched = rows > hidden.shape[0]
+    kernel, options = prepare_kernel, {}
+    if fetched:
+        kernel = fetched_prepare_kernel
+        options = dict(
+            in_specs=[pl.BlockSpec(memory_space=pltpu.HBM)] * 4,
+            scratch_shapes=[pltpu.VMEM((rows, width), jnp.float32)]
+            + [pltpu.VMEM(operand.shape, operand.dtype) for operand in operands]
+            + [pltpu.SemaphoreType.DMA((4,))],
+        )
     return pl.pallas_call(
-        functools.partial(prepare_kernel, ranking),
+        functools.partial(kernel, ranking),
         out_shape=jax.ShapeDtypeStruct((rows, width + extra), jnp.bfloat16),
-        scratch_shapes=[pltpu.VMEM((rows, width), jnp.float32)] if shifted else [],
         compiler_params=pltpu.CompilerParams(vmem_limit_bytes=32 << 20),
         name="prepare",
-    )(hidden, norm_gain.reshape(1, width), router.T, routes.T)
+        **options,
+    )(*operands)
 
 
 def expert_kernel(expert_ref, rows_ref, gate_ref, up_ref, down_ref, out_ref):
@@ -144,7 +169,6 @@
 def plane_kernel(cap, piece_rows, block_rows, *refs):
     refs = list(refs)
     ids_ref = refs.pop(0)
-    decode_ref = refs.pop(0)
     sources = [refs.pop(0) for _ in piece_rows]
     weight_refs = [refs.pop(0) for _ in range(6)]
     targets = [refs.pop(0) for _ in block_rows]
@@ -153,11 +177,21 @@
     tokens = block_rows[0]
     pair_rows = 2 * tokens
     pair_slots = 2 * cap
-    row_copies = [pltpu.make_async_copy(decode_ref, decodes, row_sem.at[len(sources)])]
+    few = decodes.shape[0]
+    row_copies = []
     at = 0
-    for i, (ref, count) in enumerate(zip(sources, piece_rows)):
-        copy = pltpu.make_async_copy(ref, rows.at[pl.ds(at, count)], row_sem.at[i])
-        row_copies.append(copy)
+    for ref, count in zip(sources, piece_rows):
+        if ref is sources[-1]:
+            count -= few
+            copy = pltpu.make_async_copy(
+                ref.at[pl.ds(count, few)], decodes, row_sem.at[len(row_copies)]
+            )
+            row_copies.append(copy)
+        if count:
+            copy = pltpu.make_async_copy(
+                ref.at[pl.ds(0, count)], rows.at[pl.ds(at, count)], row_sem.at[len(row_copies)]
+            )
+            row_copies.append(copy)
         at += count
     up_copies = [
         pltpu.make_async_copy(weight_refs[3 * e + i], weights.at[2 * e + i], weight_sem.at[2 * e + i])
@@ -172,7 +206,6 @@
         copy.start()
     for copy in row_copies:
         copy.wait()
-    few = decodes.shape[0]
     is_first = lax.broadcasted_iota(jnp.int32, (few, 1), 0) == 0
     for j in range(4):
         part = pl.ds(j * tokens, few)
@@ -270,20 +303,20 @@
         copy.wait()
 
 
-def run_plane(ids, cap, decodes, pieces, block_rows, weights):
+def run_plane(ids, cap, few, pieces, block_rows, weights):
     width, units = weights[0].shape
     padded = pieces[0].shape[1]
     piece_rows = tuple(piece.shape[0] for piece in pieces)
-    total = sum(piece_rows)
+    total = sum(piece_rows) - few
     kept = jnp.bfloat16
     anywhere = pl.BlockSpec(memory_space=pl.ANY)
     return pl.pallas_call(
         functools.partial(plane_kernel, cap, piece_rows, block_rows),
-        in_specs=[pl.BlockSpec(memory_space=pltpu.SMEM)] + [anywhere] * (len(pieces) + 7),
+        in_specs=[pl.BlockSpec(memory_space=pltpu.SMEM)] + [anywhere] * (len(pieces) + 6),
         out_specs=[anywhere] * len(block_rows),
         out_shape=[jax.ShapeDtypeStruct((count, width), kept) for count in block_rows],
         scratch_shapes=[
-            pltpu.VMEM(decodes.shape, kept),
+            pltpu.VMEM((few, padded), kept),
             pltpu.VMEM((total, padded), kept),
             pltpu.VMEM((4, width, units), kept),
             pltpu.VMEM((2, units, width), kept),
@@ -301,7 +334,7 @@
             flops=12 * total * width * units, bytes_accessed=24 << 20, transcendentals=total * units
         ),
         name="plane",
-    )(ids, decodes, *pieces, *weights)
+    )(ids, *pieces, *weights)
 
 
 def merge_kernel(cut, x_ref, y_ref, passed_0_ref, passed_1_ref, x_out, y_out):
@@ -329,10 +362,6 @@
 
 def along_y(value):
     return lax.ppermute(value, "kv", [(i, i ^ 2) for i in range(4)])
-
-
-def along_diagonal(value):
-    return lax.ppermute(value, "kv", [(i, i ^ 3) for i in range(4)])
 
 
 def around_z(value):
@@ -380,46 +409,34 @@
         [first_expert + my_blk, first_expert + (my_blk ^ 1), jnp.int32(experts)]
     ).astype(jnp.int32)
     cap = (2 * tokens * ids.shape[1] + experts - 1) // experts
-    long = (tokens // 2 + 15) // 16 * 16
-    cuts = [long, tokens - long, long, tokens - long]
-    blocks = [None] * 4
-    sides = [None] * 4
-    corners = [None] * 4
-    decodes = [None] * 4
-    sums = [None] * 4
-    passed = [None] * 4
-    back = [None] * 4
-
-    def spread_sides(step):
-        sides[step] = along_x(blocks[step]), along_y(blocks[step])
-
-    def spread_corners(step):
-        cut = cuts[step]
-        corners[step] = along_y(sides[step][0][:cut]), along_x(sides[step][1][cut:])
-
-    def apply(step):
-        counts = (tokens, tokens, tokens, cuts[step], tokens - cuts[step])
-        pieces = (blocks[step],) + sides[step] + corners[step]
-        sums[step] = run_plane(expert_ids, cap, decodes[step], pieces, counts, weights)
-
-    def return_corners(step):
-        passed[step] = along_y(sums[step][3]), along_x(sums[step][4])
-
-    def return_sides(step):
-        to_x, to_y = merge_passed(cuts[step], sums[step][1], sums[step][2], *passed[step])
-        back[step] = along_x(to_x), along_y(to_y)
+    cut = (tokens // 2 + 15) // 16 * 16
+    few = 16
+
+    def spread_sides(block):
+        return along_x(block), along_y(block)
+
+    def spread_corner(sides):
+        return along_y(sides[0][:cut]), along_x(sides[1][cut:])
+
+    def apply(pieces, counts):
+        return run_plane(expert_ids, cap, few, pieces, counts, weights)
+
+    def return_corner(sums):
+        return along_y(sums[3]), along_x(sums[4])
+
+    def return_sides(sums, passed=None):
+        to_x, to_y = sums[1:3] if passed is None else merge_passed(cut, *sums[1:3], *passed)
+        return along_x(to_x), along_y(to_y)
 
     prefill = prefill_hidden[0]
-    blocks[0] = prepare(prefill, norm_gain, router, ids, "block")
-    blocks[0], queries, cache_keys, expert_gate, expert_up = fence(
-        blocks[0], queries, cache_keys, expert_gate, expert_up
-    )
-    spread_sides(0)
-    corners[0] = (along_diagonal(blocks[0]),)
-    blocks[1] = around_z(blocks[0])
+    block_0 = prepare(prefill, norm_gain, router, ids, "block")
+    block_0, queries, cache_keys, expert_gate, expert_up = fence(
+        block_0, queries, cache_keys, expert_gate, expert_up
+    )
+    sides_0 = spread_sides(block_0)
+    block_1 = around_z(block_0)
     other_gate = across_chip(expert_gate[0])
     other_up = across_chip(expert_up[0])
-
     attended = attend(queries, cache_keys, cache_values, lengths, sinks)
     partial_proj = jnp.dot(attended, out_proj, preferred_element_type=jnp.float32)
     is_mine = jnp.arange(4)[:, None] == my_kv
@@ -427,17 +444,16 @@
     width = partial_proj.shape[1]
     ids_row = jnp.pad(ids[:1].astype(jnp.float32), ((0, 0), (0, width - ids.shape[1])))
     shared = jnp.concatenate([partial_proj, jnp.where(is_mine, ids_row, 0.0)], axis=0)
-
-    shared, other_gate = fence(shared, other_gate)
+    sides_0, other_gate, shared = fence(sides_0, other_gate, shared)
+
     shared = shared + along_x(shared)
-    sides[0], corners[0], blocks[1], shared, expert_down = fence(
-        sides[0], corners[0], blocks[1], shared, expert_down
-    )
-
-    spread_sides(1)
-    blocks[2] = around_z(blocks[1])
+    corner_0 = spread_corner(sides_0)
+    corner_0, block_1, shared, expert_down = fence(corner_0, block_1, shared, expert_down)
+
+    shared = shared + along_y(shared)
+    sides_1 = spread_sides(block_1)
+    block_2 = around_z(block_1)
     other_down = across_chip(expert_down[0])
-    shared = shared + along_y(shared)
     order = [my_kv ^ j for j in range(4)]
     decoded = jnp.concatenate(
         [lax.dynamic_slice_in_dim(shared, index, 1) for index in order], axis=0
@@ -446,61 +462,54 @@
         [lax.dynamic_slice_in_dim(shared, 4 + index, 1) for index in order], axis=0
     )[:, : ids.shape[1]].astype(jnp.int32)
     hidden = jnp.concatenate([decoded[:1], prefill], axis=0)
-    decodes[0] = prepare(
-        jnp.pad(decoded, ((0, 12), (0, 0))),
+    decodes_0 = prepare(
+        jnp.pad(decoded, ((0, few - 4), (0, 0))),
         norm_gain,
         router,
-        jnp.pad(decode_ids, ((0, 12), (0, 0))),
+        jnp.pad(decode_ids, ((0, few - 4), (0, 0))),
         "first",
     )
-    sides[1], blocks[2], decodes[0], other_up = fence(sides[1], blocks[2], decodes[0], other_up)
+    sides_1, block_2, decodes_0, other_up, other_down = fence(
+        sides_1, block_2, decodes_0, other_up, other_down
+    )
     weights = (expert_gate[0], expert_up[0], expert_down[0], other_gate, other_up, other_down)
-
-    spread_corners(1)
-    spread_sides(2)
-    arrived = around_z(jnp.concatenate([blocks[2], decodes[0]], axis=0))
-    apply(0)
-    corners[1], sides[2], arrived, sums[0] = fence(corners[1], sides[2], arrived, sums[0])
-    blocks[3], decodes[1] = arrived[:tokens], arrived[tokens:]
-
-    spread_corners(2)
-    spread_sides(3)
-    decodes[2] = around_z(decodes[1])
-    apply(1)
-    corners[2], sides[3], decodes[2], sums[1] = fence(corners[2], sides[3], decodes[2], sums[1])
-
-    spread_corners(3)
-    decodes[3] = around_z(decodes[2])
-    return_corners(1)
-    apply(2)
-    corners[3], decodes[3], passed[1], sums[1], sums[2] = fence(
-        corners[3], decodes[3], passed[1], sums[1], sums[2]
-    )
-
-    return_sides(1)
-    return_corners(2)
-    apply(3)
-    back[1], passed[2], sums[1], sums[2], sums[3] = fence(
-        back[1], passed[2], sums[1], sums[2], sums[3]
-    )
-
-    return_sides(2)
-    return_corners(3)
-    carried = around_z(added(sums[1][0], *back[1]).astype(jnp.bfloat16))
-    back[2], passed[3], carried, sums[2], sums[3], sums[0] = fence(
-        back[2], passed[3], carried, sums[2], sums[3], sums[0]
-    )
-
-    return_sides(3)
-    return_corners(0)
-    carried = around_z(added(sums[2][0], *back[2], carried).astype(jnp.bfloat16))
-    back[3], passed[0], carried, sums[3], sums[0] = fence(
-        back[3], passed[0], carried, sums[3], sums[0]
-    )
-
-    return_sides(0)
-    carried = around_z(added(sums[3][0], *back[3], carried).astype(jnp.bfloat16))
-    return added(hidden, sums[0][0], *back[0], carried).astype(jnp.bfloat16)[None]
+    halves = (tokens, tokens, tokens, cut, tokens - cut)
+
+    corner_1 = spread_corner(sides_1)
+    sides_2 = spread_sides(block_2)
+    arrived = around_z(jnp.concatenate([block_2, decodes_0], axis=0))
+    sums_0 = apply((block_0,) + sides_0 + corner_0 + (decodes_0,), halves)
+    corner_1, sides_2, arrived, sums_0 = fence(corner_1, sides_2, arrived, sums_0)
+    block_3, decodes_1 = arrived[:tokens], arrived[tokens:]
+
+    sides_3 = spread_sides(block_3)
+    risen_2 = around_z(jnp.concatenate(corner_1 + (decodes_1,), axis=0))
+    passed_0 = return_corner(sums_0)
+    sums_1 = apply((block_1,) + sides_1 + corner_1 + (decodes_1,), halves)
+    sides_3, risen_2, passed_0, sums_0, sums_1 = fence(sides_3, risen_2, passed_0, sums_0, sums_1)
+
+    risen_3 = around_z(risen_2)
+    passed_1 = return_corner(sums_1)
+    back_0 = return_sides(sums_0, passed_0)
+    sums_2 = apply((block_2,) + sides_2 + (risen_2,), (tokens,) * 4)
+    risen_3, passed_1, back_0, sums_0, sums_1, sums_2 = fence(
+        risen_3, passed_1, back_0, sums_0, sums_1, sums_2
+    )
+
+    back_1 = return_sides(sums_1, passed_1)
+    risen_sums = around_z(sums_2[3])
+    back_2 = return_sides(sums_2)
+    layer_sum = added(hidden, sums_0[0], *back_0)
+    sums_3 = apply((block_3,) + sides_3 + (risen_3,), (tokens,) * 4)
+    back_1, risen_sums, sums_1, sums_2, sums_3 = fence(back_1, risen_sums, sums_1, sums_2, sums_3)
+
+    far = added(sums_3[3], risen_sums).astype(jnp.bfloat16)
+    passed_3 = return_corner(tuple(sums_3[:3]) + (far[:cut], far[cut:]))
+    carried = around_z(added(sums_1[0], *back_1).astype(jnp.bfloat16))
+    back_3 = return_sides(sums_3, passed_3)
+    carried = around_z(added(sums_2[0], *back_2, carried).astype(jnp.bfloat16))
+    carried = around_z(added(sums_3[0], *back_3, carried).astype(jnp.bfloat16))
+    return added(layer_sum, carried).astype(jnp.bfloat16)[None]
 
 
 def chunk_cuts(tokens, devices):

time: 174 us -> 157 us (0.902)
  waiting for transfers between devices: 58.5 us -> 46.6 us
  starting transfers between devices: 48 us -> 43.7 us
    ppermute x8 -> x9, waiting for transfers between devices: 5.94 us -> 25.8 us  [around_z(): return lax.ppermute(value, 'blk', [(i, (i + 2) % 8) for i in range(8)])]
    ppermute x16 -> x14, waiting for transfers between devices: 35.1 us -> 17.2 us  [along_x(): return lax.ppermute(value, 'kv', [(i, i ^ 1) for i in range(4)])]
    ppermute x16 -> x14, waiting for transfers between devices: 17.5 us -> 3.62 us  [along_y(): return lax.ppermute(value, 'kv', [(i, i ^ 2) for i in range(4)])]
    ppermute x16 -> x14, starting transfers between devices: 20.3 us -> 15.4 us  [along_x(): return lax.ppermute(value, 'kv', [(i, i ^ 1) for i in range(4)])]
    ppermute x8 -> x9, starting transfers between devices: 9.79 us -> 13 us  [around_z(): return lax.ppermute(value, 'blk', [(i, (i + 2) % 8) for i in range(8)])]
    ppermute x16 -> x14, starting transfers between devices: 17.3 us -> 15.4 us  [along_y(): return lax.ppermute(value, 'kv', [(i, i ^ 2) for i in range(4)])]
    unnamed x28 -> x24, local copies, waits for them, and re-layouts: 7.01 us -> 6.03 us
  transfers between devices with their start and end apart: 44 -> 40, of which waited for: 11 -> 10; matrix products, arithmetic and copies ran while one was open for 5% -> 5% of each run, Pallas kernels for 28% -> 31%
where the time goes in v8:
time: 157 us
  Pallas kernels  49.9 us (32%)
  waiting for transfers between devices  46.6 us (30%)
  starting transfers between devices  43.7 us (28%)
  local copies, waits for them, and re-layouts  6.32 us (4%)
  matrix products  5.11 us (3%)
  other arithmetic  4.48 us (3%)
    pallas_call x4, Pallas kernels, run_plane(): pl.pallas_call(functools.partial(plane_kernel, cap, piece_rows, block_row...  47.8 us
    ppermute x9, waiting for transfers between devices, around_z(): return lax.ppermute(value, 'blk', [(i, (i + 2) % 8) for i in range(8)])  25.8 us
    ppermute x14, waiting for transfers between devices, along_x(): return lax.ppermute(value, 'kv', [(i, i ^ 1) for i in range(4)])  17.2 us
    ppermute x14, starting transfers between devices, along_x(): return lax.ppermute(value, 'kv', [(i, i ^ 1) for i in range(4)])  15.4 us
    ppermute x14, starting transfers between devices, along_y(): return lax.ppermute(value, 'kv', [(i, i ^ 2) for i in range(4)])  15.4 us
    ppermute x9, starting transfers between devices, around_z(): return lax.ppermute(value, 'blk', [(i, (i + 2) % 8) for i in range(8)])  13 us
    unnamed x24, local copies, waits for them, and re-layouts  6.03 us
    dot_general x1, matrix products, attend(): jnp.einsum('rgd,rjd->rgj', grouped_q, key_rows, preferred_element_type=jn...  3.74 us
  transfers between devices with their start and end apart: 40, of which 10 were waited for; matrix products, arithmetic and copies ran while one was open for 5% of the time, Pallas kernels for 31%

profile of v8, /device:TPU:0, one launch (start us, length us, event | category | flops | bytes accessed | tf_op | source)
XLA Modules:
  0.0 156.6 jit_solution(15588533020837347710)
XLA Ops:
  0.0 1.0 copy-done
  1.0 0.9 copy-done.2
  1.9 0.7 copy-done.4
  2.6 0.7 copy-done.6
  3.3 1.3 prepare.2.refs_1_
  4.6 3.0 %collective-permute-start = (bf16[112,2176]{1,0:T(8,128)(2,1)S(1)}, bf16[112,2176]{1,0:T(8,128)(2,1)S(1)}, u32[]{:S(2)}, u32[]{:S(2)}) collective-permute-start(bf16[112,2176]{1,0:T(8,128)(2,1)S(1)} %prepare.2.refs_1_), channel_id=1, source_target_pairs={{0,8},{8,0},{16,24},{24,16},{1,9},{9,1},{17,25},{25,17},{2,10},{10... | collective-permute-start | bytes 1462280 | tf_op jit(solution)/shard_map/ppermute | solution.py:360
  7.6 1.5 collective-permute-start.1
  9.1 1.6 %collective-permute-start.5 = (bf16[112,2176]{1,0:T(8,128)(2,1)S(1)}, bf16[112,2176]{1,0:T(8,128)(2,1)}, u32[]{:S(2)}, u32[]{:S(2)}) collective-permute-start(bf16[112,2176]{1,0:T(8,128)(2,1)S(1)} %prepare.2.refs_1_), channel_id=1, source_target_pairs={{0,2},{1,3},{2,4},{3,5},{4,6},{5,7},{6,0},{7,1},{8,10},{9,11},{10,... | collective-permute-start | bytes 1462280 | tf_op jit(solution)/shard_map/ppermute | solution.py:368
  10.8 0.7 broadcast_in_dim.76
  11.6 0.9 minimum_subtract_fusion
  12.5 3.7 %fusion.33 = (f32[4,8]{1,0:T(4,128)S(1)}, f32[4,8,4096]{2,1,0:T(8,128)S(1)}) fusion(bf16[4,4096,1,128]{3,1,2,0:T(8,128)(2,1)} %param.15, bf16[1,4,8,128]{3,1,2,0:T(4,128)(2,1)} %bitcast.53, pred[4,4096]{1,0:T(4,128)(4,1)S(1)} %iota_compare_fusion.1), kind=kOutput, calls=%fused_computation.58 | convolution fusion | flops 33947616 | bytes 4743296 | tf_op jit(solution)/shard_map/rgd,rjd->rgj/dot_general | solution.py:27
  16.6 0.7 fusion.10
  17.4 1.1 copy-done.10
  18.5 0.7 convolution_add_fusion
  19.2 1.0 collective-permute-done.1.refs_3_
  20.2 1.6 %collective-permute-start.3 = (bf16[64,2176]{1,0:T(8,128)(2,1)S(1)}, bf16[64,2176]{1,0:T(8,128)(2,1)S(1)}, u32[]{:S(2)}, u32[]{:S(2)}) collective-permute-start(bf16[64,2176]{1,0:T(8,128)(2,1)S(1)} %slice.35), channel_id=1, source_target_pairs={{0,16},{8,24},{16,0},{24,8},{1,17},{9,25},{17,1},{25,9},{2,18},{10... | collective-permute-start | bytes 835592 | tf_op jit(solution)/shard_map/ppermute | solution.py:364
  21.8 0.6 collective-permute-start.4
  22.4 1.5 collective-permute-start.6
  23.9 4.9 %collective-permute-done.6 = f32[8,2048]{1,0:T(8,128)S(1)} collective-permute-done((f32[8,2048]{1,0:T(8,128)S(1)}, f32[8,2048]{1,0:T(8,128)S(1)}, u32[]{:S(2)}, u32[]{:S(2)}) %collective-permute-start.6) | collective-permute-done | bytes 65568 | tf_op jit(solution)/shard_map/ppermute | solution.py:360
  28.9 0.7 copy-done.7
  29.6 1.3 collective-permute-start.7
  30.9 1.6 %collective-permute-start.10 = (bf16[112,2176]{1,0:T(8,128)(2,1)}, bf16[112,2176]{1,0:T(8,128)(2,1)S(1)}, u32[]{:S(2)}, u32[]{:S(2)}) collective-permute-start(bf16[112,2176]{1,0:T(8,128)(2,1)} %collective-permute-done.5.refs_1_), channel_id=1, source_target_pairs={{0,2},{1,3},{2,4},{3,5},{4,6},{5,7},{6,0},{7,1},{8,10},{9,11},{10,... | collective-permute-start | bytes 1462280 | tf_op jit(solution)/shard_map/ppermute | solution.py:368
  33.0 1.1 collective-permute-done.7
  34.1 1.3 collective-permute-start.9
  36.1 10.1 %collective-permute-done.10.refs_1_ = bf16[112,2176]{1,0:T(8,128)(2,1)S(1)} collective-permute-done((bf16[112,2176]{1,0:T(8,128)(2,1)}, bf16[112,2176]{1,0:T(8,128)(2,1)S(1)}, u32[]{:S(2)}, u32[]{:S(2)}) %collective-permute-start.10) | collective-permute-done | bytes 487456 | tf_op jit(solution)/shard_map/ppermute | solution.py:368
  46.2 0.9 collective-permute-done.9.refs_3_
  47.1 0.6 collective-permute-start.15
  47.7 1.2 collective-permute-start.16
  48.9 1.6 %collective-permute-start.17 = (bf16[128,2176]{1,0:T(8,128)(2,1)S(1)}, bf16[128,2176]{1,0:T(8,128)(2,1)S(1)}, u32[]{:S(2)}, u32[]{:S(2)}) collective-permute-start(bf16[128,2176]{1,0:T(8,128)(2,1)S(1)} %pad_maximum_fusion), channel_id=1, source_target_pairs={{0,2},{1,3},{2,4},{3,5},{4,6},{5,7},{6,0},{7,1},{8,10},{9,11},{10,... | collective-permute-start | bytes 1671176 | tf_op jit(solution)/shard_map/ppermute | solution.py:368
  50.5 0.9 collective-permute-start.13
  51.5 1.5 collective-permute-start.14
  53.0 0.9 copy-done.8
  53.9 12.1 %plane.4 = (bf16[112,2048]{1,0:T(8,128)(2,1)S(1)}, bf16[112,2048]{1,0:T(8,128)(2,1)S(1)}, bf16[112,2048]{1,0:T(8,128)(2,1)S(1)}, bf16[64,2048]{1,0:T(8,128)(2,1)S(1)}, bf16[48,2048]{1,0:T(8,128)(2,1)S(1)}) custom-call(s32[3]{0:T(128)S(1)} %pad_add_fusion.refs_0_, bf16[112,2176]{1,0:T(8,128)(2,1)S(1)} %prepare.2.refs_1_, ...), custom_call_target="tpu_custom_call" | custom-call | flops 8455716864 | bytes 25165824 | tf_op jit(solution)/shard_map/plane/pallas_call | solution.py:313
  66.1 0.7 collective-permute-start.18
  66.8 1.3 collective-permute-start.19
  68.1 1.8 %collective-permute-start.20 = (bf16[128,2176]{1,0:T(8,128)(2,1)S(1)}, bf16[128,2176]{1,0:T(8,128)(2,1)S(1)}, u32[]{:S(2)}, u32[]{:S(2)}) collective-permute-start(bf16[128,2176]{1,0:T(8,128)(2,1)S(1)} %pad_maximum_fusion.1), channel_id=1, source_target_pairs={{0,2},{1,3},{2,4},{3,5},{4,6},{5,7},{6,0},{7,1},{8,10},{9,11},{10,... | collective-permute-start | bytes 1671176 | tf_op jit(solution)/shard_map/ppermute | solution.py:368
  69.9 0.8 collective-permute-start.21
  70.7 1.4 collective-permute-start.22
  72.1 11.7 %plane.5 = (bf16[112,2048]{1,0:T(8,128)(2,1)S(1)}, bf16[112,2048]{1,0:T(8,128)(2,1)S(1)}, bf16[112,2048]{1,0:T(8,128)(2,1)S(1)}, bf16[64,2048]{1,0:T(8,128)(2,1)S(1)}, bf16[48,2048]{1,0:T(8,128)(2,1)S(1)}) custom-call(s32[3]{0:T(128)S(1)} %pad_add_fusion.refs_0_, bf16[112,2176]{1,0:T(8,128)(2,1)} %collective-permute-done.5.refs_1_, ...), custom_call_target="tpu_custom_call" | custom-call | flops 8455716864 | bytes 25165824 | tf_op jit(solution)/shard_map/plane/pallas_call | solution.py:313
  84.0 0.7 collective-permute-start.26
  84.7 1.3 collective-permute-start.27
  85.9 1.6 %collective-permute-start.23 = (bf16[128,2176]{1,0:T(8,128)(2,1)S(1)}, bf16[128,2176]{1,0:T(8,128)(2,1)S(1)}, u32[]{:S(2)}, u32[]{:S(2)}) collective-permute-start(bf16[128,2176]{1,0:T(8,128)(2,1)S(1)} %collective-permute-done.20.refs_4_), channel_id=1, source_target_pairs={{0,2},{1,3},{2,4},{3,5},{4,6},{5,7},{6,0},{7,1},{8,10},{9,11},{10,... | collective-permute-start | bytes 1671176 | tf_op jit(solution)/shard_map/ppermute | solution.py:368
  87.5 0.8 collective-permute-start.24
  88.3 1.4 collective-permute-start.25
  89.7 12.0 %plane.6 = (bf16[112,2048]{1,0:T(8,128)(2,1)S(1)}, bf16[112,2048]{1,0:T(8,128)(2,1)S(1)}, bf16[112,2048]{1,0:T(8,128)(2,1)S(1)}, bf16[112,2048]{1,0:T(8,128)(2,1)S(1)}) custom-call(s32[3]{0:T(128)S(1)} %pad_add_fusion.refs_0_, bf16[112,2176]{1,0:T(8,128)(2,1)S(1)} %collective-permute-done.10.refs_1_, bf16[112,2176]{1,0:T(8,128)(2,1)S(1)} %collective-permute-done.15.refs_2_, ...), custom_call_target="tpu_custom_call" | custom-call | flops 8455716864 | bytes 25165824 | tf_op jit(solution)/shard_map/plane/pallas_call | solution.py:313
  101.8 0.7 collective-permute-start.28
  102.5 1.3 collective-permute-start.29
  103.8 0.8 collective-permute-start.30
  104.6 1.4 collective-permute-start.35
  106.0 0.7 collective-permute-start.36
  106.8 12.0 %plane.7 = (bf16[112,2048]{1,0:T(8,128)(2,1)S(1)}, bf16[112,2048]{1,0:T(8,128)(2,1)S(1)}, bf16[112,2048]{1,0:T(8,128)(2,1)S(1)}, bf16[112,2048]{1,0:T(8,128)(2,1)S(1)}) custom-call(s32[3]{0:T(128)S(1)} %pad_add_fusion.refs_0_, bf16[112,2176]{1,0:T(8,128)(2,1)S(1)} %slice.41.refs_1_, bf16[112,2176]{1,0:T(8,128)(2,1)S(1)} %collective-permute-done.18.refs_2_, ...), custom_call_target="tpu_custom_call" | custom-call | flops 8455716864 | bytes 25165824 | tf_op jit(solution)/shard_map/plane/pallas_call | solution.py:313
  119.0 1.8 %collective-permute-start.37 = (bf16[112,2048]{1,0:T(8,128)(2,1)S(1)}, bf16[112,2048]{1,0:T(8,128)(2,1)S(1)}, u32[]{:S(2)}, u32[]{:S(2)}) collective-permute-start(bf16[112,2048]{1,0:T(8,128)(2,1)S(1)} %add_convert_fusion.3), channel_id=1, source_target_pairs={{0,2},{1,3},{2,4},{3,5},{4,6},{5,7},{6,0},{7,1},{8,10},{9,11},{10,... | collective-permute-start | bytes 1376264 | tf_op jit(solution)/shard_map/ppermute | solution.py:368
  120.9 0.6 collective-permute-start.31
  121.5 0.7 collective-permute-start.32
  122.2 7.1 %collective-permute-done.32.passed_1_ref = bf16[48,2048]{1,0:T(8,128)(2,1)S(1)} collective-permute-done((bf16[48,2048]{1,0:T(8,128)(2,1)S(1)}, bf16[48,2048]{1,0:T(8,128)(2,1)S(1)}, u32[]{:S(2)}, u32[]{:S(2)}) %collective-permute-start.32) | collective-permute-done | bytes 196640 | tf_op jit(solution)/shard_map/ppermute | solution.py:360
  129.5 0.7 collective-permute-start.33
  130.2 1.0 collective-permute-start.34
  131.5 1.4 collective-permute-start.38
  132.9 5.1 %collective-permute-done.33 = bf16[112,2048]{1,0:T(8,128)(2,1)S(1)} collective-permute-done((bf16[112,2048]{1,0:T(8,128)(2,1)S(1)}, bf16[112,2048]{1,0:T(8,128)(2,1)S(1)}, u32[]{:S(2)}, u32[]{:S(2)}) %collective-permute-start.33) | collective-permute-done | bytes 458784 | tf_op jit(solution)/shard_map/ppermute | solution.py:360
  138.1 0.6 collective-permute-done.34
  138.7 6.1 %collective-permute-done.38 = bf16[112,2048]{1,0:T(8,128)(2,1)S(1)} collective-permute-done((bf16[112,2048]{1,0:T(8,128)(2,1)S(1)}, bf16[112,2048]{1,0:T(8,128)(2,1)S(1)}, u32[]{:S(2)}, u32[]{:S(2)}) %collective-permute-start.38) | collective-permute-done | bytes 458784 | tf_op jit(solution)/shard_map/ppermute | solution.py:368
  145.1 0.8 collective-permute-start.39
  145.9 9.5 %collective-permute-done.39 = bf16[112,2048]{1,0:T(8,128)(2,1)S(1)} collective-permute-done((bf16[112,2048]{1,0:T(8,128)(2,1)S(1)}, bf16[112,2048]{1,0:T(8,128)(2,1)S(1)}, u32[]{:S(2)}, u32[]{:S(2)}) %collective-permute-start.39) | collective-permute-done | bytes 458784 | tf_op jit(solution)/shard_map/ppermute | solution.py:368
  155.4 1.2 fusion.13
  (87 shorter events, 3.5 us)
Async XLA Ops:
  0.0 16.3 %copy-start.11 = (f32[8]{0:T(128)S(1)}, f32[8]{0:T(128)}, u32[]{:S(2)}) copy-start(f32[8]{0:T(128)} %param.18) | copy-start | bytes 100
  0.0 1.0 copy-start
  1.0 0.9 copy-start.2
  1.9 0.7 copy-start.4
  2.6 0.7 copy-start.6
  4.6 14.6 %collective-permute-start = (bf16[112,2176]{1,0:T(8,128)(2,1)S(1)}, bf16[112,2176]{1,0:T(8,128)(2,1)S(1)}, u32[]{:S(2)}, u32[]{:S(2)}) collective-permute-start(bf16[112,2176]{1,0:T(8,128)(2,1)S(1)} %prepare.2.refs_1_), channel_id=1, source_target_pairs={{0,8},{8,0},{16,24},{24,16},{1,9},{9,1},{17,25},{25,17},{2,10},{10... | collective-permute-start | bytes 1462280 | tf_op jit(solution)/shard_map/ppermute | solution.py:360
  7.6 12.6 %collective-permute-start.1 = (bf16[112,2176]{1,0:T(8,128)(2,1)S(1)}, bf16[112,2176]{1,0:T(8,128)(2,1)S(1)}, u32[]{:S(2)}, u32[]{:S(2)}) collective-permute-start(bf16[112,2176]{1,0:T(8,128)(2,1)S(1)} %prepare.2.refs_1_), channel_id=1, source_target_pairs={{0,16},{8,24},{16,0},{24,8},{1,17},{9,25},{17,1},{25,9},{2,18},{10... | collective-permute-start | bytes 1462280 | tf_op jit(solution)/shard_map/ppermute | solution.py:364
  9.1 19.7 %collective-permute-start.5 = (bf16[112,2176]{1,0:T(8,128)(2,1)S(1)}, bf16[112,2176]{1,0:T(8,128)(2,1)}, u32[]{:S(2)}, u32[]{:S(2)}) collective-permute-start(bf16[112,2176]{1,0:T(8,128)(2,1)S(1)} %prepare.2.refs_1_), channel_id=1, source_target_pairs={{0,2},{1,3},{2,4},{3,5},{4,6},{5,7},{6,0},{7,1},{8,10},{9,11},{10,... | collective-permute-start | bytes 1462280 | tf_op jit(solution)/shard_map/ppermute | solution.py:368
  10.7 9.5 %collective-permute-start.2 = (bf16[2048,768]{1,0:T(8,128)(2,1)}, bf16[2048,768]{1,0:T(8,128)(2,1)}, u32[]{:S(2)}, u32[]{:S(2)}) collective-permute-start(bf16[2048,768]{1,0:T(8,128)(2,1)} %bitcast.55), channel_id=1, source_target_pairs={{0,1},{1,0},{2,3},{3,2},{4,5},{5,4},{6,7},{7,6},{8,9},{9,8},{10,11... | collective-permute-start | bytes 9437192 | tf_op jit(solution)/shard_map/ppermute | solution.py:372
  11.6 5.0 %copy-start.9 = (bf16[4,4096,1,128]{3,1,2,0:T(8,128)(2,1)S(1)}, bf16[4,4096,1,128]{3,1,2,0:T(8,128)(2,1)}, u32[]{:S(2)}) copy-start(bf16[4,4096,1,128]{3,1,2,0:T(8,128)(2,1)} %param.16) | copy-start | bytes 12582916
  16.3 2.2 %copy-start.10 = (bf16[1024,2048]{1,0:T(8,128)(2,1)S(1)}, bf16[1024,2048]{1,0:T(8,128)(2,1)}, u32[]{:S(2)}) copy-start(bf16[1024,2048]{1,0:T(8,128)(2,1)} %param.19) | copy-start | bytes 12582916
  17.3 18.3 %copy-start.3 = (bf16[2048,32]{0,1:T(8,128)(2,1)S(1)}, bf16[2048,32]{0,1:T(8,128)(2,1)}, u32[]{:S(2)}) copy-start(bf16[2048,32]{0,1:T(8,128)(2,1)} %param.23) | copy-start | bytes 393220
  17.3 18.3 %copy-start.5 = (f32[2048]{0:T(1024)S(1)}, f32[2048]{0:T(1024)}, u32[]{:S(2)}) copy-start(f32[2048]{0:T(1024)} %param.22) | copy-start | bytes 24580
  20.2 9.3 %collective-permute-start.3 = (bf16[64,2176]{1,0:T(8,128)(2,1)S(1)}, bf16[64,2176]{1,0:T(8,128)(2,1)S(1)}, u32[]{:S(2)}, u32[]{:S(2)}) collective-permute-start(bf16[64,2176]{1,0:T(8,128)(2,1)S(1)} %slice.35), channel_id=1, source_target_pairs={{0,16},{8,24},{16,0},{24,8},{1,17},{9,25},{17,1},{25,9},{2,18},{10... | collective-permute-start | bytes 835592 | tf_op jit(solution)/shard_map/ppermute | solution.py:364
  21.8 7.0 %collective-permute-start.4 = (bf16[48,2176]{1,0:T(8,128)(2,1)S(1)}, bf16[48,2176]{1,0:T(8,128)(2,1)S(1)}, u32[]{:S(2)}, u32[]{:S(2)}) collective-permute-start(bf16[48,2176]{1,0:T(8,128)(2,1)S(1)} %slice.36), channel_id=1, source_target_pairs={{0,8},{8,0},{16,24},{24,16},{1,9},{9,1},{17,25},{25,17},{2,10},{10... | collective-permute-start | bytes 626696 | tf_op jit(solution)/shard_map/ppermute | solution.py:360
  22.4 6.4 %collective-permute-start.6 = (f32[8,2048]{1,0:T(8,128)S(1)}, f32[8,2048]{1,0:T(8,128)S(1)}, u32[]{:S(2)}, u32[]{:S(2)}) collective-permute-start(f32[8,2048]{1,0:T(8,128)S(1)} %pad_maximum_fusion.2), channel_id=1, source_target_pairs={{0,8},{8,0},{16,24},{24,16},{1,9},{9,1},{17,25},{25,17},{2,10},{10... | collective-permute-start | bytes 196616 | tf_op jit(solution)/shard_map/ppermute | solution.py:360
  23.9 12.1 %collective-permute-start.11 = (bf16[2048,768]{1,0:T(8,128)(2,1)}, bf16[2048,768]{1,0:T(8,128)(2,1)}, u32[]{:S(2)}, u32[]{:S(2)}) collective-permute-start(bf16[2048,768]{1,0:T(8,128)(2,1)} %bitcast.11.refs_8_.refs_6_), channel_id=1, source_target_pairs={{0,1},{1,0},{2,3},{3,2},{4,5},{5,4},{6,7},{7,6},{8,9},{9,8},{10,11... | collective-permute-start | bytes 9437192 | tf_op jit(solution)/shard_map/ppermute | solution.py:372
  28.9 0.7 copy-start.7
  29.6 17.5 %collective-permute-start.12 = (bf16[768,2048]{1,0:T(8,128)(2,1)}, bf16[768,2048]{1,0:T(8,128)(2,1)}, u32[]{:S(2)}, u32[]{:S(2)}) collective-permute-start(bf16[768,2048]{1,0:T(8,128)(2,1)} %bitcast.12.refs_9_.refs_7_), channel_id=1, source_target_pairs={{0,1},{1,0},{2,3},{3,2},{4,5},{5,4},{6,7},{7,6},{8,9},{9,8},{10,11... | collective-permute-start | bytes 9437192 | tf_op jit(solution)/shard_map/ppermute | solution.py:372
  29.6 4.5 %collective-permute-start.7 = (f32[8,2048]{1,0:T(8,128)S(1)}, f32[8,2048]{1,0:T(8,128)S(1)}, u32[]{:S(2)}, u32[]{:S(2)}) collective-permute-start(f32[8,2048]{1,0:T(8,128)S(1)} %add.117), channel_id=1, source_target_pairs={{0,16},{8,24},{16,0},{24,8},{1,17},{9,25},{17,1},{25,9},{2,18},{10... | collective-permute-start | bytes 196616 | tf_op jit(solution)/shard_map/ppermute | solution.py:364
  30.9 15.3 %collective-permute-start.10 = (bf16[112,2176]{1,0:T(8,128)(2,1)}, bf16[112,2176]{1,0:T(8,128)(2,1)S(1)}, u32[]{:S(2)}, u32[]{:S(2)}) collective-permute-start(bf16[112,2176]{1,0:T(8,128)(2,1)} %collective-permute-done.5.refs_1_), channel_id=1, source_target_pairs={{0,2},{1,3},{2,4},{3,5},{4,6},{5,7},{6,0},{7,1},{8,10},{9,11},{10,... | collective-permute-start | bytes 1462280 | tf_op jit(solution)/shard_map/ppermute | solution.py:368
  32.5 13.7 %collective-permute-start.8 = (bf16[112,2176]{1,0:T(8,128)(2,1)}, bf16[112,2176]{1,0:T(8,128)(2,1)S(1)}, u32[]{:S(2)}, u32[]{:S(2)}) collective-permute-start(bf16[112,2176]{1,0:T(8,128)(2,1)} %collective-permute-done.5.refs_1_), channel_id=1, source_target_pairs={{0,8},{8,0},{16,24},{24,16},{1,9},{9,1},{17,25},{25,17},{2,10},{10... | collective-permute-start | bytes 1462280 | tf_op jit(solution)/shard_map/ppermute | solution.py:360
  34.1 13.0 %collective-permute-start.9 = (bf16[112,2176]{1,0:T(8,128)(2,1)}, bf16[112,2176]{1,0:T(8,128)(2,1)S(1)}, u32[]{:S(2)}, u32[]{:S(2)}) collective-permute-start(bf16[112,2176]{1,0:T(8,128)(2,1)} %collective-permute-done.5.refs_1_), channel_id=1, source_target_pairs={{0,16},{8,24},{16,0},{24,8},{1,17},{9,25},{17,1},{25,9},{2,18},{10... | collective-permute-start | bytes 1462280 | tf_op jit(solution)/shard_map/ppermute | solution.py:364
  47.1 18.9 %collective-permute-start.15 = (bf16[112,2176]{1,0:T(8,128)(2,1)S(1)}, bf16[112,2176]{1,0:T(8,128)(2,1)S(1)}, u32[]{:S(2)}, u32[]{:S(2)}) collective-permute-start(bf16[112,2176]{1,0:T(8,128)(2,1)S(1)} %collective-permute-done.10.refs_1_), channel_id=1, source_target_pairs={{0,8},{8,0},{16,24},{24,16},{1,9},{9,1},{17,25},{25,17},{2,10},{10... | collective-permute-start | bytes 1462280 | tf_op jit(solution)/shard_map/ppermute | solution.py:360
  47.7 18.4 %collective-permute-start.16 = (bf16[112,2176]{1,0:T(8,128)(2,1)S(1)}, bf16[112,2176]{1,0:T(8,128)(2,1)S(1)}, u32[]{:S(2)}, u32[]{:S(2)}) collective-permute-start(bf16[112,2176]{1,0:T(8,128)(2,1)S(1)} %collective-permute-done.10.refs_1_), channel_id=1, source_target_pairs={{0,16},{8,24},{16,0},{24,8},{1,17},{9,25},{17,1},{25,9},{2,18},{10... | collective-permute-start | bytes 1462280 | tf_op jit(solution)/shard_map/ppermute | solution.py:364
  48.9 17.1 %collective-permute-start.17 = (bf16[128,2176]{1,0:T(8,128)(2,1)S(1)}, bf16[128,2176]{1,0:T(8,128)(2,1)S(1)}, u32[]{:S(2)}, u32[]{:S(2)}) collective-permute-start(bf16[128,2176]{1,0:T(8,128)(2,1)S(1)} %pad_maximum_fusion), channel_id=1, source_target_pairs={{0,2},{1,3},{2,4},{3,5},{4,6},{5,7},{6,0},{7,1},{8,10},{9,11},{10,... | collective-permute-start | bytes 1671176 | tf_op jit(solution)/shard_map/ppermute | solution.py:368
  50.5 15.4 %collective-permute-start.13 = (bf16[64,2176]{1,0:T(8,128)(2,1)S(1)}, bf16[64,2176]{1,0:T(8,128)(2,1)S(1)}, u32[]{:S(2)}, u32[]{:S(2)}) collective-permute-start(bf16[64,2176]{1,0:T(8,128)(2,1)S(1)} %slice.39), channel_id=1, source_target_pairs={{0,16},{8,24},{16,0},{24,8},{1,17},{9,25},{17,1},{25,9},{2,18},{10... | collective-permute-start | bytes 835592 | tf_op jit(solution)/shard_map/ppermute | solution.py:364
  51.5 14.5 %collective-permute-start.14 = (bf16[48,2176]{1,0:T(8,128)(2,1)S(1)}, bf16[48,2176]{1,0:T(8,128)(2,1)S(1)}, u32[]{:S(2)}, u32[]{:S(2)}) collective-permute-start(bf16[48,2176]{1,0:T(8,128)(2,1)S(1)} %slice.40), channel_id=1, source_target_pairs={{0,8},{8,0},{16,24},{24,16},{1,9},{9,1},{17,25},{25,17},{2,10},{10... | collective-permute-start | bytes 626696 | tf_op jit(solution)/shard_map/ppermute | solution.py:360
  53.0 0.9 copy-start.8
  66.1 17.7 %collective-permute-start.18 = (bf16[112,2176]{1,0:T(8,128)(2,1)S(1)}, bf16[112,2176]{1,0:T(8,128)(2,1)S(1)}, u32[]{:S(2)}, u32[]{:S(2)}) collective-permute-start(bf16[112,2176]{1,0:T(8,128)(2,1)S(1)} %slice.41.refs_1_), channel_id=1, source_target_pairs={{0,8},{8,0},{16,24},{24,16},{1,9},{9,1},{17,25},{25,17},{2,10},{10... | collective-permute-start | bytes 1462280 | tf_op jit(solution)/shard_map/ppermute | solution.py:360
  66.8 17.0 %collective-permute-start.19 = (bf16[112,2176]{1,0:T(8,128)(2,1)S(1)}, bf16[112,2176]{1,0:T(8,128)(2,1)S(1)}, u32[]{:S(2)}, u32[]{:S(2)}) collective-permute-start(bf16[112,2176]{1,0:T(8,128)(2,1)S(1)} %slice.41.refs_1_), channel_id=1, source_target_pairs={{0,16},{8,24},{16,0},{24,8},{1,17},{9,25},{17,1},{25,9},{2,18},{10... | collective-permute-start | bytes 1462280 | tf_op jit(solution)/shard_map/ppermute | solution.py:364
  68.1 15.7 %collective-permute-start.20 = (bf16[128,2176]{1,0:T(8,128)(2,1)S(1)}, bf16[128,2176]{1,0:T(8,128)(2,1)S(1)}, u32[]{:S(2)}, u32[]{:S(2)}) collective-permute-start(bf16[128,2176]{1,0:T(8,128)(2,1)S(1)} %pad_maximum_fusion.1), channel_id=1, source_target_pairs={{0,2},{1,3},{2,4},{3,5},{4,6},{5,7},{6,0},{7,1},{8,10},{9,11},{10,... | collective-permute-start | bytes 1671176 | tf_op jit(solution)/shard_map/ppermute | solution.py:368
  69.9 13.9 %collective-permute-start.21 = (bf16[64,2048]{1,0:T(8,128)(2,1)S(1)}, bf16[64,2048]{1,0:T(8,128)(2,1)S(1)}, u32[]{:S(2)}, u32[]{:S(2)}) collective-permute-start(bf16[64,2048]{1,0:T(8,128)(2,1)S(1)} %get-tuple-element.122), channel_id=1, source_target_pairs={{0,16},{8,24},{16,0},{24,8},{1,17},{9,25},{17,1},{25,9},{2,18},{10... | collective-permute-start | bytes 786440 | tf_op jit(solution)/shard_map/ppermute | solution.py:364
  70.7 13.1 %collective-permute-start.22 = (bf16[48,2048]{1,0:T(8,128)(2,1)S(1)}, bf16[48,2048]{1,0:T(8,128)(2,1)S(1)}, u32[]{:S(2)}, u32[]{:S(2)}) collective-permute-start(bf16[48,2048]{1,0:T(8,128)(2,1)S(1)} %get-tuple-element.123), channel_id=1, source_target_pairs={{0,8},{8,0},{16,24},{24,16},{1,9},{9,1},{17,25},{25,17},{2,10},{10... | collective-permute-start | bytes 589832 | tf_op jit(solution)/shard_map/ppermute | solution.py:360
  84.0 17.7 %collective-permute-start.26 = (bf16[112,2048]{1,0:T(8,128)(2,1)S(1)}, bf16[112,2048]{1,0:T(8,128)(2,1)S(1)}, u32[]{:S(2)}, u32[]{:S(2)}) collective-permute-start(bf16[112,2048]{1,0:T(8,128)(2,1)S(1)} %get-tuple-element.139), channel_id=1, source_target_pairs={{0,8},{8,0},{16,24},{24,16},{1,9},{9,1},{17,25},{25,17},{2,10},{10... | collective-permute-start | bytes 1376264 | tf_op jit(solution)/shard_map/ppermute | solution.py:360
  84.7 17.0 %collective-permute-start.27 = (bf16[112,2048]{1,0:T(8,128)(2,1)S(1)}, bf16[112,2048]{1,0:T(8,128)(2,1)S(1)}, u32[]{:S(2)}, u32[]{:S(2)}) collective-permute-start(bf16[112,2048]{1,0:T(8,128)(2,1)S(1)} %get-tuple-element.140), channel_id=1, source_target_pairs={{0,16},{8,24},{16,0},{24,8},{1,17},{9,25},{17,1},{25,9},{2,18},{10... | collective-permute-start | bytes 1376264 | tf_op jit(solution)/shard_map/ppermute | solution.py:364
  85.9 15.8 %collective-permute-start.23 = (bf16[128,2176]{1,0:T(8,128)(2,1)S(1)}, bf16[128,2176]{1,0:T(8,128)(2,1)S(1)}, u32[]{:S(2)}, u32[]{:S(2)}) collective-permute-start(bf16[128,2176]{1,0:T(8,128)(2,1)S(1)} %collective-permute-done.20.refs_4_), channel_id=1, source_target_pairs={{0,2},{1,3},{2,4},{3,5},{4,6},{5,7},{6,0},{7,1},{8,10},{9,11},{10,... | collective-permute-start | bytes 1671176 | tf_op jit(solution)/shard_map/ppermute | solution.py:368
  87.5 14.2 %collective-permute-start.24 = (bf16[64,2048]{1,0:T(8,128)(2,1)S(1)}, bf16[64,2048]{1,0:T(8,128)(2,1)S(1)}, u32[]{:S(2)}, u32[]{:S(2)}) collective-permute-start(bf16[64,2048]{1,0:T(8,128)(2,1)S(1)} %get-tuple-element.133), channel_id=1, source_target_pairs={{0,16},{8,24},{16,0},{24,8},{1,17},{9,25},{17,1},{25,9},{2,18},{10... | collective-permute-start | bytes 786440 | tf_op jit(solution)/shard_map/ppermute | solution.py:364
  88.3 13.4 %collective-permute-start.25 = (bf16[48,2048]{1,0:T(8,128)(2,1)S(1)}, bf16[48,2048]{1,0:T(8,128)(2,1)S(1)}, u32[]{:S(2)}, u32[]{:S(2)}) collective-permute-start(bf16[48,2048]{1,0:T(8,128)(2,1)S(1)} %get-tuple-element.134), channel_id=1, source_target_pairs={{0,8},{8,0},{16,24},{24,16},{1,9},{9,1},{17,25},{25,17},{2,10},{10... | collective-permute-start | bytes 589832 | tf_op jit(solution)/shard_map/ppermute | solution.py:360
  101.8 16.9 %collective-permute-start.28 = (bf16[112,2048]{1,0:T(8,128)(2,1)S(1)}, bf16[112,2048]{1,0:T(8,128)(2,1)S(1)}, u32[]{:S(2)}, u32[]{:S(2)}) collective-permute-start(bf16[112,2048]{1,0:T(8,128)(2,1)S(1)} %get-tuple-element.158), channel_id=1, source_target_pairs={{0,8},{8,0},{16,24},{24,16},{1,9},{9,1},{17,25},{25,17},{2,10},{10... | collective-permute-start | bytes 1376264 | tf_op jit(solution)/shard_map/ppermute | solution.py:360
  102.5 16.2 %collective-permute-start.29 = (bf16[112,2048]{1,0:T(8,128)(2,1)S(1)}, bf16[112,2048]{1,0:T(8,128)(2,1)S(1)}, u32[]{:S(2)}, u32[]{:S(2)}) collective-permute-start(bf16[112,2048]{1,0:T(8,128)(2,1)S(1)} %get-tuple-element.159), channel_id=1, source_target_pairs={{0,16},{8,24},{16,0},{24,8},{1,17},{9,25},{17,1},{25,9},{2,18},{10... | collective-permute-start | bytes 1376264 | tf_op jit(solution)/shard_map/ppermute | solution.py:364
  103.8 15.0 %collective-permute-start.30 = (bf16[112,2048]{1,0:T(8,128)(2,1)S(1)}, bf16[112,2048]{1,0:T(8,128)(2,1)S(1)}, u32[]{:S(2)}, u32[]{:S(2)}) collective-permute-start(bf16[112,2048]{1,0:T(8,128)(2,1)S(1)} %get-tuple-element.160), channel_id=1, source_target_pairs={{0,2},{1,3},{2,4},{3,5},{4,6},{5,7},{6,0},{7,1},{8,10},{9,11},{10,... | collective-permute-start | bytes 1376264 | tf_op jit(solution)/shard_map/ppermute | solution.py:368
  104.6 26.6 %collective-permute-start.35 = (bf16[112,2048]{1,0:T(8,128)(2,1)S(1)}, bf16[112,2048]{1,0:T(8,128)(2,1)S(1)}, u32[]{:S(2)}, u32[]{:S(2)}) collective-permute-start(bf16[112,2048]{1,0:T(8,128)(2,1)S(1)} %get-tuple-element.163), channel_id=1, source_target_pairs={{0,8},{8,0},{16,24},{24,16},{1,9},{9,1},{17,25},{25,17},{2,10},{10... | collective-permute-start | bytes 1376264 | tf_op jit(solution)/shard_map/ppermute | solution.py:360
  106.0 25.2 %collective-permute-start.36 = (bf16[112,2048]{1,0:T(8,128)(2,1)S(1)}, bf16[112,2048]{1,0:T(8,128)(2,1)S(1)}, u32[]{:S(2)}, u32[]{:S(2)}) collective-permute-start(bf16[112,2048]{1,0:T(8,128)(2,1)S(1)} %get-tuple-element.164), channel_id=1, source_target_pairs={{0,16},{8,24},{16,0},{24,8},{1,17},{9,25},{17,1},{25,9},{2,18},{10... | collective-permute-start | bytes 1376264 | tf_op jit(solution)/shard_map/ppermute | solution.py:364
  119.0 12.2 %collective-permute-start.37 = (bf16[112,2048]{1,0:T(8,128)(2,1)S(1)}, bf16[112,2048]{1,0:T(8,128)(2,1)S(1)}, u32[]{:S(2)}, u32[]{:S(2)}) collective-permute-start(bf16[112,2048]{1,0:T(8,128)(2,1)S(1)} %add_convert_fusion.3), channel_id=1, source_target_pairs={{0,2},{1,3},{2,4},{3,5},{4,6},{5,7},{6,0},{7,1},{8,10},{9,11},{10,... | collective-permute-start | bytes 1376264 | tf_op jit(solution)/shard_map/ppermute | solution.py:368
  120.9 34.6 %copy-start.1 = (bf16[1,111,2048]{2,1,0:T(8,128)(2,1)S(1)}, bf16[1,111,2048]{2,1,0:T(8,128)(2,1)}, u32[]{:S(2)}) copy-start(bf16[1,111,2048]{2,1,0:T(8,128)(2,1)} %param.21) | copy-start | bytes 1363972
  120.9 8.5 %collective-permute-start.31 = (bf16[64,2048]{1,0:T(8,128)(2,1)S(1)}, bf16[64,2048]{1,0:T(8,128)(2,1)S(1)}, u32[]{:S(2)}, u32[]{:S(2)}) collective-permute-start(bf16[64,2048]{1,0:T(8,128)(2,1)S(1)} %slice.45), channel_id=1, source_target_pairs={{0,16},{8,24},{16,0},{24,8},{1,17},{9,25},{17,1},{25,9},{2,18},{10... | collective-permute-start | bytes 786440 | tf_op jit(solution)/shard_map/ppermute | solution.py:364
  121.5 7.8 %collective-permute-start.32 = (bf16[48,2048]{1,0:T(8,128)(2,1)S(1)}, bf16[48,2048]{1,0:T(8,128)(2,1)S(1)}, u32[]{:S(2)}, u32[]{:S(2)}) collective-permute-start(bf16[48,2048]{1,0:T(8,128)(2,1)S(1)} %slice.46), channel_id=1, source_target_pairs={{0,8},{8,0},{16,24},{24,16},{1,9},{9,1},{17,25},{25,17},{2,10},{10... | collective-permute-start | bytes 589832 | tf_op jit(solution)/shard_map/ppermute | solution.py:360
  129.5 8.5 %collective-permute-start.33 = (bf16[112,2048]{1,0:T(8,128)(2,1)S(1)}, bf16[112,2048]{1,0:T(8,128)(2,1)S(1)}, u32[]{:S(2)}, u32[]{:S(2)}) collective-permute-start(bf16[112,2048]{1,0:T(8,128)(2,1)S(1)} %get-tuple-element.177), channel_id=1, source_target_pairs={{0,8},{8,0},{16,24},{24,16},{1,9},{9,1},{17,25},{25,17},{2,10},{10... | collective-permute-start | bytes 1376264 | tf_op jit(solution)/shard_map/ppermute | solution.py:360
  130.2 8.5 %collective-permute-start.34 = (bf16[112,2048]{1,0:T(8,128)(2,1)S(1)}, bf16[112,2048]{1,0:T(8,128)(2,1)S(1)}, u32[]{:S(2)}, u32[]{:S(2)}) collective-permute-start(bf16[112,2048]{1,0:T(8,128)(2,1)S(1)} %get-tuple-element.178), channel_id=1, source_target_pairs={{0,16},{8,24},{16,0},{24,8},{1,17},{9,25},{17,1},{25,9},{2,18},{10... | collective-permute-start | bytes 1376264 | tf_op jit(solution)/shard_map/ppermute | solution.py:364
  131.5 13.3 %collective-permute-start.38 = (bf16[112,2048]{1,0:T(8,128)(2,1)S(1)}, bf16[112,2048]{1,0:T(8,128)(2,1)S(1)}, u32[]{:S(2)}, u32[]{:S(2)}) collective-permute-start(bf16[112,2048]{1,0:T(8,128)(2,1)S(1)} %add_convert_fusion.2), channel_id=1, source_target_pairs={{0,2},{1,3},{2,4},{3,5},{4,6},{5,7},{6,0},{7,1},{8,10},{9,11},{10,... | collective-permute-start | bytes 1376264 | tf_op jit(solution)/shard_map/ppermute | solution.py:368
  145.1 10.3 %collective-permute-start.39 = (bf16[112,2048]{1,0:T(8,128)(2,1)S(1)}, bf16[112,2048]{1,0:T(8,128)(2,1)S(1)}, u32[]{:S(2)}, u32[]{:S(2)}) collective-permute-start(bf16[112,2048]{1,0:T(8,128)(2,1)S(1)} %add_convert_fusion.1), channel_id=1, source_target_pairs={{0,2},{1,3},{2,4},{3,5},{4,6},{5,7},{6,0},{7,1},{8,10},{9,11},{10,... | collective-permute-start | bytes 1376264 | tf_op jit(solution)/shard_map/ppermute | solution.py:368

commit v9 on v8

--- a/solution.py
+++ b/solution.py
@@ -356,6 +356,21 @@
     )(to_x, to_y, passed_0, passed_1)
 
 
+def join_kernel(far_ref, risen_ref, own_ref, x_ref, y_ref, far_out, own_out):
+    far_out[...] = (far_ref[...].astype(jnp.float32) + risen_ref[...].astype(jnp.float32)).astype(jnp.bfloat16)
+    total = own_ref[...].astype(jnp.float32) + x_ref[...].astype(jnp.float32) + y_ref[...].astype(jnp.float32)
+    own_out[...] = total.astype(jnp.bfloat16)
+
+
+def join(far, risen, own, from_x, from_y):
+    return pl.pallas_call(
+        join_kernel,
+        out_shape=[jax.ShapeDtypeStruct(own.shape, own.dtype)] * 2,
+        compiler_params=pltpu.CompilerParams(vmem_limit_bytes=16 << 20),
+        name="join",
+    )(far, risen, own, from_x, from_y)
+
+
 def along_x(value):
     return lax.ppermute(value, "kv", [(i, i ^ 1) for i in range(4)])
 
@@ -444,13 +459,14 @@
     width = partial_proj.shape[1]
     ids_row = jnp.pad(ids[:1].astype(jnp.float32), ((0, 0), (0, width - ids.shape[1])))
     shared = jnp.concatenate([partial_proj, jnp.where(is_mine, ids_row, 0.0)], axis=0)
-    sides_0, other_gate, shared = fence(sides_0, other_gate, shared)
-
     shared = shared + along_x(shared)
+    sides_0, block_1, other_gate = fence(sides_0, block_1, other_gate)
+
     corner_0 = spread_corner(sides_0)
-    corner_0, block_1, shared, expert_down = fence(corner_0, block_1, shared, expert_down)
+    corner_0, shared = fence(corner_0, shared)
 
     shared = shared + along_y(shared)
+    shared, expert_down = fence(shared, expert_down)
     sides_1 = spread_sides(block_1)
     block_2 = around_z(block_1)
     other_down = across_chip(expert_down[0])
@@ -483,33 +499,36 @@
     block_3, decodes_1 = arrived[:tokens], arrived[tokens:]
 
     sides_3 = spread_sides(block_3)
-    risen_2 = around_z(jnp.concatenate(corner_1 + (decodes_1,), axis=0))
+    risen = around_z(jnp.concatenate(corner_1 + (decodes_1,), axis=0))
     passed_0 = return_corner(sums_0)
-    sums_1 = apply((block_1,) + sides_1 + corner_1 + (decodes_1,), halves)
-    sides_3, risen_2, passed_0, sums_0, sums_1 = fence(sides_3, risen_2, passed_0, sums_0, sums_1)
-
-    risen_3 = around_z(risen_2)
-    passed_1 = return_corner(sums_1)
-    back_0 = return_sides(sums_0, passed_0)
-    sums_2 = apply((block_2,) + sides_2 + (risen_2,), (tokens,) * 4)
-    risen_3, passed_1, back_0, sums_0, sums_1, sums_2 = fence(
-        risen_3, passed_1, back_0, sums_0, sums_1, sums_2
-    )
-
-    back_1 = return_sides(sums_1, passed_1)
-    risen_sums = around_z(sums_2[3])
+    sums_1 = apply((block_1,) + sides_1 + corner_1 + (decodes_1,), (tokens,) * 4)
+    sides_3, risen, passed_0, sums_0, sums_1 = fence(sides_3, risen, passed_0, sums_0, sums_1)
+
+    decodes_3 = around_z(risen[tokens:])
+    decodes_3, far = fence(decodes_3, sums_1[3])
+    far = around_z(far)
+    corner_3 = spread_corner(sides_3)
+    back_1 = return_sides(sums_1)
+    sums_2 = apply((block_2,) + sides_2 + (risen,), (tokens,) * 4)
+    decodes_3, far, corner_3, back_1, sums_1, sums_2 = fence(
+        decodes_3, far, corner_3, back_1, sums_1, sums_2
+    )
+
+    far, first = join(sums_2[3], far, sums_1[0], *back_1)
+    far = around_z(far)
     back_2 = return_sides(sums_2)
-    layer_sum = added(hidden, sums_0[0], *back_0)
-    sums_3 = apply((block_3,) + sides_3 + (risen_3,), (tokens,) * 4)
-    back_1, risen_sums, sums_1, sums_2, sums_3 = fence(back_1, risen_sums, sums_1, sums_2, sums_3)
-
-    far = added(sums_3[3], risen_sums).astype(jnp.bfloat16)
+    carried = around_z(first)
+    sums_3 = apply((block_3,) + sides_3 + corner_3 + (decodes_3,), (tokens,) * 4)
+    far, sums_2, sums_3 = fence(far, sums_2, sums_3)
+
+    far = added(sums_3[3], far).astype(jnp.bfloat16)
     passed_3 = return_corner(tuple(sums_3[:3]) + (far[:cut], far[cut:]))
-    carried = around_z(added(sums_1[0], *back_1).astype(jnp.bfloat16))
     back_3 = return_sides(sums_3, passed_3)
     carried = around_z(added(sums_2[0], *back_2, carried).astype(jnp.bfloat16))
+    back_3, passed_0, sums_0 = fence(back_3, passed_0, sums_0)
     carried = around_z(added(sums_3[0], *back_3, carried).astype(jnp.bfloat16))
-    return added(layer_sum, carried).astype(jnp.bfloat16)[None]
+    back_0 = return_sides(sums_0, passed_0)
+    return added(hidden, sums_0[0], *back_0, carried).astype(jnp.bfloat16)[None]
 
 
 def chunk_cuts(tokens, devices):

time: 157 us -> 161 us (1.025)
  waiting for transfers between devices: 46.6 us -> 52.7 us
    ppermute x14, waiting for transfers between devices: 3.62 us -> 7.69 us  [along_y(): return lax.ppermute(value, 'kv', [(i, i ^ 2) for i in range(4)])]
    ppermute x9 -> x10, waiting for transfers between devices: 25.8 us -> 27.4 us  [around_z(): return lax.ppermute(value, 'blk', [(i, (i + 2) % 8) for i in range(8)])]
    ppermute x9 -> x10, starting transfers between devices: 13 us -> 13.3 us  [around_z(): return lax.ppermute(value, 'blk', [(i, (i + 2) % 8) for i in range(8)])]
  transfers between devices with their start and end apart: 40 -> 41, of which waited for: 10 -> 17; matrix products, arithmetic and copies ran while one was open for 5% -> 5% of each run, Pallas kernels for 31% -> 30%
where the time goes in v9:
time: 161 us; the launch traced here: 160 us
  waiting for transfers between devices  52.7 us (33%)
  Pallas kernels  50.1 us (31%)
  starting transfers between devices  42.1 us (26%)
  local copies, waits for them, and re-layouts  5.69 us (4%)
  matrix products  5.11 us (3%)
  other arithmetic  4.31 us (3%)
    pallas_call x4, Pallas kernels, run_plane(): pl.pallas_call(functools.partial(plane_kernel, cap, piece_rows, block_row...  47.8 us
    ppermute x10, waiting for transfers between devices, around_z(): return lax.ppermute(value, 'blk', [(i, (i + 2) % 8) for i in range(8)])  27.4 us
    ppermute x14, waiting for transfers between devices, along_x(): return lax.ppermute(value, 'kv', [(i, i ^ 1) for i in range(4)])  17.6 us
    ppermute x14, starting transfers between devices, along_y(): return lax.ppermute(value, 'kv', [(i, i ^ 2) for i in range(4)])  14.5 us
    ppermute x14, starting transfers between devices, along_x(): return lax.ppermute(value, 'kv', [(i, i ^ 1) for i in range(4)])  14.1 us
    ppermute x10, starting transfers between devices, around_z(): return lax.ppermute(value, 'blk', [(i, (i + 2) % 8) for i in range(8)])  13.3 us
    ppermute x14, waiting for transfers between devices, along_y(): return lax.ppermute(value, 'kv', [(i, i ^ 2) for i in range(4)])  7.69 us
    unnamed x24, local copies, waits for them, and re-layouts  5.36 us
  transfers between devices with their start and end apart: 41, of which 17 were waited for; matrix products, arithmetic and copies ran while one was open for 5% of the time, Pallas kernels for 30%

profile of v9, /device:TPU:0, one launch (start us, length us, event | category | flops | bytes accessed | tf_op | source)
XLA Modules:
  0.0 160.4 jit_solution(11810963271339231018)
XLA Ops:
  0.0 1.0 copy-done
  1.0 0.9 copy-done.2
  1.9 0.7 copy-done.4
  2.6 0.7 copy-done.6
  3.3 1.3 prepare.2.refs_1_
  4.6 3.1 %collective-permute-start.2 = (bf16[112,2176]{1,0:T(8,128)(2,1)S(1)}, bf16[112,2176]{1,0:T(8,128)(2,1)}, u32[]{:S(2)}, u32[]{:S(2)}) collective-permute-start(bf16[112,2176]{1,0:T(8,128)(2,1)S(1)} %prepare.2.refs_1_), channel_id=1, source_target_pairs={{0,2},{1,3},{2,4},{3,5},{4,6},{5,7},{6,0},{7,1},{8,10},{9,11},{10,... | collective-permute-start | bytes 1462280 | tf_op jit(solution)/shard_map/ppermute | solution.py:383
  7.7 1.5 collective-permute-start.1
  9.2 1.5 collective-permute-start
  10.8 0.7 broadcast_in_dim.76
  11.6 0.9 minimum_subtract_fusion
  12.5 3.7 %fusion.34 = (f32[4,8]{1,0:T(4,128)S(1)}, f32[4,8,4096]{2,1,0:T(8,128)S(1)}) fusion(bf16[4,4096,1,128]{3,1,2,0:T(8,128)(2,1)} %param.15, bf16[1,4,8,128]{3,1,2,0:T(4,128)(2,1)} %bitcast.53, pred[4,4096]{1,0:T(4,128)(4,1)S(1)} %iota_compare_fusion.1), kind=kOutput, calls=%fused_computation.58 | convolution fusion | flops 33947616 | bytes 4743296 | tf_op jit(solution)/shard_map/rgd,rjd->rgj/dot_general | solution.py:27
  16.6 0.7 fusion.10
  17.4 1.1 copy-done.10
  18.5 0.7 convolution_add_fusion
  19.2 0.6 collective-permute-start.6
  19.8 1.2 collective-permute-done.2.refs_1_
  21.0 0.6 collective-permute-done.refs_2_
  21.5 1.6 %collective-permute-start.5 = (bf16[48,2176]{1,0:T(8,128)(2,1)S(1)}, bf16[48,2176]{1,0:T(8,128)(2,1)S(1)}, u32[]{:S(2)}, u32[]{:S(2)}) collective-permute-start(bf16[48,2176]{1,0:T(8,128)(2,1)S(1)} %slice.44), channel_id=1, source_target_pairs={{0,8},{8,0},{16,24},{24,16},{1,9},{9,1},{17,25},{25,17},{2,10},{10... | collective-permute-start | bytes 626696 | tf_op jit(solution)/shard_map/ppermute | solution.py:375
  23.2 0.9 collective-permute-start.4
  24.2 4.0 %collective-permute-done.5.refs_5_ = bf16[48,2176]{1,0:T(8,128)(2,1)S(1)} collective-permute-done((bf16[48,2176]{1,0:T(8,128)(2,1)S(1)}, bf16[48,2176]{1,0:T(8,128)(2,1)S(1)}, u32[]{:S(2)}, u32[]{:S(2)}) %collective-permute-start.5) | collective-permute-done | bytes 208928 | tf_op jit(solution)/shard_map/ppermute | solution.py:375
  28.2 1.8 %collective-permute-done.4.refs_4_ = bf16[64,2176]{1,0:T(8,128)(2,1)S(1)} collective-permute-done((bf16[64,2176]{1,0:T(8,128)(2,1)S(1)}, bf16[64,2176]{1,0:T(8,128)(2,1)S(1)}, u32[]{:S(2)}, u32[]{:S(2)}) %collective-permute-start.4) | collective-permute-done | bytes 278560 | tf_op jit(solution)/shard_map/ppermute | solution.py:379
  30.0 1.5 collective-permute-start.7
  31.5 2.7 %collective-permute-done.7 = f32[8,2048]{1,0:T(8,128)S(1)} collective-permute-done((f32[8,2048]{1,0:T(8,128)S(1)}, f32[8,2048]{1,0:T(8,128)S(1)}, u32[]{:S(2)}, u32[]{:S(2)}) %collective-permute-start.7) | collective-permute-done | bytes 65568 | tf_op jit(solution)/shard_map/ppermute | solution.py:379
  34.4 1.7 %collective-permute-start.10 = (bf16[112,2176]{1,0:T(8,128)(2,1)}, bf16[112,2176]{1,0:T(8,128)(2,1)S(1)}, u32[]{:S(2)}, u32[]{:S(2)}) collective-permute-start(bf16[112,2176]{1,0:T(8,128)(2,1)} %collective-permute-done.2.refs_1_), channel_id=1, source_target_pairs={{0,2},{1,3},{2,4},{3,5},{4,6},{5,7},{6,0},{7,1},{8,10},{9,11},{10,... | collective-permute-start | bytes 1462280 | tf_op jit(solution)/shard_map/ppermute | solution.py:383
  37.8 12.1 %collective-permute-done.10.refs_1_ = bf16[112,2176]{1,0:T(8,128)(2,1)S(1)} collective-permute-done((bf16[112,2176]{1,0:T(8,128)(2,1)}, bf16[112,2176]{1,0:T(8,128)(2,1)S(1)}, u32[]{:S(2)}, u32[]{:S(2)}) %collective-permute-start.10) | collective-permute-done | bytes 487456 | tf_op jit(solution)/shard_map/ppermute | solution.py:383
  50.0 1.6 collective-permute-start.16
  51.5 0.5 collective-permute-start.15
  52.1 1.6 collective-permute-start.14
  53.7 0.6 collective-permute-start.13
  54.3 1.4 collective-permute-start.17
  55.7 0.9 copy-done.8
  56.7 12.1 %plane.4 = (bf16[112,2048]{1,0:T(8,128)(2,1)S(1)}, bf16[112,2048]{1,0:T(8,128)(2,1)S(1)}, bf16[112,2048]{1,0:T(8,128)(2,1)S(1)}, bf16[64,2048]{1,0:T(8,128)(2,1)S(1)}, bf16[48,2048]{1,0:T(8,128)(2,1)S(1)}) custom-call(s32[3]{0:T(128)S(1)} %pad_add_fusion.refs_0_, bf16[112,2176]{1,0:T(8,128)(2,1)S(1)} %prepare.2.refs_1_, ...), custom_call_target="tpu_custom_call" | custom-call | flops 8455716864 | bytes 25165824 | tf_op jit(solution)/shard_map/plane/pallas_call | solution.py:313
  69.3 1.6 collective-permute-start.19
  70.8 0.5 collective-permute-start.18
  71.4 1.5 collective-permute-start.22
  72.9 0.5 collective-permute-start.21
  73.4 0.6 collective-permute-start.20
  74.0 11.7 %plane.5 = (bf16[112,2048]{1,0:T(8,128)(2,1)S(1)}, bf16[112,2048]{1,0:T(8,128)(2,1)S(1)}, bf16[112,2048]{1,0:T(8,128)(2,1)S(1)}, bf16[112,2048]{1,0:T(8,128)(2,1)S(1)}) custom-call(s32[3]{0:T(128)S(1)} %pad_add_fusion.refs_0_, bf16[112,2176]{1,0:T(8,128)(2,1)} %collective-permute-done.2.refs_1_, bf16[112,2176]{1,0:T(8,128)(2,1)S(1)} %collective-permute-done.8.refs_2_, ...), custom_call_target="tpu_custom_call" | custom-call | flops 8455716864 | bytes 25165824 | tf_op jit(solution)/shard_map/plane/pallas_call | solution.py:313
  86.3 0.9 collective-permute-done.20.refs_4_
  87.1 0.6 collective-permute-start.23
  87.8 0.6 collective-permute-start.26
  88.4 1.0 collective-permute-start.25
  89.4 1.5 collective-permute-start.27
  90.9 1.1 collective-permute-start.28
  92.0 1.6 collective-permute-done.23.refs_6_
  93.5 12.0 %plane.6 = (bf16[112,2048]{1,0:T(8,128)(2,1)S(1)}, bf16[112,2048]{1,0:T(8,128)(2,1)S(1)}, bf16[112,2048]{1,0:T(8,128)(2,1)S(1)}, bf16[112,2048]{1,0:T(8,128)(2,1)S(1)}) custom-call(s32[3]{0:T(128)S(1)} %pad_add_fusion.refs_0_, bf16[112,2176]{1,0:T(8,128)(2,1)S(1)} %collective-permute-done.10.refs_1_, bf16[112,2176]{1,0:T(8,128)(2,1)S(1)} %collective-permute-done.15.refs_2_, ...), custom_call_target="tpu_custom_call" | custom-call | flops 8455716864 | bytes 25165824 | tf_op jit(solution)/shard_map/plane/pallas_call | solution.py:313
  105.9 1.2 collective-permute-start.29
  107.1 1.6 %collective-permute-start.38 = (bf16[112,2048]{1,0:T(8,128)(2,1)S(1)}, bf16[112,2048]{1,0:T(8,128)(2,1)S(1)}, u32[]{:S(2)}, u32[]{:S(2)}) collective-permute-start(bf16[112,2048]{1,0:T(8,128)(2,1)S(1)} %get-tuple-element.186), channel_id=1, source_target_pairs={{0,2},{1,3},{2,4},{3,5},{4,6},{5,7},{6,0},{7,1},{8,10},{9,11},{10,... | collective-permute-start | bytes 1376264 | tf_op jit(solution)/shard_map/ppermute | solution.py:383
  108.7 0.8 collective-permute-start.36
  109.5 1.3 collective-permute-start.37
  110.8 12.0 %plane.7 = (bf16[112,2048]{1,0:T(8,128)(2,1)S(1)}, bf16[112,2048]{1,0:T(8,128)(2,1)S(1)}, bf16[112,2048]{1,0:T(8,128)(2,1)S(1)}, bf16[112,2048]{1,0:T(8,128)(2,1)S(1)}) custom-call(s32[3]{0:T(128)S(1)} %pad_add_fusion.refs_0_, bf16[112,2176]{1,0:T(8,128)(2,1)S(1)} %slice.50.refs_1_, bf16[112,2176]{1,0:T(8,128)(2,1)S(1)} %collective-permute-done.18.refs_2_, ...), custom_call_target="tpu_custom_call" | custom-call | flops 8455716864 | bytes 25165824 | tf_op jit(solution)/shard_map/plane/pallas_call | solution.py:313
  122.9 0.8 collective-permute-start.30
  123.8 1.3 collective-permute-start.31
  125.1 6.6 %collective-permute-done.31.passed_1_ref = bf16[48,2048]{1,0:T(8,128)(2,1)S(1)} collective-permute-done((bf16[48,2048]{1,0:T(8,128)(2,1)S(1)}, bf16[48,2048]{1,0:T(8,128)(2,1)S(1)}, u32[]{:S(2)}, u32[]{:S(2)}) %collective-permute-start.31) | collective-permute-done | bytes 196640 | tf_op jit(solution)/shard_map/ppermute | solution.py:375
  132.3 1.6 collective-permute-start.32
  133.9 0.7 collective-permute-start.33
  135.0 2.1 %collective-permute-start.39 = (bf16[112,2048]{1,0:T(8,128)(2,1)S(1)}, bf16[112,2048]{1,0:T(8,128)(2,1)S(1)}, u32[]{:S(2)}, u32[]{:S(2)}) collective-permute-start(bf16[112,2048]{1,0:T(8,128)(2,1)S(1)} %add_convert_fusion.2), channel_id=1, source_target_pairs={{0,2},{1,3},{2,4},{3,5},{4,6},{5,7},{6,0},{7,1},{8,10},{9,11},{10,... | collective-permute-start | bytes 1376264 | tf_op jit(solution)/shard_map/ppermute | solution.py:383
  137.1 6.1 %collective-permute-done.32 = bf16[112,2048]{1,0:T(8,128)(2,1)S(1)} collective-permute-done((bf16[112,2048]{1,0:T(8,128)(2,1)S(1)}, bf16[112,2048]{1,0:T(8,128)(2,1)S(1)}, u32[]{:S(2)}, u32[]{:S(2)}) %collective-permute-start.32) | collective-permute-done | bytes 458784 | tf_op jit(solution)/shard_map/ppermute | solution.py:375
  143.2 2.5 %collective-permute-done.33 = bf16[112,2048]{1,0:T(8,128)(2,1)S(1)} collective-permute-done((bf16[112,2048]{1,0:T(8,128)(2,1)S(1)}, bf16[112,2048]{1,0:T(8,128)(2,1)S(1)}, u32[]{:S(2)}, u32[]{:S(2)}) %collective-permute-start.33) | collective-permute-done | bytes 458784 | tf_op jit(solution)/shard_map/ppermute | solution.py:379
  145.7 2.9 %collective-permute-done.39 = bf16[112,2048]{1,0:T(8,128)(2,1)S(1)} collective-permute-done((bf16[112,2048]{1,0:T(8,128)(2,1)S(1)}, bf16[112,2048]{1,0:T(8,128)(2,1)S(1)}, u32[]{:S(2)}, u32[]{:S(2)}) %collective-permute-start.39) | collective-permute-done | bytes 458784 | tf_op jit(solution)/shard_map/ppermute | solution.py:383
  148.9 1.0 collective-permute-start.40
  150.0 0.9 collective-permute-start.35
  150.9 8.3 %collective-permute-done.40 = bf16[112,2048]{1,0:T(8,128)(2,1)S(1)} collective-permute-done((bf16[112,2048]{1,0:T(8,128)(2,1)S(1)}, bf16[112,2048]{1,0:T(8,128)(2,1)S(1)}, u32[]{:S(2)}, u32[]{:S(2)}) %collective-permute-start.40) | collective-permute-done | bytes 458784 | tf_op jit(solution)/shard_map/ppermute | solution.py:383
  159.2 1.2 fusion.13
  (91 shorter events, 5.6 us)
Async XLA Ops:
  0.0 16.3 %copy-start.11 = (f32[8]{0:T(128)S(1)}, f32[8]{0:T(128)}, u32[]{:S(2)}) copy-start(f32[8]{0:T(128)} %param.18) | copy-start | bytes 100
  0.0 1.0 copy-start
  1.0 0.9 copy-start.2
  1.9 0.7 copy-start.4
  2.6 0.7 copy-start.6
  4.6 16.3 %collective-permute-start.2 = (bf16[112,2176]{1,0:T(8,128)(2,1)S(1)}, bf16[112,2176]{1,0:T(8,128)(2,1)}, u32[]{:S(2)}, u32[]{:S(2)}) collective-permute-start(bf16[112,2176]{1,0:T(8,128)(2,1)S(1)} %prepare.2.refs_1_), channel_id=1, source_target_pairs={{0,2},{1,3},{2,4},{3,5},{4,6},{5,7},{6,0},{7,1},{8,10},{9,11},{10,... | collective-permute-start | bytes 1462280 | tf_op jit(solution)/shard_map/ppermute | solution.py:383
  7.7 13.3 %collective-permute-start.1 = (bf16[112,2176]{1,0:T(8,128)(2,1)S(1)}, bf16[112,2176]{1,0:T(8,128)(2,1)S(1)}, u32[]{:S(2)}, u32[]{:S(2)}) collective-permute-start(bf16[112,2176]{1,0:T(8,128)(2,1)S(1)} %prepare.2.refs_1_), channel_id=1, source_target_pairs={{0,16},{8,24},{16,0},{24,8},{1,17},{9,25},{17,1},{25,9},{2,18},{10... | collective-permute-start | bytes 1462280 | tf_op jit(solution)/shard_map/ppermute | solution.py:379
  9.2 12.3 %collective-permute-start = (bf16[112,2176]{1,0:T(8,128)(2,1)S(1)}, bf16[112,2176]{1,0:T(8,128)(2,1)S(1)}, u32[]{:S(2)}, u32[]{:S(2)}) collective-permute-start(bf16[112,2176]{1,0:T(8,128)(2,1)S(1)} %prepare.2.refs_1_), channel_id=1, source_target_pairs={{0,8},{8,0},{16,24},{24,16},{1,9},{9,1},{17,25},{25,17},{2,10},{10... | collective-permute-start | bytes 1462280 | tf_op jit(solution)/shard_map/ppermute | solution.py:375
  10.7 10.8 %collective-permute-start.3 = (bf16[2048,768]{1,0:T(8,128)(2,1)}, bf16[2048,768]{1,0:T(8,128)(2,1)}, u32[]{:S(2)}, u32[]{:S(2)}) collective-permute-start(bf16[2048,768]{1,0:T(8,128)(2,1)} %bitcast.55), channel_id=1, source_target_pairs={{0,1},{1,0},{2,3},{3,2},{4,5},{5,4},{6,7},{7,6},{8,9},{9,8},{10,11... | collective-permute-start | bytes 9437192 | tf_op jit(solution)/shard_map/ppermute | solution.py:387
  11.5 5.0 %copy-start.9 = (bf16[4,4096,1,128]{3,1,2,0:T(8,128)(2,1)S(1)}, bf16[4,4096,1,128]{3,1,2,0:T(8,128)(2,1)}, u32[]{:S(2)}) copy-start(bf16[4,4096,1,128]{3,1,2,0:T(8,128)(2,1)} %param.16) | copy-start | bytes 12582916
  16.3 2.2 %copy-start.10 = (bf16[1024,2048]{1,0:T(8,128)(2,1)S(1)}, bf16[1024,2048]{1,0:T(8,128)(2,1)}, u32[]{:S(2)}) copy-start(bf16[1024,2048]{1,0:T(8,128)(2,1)} %param.19) | copy-start | bytes 12582916
  17.3 20.1 %copy-start.3 = (bf16[2048,32]{0,1:T(8,128)(2,1)S(1)}, bf16[2048,32]{0,1:T(8,128)(2,1)}, u32[]{:S(2)}) copy-start(bf16[2048,32]{0,1:T(8,128)(2,1)} %param.23) | copy-start | bytes 393220
  17.3 20.1 %copy-start.5 = (f32[2048]{0:T(1024)S(1)}, f32[2048]{0:T(1024)}, u32[]{:S(2)}) copy-start(f32[2048]{0:T(1024)} %param.22) | copy-start | bytes 24580
  19.2 5.0 %collective-permute-start.6 = (f32[8,2048]{1,0:T(8,128)S(1)}, f32[8,2048]{1,0:T(8,128)S(1)}, u32[]{:S(2)}, u32[]{:S(2)}) collective-permute-start(f32[8,2048]{1,0:T(8,128)S(1)} %pad_maximum_fusion.2), channel_id=1, source_target_pairs={{0,8},{8,0},{16,24},{24,16},{1,9},{9,1},{17,25},{25,17},{2,10},{10... | collective-permute-start | bytes 196616 | tf_op jit(solution)/shard_map/ppermute | solution.py:375
  21.5 6.7 %collective-permute-start.5 = (bf16[48,2176]{1,0:T(8,128)(2,1)S(1)}, bf16[48,2176]{1,0:T(8,128)(2,1)S(1)}, u32[]{:S(2)}, u32[]{:S(2)}) collective-permute-start(bf16[48,2176]{1,0:T(8,128)(2,1)S(1)} %slice.44), channel_id=1, source_target_pairs={{0,8},{8,0},{16,24},{24,16},{1,9},{9,1},{17,25},{25,17},{2,10},{10... | collective-permute-start | bytes 626696 | tf_op jit(solution)/shard_map/ppermute | solution.py:375
  23.2 6.7 %collective-permute-start.4 = (bf16[64,2176]{1,0:T(8,128)(2,1)S(1)}, bf16[64,2176]{1,0:T(8,128)(2,1)S(1)}, u32[]{:S(2)}, u32[]{:S(2)}) collective-permute-start(bf16[64,2176]{1,0:T(8,128)(2,1)S(1)} %slice.43), channel_id=1, source_target_pairs={{0,16},{8,24},{16,0},{24,8},{1,17},{9,25},{17,1},{25,9},{2,18},{10... | collective-permute-start | bytes 835592 | tf_op jit(solution)/shard_map/ppermute | solution.py:379
  28.2 6.2 %copy-start.7 = (bf16[48,2176]{1,0:T(8,128)(2,1)}, bf16[48,2176]{1,0:T(8,128)(2,1)S(1)}, u32[]{:S(2)}) copy-start(bf16[48,2176]{1,0:T(8,128)(2,1)S(1)} %collective-permute-done.5.refs_5_) | copy-start | bytes 626692
  30.0 4.3 %collective-permute-start.7 = (f32[8,2048]{1,0:T(8,128)S(1)}, f32[8,2048]{1,0:T(8,128)S(1)}, u32[]{:S(2)}, u32[]{:S(2)}) collective-permute-start(f32[8,2048]{1,0:T(8,128)S(1)} %fusion.33), channel_id=1, source_target_pairs={{0,16},{8,24},{16,0},{24,8},{1,17},{9,25},{17,1},{25,9},{2,18},{10... | collective-permute-start | bytes 196616 | tf_op jit(solution)/shard_map/ppermute | solution.py:379
  31.5 6.4 %collective-permute-start.11 = (bf16[2048,768]{1,0:T(8,128)(2,1)}, bf16[2048,768]{1,0:T(8,128)(2,1)}, u32[]{:S(2)}, u32[]{:S(2)}) collective-permute-start(bf16[2048,768]{1,0:T(8,128)(2,1)} %bitcast.11.refs_8_.refs_6_), channel_id=1, source_target_pairs={{0,1},{1,0},{2,3},{3,2},{4,5},{5,4},{6,7},{7,6},{8,9},{9,8},{10,11... | collective-permute-start | bytes 9437192 | tf_op jit(solution)/shard_map/ppermute | solution.py:387
  34.2 15.7 %collective-permute-start.12 = (bf16[768,2048]{1,0:T(8,128)(2,1)}, bf16[768,2048]{1,0:T(8,128)(2,1)}, u32[]{:S(2)}, u32[]{:S(2)}) collective-permute-start(bf16[768,2048]{1,0:T(8,128)(2,1)} %bitcast.12.refs_9_.refs_7_), channel_id=1, source_target_pairs={{0,1},{1,0},{2,3},{3,2},{4,5},{5,4},{6,7},{7,6},{8,9},{9,8},{10,11... | collective-permute-start | bytes 9437192 | tf_op jit(solution)/shard_map/ppermute | solution.py:387
  34.4 15.5 %collective-permute-start.10 = (bf16[112,2176]{1,0:T(8,128)(2,1)}, bf16[112,2176]{1,0:T(8,128)(2,1)S(1)}, u32[]{:S(2)}, u32[]{:S(2)}) collective-permute-start(bf16[112,2176]{1,0:T(8,128)(2,1)} %collective-permute-done.2.refs_1_), channel_id=1, source_target_pairs={{0,2},{1,3},{2,4},{3,5},{4,6},{5,7},{6,0},{7,1},{8,10},{9,11},{10,... | collective-permute-start | bytes 1462280 | tf_op jit(solution)/shard_map/ppermute | solution.py:383
  36.2 13.8 %collective-permute-start.9 = (bf16[112,2176]{1,0:T(8,128)(2,1)}, bf16[112,2176]{1,0:T(8,128)(2,1)S(1)}, u32[]{:S(2)}, u32[]{:S(2)}) collective-permute-start(bf16[112,2176]{1,0:T(8,128)(2,1)} %collective-permute-done.2.refs_1_), channel_id=1, source_target_pairs={{0,16},{8,24},{16,0},{24,8},{1,17},{9,25},{17,1},{25,9},{2,18},{10... | collective-permute-start | bytes 1462280 | tf_op jit(solution)/shard_map/ppermute | solution.py:379
  36.7 13.3 %collective-permute-start.8 = (bf16[112,2176]{1,0:T(8,128)(2,1)}, bf16[112,2176]{1,0:T(8,128)(2,1)S(1)}, u32[]{:S(2)}, u32[]{:S(2)}) collective-permute-start(bf16[112,2176]{1,0:T(8,128)(2,1)} %collective-permute-done.2.refs_1_), channel_id=1, source_target_pairs={{0,8},{8,0},{16,24},{24,16},{1,9},{9,1},{17,25},{25,17},{2,10},{10... | collective-permute-start | bytes 1462280 | tf_op jit(solution)/shard_map/ppermute | solution.py:375
  50.0 18.8 %collective-permute-start.16 = (bf16[112,2176]{1,0:T(8,128)(2,1)S(1)}, bf16[112,2176]{1,0:T(8,128)(2,1)S(1)}, u32[]{:S(2)}, u32[]{:S(2)}) collective-permute-start(bf16[112,2176]{1,0:T(8,128)(2,1)S(1)} %collective-permute-done.10.refs_1_), channel_id=1, source_target_pairs={{0,16},{8,24},{16,0},{24,8},{1,17},{9,25},{17,1},{25,9},{2,18},{10... | collective-permute-start | bytes 1462280 | tf_op jit(solution)/shard_map/ppermute | solution.py:379
  51.5 17.2 %collective-permute-start.15 = (bf16[112,2176]{1,0:T(8,128)(2,1)S(1)}, bf16[112,2176]{1,0:T(8,128)(2,1)S(1)}, u32[]{:S(2)}, u32[]{:S(2)}) collective-permute-start(bf16[112,2176]{1,0:T(8,128)(2,1)S(1)} %collective-permute-done.10.refs_1_), channel_id=1, source_target_pairs={{0,8},{8,0},{16,24},{24,16},{1,9},{9,1},{17,25},{25,17},{2,10},{10... | collective-permute-start | bytes 1462280 | tf_op jit(solution)/shard_map/ppermute | solution.py:375
  52.1 16.7 %collective-permute-start.14 = (bf16[48,2176]{1,0:T(8,128)(2,1)S(1)}, bf16[48,2176]{1,0:T(8,128)(2,1)S(1)}, u32[]{:S(2)}, u32[]{:S(2)}) collective-permute-start(bf16[48,2176]{1,0:T(8,128)(2,1)S(1)} %slice.49), channel_id=1, source_target_pairs={{0,8},{8,0},{16,24},{24,16},{1,9},{9,1},{17,25},{25,17},{2,10},{10... | collective-permute-start | bytes 626696 | tf_op jit(solution)/shard_map/ppermute | solution.py:375
  53.7 15.1 %collective-permute-start.13 = (bf16[64,2176]{1,0:T(8,128)(2,1)S(1)}, bf16[64,2176]{1,0:T(8,128)(2,1)S(1)}, u32[]{:S(2)}, u32[]{:S(2)}) collective-permute-start(bf16[64,2176]{1,0:T(8,128)(2,1)S(1)} %slice.48), channel_id=1, source_target_pairs={{0,16},{8,24},{16,0},{24,8},{1,17},{9,25},{17,1},{25,9},{2,18},{10... | collective-permute-start | bytes 835592 | tf_op jit(solution)/shard_map/ppermute | solution.py:379
  54.3 14.9 %collective-permute-start.17 = (bf16[128,2176]{1,0:T(8,128)(2,1)S(1)}, bf16[128,2176]{1,0:T(8,128)(2,1)S(1)}, u32[]{:S(2)}, u32[]{:S(2)}) collective-permute-start(bf16[128,2176]{1,0:T(8,128)(2,1)S(1)} %pad_maximum_fusion), channel_id=1, source_target_pairs={{0,2},{1,3},{2,4},{3,5},{4,6},{5,7},{6,0},{7,1},{8,10},{9,11},{10,... | collective-permute-start | bytes 1671176 | tf_op jit(solution)/shard_map/ppermute | solution.py:383
  55.7 0.9 copy-start.8
  69.3 17.0 %collective-permute-start.19 = (bf16[112,2176]{1,0:T(8,128)(2,1)S(1)}, bf16[112,2176]{1,0:T(8,128)(2,1)S(1)}, u32[]{:S(2)}, u32[]{:S(2)}) collective-permute-start(bf16[112,2176]{1,0:T(8,128)(2,1)S(1)} %slice.50.refs_1_), channel_id=1, source_target_pairs={{0,16},{8,24},{16,0},{24,8},{1,17},{9,25},{17,1},{25,9},{2,18},{10... | collective-permute-start | bytes 1462280 | tf_op jit(solution)/shard_map/ppermute | solution.py:379
  70.8 15.4 %collective-permute-start.18 = (bf16[112,2176]{1,0:T(8,128)(2,1)S(1)}, bf16[112,2176]{1,0:T(8,128)(2,1)S(1)}, u32[]{:S(2)}, u32[]{:S(2)}) collective-permute-start(bf16[112,2176]{1,0:T(8,128)(2,1)S(1)} %slice.50.refs_1_), channel_id=1, source_target_pairs={{0,8},{8,0},{16,24},{24,16},{1,9},{9,1},{17,25},{25,17},{2,10},{10... | collective-permute-start | bytes 1462280 | tf_op jit(solution)/shard_map/ppermute | solution.py:375
  71.4 14.7 %collective-permute-start.22 = (bf16[48,2048]{1,0:T(8,128)(2,1)S(1)}, bf16[48,2048]{1,0:T(8,128)(2,1)S(1)}, u32[]{:S(2)}, u32[]{:S(2)}) collective-permute-start(bf16[48,2048]{1,0:T(8,128)(2,1)S(1)} %get-tuple-element.125), channel_id=1, source_target_pairs={{0,8},{8,0},{16,24},{24,16},{1,9},{9,1},{17,25},{25,17},{2,10},{10... | collective-permute-start | bytes 589832 | tf_op jit(solution)/shard_map/ppermute | solution.py:375
  72.9 13.4 %collective-permute-start.21 = (bf16[64,2048]{1,0:T(8,128)(2,1)S(1)}, bf16[64,2048]{1,0:T(8,128)(2,1)S(1)}, u32[]{:S(2)}, u32[]{:S(2)}) collective-permute-start(bf16[64,2048]{1,0:T(8,128)(2,1)S(1)} %get-tuple-element.124), channel_id=1, source_target_pairs={{0,16},{8,24},{16,0},{24,8},{1,17},{9,25},{17,1},{25,9},{2,18},{10... | collective-permute-start | bytes 786440 | tf_op jit(solution)/shard_map/ppermute | solution.py:379
  73.4 13.7 %collective-permute-start.20 = (bf16[128,2176]{1,0:T(8,128)(2,1)S(1)}, bf16[128,2176]{1,0:T(8,128)(2,1)S(1)}, u32[]{:S(2)}, u32[]{:S(2)}) collective-permute-start(bf16[128,2176]{1,0:T(8,128)(2,1)S(1)} %pad_maximum_fusion.1), channel_id=1, source_target_pairs={{0,2},{1,3},{2,4},{3,5},{4,6},{5,7},{6,0},{7,1},{8,10},{9,11},{10,... | collective-permute-start | bytes 1671176 | tf_op jit(solution)/shard_map/ppermute | solution.py:383
  87.1 6.4 %collective-permute-start.23 = (bf16[16,2176]{1,0:T(8,128)(2,1)S(1)}, bf16[16,2176]{1,0:T(8,128)(2,1)S(1)}, u32[]{:S(2)}, u32[]{:S(2)}) collective-permute-start(bf16[16,2176]{1,0:T(8,128)(2,1)S(1)} %slice.52), channel_id=1, source_target_pairs={{0,2},{1,3},{2,4},{3,5},{4,6},{5,7},{6,0},{7,1},{8,10},{9,11},{10,... | collective-permute-start | bytes 208904 | tf_op jit(solution)/shard_map/ppermute | solution.py:383
  87.8 17.8 %collective-permute-start.26 = (bf16[48,2176]{1,0:T(8,128)(2,1)S(1)}, bf16[48,2176]{1,0:T(8,128)(2,1)S(1)}, u32[]{:S(2)}, u32[]{:S(2)}) collective-permute-start(bf16[48,2176]{1,0:T(8,128)(2,1)S(1)} %slice.54), channel_id=1, source_target_pairs={{0,8},{8,0},{16,24},{24,16},{1,9},{9,1},{17,25},{25,17},{2,10},{10... | collective-permute-start | bytes 626696 | tf_op jit(solution)/shard_map/ppermute | solution.py:375
  88.4 17.2 %collective-permute-start.25 = (bf16[64,2176]{1,0:T(8,128)(2,1)S(1)}, bf16[64,2176]{1,0:T(8,128)(2,1)S(1)}, u32[]{:S(2)}, u32[]{:S(2)}) collective-permute-start(bf16[64,2176]{1,0:T(8,128)(2,1)S(1)} %slice.53), channel_id=1, source_target_pairs={{0,16},{8,24},{16,0},{24,8},{1,17},{9,25},{17,1},{25,9},{2,18},{10... | collective-permute-start | bytes 835592 | tf_op jit(solution)/shard_map/ppermute | solution.py:379
  89.4 16.2 %collective-permute-start.27 = (bf16[112,2048]{1,0:T(8,128)(2,1)S(1)}, bf16[112,2048]{1,0:T(8,128)(2,1)S(1)}, u32[]{:S(2)}, u32[]{:S(2)}) collective-permute-start(bf16[112,2048]{1,0:T(8,128)(2,1)S(1)} %get-tuple-element.139), channel_id=1, source_target_pairs={{0,8},{8,0},{16,24},{24,16},{1,9},{9,1},{17,25},{25,17},{2,10},{10... | collective-permute-start | bytes 1376264 | tf_op jit(solution)/shard_map/ppermute | solution.py:375
  90.9 14.7 %collective-permute-start.28 = (bf16[112,2048]{1,0:T(8,128)(2,1)S(1)}, bf16[112,2048]{1,0:T(8,128)(2,1)S(1)}, u32[]{:S(2)}, u32[]{:S(2)}) collective-permute-start(bf16[112,2048]{1,0:T(8,128)(2,1)S(1)} %get-tuple-element.140), channel_id=1, source_target_pairs={{0,16},{8,24},{16,0},{24,8},{1,17},{9,25},{17,1},{25,9},{2,18},{10... | collective-permute-start | bytes 1376264 | tf_op jit(solution)/shard_map/ppermute | solution.py:379
  93.5 12.1 %collective-permute-start.24 = (bf16[112,2048]{1,0:T(8,128)(2,1)S(1)}, bf16[112,2048]{1,0:T(8,128)(2,1)S(1)}, u32[]{:S(2)}, u32[]{:S(2)}) collective-permute-start(bf16[112,2048]{1,0:T(8,128)(2,1)S(1)} %get-tuple-element.136), channel_id=1, source_target_pairs={{0,2},{1,3},{2,4},{3,5},{4,6},{5,7},{6,0},{7,1},{8,10},{9,11},{10,... | collective-permute-start | bytes 1376264 | tf_op jit(solution)/shard_map/ppermute | solution.py:383
  105.9 16.9 %collective-permute-start.29 = (bf16[112,2048]{1,0:T(8,128)(2,1)S(1)}, bf16[112,2048]{1,0:T(8,128)(2,1)S(1)}, u32[]{:S(2)}, u32[]{:S(2)}) collective-permute-start(bf16[112,2048]{1,0:T(8,128)(2,1)S(1)} %get-tuple-element.153), channel_id=1, source_target_pairs={{0,2},{1,3},{2,4},{3,5},{4,6},{5,7},{6,0},{7,1},{8,10},{9,11},{10,... | collective-permute-start | bytes 1376264 | tf_op jit(solution)/shard_map/ppermute | solution.py:383
  107.1 27.6 %collective-permute-start.38 = (bf16[112,2048]{1,0:T(8,128)(2,1)S(1)}, bf16[112,2048]{1,0:T(8,128)(2,1)S(1)}, u32[]{:S(2)}, u32[]{:S(2)}) collective-permute-start(bf16[112,2048]{1,0:T(8,128)(2,1)S(1)} %get-tuple-element.186), channel_id=1, source_target_pairs={{0,2},{1,3},{2,4},{3,5},{4,6},{5,7},{6,0},{7,1},{8,10},{9,11},{10,... | collective-permute-start | bytes 1376264 | tf_op jit(solution)/shard_map/ppermute | solution.py:383
  108.7 26.0 %collective-permute-start.36 = (bf16[112,2048]{1,0:T(8,128)(2,1)S(1)}, bf16[112,2048]{1,0:T(8,128)(2,1)S(1)}, u32[]{:S(2)}, u32[]{:S(2)}) collective-permute-start(bf16[112,2048]{1,0:T(8,128)(2,1)S(1)} %get-tuple-element.155), channel_id=1, source_target_pairs={{0,8},{8,0},{16,24},{24,16},{1,9},{9,1},{17,25},{25,17},{2,10},{10... | collective-permute-start | bytes 1376264 | tf_op jit(solution)/shard_map/ppermute | solution.py:375
  109.5 25.2 %collective-permute-start.37 = (bf16[112,2048]{1,0:T(8,128)(2,1)S(1)}, bf16[112,2048]{1,0:T(8,128)(2,1)S(1)}, u32[]{:S(2)}, u32[]{:S(2)}) collective-permute-start(bf16[112,2048]{1,0:T(8,128)(2,1)S(1)} %get-tuple-element.156), channel_id=1, source_target_pairs={{0,16},{8,24},{16,0},{24,8},{1,17},{9,25},{17,1},{25,9},{2,18},{10... | collective-permute-start | bytes 1376264 | tf_op jit(solution)/shard_map/ppermute | solution.py:379
  122.9 9.2 %collective-permute-start.30 = (bf16[64,2048]{1,0:T(8,128)(2,1)S(1)}, bf16[64,2048]{1,0:T(8,128)(2,1)S(1)}, u32[]{:S(2)}, u32[]{:S(2)}) collective-permute-start(bf16[64,2048]{1,0:T(8,128)(2,1)S(1)} %slice.57), channel_id=1, source_target_pairs={{0,16},{8,24},{16,0},{24,8},{1,17},{9,25},{17,1},{25,9},{2,18},{10... | collective-permute-start | bytes 786440 | tf_op jit(solution)/shard_map/ppermute | solution.py:379
  123.8 7.9 %collective-permute-start.31 = (bf16[48,2048]{1,0:T(8,128)(2,1)S(1)}, bf16[48,2048]{1,0:T(8,128)(2,1)S(1)}, u32[]{:S(2)}, u32[]{:S(2)}) collective-permute-start(bf16[48,2048]{1,0:T(8,128)(2,1)S(1)} %slice.58), channel_id=1, source_target_pairs={{0,8},{8,0},{16,24},{24,16},{1,9},{9,1},{17,25},{25,17},{2,10},{10... | collective-permute-start | bytes 589832 | tf_op jit(solution)/shard_map/ppermute | solution.py:375
  132.3 26.9 %copy-start.1 = (bf16[1,111,2048]{2,1,0:T(8,128)(2,1)S(1)}, bf16[1,111,2048]{2,1,0:T(8,128)(2,1)}, u32[]{:S(2)}) copy-start(bf16[1,111,2048]{2,1,0:T(8,128)(2,1)} %param.21) | copy-start | bytes 1363972
  132.3 10.8 %collective-permute-start.32 = (bf16[112,2048]{1,0:T(8,128)(2,1)S(1)}, bf16[112,2048]{1,0:T(8,128)(2,1)S(1)}, u32[]{:S(2)}, u32[]{:S(2)}) collective-permute-start(bf16[112,2048]{1,0:T(8,128)(2,1)S(1)} %get-tuple-element.168), channel_id=1, source_target_pairs={{0,8},{8,0},{16,24},{24,16},{1,9},{9,1},{17,25},{25,17},{2,10},{10... | collective-permute-start | bytes 1376264 | tf_op jit(solution)/shard_map/ppermute | solution.py:375
  133.9 11.7 %collective-permute-start.33 = (bf16[112,2048]{1,0:T(8,128)(2,1)S(1)}, bf16[112,2048]{1,0:T(8,128)(2,1)S(1)}, u32[]{:S(2)}, u32[]{:S(2)}) collective-permute-start(bf16[112,2048]{1,0:T(8,128)(2,1)S(1)} %get-tuple-element.169), channel_id=1, source_target_pairs={{0,16},{8,24},{16,0},{24,8},{1,17},{9,25},{17,1},{25,9},{2,18},{10... | collective-permute-start | bytes 1376264 | tf_op jit(solution)/shard_map/ppermute | solution.py:379
  135.0 13.6 %collective-permute-start.39 = (bf16[112,2048]{1,0:T(8,128)(2,1)S(1)}, bf16[112,2048]{1,0:T(8,128)(2,1)S(1)}, u32[]{:S(2)}, u32[]{:S(2)}) collective-permute-start(bf16[112,2048]{1,0:T(8,128)(2,1)S(1)} %add_convert_fusion.2), channel_id=1, source_target_pairs={{0,2},{1,3},{2,4},{3,5},{4,6},{5,7},{6,0},{7,1},{8,10},{9,11},{10,... | collective-permute-start | bytes 1376264 | tf_op jit(solution)/shard_map/ppermute | solution.py:383
  148.9 10.3 %collective-permute-start.40 = (bf16[112,2048]{1,0:T(8,128)(2,1)S(1)}, bf16[112,2048]{1,0:T(8,128)(2,1)S(1)}, u32[]{:S(2)}, u32[]{:S(2)}) collective-permute-start(bf16[112,2048]{1,0:T(8,128)(2,1)S(1)} %add_convert_fusion.1), channel_id=1, source_target_pairs={{0,2},{1,3},{2,4},{3,5},{4,6},{5,7},{6,0},{7,1},{8,10},{9,11},{10,... | collective-permute-start | bytes 1376264 | tf_op jit(solution)/shard_map/ppermute | solution.py:383
  150.0 9.2 %collective-permute-start.34 = (bf16[112,2048]{1,0:T(8,128)(2,1)S(1)}, bf16[112,2048]{1,0:T(8,128)(2,1)S(1)}, u32[]{:S(2)}, u32[]{:S(2)}) collective-permute-start(bf16[112,2048]{1,0:T(8,128)(2,1)S(1)} %get-tuple-element.180), channel_id=1, source_target_pairs={{0,8},{8,0},{16,24},{24,16},{1,9},{9,1},{17,25},{25,17},{2,10},{10... | collective-permute-start | bytes 1376264 | tf_op jit(solution)/shard_map/ppermute | solution.py:375
  150.0 9.2 %collective-permute-start.35 = (bf16[112,2048]{1,0:T(8,128)(2,1)S(1)}, bf16[112,2048]{1,0:T(8,128)(2,1)S(1)}, u32[]{:S(2)}, u32[]{:S(2)}) collective-permute-start(bf16[112,2048]{1,0:T(8,128)(2,1)S(1)} %get-tuple-element.181), channel_id=1, source_target_pairs={{0,16},{8,24},{16,0},{24,8},{1,17},{9,25},{17,1},{25,9},{2,18},{10... | collective-permute-start | bytes 1376264 | tf_op jit(solution)/shard_map/ppermute | solution.py:379

commit v10 on v9

--- a/solution.py
+++ b/solution.py
@@ -379,8 +379,8 @@
     return lax.ppermute(value, "kv", [(i, i ^ 2) for i in range(4)])
 
 
-def around_z(value):
-    return lax.ppermute(value, "blk", [(i, (i + 2) % 8) for i in range(8)])
+def around_z(value, hops=1):
+    return lax.ppermute(value, "blk", [(i, (i + 2 * hops) % 8) for i in range(8)])
 
 
 def across_chip(value):
@@ -445,13 +445,10 @@
 
     prefill = prefill_hidden[0]
     block_0 = prepare(prefill, norm_gain, router, ids, "block")
-    block_0, queries, cache_keys, expert_gate, expert_up = fence(
-        block_0, queries, cache_keys, expert_gate, expert_up
-    )
+    block_0, queries, cache_keys, expert_gate = fence(block_0, queries, cache_keys, expert_gate)
     sides_0 = spread_sides(block_0)
     block_1 = around_z(block_0)
     other_gate = across_chip(expert_gate[0])
-    other_up = across_chip(expert_up[0])
     attended = attend(queries, cache_keys, cache_values, lengths, sinks)
     partial_proj = jnp.dot(attended, out_proj, preferred_element_type=jnp.float32)
     is_mine = jnp.arange(4)[:, None] == my_kv
@@ -459,14 +456,18 @@
     width = partial_proj.shape[1]
     ids_row = jnp.pad(ids[:1].astype(jnp.float32), ((0, 0), (0, width - ids.shape[1])))
     shared = jnp.concatenate([partial_proj, jnp.where(is_mine, ids_row, 0.0)], axis=0)
+    sides_0, block_1, other_gate, expert_up, shared = fence(
+        sides_0, block_1, other_gate, expert_up, shared
+    )
+
     shared = shared + along_x(shared)
-    sides_0, block_1, other_gate = fence(sides_0, block_1, other_gate)
-
     corner_0 = spread_corner(sides_0)
-    corner_0, shared = fence(corner_0, shared)
+    other_up = across_chip(expert_up[0])
+    corner_0, shared, block_1, other_up, expert_down = fence(
+        corner_0, shared, block_1, other_up, expert_down
+    )
 
     shared = shared + along_y(shared)
-    shared, expert_down = fence(shared, expert_down)
     sides_1 = spread_sides(block_1)
     block_2 = around_z(block_1)
     other_down = across_chip(expert_down[0])
@@ -485,9 +486,7 @@
         jnp.pad(decode_ids, ((0, few - 4), (0, 0))),
         "first",
     )
-    sides_1, block_2, decodes_0, other_up, other_down = fence(
-        sides_1, block_2, decodes_0, other_up, other_down
-    )
+    sides_1, block_2, decodes_0, other_down = fence(sides_1, block_2, decodes_0, other_down)
     weights = (expert_gate[0], expert_up[0], expert_down[0], other_gate, other_up, other_down)
     halves = (tokens, tokens, tokens, cut, tokens - cut)
 
@@ -517,18 +516,19 @@
     far, first = join(sums_2[3], far, sums_1[0], *back_1)
     far = around_z(far)
     back_2 = return_sides(sums_2)
-    carried = around_z(first)
+    carried_1 = around_z(first, -1)
     sums_3 = apply((block_3,) + sides_3 + corner_3 + (decodes_3,), (tokens,) * 4)
     far, sums_2, sums_3 = fence(far, sums_2, sums_3)
 
     far = added(sums_3[3], far).astype(jnp.bfloat16)
     passed_3 = return_corner(tuple(sums_3[:3]) + (far[:cut], far[cut:]))
+    passed_3, passed_0, sums_0 = fence(passed_3, passed_0, sums_0)
     back_3 = return_sides(sums_3, passed_3)
-    carried = around_z(added(sums_2[0], *back_2, carried).astype(jnp.bfloat16))
-    back_3, passed_0, sums_0 = fence(back_3, passed_0, sums_0)
+    carried = around_z(added(sums_2[0], *back_2).astype(jnp.bfloat16))
+    back_3, carried_1 = fence(back_3, carried_1)
     carried = around_z(added(sums_3[0], *back_3, carried).astype(jnp.bfloat16))
     back_0 = return_sides(sums_0, passed_0)
-    return added(hidden, sums_0[0], *back_0, carried).astype(jnp.bfloat16)[None]
+    return added(hidden, sums_0[0], carried_1, *back_0, carried).astype(jnp.bfloat16)[None]
 
 
 def chunk_cuts(tokens, devices):

time: 161 us -> 160 us (level)
  waiting for transfers between devices: 52.7 us -> 49.5 us
  local copies, waits for them, and re-layouts: 5.69 us -> 8.03 us
    ppermute x14, waiting for transfers between devices: 7.69 us -> 1.84 us  [along_y(): return lax.ppermute(value, 'kv', [(i, i ^ 2) for i in range(4)])]
    ppermute x10, waiting for transfers between devices: 27.4 us -> 32.8 us  [around_z(): lax.ppermute(value, 'blk', [(i, (i + 2 * hops) % 8) for i in range(8)])]
    ppermute x14, waiting for transfers between devices: 17.6 us -> 14.8 us  [along_x(): return lax.ppermute(value, 'kv', [(i, i ^ 1) for i in range(4)])]
    unnamed x24 -> x28, local copies, waits for them, and re-layouts: 5.36 us -> 7.7 us
  transfers between devices with their start and end apart: 41 -> 41, of which waited for: 17 -> 15; matrix products, arithmetic and copies ran while one was open for 5% -> 5% of each run, Pallas kernels for 30% -> 30%
where the time goes in v10:
time: 160 us
  Pallas kernels  50 us (31%)
  waiting for transfers between devices  49.5 us (31%)
  starting transfers between devices  42.7 us (27%)
  local copies, waits for them, and re-layouts  8.03 us (5%)
  matrix products  5.11 us (3%)
  other arithmetic  4.26 us (3%)
    pallas_call x4, Pallas kernels, run_plane(): pl.pallas_call(functools.partial(plane_kernel, cap, piece_rows, block_row...  47.8 us
    ppermute x10, waiting for transfers between devices, around_z(): lax.ppermute(value, 'blk', [(i, (i + 2 * hops) % 8) for i in range(8)])  32.8 us
    ppermute x14, starting transfers between devices, along_x(): return lax.ppermute(value, 'kv', [(i, i ^ 1) for i in range(4)])  15.5 us
    ppermute x14, waiting for transfers between devices, along_x(): return lax.ppermute(value, 'kv', [(i, i ^ 1) for i in range(4)])  14.8 us
    ppermute x14, starting transfers between devices, along_y(): return lax.ppermute(value, 'kv', [(i, i ^ 2) for i in range(4)])  14.6 us
    ppermute x10, starting transfers between devices, around_z(): lax.ppermute(value, 'blk', [(i, (i + 2 * hops) % 8) for i in range(8)])  12.6 us
    unnamed x28, local copies, waits for them, and re-layouts  7.7 us
    dot_general x1, matrix products, attend(): jnp.einsum('rgd,rjd->rgj', grouped_q, key_rows, preferred_element_type=jn...  3.73 us
  transfers between devices with their start and end apart: 41, of which 15 were waited for; matrix products, arithmetic and copies ran while one was open for 5% of the time, Pallas kernels for 30%

profile of v10, /device:TPU:0, one launch (start us, length us, event | category | flops | bytes accessed | tf_op | source)
XLA Modules:
  0.0 160.0 jit_solution(3857273892670631976)
XLA Ops:
  0.0 1.0 copy-done
  1.0 0.9 copy-done.2
  1.9 0.7 copy-done.4
  2.6 0.7 copy-done.6
  3.3 1.3 prepare.2.refs_1_
  4.6 3.1 %collective-permute-start.2 = (bf16[112,2176]{1,0:T(8,128)(2,1)S(1)}, bf16[112,2176]{1,0:T(8,128)(2,1)}, u32[]{:S(2)}, u32[]{:S(2)}) collective-permute-start(bf16[112,2176]{1,0:T(8,128)(2,1)S(1)} %prepare.2.refs_1_), channel_id=1, source_target_pairs={{0,2},{1,3},{2,4},{3,5},{4,6},{5,7},{6,0},{7,1},{8,10},{9,11},{10,... | collective-permute-start | bytes 1462280 | tf_op jit(solution)/shard_map/ppermute | solution.py:383
  7.7 1.5 collective-permute-start.1
  9.2 1.5 collective-permute-start
  10.8 0.7 broadcast_in_dim.76
  11.6 0.9 minimum_subtract_fusion
  12.5 3.7 %fusion.33 = (f32[4,8]{1,0:T(4,128)S(1)}, f32[4,8,4096]{2,1,0:T(8,128)S(1)}) fusion(bf16[4,4096,1,128]{3,1,2,0:T(8,128)(2,1)} %param.15, bf16[1,4,8,128]{3,1,2,0:T(4,128)(2,1)} %bitcast.53, pred[4,4096]{1,0:T(4,128)(4,1)S(1)} %iota_compare_fusion.1), kind=kOutput, calls=%fused_computation.57 | convolution fusion | flops 33947616 | bytes 4743296 | tf_op jit(solution)/shard_map/rgd,rjd->rgj/dot_general | solution.py:27
  16.6 0.7 fusion.10
  17.4 1.1 copy-done.10
  18.5 0.7 convolution_add_fusion
  19.2 1.8 %collective-permute-done.2.refs_1_ = bf16[112,2176]{1,0:T(8,128)(2,1)} collective-permute-done((bf16[112,2176]{1,0:T(8,128)(2,1)S(1)}, bf16[112,2176]{1,0:T(8,128)(2,1)}, u32[]{:S(2)}, u32[]{:S(2)}) %collective-permute-start.2) | collective-permute-done | bytes 487456 | tf_op jit(solution)/shard_map/ppermute | solution.py:383
  21.0 0.6 collective-permute-done.refs_2_
  21.6 1.1 collective-permute-start.4
  22.7 1.6 collective-permute-start.5
  24.2 0.5 collective-permute-start.6
  24.8 6.7 %collective-permute-done.6 = f32[8,2048]{1,0:T(8,128)S(1)} collective-permute-done((f32[8,2048]{1,0:T(8,128)S(1)}, f32[8,2048]{1,0:T(8,128)S(1)}, u32[]{:S(2)}, u32[]{:S(2)}) %collective-permute-start.6) | collective-permute-done | bytes 65568 | tf_op jit(solution)/shard_map/ppermute | solution.py:375
  31.5 0.7 copy-done.7
  32.2 1.7 %copy-done.13 = bf16[2048,768]{1,0:T(8,128)(2,1)} copy-done((bf16[2048,768]{1,0:T(8,128)(2,1)}, bf16[2048,768]{1,0:T(8,128)(2,1)S(1)}, u32[]{:S(2)}) %copy-start.13) | copy-done | bytes 3145752
  33.8 1.0 collective-permute-start.8
  34.9 1.6 collective-permute-start.11
  37.0 1.5 collective-permute-start.9
  39.2 11.0 %collective-permute-done.11.refs_1_ = bf16[112,2176]{1,0:T(8,128)(2,1)S(1)} collective-permute-done((bf16[112,2176]{1,0:T(8,128)(2,1)}, bf16[112,2176]{1,0:T(8,128)(2,1)S(1)}, u32[]{:S(2)}, u32[]{:S(2)}) %collective-permute-start.11) | collective-permute-done | bytes 487456 | tf_op jit(solution)/shard_map/ppermute | solution.py:383
  50.2 1.2 collective-permute-start.16
  51.4 1.5 collective-permute-start.15
  52.9 0.6 collective-permute-start.14
  53.6 0.9 collective-permute-start.13
  54.5 1.3 collective-permute-start.17
  55.8 0.9 copy-done.8
  56.7 12.1 %plane.4 = (bf16[112,2048]{1,0:T(8,128)(2,1)S(1)}, bf16[112,2048]{1,0:T(8,128)(2,1)S(1)}, bf16[112,2048]{1,0:T(8,128)(2,1)S(1)}, bf16[64,2048]{1,0:T(8,128)(2,1)S(1)}, bf16[48,2048]{1,0:T(8,128)(2,1)S(1)}) custom-call(s32[3]{0:T(128)S(1)} %pad_add_fusion.refs_0_, bf16[112,2176]{1,0:T(8,128)(2,1)S(1)} %prepare.2.refs_1_, ...), custom_call_target="tpu_custom_call" | custom-call | flops 8455716864 | bytes 25165824 | tf_op jit(solution)/shard_map/plane/pallas_call | solution.py:313
  69.2 1.3 collective-permute-start.19
  70.5 1.5 collective-permute-start.18
  72.0 0.5 collective-permute-start.22
  72.5 0.8 collective-permute-start.21
  73.8 11.7 %plane.5 = (bf16[112,2048]{1,0:T(8,128)(2,1)S(1)}, bf16[112,2048]{1,0:T(8,128)(2,1)S(1)}, bf16[112,2048]{1,0:T(8,128)(2,1)S(1)}, bf16[112,2048]{1,0:T(8,128)(2,1)S(1)}) custom-call(s32[3]{0:T(128)S(1)} %pad_add_fusion.refs_0_, bf16[112,2176]{1,0:T(8,128)(2,1)} %collective-permute-done.2.refs_1_, bf16[112,2176]{1,0:T(8,128)(2,1)S(1)} %collective-permute-done.9.refs_2_, ...), custom_call_target="tpu_custom_call" | custom-call | flops 8455716864 | bytes 25165824 | tf_op jit(solution)/shard_map/plane/pallas_call | solution.py:313
  86.0 0.9 collective-permute-done.20.refs_4_
  86.8 0.6 collective-permute-start.23
  87.5 1.6 collective-permute-start.26
  89.1 1.1 collective-permute-start.25
  90.2 0.5 collective-permute-start.27
  90.7 1.0 collective-permute-start.28
  91.7 1.7 %collective-permute-done.23.refs_6_ = bf16[16,2176]{1,0:T(8,128)(2,1)S(1)} collective-permute-done((bf16[16,2176]{1,0:T(8,128)(2,1)S(1)}, bf16[16,2176]{1,0:T(8,128)(2,1)S(1)}, u32[]{:S(2)}, u32[]{:S(2)}) %collective-permute-start.23) | collective-permute-done | bytes 69664 | tf_op jit(solution)/shard_map/ppermute | solution.py:383
  93.5 12.0 %plane.6 = (bf16[112,2048]{1,0:T(8,128)(2,1)S(1)}, bf16[112,2048]{1,0:T(8,128)(2,1)S(1)}, bf16[112,2048]{1,0:T(8,128)(2,1)S(1)}, bf16[112,2048]{1,0:T(8,128)(2,1)S(1)}) custom-call(s32[3]{0:T(128)S(1)} %pad_add_fusion.refs_0_, bf16[112,2176]{1,0:T(8,128)(2,1)S(1)} %collective-permute-done.11.refs_1_, bf16[112,2176]{1,0:T(8,128)(2,1)S(1)} %collective-permute-done.15.refs_2_, ...), custom_call_target="tpu_custom_call" | custom-call | flops 8455716864 | bytes 25165824 | tf_op jit(solution)/shard_map/plane/pallas_call | solution.py:313
  105.8 1.5 collective-permute-start.29
  107.3 1.5 collective-permute-start.37
  108.8 1.2 collective-permute-start.38
  110.0 12.0 %plane.7 = (bf16[112,2048]{1,0:T(8,128)(2,1)S(1)}, bf16[112,2048]{1,0:T(8,128)(2,1)S(1)}, bf16[112,2048]{1,0:T(8,128)(2,1)S(1)}, bf16[112,2048]{1,0:T(8,128)(2,1)S(1)}) custom-call(s32[3]{0:T(128)S(1)} %pad_add_fusion.refs_0_, bf16[112,2176]{1,0:T(8,128)(2,1)S(1)} %slice.50.refs_1_, bf16[112,2176]{1,0:T(8,128)(2,1)S(1)} %collective-permute-done.18.refs_2_, ...), custom_call_target="tpu_custom_call" | custom-call | flops 8455716864 | bytes 25165824 | tf_op jit(solution)/shard_map/plane/pallas_call | solution.py:313
  122.1 0.9 collective-permute-start.30
  123.1 0.6 collective-permute-start.31
  123.6 2.7 %collective-permute-start.34 = (bf16[112,2048]{1,0:T(8,128)(2,1)S(1)}, bf16[112,2048]{1,0:T(8,128)(2,1)S(1)}, u32[]{:S(2)}, u32[]{:S(2)}) collective-permute-start(bf16[112,2048]{1,0:T(8,128)(2,1)S(1)} %get-tuple-element.183), channel_id=1, source_target_pairs={{0,6},{1,7},{2,0},{3,1},{4,2},{5,3},{6,4},{7,5},{8,14},{9,15},{10,... | collective-permute-start | bytes 1376264 | tf_op jit(solution)/shard_map/ppermute | solution.py:383
  126.3 4.6 %collective-permute-done.31.passed_1_ref = bf16[48,2048]{1,0:T(8,128)(2,1)S(1)} collective-permute-done((bf16[48,2048]{1,0:T(8,128)(2,1)S(1)}, bf16[48,2048]{1,0:T(8,128)(2,1)S(1)}, u32[]{:S(2)}, u32[]{:S(2)}) %collective-permute-start.31) | collective-permute-done | bytes 196640 | tf_op jit(solution)/shard_map/ppermute | solution.py:375
  132.0 0.9 collective-permute-start.33
  133.1 1.4 collective-permute-start.39
  134.6 1.7 %collective-permute-start.35 = (bf16[112,2048]{1,0:T(8,128)(2,1)S(1)}, bf16[112,2048]{1,0:T(8,128)(2,1)S(1)}, u32[]{:S(2)}, u32[]{:S(2)}) collective-permute-start(bf16[112,2048]{1,0:T(8,128)(2,1)S(1)} %get-tuple-element.189), channel_id=1, source_target_pairs={{0,8},{8,0},{16,24},{24,16},{1,9},{9,1},{17,25},{25,17},{2,10},{10... | collective-permute-start | bytes 1376264 | tf_op jit(solution)/shard_map/ppermute | solution.py:375
  136.3 0.7 collective-permute-done.34
  136.9 1.1 collective-permute-start.36
  138.1 3.0 %collective-permute-done.32 = bf16[112,2048]{1,0:T(8,128)(2,1)S(1)} collective-permute-done((bf16[112,2048]{1,0:T(8,128)(2,1)S(1)}, bf16[112,2048]{1,0:T(8,128)(2,1)S(1)}, u32[]{:S(2)}, u32[]{:S(2)}) %collective-permute-start.32) | collective-permute-done | bytes 458784 | tf_op jit(solution)/shard_map/ppermute | solution.py:375
  141.0 1.0 collective-permute-done.33
  142.0 6.2 %collective-permute-done.39 = bf16[112,2048]{1,0:T(8,128)(2,1)S(1)} collective-permute-done((bf16[112,2048]{1,0:T(8,128)(2,1)S(1)}, bf16[112,2048]{1,0:T(8,128)(2,1)S(1)}, u32[]{:S(2)}, u32[]{:S(2)}) %collective-permute-start.39) | collective-permute-done | bytes 458784 | tf_op jit(solution)/shard_map/ppermute | solution.py:383
  148.5 10.2 %collective-permute-done.40 = bf16[112,2048]{1,0:T(8,128)(2,1)S(1)} collective-permute-done((bf16[112,2048]{1,0:T(8,128)(2,1)S(1)}, bf16[112,2048]{1,0:T(8,128)(2,1)S(1)}, u32[]{:S(2)}, u32[]{:S(2)}) %collective-permute-start.40) | collective-permute-done | bytes 458784 | tf_op jit(solution)/shard_map/ppermute | solution.py:383
  158.8 1.2 fusion.13
  (95 shorter events, 5.5 us)
Async XLA Ops:
  0.0 16.3 %copy-start.11 = (f32[8]{0:T(128)S(1)}, f32[8]{0:T(128)}, u32[]{:S(2)}) copy-start(f32[8]{0:T(128)} %param.18) | copy-start | bytes 100
  0.0 1.0 copy-start
  1.0 0.9 copy-start.2
  1.9 0.7 copy-start.4
  2.6 0.7 copy-start.6
  4.6 16.3 %collective-permute-start.2 = (bf16[112,2176]{1,0:T(8,128)(2,1)S(1)}, bf16[112,2176]{1,0:T(8,128)(2,1)}, u32[]{:S(2)}, u32[]{:S(2)}) collective-permute-start(bf16[112,2176]{1,0:T(8,128)(2,1)S(1)} %prepare.2.refs_1_), channel_id=1, source_target_pairs={{0,2},{1,3},{2,4},{3,5},{4,6},{5,7},{6,0},{7,1},{8,10},{9,11},{10,... | collective-permute-start | bytes 1462280 | tf_op jit(solution)/shard_map/ppermute | solution.py:383
  7.7 13.3 %collective-permute-start.1 = (bf16[112,2176]{1,0:T(8,128)(2,1)S(1)}, bf16[112,2176]{1,0:T(8,128)(2,1)S(1)}, u32[]{:S(2)}, u32[]{:S(2)}) collective-permute-start(bf16[112,2176]{1,0:T(8,128)(2,1)S(1)} %prepare.2.refs_1_), channel_id=1, source_target_pairs={{0,16},{8,24},{16,0},{24,8},{1,17},{9,25},{17,1},{25,9},{2,18},{10... | collective-permute-start | bytes 1462280 | tf_op jit(solution)/shard_map/ppermute | solution.py:379
  9.2 12.3 %collective-permute-start = (bf16[112,2176]{1,0:T(8,128)(2,1)S(1)}, bf16[112,2176]{1,0:T(8,128)(2,1)S(1)}, u32[]{:S(2)}, u32[]{:S(2)}) collective-permute-start(bf16[112,2176]{1,0:T(8,128)(2,1)S(1)} %prepare.2.refs_1_), channel_id=1, source_target_pairs={{0,8},{8,0},{16,24},{24,16},{1,9},{9,1},{17,25},{25,17},{2,10},{10... | collective-permute-start | bytes 1462280 | tf_op jit(solution)/shard_map/ppermute | solution.py:375
  10.7 10.8 %collective-permute-start.3 = (bf16[2048,768]{1,0:T(8,128)(2,1)}, bf16[2048,768]{1,0:T(8,128)(2,1)}, u32[]{:S(2)}, u32[]{:S(2)}) collective-permute-start(bf16[2048,768]{1,0:T(8,128)(2,1)} %bitcast.55), channel_id=1, source_target_pairs={{0,1},{1,0},{2,3},{3,2},{4,5},{5,4},{6,7},{7,6},{8,9},{9,8},{10,11... | collective-permute-start | bytes 9437192 | tf_op jit(solution)/shard_map/ppermute | solution.py:387
  11.5 5.0 %copy-start.9 = (bf16[4,4096,1,128]{3,1,2,0:T(8,128)(2,1)S(1)}, bf16[4,4096,1,128]{3,1,2,0:T(8,128)(2,1)}, u32[]{:S(2)}) copy-start(bf16[4,4096,1,128]{3,1,2,0:T(8,128)(2,1)} %param.16) | copy-start | bytes 12582916
  16.3 2.2 %copy-start.10 = (bf16[1024,2048]{1,0:T(8,128)(2,1)S(1)}, bf16[1024,2048]{1,0:T(8,128)(2,1)}, u32[]{:S(2)}) copy-start(bf16[1024,2048]{1,0:T(8,128)(2,1)} %param.19) | copy-start | bytes 12582916
  17.3 4.2 %copy-start.12 = (bf16[1,2048,768]{2,1,0:T(8,128)(2,1)S(1)}, bf16[1,2048,768]{2,1,0:T(8,128)(2,1)}, u32[]{:S(2)}) copy-start(bf16[1,2048,768]{2,1,0:T(8,128)(2,1)} %param.26) | copy-start | bytes 9437188
  17.3 21.4 %copy-start.3 = (bf16[2048,32]{0,1:T(8,128)(2,1)S(1)}, bf16[2048,32]{0,1:T(8,128)(2,1)}, u32[]{:S(2)}) copy-start(bf16[2048,32]{0,1:T(8,128)(2,1)} %param.23) | copy-start | bytes 393220
  17.3 21.4 %copy-start.5 = (f32[2048]{0:T(1024)S(1)}, f32[2048]{0:T(1024)}, u32[]{:S(2)}) copy-start(f32[2048]{0:T(1024)} %param.22) | copy-start | bytes 24580
  21.5 10.6 %collective-permute-start.7 = (bf16[2048,768]{1,0:T(8,128)(2,1)S(1)}, bf16[2048,768]{1,0:T(8,128)(2,1)S(1)}, u32[]{:S(2)}, u32[]{:S(2)}) collective-permute-start(bf16[2048,768]{1,0:T(8,128)(2,1)S(1)} %bitcast.64), channel_id=1, source_target_pairs={{0,1},{1,0},{2,3},{3,2},{4,5},{5,4},{6,7},{7,6},{8,9},{9,8},{10,11... | collective-permute-start | bytes 9437192 | tf_op jit(solution)/shard_map/ppermute | solution.py:387
  21.6 10.6 %collective-permute-start.4 = (bf16[64,2176]{1,0:T(8,128)(2,1)S(1)}, bf16[64,2176]{1,0:T(8,128)(2,1)S(1)}, u32[]{:S(2)}, u32[]{:S(2)}) collective-permute-start(bf16[64,2176]{1,0:T(8,128)(2,1)S(1)} %slice.44), channel_id=1, source_target_pairs={{0,16},{8,24},{16,0},{24,8},{1,17},{9,25},{17,1},{25,9},{2,18},{10... | collective-permute-start | bytes 835592 | tf_op jit(solution)/shard_map/ppermute | solution.py:379
  22.7 8.8 %collective-permute-start.5 = (bf16[48,2176]{1,0:T(8,128)(2,1)S(1)}, bf16[48,2176]{1,0:T(8,128)(2,1)S(1)}, u32[]{:S(2)}, u32[]{:S(2)}) collective-permute-start(bf16[48,2176]{1,0:T(8,128)(2,1)S(1)} %slice.45), channel_id=1, source_target_pairs={{0,8},{8,0},{16,24},{24,16},{1,9},{9,1},{17,25},{25,17},{2,10},{10... | collective-permute-start | bytes 626696 | tf_op jit(solution)/shard_map/ppermute | solution.py:375
  24.2 7.2 %collective-permute-start.6 = (f32[8,2048]{1,0:T(8,128)S(1)}, f32[8,2048]{1,0:T(8,128)S(1)}, u32[]{:S(2)}, u32[]{:S(2)}) collective-permute-start(f32[8,2048]{1,0:T(8,128)S(1)} %pad_maximum_fusion.2), channel_id=1, source_target_pairs={{0,8},{8,0},{16,24},{24,16},{1,9},{9,1},{17,25},{25,17},{2,10},{10... | collective-permute-start | bytes 196616 | tf_op jit(solution)/shard_map/ppermute | solution.py:375
  31.5 0.7 copy-start.7
  32.2 1.7 %copy-start.13 = (bf16[2048,768]{1,0:T(8,128)(2,1)}, bf16[2048,768]{1,0:T(8,128)(2,1)S(1)}, u32[]{:S(2)}) copy-start(bf16[2048,768]{1,0:T(8,128)(2,1)S(1)} %collective-permute-done.7.refs_11_.refs_9_) | copy-start | bytes 9437188
  33.8 16.4 %collective-permute-start.12 = (bf16[768,2048]{1,0:T(8,128)(2,1)}, bf16[768,2048]{1,0:T(8,128)(2,1)}, u32[]{:S(2)}, u32[]{:S(2)}) collective-permute-start(bf16[768,2048]{1,0:T(8,128)(2,1)} %bitcast.65), channel_id=1, source_target_pairs={{0,1},{1,0},{2,3},{3,2},{4,5},{5,4},{6,7},{7,6},{8,9},{9,8},{10,11... | collective-permute-start | bytes 9437192 | tf_op jit(solution)/shard_map/ppermute | solution.py:387
  33.8 4.7 %collective-permute-start.8 = (f32[8,2048]{1,0:T(8,128)S(1)}, f32[8,2048]{1,0:T(8,128)S(1)}, u32[]{:S(2)}, u32[]{:S(2)}) collective-permute-start(f32[8,2048]{1,0:T(8,128)S(1)} %add.111), channel_id=1, source_target_pairs={{0,16},{8,24},{16,0},{24,8},{1,17},{9,25},{17,1},{25,9},{2,18},{10... | collective-permute-start | bytes 196616 | tf_op jit(solution)/shard_map/ppermute | solution.py:379
  34.9 15.3 %collective-permute-start.11 = (bf16[112,2176]{1,0:T(8,128)(2,1)}, bf16[112,2176]{1,0:T(8,128)(2,1)S(1)}, u32[]{:S(2)}, u32[]{:S(2)}) collective-permute-start(bf16[112,2176]{1,0:T(8,128)(2,1)} %collective-permute-done.2.refs_1_), channel_id=1, source_target_pairs={{0,2},{1,3},{2,4},{3,5},{4,6},{5,7},{6,0},{7,1},{8,10},{9,11},{10,... | collective-permute-start | bytes 1462280 | tf_op jit(solution)/shard_map/ppermute | solution.py:383
  36.5 13.7 %collective-permute-start.10 = (bf16[112,2176]{1,0:T(8,128)(2,1)}, bf16[112,2176]{1,0:T(8,128)(2,1)S(1)}, u32[]{:S(2)}, u32[]{:S(2)}) collective-permute-start(bf16[112,2176]{1,0:T(8,128)(2,1)} %collective-permute-done.2.refs_1_), channel_id=1, source_target_pairs={{0,16},{8,24},{16,0},{24,8},{1,17},{9,25},{17,1},{25,9},{2,18},{10... | collective-permute-start | bytes 1462280 | tf_op jit(solution)/shard_map/ppermute | solution.py:379
  37.0 13.2 %collective-permute-start.9 = (bf16[112,2176]{1,0:T(8,128)(2,1)}, bf16[112,2176]{1,0:T(8,128)(2,1)S(1)}, u32[]{:S(2)}, u32[]{:S(2)}) collective-permute-start(bf16[112,2176]{1,0:T(8,128)(2,1)} %collective-permute-done.2.refs_1_), channel_id=1, source_target_pairs={{0,8},{8,0},{16,24},{24,16},{1,9},{9,1},{17,25},{25,17},{2,10},{10... | collective-permute-start | bytes 1462280 | tf_op jit(solution)/shard_map/ppermute | solution.py:375
  50.2 18.7 %collective-permute-start.16 = (bf16[112,2176]{1,0:T(8,128)(2,1)S(1)}, bf16[112,2176]{1,0:T(8,128)(2,1)S(1)}, u32[]{:S(2)}, u32[]{:S(2)}) collective-permute-start(bf16[112,2176]{1,0:T(8,128)(2,1)S(1)} %collective-permute-done.11.refs_1_), channel_id=1, source_target_pairs={{0,16},{8,24},{16,0},{24,8},{1,17},{9,25},{17,1},{25,9},{2,18},{10... | collective-permute-start | bytes 1462280 | tf_op jit(solution)/shard_map/ppermute | solution.py:379
  51.4 17.4 %collective-permute-start.15 = (bf16[112,2176]{1,0:T(8,128)(2,1)S(1)}, bf16[112,2176]{1,0:T(8,128)(2,1)S(1)}, u32[]{:S(2)}, u32[]{:S(2)}) collective-permute-start(bf16[112,2176]{1,0:T(8,128)(2,1)S(1)} %collective-permute-done.11.refs_1_), channel_id=1, source_target_pairs={{0,8},{8,0},{16,24},{24,16},{1,9},{9,1},{17,25},{25,17},{2,10},{10... | collective-permute-start | bytes 1462280 | tf_op jit(solution)/shard_map/ppermute | solution.py:375
  52.9 15.9 %collective-permute-start.14 = (bf16[48,2176]{1,0:T(8,128)(2,1)S(1)}, bf16[48,2176]{1,0:T(8,128)(2,1)S(1)}, u32[]{:S(2)}, u32[]{:S(2)}) collective-permute-start(bf16[48,2176]{1,0:T(8,128)(2,1)S(1)} %slice.49), channel_id=1, source_target_pairs={{0,8},{8,0},{16,24},{24,16},{1,9},{9,1},{17,25},{25,17},{2,10},{10... | collective-permute-start | bytes 626696 | tf_op jit(solution)/shard_map/ppermute | solution.py:375
  53.6 15.3 %collective-permute-start.13 = (bf16[64,2176]{1,0:T(8,128)(2,1)S(1)}, bf16[64,2176]{1,0:T(8,128)(2,1)S(1)}, u32[]{:S(2)}, u32[]{:S(2)}) collective-permute-start(bf16[64,2176]{1,0:T(8,128)(2,1)S(1)} %slice.48), channel_id=1, source_target_pairs={{0,16},{8,24},{16,0},{24,8},{1,17},{9,25},{17,1},{25,9},{2,18},{10... | collective-permute-start | bytes 835592 | tf_op jit(solution)/shard_map/ppermute | solution.py:379
  54.5 14.7 %collective-permute-start.17 = (bf16[128,2176]{1,0:T(8,128)(2,1)S(1)}, bf16[128,2176]{1,0:T(8,128)(2,1)S(1)}, u32[]{:S(2)}, u32[]{:S(2)}) collective-permute-start(bf16[128,2176]{1,0:T(8,128)(2,1)S(1)} %pad_maximum_fusion), channel_id=1, source_target_pairs={{0,2},{1,3},{2,4},{3,5},{4,6},{5,7},{6,0},{7,1},{8,10},{9,11},{10,... | collective-permute-start | bytes 1671176 | tf_op jit(solution)/shard_map/ppermute | solution.py:383
  55.8 0.9 copy-start.8
  69.2 16.7 %collective-permute-start.19 = (bf16[112,2176]{1,0:T(8,128)(2,1)S(1)}, bf16[112,2176]{1,0:T(8,128)(2,1)S(1)}, u32[]{:S(2)}, u32[]{:S(2)}) collective-permute-start(bf16[112,2176]{1,0:T(8,128)(2,1)S(1)} %slice.50.refs_1_), channel_id=1, source_target_pairs={{0,16},{8,24},{16,0},{24,8},{1,17},{9,25},{17,1},{25,9},{2,18},{10... | collective-permute-start | bytes 1462280 | tf_op jit(solution)/shard_map/ppermute | solution.py:379
  70.5 15.4 %collective-permute-start.18 = (bf16[112,2176]{1,0:T(8,128)(2,1)S(1)}, bf16[112,2176]{1,0:T(8,128)(2,1)S(1)}, u32[]{:S(2)}, u32[]{:S(2)}) collective-permute-start(bf16[112,2176]{1,0:T(8,128)(2,1)S(1)} %slice.50.refs_1_), channel_id=1, source_target_pairs={{0,8},{8,0},{16,24},{24,16},{1,9},{9,1},{17,25},{25,17},{2,10},{10... | collective-permute-start | bytes 1462280 | tf_op jit(solution)/shard_map/ppermute | solution.py:375
  72.0 13.5 %collective-permute-start.22 = (bf16[48,2048]{1,0:T(8,128)(2,1)S(1)}, bf16[48,2048]{1,0:T(8,128)(2,1)S(1)}, u32[]{:S(2)}, u32[]{:S(2)}) collective-permute-start(bf16[48,2048]{1,0:T(8,128)(2,1)S(1)} %get-tuple-element.130), channel_id=1, source_target_pairs={{0,8},{8,0},{16,24},{24,16},{1,9},{9,1},{17,25},{25,17},{2,10},{10... | collective-permute-start | bytes 589832 | tf_op jit(solution)/shard_map/ppermute | solution.py:375
  72.5 13.4 %collective-permute-start.21 = (bf16[64,2048]{1,0:T(8,128)(2,1)S(1)}, bf16[64,2048]{1,0:T(8,128)(2,1)S(1)}, u32[]{:S(2)}, u32[]{:S(2)}) collective-permute-start(bf16[64,2048]{1,0:T(8,128)(2,1)S(1)} %get-tuple-element.129), channel_id=1, source_target_pairs={{0,16},{8,24},{16,0},{24,8},{1,17},{9,25},{17,1},{25,9},{2,18},{10... | collective-permute-start | bytes 786440 | tf_op jit(solution)/shard_map/ppermute | solution.py:379
  73.4 13.4 %collective-permute-start.20 = (bf16[128,2176]{1,0:T(8,128)(2,1)S(1)}, bf16[128,2176]{1,0:T(8,128)(2,1)S(1)}, u32[]{:S(2)}, u32[]{:S(2)}) collective-permute-start(bf16[128,2176]{1,0:T(8,128)(2,1)S(1)} %pad_maximum_fusion.1), channel_id=1, source_target_pairs={{0,2},{1,3},{2,4},{3,5},{4,6},{5,7},{6,0},{7,1},{8,10},{9,11},{10,... | collective-permute-start | bytes 1671176 | tf_op jit(solution)/shard_map/ppermute | solution.py:383
  86.8 6.6 %collective-permute-start.23 = (bf16[16,2176]{1,0:T(8,128)(2,1)S(1)}, bf16[16,2176]{1,0:T(8,128)(2,1)S(1)}, u32[]{:S(2)}, u32[]{:S(2)}) collective-permute-start(bf16[16,2176]{1,0:T(8,128)(2,1)S(1)} %slice.52), channel_id=1, source_target_pairs={{0,2},{1,3},{2,4},{3,5},{4,6},{5,7},{6,0},{7,1},{8,10},{9,11},{10,... | collective-permute-start | bytes 208904 | tf_op jit(solution)/shard_map/ppermute | solution.py:383
  87.5 18.0 %collective-permute-start.26 = (bf16[48,2176]{1,0:T(8,128)(2,1)S(1)}, bf16[48,2176]{1,0:T(8,128)(2,1)S(1)}, u32[]{:S(2)}, u32[]{:S(2)}) collective-permute-start(bf16[48,2176]{1,0:T(8,128)(2,1)S(1)} %slice.54), channel_id=1, source_target_pairs={{0,8},{8,0},{16,24},{24,16},{1,9},{9,1},{17,25},{25,17},{2,10},{10... | collective-permute-start | bytes 626696 | tf_op jit(solution)/shard_map/ppermute | solution.py:375
  89.1 16.4 %collective-permute-start.25 = (bf16[64,2176]{1,0:T(8,128)(2,1)S(1)}, bf16[64,2176]{1,0:T(8,128)(2,1)S(1)}, u32[]{:S(2)}, u32[]{:S(2)}) collective-permute-start(bf16[64,2176]{1,0:T(8,128)(2,1)S(1)} %slice.53), channel_id=1, source_target_pairs={{0,16},{8,24},{16,0},{24,8},{1,17},{9,25},{17,1},{25,9},{2,18},{10... | collective-permute-start | bytes 835592 | tf_op jit(solution)/shard_map/ppermute | solution.py:379
  90.2 15.3 %collective-permute-start.27 = (bf16[112,2048]{1,0:T(8,128)(2,1)S(1)}, bf16[112,2048]{1,0:T(8,128)(2,1)S(1)}, u32[]{:S(2)}, u32[]{:S(2)}) collective-permute-start(bf16[112,2048]{1,0:T(8,128)(2,1)S(1)} %get-tuple-element.144), channel_id=1, source_target_pairs={{0,8},{8,0},{16,24},{24,16},{1,9},{9,1},{17,25},{25,17},{2,10},{10... | collective-permute-start | bytes 1376264 | tf_op jit(solution)/shard_map/ppermute | solution.py:375
  90.7 14.8 %collective-permute-start.28 = (bf16[112,2048]{1,0:T(8,128)(2,1)S(1)}, bf16[112,2048]{1,0:T(8,128)(2,1)S(1)}, u32[]{:S(2)}, u32[]{:S(2)}) collective-permute-start(bf16[112,2048]{1,0:T(8,128)(2,1)S(1)} %get-tuple-element.145), channel_id=1, source_target_pairs={{0,16},{8,24},{16,0},{24,8},{1,17},{9,25},{17,1},{25,9},{2,18},{10... | collective-permute-start | bytes 1376264 | tf_op jit(solution)/shard_map/ppermute | solution.py:379
  93.5 12.0 %collective-permute-start.24 = (bf16[112,2048]{1,0:T(8,128)(2,1)S(1)}, bf16[112,2048]{1,0:T(8,128)(2,1)S(1)}, u32[]{:S(2)}, u32[]{:S(2)}) collective-permute-start(bf16[112,2048]{1,0:T(8,128)(2,1)S(1)} %get-tuple-element.141), channel_id=1, source_target_pairs={{0,2},{1,3},{2,4},{3,5},{4,6},{5,7},{6,0},{7,1},{8,10},{9,11},{10,... | collective-permute-start | bytes 1376264 | tf_op jit(solution)/shard_map/ppermute | solution.py:383
  105.8 16.2 %collective-permute-start.29 = (bf16[112,2048]{1,0:T(8,128)(2,1)S(1)}, bf16[112,2048]{1,0:T(8,128)(2,1)S(1)}, u32[]{:S(2)}, u32[]{:S(2)}) collective-permute-start(bf16[112,2048]{1,0:T(8,128)(2,1)S(1)} %get-tuple-element.158), channel_id=1, source_target_pairs={{0,2},{1,3},{2,4},{3,5},{4,6},{5,7},{6,0},{7,1},{8,10},{9,11},{10,... | collective-permute-start | bytes 1376264 | tf_op jit(solution)/shard_map/ppermute | solution.py:383
  107.3 25.7 %collective-permute-start.37 = (bf16[112,2048]{1,0:T(8,128)(2,1)S(1)}, bf16[112,2048]{1,0:T(8,128)(2,1)S(1)}, u32[]{:S(2)}, u32[]{:S(2)}) collective-permute-start(bf16[112,2048]{1,0:T(8,128)(2,1)S(1)} %get-tuple-element.160), channel_id=1, source_target_pairs={{0,8},{8,0},{16,24},{24,16},{1,9},{9,1},{17,25},{25,17},{2,10},{10... | collective-permute-start | bytes 1376264 | tf_op jit(solution)/shard_map/ppermute | solution.py:375
  108.8 24.2 %collective-permute-start.38 = (bf16[112,2048]{1,0:T(8,128)(2,1)S(1)}, bf16[112,2048]{1,0:T(8,128)(2,1)S(1)}, u32[]{:S(2)}, u32[]{:S(2)}) collective-permute-start(bf16[112,2048]{1,0:T(8,128)(2,1)S(1)} %get-tuple-element.161), channel_id=1, source_target_pairs={{0,16},{8,24},{16,0},{24,8},{1,17},{9,25},{17,1},{25,9},{2,18},{10... | collective-permute-start | bytes 1376264 | tf_op jit(solution)/shard_map/ppermute | solution.py:379
  122.1 9.3 %collective-permute-start.30 = (bf16[64,2048]{1,0:T(8,128)(2,1)S(1)}, bf16[64,2048]{1,0:T(8,128)(2,1)S(1)}, u32[]{:S(2)}, u32[]{:S(2)}) collective-permute-start(bf16[64,2048]{1,0:T(8,128)(2,1)S(1)} %slice.57), channel_id=1, source_target_pairs={{0,16},{8,24},{16,0},{24,8},{1,17},{9,25},{17,1},{25,9},{2,18},{10... | collective-permute-start | bytes 786440 | tf_op jit(solution)/shard_map/ppermute | solution.py:379
  123.1 7.9 %collective-permute-start.31 = (bf16[48,2048]{1,0:T(8,128)(2,1)S(1)}, bf16[48,2048]{1,0:T(8,128)(2,1)S(1)}, u32[]{:S(2)}, u32[]{:S(2)}) collective-permute-start(bf16[48,2048]{1,0:T(8,128)(2,1)S(1)} %slice.58), channel_id=1, source_target_pairs={{0,8},{8,0},{16,24},{24,16},{1,9},{9,1},{17,25},{25,17},{2,10},{10... | collective-permute-start | bytes 589832 | tf_op jit(solution)/shard_map/ppermute | solution.py:375
  123.6 35.1 %copy-start.1 = (bf16[1,111,2048]{2,1,0:T(8,128)(2,1)S(1)}, bf16[1,111,2048]{2,1,0:T(8,128)(2,1)}, u32[]{:S(2)}) copy-start(bf16[1,111,2048]{2,1,0:T(8,128)(2,1)} %param.21) | copy-start | bytes 1363972
  123.6 13.3 %collective-permute-start.34 = (bf16[112,2048]{1,0:T(8,128)(2,1)S(1)}, bf16[112,2048]{1,0:T(8,128)(2,1)S(1)}, u32[]{:S(2)}, u32[]{:S(2)}) collective-permute-start(bf16[112,2048]{1,0:T(8,128)(2,1)S(1)} %get-tuple-element.183), channel_id=1, source_target_pairs={{0,6},{1,7},{2,0},{3,1},{4,2},{5,3},{6,4},{7,5},{8,14},{9,15},{10,... | collective-permute-start | bytes 1376264 | tf_op jit(solution)/shard_map/ppermute | solution.py:383
  131.5 9.5 %collective-permute-start.32 = (bf16[112,2048]{1,0:T(8,128)(2,1)S(1)}, bf16[112,2048]{1,0:T(8,128)(2,1)S(1)}, u32[]{:S(2)}, u32[]{:S(2)}) collective-permute-start(bf16[112,2048]{1,0:T(8,128)(2,1)S(1)} %get-tuple-element.181), channel_id=1, source_target_pairs={{0,8},{8,0},{16,24},{24,16},{1,9},{9,1},{17,25},{25,17},{2,10},{10... | collective-permute-start | bytes 1376264 | tf_op jit(solution)/shard_map/ppermute | solution.py:375
  132.0 10.0 %collective-permute-start.33 = (bf16[112,2048]{1,0:T(8,128)(2,1)S(1)}, bf16[112,2048]{1,0:T(8,128)(2,1)S(1)}, u32[]{:S(2)}, u32[]{:S(2)}) collective-permute-start(bf16[112,2048]{1,0:T(8,128)(2,1)S(1)} %get-tuple-element.182), channel_id=1, source_target_pairs={{0,16},{8,24},{16,0},{24,8},{1,17},{9,25},{17,1},{25,9},{2,18},{10... | collective-permute-start | bytes 1376264 | tf_op jit(solution)/shard_map/ppermute | solution.py:379
  133.1 15.0 %collective-permute-start.39 = (bf16[112,2048]{1,0:T(8,128)(2,1)S(1)}, bf16[112,2048]{1,0:T(8,128)(2,1)S(1)}, u32[]{:S(2)}, u32[]{:S(2)}) collective-permute-start(bf16[112,2048]{1,0:T(8,128)(2,1)S(1)} %add_convert_fusion.2), channel_id=1, source_target_pairs={{0,2},{1,3},{2,4},{3,5},{4,6},{5,7},{6,0},{7,1},{8,10},{9,11},{10,... | collective-permute-start | bytes 1376264 | tf_op jit(solution)/shard_map/ppermute | solution.py:383
  134.6 13.9 %collective-permute-start.35 = (bf16[112,2048]{1,0:T(8,128)(2,1)S(1)}, bf16[112,2048]{1,0:T(8,128)(2,1)S(1)}, u32[]{:S(2)}, u32[]{:S(2)}) collective-permute-start(bf16[112,2048]{1,0:T(8,128)(2,1)S(1)} %get-tuple-element.189), channel_id=1, source_target_pairs={{0,8},{8,0},{16,24},{24,16},{1,9},{9,1},{17,25},{25,17},{2,10},{10... | collective-permute-start | bytes 1376264 | tf_op jit(solution)/shard_map/ppermute | solution.py:375
  136.9 11.6 %collective-permute-start.36 = (bf16[112,2048]{1,0:T(8,128)(2,1)S(1)}, bf16[112,2048]{1,0:T(8,128)(2,1)S(1)}, u32[]{:S(2)}, u32[]{:S(2)}) collective-permute-start(bf16[112,2048]{1,0:T(8,128)(2,1)S(1)} %get-tuple-element.190), channel_id=1, source_target_pairs={{0,16},{8,24},{16,0},{24,8},{1,17},{9,25},{17,1},{25,9},{2,18},{10... | collective-permute-start | bytes 1376264 | tf_op jit(solution)/shard_map/ppermute | solution.py:379
  148.5 10.3 %collective-permute-start.40 = (bf16[112,2048]{1,0:T(8,128)(2,1)S(1)}, bf16[112,2048]{1,0:T(8,128)(2,1)S(1)}, u32[]{:S(2)}, u32[]{:S(2)}) collective-permute-start(bf16[112,2048]{1,0:T(8,128)(2,1)S(1)} %add_convert_fusion.1), channel_id=1, source_target_pairs={{0,2},{1,3},{2,4},{3,5},{4,6},{5,7},{6,0},{7,1},{8,10},{9,11},{10,... | collective-permute-start | bytes 1376264 | tf_op jit(solution)/shard_map/ppermute | solution.py:383

commit v11 on v10

--- a/solution.py
+++ b/solution.py
@@ -456,11 +456,9 @@
     width = partial_proj.shape[1]
     ids_row = jnp.pad(ids[:1].astype(jnp.float32), ((0, 0), (0, width - ids.shape[1])))
     shared = jnp.concatenate([partial_proj, jnp.where(is_mine, ids_row, 0.0)], axis=0)
-    sides_0, block_1, other_gate, expert_up, shared = fence(
-        sides_0, block_1, other_gate, expert_up, shared
-    )
-
     shared = shared + along_x(shared)
+    sides_0, block_1, other_gate = fence(sides_0, block_1, other_gate)
+
     corner_0 = spread_corner(sides_0)
     other_up = across_chip(expert_up[0])
     corner_0, shared, block_1, other_up, expert_down = fence(
@@ -522,12 +520,12 @@
 
     far = added(sums_3[3], far).astype(jnp.bfloat16)
     passed_3 = return_corner(tuple(sums_3[:3]) + (far[:cut], far[cut:]))
-    passed_3, passed_0, sums_0 = fence(passed_3, passed_0, sums_0)
+    passed_3, carried_1 = fence(passed_3, carried_1)
     back_3 = return_sides(sums_3, passed_3)
     carried = around_z(added(sums_2[0], *back_2).astype(jnp.bfloat16))
-    back_3, carried_1 = fence(back_3, carried_1)
+    carried, passed_0, sums_0 = fence(carried, passed_0, sums_0)
+    back_0 = return_sides(sums_0, passed_0)
     carried = around_z(added(sums_3[0], *back_3, carried).astype(jnp.bfloat16))
-    back_0 = return_sides(sums_0, passed_0)
     return added(hidden, sums_0[0], carried_1, *back_0, carried).astype(jnp.bfloat16)[None]
 
 

time: 160 us -> 154 us (0.963)
  waiting for transfers between devices: 49.5 us -> 44.5 us
  local copies, waits for them, and re-layouts: 8.03 us -> 6.36 us
    ppermute x10, waiting for transfers between devices: 32.8 us -> 20.4 us  [around_z(): lax.ppermute(value, 'blk', [(i, (i + 2 * hops) % 8) for i in range(8)])]
    ppermute x14, waiting for transfers between devices: 1.84 us -> 6.62 us  [along_y(): return lax.ppermute(value, 'kv', [(i, i ^ 2) for i in range(4)])]
    ppermute x14, waiting for transfers between devices: 14.8 us -> 17.4 us  [along_x(): return lax.ppermute(value, 'kv', [(i, i ^ 1) for i in range(4)])]
    unnamed x28 -> x24, local copies, waits for them, and re-layouts: 7.7 us -> 6.02 us
  transfers between devices with their start and end apart: 41 -> 41, of which waited for: 15 -> 17; matrix products, arithmetic and copies ran while one was open for 5% -> 6% of each run, Pallas kernels for 30% -> 32%
where the time goes in v11:
time: 154 us
  Pallas kernels  50.1 us (33%)
  waiting for transfers between devices  44.5 us (29%)
  starting transfers between devices  42.5 us (28%)
  local copies, waits for them, and re-layouts  6.36 us (4%)
  other arithmetic  5.15 us (3%)
  matrix products  4.87 us (3%)
    pallas_call x4, Pallas kernels, run_plane(): pl.pallas_call(functools.partial(plane_kernel, cap, piece_rows, block_row...  47.8 us
    ppermute x10, waiting for transfers between devices, around_z(): lax.ppermute(value, 'blk', [(i, (i + 2 * hops) % 8) for i in range(8)])  20.4 us
    ppermute x14, waiting for transfers between devices, along_x(): return lax.ppermute(value, 'kv', [(i, i ^ 1) for i in range(4)])  17.4 us
    ppermute x14, starting transfers between devices, along_y(): return lax.ppermute(value, 'kv', [(i, i ^ 2) for i in range(4)])  16.2 us
    ppermute x14, starting transfers between devices, along_x(): return lax.ppermute(value, 'kv', [(i, i ^ 1) for i in range(4)])  14.7 us
    ppermute x10, starting transfers between devices, around_z(): lax.ppermute(value, 'blk', [(i, (i + 2 * hops) % 8) for i in range(8)])  11.1 us
    ppermute x14, waiting for transfers between devices, along_y(): return lax.ppermute(value, 'kv', [(i, i ^ 2) for i in range(4)])  6.62 us
    unnamed x24, local copies, waits for them, and re-layouts  6.02 us
  transfers between devices with their start and end apart: 41, of which 17 were waited for; matrix products, arithmetic and copies ran while one was open for 6% of the time, Pallas kernels for 32%

profile of v11, /device:TPU:0, one launch (start us, length us, event | category | flops | bytes accessed | tf_op | source)
XLA Modules:
  0.0 153.8 jit_solution(7442188521941730069)
XLA Ops:
  0.0 1.0 copy-done
  1.0 0.9 copy-done.2
  1.9 0.7 copy-done.4
  2.6 0.7 copy-done.6
  3.3 1.3 prepare.2.refs_1_
  4.6 3.1 %collective-permute-start.2 = (bf16[112,2176]{1,0:T(8,128)(2,1)S(1)}, bf16[112,2176]{1,0:T(8,128)(2,1)}, u32[]{:S(2)}, u32[]{:S(2)}) collective-permute-start(bf16[112,2176]{1,0:T(8,128)(2,1)S(1)} %prepare.2.refs_1_), channel_id=1, source_target_pairs={{0,2},{1,3},{2,4},{3,5},{4,6},{5,7},{6,0},{7,1},{8,10},{9,11},{10,... | collective-permute-start | bytes 1462280 | tf_op jit(solution)/shard_map/ppermute | solution.py:383
  7.7 1.5 collective-permute-start.1
  9.2 1.5 collective-permute-start
  11.2 0.7 minimum_subtract_fusion
  12.1 0.9 broadcast_in_dim.76
  12.9 1.0 convert_reduce_fusion
  13.9 3.5 %fusion.34 = (f32[4,8]{1,0:T(4,128)S(1)}, f32[4,8,4096]{2,1,0:T(8,128)S(1)}) fusion(bf16[4,4096,1,128]{3,1,2,0:T(8,128)(2,1)} %param.15, bf16[1,4,8,128]{3,1,2,0:T(4,128)(2,1)} %bitcast.53, pred[4,4096]{1,0:T(4,128)(4,1)S(1)} %iota_compare_fusion.1), kind=kOutput, calls=%fused_computation.58 | convolution fusion | flops 33947616 | bytes 4743296 | tf_op jit(solution)/shard_map/rgd,rjd->rgj/dot_general | solution.py:27
  17.7 0.7 fusion.10
  18.5 1.1 copy-done.10
  19.6 0.7 convolution_add_fusion
  20.3 0.7 collective-permute-done.2.refs_1_
  21.0 1.5 collective-permute-start.6
  22.5 0.6 collective-permute-start.5
  23.1 1.6 %collective-permute-start.4 = (bf16[64,2176]{1,0:T(8,128)(2,1)S(1)}, bf16[64,2176]{1,0:T(8,128)(2,1)S(1)}, u32[]{:S(2)}, u32[]{:S(2)}) collective-permute-start(bf16[64,2176]{1,0:T(8,128)(2,1)S(1)} %slice.43), channel_id=1, source_target_pairs={{0,16},{8,24},{16,0},{24,8},{1,17},{9,25},{17,1},{25,9},{2,18},{10... | collective-permute-start | bytes 835592 | tf_op jit(solution)/shard_map/ppermute | solution.py:379
  24.7 1.2 collective-permute-done.6
  25.9 3.2 %collective-permute-done.5.refs_5_ = bf16[48,2176]{1,0:T(8,128)(2,1)S(1)} collective-permute-done((bf16[48,2176]{1,0:T(8,128)(2,1)S(1)}, bf16[48,2176]{1,0:T(8,128)(2,1)S(1)}, u32[]{:S(2)}, u32[]{:S(2)}) %collective-permute-start.5) | collective-permute-done | bytes 208928 | tf_op jit(solution)/shard_map/ppermute | solution.py:375
  29.1 0.7 copy-done.7
  29.8 0.8 collective-permute-done.4.refs_4_
  30.6 1.1 collective-permute-start.8
  31.8 1.0 collective-permute-start.11
  32.8 1.5 collective-permute-start.10
  35.8 11.2 %collective-permute-done.11.refs_1_ = bf16[112,2176]{1,0:T(8,128)(2,1)S(1)} collective-permute-done((bf16[112,2176]{1,0:T(8,128)(2,1)}, bf16[112,2176]{1,0:T(8,128)(2,1)S(1)}, u32[]{:S(2)}, u32[]{:S(2)}) %collective-permute-start.11) | collective-permute-done | bytes 487456 | tf_op jit(solution)/shard_map/ppermute | solution.py:383
  47.2 0.9 collective-permute-start.16
  48.1 1.1 collective-permute-start.15
  49.2 1.0 collective-permute-start.14
  50.2 1.3 collective-permute-start.13
  51.5 1.6 %collective-permute-start.17 = (bf16[128,2176]{1,0:T(8,128)(2,1)S(1)}, bf16[128,2176]{1,0:T(8,128)(2,1)S(1)}, u32[]{:S(2)}, u32[]{:S(2)}) collective-permute-start(bf16[128,2176]{1,0:T(8,128)(2,1)S(1)} %pad_maximum_fusion), channel_id=1, source_target_pairs={{0,2},{1,3},{2,4},{3,5},{4,6},{5,7},{6,0},{7,1},{8,10},{9,11},{10,... | collective-permute-start | bytes 1671176 | tf_op jit(solution)/shard_map/ppermute | solution.py:383
  53.1 0.9 copy-done.8
  54.0 12.1 %plane.4 = (bf16[112,2048]{1,0:T(8,128)(2,1)S(1)}, bf16[112,2048]{1,0:T(8,128)(2,1)S(1)}, bf16[112,2048]{1,0:T(8,128)(2,1)S(1)}, bf16[64,2048]{1,0:T(8,128)(2,1)S(1)}, bf16[48,2048]{1,0:T(8,128)(2,1)S(1)}) custom-call(s32[3]{0:T(128)S(1)} %pad_add_fusion.refs_0_, bf16[112,2176]{1,0:T(8,128)(2,1)S(1)} %prepare.2.refs_1_, ...), custom_call_target="tpu_custom_call" | custom-call | flops 8455716864 | bytes 25165824 | tf_op jit(solution)/shard_map/plane/pallas_call | solution.py:313
  66.2 0.9 collective-permute-start.19
  67.1 1.1 collective-permute-start.18
  68.2 0.9 collective-permute-start.22
  69.1 1.2 collective-permute-start.21
  70.4 0.6 collective-permute-start.20
  71.0 11.7 %plane.5 = (bf16[112,2048]{1,0:T(8,128)(2,1)S(1)}, bf16[112,2048]{1,0:T(8,128)(2,1)S(1)}, bf16[112,2048]{1,0:T(8,128)(2,1)S(1)}, bf16[112,2048]{1,0:T(8,128)(2,1)S(1)}) custom-call(s32[3]{0:T(128)S(1)} %pad_add_fusion.refs_0_, bf16[112,2176]{1,0:T(8,128)(2,1)} %collective-permute-done.2.refs_1_, bf16[112,2176]{1,0:T(8,128)(2,1)S(1)} %collective-permute-done.9.refs_2_, ...), custom_call_target="tpu_custom_call" | custom-call | flops 8455716864 | bytes 25165824 | tf_op jit(solution)/shard_map/plane/pallas_call | solution.py:313
  82.8 0.9 collective-permute-done.20.refs_4_
  83.7 0.6 collective-permute-start.23
  84.3 1.2 collective-permute-start.26
  85.5 1.6 %collective-permute-start.25 = (bf16[64,2176]{1,0:T(8,128)(2,1)S(1)}, bf16[64,2176]{1,0:T(8,128)(2,1)S(1)}, u32[]{:S(2)}, u32[]{:S(2)}) collective-permute-start(bf16[64,2176]{1,0:T(8,128)(2,1)S(1)} %slice.53), channel_id=1, source_target_pairs={{0,16},{8,24},{16,0},{24,8},{1,17},{9,25},{17,1},{25,9},{2,18},{10... | collective-permute-start | bytes 835592 | tf_op jit(solution)/shard_map/ppermute | solution.py:379
  87.6 0.9 collective-permute-start.28
  88.5 1.9 %collective-permute-done.23.refs_6_ = bf16[16,2176]{1,0:T(8,128)(2,1)S(1)} collective-permute-done((bf16[16,2176]{1,0:T(8,128)(2,1)S(1)}, bf16[16,2176]{1,0:T(8,128)(2,1)S(1)}, u32[]{:S(2)}, u32[]{:S(2)}) %collective-permute-start.23) | collective-permute-done | bytes 69664 | tf_op jit(solution)/shard_map/ppermute | solution.py:383
  90.4 12.0 %plane.6 = (bf16[112,2048]{1,0:T(8,128)(2,1)S(1)}, bf16[112,2048]{1,0:T(8,128)(2,1)S(1)}, bf16[112,2048]{1,0:T(8,128)(2,1)S(1)}, bf16[112,2048]{1,0:T(8,128)(2,1)S(1)}) custom-call(s32[3]{0:T(128)S(1)} %pad_add_fusion.refs_0_, bf16[112,2176]{1,0:T(8,128)(2,1)S(1)} %collective-permute-done.11.refs_1_, bf16[112,2176]{1,0:T(8,128)(2,1)S(1)} %collective-permute-done.15.refs_2_, ...), custom_call_target="tpu_custom_call" | custom-call | flops 8455716864 | bytes 25165824 | tf_op jit(solution)/shard_map/plane/pallas_call | solution.py:313
  102.8 1.3 collective-permute-start.29
  104.0 2.9 %collective-permute-start.35 = (bf16[112,2048]{1,0:T(8,128)(2,1)S(1)}, bf16[112,2048]{1,0:T(8,128)(2,1)S(1)}, u32[]{:S(2)}, u32[]{:S(2)}) collective-permute-start(bf16[112,2048]{1,0:T(8,128)(2,1)S(1)} %get-tuple-element.173), channel_id=1, source_target_pairs={{0,6},{1,7},{2,0},{3,1},{4,2},{5,3},{6,4},{7,5},{8,14},{9,15},{10,... | collective-permute-start | bytes 1376264 | tf_op jit(solution)/shard_map/ppermute | solution.py:383
  107.0 1.4 collective-permute-start.30
  108.9 12.0 %plane.7 = (bf16[112,2048]{1,0:T(8,128)(2,1)S(1)}, bf16[112,2048]{1,0:T(8,128)(2,1)S(1)}, bf16[112,2048]{1,0:T(8,128)(2,1)S(1)}, bf16[112,2048]{1,0:T(8,128)(2,1)S(1)}) custom-call(s32[3]{0:T(128)S(1)} %pad_add_fusion.refs_0_, bf16[112,2176]{1,0:T(8,128)(2,1)S(1)} %slice.50.refs_1_, bf16[112,2176]{1,0:T(8,128)(2,1)S(1)} %collective-permute-done.18.refs_2_, ...), custom_call_target="tpu_custom_call" | custom-call | flops 8455716864 | bytes 25165824 | tf_op jit(solution)/shard_map/plane/pallas_call | solution.py:313
  121.1 1.0 collective-permute-start.34
  122.1 1.2 collective-permute-start.33
  123.6 5.4 %collective-permute-done.34.passed_1_ref = bf16[48,2048]{1,0:T(8,128)(2,1)S(1)} collective-permute-done((bf16[48,2048]{1,0:T(8,128)(2,1)S(1)}, bf16[48,2048]{1,0:T(8,128)(2,1)S(1)}, u32[]{:S(2)}, u32[]{:S(2)}) %collective-permute-start.34) | collective-permute-done | bytes 196640 | tf_op jit(solution)/shard_map/ppermute | solution.py:375
  129.0 2.3 %collective-permute-done.33.passed_0_ref = bf16[64,2048]{1,0:T(8,128)(2,1)S(1)} collective-permute-done((bf16[64,2048]{1,0:T(8,128)(2,1)S(1)}, bf16[64,2048]{1,0:T(8,128)(2,1)S(1)}, u32[]{:S(2)}, u32[]{:S(2)}) %collective-permute-start.33) | collective-permute-done | bytes 262176 | tf_op jit(solution)/shard_map/ppermute | solution.py:379
  131.4 1.2 collective-permute-start.38
  132.6 1.5 collective-permute-start.39
  134.3 1.1 collective-permute-start.36
  135.9 4.5 %collective-permute-done.38 = bf16[112,2048]{1,0:T(8,128)(2,1)S(1)} collective-permute-done((bf16[112,2048]{1,0:T(8,128)(2,1)S(1)}, bf16[112,2048]{1,0:T(8,128)(2,1)S(1)}, u32[]{:S(2)}, u32[]{:S(2)}) %collective-permute-start.38) | collective-permute-done | bytes 458784 | tf_op jit(solution)/shard_map/ppermute | solution.py:375
  140.4 1.5 collective-permute-done.39
  142.3 3.0 %collective-permute-done.36 = bf16[112,2048]{1,0:T(8,128)(2,1)S(1)} collective-permute-done((bf16[112,2048]{1,0:T(8,128)(2,1)S(1)}, bf16[112,2048]{1,0:T(8,128)(2,1)S(1)}, u32[]{:S(2)}, u32[]{:S(2)}) %collective-permute-start.36) | collective-permute-done | bytes 458784 | tf_op jit(solution)/shard_map/ppermute | solution.py:375
  145.4 1.5 collective-permute-done.37
  146.9 5.7 %collective-permute-done.40 = bf16[112,2048]{1,0:T(8,128)(2,1)S(1)} collective-permute-done((bf16[112,2048]{1,0:T(8,128)(2,1)S(1)}, bf16[112,2048]{1,0:T(8,128)(2,1)S(1)}, u32[]{:S(2)}, u32[]{:S(2)}) %collective-permute-start.40) | collective-permute-done | bytes 458784 | tf_op jit(solution)/shard_map/ppermute | solution.py:383
  152.6 1.2 fusion.13
  (91 shorter events, 5.9 us)
Async XLA Ops:
  0.0 17.4 %copy-start.11 = (f32[8]{0:T(128)S(1)}, f32[8]{0:T(128)}, u32[]{:S(2)}) copy-start(f32[8]{0:T(128)} %param.18) | copy-start | bytes 100
  0.0 1.0 copy-start
  1.0 0.9 copy-start.2
  1.9 0.7 copy-start.4
  2.6 0.7 copy-start.6
  4.6 16.3 %collective-permute-start.2 = (bf16[112,2176]{1,0:T(8,128)(2,1)S(1)}, bf16[112,2176]{1,0:T(8,128)(2,1)}, u32[]{:S(2)}, u32[]{:S(2)}) collective-permute-start(bf16[112,2176]{1,0:T(8,128)(2,1)S(1)} %prepare.2.refs_1_), channel_id=1, source_target_pairs={{0,2},{1,3},{2,4},{3,5},{4,6},{5,7},{6,0},{7,1},{8,10},{9,11},{10,... | collective-permute-start | bytes 1462280 | tf_op jit(solution)/shard_map/ppermute | solution.py:383
  7.7 14.8 %collective-permute-start.1 = (bf16[112,2176]{1,0:T(8,128)(2,1)S(1)}, bf16[112,2176]{1,0:T(8,128)(2,1)S(1)}, u32[]{:S(2)}, u32[]{:S(2)}) collective-permute-start(bf16[112,2176]{1,0:T(8,128)(2,1)S(1)} %prepare.2.refs_1_), channel_id=1, source_target_pairs={{0,16},{8,24},{16,0},{24,8},{1,17},{9,25},{17,1},{25,9},{2,18},{10... | collective-permute-start | bytes 1462280 | tf_op jit(solution)/shard_map/ppermute | solution.py:379
  9.2 13.2 %collective-permute-start = (bf16[112,2176]{1,0:T(8,128)(2,1)S(1)}, bf16[112,2176]{1,0:T(8,128)(2,1)S(1)}, u32[]{:S(2)}, u32[]{:S(2)}) collective-permute-start(bf16[112,2176]{1,0:T(8,128)(2,1)S(1)} %prepare.2.refs_1_), channel_id=1, source_target_pairs={{0,8},{8,0},{16,24},{24,16},{1,9},{9,1},{17,25},{25,17},{2,10},{10... | collective-permute-start | bytes 1462280 | tf_op jit(solution)/shard_map/ppermute | solution.py:375
  10.7 11.8 %collective-permute-start.3 = (bf16[2048,768]{1,0:T(8,128)(2,1)}, bf16[2048,768]{1,0:T(8,128)(2,1)}, u32[]{:S(2)}, u32[]{:S(2)}) collective-permute-start(bf16[2048,768]{1,0:T(8,128)(2,1)} %bitcast.55), channel_id=1, source_target_pairs={{0,1},{1,0},{2,3},{3,2},{4,5},{5,4},{6,7},{7,6},{8,9},{9,8},{10,11... | collective-permute-start | bytes 9437192 | tf_op jit(solution)/shard_map/ppermute | solution.py:387
  10.7 15.2 %collective-permute-start.7 = (bf16[2048,768]{1,0:T(8,128)(2,1)}, bf16[2048,768]{1,0:T(8,128)(2,1)}, u32[]{:S(2)}, u32[]{:S(2)}) collective-permute-start(bf16[2048,768]{1,0:T(8,128)(2,1)} %bitcast.60), channel_id=1, source_target_pairs={{0,1},{1,0},{2,3},{3,2},{4,5},{5,4},{6,7},{7,6},{8,9},{9,8},{10,11... | collective-permute-start | bytes 9437192 | tf_op jit(solution)/shard_map/ppermute | solution.py:387
  12.0 5.7 %copy-start.9 = (bf16[4,4096,1,128]{3,1,2,0:T(8,128)(2,1)S(1)}, bf16[4,4096,1,128]{3,1,2,0:T(8,128)(2,1)}, u32[]{:S(2)}) copy-start(bf16[4,4096,1,128]{3,1,2,0:T(8,128)(2,1)} %param.16) | copy-start | bytes 12582916
  17.4 2.2 %copy-start.10 = (bf16[1024,2048]{1,0:T(8,128)(2,1)S(1)}, bf16[1024,2048]{1,0:T(8,128)(2,1)}, u32[]{:S(2)}) copy-start(bf16[1024,2048]{1,0:T(8,128)(2,1)} %param.19) | copy-start | bytes 12582916
  18.4 16.9 %copy-start.3 = (bf16[2048,32]{0,1:T(8,128)(2,1)S(1)}, bf16[2048,32]{0,1:T(8,128)(2,1)}, u32[]{:S(2)}) copy-start(bf16[2048,32]{0,1:T(8,128)(2,1)} %param.23) | copy-start | bytes 393220
  18.5 16.9 %copy-start.5 = (f32[2048]{0:T(1024)S(1)}, f32[2048]{0:T(1024)}, u32[]{:S(2)}) copy-start(f32[2048]{0:T(1024)} %param.22) | copy-start | bytes 24580
  21.0 4.9 %collective-permute-start.6 = (f32[8,2048]{1,0:T(8,128)S(1)}, f32[8,2048]{1,0:T(8,128)S(1)}, u32[]{:S(2)}, u32[]{:S(2)}) collective-permute-start(f32[8,2048]{1,0:T(8,128)S(1)} %pad_maximum_fusion.2), channel_id=1, source_target_pairs={{0,8},{8,0},{16,24},{24,16},{1,9},{9,1},{17,25},{25,17},{2,10},{10... | collective-permute-start | bytes 196616 | tf_op jit(solution)/shard_map/ppermute | solution.py:375
  22.5 6.6 %collective-permute-start.5 = (bf16[48,2176]{1,0:T(8,128)(2,1)S(1)}, bf16[48,2176]{1,0:T(8,128)(2,1)S(1)}, u32[]{:S(2)}, u32[]{:S(2)}) collective-permute-start(bf16[48,2176]{1,0:T(8,128)(2,1)S(1)} %slice.44), channel_id=1, source_target_pairs={{0,8},{8,0},{16,24},{24,16},{1,9},{9,1},{17,25},{25,17},{2,10},{10... | collective-permute-start | bytes 626696 | tf_op jit(solution)/shard_map/ppermute | solution.py:375
  23.1 7.5 %collective-permute-start.4 = (bf16[64,2176]{1,0:T(8,128)(2,1)S(1)}, bf16[64,2176]{1,0:T(8,128)(2,1)S(1)}, u32[]{:S(2)}, u32[]{:S(2)}) collective-permute-start(bf16[64,2176]{1,0:T(8,128)(2,1)S(1)} %slice.43), channel_id=1, source_target_pairs={{0,16},{8,24},{16,0},{24,8},{1,17},{9,25},{17,1},{25,9},{2,18},{10... | collective-permute-start | bytes 835592 | tf_op jit(solution)/shard_map/ppermute | solution.py:379
  29.1 0.7 copy-start.7
  30.6 16.6 %collective-permute-start.12 = (bf16[768,2048]{1,0:T(8,128)(2,1)}, bf16[768,2048]{1,0:T(8,128)(2,1)}, u32[]{:S(2)}, u32[]{:S(2)}) collective-permute-start(bf16[768,2048]{1,0:T(8,128)(2,1)} %bitcast.12.refs_9_.refs_7_), channel_id=1, source_target_pairs={{0,1},{1,0},{2,3},{3,2},{4,5},{5,4},{6,7},{7,6},{8,9},{9,8},{10,11... | collective-permute-start | bytes 9437192 | tf_op jit(solution)/shard_map/ppermute | solution.py:387
  30.6 4.5 %collective-permute-start.8 = (f32[8,2048]{1,0:T(8,128)S(1)}, f32[8,2048]{1,0:T(8,128)S(1)}, u32[]{:S(2)}, u32[]{:S(2)}) collective-permute-start(f32[8,2048]{1,0:T(8,128)S(1)} %fusion.33), channel_id=1, source_target_pairs={{0,16},{8,24},{16,0},{24,8},{1,17},{9,25},{17,1},{25,9},{2,18},{10... | collective-permute-start | bytes 196616 | tf_op jit(solution)/shard_map/ppermute | solution.py:379
  31.8 15.3 %collective-permute-start.11 = (bf16[112,2176]{1,0:T(8,128)(2,1)}, bf16[112,2176]{1,0:T(8,128)(2,1)S(1)}, u32[]{:S(2)}, u32[]{:S(2)}) collective-permute-start(bf16[112,2176]{1,0:T(8,128)(2,1)} %collective-permute-done.2.refs_1_), channel_id=1, source_target_pairs={{0,2},{1,3},{2,4},{3,5},{4,6},{5,7},{6,0},{7,1},{8,10},{9,11},{10,... | collective-permute-start | bytes 1462280 | tf_op jit(solution)/shard_map/ppermute | solution.py:383
  32.8 14.3 %collective-permute-start.10 = (bf16[112,2176]{1,0:T(8,128)(2,1)}, bf16[112,2176]{1,0:T(8,128)(2,1)S(1)}, u32[]{:S(2)}, u32[]{:S(2)}) collective-permute-start(bf16[112,2176]{1,0:T(8,128)(2,1)} %collective-permute-done.2.refs_1_), channel_id=1, source_target_pairs={{0,16},{8,24},{16,0},{24,8},{1,17},{9,25},{17,1},{25,9},{2,18},{10... | collective-permute-start | bytes 1462280 | tf_op jit(solution)/shard_map/ppermute | solution.py:379
  34.3 12.9 %collective-permute-start.9 = (bf16[112,2176]{1,0:T(8,128)(2,1)}, bf16[112,2176]{1,0:T(8,128)(2,1)S(1)}, u32[]{:S(2)}, u32[]{:S(2)}) collective-permute-start(bf16[112,2176]{1,0:T(8,128)(2,1)} %collective-permute-done.2.refs_1_), channel_id=1, source_target_pairs={{0,8},{8,0},{16,24},{24,16},{1,9},{9,1},{17,25},{25,17},{2,10},{10... | collective-permute-start | bytes 1462280 | tf_op jit(solution)/shard_map/ppermute | solution.py:375
  47.2 18.9 %collective-permute-start.16 = (bf16[112,2176]{1,0:T(8,128)(2,1)S(1)}, bf16[112,2176]{1,0:T(8,128)(2,1)S(1)}, u32[]{:S(2)}, u32[]{:S(2)}) collective-permute-start(bf16[112,2176]{1,0:T(8,128)(2,1)S(1)} %collective-permute-done.11.refs_1_), channel_id=1, source_target_pairs={{0,16},{8,24},{16,0},{24,8},{1,17},{9,25},{17,1},{25,9},{2,18},{10... | collective-permute-start | bytes 1462280 | tf_op jit(solution)/shard_map/ppermute | solution.py:379
  48.1 18.1 %collective-permute-start.15 = (bf16[112,2176]{1,0:T(8,128)(2,1)S(1)}, bf16[112,2176]{1,0:T(8,128)(2,1)S(1)}, u32[]{:S(2)}, u32[]{:S(2)}) collective-permute-start(bf16[112,2176]{1,0:T(8,128)(2,1)S(1)} %collective-permute-done.11.refs_1_), channel_id=1, source_target_pairs={{0,8},{8,0},{16,24},{24,16},{1,9},{9,1},{17,25},{25,17},{2,10},{10... | collective-permute-start | bytes 1462280 | tf_op jit(solution)/shard_map/ppermute | solution.py:375
  49.2 16.9 %collective-permute-start.14 = (bf16[48,2176]{1,0:T(8,128)(2,1)S(1)}, bf16[48,2176]{1,0:T(8,128)(2,1)S(1)}, u32[]{:S(2)}, u32[]{:S(2)}) collective-permute-start(bf16[48,2176]{1,0:T(8,128)(2,1)S(1)} %slice.49), channel_id=1, source_target_pairs={{0,8},{8,0},{16,24},{24,16},{1,9},{9,1},{17,25},{25,17},{2,10},{10... | collective-permute-start | bytes 626696 | tf_op jit(solution)/shard_map/ppermute | solution.py:375
  50.2 15.9 %collective-permute-start.13 = (bf16[64,2176]{1,0:T(8,128)(2,1)S(1)}, bf16[64,2176]{1,0:T(8,128)(2,1)S(1)}, u32[]{:S(2)}, u32[]{:S(2)}) collective-permute-start(bf16[64,2176]{1,0:T(8,128)(2,1)S(1)} %slice.48), channel_id=1, source_target_pairs={{0,16},{8,24},{16,0},{24,8},{1,17},{9,25},{17,1},{25,9},{2,18},{10... | collective-permute-start | bytes 835592 | tf_op jit(solution)/shard_map/ppermute | solution.py:379
  51.5 14.7 %collective-permute-start.17 = (bf16[128,2176]{1,0:T(8,128)(2,1)S(1)}, bf16[128,2176]{1,0:T(8,128)(2,1)S(1)}, u32[]{:S(2)}, u32[]{:S(2)}) collective-permute-start(bf16[128,2176]{1,0:T(8,128)(2,1)S(1)} %pad_maximum_fusion), channel_id=1, source_target_pairs={{0,2},{1,3},{2,4},{3,5},{4,6},{5,7},{6,0},{7,1},{8,10},{9,11},{10,... | collective-permute-start | bytes 1671176 | tf_op jit(solution)/shard_map/ppermute | solution.py:383
  53.1 0.9 copy-start.8
  66.2 16.6 %collective-permute-start.19 = (bf16[112,2176]{1,0:T(8,128)(2,1)S(1)}, bf16[112,2176]{1,0:T(8,128)(2,1)S(1)}, u32[]{:S(2)}, u32[]{:S(2)}) collective-permute-start(bf16[112,2176]{1,0:T(8,128)(2,1)S(1)} %slice.50.refs_1_), channel_id=1, source_target_pairs={{0,16},{8,24},{16,0},{24,8},{1,17},{9,25},{17,1},{25,9},{2,18},{10... | collective-permute-start | bytes 1462280 | tf_op jit(solution)/shard_map/ppermute | solution.py:379
  67.1 15.7 %collective-permute-start.18 = (bf16[112,2176]{1,0:T(8,128)(2,1)S(1)}, bf16[112,2176]{1,0:T(8,128)(2,1)S(1)}, u32[]{:S(2)}, u32[]{:S(2)}) collective-permute-start(bf16[112,2176]{1,0:T(8,128)(2,1)S(1)} %slice.50.refs_1_), channel_id=1, source_target_pairs={{0,8},{8,0},{16,24},{24,16},{1,9},{9,1},{17,25},{25,17},{2,10},{10... | collective-permute-start | bytes 1462280 | tf_op jit(solution)/shard_map/ppermute | solution.py:375
  68.2 14.5 %collective-permute-start.22 = (bf16[48,2048]{1,0:T(8,128)(2,1)S(1)}, bf16[48,2048]{1,0:T(8,128)(2,1)S(1)}, u32[]{:S(2)}, u32[]{:S(2)}) collective-permute-start(bf16[48,2048]{1,0:T(8,128)(2,1)S(1)} %get-tuple-element.125), channel_id=1, source_target_pairs={{0,8},{8,0},{16,24},{24,16},{1,9},{9,1},{17,25},{25,17},{2,10},{10... | collective-permute-start | bytes 589832 | tf_op jit(solution)/shard_map/ppermute | solution.py:375
  69.1 13.7 %collective-permute-start.21 = (bf16[64,2048]{1,0:T(8,128)(2,1)S(1)}, bf16[64,2048]{1,0:T(8,128)(2,1)S(1)}, u32[]{:S(2)}, u32[]{:S(2)}) collective-permute-start(bf16[64,2048]{1,0:T(8,128)(2,1)S(1)} %get-tuple-element.124), channel_id=1, source_target_pairs={{0,16},{8,24},{16,0},{24,8},{1,17},{9,25},{17,1},{25,9},{2,18},{10... | collective-permute-start | bytes 786440 | tf_op jit(solution)/shard_map/ppermute | solution.py:379
  70.4 13.3 %collective-permute-start.20 = (bf16[128,2176]{1,0:T(8,128)(2,1)S(1)}, bf16[128,2176]{1,0:T(8,128)(2,1)S(1)}, u32[]{:S(2)}, u32[]{:S(2)}) collective-permute-start(bf16[128,2176]{1,0:T(8,128)(2,1)S(1)} %pad_maximum_fusion.1), channel_id=1, source_target_pairs={{0,2},{1,3},{2,4},{3,5},{4,6},{5,7},{6,0},{7,1},{8,10},{9,11},{10,... | collective-permute-start | bytes 1671176 | tf_op jit(solution)/shard_map/ppermute | solution.py:383
  83.7 6.7 %collective-permute-start.23 = (bf16[16,2176]{1,0:T(8,128)(2,1)S(1)}, bf16[16,2176]{1,0:T(8,128)(2,1)S(1)}, u32[]{:S(2)}, u32[]{:S(2)}) collective-permute-start(bf16[16,2176]{1,0:T(8,128)(2,1)S(1)} %slice.52), channel_id=1, source_target_pairs={{0,2},{1,3},{2,4},{3,5},{4,6},{5,7},{6,0},{7,1},{8,10},{9,11},{10,... | collective-permute-start | bytes 208904 | tf_op jit(solution)/shard_map/ppermute | solution.py:383
  84.3 18.2 %collective-permute-start.26 = (bf16[48,2176]{1,0:T(8,128)(2,1)S(1)}, bf16[48,2176]{1,0:T(8,128)(2,1)S(1)}, u32[]{:S(2)}, u32[]{:S(2)}) collective-permute-start(bf16[48,2176]{1,0:T(8,128)(2,1)S(1)} %slice.54), channel_id=1, source_target_pairs={{0,8},{8,0},{16,24},{24,16},{1,9},{9,1},{17,25},{25,17},{2,10},{10... | collective-permute-start | bytes 626696 | tf_op jit(solution)/shard_map/ppermute | solution.py:375
  85.5 17.0 %collective-permute-start.25 = (bf16[64,2176]{1,0:T(8,128)(2,1)S(1)}, bf16[64,2176]{1,0:T(8,128)(2,1)S(1)}, u32[]{:S(2)}, u32[]{:S(2)}) collective-permute-start(bf16[64,2176]{1,0:T(8,128)(2,1)S(1)} %slice.53), channel_id=1, source_target_pairs={{0,16},{8,24},{16,0},{24,8},{1,17},{9,25},{17,1},{25,9},{2,18},{10... | collective-permute-start | bytes 835592 | tf_op jit(solution)/shard_map/ppermute | solution.py:379
  87.1 15.4 %collective-permute-start.27 = (bf16[112,2048]{1,0:T(8,128)(2,1)S(1)}, bf16[112,2048]{1,0:T(8,128)(2,1)S(1)}, u32[]{:S(2)}, u32[]{:S(2)}) collective-permute-start(bf16[112,2048]{1,0:T(8,128)(2,1)S(1)} %get-tuple-element.139), channel_id=1, source_target_pairs={{0,8},{8,0},{16,24},{24,16},{1,9},{9,1},{17,25},{25,17},{2,10},{10... | collective-permute-start | bytes 1376264 | tf_op jit(solution)/shard_map/ppermute | solution.py:375
  87.6 14.9 %collective-permute-start.28 = (bf16[112,2048]{1,0:T(8,128)(2,1)S(1)}, bf16[112,2048]{1,0:T(8,128)(2,1)S(1)}, u32[]{:S(2)}, u32[]{:S(2)}) collective-permute-start(bf16[112,2048]{1,0:T(8,128)(2,1)S(1)} %get-tuple-element.140), channel_id=1, source_target_pairs={{0,16},{8,24},{16,0},{24,8},{1,17},{9,25},{17,1},{25,9},{2,18},{10... | collective-permute-start | bytes 1376264 | tf_op jit(solution)/shard_map/ppermute | solution.py:379
  90.4 12.1 %collective-permute-start.24 = (bf16[112,2048]{1,0:T(8,128)(2,1)S(1)}, bf16[112,2048]{1,0:T(8,128)(2,1)S(1)}, u32[]{:S(2)}, u32[]{:S(2)}) collective-permute-start(bf16[112,2048]{1,0:T(8,128)(2,1)S(1)} %get-tuple-element.136), channel_id=1, source_target_pairs={{0,2},{1,3},{2,4},{3,5},{4,6},{5,7},{6,0},{7,1},{8,10},{9,11},{10,... | collective-permute-start | bytes 1376264 | tf_op jit(solution)/shard_map/ppermute | solution.py:383
  102.8 18.1 %collective-permute-start.29 = (bf16[112,2048]{1,0:T(8,128)(2,1)S(1)}, bf16[112,2048]{1,0:T(8,128)(2,1)S(1)}, u32[]{:S(2)}, u32[]{:S(2)}) collective-permute-start(bf16[112,2048]{1,0:T(8,128)(2,1)S(1)} %get-tuple-element.153), channel_id=1, source_target_pairs={{0,2},{1,3},{2,4},{3,5},{4,6},{5,7},{6,0},{7,1},{8,10},{9,11},{10,... | collective-permute-start | bytes 1376264 | tf_op jit(solution)/shard_map/ppermute | solution.py:383
  104.0 19.5 %collective-permute-start.35 = (bf16[112,2048]{1,0:T(8,128)(2,1)S(1)}, bf16[112,2048]{1,0:T(8,128)(2,1)S(1)}, u32[]{:S(2)}, u32[]{:S(2)}) collective-permute-start(bf16[112,2048]{1,0:T(8,128)(2,1)S(1)} %get-tuple-element.173), channel_id=1, source_target_pairs={{0,6},{1,7},{2,0},{3,1},{4,2},{5,3},{6,4},{7,5},{8,14},{9,15},{10,... | collective-permute-start | bytes 1376264 | tf_op jit(solution)/shard_map/ppermute | solution.py:383
  107.0 16.3 %collective-permute-start.30 = (bf16[112,2048]{1,0:T(8,128)(2,1)S(1)}, bf16[112,2048]{1,0:T(8,128)(2,1)S(1)}, u32[]{:S(2)}, u32[]{:S(2)}) collective-permute-start(bf16[112,2048]{1,0:T(8,128)(2,1)S(1)} %get-tuple-element.155), channel_id=1, source_target_pairs={{0,8},{8,0},{16,24},{24,16},{1,9},{9,1},{17,25},{25,17},{2,10},{10... | collective-permute-start | bytes 1376264 | tf_op jit(solution)/shard_map/ppermute | solution.py:375
  108.4 14.9 %collective-permute-start.31 = (bf16[112,2048]{1,0:T(8,128)(2,1)S(1)}, bf16[112,2048]{1,0:T(8,128)(2,1)S(1)}, u32[]{:S(2)}, u32[]{:S(2)}) collective-permute-start(bf16[112,2048]{1,0:T(8,128)(2,1)S(1)} %get-tuple-element.156), channel_id=1, source_target_pairs={{0,16},{8,24},{16,0},{24,8},{1,17},{9,25},{17,1},{25,9},{2,18},{10... | collective-permute-start | bytes 1376264 | tf_op jit(solution)/shard_map/ppermute | solution.py:379
  121.1 31.5 %copy-start.1 = (bf16[1,111,2048]{2,1,0:T(8,128)(2,1)S(1)}, bf16[1,111,2048]{2,1,0:T(8,128)(2,1)}, u32[]{:S(2)}) copy-start(bf16[1,111,2048]{2,1,0:T(8,128)(2,1)} %param.21) | copy-start | bytes 1363972
  121.1 7.9 %collective-permute-start.34 = (bf16[48,2048]{1,0:T(8,128)(2,1)S(1)}, bf16[48,2048]{1,0:T(8,128)(2,1)S(1)}, u32[]{:S(2)}, u32[]{:S(2)}) collective-permute-start(bf16[48,2048]{1,0:T(8,128)(2,1)S(1)} %slice.58), channel_id=1, source_target_pairs={{0,8},{8,0},{16,24},{24,16},{1,9},{9,1},{17,25},{25,17},{2,10},{10... | collective-permute-start | bytes 589832 | tf_op jit(solution)/shard_map/ppermute | solution.py:375
  122.1 9.2 %collective-permute-start.33 = (bf16[64,2048]{1,0:T(8,128)(2,1)S(1)}, bf16[64,2048]{1,0:T(8,128)(2,1)S(1)}, u32[]{:S(2)}, u32[]{:S(2)}) collective-permute-start(bf16[64,2048]{1,0:T(8,128)(2,1)S(1)} %slice.57), channel_id=1, source_target_pairs={{0,16},{8,24},{16,0},{24,8},{1,17},{9,25},{17,1},{25,9},{2,18},{10... | collective-permute-start | bytes 786440 | tf_op jit(solution)/shard_map/ppermute | solution.py:379
  123.5 10.7 %collective-permute-start.32 = (bf16[112,2048]{1,0:T(8,128)(2,1)S(1)}, bf16[112,2048]{1,0:T(8,128)(2,1)S(1)}, u32[]{:S(2)}, u32[]{:S(2)}) collective-permute-start(bf16[112,2048]{1,0:T(8,128)(2,1)S(1)} %add_convert_fusion.3), channel_id=1, source_target_pairs={{0,2},{1,3},{2,4},{3,5},{4,6},{5,7},{6,0},{7,1},{8,10},{9,11},{10,... | collective-permute-start | bytes 1376264 | tf_op jit(solution)/shard_map/ppermute | solution.py:383
  131.4 9.0 %collective-permute-start.38 = (bf16[112,2048]{1,0:T(8,128)(2,1)S(1)}, bf16[112,2048]{1,0:T(8,128)(2,1)S(1)}, u32[]{:S(2)}, u32[]{:S(2)}) collective-permute-start(bf16[112,2048]{1,0:T(8,128)(2,1)S(1)} %get-tuple-element.186), channel_id=1, source_target_pairs={{0,8},{8,0},{16,24},{24,16},{1,9},{9,1},{17,25},{25,17},{2,10},{10... | collective-permute-start | bytes 1376264 | tf_op jit(solution)/shard_map/ppermute | solution.py:375
  132.6 9.4 %collective-permute-start.39 = (bf16[112,2048]{1,0:T(8,128)(2,1)S(1)}, bf16[112,2048]{1,0:T(8,128)(2,1)S(1)}, u32[]{:S(2)}, u32[]{:S(2)}) collective-permute-start(bf16[112,2048]{1,0:T(8,128)(2,1)S(1)} %get-tuple-element.187), channel_id=1, source_target_pairs={{0,16},{8,24},{16,0},{24,8},{1,17},{9,25},{17,1},{25,9},{2,18},{10... | collective-permute-start | bytes 1376264 | tf_op jit(solution)/shard_map/ppermute | solution.py:379
  134.3 11.1 %collective-permute-start.36 = (bf16[112,2048]{1,0:T(8,128)(2,1)S(1)}, bf16[112,2048]{1,0:T(8,128)(2,1)S(1)}, u32[]{:S(2)}, u32[]{:S(2)}) collective-permute-start(bf16[112,2048]{1,0:T(8,128)(2,1)S(1)} %get-tuple-element.179), channel_id=1, source_target_pairs={{0,8},{8,0},{16,24},{24,16},{1,9},{9,1},{17,25},{25,17},{2,10},{10... | collective-permute-start | bytes 1376264 | tf_op jit(solution)/shard_map/ppermute | solution.py:375
  135.4 11.5 %collective-permute-start.37 = (bf16[112,2048]{1,0:T(8,128)(2,1)S(1)}, bf16[112,2048]{1,0:T(8,128)(2,1)S(1)}, u32[]{:S(2)}, u32[]{:S(2)}) collective-permute-start(bf16[112,2048]{1,0:T(8,128)(2,1)S(1)} %get-tuple-element.180), channel_id=1, source_target_pairs={{0,16},{8,24},{16,0},{24,8},{1,17},{9,25},{17,1},{25,9},{2,18},{10... | collective-permute-start | bytes 1376264 | tf_op jit(solution)/shard_map/ppermute | solution.py:379
  142.3 10.3 %collective-permute-start.40 = (bf16[112,2048]{1,0:T(8,128)(2,1)S(1)}, bf16[112,2048]{1,0:T(8,128)(2,1)S(1)}, u32[]{:S(2)}, u32[]{:S(2)}) collective-permute-start(bf16[112,2048]{1,0:T(8,128)(2,1)S(1)} %add_convert_fusion.1), channel_id=1, source_target_pairs={{0,2},{1,3},{2,4},{3,5},{4,6},{5,7},{6,0},{7,1},{8,10},{9,11},{10,... | collective-permute-start | bytes 1376264 | tf_op jit(solution)/shard_map/ppermute | solution.py:383

commit v12 on v11

--- a/solution.py
+++ b/solution.py
@@ -178,20 +178,20 @@
     pair_rows = 2 * tokens
     pair_slots = 2 * cap
     few = decodes.shape[0]
-    row_copies = []
+    row_copies = ([], [])
     at = 0
     for ref, count in zip(sources, piece_rows):
         if ref is sources[-1]:
             count -= few
+            copy = pltpu.make_async_copy(ref.at[pl.ds(count, few)], decodes, row_sem.at[len(sources)])
+            row_copies[0].append(copy)
+        if count:
+            p = 0 if at < pair_rows else 1
+            index = len(row_copies[0]) + len(row_copies[1]) if ref is not sources[-1] else len(sources) - 1
             copy = pltpu.make_async_copy(
-                ref.at[pl.ds(count, few)], decodes, row_sem.at[len(row_copies)]
+                ref.at[pl.ds(0, count)], rows.at[pl.ds(at, count)], row_sem.at[index]
             )
-            row_copies.append(copy)
-        if count:
-            copy = pltpu.make_async_copy(
-                ref.at[pl.ds(0, count)], rows.at[pl.ds(at, count)], row_sem.at[len(row_copies)]
-            )
-            row_copies.append(copy)
+            row_copies[p].append(copy)
         at += count
     up_copies = [
         pltpu.make_async_copy(weight_refs[3 * e + i], weights.at[2 * e + i], weight_sem.at[2 * e + i])
@@ -202,16 +202,18 @@
         pltpu.make_async_copy(weight_refs[3 * e + 2], downs.at[e], weight_sem.at[4 + e])
         for e in range(2)
     ]
-    for copy in row_copies + up_copies + down_copies:
+    for copy in row_copies[0] + row_copies[1] + up_copies + down_copies:
         copy.start()
-    for copy in row_copies:
-        copy.wait()
     is_first = lax.broadcasted_iota(jnp.int32, (few, 1), 0) == 0
-    for j in range(4):
-        part = pl.ds(j * tokens, few)
-        decode_row = decodes[...].astype(jnp.float32)[j : j + 1]
-        kept = rows[part, :].astype(jnp.float32)
-        rows[part, :] = jnp.where(is_first, decode_row, kept).astype(jnp.bfloat16)
+
+    def receive(p):
+        for copy in row_copies[p]:
+            copy.wait()
+        for j in (2 * p, 2 * p + 1):
+            part = pl.ds(j * tokens, few)
+            decode_row = decodes[...].astype(jnp.float32)[j : j + 1]
+            kept = rows[part, :].astype(jnp.float32)
+            rows[part, :] = jnp.where(is_first, decode_row, kept).astype(jnp.bfloat16)
 
     experts = ids_ref[2]
     extra = rows.shape[1] - width
@@ -228,6 +230,7 @@
         return jnp.where(second, float(cap), 0.0)
 
     for p in range(2):
+        receive(p)
         ranks = lax.dot_general(
             wanted, rows[pairs[p], width:], (((1,), (1,)), ((), ())), preferred_element_type=jnp.float32
         )
@@ -357,7 +360,9 @@
 
 
 def join_kernel(far_ref, risen_ref, own_ref, x_ref, y_ref, far_out, own_out):
-    far_out[...] = (far_ref[...].astype(jnp.float32) + risen_ref[...].astype(jnp.float32)).astype(jnp.bfloat16)
+    rows, width = far_ref.shape
+    far = far_ref[...].astype(jnp.float32) + risen_ref[:rows, :width].astype(jnp.float32)
+    far_out[...] = far.astype(jnp.bfloat16)
     total = own_ref[...].astype(jnp.float32) + x_ref[...].astype(jnp.float32) + y_ref[...].astype(jnp.float32)
     own_out[...] = total.astype(jnp.bfloat16)
 
@@ -369,6 +374,42 @@
         compiler_params=pltpu.CompilerParams(vmem_limit_bytes=16 << 20),
         name="join",
     )(far, risen, own, from_x, from_y)
+
+
+def meet_kernel(far_0_ref, far_1_ref, risen_ref, x_ref, y_ref, out_0, out_1, x_out, y_out):
+    x_out[...] = x_ref[...]
+    y_out[...] = y_ref[...]
+    cut = out_0.shape[0]
+    risen = risen_ref[...].astype(jnp.float32)
+    out_0[...] = (far_0_ref[...].astype(jnp.float32) + risen[:cut]).astype(jnp.bfloat16)
+    out_1[...] = (far_1_ref[...].astype(jnp.float32) + risen[cut:]).astype(jnp.bfloat16)
+
+
+def meet(far_0, far_1, risen, x_part, y_part):
+    outputs = (far_0, far_1, x_part, y_part)
+    return pl.pallas_call(
+        meet_kernel,
+        out_shape=[jax.ShapeDtypeStruct(output.shape, output.dtype) for output in outputs],
+        compiler_params=pltpu.CompilerParams(vmem_limit_bytes=16 << 20),
+        name="meet",
+    )(far_0, far_1, risen, x_part, y_part)
+
+
+def gather_kernel(own_ref, x_0_ref, x_1_ref, y_0_ref, y_1_ref, carried_ref, out_ref):
+    cut = x_0_ref.shape[0]
+    for part, x_ref, y_ref in ((slice(0, cut), x_0_ref, y_0_ref), (slice(cut, None), x_1_ref, y_1_ref)):
+        total = own_ref[part, :].astype(jnp.float32) + carried_ref[part, :].astype(jnp.float32)
+        total += x_ref[...].astype(jnp.float32) + y_ref[...].astype(jnp.float32)
+        out_ref[part, :] = total.astype(jnp.bfloat16)
+
+
+def gather_sums(own, x_0, x_1, y_0, y_1, carried):
+    return pl.pallas_call(
+        gather_kernel,
+        out_shape=jax.ShapeDtypeStruct(own.shape, own.dtype),
+        compiler_params=pltpu.CompilerParams(vmem_limit_bytes=16 << 20),
+        name="gather",
+    )(own, x_0, x_1, y_0, y_1, carried)
 
 
 def along_x(value):
@@ -501,31 +542,33 @@
     sums_1 = apply((block_1,) + sides_1 + corner_1 + (decodes_1,), (tokens,) * 4)
     sides_3, risen, passed_0, sums_0, sums_1 = fence(sides_3, risen, passed_0, sums_0, sums_1)
 
-    decodes_3 = around_z(risen[tokens:])
-    decodes_3, far = fence(decodes_3, sums_1[3])
-    far = around_z(far)
+    far = jnp.pad(sums_1[3], ((0, 0), (0, risen.shape[1] - sums_1[3].shape[1])))
+    far = around_z(jnp.concatenate([far, risen[tokens:]], axis=0))
     corner_3 = spread_corner(sides_3)
     back_1 = return_sides(sums_1)
     sums_2 = apply((block_2,) + sides_2 + (risen,), (tokens,) * 4)
-    decodes_3, far, corner_3, back_1, sums_1, sums_2 = fence(
-        decodes_3, far, corner_3, back_1, sums_1, sums_2
-    )
+    far, corner_3, back_1, sums_1, sums_2 = fence(far, corner_3, back_1, sums_1, sums_2)
+    decodes_3 = far[tokens:]
 
     far, first = join(sums_2[3], far, sums_1[0], *back_1)
     far = around_z(far)
     back_2 = return_sides(sums_2)
     carried_1 = around_z(first, -1)
-    sums_3 = apply((block_3,) + sides_3 + corner_3 + (decodes_3,), (tokens,) * 4)
+    parts = (cut, tokens - cut)
+    sums_3 = apply((block_3,) + sides_3 + corner_3 + (decodes_3,), (tokens,) + parts * 3)
     far, sums_2, sums_3 = fence(far, sums_2, sums_3)
 
-    far = added(sums_3[3], far).astype(jnp.bfloat16)
-    passed_3 = return_corner(tuple(sums_3[:3]) + (far[:cut], far[cut:]))
+    own, x_0, x_1, y_0, y_1, far_0, far_1 = sums_3
+    far_0, far_1, x_1, y_0 = meet(far_0, far_1, far, x_1, y_0)
+    passed_3 = along_y(far_0), along_x(far_1)
+    back_x1, back_y0 = along_x(x_1), along_y(y_0)
     passed_3, carried_1 = fence(passed_3, carried_1)
-    back_3 = return_sides(sums_3, passed_3)
+    back_x0 = along_x(added(x_0, passed_3[0]).astype(jnp.bfloat16))
+    back_y1 = along_y(added(y_1, passed_3[1]).astype(jnp.bfloat16))
     carried = around_z(added(sums_2[0], *back_2).astype(jnp.bfloat16))
     carried, passed_0, sums_0 = fence(carried, passed_0, sums_0)
     back_0 = return_sides(sums_0, passed_0)
-    carried = around_z(added(sums_3[0], *back_3, carried).astype(jnp.bfloat16))
+    carried = around_z(gather_sums(own, back_x0, back_x1, back_y0, back_y1, carried))
     return added(hidden, sums_0[0], carried_1, *back_0, carried).astype(jnp.bfloat16)[None]
 
 

time: 154 us -> 150 us (0.974)
  waiting for transfers between devices: 44.5 us -> 40.9 us
    ppermute x10 -> x9, waiting for transfers between devices: 20.4 us -> 10.7 us  [around_z(): lax.ppermute(value, 'blk', [(i, (i + 2 * hops) % 8) for i in range(8)])]
    ppermute x14 -> x15, waiting for transfers between devices: 6.62 us -> 16.1 us  [along_y(): return lax.ppermute(value, 'kv', [(i, i ^ 2) for i in range(4)])]
    ppermute x10 -> x9, starting transfers between devices: 11.1 us -> 7.51 us  [around_z(): lax.ppermute(value, 'blk', [(i, (i + 2 * hops) % 8) for i in range(8)])]
    ppermute x14 -> x15, waiting for transfers between devices: 17.4 us -> 14.1 us  [along_x(): return lax.ppermute(value, 'kv', [(i, i ^ 1) for i in range(4)])]
    ppermute x14 -> x15, starting transfers between devices: 16.2 us -> 18.2 us  [along_y(): return lax.ppermute(value, 'kv', [(i, i ^ 2) for i in range(4)])]
    ppermute x14 -> x15, starting transfers between devices: 14.7 us -> 15.4 us  [along_x(): return lax.ppermute(value, 'kv', [(i, i ^ 1) for i in range(4)])]
  transfers between devices with their start and end apart: 41 -> 42, of which waited for: 17 -> 14; matrix products, arithmetic and copies ran while one was open for 6% -> 6% of each run, Pallas kernels for 32% -> 33%
where the time goes in v12:
time: 150 us
  Pallas kernels  50.5 us (34%)
  starting transfers between devices  41.6 us (28%)
  waiting for transfers between devices  40.9 us (27%)
  local copies, waits for them, and re-layouts  6.35 us (4%)
  other arithmetic  4.91 us (3%)
  matrix products  4.85 us (3%)
    pallas_call x4, Pallas kernels, run_plane(): pl.pallas_call(functools.partial(plane_kernel, cap, piece_rows, block_row...  48 us
    ppermute x15, starting transfers between devices, along_y(): return lax.ppermute(value, 'kv', [(i, i ^ 2) for i in range(4)])  18.2 us
    ppermute x15, waiting for transfers between devices, along_y(): return lax.ppermute(value, 'kv', [(i, i ^ 2) for i in range(4)])  16.1 us
    ppermute x15, starting transfers between devices, along_x(): return lax.ppermute(value, 'kv', [(i, i ^ 1) for i in range(4)])  15.4 us
    ppermute x15, waiting for transfers between devices, along_x(): return lax.ppermute(value, 'kv', [(i, i ^ 1) for i in range(4)])  14.1 us
    ppermute x9, waiting for transfers between devices, around_z(): lax.ppermute(value, 'blk', [(i, (i + 2 * hops) % 8) for i in range(8)])  10.7 us
    ppermute x9, starting transfers between devices, around_z(): lax.ppermute(value, 'blk', [(i, (i + 2 * hops) % 8) for i in range(8)])  7.51 us
    unnamed x24, local copies, waits for them, and re-layouts  6.03 us
  transfers between devices with their start and end apart: 42, of which 14 were waited for; matrix products, arithmetic and copies ran while one was open for 6% of the time, Pallas kernels for 33%

profile of v12, /device:TPU:0, one launch (start us, length us, event | category | flops | bytes accessed | tf_op | source)
XLA Modules:
  0.0 149.6 jit_solution(9700069269517788612)
XLA Ops:
  0.0 1.0 copy-done
  1.0 0.9 copy-done.2
  1.9 0.7 copy-done.4
  2.6 0.7 copy-done.6
  3.3 1.3 prepare.2.refs_1_
  4.6 3.0 %collective-permute-start = (bf16[112,2176]{1,0:T(8,128)(2,1)S(1)}, bf16[112,2176]{1,0:T(8,128)(2,1)S(1)}, u32[]{:S(2)}, u32[]{:S(2)}) collective-permute-start(bf16[112,2176]{1,0:T(8,128)(2,1)S(1)} %prepare.2.refs_1_), channel_id=1, source_target_pairs={{0,8},{8,0},{16,24},{24,16},{1,9},{9,1},{17,25},{25,17},{2,10},{10... | collective-permute-start | bytes 1462280 | tf_op jit(solution)/shard_map/ppermute | solution.py:416
  7.6 1.5 %collective-permute-start.1 = (bf16[112,2176]{1,0:T(8,128)(2,1)S(1)}, bf16[112,2176]{1,0:T(8,128)(2,1)S(1)}, u32[]{:S(2)}, u32[]{:S(2)}) collective-permute-start(bf16[112,2176]{1,0:T(8,128)(2,1)S(1)} %prepare.2.refs_1_), channel_id=1, source_target_pairs={{0,16},{8,24},{16,0},{24,8},{1,17},{9,25},{17,1},{25,9},{2,18},{10... | collective-permute-start | bytes 1462280 | tf_op jit(solution)/shard_map/ppermute | solution.py:420
  9.1 1.6 %collective-permute-start.2 = (bf16[112,2176]{1,0:T(8,128)(2,1)S(1)}, bf16[112,2176]{1,0:T(8,128)(2,1)}, u32[]{:S(2)}, u32[]{:S(2)}) collective-permute-start(bf16[112,2176]{1,0:T(8,128)(2,1)S(1)} %prepare.2.refs_1_), channel_id=1, source_target_pairs={{0,2},{1,3},{2,4},{3,5},{4,6},{5,7},{6,0},{7,1},{8,10},{9,11},{10,... | collective-permute-start | bytes 1462280 | tf_op jit(solution)/shard_map/ppermute | solution.py:424
  11.2 0.7 minimum_subtract_fusion
  12.1 0.9 broadcast_in_dim.76
  12.9 1.0 convert_reduce_fusion
  13.9 3.5 %fusion.36 = (f32[4,8]{1,0:T(4,128)S(1)}, f32[4,8,4096]{2,1,0:T(8,128)S(1)}) fusion(bf16[4,4096,1,128]{3,1,2,0:T(8,128)(2,1)} %param.15, bf16[1,4,8,128]{3,1,2,0:T(4,128)(2,1)} %bitcast.53, pred[4,4096]{1,0:T(4,128)(4,1)S(1)} %iota_compare_fusion.2), kind=kOutput, calls=%fused_computation.61 | convolution fusion | flops 33947616 | bytes 4743296 | tf_op jit(solution)/shard_map/rgd,rjd->rgj/dot_general | solution.py:27
  17.7 0.7 fusion.11
  18.5 1.1 copy-done.10
  19.6 0.7 convolution_add_fusion
  20.3 0.6 collective-permute-start.6
  20.9 2.5 %collective-permute-done.2.refs_1_ = bf16[112,2176]{1,0:T(8,128)(2,1)} collective-permute-done((bf16[112,2176]{1,0:T(8,128)(2,1)S(1)}, bf16[112,2176]{1,0:T(8,128)(2,1)}, u32[]{:S(2)}, u32[]{:S(2)}) %collective-permute-start.2) | collective-permute-done | bytes 487456 | tf_op jit(solution)/shard_map/ppermute | solution.py:424
  23.4 0.6 collective-permute-start.4
  24.0 0.6 collective-permute-start.5
  24.7 5.2 %collective-permute-done.5.refs_5_ = bf16[48,2176]{1,0:T(8,128)(2,1)S(1)} collective-permute-done((bf16[48,2176]{1,0:T(8,128)(2,1)S(1)}, bf16[48,2176]{1,0:T(8,128)(2,1)S(1)}, u32[]{:S(2)}, u32[]{:S(2)}) %collective-permute-start.5) | collective-permute-done | bytes 208928 | tf_op jit(solution)/shard_map/ppermute | solution.py:416
  29.9 0.7 copy-done.7
  30.6 1.5 %collective-permute-start.8 = (f32[8,2048]{1,0:T(8,128)S(1)}, f32[8,2048]{1,0:T(8,128)S(1)}, u32[]{:S(2)}, u32[]{:S(2)}) collective-permute-start(f32[8,2048]{1,0:T(8,128)S(1)} %fusion.35), channel_id=1, source_target_pairs={{0,16},{8,24},{16,0},{24,8},{1,17},{9,25},{17,1},{25,9},{2,18},{10... | collective-permute-start | bytes 196616 | tf_op jit(solution)/shard_map/ppermute | solution.py:420
  32.2 0.5 collective-permute-start.10
  32.7 0.5 collective-permute-start.11
  33.2 1.3 collective-permute-start.9
  34.5 0.6 collective-permute-done.8
  35.8 9.8 %collective-permute-done.10.refs_3_ = bf16[112,2176]{1,0:T(8,128)(2,1)S(1)} collective-permute-done((bf16[112,2176]{1,0:T(8,128)(2,1)}, bf16[112,2176]{1,0:T(8,128)(2,1)S(1)}, u32[]{:S(2)}, u32[]{:S(2)}) %collective-permute-start.10) | collective-permute-done | bytes 487456 | tf_op jit(solution)/shard_map/ppermute | solution.py:420
  45.7 2.0 %collective-permute-done.11.refs_1_ = bf16[112,2176]{1,0:T(8,128)(2,1)S(1)} collective-permute-done((bf16[112,2176]{1,0:T(8,128)(2,1)}, bf16[112,2176]{1,0:T(8,128)(2,1)S(1)}, u32[]{:S(2)}, u32[]{:S(2)}) %collective-permute-start.11) | collective-permute-done | bytes 487456 | tf_op jit(solution)/shard_map/ppermute | solution.py:424
  47.7 0.5 collective-permute-start.15
  48.2 1.5 %collective-permute-start.16 = (bf16[112,2176]{1,0:T(8,128)(2,1)S(1)}, bf16[112,2176]{1,0:T(8,128)(2,1)S(1)}, u32[]{:S(2)}, u32[]{:S(2)}) collective-permute-start(bf16[112,2176]{1,0:T(8,128)(2,1)S(1)} %collective-permute-done.11.refs_1_), channel_id=1, source_target_pairs={{0,16},{8,24},{16,0},{24,8},{1,17},{9,25},{17,1},{25,9},{2,18},{10... | collective-permute-start | bytes 1462280 | tf_op jit(solution)/shard_map/ppermute | solution.py:420
  50.1 1.1 collective-permute-start.13
  51.2 0.8 collective-permute-start.14
  52.0 0.9 copy-done.8
  53.0 12.1 %plane.4 = (bf16[112,2048]{1,0:T(8,128)(2,1)S(1)}, bf16[112,2048]{1,0:T(8,128)(2,1)S(1)}, bf16[112,2048]{1,0:T(8,128)(2,1)S(1)}, bf16[64,2048]{1,0:T(8,128)(2,1)S(1)}, bf16[48,2048]{1,0:T(8,128)(2,1)S(1)}) custom-call(s32[3]{0:T(128)S(1)} %pad_add_fusion.refs_0_, bf16[112,2176]{1,0:T(8,128)(2,1)S(1)} %prepare.2.refs_1_, ...), custom_call_target="tpu_custom_call" | custom-call | flops 8455716864 | bytes 25165824 | tf_op jit(solution)/shard_map/plane/pallas_call | solution.py:316
  65.1 1.0 collective-permute-done.13.refs_4_
  66.1 1.6 %collective-permute-start.18 = (bf16[112,2176]{1,0:T(8,128)(2,1)S(1)}, bf16[112,2176]{1,0:T(8,128)(2,1)S(1)}, u32[]{:S(2)}, u32[]{:S(2)}) collective-permute-start(bf16[112,2176]{1,0:T(8,128)(2,1)S(1)} %slice.47.refs_1_), channel_id=1, source_target_pairs={{0,8},{8,0},{16,24},{24,16},{1,9},{9,1},{17,25},{25,17},{2,10},{10... | collective-permute-start | bytes 1462280 | tf_op jit(solution)/shard_map/ppermute | solution.py:416
  67.7 1.5 %collective-permute-start.19 = (bf16[112,2176]{1,0:T(8,128)(2,1)S(1)}, bf16[112,2176]{1,0:T(8,128)(2,1)S(1)}, u32[]{:S(2)}, u32[]{:S(2)}) collective-permute-start(bf16[112,2176]{1,0:T(8,128)(2,1)S(1)} %slice.47.refs_1_), channel_id=1, source_target_pairs={{0,16},{8,24},{16,0},{24,8},{1,17},{9,25},{17,1},{25,9},{2,18},{10... | collective-permute-start | bytes 1462280 | tf_op jit(solution)/shard_map/ppermute | solution.py:420
  69.5 0.6 collective-permute-start.21
  70.1 0.9 collective-permute-start.22
  70.9 11.7 %plane.5 = (bf16[112,2048]{1,0:T(8,128)(2,1)S(1)}, bf16[112,2048]{1,0:T(8,128)(2,1)S(1)}, bf16[112,2048]{1,0:T(8,128)(2,1)S(1)}, bf16[112,2048]{1,0:T(8,128)(2,1)S(1)}) custom-call(s32[3]{0:T(128)S(1)} %pad_add_fusion.refs_0_, bf16[112,2176]{1,0:T(8,128)(2,1)} %collective-permute-done.2.refs_1_, bf16[112,2176]{1,0:T(8,128)(2,1)S(1)} %collective-permute-done.9.refs_2_, ...), custom_call_target="tpu_custom_call" | custom-call | flops 8455716864 | bytes 25165824 | tf_op jit(solution)/shard_map/plane/pallas_call | solution.py:316
  82.7 1.5 collective-permute-done.21.passed_0_ref
  84.5 1.6 %collective-permute-start.24 = (bf16[64,2176]{1,0:T(8,128)(2,1)S(1)}, bf16[64,2176]{1,0:T(8,128)(2,1)S(1)}, u32[]{:S(2)}, u32[]{:S(2)}) collective-permute-start(bf16[64,2176]{1,0:T(8,128)(2,1)S(1)} %slice.50), channel_id=1, source_target_pairs={{0,16},{8,24},{16,0},{24,8},{1,17},{9,25},{17,1},{25,9},{2,18},{10... | collective-permute-start | bytes 835592 | tf_op jit(solution)/shard_map/ppermute | solution.py:420
  86.1 0.5 collective-permute-start.26
  87.2 1.6 %collective-permute-start.25 = (bf16[48,2176]{1,0:T(8,128)(2,1)S(1)}, bf16[48,2176]{1,0:T(8,128)(2,1)S(1)}, u32[]{:S(2)}, u32[]{:S(2)}) collective-permute-start(bf16[48,2176]{1,0:T(8,128)(2,1)S(1)} %slice.51), channel_id=1, source_target_pairs={{0,8},{8,0},{16,24},{24,16},{1,9},{9,1},{17,25},{25,17},{2,10},{10... | collective-permute-start | bytes 626696 | tf_op jit(solution)/shard_map/ppermute | solution.py:416
  88.7 12.0 %plane.6 = (bf16[112,2048]{1,0:T(8,128)(2,1)S(1)}, bf16[112,2048]{1,0:T(8,128)(2,1)S(1)}, bf16[112,2048]{1,0:T(8,128)(2,1)S(1)}, bf16[112,2048]{1,0:T(8,128)(2,1)S(1)}) custom-call(s32[3]{0:T(128)S(1)} %pad_add_fusion.refs_0_, bf16[112,2176]{1,0:T(8,128)(2,1)S(1)} %collective-permute-done.11.refs_1_, bf16[112,2176]{1,0:T(8,128)(2,1)S(1)} %collective-permute-done.15.refs_2_, ...), custom_call_target="tpu_custom_call" | custom-call | flops 8455716864 | bytes 25165824 | tf_op jit(solution)/shard_map/plane/pallas_call | solution.py:316
  101.1 2.1 %collective-permute-start.28 = (bf16[112,2048]{1,0:T(8,128)(2,1)S(1)}, bf16[112,2048]{1,0:T(8,128)(2,1)S(1)}, u32[]{:S(2)}, u32[]{:S(2)}) collective-permute-start(bf16[112,2048]{1,0:T(8,128)(2,1)S(1)} %get-tuple-element.156), channel_id=1, source_target_pairs={{0,2},{1,3},{2,4},{3,5},{4,6},{5,7},{6,0},{7,1},{8,10},{9,11},{10,... | collective-permute-start | bytes 1376264 | tf_op jit(solution)/shard_map/ppermute | solution.py:424
  103.2 0.5 collective-permute-start.29
  103.8 1.5 %collective-permute-start.30 = (bf16[112,2048]{1,0:T(8,128)(2,1)S(1)}, bf16[112,2048]{1,0:T(8,128)(2,1)S(1)}, u32[]{:S(2)}, u32[]{:S(2)}) collective-permute-start(bf16[112,2048]{1,0:T(8,128)(2,1)S(1)} %get-tuple-element.159), channel_id=1, source_target_pairs={{0,16},{8,24},{16,0},{24,8},{1,17},{9,25},{17,1},{25,9},{2,18},{10... | collective-permute-start | bytes 1376264 | tf_op jit(solution)/shard_map/ppermute | solution.py:420
  105.3 1.8 %collective-permute-start.34 = (bf16[112,2048]{1,0:T(8,128)(2,1)S(1)}, bf16[112,2048]{1,0:T(8,128)(2,1)S(1)}, u32[]{:S(2)}, u32[]{:S(2)}) collective-permute-start(bf16[112,2048]{1,0:T(8,128)(2,1)S(1)} %get-tuple-element.183), channel_id=1, source_target_pairs={{0,6},{1,7},{2,0},{3,1},{4,2},{5,3},{6,4},{7,5},{8,14},{9,15},{10,... | collective-permute-start | bytes 1376264 | tf_op jit(solution)/shard_map/ppermute | solution.py:424
  107.1 12.3 %plane.7 = (bf16[112,2048]{1,0:T(8,128)(2,1)S(1)}, bf16[64,2048]{1,0:T(8,128)(2,1)S(1)}, bf16[48,2048]{1,0:T(8,128)(2,1)S(1)}, bf16[64,2048]{1,0:T(8,128)(2,1)S(...) custom-call(s32[3]{0:T(128)S(1)} %pad_add_fusion.refs_0_, ...), custom_call_target="tpu_custom_call" | custom-call | flops 8455716864 | bytes 25165824 | tf_op jit(solution)/shard_map/plane/pallas_call | solution.py:316
  119.5 0.6 collective-permute-start.32
  120.1 1.5 collective-permute-start.33
  122.1 1.5 %collective-permute-start.39 = (bf16[64,2048]{1,0:T(8,128)(2,1)S(1)}, bf16[64,2048]{1,0:T(8,128)(2,1)S(1)}, u32[]{:S(2)}, u32[]{:S(2)}) collective-permute-start(bf16[64,2048]{1,0:T(8,128)(2,1)S(1)} %get-tuple-element.195), channel_id=1, source_target_pairs={{0,16},{8,24},{16,0},{24,8},{1,17},{9,25},{17,1},{25,9},{2,18},{10... | collective-permute-start | bytes 786440 | tf_op jit(solution)/shard_map/ppermute | solution.py:420
  123.6 0.5 collective-permute-start.38
  124.1 3.8 %collective-permute-done.33 = bf16[48,2048]{1,0:T(8,128)(2,1)S(1)} collective-permute-done((bf16[48,2048]{1,0:T(8,128)(2,1)S(1)}, bf16[48,2048]{1,0:T(8,128)(2,1)S(1)}, u32[]{:S(2)}, u32[]{:S(2)}) %collective-permute-start.33) | collective-permute-done | bytes 196640 | tf_op jit(solution)/shard_map/ppermute | solution.py:416
  128.1 0.9 collective-permute-start.37
  129.0 2.1 %collective-permute-start.40 = (bf16[48,2048]{1,0:T(8,128)(2,1)S(1)}, bf16[48,2048]{1,0:T(8,128)(2,1)S(1)}, u32[]{:S(2)}, u32[]{:S(2)}) collective-permute-start(bf16[48,2048]{1,0:T(8,128)(2,1)S(1)} %add_convert_fusion.3), channel_id=1, source_target_pairs={{0,16},{8,24},{16,0},{24,8},{1,17},{9,25},{17,1},{25,9},{2,18},{10... | collective-permute-start | bytes 589832 | tf_op jit(solution)/shard_map/ppermute | solution.py:420
  131.2 0.9 collective-permute-done.31.carried_ref
  132.2 0.6 collective-permute-start.35
  132.8 1.5 %collective-permute-start.36 = (bf16[112,2048]{1,0:T(8,128)(2,1)S(1)}, bf16[112,2048]{1,0:T(8,128)(2,1)S(1)}, u32[]{:S(2)}, u32[]{:S(2)}) collective-permute-start(bf16[112,2048]{1,0:T(8,128)(2,1)S(1)} %get-tuple-element.190), channel_id=1, source_target_pairs={{0,16},{8,24},{16,0},{24,8},{1,17},{9,25},{17,1},{25,9},{2,18},{10... | collective-permute-start | bytes 1376264 | tf_op jit(solution)/shard_map/ppermute | solution.py:420
  134.4 3.1 %collective-permute-done.40.y_1_ref = bf16[48,2048]{1,0:T(8,128)(2,1)S(1)} collective-permute-done((bf16[48,2048]{1,0:T(8,128)(2,1)S(1)}, bf16[48,2048]{1,0:T(8,128)(2,1)S(1)}, u32[]{:S(2)}, u32[]{:S(2)}) %collective-permute-start.40) | collective-permute-done | bytes 196640 | tf_op jit(solution)/shard_map/ppermute | solution.py:420
  138.3 4.8 %collective-permute-done.35 = bf16[112,2048]{1,0:T(8,128)(2,1)S(1)} collective-permute-done((bf16[112,2048]{1,0:T(8,128)(2,1)S(1)}, bf16[112,2048]{1,0:T(8,128)(2,1)S(1)}, u32[]{:S(2)}, u32[]{:S(2)}) %collective-permute-start.35) | collective-permute-done | bytes 458784 | tf_op jit(solution)/shard_map/ppermute | solution.py:416
  143.1 5.2 %collective-permute-done.41 = bf16[112,2048]{1,0:T(8,128)(2,1)S(1)} collective-permute-done((bf16[112,2048]{1,0:T(8,128)(2,1)S(1)}, bf16[112,2048]{1,0:T(8,128)(2,1)S(1)}, u32[]{:S(2)}, u32[]{:S(2)}) %collective-permute-start.41) | collective-permute-done | bytes 458784 | tf_op jit(solution)/shard_map/ppermute | solution.py:424
  148.3 1.2 fusion.15
  (94 shorter events, 5.6 us)
Async XLA Ops:
  0.0 17.4 %copy-start.11 = (f32[8]{0:T(128)S(1)}, f32[8]{0:T(128)}, u32[]{:S(2)}) copy-start(f32[8]{0:T(128)} %param.18) | copy-start | bytes 100
  0.0 1.0 copy-start
  1.0 0.9 copy-start.2
  1.9 0.7 copy-start.4
  2.6 0.7 copy-start.6
  4.6 15.7 %collective-permute-start = (bf16[112,2176]{1,0:T(8,128)(2,1)S(1)}, bf16[112,2176]{1,0:T(8,128)(2,1)S(1)}, u32[]{:S(2)}, u32[]{:S(2)}) collective-permute-start(bf16[112,2176]{1,0:T(8,128)(2,1)S(1)} %prepare.2.refs_1_), channel_id=1, source_target_pairs={{0,8},{8,0},{16,24},{24,16},{1,9},{9,1},{17,25},{25,17},{2,10},{10... | collective-permute-start | bytes 1462280 | tf_op jit(solution)/shard_map/ppermute | solution.py:416
  7.6 13.3 %collective-permute-start.1 = (bf16[112,2176]{1,0:T(8,128)(2,1)S(1)}, bf16[112,2176]{1,0:T(8,128)(2,1)S(1)}, u32[]{:S(2)}, u32[]{:S(2)}) collective-permute-start(bf16[112,2176]{1,0:T(8,128)(2,1)S(1)} %prepare.2.refs_1_), channel_id=1, source_target_pairs={{0,16},{8,24},{16,0},{24,8},{1,17},{9,25},{17,1},{25,9},{2,18},{10... | collective-permute-start | bytes 1462280 | tf_op jit(solution)/shard_map/ppermute | solution.py:420
  9.1 14.3 %collective-permute-start.2 = (bf16[112,2176]{1,0:T(8,128)(2,1)S(1)}, bf16[112,2176]{1,0:T(8,128)(2,1)}, u32[]{:S(2)}, u32[]{:S(2)}) collective-permute-start(bf16[112,2176]{1,0:T(8,128)(2,1)S(1)} %prepare.2.refs_1_), channel_id=1, source_target_pairs={{0,2},{1,3},{2,4},{3,5},{4,6},{5,7},{6,0},{7,1},{8,10},{9,11},{10,... | collective-permute-start | bytes 1462280 | tf_op jit(solution)/shard_map/ppermute | solution.py:424
  10.7 12.7 %collective-permute-start.3 = (bf16[2048,768]{1,0:T(8,128)(2,1)}, bf16[2048,768]{1,0:T(8,128)(2,1)}, u32[]{:S(2)}, u32[]{:S(2)}) collective-permute-start(bf16[2048,768]{1,0:T(8,128)(2,1)} %bitcast.55), channel_id=1, source_target_pairs={{0,1},{1,0},{2,3},{3,2},{4,5},{5,4},{6,7},{7,6},{8,9},{9,8},{10,11... | collective-permute-start | bytes 9437192 | tf_op jit(solution)/shard_map/ppermute | solution.py:428
  10.7 14.0 %collective-permute-start.7 = (bf16[2048,768]{1,0:T(8,128)(2,1)}, bf16[2048,768]{1,0:T(8,128)(2,1)}, u32[]{:S(2)}, u32[]{:S(2)}) collective-permute-start(bf16[2048,768]{1,0:T(8,128)(2,1)} %bitcast.60), channel_id=1, source_target_pairs={{0,1},{1,0},{2,3},{3,2},{4,5},{5,4},{6,7},{7,6},{8,9},{9,8},{10,11... | collective-permute-start | bytes 9437192 | tf_op jit(solution)/shard_map/ppermute | solution.py:428
  12.1 5.7 %copy-start.9 = (bf16[4,4096,1,128]{3,1,2,0:T(8,128)(2,1)S(1)}, bf16[4,4096,1,128]{3,1,2,0:T(8,128)(2,1)}, u32[]{:S(2)}) copy-start(bf16[4,4096,1,128]{3,1,2,0:T(8,128)(2,1)} %param.16) | copy-start | bytes 12582916
  17.4 2.2 %copy-start.10 = (bf16[1024,2048]{1,0:T(8,128)(2,1)S(1)}, bf16[1024,2048]{1,0:T(8,128)(2,1)}, u32[]{:S(2)}) copy-start(bf16[1024,2048]{1,0:T(8,128)(2,1)} %param.19) | copy-start | bytes 12582916
  18.4 16.9 %copy-start.3 = (bf16[2048,32]{0,1:T(8,128)(2,1)S(1)}, bf16[2048,32]{0,1:T(8,128)(2,1)}, u32[]{:S(2)}) copy-start(bf16[2048,32]{0,1:T(8,128)(2,1)} %param.23) | copy-start | bytes 393220
  18.5 16.9 %copy-start.5 = (f32[2048]{0:T(1024)S(1)}, f32[2048]{0:T(1024)}, u32[]{:S(2)}) copy-start(f32[2048]{0:T(1024)} %param.22) | copy-start | bytes 24580
  20.3 4.3 %collective-permute-start.6 = (f32[8,2048]{1,0:T(8,128)S(1)}, f32[8,2048]{1,0:T(8,128)S(1)}, u32[]{:S(2)}, u32[]{:S(2)}) collective-permute-start(f32[8,2048]{1,0:T(8,128)S(1)} %pad_maximum_fusion.2), channel_id=1, source_target_pairs={{0,8},{8,0},{16,24},{24,16},{1,9},{9,1},{17,25},{25,17},{2,10},{10... | collective-permute-start | bytes 196616 | tf_op jit(solution)/shard_map/ppermute | solution.py:416
  23.4 7.1 %collective-permute-start.4 = (bf16[64,2176]{1,0:T(8,128)(2,1)S(1)}, bf16[64,2176]{1,0:T(8,128)(2,1)S(1)}, u32[]{:S(2)}, u32[]{:S(2)}) collective-permute-start(bf16[64,2176]{1,0:T(8,128)(2,1)S(1)} %slice.40), channel_id=1, source_target_pairs={{0,16},{8,24},{16,0},{24,8},{1,17},{9,25},{17,1},{25,9},{2,18},{10... | collective-permute-start | bytes 835592 | tf_op jit(solution)/shard_map/ppermute | solution.py:420
  24.0 5.9 %collective-permute-start.5 = (bf16[48,2176]{1,0:T(8,128)(2,1)S(1)}, bf16[48,2176]{1,0:T(8,128)(2,1)S(1)}, u32[]{:S(2)}, u32[]{:S(2)}) collective-permute-start(bf16[48,2176]{1,0:T(8,128)(2,1)S(1)} %slice.41), channel_id=1, source_target_pairs={{0,8},{8,0},{16,24},{24,16},{1,9},{9,1},{17,25},{25,17},{2,10},{10... | collective-permute-start | bytes 626696 | tf_op jit(solution)/shard_map/ppermute | solution.py:416
  29.9 0.7 copy-start.7
  30.6 17.1 %collective-permute-start.12 = (bf16[768,2048]{1,0:T(8,128)(2,1)}, bf16[768,2048]{1,0:T(8,128)(2,1)}, u32[]{:S(2)}, u32[]{:S(2)}) collective-permute-start(bf16[768,2048]{1,0:T(8,128)(2,1)} %bitcast.12.refs_9_.refs_7_), channel_id=1, source_target_pairs={{0,1},{1,0},{2,3},{3,2},{4,5},{5,4},{6,7},{7,6},{8,9},{9,8},{10,11... | collective-permute-start | bytes 9437192 | tf_op jit(solution)/shard_map/ppermute | solution.py:428
  30.6 4.5 %collective-permute-start.8 = (f32[8,2048]{1,0:T(8,128)S(1)}, f32[8,2048]{1,0:T(8,128)S(1)}, u32[]{:S(2)}, u32[]{:S(2)}) collective-permute-start(f32[8,2048]{1,0:T(8,128)S(1)} %fusion.35), channel_id=1, source_target_pairs={{0,16},{8,24},{16,0},{24,8},{1,17},{9,25},{17,1},{25,9},{2,18},{10... | collective-permute-start | bytes 196616 | tf_op jit(solution)/shard_map/ppermute | solution.py:420
  32.2 13.5 %collective-permute-start.10 = (bf16[112,2176]{1,0:T(8,128)(2,1)}, bf16[112,2176]{1,0:T(8,128)(2,1)S(1)}, u32[]{:S(2)}, u32[]{:S(2)}) collective-permute-start(bf16[112,2176]{1,0:T(8,128)(2,1)} %collective-permute-done.2.refs_1_), channel_id=1, source_target_pairs={{0,16},{8,24},{16,0},{24,8},{1,17},{9,25},{17,1},{25,9},{2,18},{10... | collective-permute-start | bytes 1462280 | tf_op jit(solution)/shard_map/ppermute | solution.py:420
  32.7 15.0 %collective-permute-start.11 = (bf16[112,2176]{1,0:T(8,128)(2,1)}, bf16[112,2176]{1,0:T(8,128)(2,1)S(1)}, u32[]{:S(2)}, u32[]{:S(2)}) collective-permute-start(bf16[112,2176]{1,0:T(8,128)(2,1)} %collective-permute-done.2.refs_1_), channel_id=1, source_target_pairs={{0,2},{1,3},{2,4},{3,5},{4,6},{5,7},{6,0},{7,1},{8,10},{9,11},{10,... | collective-permute-start | bytes 1462280 | tf_op jit(solution)/shard_map/ppermute | solution.py:424
  33.2 14.5 %collective-permute-start.9 = (bf16[112,2176]{1,0:T(8,128)(2,1)}, bf16[112,2176]{1,0:T(8,128)(2,1)S(1)}, u32[]{:S(2)}, u32[]{:S(2)}) collective-permute-start(bf16[112,2176]{1,0:T(8,128)(2,1)} %collective-permute-done.2.refs_1_), channel_id=1, source_target_pairs={{0,8},{8,0},{16,24},{24,16},{1,9},{9,1},{17,25},{25,17},{2,10},{10... | collective-permute-start | bytes 1462280 | tf_op jit(solution)/shard_map/ppermute | solution.py:416
  47.7 18.4 %collective-permute-start.15 = (bf16[112,2176]{1,0:T(8,128)(2,1)S(1)}, bf16[112,2176]{1,0:T(8,128)(2,1)S(1)}, u32[]{:S(2)}, u32[]{:S(2)}) collective-permute-start(bf16[112,2176]{1,0:T(8,128)(2,1)S(1)} %collective-permute-done.11.refs_1_), channel_id=1, source_target_pairs={{0,8},{8,0},{16,24},{24,16},{1,9},{9,1},{17,25},{25,17},{2,10},{10... | collective-permute-start | bytes 1462280 | tf_op jit(solution)/shard_map/ppermute | solution.py:416
  48.2 17.8 %collective-permute-start.16 = (bf16[112,2176]{1,0:T(8,128)(2,1)S(1)}, bf16[112,2176]{1,0:T(8,128)(2,1)S(1)}, u32[]{:S(2)}, u32[]{:S(2)}) collective-permute-start(bf16[112,2176]{1,0:T(8,128)(2,1)S(1)} %collective-permute-done.11.refs_1_), channel_id=1, source_target_pairs={{0,16},{8,24},{16,0},{24,8},{1,17},{9,25},{17,1},{25,9},{2,18},{10... | collective-permute-start | bytes 1462280 | tf_op jit(solution)/shard_map/ppermute | solution.py:420
  49.8 16.3 %collective-permute-start.17 = (bf16[128,2176]{1,0:T(8,128)(2,1)S(1)}, bf16[128,2176]{1,0:T(8,128)(2,1)S(1)}, u32[]{:S(2)}, u32[]{:S(2)}) collective-permute-start(bf16[128,2176]{1,0:T(8,128)(2,1)S(1)} %pad_maximum_fusion), channel_id=1, source_target_pairs={{0,2},{1,3},{2,4},{3,5},{4,6},{5,7},{6,0},{7,1},{8,10},{9,11},{10,... | collective-permute-start | bytes 1671176 | tf_op jit(solution)/shard_map/ppermute | solution.py:424
  50.1 15.9 %collective-permute-start.13 = (bf16[64,2176]{1,0:T(8,128)(2,1)S(1)}, bf16[64,2176]{1,0:T(8,128)(2,1)S(1)}, u32[]{:S(2)}, u32[]{:S(2)}) collective-permute-start(bf16[64,2176]{1,0:T(8,128)(2,1)S(1)} %slice.45), channel_id=1, source_target_pairs={{0,16},{8,24},{16,0},{24,8},{1,17},{9,25},{17,1},{25,9},{2,18},{10... | collective-permute-start | bytes 835592 | tf_op jit(solution)/shard_map/ppermute | solution.py:420
  51.2 13.9 %collective-permute-start.14 = (bf16[48,2176]{1,0:T(8,128)(2,1)S(1)}, bf16[48,2176]{1,0:T(8,128)(2,1)S(1)}, u32[]{:S(2)}, u32[]{:S(2)}) collective-permute-start(bf16[48,2176]{1,0:T(8,128)(2,1)S(1)} %slice.46), channel_id=1, source_target_pairs={{0,8},{8,0},{16,24},{24,16},{1,9},{9,1},{17,25},{25,17},{2,10},{10... | collective-permute-start | bytes 626696 | tf_op jit(solution)/shard_map/ppermute | solution.py:416
  52.0 0.9 copy-start.8
  66.1 18.0 %collective-permute-start.18 = (bf16[112,2176]{1,0:T(8,128)(2,1)S(1)}, bf16[112,2176]{1,0:T(8,128)(2,1)S(1)}, u32[]{:S(2)}, u32[]{:S(2)}) collective-permute-start(bf16[112,2176]{1,0:T(8,128)(2,1)S(1)} %slice.47.refs_1_), channel_id=1, source_target_pairs={{0,8},{8,0},{16,24},{24,16},{1,9},{9,1},{17,25},{25,17},{2,10},{10... | collective-permute-start | bytes 1462280 | tf_op jit(solution)/shard_map/ppermute | solution.py:416
  67.7 16.5 %collective-permute-start.19 = (bf16[112,2176]{1,0:T(8,128)(2,1)S(1)}, bf16[112,2176]{1,0:T(8,128)(2,1)S(1)}, u32[]{:S(2)}, u32[]{:S(2)}) collective-permute-start(bf16[112,2176]{1,0:T(8,128)(2,1)S(1)} %slice.47.refs_1_), channel_id=1, source_target_pairs={{0,16},{8,24},{16,0},{24,8},{1,17},{9,25},{17,1},{25,9},{2,18},{10... | collective-permute-start | bytes 1462280 | tf_op jit(solution)/shard_map/ppermute | solution.py:420
  69.2 14.9 %collective-permute-start.20 = (bf16[128,2176]{1,0:T(8,128)(2,1)S(1)}, bf16[128,2176]{1,0:T(8,128)(2,1)S(1)}, u32[]{:S(2)}, u32[]{:S(2)}) collective-permute-start(bf16[128,2176]{1,0:T(8,128)(2,1)S(1)} %pad_maximum_fusion.1), channel_id=1, source_target_pairs={{0,2},{1,3},{2,4},{3,5},{4,6},{5,7},{6,0},{7,1},{8,10},{9,11},{10,... | collective-permute-start | bytes 1671176 | tf_op jit(solution)/shard_map/ppermute | solution.py:424
  69.5 14.6 %collective-permute-start.21 = (bf16[64,2048]{1,0:T(8,128)(2,1)S(1)}, bf16[64,2048]{1,0:T(8,128)(2,1)S(1)}, u32[]{:S(2)}, u32[]{:S(2)}) collective-permute-start(bf16[64,2048]{1,0:T(8,128)(2,1)S(1)} %get-tuple-element.129), channel_id=1, source_target_pairs={{0,16},{8,24},{16,0},{24,8},{1,17},{9,25},{17,1},{25,9},{2,18},{10... | collective-permute-start | bytes 786440 | tf_op jit(solution)/shard_map/ppermute | solution.py:420
  70.1 12.6 %collective-permute-start.22 = (bf16[48,2048]{1,0:T(8,128)(2,1)S(1)}, bf16[48,2048]{1,0:T(8,128)(2,1)S(1)}, u32[]{:S(2)}, u32[]{:S(2)}) collective-permute-start(bf16[48,2048]{1,0:T(8,128)(2,1)S(1)} %get-tuple-element.130), channel_id=1, source_target_pairs={{0,8},{8,0},{16,24},{24,16},{1,9},{9,1},{17,25},{25,17},{2,10},{10... | collective-permute-start | bytes 589832 | tf_op jit(solution)/shard_map/ppermute | solution.py:416
  84.2 16.6 %collective-permute-start.23 = (bf16[128,2176]{1,0:T(8,128)(2,1)S(1)}, bf16[128,2176]{1,0:T(8,128)(2,1)S(1)}, u32[]{:S(2)}, u32[]{:S(2)}) collective-permute-start(bf16[128,2176]{1,0:T(8,128)(2,1)S(1)} %fusion.14), channel_id=1, source_target_pairs={{0,2},{1,3},{2,4},{3,5},{4,6},{5,7},{6,0},{7,1},{8,10},{9,11},{10,... | collective-permute-start | bytes 1671176 | tf_op jit(solution)/shard_map/ppermute | solution.py:424
  84.5 16.2 %collective-permute-start.24 = (bf16[64,2176]{1,0:T(8,128)(2,1)S(1)}, bf16[64,2176]{1,0:T(8,128)(2,1)S(1)}, u32[]{:S(2)}, u32[]{:S(2)}) collective-permute-start(bf16[64,2176]{1,0:T(8,128)(2,1)S(1)} %slice.50), channel_id=1, source_target_pairs={{0,16},{8,24},{16,0},{24,8},{1,17},{9,25},{17,1},{25,9},{2,18},{10... | collective-permute-start | bytes 835592 | tf_op jit(solution)/shard_map/ppermute | solution.py:420
  86.1 14.6 %collective-permute-start.26 = (bf16[112,2048]{1,0:T(8,128)(2,1)S(1)}, bf16[112,2048]{1,0:T(8,128)(2,1)S(1)}, u32[]{:S(2)}, u32[]{:S(2)}) collective-permute-start(bf16[112,2048]{1,0:T(8,128)(2,1)S(1)} %get-tuple-element.142), channel_id=1, source_target_pairs={{0,8},{8,0},{16,24},{24,16},{1,9},{9,1},{17,25},{25,17},{2,10},{10... | collective-permute-start | bytes 1376264 | tf_op jit(solution)/shard_map/ppermute | solution.py:416
  86.7 14.1 %collective-permute-start.27 = (bf16[112,2048]{1,0:T(8,128)(2,1)S(1)}, bf16[112,2048]{1,0:T(8,128)(2,1)S(1)}, u32[]{:S(2)}, u32[]{:S(2)}) collective-permute-start(bf16[112,2048]{1,0:T(8,128)(2,1)S(1)} %get-tuple-element.143), channel_id=1, source_target_pairs={{0,16},{8,24},{16,0},{24,8},{1,17},{9,25},{17,1},{25,9},{2,18},{10... | collective-permute-start | bytes 1376264 | tf_op jit(solution)/shard_map/ppermute | solution.py:420
  87.2 13.6 %collective-permute-start.25 = (bf16[48,2176]{1,0:T(8,128)(2,1)S(1)}, bf16[48,2176]{1,0:T(8,128)(2,1)S(1)}, u32[]{:S(2)}, u32[]{:S(2)}) collective-permute-start(bf16[48,2176]{1,0:T(8,128)(2,1)S(1)} %slice.51), channel_id=1, source_target_pairs={{0,8},{8,0},{16,24},{24,16},{1,9},{9,1},{17,25},{25,17},{2,10},{10... | collective-permute-start | bytes 626696 | tf_op jit(solution)/shard_map/ppermute | solution.py:416
  101.1 18.3 %collective-permute-start.28 = (bf16[112,2048]{1,0:T(8,128)(2,1)S(1)}, bf16[112,2048]{1,0:T(8,128)(2,1)S(1)}, u32[]{:S(2)}, u32[]{:S(2)}) collective-permute-start(bf16[112,2048]{1,0:T(8,128)(2,1)S(1)} %get-tuple-element.156), channel_id=1, source_target_pairs={{0,2},{1,3},{2,4},{3,5},{4,6},{5,7},{6,0},{7,1},{8,10},{9,11},{10,... | collective-permute-start | bytes 1376264 | tf_op jit(solution)/shard_map/ppermute | solution.py:424
  103.2 18.3 %collective-permute-start.29 = (bf16[112,2048]{1,0:T(8,128)(2,1)S(1)}, bf16[112,2048]{1,0:T(8,128)(2,1)S(1)}, u32[]{:S(2)}, u32[]{:S(2)}) collective-permute-start(bf16[112,2048]{1,0:T(8,128)(2,1)S(1)} %get-tuple-element.158), channel_id=1, source_target_pairs={{0,8},{8,0},{16,24},{24,16},{1,9},{9,1},{17,25},{25,17},{2,10},{10... | collective-permute-start | bytes 1376264 | tf_op jit(solution)/shard_map/ppermute | solution.py:416
  103.8 17.8 %collective-permute-start.30 = (bf16[112,2048]{1,0:T(8,128)(2,1)S(1)}, bf16[112,2048]{1,0:T(8,128)(2,1)S(1)}, u32[]{:S(2)}, u32[]{:S(2)}) collective-permute-start(bf16[112,2048]{1,0:T(8,128)(2,1)S(1)} %get-tuple-element.159), channel_id=1, source_target_pairs={{0,16},{8,24},{16,0},{24,8},{1,17},{9,25},{17,1},{25,9},{2,18},{10... | collective-permute-start | bytes 1376264 | tf_op jit(solution)/shard_map/ppermute | solution.py:420
  105.3 18.3 %collective-permute-start.34 = (bf16[112,2048]{1,0:T(8,128)(2,1)S(1)}, bf16[112,2048]{1,0:T(8,128)(2,1)S(1)}, u32[]{:S(2)}, u32[]{:S(2)}) collective-permute-start(bf16[112,2048]{1,0:T(8,128)(2,1)S(1)} %get-tuple-element.183), channel_id=1, source_target_pairs={{0,6},{1,7},{2,0},{3,1},{4,2},{5,3},{6,4},{7,5},{8,14},{9,15},{10,... | collective-permute-start | bytes 1376264 | tf_op jit(solution)/shard_map/ppermute | solution.py:424
  119.5 8.5 %collective-permute-start.32 = (bf16[64,2048]{1,0:T(8,128)(2,1)S(1)}, bf16[64,2048]{1,0:T(8,128)(2,1)S(1)}, u32[]{:S(2)}, u32[]{:S(2)}) collective-permute-start(bf16[64,2048]{1,0:T(8,128)(2,1)S(1)} %get-tuple-element.181), channel_id=1, source_target_pairs={{0,16},{8,24},{16,0},{24,8},{1,17},{9,25},{17,1},{25,9},{2,18},{10... | collective-permute-start | bytes 786440 | tf_op jit(solution)/shard_map/ppermute | solution.py:420
  120.1 28.2 %copy-start.1 = (bf16[1,111,2048]{2,1,0:T(8,128)(2,1)S(1)}, bf16[1,111,2048]{2,1,0:T(8,128)(2,1)}, u32[]{:S(2)}) copy-start(bf16[1,111,2048]{2,1,0:T(8,128)(2,1)} %param.21) | copy-start | bytes 1363972
  120.1 7.8 %collective-permute-start.33 = (bf16[48,2048]{1,0:T(8,128)(2,1)S(1)}, bf16[48,2048]{1,0:T(8,128)(2,1)S(1)}, u32[]{:S(2)}, u32[]{:S(2)}) collective-permute-start(bf16[48,2048]{1,0:T(8,128)(2,1)S(1)} %get-tuple-element.182), channel_id=1, source_target_pairs={{0,8},{8,0},{16,24},{24,16},{1,9},{9,1},{17,25},{25,17},{2,10},{10... | collective-permute-start | bytes 589832 | tf_op jit(solution)/shard_map/ppermute | solution.py:416
  121.8 10.3 %collective-permute-start.31 = (bf16[112,2048]{1,0:T(8,128)(2,1)S(1)}, bf16[112,2048]{1,0:T(8,128)(2,1)S(1)}, u32[]{:S(2)}, u32[]{:S(2)}) collective-permute-start(bf16[112,2048]{1,0:T(8,128)(2,1)S(1)} %add_convert_fusion.1), channel_id=1, source_target_pairs={{0,2},{1,3},{2,4},{3,5},{4,6},{5,7},{6,0},{7,1},{8,10},{9,11},{10,... | collective-permute-start | bytes 1376264 | tf_op jit(solution)/shard_map/ppermute | solution.py:424
  122.1 12.3 %collective-permute-start.39 = (bf16[64,2048]{1,0:T(8,128)(2,1)S(1)}, bf16[64,2048]{1,0:T(8,128)(2,1)S(1)}, u32[]{:S(2)}, u32[]{:S(2)}) collective-permute-start(bf16[64,2048]{1,0:T(8,128)(2,1)S(1)} %get-tuple-element.195), channel_id=1, source_target_pairs={{0,16},{8,24},{16,0},{24,8},{1,17},{9,25},{17,1},{25,9},{2,18},{10... | collective-permute-start | bytes 786440 | tf_op jit(solution)/shard_map/ppermute | solution.py:420
  123.6 9.2 %collective-permute-start.38 = (bf16[48,2048]{1,0:T(8,128)(2,1)S(1)}, bf16[48,2048]{1,0:T(8,128)(2,1)S(1)}, u32[]{:S(2)}, u32[]{:S(2)}) collective-permute-start(bf16[48,2048]{1,0:T(8,128)(2,1)S(1)} %get-tuple-element.194), channel_id=1, source_target_pairs={{0,8},{8,0},{16,24},{24,16},{1,9},{9,1},{17,25},{25,17},{2,10},{10... | collective-permute-start | bytes 589832 | tf_op jit(solution)/shard_map/ppermute | solution.py:416
  128.1 9.6 %collective-permute-start.37 = (bf16[64,2048]{1,0:T(8,128)(2,1)S(1)}, bf16[64,2048]{1,0:T(8,128)(2,1)S(1)}, u32[]{:S(2)}, u32[]{:S(2)}) collective-permute-start(bf16[64,2048]{1,0:T(8,128)(2,1)S(1)} %add_convert_fusion.2), channel_id=1, source_target_pairs={{0,8},{8,0},{16,24},{24,16},{1,9},{9,1},{17,25},{25,17},{2,10},{10... | collective-permute-start | bytes 786440 | tf_op jit(solution)/shard_map/ppermute | solution.py:416
  129.0 8.4 %collective-permute-start.40 = (bf16[48,2048]{1,0:T(8,128)(2,1)S(1)}, bf16[48,2048]{1,0:T(8,128)(2,1)S(1)}, u32[]{:S(2)}, u32[]{:S(2)}) collective-permute-start(bf16[48,2048]{1,0:T(8,128)(2,1)S(1)} %add_convert_fusion.3), channel_id=1, source_target_pairs={{0,16},{8,24},{16,0},{24,8},{1,17},{9,25},{17,1},{25,9},{2,18},{10... | collective-permute-start | bytes 589832 | tf_op jit(solution)/shard_map/ppermute | solution.py:420
  132.2 10.8 %collective-permute-start.35 = (bf16[112,2048]{1,0:T(8,128)(2,1)S(1)}, bf16[112,2048]{1,0:T(8,128)(2,1)S(1)}, u32[]{:S(2)}, u32[]{:S(2)}) collective-permute-start(bf16[112,2048]{1,0:T(8,128)(2,1)S(1)} %get-tuple-element.189), channel_id=1, source_target_pairs={{0,8},{8,0},{16,24},{24,16},{1,9},{9,1},{17,25},{25,17},{2,10},{10... | collective-permute-start | bytes 1376264 | tf_op jit(solution)/shard_map/ppermute | solution.py:416
  132.8 10.2 %collective-permute-start.36 = (bf16[112,2048]{1,0:T(8,128)(2,1)S(1)}, bf16[112,2048]{1,0:T(8,128)(2,1)S(1)}, u32[]{:S(2)}, u32[]{:S(2)}) collective-permute-start(bf16[112,2048]{1,0:T(8,128)(2,1)S(1)} %get-tuple-element.190), channel_id=1, source_target_pairs={{0,16},{8,24},{16,0},{24,8},{1,17},{9,25},{17,1},{25,9},{2,18},{10... | collective-permute-start | bytes 1376264 | tf_op jit(solution)/shard_map/ppermute | solution.py:420
  138.0 10.3 %collective-permute-start.41 = (bf16[112,2048]{1,0:T(8,128)(2,1)S(1)}, bf16[112,2048]{1,0:T(8,128)(2,1)S(1)}, u32[]{:S(2)}, u32[]{:S(2)}) collective-permute-start(bf16[112,2048]{1,0:T(8,128)(2,1)S(1)} %gather.1), channel_id=1, source_target_pairs={{0,2},{1,3},{2,4},{3,5},{4,6},{5,7},{6,0},{7,1},{8,10},{9,11},{10,... | collective-permute-start | bytes 1376264 | tf_op jit(solution)/shard_map/ppermute | solution.py:424

commit v13 on v12

--- a/solution.py
+++ b/solution.py
@@ -43,21 +43,6 @@
     )
 
 
-def fetched_prepare_kernel(ranking, hidden_in, gain_in, router_in, routes_in, out_ref, *scratch):
-    shifted, hidden_ref, gain_ref, router_ref, routes_ref, sems = scratch
-    sources = (hidden_in, gain_in, router_in, routes_in)
-    targets = (hidden_ref, gain_ref, router_ref, routes_ref)
-    copies = [
-        pltpu.make_async_copy(source, target, sems.at[i])
-        for i, (source, target) in enumerate(zip(sources, targets))
-    ]
-    for copy in copies:
-        copy.start()
-    for copy in copies:
-        copy.wait()
-    prepare_kernel(ranking, *targets, out_ref, shifted)
-
-
 def prepare_kernel(ranking, hidden_ref, gain_ref, router_ref, routes_ref, out_ref, *scratch):
     experts, width = router_ref.shape
     if scratch:
@@ -106,24 +91,14 @@
     width = hidden.shape[1]
     rows = routes.shape[0]
     extra = -(-(3 if ranking else 2) * router.shape[1] // 128) * 128
-    operands = (hidden, norm_gain.reshape(1, width), router.T, routes.T)
-    fetched = rows > hidden.shape[0]
-    kernel, options = prepare_kernel, {}
-    if fetched:
-        kernel = fetched_prepare_kernel
-        options = dict(
-            in_specs=[pl.BlockSpec(memory_space=pltpu.HBM)] * 4,
-            scratch_shapes=[pltpu.VMEM((rows, width), jnp.float32)]
-            + [pltpu.VMEM(operand.shape, operand.dtype) for operand in operands]
-            + [pltpu.SemaphoreType.DMA((4,))],
-        )
+    shifted = rows > hidden.shape[0]
     return pl.pallas_call(
-        functools.partial(kernel, ranking),
+        functools.partial(prepare_kernel, ranking),
         out_shape=jax.ShapeDtypeStruct((rows, width + extra), jnp.bfloat16),
+        scratch_shapes=[pltpu.VMEM((rows, width), jnp.float32)] if shifted else [],
         compiler_params=pltpu.CompilerParams(vmem_limit_bytes=32 << 20),
         name="prepare",
-        **options,
-    )(*operands)
+    )(hidden, norm_gain.reshape(1, width), router.T, routes.T)
 
 
 def expert_kernel(expert_ref, rows_ref, gate_ref, up_ref, down_ref, out_ref):
@@ -172,27 +147,11 @@
     sources = [refs.pop(0) for _ in piece_rows]
     weight_refs = [refs.pop(0) for _ in range(6)]
     targets = [refs.pop(0) for _ in block_rows]
-    decodes, rows, weights, downs, slots, inner, results, spread, sums, row_sem, weight_sem, out_sem = refs
-    width = sums.shape[1]
+    rows, weights, downs, slots, inner, results, spread, weight_sem = refs
+    width = results.shape[2]
     tokens = block_rows[0]
     pair_rows = 2 * tokens
     pair_slots = 2 * cap
-    few = decodes.shape[0]
-    row_copies = ([], [])
-    at = 0
-    for ref, count in zip(sources, piece_rows):
-        if ref is sources[-1]:
-            count -= few
-            copy = pltpu.make_async_copy(ref.at[pl.ds(count, few)], decodes, row_sem.at[len(sources)])
-            row_copies[0].append(copy)
-        if count:
-            p = 0 if at < pair_rows else 1
-            index = len(row_copies[0]) + len(row_copies[1]) if ref is not sources[-1] else len(sources) - 1
-            copy = pltpu.make_async_copy(
-                ref.at[pl.ds(0, count)], rows.at[pl.ds(at, count)], row_sem.at[index]
-            )
-            row_copies[p].append(copy)
-        at += count
     up_copies = [
         pltpu.make_async_copy(weight_refs[3 * e + i], weights.at[2 * e + i], weight_sem.at[2 * e + i])
         for e in range(2)
@@ -202,18 +161,22 @@
         pltpu.make_async_copy(weight_refs[3 * e + 2], downs.at[e], weight_sem.at[4 + e])
         for e in range(2)
     ]
-    for copy in row_copies[0] + row_copies[1] + up_copies + down_copies:
+    for copy in up_copies + down_copies:
         copy.start()
+    few = piece_rows[-1] - (2 * pair_rows - sum(piece_rows[:-1]))
+    at = 0
+    for ref, count in zip(sources, piece_rows):
+        if ref is sources[-1]:
+            count -= few
+            decodes = ref[count:, :].astype(jnp.float32)
+        if count:
+            rows[pl.ds(at, count), :] = ref[:count, :]
+        at += count
     is_first = lax.broadcasted_iota(jnp.int32, (few, 1), 0) == 0
-
-    def receive(p):
-        for copy in row_copies[p]:
-            copy.wait()
-        for j in (2 * p, 2 * p + 1):
-            part = pl.ds(j * tokens, few)
-            decode_row = decodes[...].astype(jnp.float32)[j : j + 1]
-            kept = rows[part, :].astype(jnp.float32)
-            rows[part, :] = jnp.where(is_first, decode_row, kept).astype(jnp.bfloat16)
+    for j in range(4):
+        part = pl.ds(j * tokens, few)
+        kept = rows[part, :].astype(jnp.float32)
+        rows[part, :] = jnp.where(is_first, decodes[j : j + 1], kept).astype(jnp.bfloat16)
 
     experts = ids_ref[2]
     extra = rows.shape[1] - width
@@ -230,7 +193,6 @@
         return jnp.where(second, float(cap), 0.0)
 
     for p in range(2):
-        receive(p)
         ranks = lax.dot_general(
             wanted, rows[pairs[p], width:], (((1,), (1,)), ((), ())), preferred_element_type=jnp.float32
         )
@@ -289,21 +251,14 @@
     activate(1, gate_1, up_1)
     down_copies[1].wait()
     finish(1)
-    out_copies = []
-    at = 0
+    ends = [sum(block_rows[: i + 1]) for i in range(len(block_rows))]
     for p in range(2):
         total = jnp.dot(spread[p], results[p], preferred_element_type=jnp.float32)
-        sums[pairs[p], :] = total.astype(jnp.bfloat16)
-        while len(out_copies) < len(targets) and at < (p + 1) * pair_rows:
-            count = block_rows[len(out_copies)]
-            copy = pltpu.make_async_copy(
-                sums.at[pl.ds(at, count)], targets[len(out_copies)], out_sem.at[len(out_copies)]
-            )
-            copy.start()
-            out_copies.append(copy)
-            at += count
-    for copy in out_copies:
-        copy.wait()
+        total = total.astype(jnp.bfloat16)
+        for ref, count, end in zip(targets, block_rows, ends):
+            if p * pair_rows < end <= (p + 1) * pair_rows:
+                at = end - count - p * pair_rows
+                ref[...] = total[at : at + count]
 
 
 def run_plane(ids, cap, few, pieces, block_rows, weights):
@@ -315,11 +270,12 @@
     anywhere = pl.BlockSpec(memory_space=pl.ANY)
     return pl.pallas_call(
         functools.partial(plane_kernel, cap, piece_rows, block_rows),
-        in_specs=[pl.BlockSpec(memory_space=pltpu.SMEM)] + [anywhere] * (len(pieces) + 6),
-        out_specs=[anywhere] * len(block_rows),
+        in_specs=[pl.BlockSpec(memory_space=pltpu.SMEM)]
+        + [pl.BlockSpec(memory_space=pltpu.VMEM)] * len(pieces)
+        + [anywhere] * 6,
+        out_specs=[pl.BlockSpec(memory_space=pltpu.VMEM)] * len(block_rows),
         out_shape=[jax.ShapeDtypeStruct((count, width), kept) for count in block_rows],
         scratch_shapes=[
-            pltpu.VMEM((few, padded), kept),
             pltpu.VMEM((total, padded), kept),
             pltpu.VMEM((4, width, units), kept),
             pltpu.VMEM((2, units, width), kept),
@@ -327,10 +283,7 @@
             pltpu.VMEM((2, 4 * cap, units), kept),
             pltpu.VMEM((2, 4 * cap, width), kept),
             pltpu.VMEM((2, total // 2, 4 * cap), kept),
-            pltpu.VMEM((total, width), kept),
-            pltpu.SemaphoreType.DMA((len(pieces) + 1,)),
             pltpu.SemaphoreType.DMA((6,)),
-            pltpu.SemaphoreType.DMA((len(block_rows),)),
         ],
         compiler_params=pltpu.CompilerParams(vmem_limit_bytes=48 << 20),
         cost_estimate=pl.CostEstimate(
@@ -465,7 +418,7 @@
         [first_expert + my_blk, first_expert + (my_blk ^ 1), jnp.int32(experts)]
     ).astype(jnp.int32)
     cap = (2 * tokens * ids.shape[1] + experts - 1) // experts
-    cut = (tokens // 2 + 15) // 16 * 16
+    cut = tokens // 2 // 16 * 16
     few = 16
 
     def spread_sides(block):
@@ -487,8 +440,8 @@
     prefill = prefill_hidden[0]
     block_0 = prepare(prefill, norm_gain, router, ids, "block")
     block_0, queries, cache_keys, expert_gate = fence(block_0, queries, cache_keys, expert_gate)
+    block_1 = around_z(block_0)
     sides_0 = spread_sides(block_0)
-    block_1 = around_z(block_0)
     other_gate = across_chip(expert_gate[0])
     attended = attend(queries, cache_keys, cache_values, lengths, sinks)
     partial_proj = jnp.dot(attended, out_proj, preferred_element_type=jnp.float32)

time: 150 us -> 147 us (0.980)
  Pallas kernels: 50.5 us -> 42.8 us
  waiting for transfers between devices: 40.9 us -> 44.2 us
  starting transfers between devices: 41.6 us -> 43.3 us
    ppermute x15, waiting for transfers between devices: 14.1 us -> 4.43 us  [along_x(): return lax.ppermute(value, 'kv', [(i, i ^ 1) for i in range(4)])]
    ppermute x15, waiting for transfers between devices: 16.1 us -> 25.7 us  [along_y(): return lax.ppermute(value, 'kv', [(i, i ^ 2) for i in range(4)])]
    pallas_call x4, Pallas kernels: 48 us -> 40.8 us  [run_plane(): pl.pallas_call(functools.partial(plane_kernel, cap, piece_rows, block_row...]
    ppermute x9, waiting for transfers between devices: 10.7 us -> 14.1 us  [around_z(): lax.ppermute(value, 'blk', [(i, (i + 2 * hops) % 8) for i in range(8)])]
    ppermute x9, starting transfers between devices: 7.51 us -> 10.8 us  [around_z(): lax.ppermute(value, 'blk', [(i, (i + 2 * hops) % 8) for i in range(8)])]
    ppermute x15, starting transfers between devices: 18.2 us -> 15.1 us  [along_y(): return lax.ppermute(value, 'kv', [(i, i ^ 2) for i in range(4)])]
    ppermute x15, starting transfers between devices: 15.4 us -> 17 us  [along_x(): return lax.ppermute(value, 'kv', [(i, i ^ 1) for i in range(4)])]
  transfers between devices with their start and end apart: 42 -> 42, of which waited for: 14 -> 18; matrix products, arithmetic and copies ran while one was open for 6% -> 6% of each run, Pallas kernels for 33% -> 28%
where the time goes in v13:
time: 147 us
  waiting for transfers between devices  44.2 us (30%)
  starting transfers between devices  43.3 us (29%)
  Pallas kernels  42.8 us (29%)
  local copies, waits for them, and re-layouts  6.34 us (4%)
  other arithmetic  4.91 us (3%)
  matrix products  4.85 us (3%)
    pallas_call x4, Pallas kernels, run_plane(): pl.pallas_call(functools.partial(plane_kernel, cap, piece_rows, block_row...  40.8 us
    ppermute x15, waiting for transfers between devices, along_y(): return lax.ppermute(value, 'kv', [(i, i ^ 2) for i in range(4)])  25.7 us
    ppermute x15, starting transfers between devices, along_x(): return lax.ppermute(value, 'kv', [(i, i ^ 1) for i in range(4)])  17 us
    ppermute x15, starting transfers between devices, along_y(): return lax.ppermute(value, 'kv', [(i, i ^ 2) for i in range(4)])  15.1 us
    ppermute x9, waiting for transfers between devices, around_z(): lax.ppermute(value, 'blk', [(i, (i + 2 * hops) % 8) for i in range(8)])  14.1 us
    ppermute x9, starting transfers between devices, around_z(): lax.ppermute(value, 'blk', [(i, (i + 2 * hops) % 8) for i in range(8)])  10.8 us
    unnamed x24, local copies, waits for them, and re-layouts  6.03 us
    ppermute x15, waiting for transfers between devices, along_x(): return lax.ppermute(value, 'kv', [(i, i ^ 1) for i in range(4)])  4.43 us
  transfers between devices with their start and end apart: 42, of which 18 were waited for; matrix products, arithmetic and copies ran while one was open for 6% of the time, Pallas kernels for 28%

profile of v13, /device:TPU:0, one launch (start us, length us, event | category | flops | bytes accessed | tf_op | source)
XLA Modules:
  0.0 146.8 jit_solution(11318748022750078597)
XLA Ops:
  0.0 1.0 copy-done
  1.0 0.9 copy-done.2
  1.9 0.7 copy-done.4
  2.6 0.7 copy-done.6
  3.3 0.8 prepare.2.refs_1_
  4.1 3.0 %collective-permute-start = (bf16[112,2176]{1,0:T(8,128)(2,1)S(1)}, bf16[112,2176]{1,0:T(8,128)(2,1)S(1)}, u32[]{:S(2)}, u32[]{:S(2)}) collective-permute-start(bf16[112,2176]{1,0:T(8,128)(2,1)S(1)} %prepare.2.refs_1_), channel_id=1, source_target_pairs={{0,8},{8,0},{16,24},{24,16},{1,9},{9,1},{17,25},{25,17},{2,10},{10... | collective-permute-start | bytes 1462280 | tf_op jit(solution)/shard_map/ppermute | solution.py:369
  7.1 1.5 %collective-permute-start.1 = (bf16[112,2176]{1,0:T(8,128)(2,1)S(1)}, bf16[112,2176]{1,0:T(8,128)(2,1)S(1)}, u32[]{:S(2)}, u32[]{:S(2)}) collective-permute-start(bf16[112,2176]{1,0:T(8,128)(2,1)S(1)} %prepare.2.refs_1_), channel_id=1, source_target_pairs={{0,16},{8,24},{16,0},{24,8},{1,17},{9,25},{17,1},{25,9},{2,18},{10... | collective-permute-start | bytes 1462280 | tf_op jit(solution)/shard_map/ppermute | solution.py:373
  8.6 1.6 %collective-permute-start.2 = (bf16[112,2176]{1,0:T(8,128)(2,1)S(1)}, bf16[112,2176]{1,0:T(8,128)(2,1)}, u32[]{:S(2)}, u32[]{:S(2)}) collective-permute-start(bf16[112,2176]{1,0:T(8,128)(2,1)S(1)} %prepare.2.refs_1_), channel_id=1, source_target_pairs={{0,2},{1,3},{2,4},{3,5},{4,6},{5,7},{6,0},{7,1},{8,10},{9,11},{10,... | collective-permute-start | bytes 1462280 | tf_op jit(solution)/shard_map/ppermute | solution.py:377
  10.7 0.7 minimum_subtract_fusion
  11.5 0.9 broadcast_in_dim.76
  12.4 1.0 convert_reduce_fusion
  13.4 3.5 %fusion.36 = (f32[4,8]{1,0:T(4,128)S(1)}, f32[4,8,4096]{2,1,0:T(8,128)S(1)}) fusion(bf16[4,4096,1,128]{3,1,2,0:T(8,128)(2,1)} %param.15, bf16[1,4,8,128]{3,1,2,0:T(4,128)(2,1)} %bitcast.53, pred[4,4096]{1,0:T(4,128)(4,1)S(1)} %iota_compare_fusion.2), kind=kOutput, calls=%fused_computation.61 | convolution fusion | flops 33947616 | bytes 4743296 | tf_op jit(solution)/shard_map/rgd,rjd->rgj/dot_general | solution.py:27
  17.2 0.7 fusion.11
  18.0 1.1 copy-done.10
  19.1 0.7 convolution_add_fusion
  19.8 0.6 collective-permute-start.6
  20.4 2.5 %collective-permute-done.2.refs_1_ = bf16[112,2176]{1,0:T(8,128)(2,1)} collective-permute-done((bf16[112,2176]{1,0:T(8,128)(2,1)S(1)}, bf16[112,2176]{1,0:T(8,128)(2,1)}, u32[]{:S(2)}, u32[]{:S(2)}) %collective-permute-start.2) | collective-permute-done | bytes 487456 | tf_op jit(solution)/shard_map/ppermute | solution.py:377
  22.9 0.6 collective-permute-start.5
  23.5 0.6 collective-permute-start.4
  24.3 5.1 %collective-permute-done.4.refs_4_ = bf16[48,2176]{1,0:T(8,128)(2,1)S(1)} collective-permute-done((bf16[48,2176]{1,0:T(8,128)(2,1)S(1)}, bf16[48,2176]{1,0:T(8,128)(2,1)S(1)}, u32[]{:S(2)}, u32[]{:S(2)}) %collective-permute-start.4) | collective-permute-done | bytes 208928 | tf_op jit(solution)/shard_map/ppermute | solution.py:373
  29.4 0.7 copy-done.7
  30.7 1.5 %collective-permute-start.10 = (bf16[112,2176]{1,0:T(8,128)(2,1)}, bf16[112,2176]{1,0:T(8,128)(2,1)S(1)}, u32[]{:S(2)}, u32[]{:S(2)}) collective-permute-start(bf16[112,2176]{1,0:T(8,128)(2,1)} %collective-permute-done.2.refs_1_), channel_id=1, source_target_pairs={{0,16},{8,24},{16,0},{24,8},{1,17},{9,25},{17,1},{25,9},{2,18},{10... | collective-permute-start | bytes 1462280 | tf_op jit(solution)/shard_map/ppermute | solution.py:373
  32.2 1.3 collective-permute-start.11
  33.5 0.8 collective-permute-start.9
  34.3 0.7 collective-permute-done.8
  35.7 9.3 %collective-permute-done.10.refs_3_ = bf16[112,2176]{1,0:T(8,128)(2,1)S(1)} collective-permute-done((bf16[112,2176]{1,0:T(8,128)(2,1)}, bf16[112,2176]{1,0:T(8,128)(2,1)S(1)}, u32[]{:S(2)}, u32[]{:S(2)}) %collective-permute-start.10) | collective-permute-done | bytes 487456 | tf_op jit(solution)/shard_map/ppermute | solution.py:373
  45.0 2.1 %collective-permute-done.11.refs_1_ = bf16[112,2176]{1,0:T(8,128)(2,1)S(1)} collective-permute-done((bf16[112,2176]{1,0:T(8,128)(2,1)}, bf16[112,2176]{1,0:T(8,128)(2,1)S(1)}, u32[]{:S(2)}, u32[]{:S(2)}) %collective-permute-start.11) | collective-permute-done | bytes 487456 | tf_op jit(solution)/shard_map/ppermute | solution.py:377
  47.2 1.5 %collective-permute-start.15 = (bf16[112,2176]{1,0:T(8,128)(2,1)S(1)}, bf16[112,2176]{1,0:T(8,128)(2,1)S(1)}, u32[]{:S(2)}, u32[]{:S(2)}) collective-permute-start(bf16[112,2176]{1,0:T(8,128)(2,1)S(1)} %collective-permute-done.11.refs_1_), channel_id=1, source_target_pairs={{0,8},{8,0},{16,24},{24,16},{1,9},{9,1},{17,25},{25,17},{2,10},{10... | collective-permute-start | bytes 1462280 | tf_op jit(solution)/shard_map/ppermute | solution.py:369
  48.7 0.5 collective-permute-start.16
  49.2 0.5 collective-permute-start.17
  49.8 0.9 collective-permute-start.14
  50.7 1.6 %collective-permute-start.13 = (bf16[48,2176]{1,0:T(8,128)(2,1)S(1)}, bf16[48,2176]{1,0:T(8,128)(2,1)S(1)}, u32[]{:S(2)}, u32[]{:S(2)}) collective-permute-start(bf16[48,2176]{1,0:T(8,128)(2,1)S(1)} %slice.45), channel_id=1, source_target_pairs={{0,16},{8,24},{16,0},{24,8},{1,17},{9,25},{17,1},{25,9},{2,18},{10... | collective-permute-start | bytes 626696 | tf_op jit(solution)/shard_map/ppermute | solution.py:373
  52.3 0.9 copy-done.8
  53.3 10.1 %plane.4 = (bf16[112,2048]{1,0:T(8,128)(2,1)S(1)}, bf16[112,2048]{1,0:T(8,128)(2,1)S(1)}, bf16[112,2048]{1,0:T(8,128)(2,1)S(1)}, bf16[48,2048]{1,0:T(8,128)(2,1)S(1)}, bf16[64,2048]{1,0:T(8,128)(2,1)S(1)}) custom-call(s32[3]{0:T(128)S(1)} %pad_add_fusion.refs_0_, bf16[112,2176]{1,0:T(8,128)(2,1)S(1)} %prepare.2.refs_1_, ...), custom_call_target="tpu_custom_call" | custom-call | flops 8455716864 | bytes 25165824 | tf_op jit(solution)/shard_map/plane/pallas_call | solution.py:271
  63.4 1.7 %collective-permute-done.13.refs_4_ = bf16[48,2176]{1,0:T(8,128)(2,1)S(1)} collective-permute-done((bf16[48,2176]{1,0:T(8,128)(2,1)S(1)}, bf16[48,2176]{1,0:T(8,128)(2,1)S(1)}, u32[]{:S(2)}, u32[]{:S(2)}) %collective-permute-start.13) | collective-permute-done | bytes 208928 | tf_op jit(solution)/shard_map/ppermute | solution.py:373
  65.4 1.6 %collective-permute-start.18 = (bf16[112,2176]{1,0:T(8,128)(2,1)S(1)}, bf16[112,2176]{1,0:T(8,128)(2,1)S(1)}, u32[]{:S(2)}, u32[]{:S(2)}) collective-permute-start(bf16[112,2176]{1,0:T(8,128)(2,1)S(1)} %slice.47.refs_1_), channel_id=1, source_target_pairs={{0,8},{8,0},{16,24},{24,16},{1,9},{9,1},{17,25},{25,17},{2,10},{10... | collective-permute-start | bytes 1462280 | tf_op jit(solution)/shard_map/ppermute | solution.py:369
  67.9 0.9 collective-permute-start.22
  68.7 1.5 %collective-permute-start.21 = (bf16[48,2048]{1,0:T(8,128)(2,1)S(1)}, bf16[48,2048]{1,0:T(8,128)(2,1)S(1)}, u32[]{:S(2)}, u32[]{:S(2)}) collective-permute-start(bf16[48,2048]{1,0:T(8,128)(2,1)S(1)} %get-tuple-element.129), channel_id=1, source_target_pairs={{0,16},{8,24},{16,0},{24,8},{1,17},{9,25},{17,1},{25,9},{2,18},{10... | collective-permute-start | bytes 589832 | tf_op jit(solution)/shard_map/ppermute | solution.py:373
  70.3 10.6 %plane.5 = (bf16[112,2048]{1,0:T(8,128)(2,1)S(1)}, bf16[112,2048]{1,0:T(8,128)(2,1)S(1)}, bf16[112,2048]{1,0:T(8,128)(2,1)S(1)}, bf16[112,2048]{1,0:T(8,128)(2,1)S(1)}) custom-call(s32[3]{0:T(128)S(1)} %pad_add_fusion.refs_0_, bf16[112,2176]{1,0:T(8,128)(2,1)} %collective-permute-done.2.refs_1_, bf16[112,2176]{1,0:T(8,128)(2,1)S(1)} %collective-permute-done.9.refs_2_, ...), custom_call_target="tpu_custom_call" | custom-call | flops 8455716864 | bytes 25165824 | tf_op jit(solution)/shard_map/plane/pallas_call | solution.py:271
  80.8 1.2 collective-permute-done.21.passed_0_ref
  82.8 1.4 collective-permute-start.25
  84.2 0.7 collective-permute-start.26
  84.9 0.7 collective-permute-start.27
  85.7 1.4 collective-permute-start.24
  87.0 10.1 %plane.6 = (bf16[112,2048]{1,0:T(8,128)(2,1)S(1)}, bf16[112,2048]{1,0:T(8,128)(2,1)S(1)}, bf16[112,2048]{1,0:T(8,128)(2,1)S(1)}, bf16[112,2048]{1,0:T(8,128)(2,1)S(1)}) custom-call(s32[3]{0:T(128)S(1)} %pad_add_fusion.refs_0_, bf16[112,2176]{1,0:T(8,128)(2,1)S(1)} %collective-permute-done.11.refs_1_, bf16[112,2176]{1,0:T(8,128)(2,1)S(1)} %collective-permute-done.15.refs_2_, ...), custom_call_target="tpu_custom_call" | custom-call | flops 8455716864 | bytes 25165824 | tf_op jit(solution)/shard_map/plane/pallas_call | solution.py:271
  97.1 1.2 collective-permute-done.24.refs_4_
  98.7 2.2 %collective-permute-start.28 = (bf16[112,2048]{1,0:T(8,128)(2,1)S(1)}, bf16[112,2048]{1,0:T(8,128)(2,1)S(1)}, u32[]{:S(2)}, u32[]{:S(2)}) collective-permute-start(bf16[112,2048]{1,0:T(8,128)(2,1)S(1)} %get-tuple-element.156), channel_id=1, source_target_pairs={{0,2},{1,3},{2,4},{3,5},{4,6},{5,7},{6,0},{7,1},{8,10},{9,11},{10,... | collective-permute-start | bytes 1376264 | tf_op jit(solution)/shard_map/ppermute | solution.py:377
  101.4 3.7 %collective-permute-start.34 = (bf16[112,2048]{1,0:T(8,128)(2,1)S(1)}, bf16[112,2048]{1,0:T(8,128)(2,1)S(1)}, u32[]{:S(2)}, u32[]{:S(2)}) collective-permute-start(bf16[112,2048]{1,0:T(8,128)(2,1)S(1)} %get-tuple-element.183), channel_id=1, source_target_pairs={{0,6},{1,7},{2,0},{3,1},{4,2},{5,3},{6,4},{7,5},{8,14},{9,15},{10,... | collective-permute-start | bytes 1376264 | tf_op jit(solution)/shard_map/ppermute | solution.py:377
  105.1 10.1 %plane.7 = (bf16[112,2048]{1,0:T(8,128)(2,1)S(1)}, bf16[48,2048]{1,0:T(8,128)(2,1)S(1)}, bf16[64,2048]{1,0:T(8,128)(2,1)S(1)}, bf16[48,2048]{1,0:T(8,128)(2,1)S(...) custom-call(s32[3]{0:T(128)S(1)} %pad_add_fusion.refs_0_, ...), custom_call_target="tpu_custom_call" | custom-call | flops 8455716864 | bytes 25165824 | tf_op jit(solution)/shard_map/plane/pallas_call | solution.py:271
  115.4 0.7 collective-permute-start.33
  116.1 1.4 collective-permute-start.32
  117.7 1.6 %collective-permute-start.38 = (bf16[64,2048]{1,0:T(8,128)(2,1)S(1)}, bf16[64,2048]{1,0:T(8,128)(2,1)S(1)}, u32[]{:S(2)}, u32[]{:S(2)}) collective-permute-start(bf16[64,2048]{1,0:T(8,128)(2,1)S(1)} %get-tuple-element.194), channel_id=1, source_target_pairs={{0,8},{8,0},{16,24},{24,16},{1,9},{9,1},{17,25},{25,17},{2,10},{10... | collective-permute-start | bytes 786440 | tf_op jit(solution)/shard_map/ppermute | solution.py:369
  119.3 2.2 %collective-permute-done.34 = bf16[112,2048]{1,0:T(8,128)(2,1)S(1)} collective-permute-done((bf16[112,2048]{1,0:T(8,128)(2,1)S(1)}, bf16[112,2048]{1,0:T(8,128)(2,1)S(1)}, u32[]{:S(2)}, u32[]{:S(2)}) %collective-permute-start.34) | collective-permute-done | bytes 458784 | tf_op jit(solution)/shard_map/ppermute | solution.py:377
  121.9 1.8 %collective-permute-start.40 = (bf16[64,2048]{1,0:T(8,128)(2,1)S(1)}, bf16[64,2048]{1,0:T(8,128)(2,1)S(1)}, u32[]{:S(2)}, u32[]{:S(2)}) collective-permute-start(bf16[64,2048]{1,0:T(8,128)(2,1)S(1)} %add_convert_fusion.2), channel_id=1, source_target_pairs={{0,16},{8,24},{16,0},{24,8},{1,17},{9,25},{17,1},{25,9},{2,18},{10... | collective-permute-start | bytes 786440 | tf_op jit(solution)/shard_map/ppermute | solution.py:373
  123.7 1.8 %collective-permute-start.37 = (bf16[48,2048]{1,0:T(8,128)(2,1)S(1)}, bf16[48,2048]{1,0:T(8,128)(2,1)S(1)}, u32[]{:S(2)}, u32[]{:S(2)}) collective-permute-start(bf16[48,2048]{1,0:T(8,128)(2,1)S(1)} %add_convert_fusion.3), channel_id=1, source_target_pairs={{0,8},{8,0},{16,24},{24,16},{1,9},{9,1},{17,25},{25,17},{2,10},{10... | collective-permute-start | bytes 589832 | tf_op jit(solution)/shard_map/ppermute | solution.py:369
  125.5 4.1 %collective-permute-done.31.carried_ref = bf16[112,2048]{1,0:T(8,128)(2,1)S(1)} collective-permute-done((bf16[112,2048]{1,0:T(8,128)(2,1)S(1)}, bf16[112,2048]{1,0:T(8,128)(2,1)S(1)}, u32[]{:S(2)}, u32[]{:S(2)}) %collective-permute-start.31) | collective-permute-done | bytes 458784 | tf_op jit(solution)/shard_map/ppermute | solution.py:377
  129.7 0.9 collective-permute-start.35
  130.6 0.7 collective-permute-start.36
  131.5 3.5 %collective-permute-done.40.y_1_ref = bf16[64,2048]{1,0:T(8,128)(2,1)S(1)} collective-permute-done((bf16[64,2048]{1,0:T(8,128)(2,1)S(1)}, bf16[64,2048]{1,0:T(8,128)(2,1)S(1)}, u32[]{:S(2)}, u32[]{:S(2)}) %collective-permute-start.40) | collective-permute-done | bytes 262176 | tf_op jit(solution)/shard_map/ppermute | solution.py:373
  135.2 0.5 collective-permute-start.41
  135.7 3.6 %collective-permute-done.35 = bf16[112,2048]{1,0:T(8,128)(2,1)S(1)} collective-permute-done((bf16[112,2048]{1,0:T(8,128)(2,1)S(1)}, bf16[112,2048]{1,0:T(8,128)(2,1)S(1)}, u32[]{:S(2)}, u32[]{:S(2)}) %collective-permute-start.35) | collective-permute-done | bytes 458784 | tf_op jit(solution)/shard_map/ppermute | solution.py:369
  139.3 3.0 %collective-permute-done.36 = bf16[112,2048]{1,0:T(8,128)(2,1)S(1)} collective-permute-done((bf16[112,2048]{1,0:T(8,128)(2,1)S(1)}, bf16[112,2048]{1,0:T(8,128)(2,1)S(1)}, u32[]{:S(2)}, u32[]{:S(2)}) %collective-permute-start.36) | collective-permute-done | bytes 458784 | tf_op jit(solution)/shard_map/ppermute | solution.py:373
  142.3 3.2 %collective-permute-done.41 = bf16[112,2048]{1,0:T(8,128)(2,1)S(1)} collective-permute-done((bf16[112,2048]{1,0:T(8,128)(2,1)S(1)}, bf16[112,2048]{1,0:T(8,128)(2,1)S(1)}, u32[]{:S(2)}, u32[]{:S(2)}) %collective-permute-start.41) | collective-permute-done | bytes 458784 | tf_op jit(solution)/shard_map/ppermute | solution.py:377
  145.5 1.2 fusion.15
  (94 shorter events, 6.7 us)
Async XLA Ops:
  0.0 16.9 %copy-start.11 = (f32[8]{0:T(128)S(1)}, f32[8]{0:T(128)}, u32[]{:S(2)}) copy-start(f32[8]{0:T(128)} %param.18) | copy-start | bytes 100
  0.0 1.0 copy-start
  1.0 0.9 copy-start.2
  1.9 0.7 copy-start.4
  2.6 0.7 copy-start.6
  4.1 15.7 %collective-permute-start = (bf16[112,2176]{1,0:T(8,128)(2,1)S(1)}, bf16[112,2176]{1,0:T(8,128)(2,1)S(1)}, u32[]{:S(2)}, u32[]{:S(2)}) collective-permute-start(bf16[112,2176]{1,0:T(8,128)(2,1)S(1)} %prepare.2.refs_1_), channel_id=1, source_target_pairs={{0,8},{8,0},{16,24},{24,16},{1,9},{9,1},{17,25},{25,17},{2,10},{10... | collective-permute-start | bytes 1462280 | tf_op jit(solution)/shard_map/ppermute | solution.py:369
  7.1 13.3 %collective-permute-start.1 = (bf16[112,2176]{1,0:T(8,128)(2,1)S(1)}, bf16[112,2176]{1,0:T(8,128)(2,1)S(1)}, u32[]{:S(2)}, u32[]{:S(2)}) collective-permute-start(bf16[112,2176]{1,0:T(8,128)(2,1)S(1)} %prepare.2.refs_1_), channel_id=1, source_target_pairs={{0,16},{8,24},{16,0},{24,8},{1,17},{9,25},{17,1},{25,9},{2,18},{10... | collective-permute-start | bytes 1462280 | tf_op jit(solution)/shard_map/ppermute | solution.py:373
  8.6 14.3 %collective-permute-start.2 = (bf16[112,2176]{1,0:T(8,128)(2,1)S(1)}, bf16[112,2176]{1,0:T(8,128)(2,1)}, u32[]{:S(2)}, u32[]{:S(2)}) collective-permute-start(bf16[112,2176]{1,0:T(8,128)(2,1)S(1)} %prepare.2.refs_1_), channel_id=1, source_target_pairs={{0,2},{1,3},{2,4},{3,5},{4,6},{5,7},{6,0},{7,1},{8,10},{9,11},{10,... | collective-permute-start | bytes 1462280 | tf_op jit(solution)/shard_map/ppermute | solution.py:377
  10.2 12.7 %collective-permute-start.3 = (bf16[2048,768]{1,0:T(8,128)(2,1)}, bf16[2048,768]{1,0:T(8,128)(2,1)}, u32[]{:S(2)}, u32[]{:S(2)}) collective-permute-start(bf16[2048,768]{1,0:T(8,128)(2,1)} %bitcast.55), channel_id=1, source_target_pairs={{0,1},{1,0},{2,3},{3,2},{4,5},{5,4},{6,7},{7,6},{8,9},{9,8},{10,11... | collective-permute-start | bytes 9437192 | tf_op jit(solution)/shard_map/ppermute | solution.py:381
  10.2 14.1 %collective-permute-start.7 = (bf16[2048,768]{1,0:T(8,128)(2,1)}, bf16[2048,768]{1,0:T(8,128)(2,1)}, u32[]{:S(2)}, u32[]{:S(2)}) collective-permute-start(bf16[2048,768]{1,0:T(8,128)(2,1)} %bitcast.60), channel_id=1, source_target_pairs={{0,1},{1,0},{2,3},{3,2},{4,5},{5,4},{6,7},{7,6},{8,9},{9,8},{10,11... | collective-permute-start | bytes 9437192 | tf_op jit(solution)/shard_map/ppermute | solution.py:381
  11.5 5.7 %copy-start.9 = (bf16[4,4096,1,128]{3,1,2,0:T(8,128)(2,1)S(1)}, bf16[4,4096,1,128]{3,1,2,0:T(8,128)(2,1)}, u32[]{:S(2)}) copy-start(bf16[4,4096,1,128]{3,1,2,0:T(8,128)(2,1)} %param.16) | copy-start | bytes 12582916
  16.9 2.2 %copy-start.10 = (bf16[1024,2048]{1,0:T(8,128)(2,1)S(1)}, bf16[1024,2048]{1,0:T(8,128)(2,1)}, u32[]{:S(2)}) copy-start(bf16[1024,2048]{1,0:T(8,128)(2,1)} %param.19) | copy-start | bytes 12582916
  17.9 17.3 %copy-start.3 = (bf16[2048,32]{0,1:T(8,128)(2,1)S(1)}, bf16[2048,32]{0,1:T(8,128)(2,1)}, u32[]{:S(2)}) copy-start(bf16[2048,32]{0,1:T(8,128)(2,1)} %param.23) | copy-start | bytes 393220
  17.9 17.3 %copy-start.5 = (f32[2048]{0:T(1024)S(1)}, f32[2048]{0:T(1024)}, u32[]{:S(2)}) copy-start(f32[2048]{0:T(1024)} %param.22) | copy-start | bytes 24580
  19.8 4.5 %collective-permute-start.6 = (f32[8,2048]{1,0:T(8,128)S(1)}, f32[8,2048]{1,0:T(8,128)S(1)}, u32[]{:S(2)}, u32[]{:S(2)}) collective-permute-start(f32[8,2048]{1,0:T(8,128)S(1)} %pad_maximum_fusion.2), channel_id=1, source_target_pairs={{0,8},{8,0},{16,24},{24,16},{1,9},{9,1},{17,25},{25,17},{2,10},{10... | collective-permute-start | bytes 196616 | tf_op jit(solution)/shard_map/ppermute | solution.py:369
  22.9 7.2 %collective-permute-start.5 = (bf16[64,2176]{1,0:T(8,128)(2,1)S(1)}, bf16[64,2176]{1,0:T(8,128)(2,1)S(1)}, u32[]{:S(2)}, u32[]{:S(2)}) collective-permute-start(bf16[64,2176]{1,0:T(8,128)(2,1)S(1)} %slice.41), channel_id=1, source_target_pairs={{0,8},{8,0},{16,24},{24,16},{1,9},{9,1},{17,25},{25,17},{2,10},{10... | collective-permute-start | bytes 835592 | tf_op jit(solution)/shard_map/ppermute | solution.py:369
  23.5 5.9 %collective-permute-start.4 = (bf16[48,2176]{1,0:T(8,128)(2,1)S(1)}, bf16[48,2176]{1,0:T(8,128)(2,1)S(1)}, u32[]{:S(2)}, u32[]{:S(2)}) collective-permute-start(bf16[48,2176]{1,0:T(8,128)(2,1)S(1)} %slice.40), channel_id=1, source_target_pairs={{0,16},{8,24},{16,0},{24,8},{1,17},{9,25},{17,1},{25,9},{2,18},{10... | collective-permute-start | bytes 626696 | tf_op jit(solution)/shard_map/ppermute | solution.py:373
  29.4 0.7 copy-start.7
  30.1 17.1 %collective-permute-start.12 = (bf16[768,2048]{1,0:T(8,128)(2,1)}, bf16[768,2048]{1,0:T(8,128)(2,1)}, u32[]{:S(2)}, u32[]{:S(2)}) collective-permute-start(bf16[768,2048]{1,0:T(8,128)(2,1)} %bitcast.12.refs_9_.refs_7_), channel_id=1, source_target_pairs={{0,1},{1,0},{2,3},{3,2},{4,5},{5,4},{6,7},{7,6},{8,9},{9,8},{10,11... | collective-permute-start | bytes 9437192 | tf_op jit(solution)/shard_map/ppermute | solution.py:381
  30.1 4.9 %collective-permute-start.8 = (f32[8,2048]{1,0:T(8,128)S(1)}, f32[8,2048]{1,0:T(8,128)S(1)}, u32[]{:S(2)}, u32[]{:S(2)}) collective-permute-start(f32[8,2048]{1,0:T(8,128)S(1)} %fusion.35), channel_id=1, source_target_pairs={{0,16},{8,24},{16,0},{24,8},{1,17},{9,25},{17,1},{25,9},{2,18},{10... | collective-permute-start | bytes 196616 | tf_op jit(solution)/shard_map/ppermute | solution.py:373
  30.7 14.4 %collective-permute-start.10 = (bf16[112,2176]{1,0:T(8,128)(2,1)}, bf16[112,2176]{1,0:T(8,128)(2,1)S(1)}, u32[]{:S(2)}, u32[]{:S(2)}) collective-permute-start(bf16[112,2176]{1,0:T(8,128)(2,1)} %collective-permute-done.2.refs_1_), channel_id=1, source_target_pairs={{0,16},{8,24},{16,0},{24,8},{1,17},{9,25},{17,1},{25,9},{2,18},{10... | collective-permute-start | bytes 1462280 | tf_op jit(solution)/shard_map/ppermute | solution.py:373
  32.2 15.0 %collective-permute-start.11 = (bf16[112,2176]{1,0:T(8,128)(2,1)}, bf16[112,2176]{1,0:T(8,128)(2,1)S(1)}, u32[]{:S(2)}, u32[]{:S(2)}) collective-permute-start(bf16[112,2176]{1,0:T(8,128)(2,1)} %collective-permute-done.2.refs_1_), channel_id=1, source_target_pairs={{0,2},{1,3},{2,4},{3,5},{4,6},{5,7},{6,0},{7,1},{8,10},{9,11},{10,... | collective-permute-start | bytes 1462280 | tf_op jit(solution)/shard_map/ppermute | solution.py:377
  33.5 13.7 %collective-permute-start.9 = (bf16[112,2176]{1,0:T(8,128)(2,1)}, bf16[112,2176]{1,0:T(8,128)(2,1)S(1)}, u32[]{:S(2)}, u32[]{:S(2)}) collective-permute-start(bf16[112,2176]{1,0:T(8,128)(2,1)} %collective-permute-done.2.refs_1_), channel_id=1, source_target_pairs={{0,8},{8,0},{16,24},{24,16},{1,9},{9,1},{17,25},{25,17},{2,10},{10... | collective-permute-start | bytes 1462280 | tf_op jit(solution)/shard_map/ppermute | solution.py:369
  47.2 18.1 %collective-permute-start.15 = (bf16[112,2176]{1,0:T(8,128)(2,1)S(1)}, bf16[112,2176]{1,0:T(8,128)(2,1)S(1)}, u32[]{:S(2)}, u32[]{:S(2)}) collective-permute-start(bf16[112,2176]{1,0:T(8,128)(2,1)S(1)} %collective-permute-done.11.refs_1_), channel_id=1, source_target_pairs={{0,8},{8,0},{16,24},{24,16},{1,9},{9,1},{17,25},{25,17},{2,10},{10... | collective-permute-start | bytes 1462280 | tf_op jit(solution)/shard_map/ppermute | solution.py:369
  48.7 16.6 %collective-permute-start.16 = (bf16[112,2176]{1,0:T(8,128)(2,1)S(1)}, bf16[112,2176]{1,0:T(8,128)(2,1)S(1)}, u32[]{:S(2)}, u32[]{:S(2)}) collective-permute-start(bf16[112,2176]{1,0:T(8,128)(2,1)S(1)} %collective-permute-done.11.refs_1_), channel_id=1, source_target_pairs={{0,16},{8,24},{16,0},{24,8},{1,17},{9,25},{17,1},{25,9},{2,18},{10... | collective-permute-start | bytes 1462280 | tf_op jit(solution)/shard_map/ppermute | solution.py:373
  49.2 16.1 %collective-permute-start.17 = (bf16[128,2176]{1,0:T(8,128)(2,1)S(1)}, bf16[128,2176]{1,0:T(8,128)(2,1)S(1)}, u32[]{:S(2)}, u32[]{:S(2)}) collective-permute-start(bf16[128,2176]{1,0:T(8,128)(2,1)S(1)} %pad_maximum_fusion), channel_id=1, source_target_pairs={{0,2},{1,3},{2,4},{3,5},{4,6},{5,7},{6,0},{7,1},{8,10},{9,11},{10,... | collective-permute-start | bytes 1671176 | tf_op jit(solution)/shard_map/ppermute | solution.py:377
  49.8 15.5 %collective-permute-start.14 = (bf16[64,2176]{1,0:T(8,128)(2,1)S(1)}, bf16[64,2176]{1,0:T(8,128)(2,1)S(1)}, u32[]{:S(2)}, u32[]{:S(2)}) collective-permute-start(bf16[64,2176]{1,0:T(8,128)(2,1)S(1)} %slice.46), channel_id=1, source_target_pairs={{0,8},{8,0},{16,24},{24,16},{1,9},{9,1},{17,25},{25,17},{2,10},{10... | collective-permute-start | bytes 835592 | tf_op jit(solution)/shard_map/ppermute | solution.py:369
  50.7 14.3 %collective-permute-start.13 = (bf16[48,2176]{1,0:T(8,128)(2,1)S(1)}, bf16[48,2176]{1,0:T(8,128)(2,1)S(1)}, u32[]{:S(2)}, u32[]{:S(2)}) collective-permute-start(bf16[48,2176]{1,0:T(8,128)(2,1)S(1)} %slice.45), channel_id=1, source_target_pairs={{0,16},{8,24},{16,0},{24,8},{1,17},{9,25},{17,1},{25,9},{2,18},{10... | collective-permute-start | bytes 626696 | tf_op jit(solution)/shard_map/ppermute | solution.py:373
  52.3 0.9 copy-start.8
  65.4 16.9 %collective-permute-start.18 = (bf16[112,2176]{1,0:T(8,128)(2,1)S(1)}, bf16[112,2176]{1,0:T(8,128)(2,1)S(1)}, u32[]{:S(2)}, u32[]{:S(2)}) collective-permute-start(bf16[112,2176]{1,0:T(8,128)(2,1)S(1)} %slice.47.refs_1_), channel_id=1, source_target_pairs={{0,8},{8,0},{16,24},{24,16},{1,9},{9,1},{17,25},{25,17},{2,10},{10... | collective-permute-start | bytes 1462280 | tf_op jit(solution)/shard_map/ppermute | solution.py:369
  66.9 15.3 %collective-permute-start.19 = (bf16[112,2176]{1,0:T(8,128)(2,1)S(1)}, bf16[112,2176]{1,0:T(8,128)(2,1)S(1)}, u32[]{:S(2)}, u32[]{:S(2)}) collective-permute-start(bf16[112,2176]{1,0:T(8,128)(2,1)S(1)} %slice.47.refs_1_), channel_id=1, source_target_pairs={{0,16},{8,24},{16,0},{24,8},{1,17},{9,25},{17,1},{25,9},{2,18},{10... | collective-permute-start | bytes 1462280 | tf_op jit(solution)/shard_map/ppermute | solution.py:373
  67.5 14.8 %collective-permute-start.20 = (bf16[128,2176]{1,0:T(8,128)(2,1)S(1)}, bf16[128,2176]{1,0:T(8,128)(2,1)S(1)}, u32[]{:S(2)}, u32[]{:S(2)}) collective-permute-start(bf16[128,2176]{1,0:T(8,128)(2,1)S(1)} %pad_maximum_fusion.1), channel_id=1, source_target_pairs={{0,2},{1,3},{2,4},{3,5},{4,6},{5,7},{6,0},{7,1},{8,10},{9,11},{10,... | collective-permute-start | bytes 1671176 | tf_op jit(solution)/shard_map/ppermute | solution.py:377
  67.9 14.4 %collective-permute-start.22 = (bf16[64,2048]{1,0:T(8,128)(2,1)S(1)}, bf16[64,2048]{1,0:T(8,128)(2,1)S(1)}, u32[]{:S(2)}, u32[]{:S(2)}) collective-permute-start(bf16[64,2048]{1,0:T(8,128)(2,1)S(1)} %get-tuple-element.130), channel_id=1, source_target_pairs={{0,8},{8,0},{16,24},{24,16},{1,9},{9,1},{17,25},{25,17},{2,10},{10... | collective-permute-start | bytes 786440 | tf_op jit(solution)/shard_map/ppermute | solution.py:369
  68.7 13.3 %collective-permute-start.21 = (bf16[48,2048]{1,0:T(8,128)(2,1)S(1)}, bf16[48,2048]{1,0:T(8,128)(2,1)S(1)}, u32[]{:S(2)}, u32[]{:S(2)}) collective-permute-start(bf16[48,2048]{1,0:T(8,128)(2,1)S(1)} %get-tuple-element.129), channel_id=1, source_target_pairs={{0,16},{8,24},{16,0},{24,8},{1,17},{9,25},{17,1},{25,9},{2,18},{10... | collective-permute-start | bytes 589832 | tf_op jit(solution)/shard_map/ppermute | solution.py:373
  82.3 16.0 %collective-permute-start.23 = (bf16[128,2176]{1,0:T(8,128)(2,1)S(1)}, bf16[128,2176]{1,0:T(8,128)(2,1)S(1)}, u32[]{:S(2)}, u32[]{:S(2)}) collective-permute-start(bf16[128,2176]{1,0:T(8,128)(2,1)S(1)} %fusion.14), channel_id=1, source_target_pairs={{0,2},{1,3},{2,4},{3,5},{4,6},{5,7},{6,0},{7,1},{8,10},{9,11},{10,... | collective-permute-start | bytes 1671176 | tf_op jit(solution)/shard_map/ppermute | solution.py:377
  82.8 15.5 %collective-permute-start.25 = (bf16[64,2176]{1,0:T(8,128)(2,1)S(1)}, bf16[64,2176]{1,0:T(8,128)(2,1)S(1)}, u32[]{:S(2)}, u32[]{:S(2)}) collective-permute-start(bf16[64,2176]{1,0:T(8,128)(2,1)S(1)} %slice.51), channel_id=1, source_target_pairs={{0,8},{8,0},{16,24},{24,16},{1,9},{9,1},{17,25},{25,17},{2,10},{10... | collective-permute-start | bytes 835592 | tf_op jit(solution)/shard_map/ppermute | solution.py:369
  84.2 14.1 %collective-permute-start.26 = (bf16[112,2048]{1,0:T(8,128)(2,1)S(1)}, bf16[112,2048]{1,0:T(8,128)(2,1)S(1)}, u32[]{:S(2)}, u32[]{:S(2)}) collective-permute-start(bf16[112,2048]{1,0:T(8,128)(2,1)S(1)} %get-tuple-element.142), channel_id=1, source_target_pairs={{0,8},{8,0},{16,24},{24,16},{1,9},{9,1},{17,25},{25,17},{2,10},{10... | collective-permute-start | bytes 1376264 | tf_op jit(solution)/shard_map/ppermute | solution.py:369
  84.9 13.5 %collective-permute-start.27 = (bf16[112,2048]{1,0:T(8,128)(2,1)S(1)}, bf16[112,2048]{1,0:T(8,128)(2,1)S(1)}, u32[]{:S(2)}, u32[]{:S(2)}) collective-permute-start(bf16[112,2048]{1,0:T(8,128)(2,1)S(1)} %get-tuple-element.143), channel_id=1, source_target_pairs={{0,16},{8,24},{16,0},{24,8},{1,17},{9,25},{17,1},{25,9},{2,18},{10... | collective-permute-start | bytes 1376264 | tf_op jit(solution)/shard_map/ppermute | solution.py:373
  85.7 12.7 %collective-permute-start.24 = (bf16[48,2176]{1,0:T(8,128)(2,1)S(1)}, bf16[48,2176]{1,0:T(8,128)(2,1)S(1)}, u32[]{:S(2)}, u32[]{:S(2)}) collective-permute-start(bf16[48,2176]{1,0:T(8,128)(2,1)S(1)} %slice.50), channel_id=1, source_target_pairs={{0,16},{8,24},{16,0},{24,8},{1,17},{9,25},{17,1},{25,9},{2,18},{10... | collective-permute-start | bytes 626696 | tf_op jit(solution)/shard_map/ppermute | solution.py:373
  98.7 16.5 %collective-permute-start.28 = (bf16[112,2048]{1,0:T(8,128)(2,1)S(1)}, bf16[112,2048]{1,0:T(8,128)(2,1)S(1)}, u32[]{:S(2)}, u32[]{:S(2)}) collective-permute-start(bf16[112,2048]{1,0:T(8,128)(2,1)S(1)} %get-tuple-element.156), channel_id=1, source_target_pairs={{0,2},{1,3},{2,4},{3,5},{4,6},{5,7},{6,0},{7,1},{8,10},{9,11},{10,... | collective-permute-start | bytes 1376264 | tf_op jit(solution)/shard_map/ppermute | solution.py:377
  100.9 16.6 %collective-permute-start.29 = (bf16[112,2048]{1,0:T(8,128)(2,1)S(1)}, bf16[112,2048]{1,0:T(8,128)(2,1)S(1)}, u32[]{:S(2)}, u32[]{:S(2)}) collective-permute-start(bf16[112,2048]{1,0:T(8,128)(2,1)S(1)} %get-tuple-element.158), channel_id=1, source_target_pairs={{0,8},{8,0},{16,24},{24,16},{1,9},{9,1},{17,25},{25,17},{2,10},{10... | collective-permute-start | bytes 1376264 | tf_op jit(solution)/shard_map/ppermute | solution.py:369
  100.9 16.6 %collective-permute-start.30 = (bf16[112,2048]{1,0:T(8,128)(2,1)S(1)}, bf16[112,2048]{1,0:T(8,128)(2,1)S(1)}, u32[]{:S(2)}, u32[]{:S(2)}) collective-permute-start(bf16[112,2048]{1,0:T(8,128)(2,1)S(1)} %get-tuple-element.159), channel_id=1, source_target_pairs={{0,16},{8,24},{16,0},{24,8},{1,17},{9,25},{17,1},{25,9},{2,18},{10... | collective-permute-start | bytes 1376264 | tf_op jit(solution)/shard_map/ppermute | solution.py:373
  101.4 20.1 %collective-permute-start.34 = (bf16[112,2048]{1,0:T(8,128)(2,1)S(1)}, bf16[112,2048]{1,0:T(8,128)(2,1)S(1)}, u32[]{:S(2)}, u32[]{:S(2)}) collective-permute-start(bf16[112,2048]{1,0:T(8,128)(2,1)S(1)} %get-tuple-element.183), channel_id=1, source_target_pairs={{0,6},{1,7},{2,0},{3,1},{4,2},{5,3},{6,4},{7,5},{8,14},{9,15},{10,... | collective-permute-start | bytes 1376264 | tf_op jit(solution)/shard_map/ppermute | solution.py:377
  115.4 6.5 %collective-permute-start.33 = (bf16[64,2048]{1,0:T(8,128)(2,1)S(1)}, bf16[64,2048]{1,0:T(8,128)(2,1)S(1)}, u32[]{:S(2)}, u32[]{:S(2)}) collective-permute-start(bf16[64,2048]{1,0:T(8,128)(2,1)S(1)} %get-tuple-element.182), channel_id=1, source_target_pairs={{0,8},{8,0},{16,24},{24,16},{1,9},{9,1},{17,25},{25,17},{2,10},{10... | collective-permute-start | bytes 786440 | tf_op jit(solution)/shard_map/ppermute | solution.py:369
  116.0 29.5 %copy-start.1 = (bf16[1,111,2048]{2,1,0:T(8,128)(2,1)S(1)}, bf16[1,111,2048]{2,1,0:T(8,128)(2,1)}, u32[]{:S(2)}) copy-start(bf16[1,111,2048]{2,1,0:T(8,128)(2,1)} %param.21) | copy-start | bytes 1363972
  116.1 5.8 %collective-permute-start.32 = (bf16[48,2048]{1,0:T(8,128)(2,1)S(1)}, bf16[48,2048]{1,0:T(8,128)(2,1)S(1)}, u32[]{:S(2)}, u32[]{:S(2)}) collective-permute-start(bf16[48,2048]{1,0:T(8,128)(2,1)S(1)} %get-tuple-element.181), channel_id=1, source_target_pairs={{0,16},{8,24},{16,0},{24,8},{1,17},{9,25},{17,1},{25,9},{2,18},{10... | collective-permute-start | bytes 589832 | tf_op jit(solution)/shard_map/ppermute | solution.py:373
  117.7 11.9 %collective-permute-start.31 = (bf16[112,2048]{1,0:T(8,128)(2,1)S(1)}, bf16[112,2048]{1,0:T(8,128)(2,1)S(1)}, u32[]{:S(2)}, u32[]{:S(2)}) collective-permute-start(bf16[112,2048]{1,0:T(8,128)(2,1)S(1)} %add_convert_fusion.1), channel_id=1, source_target_pairs={{0,2},{1,3},{2,4},{3,5},{4,6},{5,7},{6,0},{7,1},{8,10},{9,11},{10,... | collective-permute-start | bytes 1376264 | tf_op jit(solution)/shard_map/ppermute | solution.py:377
  117.7 13.6 %collective-permute-start.38 = (bf16[64,2048]{1,0:T(8,128)(2,1)S(1)}, bf16[64,2048]{1,0:T(8,128)(2,1)S(1)}, u32[]{:S(2)}, u32[]{:S(2)}) collective-permute-start(bf16[64,2048]{1,0:T(8,128)(2,1)S(1)} %get-tuple-element.194), channel_id=1, source_target_pairs={{0,8},{8,0},{16,24},{24,16},{1,9},{9,1},{17,25},{25,17},{2,10},{10... | collective-permute-start | bytes 786440 | tf_op jit(solution)/shard_map/ppermute | solution.py:369
  121.5 9.1 %collective-permute-start.39 = (bf16[48,2048]{1,0:T(8,128)(2,1)S(1)}, bf16[48,2048]{1,0:T(8,128)(2,1)S(1)}, u32[]{:S(2)}, u32[]{:S(2)}) collective-permute-start(bf16[48,2048]{1,0:T(8,128)(2,1)S(1)} %get-tuple-element.195), channel_id=1, source_target_pairs={{0,16},{8,24},{16,0},{24,8},{1,17},{9,25},{17,1},{25,9},{2,18},{10... | collective-permute-start | bytes 589832 | tf_op jit(solution)/shard_map/ppermute | solution.py:373
  121.9 13.1 %collective-permute-start.40 = (bf16[64,2048]{1,0:T(8,128)(2,1)S(1)}, bf16[64,2048]{1,0:T(8,128)(2,1)S(1)}, u32[]{:S(2)}, u32[]{:S(2)}) collective-permute-start(bf16[64,2048]{1,0:T(8,128)(2,1)S(1)} %add_convert_fusion.2), channel_id=1, source_target_pairs={{0,16},{8,24},{16,0},{24,8},{1,17},{9,25},{17,1},{25,9},{2,18},{10... | collective-permute-start | bytes 786440 | tf_op jit(solution)/shard_map/ppermute | solution.py:373
  123.7 7.8 %collective-permute-start.37 = (bf16[48,2048]{1,0:T(8,128)(2,1)S(1)}, bf16[48,2048]{1,0:T(8,128)(2,1)S(1)}, u32[]{:S(2)}, u32[]{:S(2)}) collective-permute-start(bf16[48,2048]{1,0:T(8,128)(2,1)S(1)} %add_convert_fusion.3), channel_id=1, source_target_pairs={{0,8},{8,0},{16,24},{24,16},{1,9},{9,1},{17,25},{25,17},{2,10},{10... | collective-permute-start | bytes 589832 | tf_op jit(solution)/shard_map/ppermute | solution.py:369
  129.7 9.6 %collective-permute-start.35 = (bf16[112,2048]{1,0:T(8,128)(2,1)S(1)}, bf16[112,2048]{1,0:T(8,128)(2,1)S(1)}, u32[]{:S(2)}, u32[]{:S(2)}) collective-permute-start(bf16[112,2048]{1,0:T(8,128)(2,1)S(1)} %get-tuple-element.189), channel_id=1, source_target_pairs={{0,8},{8,0},{16,24},{24,16},{1,9},{9,1},{17,25},{25,17},{2,10},{10... | collective-permute-start | bytes 1376264 | tf_op jit(solution)/shard_map/ppermute | solution.py:369
  130.6 11.6 %collective-permute-start.36 = (bf16[112,2048]{1,0:T(8,128)(2,1)S(1)}, bf16[112,2048]{1,0:T(8,128)(2,1)S(1)}, u32[]{:S(2)}, u32[]{:S(2)}) collective-permute-start(bf16[112,2048]{1,0:T(8,128)(2,1)S(1)} %get-tuple-element.190), channel_id=1, source_target_pairs={{0,16},{8,24},{16,0},{24,8},{1,17},{9,25},{17,1},{25,9},{2,18},{10... | collective-permute-start | bytes 1376264 | tf_op jit(solution)/shard_map/ppermute | solution.py:373
  135.2 10.3 %collective-permute-start.41 = (bf16[112,2048]{1,0:T(8,128)(2,1)S(1)}, bf16[112,2048]{1,0:T(8,128)(2,1)S(1)}, u32[]{:S(2)}, u32[]{:S(2)}) collective-permute-start(bf16[112,2048]{1,0:T(8,128)(2,1)S(1)} %gather.1), channel_id=1, source_target_pairs={{0,2},{1,3},{2,4},{3,5},{4,6},{5,7},{6,0},{7,1},{8,10},{9,11},{10,... | collective-permute-start | bytes 1376264 | tf_op jit(solution)/shard_map/ppermute | solution.py:377

commit v14 on v13

--- a/solution.py
+++ b/solution.py
@@ -58,20 +58,26 @@
     out_ref[:, :width] = normed
     by_lanes = (((1,), (1,)), ((), ()))
     logits = lax.dot_general(normed, router_ref[...], by_lanes, preferred_element_type=jnp.float32)
-    expert = lax.broadcasted_iota(jnp.int32, (experts, rows), 0)
     routes = routes_ref[...]
-    chosen = jnp.zeros(expert.shape, jnp.bool_)
-    for k in range(routes.shape[0]):
-        chosen = chosen | (expert == routes[k : k + 1, :])
-    chosen = jnp.where(chosen, 1.0, 0.0).astype(jnp.bfloat16)
-    row = lax.broadcasted_iota(jnp.int32, (rows, rows), 0)
-    other = lax.broadcasted_iota(jnp.int32, (rows, rows), 1)
-
-    def of_rows(taken):
-        taken = jnp.where(taken, 1.0, 0.0).astype(jnp.bfloat16)
-        return lax.dot_general(taken, chosen, by_lanes, preferred_element_type=jnp.float32)
-
-    mine = of_rows(row == other) > 0.5
+    if ranking == "first":
+        expert = lax.broadcasted_iota(jnp.int32, logits.shape, 1)
+        mine = jnp.zeros(logits.shape, jnp.bool_)
+        for k in range(routes.shape[1]):
+            mine = mine | (expert == routes[:, k : k + 1])
+    else:
+        expert = lax.broadcasted_iota(jnp.int32, (experts, rows), 0)
+        chosen = jnp.zeros(expert.shape, jnp.bool_)
+        for k in range(routes.shape[0]):
+            chosen = chosen | (expert == routes[k : k + 1, :])
+        chosen = jnp.where(chosen, 1.0, 0.0).astype(jnp.bfloat16)
+        row = lax.broadcasted_iota(jnp.int32, (rows, rows), 0)
+        other = lax.broadcasted_iota(jnp.int32, (rows, rows), 1)
+
+        def of_rows(taken):
+            taken = jnp.where(taken, 1.0, 0.0).astype(jnp.bfloat16)
+            return lax.dot_general(taken, chosen, by_lanes, preferred_element_type=jnp.float32)
+
+        mine = of_rows(row == other) > 0.5
     top = jnp.max(jnp.where(mine, logits, NEG_FILL), axis=1, keepdims=True)
     raised = jnp.where(mine, jnp.exp(jnp.minimum(logits - top, 0.0)), 0.0)
     gates = raised / jnp.sum(raised, axis=1, keepdims=True)
@@ -98,7 +104,7 @@
         scratch_shapes=[pltpu.VMEM((rows, width), jnp.float32)] if shifted else [],
         compiler_params=pltpu.CompilerParams(vmem_limit_bytes=32 << 20),
         name="prepare",
-    )(hidden, norm_gain.reshape(1, width), router.T, routes.T)
+    )(hidden, norm_gain.reshape(1, width), router.T, routes if ranking == "first" else routes.T)
 
 
 def expert_kernel(expert_ref, rows_ref, gate_ref, up_ref, down_ref, out_ref):
@@ -329,40 +335,36 @@
     )(far, risen, own, from_x, from_y)
 
 
-def meet_kernel(far_0_ref, far_1_ref, risen_ref, x_ref, y_ref, out_0, out_1, x_out, y_out):
+def meet_kernel(far_0_ref, far_1_ref, risen_ref, x_ref, out_0, out_1, x_out):
     x_out[...] = x_ref[...]
-    y_out[...] = y_ref[...]
     cut = out_0.shape[0]
     risen = risen_ref[...].astype(jnp.float32)
     out_0[...] = (far_0_ref[...].astype(jnp.float32) + risen[:cut]).astype(jnp.bfloat16)
     out_1[...] = (far_1_ref[...].astype(jnp.float32) + risen[cut:]).astype(jnp.bfloat16)
 
 
-def meet(far_0, far_1, risen, x_part, y_part):
-    outputs = (far_0, far_1, x_part, y_part)
+def meet(far_0, far_1, risen, x_part):
+    outputs = (far_0, far_1, x_part)
     return pl.pallas_call(
         meet_kernel,
         out_shape=[jax.ShapeDtypeStruct(output.shape, output.dtype) for output in outputs],
         compiler_params=pltpu.CompilerParams(vmem_limit_bytes=16 << 20),
         name="meet",
-    )(far_0, far_1, risen, x_part, y_part)
-
-
-def gather_kernel(own_ref, x_0_ref, x_1_ref, y_0_ref, y_1_ref, carried_ref, out_ref):
-    cut = x_0_ref.shape[0]
-    for part, x_ref, y_ref in ((slice(0, cut), x_0_ref, y_0_ref), (slice(cut, None), x_1_ref, y_1_ref)):
-        total = own_ref[part, :].astype(jnp.float32) + carried_ref[part, :].astype(jnp.float32)
-        total += x_ref[...].astype(jnp.float32) + y_ref[...].astype(jnp.float32)
-        out_ref[part, :] = total.astype(jnp.bfloat16)
-
-
-def gather_sums(own, x_0, x_1, y_0, y_1, carried):
+    )(far_0, far_1, risen, x_part)
+
+
+def join_passed_kernel(one_ref, passed_ref, other_ref, one_out, other_out):
+    one_out[...] = (one_ref[...].astype(jnp.float32) + passed_ref[...].astype(jnp.float32)).astype(jnp.bfloat16)
+    other_out[...] = other_ref[...]
+
+
+def join_passed(one, passed, other):
     return pl.pallas_call(
-        gather_kernel,
-        out_shape=jax.ShapeDtypeStruct(own.shape, own.dtype),
+        join_passed_kernel,
+        out_shape=[jax.ShapeDtypeStruct(part.shape, part.dtype) for part in (one, other)],
         compiler_params=pltpu.CompilerParams(vmem_limit_bytes=16 << 20),
-        name="gather",
-    )(own, x_0, x_1, y_0, y_1, carried)
+        name="join_passed",
+    )(one, passed, other)
 
 
 def along_x(value):
@@ -512,16 +514,20 @@
     far, sums_2, sums_3 = fence(far, sums_2, sums_3)
 
     own, x_0, x_1, y_0, y_1, far_0, far_1 = sums_3
-    far_0, far_1, x_1, y_0 = meet(far_0, far_1, far, x_1, y_0)
+    far_0, far_1, x_1 = meet(far_0, far_1, far, x_1)
     passed_3 = along_y(far_0), along_x(far_1)
-    back_x1, back_y0 = along_x(x_1), along_y(y_0)
+    back_x1 = along_x(x_1)
     passed_3, carried_1 = fence(passed_3, carried_1)
+    y_1, y_0 = join_passed(y_1, passed_3[1], y_0)
+    back_y1 = along_y(y_1)
     back_x0 = along_x(added(x_0, passed_3[0]).astype(jnp.bfloat16))
-    back_y1 = along_y(added(y_1, passed_3[1]).astype(jnp.bfloat16))
+    back_y0 = along_y(y_0)
     carried = around_z(added(sums_2[0], *back_2).astype(jnp.bfloat16))
     carried, passed_0, sums_0 = fence(carried, passed_0, sums_0)
     back_0 = return_sides(sums_0, passed_0)
-    carried = around_z(gather_sums(own, back_x0, back_x1, back_y0, back_y1, carried))
+    late = around_z(added(own[cut:], back_x1, back_y1, carried[cut:]).astype(jnp.bfloat16))
+    early = around_z(added(own[:cut], back_x0, back_y0, carried[:cut]).astype(jnp.bfloat16))
+    carried = jnp.concatenate([early, late], axis=0)
     return added(hidden, sums_0[0], carried_1, *back_0, carried).astype(jnp.bfloat16)[None]
 
 

time: 147 us -> 145 us (0.986)
  waiting for transfers between devices: 44.2 us -> 46.9 us
  starting transfers between devices: 43.3 us -> 40.8 us
  local copies, waits for them, and re-layouts: 6.34 us -> 4.65 us
    ppermute x9 -> x10, waiting for transfers between devices: 14.1 us -> 20.4 us  [around_z(): lax.ppermute(value, 'blk', [(i, (i + 2 * hops) % 8) for i in range(8)])]
    ppermute x15, starting transfers between devices: 17 us -> 14 us  [along_x(): return lax.ppermute(value, 'kv', [(i, i ^ 1) for i in range(4)])]
    ppermute x15, waiting for transfers between devices: 25.7 us -> 23.2 us  [along_y(): return lax.ppermute(value, 'kv', [(i, i ^ 2) for i in range(4)])]
    unnamed x24 -> x20, local copies, waits for them, and re-layouts: 6.03 us -> 4.4 us
    ppermute x9 -> x10, starting transfers between devices: 10.8 us -> 10.1 us  [around_z(): lax.ppermute(value, 'blk', [(i, (i + 2 * hops) % 8) for i in range(8)])]
  transfers between devices with their start and end apart: 42 -> 43, of which waited for: 18 -> 17; matrix products, arithmetic and copies ran while one was open for 6% -> 6% of each run, Pallas kernels for 28% -> 28%
where the time goes in v14:
time: 145 us
  waiting for transfers between devices  46.9 us (32%)
  Pallas kernels  42.1 us (29%)
  starting transfers between devices  40.8 us (28%)
  other arithmetic  5.08 us (4%)
  matrix products  4.86 us (3%)
  local copies, waits for them, and re-layouts  4.65 us (3%)
    pallas_call x4, Pallas kernels, run_plane(): pl.pallas_call(functools.partial(plane_kernel, cap, piece_rows, block_row...  40.3 us
    ppermute x15, waiting for transfers between devices, along_y(): return lax.ppermute(value, 'kv', [(i, i ^ 2) for i in range(4)])  23.2 us
    ppermute x10, waiting for transfers between devices, around_z(): lax.ppermute(value, 'blk', [(i, (i + 2 * hops) % 8) for i in range(8)])  20.4 us
    ppermute x15, starting transfers between devices, along_y(): return lax.ppermute(value, 'kv', [(i, i ^ 2) for i in range(4)])  16.3 us
    ppermute x15, starting transfers between devices, along_x(): return lax.ppermute(value, 'kv', [(i, i ^ 1) for i in range(4)])  14 us
    ppermute x10, starting transfers between devices, around_z(): lax.ppermute(value, 'blk', [(i, (i + 2 * hops) % 8) for i in range(8)])  10.1 us
    unnamed x20, local copies, waits for them, and re-layouts  4.4 us
    dot_general x1, matrix products, attend(): jnp.einsum('rgd,rjd->rgj', grouped_q, key_rows, preferred_element_type=jn...  3.47 us
  transfers between devices with their start and end apart: 43, of which 17 were waited for; matrix products, arithmetic and copies ran while one was open for 6% of the time, Pallas kernels for 28%

profile of v14, /device:TPU:0, one launch (start us, length us, event | category | flops | bytes accessed | tf_op | source)
XLA Modules:
  0.0 144.8 jit_solution(16581208574008872848)
XLA Ops:
  0.0 1.0 copy-done
  1.0 0.9 copy-done.2
  1.9 0.7 copy-done.4
  2.6 0.7 copy-done.6
  3.3 0.8 prepare.2.refs_1_
  4.1 3.0 %collective-permute-start = (bf16[112,2176]{1,0:T(8,128)(2,1)S(1)}, bf16[112,2176]{1,0:T(8,128)(2,1)S(1)}, u32[]{:S(2)}, u32[]{:S(2)}) collective-permute-start(bf16[112,2176]{1,0:T(8,128)(2,1)S(1)} %prepare.2.refs_1_), channel_id=1, source_target_pairs={{0,8},{8,0},{16,24},{24,16},{1,9},{9,1},{17,25},{25,17},{2,10},{10... | collective-permute-start | bytes 1462280 | tf_op jit(solution)/shard_map/ppermute | solution.py:371
  7.1 1.5 %collective-permute-start.1 = (bf16[112,2176]{1,0:T(8,128)(2,1)S(1)}, bf16[112,2176]{1,0:T(8,128)(2,1)S(1)}, u32[]{:S(2)}, u32[]{:S(2)}) collective-permute-start(bf16[112,2176]{1,0:T(8,128)(2,1)S(1)} %prepare.2.refs_1_), channel_id=1, source_target_pairs={{0,16},{8,24},{16,0},{24,8},{1,17},{9,25},{17,1},{25,9},{2,18},{10... | collective-permute-start | bytes 1462280 | tf_op jit(solution)/shard_map/ppermute | solution.py:375
  8.6 1.6 %collective-permute-start.2 = (bf16[112,2176]{1,0:T(8,128)(2,1)S(1)}, bf16[112,2176]{1,0:T(8,128)(2,1)S(1)}, u32[]{:S(2)}, u32[]{:S(2)}) collective-permute-start(bf16[112,2176]{1,0:T(8,128)(2,1)S(1)} %prepare.2.refs_1_), channel_id=1, source_target_pairs={{0,2},{1,3},{2,4},{3,5},{4,6},{5,7},{6,0},{7,1},{8,10},{9,11},{10,... | collective-permute-start | bytes 1462280 | tf_op jit(solution)/shard_map/ppermute | solution.py:379
  10.7 0.7 minimum_subtract_fusion
  11.5 0.9 broadcast_in_dim.76
  12.4 1.0 convert_reduce_fusion
  13.4 3.5 %fusion.36 = (f32[4,8]{1,0:T(4,128)S(1)}, f32[4,8,4096]{2,1,0:T(8,128)S(1)}) fusion(bf16[4,4096,1,128]{3,1,2,0:T(8,128)(2,1)} %param.15, bf16[1,4,8,128]{3,1,2,0:T(4,128)(2,1)} %bitcast.51, pred[4,4096]{1,0:T(4,128)(4,1)S(1)} %iota_compare_fusion.2), kind=kOutput, calls=%fused_computation.61 | convolution fusion | flops 33947616 | bytes 4743296 | tf_op jit(solution)/shard_map/rgd,rjd->rgj/dot_general | solution.py:27
  17.2 0.7 fusion.11
  18.0 1.1 copy-done.8
  19.1 0.7 convolution_add_fusion
  19.8 0.6 collective-permute-start.6
  20.4 2.4 %collective-permute-done.2.refs_1_ = bf16[112,2176]{1,0:T(8,128)(2,1)S(1)} collective-permute-done((bf16[112,2176]{1,0:T(8,128)(2,1)S(1)}, bf16[112,2176]{1,0:T(8,128)(2,1)S(1)}, u32[]{:S(2)}, u32[]{:S(2)}) %collective-permute-start.2) | collective-permute-done | bytes 487456 | tf_op jit(solution)/shard_map/ppermute | solution.py:379
  24.5 4.8 %collective-permute-done.4.refs_4_ = bf16[48,2176]{1,0:T(8,128)(2,1)S(1)} collective-permute-done((bf16[48,2176]{1,0:T(8,128)(2,1)S(1)}, bf16[48,2176]{1,0:T(8,128)(2,1)S(1)}, u32[]{:S(2)}, u32[]{:S(2)}) %collective-permute-start.4) | collective-permute-done | bytes 208928 | tf_op jit(solution)/shard_map/ppermute | solution.py:375
  29.3 0.8 collective-permute-done.5.refs_5_
  30.7 1.5 %collective-permute-start.10 = (bf16[112,2176]{1,0:T(8,128)(2,1)S(1)}, bf16[112,2176]{1,0:T(8,128)(2,1)S(1)}, u32[]{:S(2)}, u32[]{:S(2)}) collective-permute-start(bf16[112,2176]{1,0:T(8,128)(2,1)S(1)} %collective-permute-done.2.refs_1_), channel_id=1, source_target_pairs={{0,16},{8,24},{16,0},{24,8},{1,17},{9,25},{17,1},{25,9},{2,18},{10... | collective-permute-start | bytes 1462280 | tf_op jit(solution)/shard_map/ppermute | solution.py:375
  32.2 1.3 collective-permute-start.11
  33.5 0.8 collective-permute-start.9
  34.3 0.7 collective-permute-done.8
  35.7 9.3 %collective-permute-done.10.refs_3_ = bf16[112,2176]{1,0:T(8,128)(2,1)S(1)} collective-permute-done((bf16[112,2176]{1,0:T(8,128)(2,1)S(1)}, bf16[112,2176]{1,0:T(8,128)(2,1)S(1)}, u32[]{:S(2)}, u32[]{:S(2)}) %collective-permute-start.10) | collective-permute-done | bytes 487456 | tf_op jit(solution)/shard_map/ppermute | solution.py:375
  45.0 1.9 %collective-permute-done.11.refs_1_ = bf16[112,2176]{1,0:T(8,128)(2,1)S(1)} collective-permute-done((bf16[112,2176]{1,0:T(8,128)(2,1)S(1)}, bf16[112,2176]{1,0:T(8,128)(2,1)S(1)}, u32[]{:S(2)}, u32[]{:S(2)}) %collective-permute-start.11) | collective-permute-done | bytes 487456 | tf_op jit(solution)/shard_map/ppermute | solution.py:379
  47.0 0.7 collective-permute-start.15
  47.7 0.9 collective-permute-start.16
  48.7 0.9 collective-permute-start.17
  49.6 0.9 collective-permute-start.14
  50.5 1.6 %collective-permute-start.13 = (bf16[48,2176]{1,0:T(8,128)(2,1)S(1)}, bf16[48,2176]{1,0:T(8,128)(2,1)S(1)}, u32[]{:S(2)}, u32[]{:S(2)}) collective-permute-start(bf16[48,2176]{1,0:T(8,128)(2,1)S(1)} %slice.57), channel_id=1, source_target_pairs={{0,16},{8,24},{16,0},{24,8},{1,17},{9,25},{17,1},{25,9},{2,18},{10... | collective-permute-start | bytes 626696 | tf_op jit(solution)/shard_map/ppermute | solution.py:375
  52.1 10.1 %plane.4 = (bf16[112,2048]{1,0:T(8,128)(2,1)S(1)}, bf16[112,2048]{1,0:T(8,128)(2,1)S(1)}, bf16[112,2048]{1,0:T(8,128)(2,1)S(1)}, bf16[48,2048]{1,0:T(8,128)(2,1)S(1)}, bf16[64,2048]{1,0:T(8,128)(2,1)S(1)}) custom-call(s32[3]{0:T(128)S(1)} %pad_add_fusion.refs_0_, bf16[112,2176]{1,0:T(8,128)(2,1)S(1)} %prepare.2.refs_1_, ...), custom_call_target="tpu_custom_call" | custom-call | flops 8455716864 | bytes 25165824 | tf_op jit(solution)/shard_map/plane/pallas_call | solution.py:277
  62.2 1.8 %collective-permute-done.13.refs_4_ = bf16[48,2176]{1,0:T(8,128)(2,1)S(1)} collective-permute-done((bf16[48,2176]{1,0:T(8,128)(2,1)S(1)}, bf16[48,2176]{1,0:T(8,128)(2,1)S(1)}, u32[]{:S(2)}, u32[]{:S(2)}) %collective-permute-start.13) | collective-permute-done | bytes 208928 | tf_op jit(solution)/shard_map/ppermute | solution.py:375
  64.0 1.1 collective-permute-done.14.refs_5_
  65.2 0.8 collective-permute-start.18
  65.9 1.0 collective-permute-start.19
  66.9 0.7 collective-permute-start.20
  67.7 0.9 collective-permute-start.22
  68.5 1.5 %collective-permute-start.21 = (bf16[48,2048]{1,0:T(8,128)(2,1)S(1)}, bf16[48,2048]{1,0:T(8,128)(2,1)S(1)}, u32[]{:S(2)}, u32[]{:S(2)}) collective-permute-start(bf16[48,2048]{1,0:T(8,128)(2,1)S(1)} %get-tuple-element.130), channel_id=1, source_target_pairs={{0,16},{8,24},{16,0},{24,8},{1,17},{9,25},{17,1},{25,9},{2,18},{10... | collective-permute-start | bytes 589832 | tf_op jit(solution)/shard_map/ppermute | solution.py:375
  70.1 10.1 %plane.5 = (bf16[112,2048]{1,0:T(8,128)(2,1)S(1)}, bf16[112,2048]{1,0:T(8,128)(2,1)S(1)}, bf16[112,2048]{1,0:T(8,128)(2,1)S(1)}, bf16[112,2048]{1,0:T(8,128)(2,1)S(1)}) custom-call(s32[3]{0:T(128)S(1)} %pad_add_fusion.refs_0_, bf16[112,2176]{1,0:T(8,128)(2,1)S(1)} %collective-permute-done.2.refs_1_, bf16[112,2176]{1,0:T(8,128)(2,1)S(1)} %collective-permute-done.9.refs_2_, ...), custom_call_target="tpu_custom_call" | custom-call | flops 8455716864 | bytes 25165824 | tf_op jit(solution)/shard_map/plane/pallas_call | solution.py:277
  80.1 0.9 collective-permute-done.21.passed_0_ref
  81.1 1.0 collective-permute-done.22.passed_1_ref
  82.6 0.9 collective-permute-start.25
  83.5 1.2 collective-permute-start.26
  85.2 1.6 %collective-permute-start.24 = (bf16[48,2176]{1,0:T(8,128)(2,1)S(1)}, bf16[48,2176]{1,0:T(8,128)(2,1)S(1)}, u32[]{:S(2)}, u32[]{:S(2)}) collective-permute-start(bf16[48,2176]{1,0:T(8,128)(2,1)S(1)} %slice.62), channel_id=1, source_target_pairs={{0,16},{8,24},{16,0},{24,8},{1,17},{9,25},{17,1},{25,9},{2,18},{10... | collective-permute-start | bytes 626696 | tf_op jit(solution)/shard_map/ppermute | solution.py:375
  86.8 10.1 %plane.6 = (bf16[112,2048]{1,0:T(8,128)(2,1)S(1)}, bf16[112,2048]{1,0:T(8,128)(2,1)S(1)}, bf16[112,2048]{1,0:T(8,128)(2,1)S(1)}, bf16[112,2048]{1,0:T(8,128)(2,1)S(1)}) custom-call(s32[3]{0:T(128)S(1)} %pad_add_fusion.refs_0_, bf16[112,2176]{1,0:T(8,128)(2,1)S(1)} %collective-permute-done.11.refs_1_, bf16[112,2176]{1,0:T(8,128)(2,1)S(1)} %collective-permute-done.15.refs_2_, ...), custom_call_target="tpu_custom_call" | custom-call | flops 8455716864 | bytes 25165824 | tf_op jit(solution)/shard_map/plane/pallas_call | solution.py:277
  96.9 1.2 collective-permute-done.24.refs_4_
  98.4 2.3 %collective-permute-start.28 = (bf16[112,2048]{1,0:T(8,128)(2,1)S(1)}, bf16[112,2048]{1,0:T(8,128)(2,1)S(1)}, u32[]{:S(2)}, u32[]{:S(2)}) collective-permute-start(bf16[112,2048]{1,0:T(8,128)(2,1)S(1)} %get-tuple-element.157), channel_id=1, source_target_pairs={{0,2},{1,3},{2,4},{3,5},{4,6},{5,7},{6,0},{7,1},{8,10},{9,11},{10,... | collective-permute-start | bytes 1376264 | tf_op jit(solution)/shard_map/ppermute | solution.py:379
  100.8 1.6 %collective-permute-start.34 = (bf16[112,2048]{1,0:T(8,128)(2,1)S(1)}, bf16[112,2048]{1,0:T(8,128)(2,1)S(1)}, u32[]{:S(2)}, u32[]{:S(2)}) collective-permute-start(bf16[112,2048]{1,0:T(8,128)(2,1)S(1)} %get-tuple-element.183), channel_id=1, source_target_pairs={{0,6},{1,7},{2,0},{3,1},{4,2},{5,3},{6,4},{7,5},{8,14},{9,15},{10,... | collective-permute-start | bytes 1376264 | tf_op jit(solution)/shard_map/ppermute | solution.py:379
  102.4 0.7 collective-permute-start.29
  103.1 0.9 collective-permute-start.30
  104.0 10.1 %plane.7 = (bf16[112,2048]{1,0:T(8,128)(2,1)S(1)}, bf16[48,2048]{1,0:T(8,128)(2,1)S(1)}, bf16[64,2048]{1,0:T(8,128)(2,1)S(1)}, bf16[48,2048]{1,0:T(8,128)(2,1)S(...) custom-call(s32[3]{0:T(128)S(1)} %pad_add_fusion.refs_0_, ...), custom_call_target="tpu_custom_call" | custom-call | flops 8455716864 | bytes 25165824 | tf_op jit(solution)/shard_map/plane/pallas_call | solution.py:277
  114.2 1.0 collective-permute-start.33
  115.2 1.5 %collective-permute-start.32 = (bf16[48,2048]{1,0:T(8,128)(2,1)S(1)}, bf16[48,2048]{1,0:T(8,128)(2,1)S(1)}, u32[]{:S(2)}, u32[]{:S(2)}) collective-permute-start(bf16[48,2048]{1,0:T(8,128)(2,1)S(1)} %get-tuple-element.181), channel_id=1, source_target_pairs={{0,16},{8,24},{16,0},{24,8},{1,17},{9,25},{17,1},{25,9},{2,18},{10... | collective-permute-start | bytes 589832 | tf_op jit(solution)/shard_map/ppermute | solution.py:375
  117.8 3.8 %collective-permute-done.34 = bf16[112,2048]{1,0:T(8,128)(2,1)S(1)} collective-permute-done((bf16[112,2048]{1,0:T(8,128)(2,1)S(1)}, bf16[112,2048]{1,0:T(8,128)(2,1)S(1)}, u32[]{:S(2)}, u32[]{:S(2)}) %collective-permute-start.34) | collective-permute-done | bytes 458784 | tf_op jit(solution)/shard_map/ppermute | solution.py:379
  121.7 0.8 collective-permute-start.41
  122.6 0.8 collective-permute-start.37
  123.3 0.9 collective-permute-start.38
  124.2 4.4 %collective-permute-done.31 = bf16[112,2048]{1,0:T(8,128)(2,1)S(1)} collective-permute-done((bf16[112,2048]{1,0:T(8,128)(2,1)S(1)}, bf16[112,2048]{1,0:T(8,128)(2,1)S(1)}, u32[]{:S(2)}, u32[]{:S(2)}) %collective-permute-start.31) | collective-permute-done | bytes 458784 | tf_op jit(solution)/shard_map/ppermute | solution.py:379
  128.7 0.7 collective-permute-start.35
  129.4 0.9 collective-permute-start.36
  130.3 0.6 collective-permute-done.41
  131.5 3.7 %collective-permute-done.38 = bf16[48,2048]{1,0:T(8,128)(2,1)S(1)} collective-permute-done((bf16[48,2048]{1,0:T(8,128)(2,1)S(1)}, bf16[48,2048]{1,0:T(8,128)(2,1)S(1)}, u32[]{:S(2)}, u32[]{:S(2)}) %collective-permute-start.38) | collective-permute-done | bytes 196640 | tf_op jit(solution)/shard_map/ppermute | solution.py:375
  135.6 7.9 %collective-permute-done.39 = bf16[48,2048]{1,0:T(8,128)(2,1)S(1)} collective-permute-done((bf16[48,2048]{1,0:T(8,128)(2,1)S(1)}, bf16[48,2048]{1,0:T(8,128)(2,1)S(1)}, u32[]{:S(2)}, u32[]{:S(2)}) %collective-permute-start.39) | collective-permute-done | bytes 196640 | tf_op jit(solution)/shard_map/ppermute | solution.py:379
  143.6 1.2 fusion.15
  (92 shorter events, 7.9 us)
Async XLA Ops:
  0.0 16.9 %copy-start.9 = (f32[8]{0:T(128)S(1)}, f32[8]{0:T(128)}, u32[]{:S(2)}) copy-start(f32[8]{0:T(128)} %param.18) | copy-start | bytes 100
  0.0 1.0 copy-start
  1.0 0.9 copy-start.2
  1.9 0.7 copy-start.4
  2.6 0.7 copy-start.6
  4.1 15.7 %collective-permute-start = (bf16[112,2176]{1,0:T(8,128)(2,1)S(1)}, bf16[112,2176]{1,0:T(8,128)(2,1)S(1)}, u32[]{:S(2)}, u32[]{:S(2)}) collective-permute-start(bf16[112,2176]{1,0:T(8,128)(2,1)S(1)} %prepare.2.refs_1_), channel_id=1, source_target_pairs={{0,8},{8,0},{16,24},{24,16},{1,9},{9,1},{17,25},{25,17},{2,10},{10... | collective-permute-start | bytes 1462280 | tf_op jit(solution)/shard_map/ppermute | solution.py:371
  7.1 13.3 %collective-permute-start.1 = (bf16[112,2176]{1,0:T(8,128)(2,1)S(1)}, bf16[112,2176]{1,0:T(8,128)(2,1)S(1)}, u32[]{:S(2)}, u32[]{:S(2)}) collective-permute-start(bf16[112,2176]{1,0:T(8,128)(2,1)S(1)} %prepare.2.refs_1_), channel_id=1, source_target_pairs={{0,16},{8,24},{16,0},{24,8},{1,17},{9,25},{17,1},{25,9},{2,18},{10... | collective-permute-start | bytes 1462280 | tf_op jit(solution)/shard_map/ppermute | solution.py:375
  8.6 14.2 %collective-permute-start.2 = (bf16[112,2176]{1,0:T(8,128)(2,1)S(1)}, bf16[112,2176]{1,0:T(8,128)(2,1)S(1)}, u32[]{:S(2)}, u32[]{:S(2)}) collective-permute-start(bf16[112,2176]{1,0:T(8,128)(2,1)S(1)} %prepare.2.refs_1_), channel_id=1, source_target_pairs={{0,2},{1,3},{2,4},{3,5},{4,6},{5,7},{6,0},{7,1},{8,10},{9,11},{10,... | collective-permute-start | bytes 1462280 | tf_op jit(solution)/shard_map/ppermute | solution.py:379
  10.2 12.6 %collective-permute-start.3 = (bf16[2048,768]{1,0:T(8,128)(2,1)}, bf16[2048,768]{1,0:T(8,128)(2,1)}, u32[]{:S(2)}, u32[]{:S(2)}) collective-permute-start(bf16[2048,768]{1,0:T(8,128)(2,1)} %bitcast.53), channel_id=1, source_target_pairs={{0,1},{1,0},{2,3},{3,2},{4,5},{5,4},{6,7},{7,6},{8,9},{9,8},{10,11... | collective-permute-start | bytes 9437192 | tf_op jit(solution)/shard_map/ppermute | solution.py:383
  10.2 14.3 %collective-permute-start.7 = (bf16[2048,768]{1,0:T(8,128)(2,1)}, bf16[2048,768]{1,0:T(8,128)(2,1)}, u32[]{:S(2)}, u32[]{:S(2)}) collective-permute-start(bf16[2048,768]{1,0:T(8,128)(2,1)} %bitcast.58), channel_id=1, source_target_pairs={{0,1},{1,0},{2,3},{3,2},{4,5},{5,4},{6,7},{7,6},{8,9},{9,8},{10,11... | collective-permute-start | bytes 9437192 | tf_op jit(solution)/shard_map/ppermute | solution.py:383
  11.5 5.7 %copy-start.7 = (bf16[4,4096,1,128]{3,1,2,0:T(8,128)(2,1)S(1)}, bf16[4,4096,1,128]{3,1,2,0:T(8,128)(2,1)}, u32[]{:S(2)}) copy-start(bf16[4,4096,1,128]{3,1,2,0:T(8,128)(2,1)} %param.16) | copy-start | bytes 12582916
  16.9 2.2 %copy-start.8 = (bf16[1024,2048]{1,0:T(8,128)(2,1)S(1)}, bf16[1024,2048]{1,0:T(8,128)(2,1)}, u32[]{:S(2)}) copy-start(bf16[1024,2048]{1,0:T(8,128)(2,1)} %param.19) | copy-start | bytes 12582916
  17.9 17.2 %copy-start.3 = (bf16[2048,32]{0,1:T(8,128)(2,1)S(1)}, bf16[2048,32]{0,1:T(8,128)(2,1)}, u32[]{:S(2)}) copy-start(bf16[2048,32]{0,1:T(8,128)(2,1)} %param.23) | copy-start | bytes 393220
  18.0 17.2 %copy-start.5 = (f32[2048]{0:T(1024)S(1)}, f32[2048]{0:T(1024)}, u32[]{:S(2)}) copy-start(f32[2048]{0:T(1024)} %param.22) | copy-start | bytes 24580
  19.8 4.6 %collective-permute-start.6 = (f32[8,2048]{1,0:T(8,128)S(1)}, f32[8,2048]{1,0:T(8,128)S(1)}, u32[]{:S(2)}, u32[]{:S(2)}) collective-permute-start(f32[8,2048]{1,0:T(8,128)S(1)} %pad_maximum_fusion.2), channel_id=1, source_target_pairs={{0,8},{8,0},{16,24},{24,16},{1,9},{9,1},{17,25},{25,17},{2,10},{10... | collective-permute-start | bytes 196616 | tf_op jit(solution)/shard_map/ppermute | solution.py:371
  22.8 7.3 %collective-permute-start.5 = (bf16[64,2176]{1,0:T(8,128)(2,1)S(1)}, bf16[64,2176]{1,0:T(8,128)(2,1)S(1)}, u32[]{:S(2)}, u32[]{:S(2)}) collective-permute-start(bf16[64,2176]{1,0:T(8,128)(2,1)S(1)} %slice.53), channel_id=1, source_target_pairs={{0,8},{8,0},{16,24},{24,16},{1,9},{9,1},{17,25},{25,17},{2,10},{10... | collective-permute-start | bytes 835592 | tf_op jit(solution)/shard_map/ppermute | solution.py:371
  23.4 5.9 %collective-permute-start.4 = (bf16[48,2176]{1,0:T(8,128)(2,1)S(1)}, bf16[48,2176]{1,0:T(8,128)(2,1)S(1)}, u32[]{:S(2)}, u32[]{:S(2)}) collective-permute-start(bf16[48,2176]{1,0:T(8,128)(2,1)S(1)} %slice.52), channel_id=1, source_target_pairs={{0,16},{8,24},{16,0},{24,8},{1,17},{9,25},{17,1},{25,9},{2,18},{10... | collective-permute-start | bytes 626696 | tf_op jit(solution)/shard_map/ppermute | solution.py:375
  30.1 16.9 %collective-permute-start.12 = (bf16[768,2048]{1,0:T(8,128)(2,1)}, bf16[768,2048]{1,0:T(8,128)(2,1)}, u32[]{:S(2)}, u32[]{:S(2)}) collective-permute-start(bf16[768,2048]{1,0:T(8,128)(2,1)} %bitcast.11.refs_9_.refs_7_), channel_id=1, source_target_pairs={{0,1},{1,0},{2,3},{3,2},{4,5},{5,4},{6,7},{7,6},{8,9},{9,8},{10,11... | collective-permute-start | bytes 9437192 | tf_op jit(solution)/shard_map/ppermute | solution.py:383
  30.1 4.9 %collective-permute-start.8 = (f32[8,2048]{1,0:T(8,128)S(1)}, f32[8,2048]{1,0:T(8,128)S(1)}, u32[]{:S(2)}, u32[]{:S(2)}) collective-permute-start(f32[8,2048]{1,0:T(8,128)S(1)} %fusion.35), channel_id=1, source_target_pairs={{0,16},{8,24},{16,0},{24,8},{1,17},{9,25},{17,1},{25,9},{2,18},{10... | collective-permute-start | bytes 196616 | tf_op jit(solution)/shard_map/ppermute | solution.py:375
  30.7 14.4 %collective-permute-start.10 = (bf16[112,2176]{1,0:T(8,128)(2,1)S(1)}, bf16[112,2176]{1,0:T(8,128)(2,1)S(1)}, u32[]{:S(2)}, u32[]{:S(2)}) collective-permute-start(bf16[112,2176]{1,0:T(8,128)(2,1)S(1)} %collective-permute-done.2.refs_1_), channel_id=1, source_target_pairs={{0,16},{8,24},{16,0},{24,8},{1,17},{9,25},{17,1},{25,9},{2,18},{10... | collective-permute-start | bytes 1462280 | tf_op jit(solution)/shard_map/ppermute | solution.py:375
  32.2 14.8 %collective-permute-start.11 = (bf16[112,2176]{1,0:T(8,128)(2,1)S(1)}, bf16[112,2176]{1,0:T(8,128)(2,1)S(1)}, u32[]{:S(2)}, u32[]{:S(2)}) collective-permute-start(bf16[112,2176]{1,0:T(8,128)(2,1)S(1)} %collective-permute-done.2.refs_1_), channel_id=1, source_target_pairs={{0,2},{1,3},{2,4},{3,5},{4,6},{5,7},{6,0},{7,1},{8,10},{9,11},{10,... | collective-permute-start | bytes 1462280 | tf_op jit(solution)/shard_map/ppermute | solution.py:379
  33.5 13.5 %collective-permute-start.9 = (bf16[112,2176]{1,0:T(8,128)(2,1)S(1)}, bf16[112,2176]{1,0:T(8,128)(2,1)S(1)}, u32[]{:S(2)}, u32[]{:S(2)}) collective-permute-start(bf16[112,2176]{1,0:T(8,128)(2,1)S(1)} %collective-permute-done.2.refs_1_), channel_id=1, source_target_pairs={{0,8},{8,0},{16,24},{24,16},{1,9},{9,1},{17,25},{25,17},{2,10},{10... | collective-permute-start | bytes 1462280 | tf_op jit(solution)/shard_map/ppermute | solution.py:371
  47.0 18.1 %collective-permute-start.15 = (bf16[112,2176]{1,0:T(8,128)(2,1)S(1)}, bf16[112,2176]{1,0:T(8,128)(2,1)S(1)}, u32[]{:S(2)}, u32[]{:S(2)}) collective-permute-start(bf16[112,2176]{1,0:T(8,128)(2,1)S(1)} %collective-permute-done.11.refs_1_), channel_id=1, source_target_pairs={{0,8},{8,0},{16,24},{24,16},{1,9},{9,1},{17,25},{25,17},{2,10},{10... | collective-permute-start | bytes 1462280 | tf_op jit(solution)/shard_map/ppermute | solution.py:371
  47.7 17.4 %collective-permute-start.16 = (bf16[112,2176]{1,0:T(8,128)(2,1)S(1)}, bf16[112,2176]{1,0:T(8,128)(2,1)S(1)}, u32[]{:S(2)}, u32[]{:S(2)}) collective-permute-start(bf16[112,2176]{1,0:T(8,128)(2,1)S(1)} %collective-permute-done.11.refs_1_), channel_id=1, source_target_pairs={{0,16},{8,24},{16,0},{24,8},{1,17},{9,25},{17,1},{25,9},{2,18},{10... | collective-permute-start | bytes 1462280 | tf_op jit(solution)/shard_map/ppermute | solution.py:375
  48.7 16.4 %collective-permute-start.17 = (bf16[128,2176]{1,0:T(8,128)(2,1)S(1)}, bf16[128,2176]{1,0:T(8,128)(2,1)S(1)}, u32[]{:S(2)}, u32[]{:S(2)}) collective-permute-start(bf16[128,2176]{1,0:T(8,128)(2,1)S(1)} %pad_maximum_fusion), channel_id=1, source_target_pairs={{0,2},{1,3},{2,4},{3,5},{4,6},{5,7},{6,0},{7,1},{8,10},{9,11},{10,... | collective-permute-start | bytes 1671176 | tf_op jit(solution)/shard_map/ppermute | solution.py:379
  49.6 15.5 %collective-permute-start.14 = (bf16[64,2176]{1,0:T(8,128)(2,1)S(1)}, bf16[64,2176]{1,0:T(8,128)(2,1)S(1)}, u32[]{:S(2)}, u32[]{:S(2)}) collective-permute-start(bf16[64,2176]{1,0:T(8,128)(2,1)S(1)} %slice.58), channel_id=1, source_target_pairs={{0,8},{8,0},{16,24},{24,16},{1,9},{9,1},{17,25},{25,17},{2,10},{10... | collective-permute-start | bytes 835592 | tf_op jit(solution)/shard_map/ppermute | solution.py:371
  50.5 13.5 %collective-permute-start.13 = (bf16[48,2176]{1,0:T(8,128)(2,1)S(1)}, bf16[48,2176]{1,0:T(8,128)(2,1)S(1)}, u32[]{:S(2)}, u32[]{:S(2)}) collective-permute-start(bf16[48,2176]{1,0:T(8,128)(2,1)S(1)} %slice.57), channel_id=1, source_target_pairs={{0,16},{8,24},{16,0},{24,8},{1,17},{9,25},{17,1},{25,9},{2,18},{10... | collective-permute-start | bytes 626696 | tf_op jit(solution)/shard_map/ppermute | solution.py:375
  65.2 16.9 %collective-permute-start.18 = (bf16[112,2176]{1,0:T(8,128)(2,1)S(1)}, bf16[112,2176]{1,0:T(8,128)(2,1)S(1)}, u32[]{:S(2)}, u32[]{:S(2)}) collective-permute-start(bf16[112,2176]{1,0:T(8,128)(2,1)S(1)} %slice.59.refs_1_), channel_id=1, source_target_pairs={{0,8},{8,0},{16,24},{24,16},{1,9},{9,1},{17,25},{25,17},{2,10},{10... | collective-permute-start | bytes 1462280 | tf_op jit(solution)/shard_map/ppermute | solution.py:371
  65.9 16.1 %collective-permute-start.19 = (bf16[112,2176]{1,0:T(8,128)(2,1)S(1)}, bf16[112,2176]{1,0:T(8,128)(2,1)S(1)}, u32[]{:S(2)}, u32[]{:S(2)}) collective-permute-start(bf16[112,2176]{1,0:T(8,128)(2,1)S(1)} %slice.59.refs_1_), channel_id=1, source_target_pairs={{0,16},{8,24},{16,0},{24,8},{1,17},{9,25},{17,1},{25,9},{2,18},{10... | collective-permute-start | bytes 1462280 | tf_op jit(solution)/shard_map/ppermute | solution.py:375
  66.9 15.1 %collective-permute-start.20 = (bf16[128,2176]{1,0:T(8,128)(2,1)S(1)}, bf16[128,2176]{1,0:T(8,128)(2,1)S(1)}, u32[]{:S(2)}, u32[]{:S(2)}) collective-permute-start(bf16[128,2176]{1,0:T(8,128)(2,1)S(1)} %pad_maximum_fusion.1), channel_id=1, source_target_pairs={{0,2},{1,3},{2,4},{3,5},{4,6},{5,7},{6,0},{7,1},{8,10},{9,11},{10,... | collective-permute-start | bytes 1671176 | tf_op jit(solution)/shard_map/ppermute | solution.py:379
  67.7 14.4 %collective-permute-start.22 = (bf16[64,2048]{1,0:T(8,128)(2,1)S(1)}, bf16[64,2048]{1,0:T(8,128)(2,1)S(1)}, u32[]{:S(2)}, u32[]{:S(2)}) collective-permute-start(bf16[64,2048]{1,0:T(8,128)(2,1)S(1)} %get-tuple-element.131), channel_id=1, source_target_pairs={{0,8},{8,0},{16,24},{24,16},{1,9},{9,1},{17,25},{25,17},{2,10},{10... | collective-permute-start | bytes 786440 | tf_op jit(solution)/shard_map/ppermute | solution.py:371
  68.5 12.5 %collective-permute-start.21 = (bf16[48,2048]{1,0:T(8,128)(2,1)S(1)}, bf16[48,2048]{1,0:T(8,128)(2,1)S(1)}, u32[]{:S(2)}, u32[]{:S(2)}) collective-permute-start(bf16[48,2048]{1,0:T(8,128)(2,1)S(1)} %get-tuple-element.130), channel_id=1, source_target_pairs={{0,16},{8,24},{16,0},{24,8},{1,17},{9,25},{17,1},{25,9},{2,18},{10... | collective-permute-start | bytes 589832 | tf_op jit(solution)/shard_map/ppermute | solution.py:375
  82.1 16.0 %collective-permute-start.23 = (bf16[128,2176]{1,0:T(8,128)(2,1)S(1)}, bf16[128,2176]{1,0:T(8,128)(2,1)S(1)}, u32[]{:S(2)}, u32[]{:S(2)}) collective-permute-start(bf16[128,2176]{1,0:T(8,128)(2,1)S(1)} %fusion.14), channel_id=1, source_target_pairs={{0,2},{1,3},{2,4},{3,5},{4,6},{5,7},{6,0},{7,1},{8,10},{9,11},{10,... | collective-permute-start | bytes 1671176 | tf_op jit(solution)/shard_map/ppermute | solution.py:379
  82.6 15.5 %collective-permute-start.25 = (bf16[64,2176]{1,0:T(8,128)(2,1)S(1)}, bf16[64,2176]{1,0:T(8,128)(2,1)S(1)}, u32[]{:S(2)}, u32[]{:S(2)}) collective-permute-start(bf16[64,2176]{1,0:T(8,128)(2,1)S(1)} %slice.63), channel_id=1, source_target_pairs={{0,8},{8,0},{16,24},{24,16},{1,9},{9,1},{17,25},{25,17},{2,10},{10... | collective-permute-start | bytes 835592 | tf_op jit(solution)/shard_map/ppermute | solution.py:371
  83.5 14.7 %collective-permute-start.26 = (bf16[112,2048]{1,0:T(8,128)(2,1)S(1)}, bf16[112,2048]{1,0:T(8,128)(2,1)S(1)}, u32[]{:S(2)}, u32[]{:S(2)}) collective-permute-start(bf16[112,2048]{1,0:T(8,128)(2,1)S(1)} %get-tuple-element.143), channel_id=1, source_target_pairs={{0,8},{8,0},{16,24},{24,16},{1,9},{9,1},{17,25},{25,17},{2,10},{10... | collective-permute-start | bytes 1376264 | tf_op jit(solution)/shard_map/ppermute | solution.py:371
  84.7 13.5 %collective-permute-start.27 = (bf16[112,2048]{1,0:T(8,128)(2,1)S(1)}, bf16[112,2048]{1,0:T(8,128)(2,1)S(1)}, u32[]{:S(2)}, u32[]{:S(2)}) collective-permute-start(bf16[112,2048]{1,0:T(8,128)(2,1)S(1)} %get-tuple-element.144), channel_id=1, source_target_pairs={{0,16},{8,24},{16,0},{24,8},{1,17},{9,25},{17,1},{25,9},{2,18},{10... | collective-permute-start | bytes 1376264 | tf_op jit(solution)/shard_map/ppermute | solution.py:375
  85.2 12.9 %collective-permute-start.24 = (bf16[48,2176]{1,0:T(8,128)(2,1)S(1)}, bf16[48,2176]{1,0:T(8,128)(2,1)S(1)}, u32[]{:S(2)}, u32[]{:S(2)}) collective-permute-start(bf16[48,2176]{1,0:T(8,128)(2,1)S(1)} %slice.62), channel_id=1, source_target_pairs={{0,16},{8,24},{16,0},{24,8},{1,17},{9,25},{17,1},{25,9},{2,18},{10... | collective-permute-start | bytes 626696 | tf_op jit(solution)/shard_map/ppermute | solution.py:375
  98.4 15.6 %collective-permute-start.28 = (bf16[112,2048]{1,0:T(8,128)(2,1)S(1)}, bf16[112,2048]{1,0:T(8,128)(2,1)S(1)}, u32[]{:S(2)}, u32[]{:S(2)}) collective-permute-start(bf16[112,2048]{1,0:T(8,128)(2,1)S(1)} %get-tuple-element.157), channel_id=1, source_target_pairs={{0,2},{1,3},{2,4},{3,5},{4,6},{5,7},{6,0},{7,1},{8,10},{9,11},{10,... | collective-permute-start | bytes 1376264 | tf_op jit(solution)/shard_map/ppermute | solution.py:379
  100.8 20.8 %collective-permute-start.34 = (bf16[112,2048]{1,0:T(8,128)(2,1)S(1)}, bf16[112,2048]{1,0:T(8,128)(2,1)S(1)}, u32[]{:S(2)}, u32[]{:S(2)}) collective-permute-start(bf16[112,2048]{1,0:T(8,128)(2,1)S(1)} %get-tuple-element.183), channel_id=1, source_target_pairs={{0,6},{1,7},{2,0},{3,1},{4,2},{5,3},{6,4},{7,5},{8,14},{9,15},{10,... | collective-permute-start | bytes 1376264 | tf_op jit(solution)/shard_map/ppermute | solution.py:379
  102.4 14.4 %collective-permute-start.29 = (bf16[112,2048]{1,0:T(8,128)(2,1)S(1)}, bf16[112,2048]{1,0:T(8,128)(2,1)S(1)}, u32[]{:S(2)}, u32[]{:S(2)}) collective-permute-start(bf16[112,2048]{1,0:T(8,128)(2,1)S(1)} %get-tuple-element.159), channel_id=1, source_target_pairs={{0,8},{8,0},{16,24},{24,16},{1,9},{9,1},{17,25},{25,17},{2,10},{10... | collective-permute-start | bytes 1376264 | tf_op jit(solution)/shard_map/ppermute | solution.py:371
  103.1 13.7 %collective-permute-start.30 = (bf16[112,2048]{1,0:T(8,128)(2,1)S(1)}, bf16[112,2048]{1,0:T(8,128)(2,1)S(1)}, u32[]{:S(2)}, u32[]{:S(2)}) collective-permute-start(bf16[112,2048]{1,0:T(8,128)(2,1)S(1)} %get-tuple-element.160), channel_id=1, source_target_pairs={{0,16},{8,24},{16,0},{24,8},{1,17},{9,25},{17,1},{25,9},{2,18},{10... | collective-permute-start | bytes 1376264 | tf_op jit(solution)/shard_map/ppermute | solution.py:375
  114.2 7.4 %collective-permute-start.33 = (bf16[64,2048]{1,0:T(8,128)(2,1)S(1)}, bf16[64,2048]{1,0:T(8,128)(2,1)S(1)}, u32[]{:S(2)}, u32[]{:S(2)}) collective-permute-start(bf16[64,2048]{1,0:T(8,128)(2,1)S(1)} %get-tuple-element.182), channel_id=1, source_target_pairs={{0,8},{8,0},{16,24},{24,16},{1,9},{9,1},{17,25},{25,17},{2,10},{10... | collective-permute-start | bytes 786440 | tf_op jit(solution)/shard_map/ppermute | solution.py:371
  115.2 28.4 %copy-start.1 = (bf16[1,111,2048]{2,1,0:T(8,128)(2,1)S(1)}, bf16[1,111,2048]{2,1,0:T(8,128)(2,1)}, u32[]{:S(2)}) copy-start(bf16[1,111,2048]{2,1,0:T(8,128)(2,1)} %param.21) | copy-start | bytes 1363972
  115.2 6.4 %collective-permute-start.32 = (bf16[48,2048]{1,0:T(8,128)(2,1)S(1)}, bf16[48,2048]{1,0:T(8,128)(2,1)S(1)}, u32[]{:S(2)}, u32[]{:S(2)}) collective-permute-start(bf16[48,2048]{1,0:T(8,128)(2,1)S(1)} %get-tuple-element.181), channel_id=1, source_target_pairs={{0,16},{8,24},{16,0},{24,8},{1,17},{9,25},{17,1},{25,9},{2,18},{10... | collective-permute-start | bytes 589832 | tf_op jit(solution)/shard_map/ppermute | solution.py:375
  116.9 11.7 %collective-permute-start.31 = (bf16[112,2048]{1,0:T(8,128)(2,1)S(1)}, bf16[112,2048]{1,0:T(8,128)(2,1)S(1)}, u32[]{:S(2)}, u32[]{:S(2)}) collective-permute-start(bf16[112,2048]{1,0:T(8,128)(2,1)S(1)} %add_convert_fusion.1), channel_id=1, source_target_pairs={{0,2},{1,3},{2,4},{3,5},{4,6},{5,7},{6,0},{7,1},{8,10},{9,11},{10,... | collective-permute-start | bytes 1376264 | tf_op jit(solution)/shard_map/ppermute | solution.py:379
  117.4 12.0 %collective-permute-start.40 = (bf16[64,2048]{1,0:T(8,128)(2,1)S(1)}, bf16[64,2048]{1,0:T(8,128)(2,1)S(1)}, u32[]{:S(2)}, u32[]{:S(2)}) collective-permute-start(bf16[64,2048]{1,0:T(8,128)(2,1)S(1)} %get-tuple-element.199), channel_id=1, source_target_pairs={{0,8},{8,0},{16,24},{24,16},{1,9},{9,1},{17,25},{25,17},{2,10},{10... | collective-permute-start | bytes 786440 | tf_op jit(solution)/shard_map/ppermute | solution.py:371
  121.7 9.3 %collective-permute-start.41 = (bf16[64,2048]{1,0:T(8,128)(2,1)S(1)}, bf16[64,2048]{1,0:T(8,128)(2,1)S(1)}, u32[]{:S(2)}, u32[]{:S(2)}) collective-permute-start(bf16[64,2048]{1,0:T(8,128)(2,1)S(1)} %get-tuple-element.200), channel_id=1, source_target_pairs={{0,16},{8,24},{16,0},{24,8},{1,17},{9,25},{17,1},{25,9},{2,18},{10... | collective-permute-start | bytes 786440 | tf_op jit(solution)/shard_map/ppermute | solution.py:375
  122.6 8.9 %collective-permute-start.37 = (bf16[48,2048]{1,0:T(8,128)(2,1)S(1)}, bf16[48,2048]{1,0:T(8,128)(2,1)S(1)}, u32[]{:S(2)}, u32[]{:S(2)}) collective-permute-start(bf16[48,2048]{1,0:T(8,128)(2,1)S(1)} %add_convert_fusion.4), channel_id=1, source_target_pairs={{0,8},{8,0},{16,24},{24,16},{1,9},{9,1},{17,25},{25,17},{2,10},{10... | collective-permute-start | bytes 589832 | tf_op jit(solution)/shard_map/ppermute | solution.py:371
  123.3 11.8 %collective-permute-start.38 = (bf16[48,2048]{1,0:T(8,128)(2,1)S(1)}, bf16[48,2048]{1,0:T(8,128)(2,1)S(1)}, u32[]{:S(2)}, u32[]{:S(2)}) collective-permute-start(bf16[48,2048]{1,0:T(8,128)(2,1)S(1)} %get-tuple-element.197), channel_id=1, source_target_pairs={{0,16},{8,24},{16,0},{24,8},{1,17},{9,25},{17,1},{25,9},{2,18},{10... | collective-permute-start | bytes 589832 | tf_op jit(solution)/shard_map/ppermute | solution.py:375
  128.7 14.8 %collective-permute-start.35 = (bf16[112,2048]{1,0:T(8,128)(2,1)S(1)}, bf16[112,2048]{1,0:T(8,128)(2,1)S(1)}, u32[]{:S(2)}, u32[]{:S(2)}) collective-permute-start(bf16[112,2048]{1,0:T(8,128)(2,1)S(1)} %get-tuple-element.189), channel_id=1, source_target_pairs={{0,8},{8,0},{16,24},{24,16},{1,9},{9,1},{17,25},{25,17},{2,10},{10... | collective-permute-start | bytes 1376264 | tf_op jit(solution)/shard_map/ppermute | solution.py:371
  129.4 14.2 %collective-permute-start.36 = (bf16[112,2048]{1,0:T(8,128)(2,1)S(1)}, bf16[112,2048]{1,0:T(8,128)(2,1)S(1)}, u32[]{:S(2)}, u32[]{:S(2)}) collective-permute-start(bf16[112,2048]{1,0:T(8,128)(2,1)S(1)} %get-tuple-element.190), channel_id=1, source_target_pairs={{0,16},{8,24},{16,0},{24,8},{1,17},{9,25},{17,1},{25,9},{2,18},{10... | collective-permute-start | bytes 1376264 | tf_op jit(solution)/shard_map/ppermute | solution.py:375
  131.1 12.4 %collective-permute-start.42 = (bf16[64,2048]{1,0:T(8,128)(2,1)S(1)}, bf16[64,2048]{1,0:T(8,128)(2,1)S(1)}, u32[]{:S(2)}, u32[]{:S(2)}) collective-permute-start(bf16[64,2048]{1,0:T(8,128)(2,1)S(1)} %add_convert_fusion.2), channel_id=1, source_target_pairs={{0,2},{1,3},{2,4},{3,5},{4,6},{5,7},{6,0},{7,1},{8,10},{9,11},{10,... | collective-permute-start | bytes 786440 | tf_op jit(solution)/shard_map/ppermute | solution.py:379
  135.3 8.3 %collective-permute-start.39 = (bf16[48,2048]{1,0:T(8,128)(2,1)S(1)}, bf16[48,2048]{1,0:T(8,128)(2,1)S(1)}, u32[]{:S(2)}, u32[]{:S(2)}) collective-permute-start(bf16[48,2048]{1,0:T(8,128)(2,1)S(1)} %add_convert_fusion.3), channel_id=1, source_target_pairs={{0,2},{1,3},{2,4},{3,5},{4,6},{5,7},{6,0},{7,1},{8,10},{9,11},{10,... | collective-permute-start | bytes 589832 | tf_op jit(solution)/shard_map/ppermute | solution.py:379

commit v15 on v14

--- a/solution.py
+++ b/solution.py
@@ -453,7 +453,7 @@
     ids_row = jnp.pad(ids[:1].astype(jnp.float32), ((0, 0), (0, width - ids.shape[1])))
     shared = jnp.concatenate([partial_proj, jnp.where(is_mine, ids_row, 0.0)], axis=0)
     shared = shared + along_x(shared)
-    sides_0, block_1, other_gate = fence(sides_0, block_1, other_gate)
+    block_1, sides_0, other_gate = fence(block_1, sides_0, other_gate)
 
     corner_0 = spread_corner(sides_0)
     other_up = across_chip(expert_up[0])
@@ -480,7 +480,10 @@
         jnp.pad(decode_ids, ((0, few - 4), (0, 0))),
         "first",
     )
-    sides_1, block_2, decodes_0, other_down = fence(sides_1, block_2, decodes_0, other_down)
+    side_x, block_2, side_y, decodes_0, other_down = fence(
+        sides_1[0], block_2, sides_1[1], decodes_0, other_down
+    )
+    sides_1 = side_x, side_y
     weights = (expert_gate[0], expert_up[0], expert_down[0], other_gate, other_up, other_down)
     halves = (tokens, tokens, tokens, cut, tokens - cut)
 

time: 145 us -> 146 us (level)
  starting transfers between devices: 40.8 us -> 46.2 us
  waiting for transfers between devices: 46.9 us -> 42 us
    ppermute x15, waiting for transfers between devices: 23.2 us -> 14.2 us  [along_y(): return lax.ppermute(value, 'kv', [(i, i ^ 2) for i in range(4)])]
    ppermute x10, waiting for transfers between devices: 20.4 us -> 23 us  [around_z(): lax.ppermute(value, 'blk', [(i, (i + 2 * hops) % 8) for i in range(8)])]
    ppermute x15, starting transfers between devices: 16.3 us -> 18.6 us  [along_y(): return lax.ppermute(value, 'kv', [(i, i ^ 2) for i in range(4)])]
    ppermute x10, starting transfers between devices: 10.1 us -> 12.2 us  [around_z(): lax.ppermute(value, 'blk', [(i, (i + 2 * hops) % 8) for i in range(8)])]
    ppermute x15, waiting for transfers between devices: 3.3 us -> 4.81 us  [along_x(): return lax.ppermute(value, 'kv', [(i, i ^ 1) for i in range(4)])]
  transfers between devices with their start and end apart: 43 -> 43, of which waited for: 17 -> 18; matrix products, arithmetic and copies ran while one was open for 6% -> 6% of each run, Pallas kernels for 28% -> 28%
where the time goes in v15:
time: 146 us; the launch traced here: 145 us
  starting transfers between devices  46.2 us (32%)
  Pallas kernels  42.1 us (29%)
  waiting for transfers between devices  42 us (29%)
  other arithmetic  5.08 us (3%)
  matrix products  4.86 us (3%)
  local copies, waits for them, and re-layouts  4.65 us (3%)
    pallas_call x4, Pallas kernels, run_plane(): pl.pallas_call(functools.partial(plane_kernel, cap, piece_rows, block_row...  40.3 us
    ppermute x10, waiting for transfers between devices, around_z(): lax.ppermute(value, 'blk', [(i, (i + 2 * hops) % 8) for i in range(8)])  23 us
    ppermute x15, starting transfers between devices, along_y(): return lax.ppermute(value, 'kv', [(i, i ^ 2) for i in range(4)])  18.6 us
    ppermute x15, starting transfers between devices, along_x(): return lax.ppermute(value, 'kv', [(i, i ^ 1) for i in range(4)])  14.9 us
    ppermute x15, waiting for transfers between devices, along_y(): return lax.ppermute(value, 'kv', [(i, i ^ 2) for i in range(4)])  14.2 us
    ppermute x10, starting transfers between devices, around_z(): lax.ppermute(value, 'blk', [(i, (i + 2 * hops) % 8) for i in range(8)])  12.2 us
    ppermute x15, waiting for transfers between devices, along_x(): return lax.ppermute(value, 'kv', [(i, i ^ 1) for i in range(4)])  4.81 us
    unnamed x20, local copies, waits for them, and re-layouts  4.4 us
  transfers between devices with their start and end apart: 43, of which 18 were waited for; matrix products, arithmetic and copies ran while one was open for 6% of the time, Pallas kernels for 28%

profile of v15, /device:TPU:0, one launch (start us, length us, event | category | flops | bytes accessed | tf_op | source)
XLA Modules:
  0.0 145.3 jit_solution(180711882705133796)
XLA Ops:
  0.0 1.0 copy-done
  1.0 0.9 copy-done.2
  1.9 0.7 copy-done.4
  2.6 0.7 copy-done.6
  3.3 0.8 prepare.2.refs_1_
  4.1 3.1 %collective-permute-start = (bf16[112,2176]{1,0:T(8,128)(2,1)S(1)}, bf16[112,2176]{1,0:T(8,128)(2,1)S(1)}, u32[]{:S(2)}, u32[]{:S(2)}) collective-permute-start(bf16[112,2176]{1,0:T(8,128)(2,1)S(1)} %prepare.2.refs_1_), channel_id=1, source_target_pairs={{0,2},{1,3},{2,4},{3,5},{4,6},{5,7},{6,0},{7,1},{8,10},{9,11},{10,... | collective-permute-start | bytes 1462280 | tf_op jit(solution)/shard_map/ppermute | solution.py:379
  7.2 1.5 %collective-permute-start.1 = (bf16[112,2176]{1,0:T(8,128)(2,1)S(1)}, bf16[112,2176]{1,0:T(8,128)(2,1)S(1)}, u32[]{:S(2)}, u32[]{:S(2)}) collective-permute-start(bf16[112,2176]{1,0:T(8,128)(2,1)S(1)} %prepare.2.refs_1_), channel_id=1, source_target_pairs={{0,8},{8,0},{16,24},{24,16},{1,9},{9,1},{17,25},{25,17},{2,10},{10... | collective-permute-start | bytes 1462280 | tf_op jit(solution)/shard_map/ppermute | solution.py:371
  8.7 1.5 %collective-permute-start.2 = (bf16[112,2176]{1,0:T(8,128)(2,1)S(1)}, bf16[112,2176]{1,0:T(8,128)(2,1)S(1)}, u32[]{:S(2)}, u32[]{:S(2)}) collective-permute-start(bf16[112,2176]{1,0:T(8,128)(2,1)S(1)} %prepare.2.refs_1_), channel_id=1, source_target_pairs={{0,16},{8,24},{16,0},{24,8},{1,17},{9,25},{17,1},{25,9},{2,18},{10... | collective-permute-start | bytes 1462280 | tf_op jit(solution)/shard_map/ppermute | solution.py:375
  10.7 0.7 minimum_subtract_fusion
  11.5 0.9 broadcast_in_dim.76
  12.4 1.0 convert_reduce_fusion
  13.4 3.5 %fusion.36 = (f32[4,8]{1,0:T(4,128)S(1)}, f32[4,8,4096]{2,1,0:T(8,128)S(1)}) fusion(bf16[4,4096,1,128]{3,1,2,0:T(8,128)(2,1)} %param.15, bf16[1,4,8,128]{3,1,2,0:T(4,128)(2,1)} %bitcast.51, pred[4,4096]{1,0:T(4,128)(4,1)S(1)} %iota_compare_fusion.2), kind=kOutput, calls=%fused_computation.61 | convolution fusion | flops 33947616 | bytes 4743296 | tf_op jit(solution)/shard_map/rgd,rjd->rgj/dot_general | solution.py:27
  17.2 0.7 fusion.11
  18.0 1.1 copy-done.8
  20.3 1.5 %collective-permute-start.6 = (f32[8,2048]{1,0:T(8,128)S(1)}, f32[8,2048]{1,0:T(8,128)S(1)}, u32[]{:S(2)}, u32[]{:S(2)}) collective-permute-start(f32[8,2048]{1,0:T(8,128)S(1)} %pad_maximum_fusion.2), channel_id=1, source_target_pairs={{0,8},{8,0},{16,24},{24,16},{1,9},{9,1},{17,25},{25,17},{2,10},{10... | collective-permute-start | bytes 196616 | tf_op jit(solution)/shard_map/ppermute | solution.py:371
  22.5 1.6 %collective-permute-start.4 = (bf16[48,2176]{1,0:T(8,128)(2,1)S(1)}, bf16[48,2176]{1,0:T(8,128)(2,1)S(1)}, u32[]{:S(2)}, u32[]{:S(2)}) collective-permute-start(bf16[48,2176]{1,0:T(8,128)(2,1)S(1)} %slice.52), channel_id=1, source_target_pairs={{0,16},{8,24},{16,0},{24,8},{1,17},{9,25},{17,1},{25,9},{2,18},{10... | collective-permute-start | bytes 626696 | tf_op jit(solution)/shard_map/ppermute | solution.py:375
  24.1 1.2 collective-permute-done.6
  25.3 3.3 %collective-permute-done.4.refs_4_ = bf16[48,2176]{1,0:T(8,128)(2,1)S(1)} collective-permute-done((bf16[48,2176]{1,0:T(8,128)(2,1)S(1)}, bf16[48,2176]{1,0:T(8,128)(2,1)S(1)}, u32[]{:S(2)}, u32[]{:S(2)}) %collective-permute-start.4) | collective-permute-done | bytes 208928 | tf_op jit(solution)/shard_map/ppermute | solution.py:375
  28.6 1.4 collective-permute-done.5.refs_5_
  30.0 1.5 %collective-permute-start.8 = (f32[8,2048]{1,0:T(8,128)S(1)}, f32[8,2048]{1,0:T(8,128)S(1)}, u32[]{:S(2)}, u32[]{:S(2)}) collective-permute-start(f32[8,2048]{1,0:T(8,128)S(1)} %fusion.35), channel_id=1, source_target_pairs={{0,16},{8,24},{16,0},{24,8},{1,17},{9,25},{17,1},{25,9},{2,18},{10... | collective-permute-start | bytes 196616 | tf_op jit(solution)/shard_map/ppermute | solution.py:375
  32.0 1.5 %collective-permute-start.11 = (bf16[112,2176]{1,0:T(8,128)(2,1)S(1)}, bf16[112,2176]{1,0:T(8,128)(2,1)S(1)}, u32[]{:S(2)}, u32[]{:S(2)}) collective-permute-start(bf16[112,2176]{1,0:T(8,128)(2,1)S(1)} %collective-permute-done.refs_1_), channel_id=1, source_target_pairs={{0,16},{8,24},{16,0},{24,8},{1,17},{9,25},{17,1},{25,9},{2,18},{10... | collective-permute-start | bytes 1462280 | tf_op jit(solution)/shard_map/ppermute | solution.py:375
  33.5 0.8 collective-permute-start.9
  35.2 11.4 %collective-permute-done.10.refs_1_ = bf16[112,2176]{1,0:T(8,128)(2,1)S(1)} collective-permute-done((bf16[112,2176]{1,0:T(8,128)(2,1)S(1)}, bf16[112,2176]{1,0:T(8,128)(2,1)S(1)}, u32[]{:S(2)}, u32[]{:S(2)}) %collective-permute-start.10) | collective-permute-done | bytes 487456 | tf_op jit(solution)/shard_map/ppermute | solution.py:379
  46.6 0.9 collective-permute-start.15
  47.6 0.7 collective-permute-start.16
  48.3 1.3 collective-permute-start.17
  49.6 0.9 collective-permute-start.14
  50.5 1.6 %collective-permute-start.13 = (bf16[48,2176]{1,0:T(8,128)(2,1)S(1)}, bf16[48,2176]{1,0:T(8,128)(2,1)S(1)}, u32[]{:S(2)}, u32[]{:S(2)}) collective-permute-start(bf16[48,2176]{1,0:T(8,128)(2,1)S(1)} %slice.57), channel_id=1, source_target_pairs={{0,16},{8,24},{16,0},{24,8},{1,17},{9,25},{17,1},{25,9},{2,18},{10... | collective-permute-start | bytes 626696 | tf_op jit(solution)/shard_map/ppermute | solution.py:375
  52.1 10.1 %plane.4 = (bf16[112,2048]{1,0:T(8,128)(2,1)S(1)}, bf16[112,2048]{1,0:T(8,128)(2,1)S(1)}, bf16[112,2048]{1,0:T(8,128)(2,1)S(1)}, bf16[48,2048]{1,0:T(8,128)(2,1)S(1)}, bf16[64,2048]{1,0:T(8,128)(2,1)S(1)}) custom-call(s32[3]{0:T(128)S(1)} %pad_add_fusion.refs_0_, bf16[112,2176]{1,0:T(8,128)(2,1)S(1)} %prepare.2.refs_1_, ...), custom_call_target="tpu_custom_call" | custom-call | flops 8455716864 | bytes 25165824 | tf_op jit(solution)/shard_map/plane/pallas_call | solution.py:277
  62.2 2.0 %collective-permute-done.13.refs_4_ = bf16[48,2176]{1,0:T(8,128)(2,1)S(1)} collective-permute-done((bf16[48,2176]{1,0:T(8,128)(2,1)S(1)}, bf16[48,2176]{1,0:T(8,128)(2,1)S(1)}, u32[]{:S(2)}, u32[]{:S(2)}) %collective-permute-start.13) | collective-permute-done | bytes 208928 | tf_op jit(solution)/shard_map/ppermute | solution.py:375
  64.2 0.9 collective-permute-done.14.refs_5_
  65.2 0.9 collective-permute-start.18
  66.1 0.7 collective-permute-start.19
  66.8 0.8 collective-permute-start.20
  67.6 1.0 collective-permute-start.22
  68.6 1.4 collective-permute-start.21
  70.0 10.1 %plane.5 = (bf16[112,2048]{1,0:T(8,128)(2,1)S(1)}, bf16[112,2048]{1,0:T(8,128)(2,1)S(1)}, bf16[112,2048]{1,0:T(8,128)(2,1)S(1)}, bf16[112,2048]{1,0:T(8,128)(2,1)S(1)}) custom-call(s32[3]{0:T(128)S(1)} %pad_add_fusion.refs_0_, bf16[112,2176]{1,0:T(8,128)(2,1)S(1)} %collective-permute-done.refs_1_, bf16[112,2176]{1,0:T(8,128)(2,1)S(1)} %collective-permute-done.9.refs_2_, ...), custom_call_target="tpu_custom_call" | custom-call | flops 8455716864 | bytes 25165824 | tf_op jit(solution)/shard_map/plane/pallas_call | solution.py:277
  80.1 1.5 %collective-permute-done.21.passed_0_ref = bf16[48,2048]{1,0:T(8,128)(2,1)S(1)} collective-permute-done((bf16[48,2048]{1,0:T(8,128)(2,1)S(1)}, bf16[48,2048]{1,0:T(8,128)(2,1)S(1)}, u32[]{:S(2)}, u32[]{:S(2)}) %collective-permute-start.21) | collective-permute-done | bytes 196640 | tf_op jit(solution)/shard_map/ppermute | solution.py:375
  81.6 0.8 collective-permute-done.22.passed_1_ref
  82.8 0.9 collective-permute-start.25
  83.7 1.2 collective-permute-start.26
  85.4 1.6 %collective-permute-start.24 = (bf16[48,2176]{1,0:T(8,128)(2,1)S(1)}, bf16[48,2176]{1,0:T(8,128)(2,1)S(1)}, u32[]{:S(2)}, u32[]{:S(2)}) collective-permute-start(bf16[48,2176]{1,0:T(8,128)(2,1)S(1)} %slice.62), channel_id=1, source_target_pairs={{0,16},{8,24},{16,0},{24,8},{1,17},{9,25},{17,1},{25,9},{2,18},{10... | collective-permute-start | bytes 626696 | tf_op jit(solution)/shard_map/ppermute | solution.py:375
  87.0 10.1 %plane.6 = (bf16[112,2048]{1,0:T(8,128)(2,1)S(1)}, bf16[112,2048]{1,0:T(8,128)(2,1)S(1)}, bf16[112,2048]{1,0:T(8,128)(2,1)S(1)}, bf16[112,2048]{1,0:T(8,128)(2,1)S(1)}) custom-call(s32[3]{0:T(128)S(1)} %pad_add_fusion.refs_0_, bf16[112,2176]{1,0:T(8,128)(2,1)S(1)} %collective-permute-done.10.refs_1_, bf16[112,2176]{1,0:T(8,128)(2,1)S(1)} %collective-permute-done.15.refs_2_, ...), custom_call_target="tpu_custom_call" | custom-call | flops 8455716864 | bytes 25165824 | tf_op jit(solution)/shard_map/plane/pallas_call | solution.py:277
  97.1 1.7 %collective-permute-done.24.refs_4_ = bf16[48,2176]{1,0:T(8,128)(2,1)S(1)} collective-permute-done((bf16[48,2176]{1,0:T(8,128)(2,1)S(1)}, bf16[48,2176]{1,0:T(8,128)(2,1)S(1)}, u32[]{:S(2)}, u32[]{:S(2)}) %collective-permute-start.24) | collective-permute-done | bytes 208928 | tf_op jit(solution)/shard_map/ppermute | solution.py:375
  99.1 1.2 collective-permute-start.28
  100.3 2.7 %collective-permute-start.34 = (bf16[112,2048]{1,0:T(8,128)(2,1)S(1)}, bf16[112,2048]{1,0:T(8,128)(2,1)S(1)}, u32[]{:S(2)}, u32[]{:S(2)}) collective-permute-start(bf16[112,2048]{1,0:T(8,128)(2,1)S(1)} %get-tuple-element.183), channel_id=1, source_target_pairs={{0,6},{1,7},{2,0},{3,1},{4,2},{5,3},{6,4},{7,5},{8,14},{9,15},{10,... | collective-permute-start | bytes 1376264 | tf_op jit(solution)/shard_map/ppermute | solution.py:379
  103.0 0.9 collective-permute-start.29
  103.9 0.7 collective-permute-start.30
  104.5 10.1 %plane.7 = (bf16[112,2048]{1,0:T(8,128)(2,1)S(1)}, bf16[48,2048]{1,0:T(8,128)(2,1)S(1)}, bf16[64,2048]{1,0:T(8,128)(2,1)S(1)}, bf16[48,2048]{1,0:T(8,128)(2,1)S(...) custom-call(s32[3]{0:T(128)S(1)} %pad_add_fusion.refs_0_, ...), custom_call_target="tpu_custom_call" | custom-call | flops 8455716864 | bytes 25165824 | tf_op jit(solution)/shard_map/plane/pallas_call | solution.py:277
  114.8 1.1 collective-permute-start.33
  115.8 1.5 %collective-permute-start.32 = (bf16[48,2048]{1,0:T(8,128)(2,1)S(1)}, bf16[48,2048]{1,0:T(8,128)(2,1)S(1)}, u32[]{:S(2)}, u32[]{:S(2)}) collective-permute-start(bf16[48,2048]{1,0:T(8,128)(2,1)S(1)} %get-tuple-element.181), channel_id=1, source_target_pairs={{0,16},{8,24},{16,0},{24,8},{1,17},{9,25},{17,1},{25,9},{2,18},{10... | collective-permute-start | bytes 589832 | tf_op jit(solution)/shard_map/ppermute | solution.py:375
  117.6 0.9 collective-permute-start.40
  118.6 1.7 %collective-permute-done.34 = bf16[112,2048]{1,0:T(8,128)(2,1)S(1)} collective-permute-done((bf16[112,2048]{1,0:T(8,128)(2,1)S(1)}, bf16[112,2048]{1,0:T(8,128)(2,1)S(1)}, u32[]{:S(2)}, u32[]{:S(2)}) %collective-permute-start.34) | collective-permute-done | bytes 458784 | tf_op jit(solution)/shard_map/ppermute | solution.py:379
  120.3 2.4 %collective-permute-done.32 = bf16[48,2048]{1,0:T(8,128)(2,1)S(1)} collective-permute-done((bf16[48,2048]{1,0:T(8,128)(2,1)S(1)}, bf16[48,2048]{1,0:T(8,128)(2,1)S(1)}, u32[]{:S(2)}, u32[]{:S(2)}) %collective-permute-start.32) | collective-permute-done | bytes 196640 | tf_op jit(solution)/shard_map/ppermute | solution.py:375
  122.8 2.5 %collective-permute-start.41 = (bf16[64,2048]{1,0:T(8,128)(2,1)S(1)}, bf16[64,2048]{1,0:T(8,128)(2,1)S(1)}, u32[]{:S(2)}, u32[]{:S(2)}) collective-permute-start(bf16[64,2048]{1,0:T(8,128)(2,1)S(1)} %get-tuple-element.200), channel_id=1, source_target_pairs={{0,16},{8,24},{16,0},{24,8},{1,17},{9,25},{17,1},{25,9},{2,18},{10... | collective-permute-start | bytes 786440 | tf_op jit(solution)/shard_map/ppermute | solution.py:375
  125.3 0.9 collective-permute-start.37
  126.2 0.7 collective-permute-start.38
  126.9 3.1 %collective-permute-done.31 = bf16[112,2048]{1,0:T(8,128)(2,1)S(1)} collective-permute-done((bf16[112,2048]{1,0:T(8,128)(2,1)S(1)}, bf16[112,2048]{1,0:T(8,128)(2,1)S(1)}, u32[]{:S(2)}, u32[]{:S(2)}) %collective-permute-start.31) | collective-permute-done | bytes 458784 | tf_op jit(solution)/shard_map/ppermute | solution.py:379
  130.1 0.8 collective-permute-start.35
  130.9 0.7 collective-permute-start.36
  133.2 2.8 %collective-permute-done.38 = bf16[48,2048]{1,0:T(8,128)(2,1)S(1)} collective-permute-done((bf16[48,2048]{1,0:T(8,128)(2,1)S(1)}, bf16[48,2048]{1,0:T(8,128)(2,1)S(1)}, u32[]{:S(2)}, u32[]{:S(2)}) %collective-permute-start.38) | collective-permute-done | bytes 196640 | tf_op jit(solution)/shard_map/ppermute | solution.py:375
  136.1 1.8 %collective-permute-start.39 = (bf16[48,2048]{1,0:T(8,128)(2,1)S(1)}, bf16[48,2048]{1,0:T(8,128)(2,1)S(1)}, u32[]{:S(2)}, u32[]{:S(2)}) collective-permute-start(bf16[48,2048]{1,0:T(8,128)(2,1)S(1)} %add_convert_fusion.3), channel_id=1, source_target_pairs={{0,2},{1,3},{2,4},{3,5},{4,6},{5,7},{6,0},{7,1},{8,10},{9,11},{10,... | collective-permute-start | bytes 589832 | tf_op jit(solution)/shard_map/ppermute | solution.py:379
  137.9 6.2 %collective-permute-done.39 = bf16[48,2048]{1,0:T(8,128)(2,1)S(1)} collective-permute-done((bf16[48,2048]{1,0:T(8,128)(2,1)S(1)}, bf16[48,2048]{1,0:T(8,128)(2,1)S(1)}, u32[]{:S(2)}, u32[]{:S(2)}) %collective-permute-start.39) | collective-permute-done | bytes 196640 | tf_op jit(solution)/shard_map/ppermute | solution.py:379
  144.1 1.2 fusion.15
  (92 shorter events, 7.9 us)
Async XLA Ops:
  0.0 16.9 %copy-start.9 = (f32[8]{0:T(128)S(1)}, f32[8]{0:T(128)}, u32[]{:S(2)}) copy-start(f32[8]{0:T(128)} %param.18) | copy-start | bytes 100
  0.0 1.0 copy-start
  1.0 0.9 copy-start.2
  1.9 0.7 copy-start.4
  2.6 0.7 copy-start.6
  4.1 16.2 %collective-permute-start = (bf16[112,2176]{1,0:T(8,128)(2,1)S(1)}, bf16[112,2176]{1,0:T(8,128)(2,1)S(1)}, u32[]{:S(2)}, u32[]{:S(2)}) collective-permute-start(bf16[112,2176]{1,0:T(8,128)(2,1)S(1)} %prepare.2.refs_1_), channel_id=1, source_target_pairs={{0,2},{1,3},{2,4},{3,5},{4,6},{5,7},{6,0},{7,1},{8,10},{9,11},{10,... | collective-permute-start | bytes 1462280 | tf_op jit(solution)/shard_map/ppermute | solution.py:379
  7.2 14.7 %collective-permute-start.1 = (bf16[112,2176]{1,0:T(8,128)(2,1)S(1)}, bf16[112,2176]{1,0:T(8,128)(2,1)S(1)}, u32[]{:S(2)}, u32[]{:S(2)}) collective-permute-start(bf16[112,2176]{1,0:T(8,128)(2,1)S(1)} %prepare.2.refs_1_), channel_id=1, source_target_pairs={{0,8},{8,0},{16,24},{24,16},{1,9},{9,1},{17,25},{25,17},{2,10},{10... | collective-permute-start | bytes 1462280 | tf_op jit(solution)/shard_map/ppermute | solution.py:371
  8.7 13.2 %collective-permute-start.2 = (bf16[112,2176]{1,0:T(8,128)(2,1)S(1)}, bf16[112,2176]{1,0:T(8,128)(2,1)S(1)}, u32[]{:S(2)}, u32[]{:S(2)}) collective-permute-start(bf16[112,2176]{1,0:T(8,128)(2,1)S(1)} %prepare.2.refs_1_), channel_id=1, source_target_pairs={{0,16},{8,24},{16,0},{24,8},{1,17},{9,25},{17,1},{25,9},{2,18},{10... | collective-permute-start | bytes 1462280 | tf_op jit(solution)/shard_map/ppermute | solution.py:375
  10.2 11.7 %collective-permute-start.3 = (bf16[2048,768]{1,0:T(8,128)(2,1)}, bf16[2048,768]{1,0:T(8,128)(2,1)}, u32[]{:S(2)}, u32[]{:S(2)}) collective-permute-start(bf16[2048,768]{1,0:T(8,128)(2,1)} %bitcast.53), channel_id=1, source_target_pairs={{0,1},{1,0},{2,3},{3,2},{4,5},{5,4},{6,7},{7,6},{8,9},{9,8},{10,11... | collective-permute-start | bytes 9437192 | tf_op jit(solution)/shard_map/ppermute | solution.py:383
  10.2 15.1 %collective-permute-start.7 = (bf16[2048,768]{1,0:T(8,128)(2,1)}, bf16[2048,768]{1,0:T(8,128)(2,1)}, u32[]{:S(2)}, u32[]{:S(2)}) collective-permute-start(bf16[2048,768]{1,0:T(8,128)(2,1)} %bitcast.58), channel_id=1, source_target_pairs={{0,1},{1,0},{2,3},{3,2},{4,5},{5,4},{6,7},{7,6},{8,9},{9,8},{10,11... | collective-permute-start | bytes 9437192 | tf_op jit(solution)/shard_map/ppermute | solution.py:383
  11.5 5.7 %copy-start.7 = (bf16[4,4096,1,128]{3,1,2,0:T(8,128)(2,1)S(1)}, bf16[4,4096,1,128]{3,1,2,0:T(8,128)(2,1)}, u32[]{:S(2)}) copy-start(bf16[4,4096,1,128]{3,1,2,0:T(8,128)(2,1)} %param.16) | copy-start | bytes 12582916
  16.9 2.2 %copy-start.8 = (bf16[1024,2048]{1,0:T(8,128)(2,1)S(1)}, bf16[1024,2048]{1,0:T(8,128)(2,1)}, u32[]{:S(2)}) copy-start(bf16[1024,2048]{1,0:T(8,128)(2,1)} %param.19) | copy-start | bytes 12582916
  17.9 16.7 %copy-start.3 = (bf16[2048,32]{0,1:T(8,128)(2,1)S(1)}, bf16[2048,32]{0,1:T(8,128)(2,1)}, u32[]{:S(2)}) copy-start(bf16[2048,32]{0,1:T(8,128)(2,1)} %param.23) | copy-start | bytes 393220
  17.9 16.7 %copy-start.5 = (f32[2048]{0:T(1024)S(1)}, f32[2048]{0:T(1024)}, u32[]{:S(2)}) copy-start(f32[2048]{0:T(1024)} %param.22) | copy-start | bytes 24580
  20.3 4.9 %collective-permute-start.6 = (f32[8,2048]{1,0:T(8,128)S(1)}, f32[8,2048]{1,0:T(8,128)S(1)}, u32[]{:S(2)}, u32[]{:S(2)}) collective-permute-start(f32[8,2048]{1,0:T(8,128)S(1)} %pad_maximum_fusion.2), channel_id=1, source_target_pairs={{0,8},{8,0},{16,24},{24,16},{1,9},{9,1},{17,25},{25,17},{2,10},{10... | collective-permute-start | bytes 196616 | tf_op jit(solution)/shard_map/ppermute | solution.py:371
  21.9 8.1 %collective-permute-start.5 = (bf16[64,2176]{1,0:T(8,128)(2,1)S(1)}, bf16[64,2176]{1,0:T(8,128)(2,1)S(1)}, u32[]{:S(2)}, u32[]{:S(2)}) collective-permute-start(bf16[64,2176]{1,0:T(8,128)(2,1)S(1)} %slice.53), channel_id=1, source_target_pairs={{0,8},{8,0},{16,24},{24,16},{1,9},{9,1},{17,25},{25,17},{2,10},{10... | collective-permute-start | bytes 835592 | tf_op jit(solution)/shard_map/ppermute | solution.py:371
  22.5 6.1 %collective-permute-start.4 = (bf16[48,2176]{1,0:T(8,128)(2,1)S(1)}, bf16[48,2176]{1,0:T(8,128)(2,1)S(1)}, u32[]{:S(2)}, u32[]{:S(2)}) collective-permute-start(bf16[48,2176]{1,0:T(8,128)(2,1)S(1)} %slice.52), channel_id=1, source_target_pairs={{0,16},{8,24},{16,0},{24,8},{1,17},{9,25},{17,1},{25,9},{2,18},{10... | collective-permute-start | bytes 626696 | tf_op jit(solution)/shard_map/ppermute | solution.py:375
  30.0 16.7 %collective-permute-start.12 = (bf16[768,2048]{1,0:T(8,128)(2,1)}, bf16[768,2048]{1,0:T(8,128)(2,1)}, u32[]{:S(2)}, u32[]{:S(2)}) collective-permute-start(bf16[768,2048]{1,0:T(8,128)(2,1)} %bitcast.11.refs_9_.refs_7_), channel_id=1, source_target_pairs={{0,1},{1,0},{2,3},{3,2},{4,5},{5,4},{6,7},{7,6},{8,9},{9,8},{10,11... | collective-permute-start | bytes 9437192 | tf_op jit(solution)/shard_map/ppermute | solution.py:383
  30.0 4.5 %collective-permute-start.8 = (f32[8,2048]{1,0:T(8,128)S(1)}, f32[8,2048]{1,0:T(8,128)S(1)}, u32[]{:S(2)}, u32[]{:S(2)}) collective-permute-start(f32[8,2048]{1,0:T(8,128)S(1)} %fusion.35), channel_id=1, source_target_pairs={{0,16},{8,24},{16,0},{24,8},{1,17},{9,25},{17,1},{25,9},{2,18},{10... | collective-permute-start | bytes 196616 | tf_op jit(solution)/shard_map/ppermute | solution.py:375
  31.5 15.1 %collective-permute-start.10 = (bf16[112,2176]{1,0:T(8,128)(2,1)S(1)}, bf16[112,2176]{1,0:T(8,128)(2,1)S(1)}, u32[]{:S(2)}, u32[]{:S(2)}) collective-permute-start(bf16[112,2176]{1,0:T(8,128)(2,1)S(1)} %collective-permute-done.refs_1_), channel_id=1, source_target_pairs={{0,2},{1,3},{2,4},{3,5},{4,6},{5,7},{6,0},{7,1},{8,10},{9,11},{10,... | collective-permute-start | bytes 1462280 | tf_op jit(solution)/shard_map/ppermute | solution.py:379
  32.0 14.6 %collective-permute-start.11 = (bf16[112,2176]{1,0:T(8,128)(2,1)S(1)}, bf16[112,2176]{1,0:T(8,128)(2,1)S(1)}, u32[]{:S(2)}, u32[]{:S(2)}) collective-permute-start(bf16[112,2176]{1,0:T(8,128)(2,1)S(1)} %collective-permute-done.refs_1_), channel_id=1, source_target_pairs={{0,16},{8,24},{16,0},{24,8},{1,17},{9,25},{17,1},{25,9},{2,18},{10... | collective-permute-start | bytes 1462280 | tf_op jit(solution)/shard_map/ppermute | solution.py:375
  33.5 13.1 %collective-permute-start.9 = (bf16[112,2176]{1,0:T(8,128)(2,1)S(1)}, bf16[112,2176]{1,0:T(8,128)(2,1)S(1)}, u32[]{:S(2)}, u32[]{:S(2)}) collective-permute-start(bf16[112,2176]{1,0:T(8,128)(2,1)S(1)} %collective-permute-done.refs_1_), channel_id=1, source_target_pairs={{0,8},{8,0},{16,24},{24,16},{1,9},{9,1},{17,25},{25,17},{2,10},{10... | collective-permute-start | bytes 1462280 | tf_op jit(solution)/shard_map/ppermute | solution.py:371
  46.6 18.5 %collective-permute-start.15 = (bf16[112,2176]{1,0:T(8,128)(2,1)S(1)}, bf16[112,2176]{1,0:T(8,128)(2,1)S(1)}, u32[]{:S(2)}, u32[]{:S(2)}) collective-permute-start(bf16[112,2176]{1,0:T(8,128)(2,1)S(1)} %collective-permute-done.10.refs_1_), channel_id=1, source_target_pairs={{0,8},{8,0},{16,24},{24,16},{1,9},{9,1},{17,25},{25,17},{2,10},{10... | collective-permute-start | bytes 1462280 | tf_op jit(solution)/shard_map/ppermute | solution.py:371
  47.6 17.5 %collective-permute-start.16 = (bf16[112,2176]{1,0:T(8,128)(2,1)S(1)}, bf16[112,2176]{1,0:T(8,128)(2,1)S(1)}, u32[]{:S(2)}, u32[]{:S(2)}) collective-permute-start(bf16[112,2176]{1,0:T(8,128)(2,1)S(1)} %collective-permute-done.10.refs_1_), channel_id=1, source_target_pairs={{0,16},{8,24},{16,0},{24,8},{1,17},{9,25},{17,1},{25,9},{2,18},{10... | collective-permute-start | bytes 1462280 | tf_op jit(solution)/shard_map/ppermute | solution.py:375
  48.3 16.9 %collective-permute-start.17 = (bf16[128,2176]{1,0:T(8,128)(2,1)S(1)}, bf16[128,2176]{1,0:T(8,128)(2,1)S(1)}, u32[]{:S(2)}, u32[]{:S(2)}) collective-permute-start(bf16[128,2176]{1,0:T(8,128)(2,1)S(1)} %pad_maximum_fusion), channel_id=1, source_target_pairs={{0,2},{1,3},{2,4},{3,5},{4,6},{5,7},{6,0},{7,1},{8,10},{9,11},{10,... | collective-permute-start | bytes 1671176 | tf_op jit(solution)/shard_map/ppermute | solution.py:379
  49.6 15.5 %collective-permute-start.14 = (bf16[64,2176]{1,0:T(8,128)(2,1)S(1)}, bf16[64,2176]{1,0:T(8,128)(2,1)S(1)}, u32[]{:S(2)}, u32[]{:S(2)}) collective-permute-start(bf16[64,2176]{1,0:T(8,128)(2,1)S(1)} %slice.58), channel_id=1, source_target_pairs={{0,8},{8,0},{16,24},{24,16},{1,9},{9,1},{17,25},{25,17},{2,10},{10... | collective-permute-start | bytes 835592 | tf_op jit(solution)/shard_map/ppermute | solution.py:371
  50.5 13.7 %collective-permute-start.13 = (bf16[48,2176]{1,0:T(8,128)(2,1)S(1)}, bf16[48,2176]{1,0:T(8,128)(2,1)S(1)}, u32[]{:S(2)}, u32[]{:S(2)}) collective-permute-start(bf16[48,2176]{1,0:T(8,128)(2,1)S(1)} %slice.57), channel_id=1, source_target_pairs={{0,16},{8,24},{16,0},{24,8},{1,17},{9,25},{17,1},{25,9},{2,18},{10... | collective-permute-start | bytes 626696 | tf_op jit(solution)/shard_map/ppermute | solution.py:375
  65.2 17.2 %collective-permute-start.18 = (bf16[112,2176]{1,0:T(8,128)(2,1)S(1)}, bf16[112,2176]{1,0:T(8,128)(2,1)S(1)}, u32[]{:S(2)}, u32[]{:S(2)}) collective-permute-start(bf16[112,2176]{1,0:T(8,128)(2,1)S(1)} %slice.59.refs_1_), channel_id=1, source_target_pairs={{0,8},{8,0},{16,24},{24,16},{1,9},{9,1},{17,25},{25,17},{2,10},{10... | collective-permute-start | bytes 1462280 | tf_op jit(solution)/shard_map/ppermute | solution.py:371
  66.1 16.3 %collective-permute-start.19 = (bf16[112,2176]{1,0:T(8,128)(2,1)S(1)}, bf16[112,2176]{1,0:T(8,128)(2,1)S(1)}, u32[]{:S(2)}, u32[]{:S(2)}) collective-permute-start(bf16[112,2176]{1,0:T(8,128)(2,1)S(1)} %slice.59.refs_1_), channel_id=1, source_target_pairs={{0,16},{8,24},{16,0},{24,8},{1,17},{9,25},{17,1},{25,9},{2,18},{10... | collective-permute-start | bytes 1462280 | tf_op jit(solution)/shard_map/ppermute | solution.py:375
  66.8 15.6 %collective-permute-start.20 = (bf16[128,2176]{1,0:T(8,128)(2,1)S(1)}, bf16[128,2176]{1,0:T(8,128)(2,1)S(1)}, u32[]{:S(2)}, u32[]{:S(2)}) collective-permute-start(bf16[128,2176]{1,0:T(8,128)(2,1)S(1)} %pad_maximum_fusion.1), channel_id=1, source_target_pairs={{0,2},{1,3},{2,4},{3,5},{4,6},{5,7},{6,0},{7,1},{8,10},{9,11},{10,... | collective-permute-start | bytes 1671176 | tf_op jit(solution)/shard_map/ppermute | solution.py:379
  67.6 14.7 %collective-permute-start.22 = (bf16[64,2048]{1,0:T(8,128)(2,1)S(1)}, bf16[64,2048]{1,0:T(8,128)(2,1)S(1)}, u32[]{:S(2)}, u32[]{:S(2)}) collective-permute-start(bf16[64,2048]{1,0:T(8,128)(2,1)S(1)} %get-tuple-element.131), channel_id=1, source_target_pairs={{0,8},{8,0},{16,24},{24,16},{1,9},{9,1},{17,25},{25,17},{2,10},{10... | collective-permute-start | bytes 786440 | tf_op jit(solution)/shard_map/ppermute | solution.py:371
  68.6 13.0 %collective-permute-start.21 = (bf16[48,2048]{1,0:T(8,128)(2,1)S(1)}, bf16[48,2048]{1,0:T(8,128)(2,1)S(1)}, u32[]{:S(2)}, u32[]{:S(2)}) collective-permute-start(bf16[48,2048]{1,0:T(8,128)(2,1)S(1)} %get-tuple-element.130), channel_id=1, source_target_pairs={{0,16},{8,24},{16,0},{24,8},{1,17},{9,25},{17,1},{25,9},{2,18},{10... | collective-permute-start | bytes 589832 | tf_op jit(solution)/shard_map/ppermute | solution.py:375
  82.5 16.3 %collective-permute-start.23 = (bf16[128,2176]{1,0:T(8,128)(2,1)S(1)}, bf16[128,2176]{1,0:T(8,128)(2,1)S(1)}, u32[]{:S(2)}, u32[]{:S(2)}) collective-permute-start(bf16[128,2176]{1,0:T(8,128)(2,1)S(1)} %fusion.14), channel_id=1, source_target_pairs={{0,2},{1,3},{2,4},{3,5},{4,6},{5,7},{6,0},{7,1},{8,10},{9,11},{10,... | collective-permute-start | bytes 1671176 | tf_op jit(solution)/shard_map/ppermute | solution.py:379
  82.8 16.0 %collective-permute-start.25 = (bf16[64,2176]{1,0:T(8,128)(2,1)S(1)}, bf16[64,2176]{1,0:T(8,128)(2,1)S(1)}, u32[]{:S(2)}, u32[]{:S(2)}) collective-permute-start(bf16[64,2176]{1,0:T(8,128)(2,1)S(1)} %slice.63), channel_id=1, source_target_pairs={{0,8},{8,0},{16,24},{24,16},{1,9},{9,1},{17,25},{25,17},{2,10},{10... | collective-permute-start | bytes 835592 | tf_op jit(solution)/shard_map/ppermute | solution.py:371
  83.7 15.1 %collective-permute-start.26 = (bf16[112,2048]{1,0:T(8,128)(2,1)S(1)}, bf16[112,2048]{1,0:T(8,128)(2,1)S(1)}, u32[]{:S(2)}, u32[]{:S(2)}) collective-permute-start(bf16[112,2048]{1,0:T(8,128)(2,1)S(1)} %get-tuple-element.143), channel_id=1, source_target_pairs={{0,8},{8,0},{16,24},{24,16},{1,9},{9,1},{17,25},{25,17},{2,10},{10... | collective-permute-start | bytes 1376264 | tf_op jit(solution)/shard_map/ppermute | solution.py:371
  84.9 13.9 %collective-permute-start.27 = (bf16[112,2048]{1,0:T(8,128)(2,1)S(1)}, bf16[112,2048]{1,0:T(8,128)(2,1)S(1)}, u32[]{:S(2)}, u32[]{:S(2)}) collective-permute-start(bf16[112,2048]{1,0:T(8,128)(2,1)S(1)} %get-tuple-element.144), channel_id=1, source_target_pairs={{0,16},{8,24},{16,0},{24,8},{1,17},{9,25},{17,1},{25,9},{2,18},{10... | collective-permute-start | bytes 1376264 | tf_op jit(solution)/shard_map/ppermute | solution.py:375
  85.4 13.4 %collective-permute-start.24 = (bf16[48,2176]{1,0:T(8,128)(2,1)S(1)}, bf16[48,2176]{1,0:T(8,128)(2,1)S(1)}, u32[]{:S(2)}, u32[]{:S(2)}) collective-permute-start(bf16[48,2176]{1,0:T(8,128)(2,1)S(1)} %slice.62), channel_id=1, source_target_pairs={{0,16},{8,24},{16,0},{24,8},{1,17},{9,25},{17,1},{25,9},{2,18},{10... | collective-permute-start | bytes 626696 | tf_op jit(solution)/shard_map/ppermute | solution.py:375
  99.1 15.5 %collective-permute-start.28 = (bf16[112,2048]{1,0:T(8,128)(2,1)S(1)}, bf16[112,2048]{1,0:T(8,128)(2,1)S(1)}, u32[]{:S(2)}, u32[]{:S(2)}) collective-permute-start(bf16[112,2048]{1,0:T(8,128)(2,1)S(1)} %get-tuple-element.157), channel_id=1, source_target_pairs={{0,2},{1,3},{2,4},{3,5},{4,6},{5,7},{6,0},{7,1},{8,10},{9,11},{10,... | collective-permute-start | bytes 1376264 | tf_op jit(solution)/shard_map/ppermute | solution.py:379
  100.3 20.0 %collective-permute-start.34 = (bf16[112,2048]{1,0:T(8,128)(2,1)S(1)}, bf16[112,2048]{1,0:T(8,128)(2,1)S(1)}, u32[]{:S(2)}, u32[]{:S(2)}) collective-permute-start(bf16[112,2048]{1,0:T(8,128)(2,1)S(1)} %get-tuple-element.183), channel_id=1, source_target_pairs={{0,6},{1,7},{2,0},{3,1},{4,2},{5,3},{6,4},{7,5},{8,14},{9,15},{10,... | collective-permute-start | bytes 1376264 | tf_op jit(solution)/shard_map/ppermute | solution.py:379
  103.0 14.4 %collective-permute-start.29 = (bf16[112,2048]{1,0:T(8,128)(2,1)S(1)}, bf16[112,2048]{1,0:T(8,128)(2,1)S(1)}, u32[]{:S(2)}, u32[]{:S(2)}) collective-permute-start(bf16[112,2048]{1,0:T(8,128)(2,1)S(1)} %get-tuple-element.159), channel_id=1, source_target_pairs={{0,8},{8,0},{16,24},{24,16},{1,9},{9,1},{17,25},{25,17},{2,10},{10... | collective-permute-start | bytes 1376264 | tf_op jit(solution)/shard_map/ppermute | solution.py:371
  103.9 13.5 %collective-permute-start.30 = (bf16[112,2048]{1,0:T(8,128)(2,1)S(1)}, bf16[112,2048]{1,0:T(8,128)(2,1)S(1)}, u32[]{:S(2)}, u32[]{:S(2)}) collective-permute-start(bf16[112,2048]{1,0:T(8,128)(2,1)S(1)} %get-tuple-element.160), channel_id=1, source_target_pairs={{0,16},{8,24},{16,0},{24,8},{1,17},{9,25},{17,1},{25,9},{2,18},{10... | collective-permute-start | bytes 1376264 | tf_op jit(solution)/shard_map/ppermute | solution.py:375
  114.8 8.0 %collective-permute-start.33 = (bf16[64,2048]{1,0:T(8,128)(2,1)S(1)}, bf16[64,2048]{1,0:T(8,128)(2,1)S(1)}, u32[]{:S(2)}, u32[]{:S(2)}) collective-permute-start(bf16[64,2048]{1,0:T(8,128)(2,1)S(1)} %get-tuple-element.182), channel_id=1, source_target_pairs={{0,8},{8,0},{16,24},{24,16},{1,9},{9,1},{17,25},{25,17},{2,10},{10... | collective-permute-start | bytes 786440 | tf_op jit(solution)/shard_map/ppermute | solution.py:371
  115.8 28.3 %copy-start.1 = (bf16[1,111,2048]{2,1,0:T(8,128)(2,1)S(1)}, bf16[1,111,2048]{2,1,0:T(8,128)(2,1)}, u32[]{:S(2)}) copy-start(bf16[1,111,2048]{2,1,0:T(8,128)(2,1)} %param.21) | copy-start | bytes 1363972
  115.8 6.9 %collective-permute-start.32 = (bf16[48,2048]{1,0:T(8,128)(2,1)S(1)}, bf16[48,2048]{1,0:T(8,128)(2,1)S(1)}, u32[]{:S(2)}, u32[]{:S(2)}) collective-permute-start(bf16[48,2048]{1,0:T(8,128)(2,1)S(1)} %get-tuple-element.181), channel_id=1, source_target_pairs={{0,16},{8,24},{16,0},{24,8},{1,17},{9,25},{17,1},{25,9},{2,18},{10... | collective-permute-start | bytes 589832 | tf_op jit(solution)/shard_map/ppermute | solution.py:375
  117.6 12.5 %collective-permute-start.31 = (bf16[112,2048]{1,0:T(8,128)(2,1)S(1)}, bf16[112,2048]{1,0:T(8,128)(2,1)S(1)}, u32[]{:S(2)}, u32[]{:S(2)}) collective-permute-start(bf16[112,2048]{1,0:T(8,128)(2,1)S(1)} %add_convert_fusion.1), channel_id=1, source_target_pairs={{0,2},{1,3},{2,4},{3,5},{4,6},{5,7},{6,0},{7,1},{8,10},{9,11},{10,... | collective-permute-start | bytes 1376264 | tf_op jit(solution)/shard_map/ppermute | solution.py:379
  117.6 13.3 %collective-permute-start.40 = (bf16[64,2048]{1,0:T(8,128)(2,1)S(1)}, bf16[64,2048]{1,0:T(8,128)(2,1)S(1)}, u32[]{:S(2)}, u32[]{:S(2)}) collective-permute-start(bf16[64,2048]{1,0:T(8,128)(2,1)S(1)} %get-tuple-element.199), channel_id=1, source_target_pairs={{0,8},{8,0},{16,24},{24,16},{1,9},{9,1},{17,25},{25,17},{2,10},{10... | collective-permute-start | bytes 786440 | tf_op jit(solution)/shard_map/ppermute | solution.py:371
  122.8 9.2 %collective-permute-start.41 = (bf16[64,2048]{1,0:T(8,128)(2,1)S(1)}, bf16[64,2048]{1,0:T(8,128)(2,1)S(1)}, u32[]{:S(2)}, u32[]{:S(2)}) collective-permute-start(bf16[64,2048]{1,0:T(8,128)(2,1)S(1)} %get-tuple-element.200), channel_id=1, source_target_pairs={{0,16},{8,24},{16,0},{24,8},{1,17},{9,25},{17,1},{25,9},{2,18},{10... | collective-permute-start | bytes 786440 | tf_op jit(solution)/shard_map/ppermute | solution.py:375
  125.3 7.9 %collective-permute-start.37 = (bf16[48,2048]{1,0:T(8,128)(2,1)S(1)}, bf16[48,2048]{1,0:T(8,128)(2,1)S(1)}, u32[]{:S(2)}, u32[]{:S(2)}) collective-permute-start(bf16[48,2048]{1,0:T(8,128)(2,1)S(1)} %add_convert_fusion.4), channel_id=1, source_target_pairs={{0,8},{8,0},{16,24},{24,16},{1,9},{9,1},{17,25},{25,17},{2,10},{10... | collective-permute-start | bytes 589832 | tf_op jit(solution)/shard_map/ppermute | solution.py:371
  126.2 9.8 %collective-permute-start.38 = (bf16[48,2048]{1,0:T(8,128)(2,1)S(1)}, bf16[48,2048]{1,0:T(8,128)(2,1)S(1)}, u32[]{:S(2)}, u32[]{:S(2)}) collective-permute-start(bf16[48,2048]{1,0:T(8,128)(2,1)S(1)} %get-tuple-element.197), channel_id=1, source_target_pairs={{0,16},{8,24},{16,0},{24,8},{1,17},{9,25},{17,1},{25,9},{2,18},{10... | collective-permute-start | bytes 589832 | tf_op jit(solution)/shard_map/ppermute | solution.py:375
  130.1 14.0 %collective-permute-start.35 = (bf16[112,2048]{1,0:T(8,128)(2,1)S(1)}, bf16[112,2048]{1,0:T(8,128)(2,1)S(1)}, u32[]{:S(2)}, u32[]{:S(2)}) collective-permute-start(bf16[112,2048]{1,0:T(8,128)(2,1)S(1)} %get-tuple-element.189), channel_id=1, source_target_pairs={{0,8},{8,0},{16,24},{24,16},{1,9},{9,1},{17,25},{25,17},{2,10},{10... | collective-permute-start | bytes 1376264 | tf_op jit(solution)/shard_map/ppermute | solution.py:371
  130.9 13.1 %collective-permute-start.36 = (bf16[112,2048]{1,0:T(8,128)(2,1)S(1)}, bf16[112,2048]{1,0:T(8,128)(2,1)S(1)}, u32[]{:S(2)}, u32[]{:S(2)}) collective-permute-start(bf16[112,2048]{1,0:T(8,128)(2,1)S(1)} %get-tuple-element.190), channel_id=1, source_target_pairs={{0,16},{8,24},{16,0},{24,8},{1,17},{9,25},{17,1},{25,9},{2,18},{10... | collective-permute-start | bytes 1376264 | tf_op jit(solution)/shard_map/ppermute | solution.py:375
  132.1 12.0 %collective-permute-start.42 = (bf16[64,2048]{1,0:T(8,128)(2,1)S(1)}, bf16[64,2048]{1,0:T(8,128)(2,1)S(1)}, u32[]{:S(2)}, u32[]{:S(2)}) collective-permute-start(bf16[64,2048]{1,0:T(8,128)(2,1)S(1)} %add_convert_fusion.2), channel_id=1, source_target_pairs={{0,2},{1,3},{2,4},{3,5},{4,6},{5,7},{6,0},{7,1},{8,10},{9,11},{10,... | collective-permute-start | bytes 786440 | tf_op jit(solution)/shard_map/ppermute | solution.py:379
  136.1 8.0 %collective-permute-start.39 = (bf16[48,2048]{1,0:T(8,128)(2,1)S(1)}, bf16[48,2048]{1,0:T(8,128)(2,1)S(1)}, u32[]{:S(2)}, u32[]{:S(2)}) collective-permute-start(bf16[48,2048]{1,0:T(8,128)(2,1)S(1)} %add_convert_fusion.3), channel_id=1, source_target_pairs={{0,2},{1,3},{2,4},{3,5},{4,6},{5,7},{6,0},{7,1},{8,10},{9,11},{10,... | collective-permute-start | bytes 589832 | tf_op jit(solution)/shard_map/ppermute | solution.py:379

commit v16 on v14

--- a/solution.py
+++ b/solution.py
@@ -502,7 +502,10 @@
     corner_3 = spread_corner(sides_3)
     back_1 = return_sides(sums_1)
     sums_2 = apply((block_2,) + sides_2 + (risen,), (tokens,) * 4)
-    far, corner_3, back_1, sums_1, sums_2 = fence(far, corner_3, back_1, sums_1, sums_2)
+    back_y, far, back_x, corner_3, sums_1, sums_2 = fence(
+        back_1[1], far, back_1[0], corner_3, sums_1, sums_2
+    )
+    back_1 = back_x, back_y
     decodes_3 = far[tokens:]
 
     far, first = join(sums_2[3], far, sums_1[0], *back_1)

time: 145 us -> 145 us (level)
  transfers between devices with their start and end apart: 43 -> 43, of which waited for: 17 -> 18; matrix products, arithmetic and copies ran while one was open for 6% -> 6% of each run, Pallas kernels for 28% -> 28%
where the time goes in v16:
time: 145 us
  waiting for transfers between devices  46.9 us (32%)
  Pallas kernels  42.2 us (29%)
  starting transfers between devices  40.8 us (28%)
  other arithmetic  5.08 us (4%)
  matrix products  4.86 us (3%)
  local copies, waits for them, and re-layouts  4.65 us (3%)
    pallas_call x4, Pallas kernels, run_plane(): pl.pallas_call(functools.partial(plane_kernel, cap, piece_rows, block_row...  40.3 us
    ppermute x15, waiting for transfers between devices, along_y(): return lax.ppermute(value, 'kv', [(i, i ^ 2) for i in range(4)])  22.2 us
    ppermute x10, waiting for transfers between devices, around_z(): lax.ppermute(value, 'blk', [(i, (i + 2 * hops) % 8) for i in range(8)])  20.4 us
    ppermute x15, starting transfers between devices, along_y(): return lax.ppermute(value, 'kv', [(i, i ^ 2) for i in range(4)])  16.6 us
    ppermute x15, starting transfers between devices, along_x(): return lax.ppermute(value, 'kv', [(i, i ^ 1) for i in range(4)])  13.6 us
    ppermute x10, starting transfers between devices, around_z(): lax.ppermute(value, 'blk', [(i, (i + 2 * hops) % 8) for i in range(8)])  10.1 us
    unnamed x20, local copies, waits for them, and re-layouts  4.4 us
    ppermute x15, waiting for transfers between devices, along_x(): return lax.ppermute(value, 'kv', [(i, i ^ 1) for i in range(4)])  4.34 us
  transfers between devices with their start and end apart: 43, of which 18 were waited for; matrix products, arithmetic and copies ran while one was open for 6% of the time, Pallas kernels for 28%

profile of v16, /device:TPU:0, one launch (start us, length us, event | category | flops | bytes accessed | tf_op | source)
XLA Modules:
  0.0 144.8 jit_solution(2166805972171409082)
XLA Ops:
  0.0 1.0 copy-done
  1.0 0.9 copy-done.2
  1.9 0.7 copy-done.4
  2.6 0.7 copy-done.6
  3.3 0.8 prepare.2.refs_1_
  4.1 3.0 %collective-permute-start = (bf16[112,2176]{1,0:T(8,128)(2,1)S(1)}, bf16[112,2176]{1,0:T(8,128)(2,1)S(1)}, u32[]{:S(2)}, u32[]{:S(2)}) collective-permute-start(bf16[112,2176]{1,0:T(8,128)(2,1)S(1)} %prepare.2.refs_1_), channel_id=1, source_target_pairs={{0,8},{8,0},{16,24},{24,16},{1,9},{9,1},{17,25},{25,17},{2,10},{10... | collective-permute-start | bytes 1462280 | tf_op jit(solution)/shard_map/ppermute | solution.py:371
  7.1 1.5 %collective-permute-start.1 = (bf16[112,2176]{1,0:T(8,128)(2,1)S(1)}, bf16[112,2176]{1,0:T(8,128)(2,1)S(1)}, u32[]{:S(2)}, u32[]{:S(2)}) collective-permute-start(bf16[112,2176]{1,0:T(8,128)(2,1)S(1)} %prepare.2.refs_1_), channel_id=1, source_target_pairs={{0,16},{8,24},{16,0},{24,8},{1,17},{9,25},{17,1},{25,9},{2,18},{10... | collective-permute-start | bytes 1462280 | tf_op jit(solution)/shard_map/ppermute | solution.py:375
  8.6 1.6 %collective-permute-start.2 = (bf16[112,2176]{1,0:T(8,128)(2,1)S(1)}, bf16[112,2176]{1,0:T(8,128)(2,1)S(1)}, u32[]{:S(2)}, u32[]{:S(2)}) collective-permute-start(bf16[112,2176]{1,0:T(8,128)(2,1)S(1)} %prepare.2.refs_1_), channel_id=1, source_target_pairs={{0,2},{1,3},{2,4},{3,5},{4,6},{5,7},{6,0},{7,1},{8,10},{9,11},{10,... | collective-permute-start | bytes 1462280 | tf_op jit(solution)/shard_map/ppermute | solution.py:379
  10.7 0.7 minimum_subtract_fusion
  11.5 0.9 broadcast_in_dim.76
  12.4 1.0 convert_reduce_fusion
  13.4 3.5 %fusion.36 = (f32[4,8]{1,0:T(4,128)S(1)}, f32[4,8,4096]{2,1,0:T(8,128)S(1)}) fusion(bf16[4,4096,1,128]{3,1,2,0:T(8,128)(2,1)} %param.15, bf16[1,4,8,128]{3,1,2,0:T(4,128)(2,1)} %bitcast.51, pred[4,4096]{1,0:T(4,128)(4,1)S(1)} %iota_compare_fusion.2), kind=kOutput, calls=%fused_computation.61 | convolution fusion | flops 33947616 | bytes 4743296 | tf_op jit(solution)/shard_map/rgd,rjd->rgj/dot_general | solution.py:27
  17.2 0.7 fusion.11
  18.0 1.1 copy-done.8
  19.1 0.7 convolution_add_fusion
  20.4 2.4 %collective-permute-done.2.refs_1_ = bf16[112,2176]{1,0:T(8,128)(2,1)S(1)} collective-permute-done((bf16[112,2176]{1,0:T(8,128)(2,1)S(1)}, bf16[112,2176]{1,0:T(8,128)(2,1)S(1)}, u32[]{:S(2)}, u32[]{:S(2)}) %collective-permute-start.2) | collective-permute-done | bytes 487456 | tf_op jit(solution)/shard_map/ppermute | solution.py:379
  24.5 4.8 %collective-permute-done.4.refs_4_ = bf16[48,2176]{1,0:T(8,128)(2,1)S(1)} collective-permute-done((bf16[48,2176]{1,0:T(8,128)(2,1)S(1)}, bf16[48,2176]{1,0:T(8,128)(2,1)S(1)}, u32[]{:S(2)}, u32[]{:S(2)}) %collective-permute-start.4) | collective-permute-done | bytes 208928 | tf_op jit(solution)/shard_map/ppermute | solution.py:375
  29.3 0.8 collective-permute-done.5.refs_5_
  30.7 1.5 %collective-permute-start.10 = (bf16[112,2176]{1,0:T(8,128)(2,1)S(1)}, bf16[112,2176]{1,0:T(8,128)(2,1)S(1)}, u32[]{:S(2)}, u32[]{:S(2)}) collective-permute-start(bf16[112,2176]{1,0:T(8,128)(2,1)S(1)} %collective-permute-done.2.refs_1_), channel_id=1, source_target_pairs={{0,16},{8,24},{16,0},{24,8},{1,17},{9,25},{17,1},{25,9},{2,18},{10... | collective-permute-start | bytes 1462280 | tf_op jit(solution)/shard_map/ppermute | solution.py:375
  32.2 1.3 collective-permute-start.11
  33.5 0.8 collective-permute-start.9
  34.3 0.7 collective-permute-done.8
  35.7 9.3 %collective-permute-done.10.refs_3_ = bf16[112,2176]{1,0:T(8,128)(2,1)S(1)} collective-permute-done((bf16[112,2176]{1,0:T(8,128)(2,1)S(1)}, bf16[112,2176]{1,0:T(8,128)(2,1)S(1)}, u32[]{:S(2)}, u32[]{:S(2)}) %collective-permute-start.10) | collective-permute-done | bytes 487456 | tf_op jit(solution)/shard_map/ppermute | solution.py:375
  45.0 1.9 %collective-permute-done.11.refs_1_ = bf16[112,2176]{1,0:T(8,128)(2,1)S(1)} collective-permute-done((bf16[112,2176]{1,0:T(8,128)(2,1)S(1)}, bf16[112,2176]{1,0:T(8,128)(2,1)S(1)}, u32[]{:S(2)}, u32[]{:S(2)}) %collective-permute-start.11) | collective-permute-done | bytes 487456 | tf_op jit(solution)/shard_map/ppermute | solution.py:379
  47.0 0.7 collective-permute-start.15
  47.7 0.9 collective-permute-start.16
  48.7 0.9 collective-permute-start.17
  49.6 0.9 collective-permute-start.14
  50.5 1.6 %collective-permute-start.13 = (bf16[48,2176]{1,0:T(8,128)(2,1)S(1)}, bf16[48,2176]{1,0:T(8,128)(2,1)S(1)}, u32[]{:S(2)}, u32[]{:S(2)}) collective-permute-start(bf16[48,2176]{1,0:T(8,128)(2,1)S(1)} %slice.57), channel_id=1, source_target_pairs={{0,16},{8,24},{16,0},{24,8},{1,17},{9,25},{17,1},{25,9},{2,18},{10... | collective-permute-start | bytes 626696 | tf_op jit(solution)/shard_map/ppermute | solution.py:375
  52.1 10.1 %plane.4 = (bf16[112,2048]{1,0:T(8,128)(2,1)S(1)}, bf16[112,2048]{1,0:T(8,128)(2,1)S(1)}, bf16[112,2048]{1,0:T(8,128)(2,1)S(1)}, bf16[48,2048]{1,0:T(8,128)(2,1)S(1)}, bf16[64,2048]{1,0:T(8,128)(2,1)S(1)}) custom-call(s32[3]{0:T(128)S(1)} %pad_add_fusion.refs_0_, bf16[112,2176]{1,0:T(8,128)(2,1)S(1)} %prepare.2.refs_1_, ...), custom_call_target="tpu_custom_call" | custom-call | flops 8455716864 | bytes 25165824 | tf_op jit(solution)/shard_map/plane/pallas_call | solution.py:277
  62.2 1.8 %collective-permute-done.13.refs_4_ = bf16[48,2176]{1,0:T(8,128)(2,1)S(1)} collective-permute-done((bf16[48,2176]{1,0:T(8,128)(2,1)S(1)}, bf16[48,2176]{1,0:T(8,128)(2,1)S(1)}, u32[]{:S(2)}, u32[]{:S(2)}) %collective-permute-start.13) | collective-permute-done | bytes 208928 | tf_op jit(solution)/shard_map/ppermute | solution.py:375
  64.0 1.1 collective-permute-done.14.refs_5_
  65.2 0.8 collective-permute-start.18
  65.9 1.0 collective-permute-start.19
  66.9 0.7 collective-permute-start.20
  67.7 0.9 collective-permute-start.22
  68.5 1.5 %collective-permute-start.21 = (bf16[48,2048]{1,0:T(8,128)(2,1)S(1)}, bf16[48,2048]{1,0:T(8,128)(2,1)S(1)}, u32[]{:S(2)}, u32[]{:S(2)}) collective-permute-start(bf16[48,2048]{1,0:T(8,128)(2,1)S(1)} %get-tuple-element.130), channel_id=1, source_target_pairs={{0,16},{8,24},{16,0},{24,8},{1,17},{9,25},{17,1},{25,9},{2,18},{10... | collective-permute-start | bytes 589832 | tf_op jit(solution)/shard_map/ppermute | solution.py:375
  70.1 10.1 %plane.5 = (bf16[112,2048]{1,0:T(8,128)(2,1)S(1)}, bf16[112,2048]{1,0:T(8,128)(2,1)S(1)}, bf16[112,2048]{1,0:T(8,128)(2,1)S(1)}, bf16[112,2048]{1,0:T(8,128)(2,1)S(1)}) custom-call(s32[3]{0:T(128)S(1)} %pad_add_fusion.refs_0_, bf16[112,2176]{1,0:T(8,128)(2,1)S(1)} %collective-permute-done.2.refs_1_, bf16[112,2176]{1,0:T(8,128)(2,1)S(1)} %collective-permute-done.9.refs_2_, ...), custom_call_target="tpu_custom_call" | custom-call | flops 8455716864 | bytes 25165824 | tf_op jit(solution)/shard_map/plane/pallas_call | solution.py:277
  80.1 0.9 collective-permute-done.21.passed_0_ref
  81.1 1.0 collective-permute-done.22.passed_1_ref
  82.6 0.9 collective-permute-start.27
  83.5 0.9 collective-permute-start.23
  84.3 0.9 collective-permute-start.25
  85.2 1.6 %collective-permute-start.26 = (bf16[48,2176]{1,0:T(8,128)(2,1)S(1)}, bf16[48,2176]{1,0:T(8,128)(2,1)S(1)}, u32[]{:S(2)}, u32[]{:S(2)}) collective-permute-start(bf16[48,2176]{1,0:T(8,128)(2,1)S(1)} %slice.62), channel_id=1, source_target_pairs={{0,16},{8,24},{16,0},{24,8},{1,17},{9,25},{17,1},{25,9},{2,18},{10... | collective-permute-start | bytes 626696 | tf_op jit(solution)/shard_map/ppermute | solution.py:375
  86.8 10.1 %plane.6 = (bf16[112,2048]{1,0:T(8,128)(2,1)S(1)}, bf16[112,2048]{1,0:T(8,128)(2,1)S(1)}, bf16[112,2048]{1,0:T(8,128)(2,1)S(1)}, bf16[112,2048]{1,0:T(8,128)(2,1)S(1)}) custom-call(s32[3]{0:T(128)S(1)} %pad_add_fusion.refs_0_, bf16[112,2176]{1,0:T(8,128)(2,1)S(1)} %collective-permute-done.11.refs_1_, bf16[112,2176]{1,0:T(8,128)(2,1)S(1)} %collective-permute-done.15.refs_2_, ...), custom_call_target="tpu_custom_call" | custom-call | flops 8455716864 | bytes 25165824 | tf_op jit(solution)/shard_map/plane/pallas_call | solution.py:277
  97.1 1.1 collective-permute-done.25.x_ref
  98.4 2.3 %collective-permute-start.28 = (bf16[112,2048]{1,0:T(8,128)(2,1)S(1)}, bf16[112,2048]{1,0:T(8,128)(2,1)S(1)}, u32[]{:S(2)}, u32[]{:S(2)}) collective-permute-start(bf16[112,2048]{1,0:T(8,128)(2,1)S(1)} %get-tuple-element.157), channel_id=1, source_target_pairs={{0,2},{1,3},{2,4},{3,5},{4,6},{5,7},{6,0},{7,1},{8,10},{9,11},{10,... | collective-permute-start | bytes 1376264 | tf_op jit(solution)/shard_map/ppermute | solution.py:379
  100.8 1.6 %collective-permute-start.34 = (bf16[112,2048]{1,0:T(8,128)(2,1)S(1)}, bf16[112,2048]{1,0:T(8,128)(2,1)S(1)}, u32[]{:S(2)}, u32[]{:S(2)}) collective-permute-start(bf16[112,2048]{1,0:T(8,128)(2,1)S(1)} %get-tuple-element.183), channel_id=1, source_target_pairs={{0,6},{1,7},{2,0},{3,1},{4,2},{5,3},{6,4},{7,5},{8,14},{9,15},{10,... | collective-permute-start | bytes 1376264 | tf_op jit(solution)/shard_map/ppermute | solution.py:379
  102.3 0.7 collective-permute-start.29
  103.1 0.9 collective-permute-start.30
  103.9 10.1 %plane.7 = (bf16[112,2048]{1,0:T(8,128)(2,1)S(1)}, bf16[48,2048]{1,0:T(8,128)(2,1)S(1)}, bf16[64,2048]{1,0:T(8,128)(2,1)S(1)}, bf16[48,2048]{1,0:T(8,128)(2,1)S(...) custom-call(s32[3]{0:T(128)S(1)} %pad_add_fusion.refs_0_, ...), custom_call_target="tpu_custom_call" | custom-call | flops 8455716864 | bytes 25165824 | tf_op jit(solution)/shard_map/plane/pallas_call | solution.py:277
  114.2 1.0 collective-permute-start.33
  115.2 1.5 %collective-permute-start.32 = (bf16[48,2048]{1,0:T(8,128)(2,1)S(1)}, bf16[48,2048]{1,0:T(8,128)(2,1)S(1)}, u32[]{:S(2)}, u32[]{:S(2)}) collective-permute-start(bf16[48,2048]{1,0:T(8,128)(2,1)S(1)} %get-tuple-element.181), channel_id=1, source_target_pairs={{0,16},{8,24},{16,0},{24,8},{1,17},{9,25},{17,1},{25,9},{2,18},{10... | collective-permute-start | bytes 589832 | tf_op jit(solution)/shard_map/ppermute | solution.py:375
  117.8 3.8 %collective-permute-done.34 = bf16[112,2048]{1,0:T(8,128)(2,1)S(1)} collective-permute-done((bf16[112,2048]{1,0:T(8,128)(2,1)S(1)}, bf16[112,2048]{1,0:T(8,128)(2,1)S(1)}, u32[]{:S(2)}, u32[]{:S(2)}) %collective-permute-start.34) | collective-permute-done | bytes 458784 | tf_op jit(solution)/shard_map/ppermute | solution.py:379
  121.7 0.8 collective-permute-start.41
  122.6 0.8 collective-permute-start.37
  123.3 0.9 collective-permute-start.38
  124.2 4.4 %collective-permute-done.31 = bf16[112,2048]{1,0:T(8,128)(2,1)S(1)} collective-permute-done((bf16[112,2048]{1,0:T(8,128)(2,1)S(1)}, bf16[112,2048]{1,0:T(8,128)(2,1)S(1)}, u32[]{:S(2)}, u32[]{:S(2)}) %collective-permute-start.31) | collective-permute-done | bytes 458784 | tf_op jit(solution)/shard_map/ppermute | solution.py:379
  128.7 0.7 collective-permute-start.35
  129.4 0.9 collective-permute-start.36
  130.3 0.6 collective-permute-done.41
  131.5 3.7 %collective-permute-done.38 = bf16[48,2048]{1,0:T(8,128)(2,1)S(1)} collective-permute-done((bf16[48,2048]{1,0:T(8,128)(2,1)S(1)}, bf16[48,2048]{1,0:T(8,128)(2,1)S(1)}, u32[]{:S(2)}, u32[]{:S(2)}) %collective-permute-start.38) | collective-permute-done | bytes 196640 | tf_op jit(solution)/shard_map/ppermute | solution.py:375
  135.7 7.9 %collective-permute-done.39 = bf16[48,2048]{1,0:T(8,128)(2,1)S(1)} collective-permute-done((bf16[48,2048]{1,0:T(8,128)(2,1)S(1)}, bf16[48,2048]{1,0:T(8,128)(2,1)S(1)}, u32[]{:S(2)}, u32[]{:S(2)}) %collective-permute-start.39) | collective-permute-done | bytes 196640 | tf_op jit(solution)/shard_map/ppermute | solution.py:379
  143.6 1.2 fusion.15
  (92 shorter events, 8.2 us)
Async XLA Ops:
  0.0 16.9 %copy-start.9 = (f32[8]{0:T(128)S(1)}, f32[8]{0:T(128)}, u32[]{:S(2)}) copy-start(f32[8]{0:T(128)} %param.18) | copy-start | bytes 100
  0.0 1.0 copy-start
  1.0 0.9 copy-start.2
  1.9 0.7 copy-start.4
  2.6 0.7 copy-start.6
  4.1 15.7 %collective-permute-start = (bf16[112,2176]{1,0:T(8,128)(2,1)S(1)}, bf16[112,2176]{1,0:T(8,128)(2,1)S(1)}, u32[]{:S(2)}, u32[]{:S(2)}) collective-permute-start(bf16[112,2176]{1,0:T(8,128)(2,1)S(1)} %prepare.2.refs_1_), channel_id=1, source_target_pairs={{0,8},{8,0},{16,24},{24,16},{1,9},{9,1},{17,25},{25,17},{2,10},{10... | collective-permute-start | bytes 1462280 | tf_op jit(solution)/shard_map/ppermute | solution.py:371
  7.1 13.3 %collective-permute-start.1 = (bf16[112,2176]{1,0:T(8,128)(2,1)S(1)}, bf16[112,2176]{1,0:T(8,128)(2,1)S(1)}, u32[]{:S(2)}, u32[]{:S(2)}) collective-permute-start(bf16[112,2176]{1,0:T(8,128)(2,1)S(1)} %prepare.2.refs_1_), channel_id=1, source_target_pairs={{0,16},{8,24},{16,0},{24,8},{1,17},{9,25},{17,1},{25,9},{2,18},{10... | collective-permute-start | bytes 1462280 | tf_op jit(solution)/shard_map/ppermute | solution.py:375
  8.6 14.2 %collective-permute-start.2 = (bf16[112,2176]{1,0:T(8,128)(2,1)S(1)}, bf16[112,2176]{1,0:T(8,128)(2,1)S(1)}, u32[]{:S(2)}, u32[]{:S(2)}) collective-permute-start(bf16[112,2176]{1,0:T(8,128)(2,1)S(1)} %prepare.2.refs_1_), channel_id=1, source_target_pairs={{0,2},{1,3},{2,4},{3,5},{4,6},{5,7},{6,0},{7,1},{8,10},{9,11},{10,... | collective-permute-start | bytes 1462280 | tf_op jit(solution)/shard_map/ppermute | solution.py:379
  10.2 12.6 %collective-permute-start.3 = (bf16[2048,768]{1,0:T(8,128)(2,1)}, bf16[2048,768]{1,0:T(8,128)(2,1)}, u32[]{:S(2)}, u32[]{:S(2)}) collective-permute-start(bf16[2048,768]{1,0:T(8,128)(2,1)} %bitcast.53), channel_id=1, source_target_pairs={{0,1},{1,0},{2,3},{3,2},{4,5},{5,4},{6,7},{7,6},{8,9},{9,8},{10,11... | collective-permute-start | bytes 9437192 | tf_op jit(solution)/shard_map/ppermute | solution.py:383
  10.2 14.3 %collective-permute-start.7 = (bf16[2048,768]{1,0:T(8,128)(2,1)}, bf16[2048,768]{1,0:T(8,128)(2,1)}, u32[]{:S(2)}, u32[]{:S(2)}) collective-permute-start(bf16[2048,768]{1,0:T(8,128)(2,1)} %bitcast.58), channel_id=1, source_target_pairs={{0,1},{1,0},{2,3},{3,2},{4,5},{5,4},{6,7},{7,6},{8,9},{9,8},{10,11... | collective-permute-start | bytes 9437192 | tf_op jit(solution)/shard_map/ppermute | solution.py:383
  11.5 5.7 %copy-start.7 = (bf16[4,4096,1,128]{3,1,2,0:T(8,128)(2,1)S(1)}, bf16[4,4096,1,128]{3,1,2,0:T(8,128)(2,1)}, u32[]{:S(2)}) copy-start(bf16[4,4096,1,128]{3,1,2,0:T(8,128)(2,1)} %param.16) | copy-start | bytes 12582916
  16.9 2.2 %copy-start.8 = (bf16[1024,2048]{1,0:T(8,128)(2,1)S(1)}, bf16[1024,2048]{1,0:T(8,128)(2,1)}, u32[]{:S(2)}) copy-start(bf16[1024,2048]{1,0:T(8,128)(2,1)} %param.19) | copy-start | bytes 12582916
  17.9 17.2 %copy-start.3 = (bf16[2048,32]{0,1:T(8,128)(2,1)S(1)}, bf16[2048,32]{0,1:T(8,128)(2,1)}, u32[]{:S(2)}) copy-start(bf16[2048,32]{0,1:T(8,128)(2,1)} %param.23) | copy-start | bytes 393220
  18.0 17.2 %copy-start.5 = (f32[2048]{0:T(1024)S(1)}, f32[2048]{0:T(1024)}, u32[]{:S(2)}) copy-start(f32[2048]{0:T(1024)} %param.22) | copy-start | bytes 24580
  19.8 4.6 %collective-permute-start.6 = (f32[8,2048]{1,0:T(8,128)S(1)}, f32[8,2048]{1,0:T(8,128)S(1)}, u32[]{:S(2)}, u32[]{:S(2)}) collective-permute-start(f32[8,2048]{1,0:T(8,128)S(1)} %pad_maximum_fusion.2), channel_id=1, source_target_pairs={{0,8},{8,0},{16,24},{24,16},{1,9},{9,1},{17,25},{25,17},{2,10},{10... | collective-permute-start | bytes 196616 | tf_op jit(solution)/shard_map/ppermute | solution.py:371
  22.8 7.3 %collective-permute-start.5 = (bf16[64,2176]{1,0:T(8,128)(2,1)S(1)}, bf16[64,2176]{1,0:T(8,128)(2,1)S(1)}, u32[]{:S(2)}, u32[]{:S(2)}) collective-permute-start(bf16[64,2176]{1,0:T(8,128)(2,1)S(1)} %slice.53), channel_id=1, source_target_pairs={{0,8},{8,0},{16,24},{24,16},{1,9},{9,1},{17,25},{25,17},{2,10},{10... | collective-permute-start | bytes 835592 | tf_op jit(solution)/shard_map/ppermute | solution.py:371
  23.4 5.9 %collective-permute-start.4 = (bf16[48,2176]{1,0:T(8,128)(2,1)S(1)}, bf16[48,2176]{1,0:T(8,128)(2,1)S(1)}, u32[]{:S(2)}, u32[]{:S(2)}) collective-permute-start(bf16[48,2176]{1,0:T(8,128)(2,1)S(1)} %slice.52), channel_id=1, source_target_pairs={{0,16},{8,24},{16,0},{24,8},{1,17},{9,25},{17,1},{25,9},{2,18},{10... | collective-permute-start | bytes 626696 | tf_op jit(solution)/shard_map/ppermute | solution.py:375
  30.1 16.9 %collective-permute-start.12 = (bf16[768,2048]{1,0:T(8,128)(2,1)}, bf16[768,2048]{1,0:T(8,128)(2,1)}, u32[]{:S(2)}, u32[]{:S(2)}) collective-permute-start(bf16[768,2048]{1,0:T(8,128)(2,1)} %bitcast.11.refs_9_.refs_7_), channel_id=1, source_target_pairs={{0,1},{1,0},{2,3},{3,2},{4,5},{5,4},{6,7},{7,6},{8,9},{9,8},{10,11... | collective-permute-start | bytes 9437192 | tf_op jit(solution)/shard_map/ppermute | solution.py:383
  30.1 4.9 %collective-permute-start.8 = (f32[8,2048]{1,0:T(8,128)S(1)}, f32[8,2048]{1,0:T(8,128)S(1)}, u32[]{:S(2)}, u32[]{:S(2)}) collective-permute-start(f32[8,2048]{1,0:T(8,128)S(1)} %fusion.35), channel_id=1, source_target_pairs={{0,16},{8,24},{16,0},{24,8},{1,17},{9,25},{17,1},{25,9},{2,18},{10... | collective-permute-start | bytes 196616 | tf_op jit(solution)/shard_map/ppermute | solution.py:375
  30.7 14.4 %collective-permute-start.10 = (bf16[112,2176]{1,0:T(8,128)(2,1)S(1)}, bf16[112,2176]{1,0:T(8,128)(2,1)S(1)}, u32[]{:S(2)}, u32[]{:S(2)}) collective-permute-start(bf16[112,2176]{1,0:T(8,128)(2,1)S(1)} %collective-permute-done.2.refs_1_), channel_id=1, source_target_pairs={{0,16},{8,24},{16,0},{24,8},{1,17},{9,25},{17,1},{25,9},{2,18},{10... | collective-permute-start | bytes 1462280 | tf_op jit(solution)/shard_map/ppermute | solution.py:375
  32.2 14.8 %collective-permute-start.11 = (bf16[112,2176]{1,0:T(8,128)(2,1)S(1)}, bf16[112,2176]{1,0:T(8,128)(2,1)S(1)}, u32[]{:S(2)}, u32[]{:S(2)}) collective-permute-start(bf16[112,2176]{1,0:T(8,128)(2,1)S(1)} %collective-permute-done.2.refs_1_), channel_id=1, source_target_pairs={{0,2},{1,3},{2,4},{3,5},{4,6},{5,7},{6,0},{7,1},{8,10},{9,11},{10,... | collective-permute-start | bytes 1462280 | tf_op jit(solution)/shard_map/ppermute | solution.py:379
  33.5 13.5 %collective-permute-start.9 = (bf16[112,2176]{1,0:T(8,128)(2,1)S(1)}, bf16[112,2176]{1,0:T(8,128)(2,1)S(1)}, u32[]{:S(2)}, u32[]{:S(2)}) collective-permute-start(bf16[112,2176]{1,0:T(8,128)(2,1)S(1)} %collective-permute-done.2.refs_1_), channel_id=1, source_target_pairs={{0,8},{8,0},{16,24},{24,16},{1,9},{9,1},{17,25},{25,17},{2,10},{10... | collective-permute-start | bytes 1462280 | tf_op jit(solution)/shard_map/ppermute | solution.py:371
  47.0 18.1 %collective-permute-start.15 = (bf16[112,2176]{1,0:T(8,128)(2,1)S(1)}, bf16[112,2176]{1,0:T(8,128)(2,1)S(1)}, u32[]{:S(2)}, u32[]{:S(2)}) collective-permute-start(bf16[112,2176]{1,0:T(8,128)(2,1)S(1)} %collective-permute-done.11.refs_1_), channel_id=1, source_target_pairs={{0,8},{8,0},{16,24},{24,16},{1,9},{9,1},{17,25},{25,17},{2,10},{10... | collective-permute-start | bytes 1462280 | tf_op jit(solution)/shard_map/ppermute | solution.py:371
  47.7 17.4 %collective-permute-start.16 = (bf16[112,2176]{1,0:T(8,128)(2,1)S(1)}, bf16[112,2176]{1,0:T(8,128)(2,1)S(1)}, u32[]{:S(2)}, u32[]{:S(2)}) collective-permute-start(bf16[112,2176]{1,0:T(8,128)(2,1)S(1)} %collective-permute-done.11.refs_1_), channel_id=1, source_target_pairs={{0,16},{8,24},{16,0},{24,8},{1,17},{9,25},{17,1},{25,9},{2,18},{10... | collective-permute-start | bytes 1462280 | tf_op jit(solution)/shard_map/ppermute | solution.py:375
  48.7 16.4 %collective-permute-start.17 = (bf16[128,2176]{1,0:T(8,128)(2,1)S(1)}, bf16[128,2176]{1,0:T(8,128)(2,1)S(1)}, u32[]{:S(2)}, u32[]{:S(2)}) collective-permute-start(bf16[128,2176]{1,0:T(8,128)(2,1)S(1)} %pad_maximum_fusion), channel_id=1, source_target_pairs={{0,2},{1,3},{2,4},{3,5},{4,6},{5,7},{6,0},{7,1},{8,10},{9,11},{10,... | collective-permute-start | bytes 1671176 | tf_op jit(solution)/shard_map/ppermute | solution.py:379
  49.6 15.5 %collective-permute-start.14 = (bf16[64,2176]{1,0:T(8,128)(2,1)S(1)}, bf16[64,2176]{1,0:T(8,128)(2,1)S(1)}, u32[]{:S(2)}, u32[]{:S(2)}) collective-permute-start(bf16[64,2176]{1,0:T(8,128)(2,1)S(1)} %slice.58), channel_id=1, source_target_pairs={{0,8},{8,0},{16,24},{24,16},{1,9},{9,1},{17,25},{25,17},{2,10},{10... | collective-permute-start | bytes 835592 | tf_op jit(solution)/shard_map/ppermute | solution.py:371
  50.5 13.5 %collective-permute-start.13 = (bf16[48,2176]{1,0:T(8,128)(2,1)S(1)}, bf16[48,2176]{1,0:T(8,128)(2,1)S(1)}, u32[]{:S(2)}, u32[]{:S(2)}) collective-permute-start(bf16[48,2176]{1,0:T(8,128)(2,1)S(1)} %slice.57), channel_id=1, source_target_pairs={{0,16},{8,24},{16,0},{24,8},{1,17},{9,25},{17,1},{25,9},{2,18},{10... | collective-permute-start | bytes 626696 | tf_op jit(solution)/shard_map/ppermute | solution.py:375
  65.2 16.9 %collective-permute-start.18 = (bf16[112,2176]{1,0:T(8,128)(2,1)S(1)}, bf16[112,2176]{1,0:T(8,128)(2,1)S(1)}, u32[]{:S(2)}, u32[]{:S(2)}) collective-permute-start(bf16[112,2176]{1,0:T(8,128)(2,1)S(1)} %slice.59.refs_1_), channel_id=1, source_target_pairs={{0,8},{8,0},{16,24},{24,16},{1,9},{9,1},{17,25},{25,17},{2,10},{10... | collective-permute-start | bytes 1462280 | tf_op jit(solution)/shard_map/ppermute | solution.py:371
  65.9 16.1 %collective-permute-start.19 = (bf16[112,2176]{1,0:T(8,128)(2,1)S(1)}, bf16[112,2176]{1,0:T(8,128)(2,1)S(1)}, u32[]{:S(2)}, u32[]{:S(2)}) collective-permute-start(bf16[112,2176]{1,0:T(8,128)(2,1)S(1)} %slice.59.refs_1_), channel_id=1, source_target_pairs={{0,16},{8,24},{16,0},{24,8},{1,17},{9,25},{17,1},{25,9},{2,18},{10... | collective-permute-start | bytes 1462280 | tf_op jit(solution)/shard_map/ppermute | solution.py:375
  66.9 15.1 %collective-permute-start.20 = (bf16[128,2176]{1,0:T(8,128)(2,1)S(1)}, bf16[128,2176]{1,0:T(8,128)(2,1)S(1)}, u32[]{:S(2)}, u32[]{:S(2)}) collective-permute-start(bf16[128,2176]{1,0:T(8,128)(2,1)S(1)} %pad_maximum_fusion.1), channel_id=1, source_target_pairs={{0,2},{1,3},{2,4},{3,5},{4,6},{5,7},{6,0},{7,1},{8,10},{9,11},{10,... | collective-permute-start | bytes 1671176 | tf_op jit(solution)/shard_map/ppermute | solution.py:379
  67.7 14.4 %collective-permute-start.22 = (bf16[64,2048]{1,0:T(8,128)(2,1)S(1)}, bf16[64,2048]{1,0:T(8,128)(2,1)S(1)}, u32[]{:S(2)}, u32[]{:S(2)}) collective-permute-start(bf16[64,2048]{1,0:T(8,128)(2,1)S(1)} %get-tuple-element.131), channel_id=1, source_target_pairs={{0,8},{8,0},{16,24},{24,16},{1,9},{9,1},{17,25},{25,17},{2,10},{10... | collective-permute-start | bytes 786440 | tf_op jit(solution)/shard_map/ppermute | solution.py:371
  68.5 12.5 %collective-permute-start.21 = (bf16[48,2048]{1,0:T(8,128)(2,1)S(1)}, bf16[48,2048]{1,0:T(8,128)(2,1)S(1)}, u32[]{:S(2)}, u32[]{:S(2)}) collective-permute-start(bf16[48,2048]{1,0:T(8,128)(2,1)S(1)} %get-tuple-element.130), channel_id=1, source_target_pairs={{0,16},{8,24},{16,0},{24,8},{1,17},{9,25},{17,1},{25,9},{2,18},{10... | collective-permute-start | bytes 589832 | tf_op jit(solution)/shard_map/ppermute | solution.py:375
  82.1 16.0 %collective-permute-start.24 = (bf16[128,2176]{1,0:T(8,128)(2,1)S(1)}, bf16[128,2176]{1,0:T(8,128)(2,1)S(1)}, u32[]{:S(2)}, u32[]{:S(2)}) collective-permute-start(bf16[128,2176]{1,0:T(8,128)(2,1)S(1)} %fusion.14), channel_id=1, source_target_pairs={{0,2},{1,3},{2,4},{3,5},{4,6},{5,7},{6,0},{7,1},{8,10},{9,11},{10,... | collective-permute-start | bytes 1671176 | tf_op jit(solution)/shard_map/ppermute | solution.py:379
  82.6 14.5 %collective-permute-start.27 = (bf16[64,2176]{1,0:T(8,128)(2,1)S(1)}, bf16[64,2176]{1,0:T(8,128)(2,1)S(1)}, u32[]{:S(2)}, u32[]{:S(2)}) collective-permute-start(bf16[64,2176]{1,0:T(8,128)(2,1)S(1)} %slice.63), channel_id=1, source_target_pairs={{0,8},{8,0},{16,24},{24,16},{1,9},{9,1},{17,25},{25,17},{2,10},{10... | collective-permute-start | bytes 835592 | tf_op jit(solution)/shard_map/ppermute | solution.py:371
  83.5 13.6 %collective-permute-start.23 = (bf16[112,2048]{1,0:T(8,128)(2,1)S(1)}, bf16[112,2048]{1,0:T(8,128)(2,1)S(1)}, u32[]{:S(2)}, u32[]{:S(2)}) collective-permute-start(bf16[112,2048]{1,0:T(8,128)(2,1)S(1)} %get-tuple-element.139), channel_id=1, source_target_pairs={{0,16},{8,24},{16,0},{24,8},{1,17},{9,25},{17,1},{25,9},{2,18},{10... | collective-permute-start | bytes 1376264 | tf_op jit(solution)/shard_map/ppermute | solution.py:375
  84.3 13.8 %collective-permute-start.25 = (bf16[112,2048]{1,0:T(8,128)(2,1)S(1)}, bf16[112,2048]{1,0:T(8,128)(2,1)S(1)}, u32[]{:S(2)}, u32[]{:S(2)}) collective-permute-start(bf16[112,2048]{1,0:T(8,128)(2,1)S(1)} %get-tuple-element.142), channel_id=1, source_target_pairs={{0,8},{8,0},{16,24},{24,16},{1,9},{9,1},{17,25},{25,17},{2,10},{10... | collective-permute-start | bytes 1376264 | tf_op jit(solution)/shard_map/ppermute | solution.py:371
  85.2 11.9 %collective-permute-start.26 = (bf16[48,2176]{1,0:T(8,128)(2,1)S(1)}, bf16[48,2176]{1,0:T(8,128)(2,1)S(1)}, u32[]{:S(2)}, u32[]{:S(2)}) collective-permute-start(bf16[48,2176]{1,0:T(8,128)(2,1)S(1)} %slice.62), channel_id=1, source_target_pairs={{0,16},{8,24},{16,0},{24,8},{1,17},{9,25},{17,1},{25,9},{2,18},{10... | collective-permute-start | bytes 626696 | tf_op jit(solution)/shard_map/ppermute | solution.py:375
  98.4 15.6 %collective-permute-start.28 = (bf16[112,2048]{1,0:T(8,128)(2,1)S(1)}, bf16[112,2048]{1,0:T(8,128)(2,1)S(1)}, u32[]{:S(2)}, u32[]{:S(2)}) collective-permute-start(bf16[112,2048]{1,0:T(8,128)(2,1)S(1)} %get-tuple-element.157), channel_id=1, source_target_pairs={{0,2},{1,3},{2,4},{3,5},{4,6},{5,7},{6,0},{7,1},{8,10},{9,11},{10,... | collective-permute-start | bytes 1376264 | tf_op jit(solution)/shard_map/ppermute | solution.py:379
  100.8 20.8 %collective-permute-start.34 = (bf16[112,2048]{1,0:T(8,128)(2,1)S(1)}, bf16[112,2048]{1,0:T(8,128)(2,1)S(1)}, u32[]{:S(2)}, u32[]{:S(2)}) collective-permute-start(bf16[112,2048]{1,0:T(8,128)(2,1)S(1)} %get-tuple-element.183), channel_id=1, source_target_pairs={{0,6},{1,7},{2,0},{3,1},{4,2},{5,3},{6,4},{7,5},{8,14},{9,15},{10,... | collective-permute-start | bytes 1376264 | tf_op jit(solution)/shard_map/ppermute | solution.py:379
  102.3 14.4 %collective-permute-start.29 = (bf16[112,2048]{1,0:T(8,128)(2,1)S(1)}, bf16[112,2048]{1,0:T(8,128)(2,1)S(1)}, u32[]{:S(2)}, u32[]{:S(2)}) collective-permute-start(bf16[112,2048]{1,0:T(8,128)(2,1)S(1)} %get-tuple-element.159), channel_id=1, source_target_pairs={{0,8},{8,0},{16,24},{24,16},{1,9},{9,1},{17,25},{25,17},{2,10},{10... | collective-permute-start | bytes 1376264 | tf_op jit(solution)/shard_map/ppermute | solution.py:371
  103.1 13.7 %collective-permute-start.30 = (bf16[112,2048]{1,0:T(8,128)(2,1)S(1)}, bf16[112,2048]{1,0:T(8,128)(2,1)S(1)}, u32[]{:S(2)}, u32[]{:S(2)}) collective-permute-start(bf16[112,2048]{1,0:T(8,128)(2,1)S(1)} %get-tuple-element.160), channel_id=1, source_target_pairs={{0,16},{8,24},{16,0},{24,8},{1,17},{9,25},{17,1},{25,9},{2,18},{10... | collective-permute-start | bytes 1376264 | tf_op jit(solution)/shard_map/ppermute | solution.py:375
  114.2 7.4 %collective-permute-start.33 = (bf16[64,2048]{1,0:T(8,128)(2,1)S(1)}, bf16[64,2048]{1,0:T(8,128)(2,1)S(1)}, u32[]{:S(2)}, u32[]{:S(2)}) collective-permute-start(bf16[64,2048]{1,0:T(8,128)(2,1)S(1)} %get-tuple-element.182), channel_id=1, source_target_pairs={{0,8},{8,0},{16,24},{24,16},{1,9},{9,1},{17,25},{25,17},{2,10},{10... | collective-permute-start | bytes 786440 | tf_op jit(solution)/shard_map/ppermute | solution.py:371
  115.2 28.4 %copy-start.1 = (bf16[1,111,2048]{2,1,0:T(8,128)(2,1)S(1)}, bf16[1,111,2048]{2,1,0:T(8,128)(2,1)}, u32[]{:S(2)}) copy-start(bf16[1,111,2048]{2,1,0:T(8,128)(2,1)} %param.21) | copy-start | bytes 1363972
  115.2 6.4 %collective-permute-start.32 = (bf16[48,2048]{1,0:T(8,128)(2,1)S(1)}, bf16[48,2048]{1,0:T(8,128)(2,1)S(1)}, u32[]{:S(2)}, u32[]{:S(2)}) collective-permute-start(bf16[48,2048]{1,0:T(8,128)(2,1)S(1)} %get-tuple-element.181), channel_id=1, source_target_pairs={{0,16},{8,24},{16,0},{24,8},{1,17},{9,25},{17,1},{25,9},{2,18},{10... | collective-permute-start | bytes 589832 | tf_op jit(solution)/shard_map/ppermute | solution.py:375
  116.9 11.7 %collective-permute-start.31 = (bf16[112,2048]{1,0:T(8,128)(2,1)S(1)}, bf16[112,2048]{1,0:T(8,128)(2,1)S(1)}, u32[]{:S(2)}, u32[]{:S(2)}) collective-permute-start(bf16[112,2048]{1,0:T(8,128)(2,1)S(1)} %add_convert_fusion.1), channel_id=1, source_target_pairs={{0,2},{1,3},{2,4},{3,5},{4,6},{5,7},{6,0},{7,1},{8,10},{9,11},{10,... | collective-permute-start | bytes 1376264 | tf_op jit(solution)/shard_map/ppermute | solution.py:379
  117.4 12.0 %collective-permute-start.40 = (bf16[64,2048]{1,0:T(8,128)(2,1)S(1)}, bf16[64,2048]{1,0:T(8,128)(2,1)S(1)}, u32[]{:S(2)}, u32[]{:S(2)}) collective-permute-start(bf16[64,2048]{1,0:T(8,128)(2,1)S(1)} %get-tuple-element.199), channel_id=1, source_target_pairs={{0,8},{8,0},{16,24},{24,16},{1,9},{9,1},{17,25},{25,17},{2,10},{10... | collective-permute-start | bytes 786440 | tf_op jit(solution)/shard_map/ppermute | solution.py:371
  121.7 9.3 %collective-permute-start.41 = (bf16[64,2048]{1,0:T(8,128)(2,1)S(1)}, bf16[64,2048]{1,0:T(8,128)(2,1)S(1)}, u32[]{:S(2)}, u32[]{:S(2)}) collective-permute-start(bf16[64,2048]{1,0:T(8,128)(2,1)S(1)} %get-tuple-element.200), channel_id=1, source_target_pairs={{0,16},{8,24},{16,0},{24,8},{1,17},{9,25},{17,1},{25,9},{2,18},{10... | collective-permute-start | bytes 786440 | tf_op jit(solution)/shard_map/ppermute | solution.py:375
  122.6 8.9 %collective-permute-start.37 = (bf16[48,2048]{1,0:T(8,128)(2,1)S(1)}, bf16[48,2048]{1,0:T(8,128)(2,1)S(1)}, u32[]{:S(2)}, u32[]{:S(2)}) collective-permute-start(bf16[48,2048]{1,0:T(8,128)(2,1)S(1)} %add_convert_fusion.4), channel_id=1, source_target_pairs={{0,8},{8,0},{16,24},{24,16},{1,9},{9,1},{17,25},{25,17},{2,10},{10... | collective-permute-start | bytes 589832 | tf_op jit(solution)/shard_map/ppermute | solution.py:371
  123.3 11.8 %collective-permute-start.38 = (bf16[48,2048]{1,0:T(8,128)(2,1)S(1)}, bf16[48,2048]{1,0:T(8,128)(2,1)S(1)}, u32[]{:S(2)}, u32[]{:S(2)}) collective-permute-start(bf16[48,2048]{1,0:T(8,128)(2,1)S(1)} %get-tuple-element.197), channel_id=1, source_target_pairs={{0,16},{8,24},{16,0},{24,8},{1,17},{9,25},{17,1},{25,9},{2,18},{10... | collective-permute-start | bytes 589832 | tf_op jit(solution)/shard_map/ppermute | solution.py:375
  128.7 14.8 %collective-permute-start.35 = (bf16[112,2048]{1,0:T(8,128)(2,1)S(1)}, bf16[112,2048]{1,0:T(8,128)(2,1)S(1)}, u32[]{:S(2)}, u32[]{:S(2)}) collective-permute-start(bf16[112,2048]{1,0:T(8,128)(2,1)S(1)} %get-tuple-element.189), channel_id=1, source_target_pairs={{0,8},{8,0},{16,24},{24,16},{1,9},{9,1},{17,25},{25,17},{2,10},{10... | collective-permute-start | bytes 1376264 | tf_op jit(solution)/shard_map/ppermute | solution.py:371
  129.4 14.2 %collective-permute-start.36 = (bf16[112,2048]{1,0:T(8,128)(2,1)S(1)}, bf16[112,2048]{1,0:T(8,128)(2,1)S(1)}, u32[]{:S(2)}, u32[]{:S(2)}) collective-permute-start(bf16[112,2048]{1,0:T(8,128)(2,1)S(1)} %get-tuple-element.190), channel_id=1, source_target_pairs={{0,16},{8,24},{16,0},{24,8},{1,17},{9,25},{17,1},{25,9},{2,18},{10... | collective-permute-start | bytes 1376264 | tf_op jit(solution)/shard_map/ppermute | solution.py:375
  131.1 12.4 %collective-permute-start.42 = (bf16[64,2048]{1,0:T(8,128)(2,1)S(1)}, bf16[64,2048]{1,0:T(8,128)(2,1)S(1)}, u32[]{:S(2)}, u32[]{:S(2)}) collective-permute-start(bf16[64,2048]{1,0:T(8,128)(2,1)S(1)} %add_convert_fusion.2), channel_id=1, source_target_pairs={{0,2},{1,3},{2,4},{3,5},{4,6},{5,7},{6,0},{7,1},{8,10},{9,11},{10,... | collective-permute-start | bytes 786440 | tf_op jit(solution)/shard_map/ppermute | solution.py:379
  135.3 8.3 %collective-permute-start.39 = (bf16[48,2048]{1,0:T(8,128)(2,1)S(1)}, bf16[48,2048]{1,0:T(8,128)(2,1)S(1)}, u32[]{:S(2)}, u32[]{:S(2)}) collective-permute-start(bf16[48,2048]{1,0:T(8,128)(2,1)S(1)} %add_convert_fusion.3), channel_id=1, source_target_pairs={{0,2},{1,3},{2,4},{3,5},{4,6},{5,7},{6,0},{7,1},{8,10},{9,11},{10,... | collective-permute-start | bytes 589832 | tf_op jit(solution)/shard_map/ppermute | solution.py:379
